TPU v7x, 128 devices: a whole 4x4x4 slice. The times are simulated.
128 devices in a mesh: loop: 8 (over x_hi, z), rep: 8 (over y, x_lo), sec: 2 (over core).
Axes of the slice: x: 4 (x_hi: 2, x_lo: 2; x = x_hi * 2 + x_lo), y: 4, z: 4, core: 2. Of those that a mesh axis runs over, the one named last changes fastest.
Arguments:
- student: bfloat16 [12288, 1024], P(('loop', 'rep'), 'sec'), may hold values from -6 to 6
- teacher: bfloat16 [12288, 4096], P(('loop', 'rep'), 'sec'), may hold values from -6 to 6
Outputs:
- student_grad: float32 [12288, 1024], P(('loop', 'rep'), 'sec')
All inputs are finite; a program needn't handle non-finite values.
Results may differ from a plain program's by a relative error of at most 0.022.
Values may be sent and summed in bfloat16 or wider, within the bound.
No kernel may reach another device: no remote copies, remote signals or barrier semaphores. Data moves between devices by JAX's collectives and lax.ppermute only.
A program may use at most 128 MiB of HBM per device.

v0:
```python
import math

import jax
import jax.numpy as jnp
from jax import lax
from jax.sharding import PartitionSpec as P

DS = 1024


def passed_along(array, axis, by):
    length = lax.axis_size(axis)
    return lax.ppermute(array, axis, [(i, (i + by) % length) for i in range(length)])


def rows_product(left, right):
    return lax.dot_general(
        left, right, (((1,), (1,)), ((), ())), preferred_element_type=jnp.float32
    )


def body(student, teacher):
    eps = 1e-06
    rows = student.shape[0]
    loops = lax.axis_size("loop")
    half = loops // 2
    passages = rows * lax.axis_size("rep") * loops
    coef = 32.0 * DS / math.sqrt(passages)
    s32 = student.astype(jnp.float32)
    t32 = teacher.astype(jnp.float32)
    ssq_s, ssq_t = lax.psum((jnp.sum(s32 * s32, axis=1), jnp.sum(t32 * t32, axis=1)), "sec")
    inv_s = lax.rsqrt(ssq_s + eps)
    norm_s = (s32 * inv_s[:, None]).astype(jnp.bfloat16)
    norm_t = (t32 * lax.rsqrt(ssq_t + eps)[:, None]).astype(jnp.bfloat16)
    home_s, home_t = (
        lax.all_gather(norm_s, "rep", axis=0, tiled=True),
        lax.all_gather(norm_t, "rep", axis=0, tiled=True),
    )
    base_s, base_t = (norm_s, norm_t)
    visit_s = base_s
    visit_t = base_t
    carried = jnp.zeros((rows, base_s.shape[1]), jnp.float32)
    row_total = jnp.zeros((home_s.shape[0], base_s.shape[1]), jnp.float32)
    for step in range(half + 1):
        if step > 0:
            visit_s, visit_t = passed_along((visit_s, visit_t), "loop", 1)
        if step > 1:
            carried = passed_along(carried, "loop", 1)
        partial_tile = rows_product(home_s, visit_s) - rows_product(home_t, visit_t)
        tile = lax.psum(partial_tile, "sec").astype(jnp.bfloat16)
        row_total = row_total + jnp.dot(tile, visit_s, preferred_element_type=jnp.float32)
        if 0 < step < half:
            carried = carried + lax.dot_general(
                tile, home_s, (((0,), (0,)), ((), ())), preferred_element_type=jnp.float32
            )
    row_part = lax.psum_scatter(row_total, "rep", scatter_dimension=0, tiled=True)
    back = passed_along(carried, "loop", half)
    grad_n = coef * (row_part + back)
    norm_f = norm_s.astype(jnp.float32)
    inner = lax.psum(jnp.sum(grad_n * norm_f, axis=1), "sec")
    return (grad_n - inner[:, None] * norm_f) * inv_s[:, None]


def solution(mesh):
    placed = (P(("loop", "rep"), "sec"), P(("loop", "rep"), "sec"))
    return jax.shard_map(
        body, mesh=mesh, in_specs=placed, out_specs=P(("loop", "rep"), "sec"), check_vma=False
    )
```

profile of v0, /device:TPU:97, one launch (start us, length us, event | category | flops | bytes accessed | tf_op | source)
XLA Modules:
  0.0 431.0 jit_solution(4953447766373892660)
XLA Ops:
  6.5 1.0 fusion.5
  7.6 1.4 fusion
  9.0 2.8 all-reduce.1
  11.8 2.2 fusion.1
  14.1 1.4 collective-permute-start.1
  15.6 0.8 fusion.6
  16.4 24.3 %collective-permute-done.1 = bf16[192,2048]{1,0:T(8,128)(2,1)S(1)} collective-permute-done((bf16[192,2048]{1,0:T(8,128)(2,1)}, bf16[192,2048]{1,0:T(8,128)(2,1)S(1)}, u32[]{:S(2)}, u32[]{:S(2)}) %collective-permute-start.1) | collective-permute-done | bytes 786464 | tf_op jit(solution)/shard_map/ppermute | solution.py:13
  40.7 5.7 %collective-permute-start.3 = (bf16[192,2048]{1,0:T(8,128)(2,1)S(1)}, bf16[192,2048]{1,0:T(8,128)(2,1)S(1)}, u32[]{:S(2)}, u32[]{:S(2)}) collective-permute-start(bf16[192,2048]{1,0:T(8,128)(2,1)S(1)} %collective-permute-done.1), channel_id=1, source_target_pairs={{0,16},{16,32},{32,48},{48,64},{64,80},{80,96},{96,112},{112,0},{1... | collective-permute-start | bytes 2359304 | tf_op jit(solution)/shard_map/ppermute | solution.py:13
  46.4 33.1 %collective-permute-done.3 = bf16[192,2048]{1,0:T(8,128)(2,1)S(1)} collective-permute-done((bf16[192,2048]{1,0:T(8,128)(2,1)S(1)}, bf16[192,2048]{1,0:T(8,128)(2,1)S(1)}, u32[]{:S(2)}, u32[]{:S(2)}) %collective-permute-start.3) | collective-permute-done | bytes 786464 | tf_op jit(solution)/shard_map/ppermute | solution.py:13
  79.5 5.8 %collective-permute-start.5 = (bf16[192,2048]{1,0:T(8,128)(2,1)S(1)}, bf16[192,2048]{1,0:T(8,128)(2,1)}, u32[]{:S(2)}, u32[]{:S(2)}) collective-permute-start(bf16[192,2048]{1,0:T(8,128)(2,1)S(1)} %collective-permute-done.3), channel_id=1, source_target_pairs={{0,16},{16,32},{32,48},{48,64},{64,80},{80,96},{96,112},{112,0},{1... | collective-permute-start | bytes 2359304 | tf_op jit(solution)/shard_map/ppermute | solution.py:13
  85.4 41.3 %collective-permute-done = bf16[192,512]{1,0:T(8,128)(2,1)S(1)} collective-permute-done((bf16[192,512]{1,0:T(8,128)(2,1)}, bf16[192,512]{1,0:T(8,128)(2,1)S(1)}, u32[]{:S(2)}, u32[]{:S(2)}) %collective-permute-start) | collective-permute-done | bytes 196640 | tf_op jit(solution)/shard_map/ppermute | solution.py:13
  126.7 0.7 copy-done.6
  127.4 5.7 %collective-permute-start.2 = (bf16[192,512]{1,0:T(8,128)(2,1)S(1)}, bf16[192,512]{1,0:T(8,128)(2,1)S(1)}, u32[]{:S(2)}, u32[]{:S(2)}) collective-permute-start(bf16[192,512]{1,0:T(8,128)(2,1)S(1)} %collective-permute-done), channel_id=1, source_target_pairs={{0,16},{16,32},{32,48},{48,64},{64,80},{80,96},{96,112},{112,0},{1... | collective-permute-start | bytes 589832 | tf_op jit(solution)/shard_map/ppermute | solution.py:13
  133.1 7.3 %collective-permute-done.2 = bf16[192,512]{1,0:T(8,128)(2,1)S(1)} collective-permute-done((bf16[192,512]{1,0:T(8,128)(2,1)S(1)}, bf16[192,512]{1,0:T(8,128)(2,1)S(1)}, u32[]{:S(2)}, u32[]{:S(2)}) %collective-permute-start.2) | collective-permute-done | bytes 196640 | tf_op jit(solution)/shard_map/ppermute | solution.py:13
  140.4 0.7 copy-done.9
  141.1 5.8 %collective-permute-start.4 = (bf16[192,512]{1,0:T(8,128)(2,1)S(1)}, bf16[192,512]{1,0:T(8,128)(2,1)}, u32[]{:S(2)}, u32[]{:S(2)}) collective-permute-start(bf16[192,512]{1,0:T(8,128)(2,1)S(1)} %collective-permute-done.2), channel_id=1, source_target_pairs={{0,16},{16,32},{32,48},{48,64},{64,80},{80,96},{96,112},{112,0},{1... | collective-permute-start | bytes 589832 | tf_op jit(solution)/shard_map/ppermute | solution.py:13
  146.9 7.0 %collective-permute-done.4 = bf16[192,512]{1,0:T(8,128)(2,1)} collective-permute-done((bf16[192,512]{1,0:T(8,128)(2,1)S(1)}, bf16[192,512]{1,0:T(8,128)(2,1)}, u32[]{:S(2)}, u32[]{:S(2)}) %collective-permute-start.4) | collective-permute-done | bytes 196640 | tf_op jit(solution)/shard_map/ppermute | solution.py:13
  153.8 5.9 %collective-permute-start.6 = (bf16[192,512]{1,0:T(8,128)(2,1)}, bf16[192,512]{1,0:T(8,128)(2,1)}, u32[]{:S(2)}, u32[]{:S(2)}) collective-permute-start(bf16[192,512]{1,0:T(8,128)(2,1)} %collective-permute-done.4), channel_id=1, source_target_pairs={{0,16},{16,32},{32,48},{48,64},{64,80},{80,96},{96,112},{112,0},{1... | collective-permute-start | bytes 589832 | tf_op jit(solution)/shard_map/ppermute | solution.py:13
  159.8 60.6 %all-gather.5.cloned.1.call-done = bf16[1536,2048]{1,0:T(8,128)(2,1)} async-done(((bf16[192,2048]{1,0:T(8,128)(2,1)}), bf16[1536,2048]{1,0:T(8,128)(2,1)}) %all-gather.5.cloned.1.call-update) | async-done | bytes 6291472 | tf_op jit(solution)/shard_map/all_gather | solution.py:37
  220.4 4.8 %fusion.18 = f32[1536,192]{1,0:T(8,128)S(1)} fusion(bf16[1536,2048]{1,0:T(8,128)(2,1)} %all-gather.5.cloned.1.call-done, bf16[192,2048]{1,0:T(8,128)(2,1)} %fusion.1), kind=kOutput, calls=%fused_computation.37 | convolution fusion | flops 1207959552 | bytes 8257536 | tf_op jit(solution)/shard_map/dot_general | solution.py:17
  225.2 38.1 %all-gather.3.cloned.1.call-done = bf16[1536,512]{1,0:T(8,128)(2,1)} async-done(((bf16[192,512]{1,0:T(8,128)(2,1)}), bf16[1536,512]{1,0:T(8,128)(2,1)}) %all-gather.3.cloned.1.call-update) | async-done | bytes 1572880 | tf_op jit(solution)/shard_map/all_gather | solution.py:36
  263.3 2.1 convolution_subtract_fusion.1
  265.5 5.3 %fusion.19 = f32[1536,192]{0,1:T(8,128)S(1)} fusion(bf16[1536,2048]{1,0:T(8,128)(2,1)} %all-gather.5.cloned.1.call-done, bf16[192,2048]{1,0:T(8,128)(2,1)} %copy-done.13), kind=kOutput, calls=%fused_computation.38 | convolution fusion | flops 1207959552 | bytes 8257536 | tf_op jit(solution)/shard_map/dot_general | solution.py:17
  270.8 1.7 convolution_subtract_fusion.4
  272.6 2.2 fusion.20
  274.8 1.7 convolution_subtract_fusion.3
  276.5 3.3 fusion.21
  279.8 3.0 fusion.22
  282.8 2.6 convolution_subtract_fusion.2
  285.5 2.7 convolution_subtract_fusion
  288.2 23.9 %all-reduce.3 = (bf16[1536,192]{1,0:T(8,128)(2,1)}, bf16[1536,192]{0,1:T(8,128)(2,1)}, bf16[1536,192]{0,1:T(8,128)(2,1)}, bf16[1536,192]{0,1:T(8,128)(2,1)}, bf16[1536,192]{1,0:T(8,128)(2,1)}) all-reduce(f32[1536,192]{1,0:T(8,128)S(1)} %convolution_subtract_fusion.1, ...), channel_id=1, replica_groups=mesh['loop'=8,'rep'=8,'sec'=2] {'sec'}, use_global_device_ids=true, to_apply=%region_4.0 | all-reduce | flops 1474560 | bytes 8847360 | tf_op jit(solution)/shard_map/psum | solution.py:50
  312.1 1.8 fusion.23
  313.9 0.6 convolution_add_fusion.3
  315.0 0.6 convolution_add_fusion.2
  316.1 1.6 convolution_add_fusion.1
  317.7 3.1 convolution_add_fusion
  321.3 2.2 collective-permute-start.8
  323.5 11.7 %collective-permute-done.8 = f32[192,512]{1,0:T(8,128)S(1)} collective-permute-done((f32[192,512]{1,0:T(8,128)S(1)}, f32[192,512]{1,0:T(8,128)S(1)}, u32[]{:S(2)}, u32[]{:S(2)}) %collective-permute-start.8) | collective-permute-done | bytes 393248 | tf_op jit(solution)/shard_map/ppermute | solution.py:13
  335.2 0.5 convolution_add_fusion.4
  335.7 5.9 %collective-permute-start.9 = (f32[192,512]{1,0:T(8,128)S(1)}, f32[192,512]{1,0:T(8,128)S(1)}, u32[]{:S(2)}, u32[]{:S(2)}) collective-permute-start(f32[192,512]{1,0:T(8,128)S(1)} %convolution_add_fusion.4), channel_id=1, source_target_pairs={{0,16},{16,32},{32,48},{48,64},{64,80},{80,96},{96,112},{112,0},{1... | collective-permute-start | bytes 1179656 | tf_op jit(solution)/shard_map/ppermute | solution.py:13
  342.0 16.3 %collective-permute-done.9 = f32[192,512]{1,0:T(8,128)S(1)} collective-permute-done((f32[192,512]{1,0:T(8,128)S(1)}, f32[192,512]{1,0:T(8,128)S(1)}, u32[]{:S(2)}, u32[]{:S(2)}) %collective-permute-start.9) | collective-permute-done | bytes 393248 | tf_op jit(solution)/shard_map/ppermute | solution.py:13
  358.4 5.9 %collective-permute-start.10 = (f32[192,512]{1,0:T(8,128)S(1)}, f32[192,512]{1,0:T(8,128)S(1)}, u32[]{:S(2)}, u32[]{:S(2)}) collective-permute-start(f32[192,512]{1,0:T(8,128)S(1)} %add.52), channel_id=1, source_target_pairs={{0,16},{16,32},{32,48},{48,64},{64,80},{80,96},{96,112},{112,0},{1... | collective-permute-start | bytes 1179656 | tf_op jit(solution)/shard_map/ppermute | solution.py:13
  364.3 16.5 %collective-permute-done.10 = f32[192,512]{1,0:T(8,128)S(1)} collective-permute-done((f32[192,512]{1,0:T(8,128)S(1)}, f32[192,512]{1,0:T(8,128)S(1)}, u32[]{:S(2)}, u32[]{:S(2)}) %collective-permute-start.10) | collective-permute-done | bytes 393248 | tf_op jit(solution)/shard_map/ppermute | solution.py:13
  380.8 19.7 %collective-permute-done.11 = f32[192,512]{1,0:T(8,128)S(1)} collective-permute-done((f32[192,512]{1,0:T(8,128)S(1)}, f32[192,512]{1,0:T(8,128)S(1)}, u32[]{:S(2)}, u32[]{:S(2)}) %collective-permute-start.11) | collective-permute-done | bytes 393248 | tf_op jit(solution)/shard_map/ppermute | solution.py:13
  400.5 18.3 %reduce-scatter.2.cloned.1.call-done = f32[192,512]{1,0:T(8,128)} async-done(((f32[1536,512]{1,0:T(8,128)}), f32[192,512]{1,0:T(8,128)}) %reduce-scatter.2.cloned.1.call-update) | async-done | bytes 393232 | tf_op jit(solution)/shard_map/reduce_scatter | solution.py:56
  418.8 1.2 fusion.7
  420.0 2.5 psum.63
  422.6 1.9 fusion.9
  (52 shorter events, 2.2 us)
Async XLA Ops:
  6.5 213.9 %all-gather.5.cloned.1.call-start = ((), (), s32[]{:S(2)}) async-start(), calls=%async_computation.2 | async-start | bytes 7077888 | tf_op jit(solution)/shard_map/all_gather | solution.py:37
  7.6 8.0 %copy-start.2 = (bf16[192,512]{1,0:T(8,128)(2,1)S(1)}, bf16[192,512]{1,0:T(8,128)(2,1)}, u32[]{:S(2)}) copy-start(bf16[192,512]{1,0:T(8,128)(2,1)} %param.2) | copy-start | bytes 589828
  14.0 249.3 %all-gather.3.cloned.1.call-start = ((), (), s32[]{:S(2)}) async-start(), calls=%async_computation.1 | async-start | bytes 1769472 | tf_op jit(solution)/shard_map/all_gather | solution.py:36
  14.1 26.6 %collective-permute-start.1 = (bf16[192,2048]{1,0:T(8,128)(2,1)}, bf16[192,2048]{1,0:T(8,128)(2,1)S(1)}, u32[]{:S(2)}, u32[]{:S(2)}) collective-permute-start(bf16[192,2048]{1,0:T(8,128)(2,1)} %fusion.1), channel_id=1, source_target_pairs={{0,16},{16,32},{32,48},{48,64},{64,80},{80,96},{96,112},{112,0},{1... | collective-permute-start | bytes 2359304 | tf_op jit(solution)/shard_map/ppermute | solution.py:13
  16.4 246.9 %copy-start.1 = (bf16[192,512]{1,0:T(8,128)(2,1)S(1)}, bf16[192,512]{1,0:T(8,128)(2,1)}, u32[]{:S(2)}) copy-start(bf16[192,512]{1,0:T(8,128)(2,1)} %fusion.6) | copy-start | bytes 589828
  16.4 402.5 %reduce-scatter.2.cloned.1.call-start = ((), (), s32[]{:S(2)}) async-start(), calls=%async_computation.3 | async-start | bytes 3538944 | tf_op jit(solution)/shard_map/reduce_scatter | solution.py:56
  40.7 119.1 %copy-start.13 = (bf16[192,2048]{1,0:T(8,128)(2,1)}, bf16[192,2048]{1,0:T(8,128)(2,1)S(1)}, u32[]{:S(2)}) copy-start(bf16[192,2048]{1,0:T(8,128)(2,1)S(1)} %collective-permute-done.1) | copy-start | bytes 2359300
  40.7 38.8 %collective-permute-start.3 = (bf16[192,2048]{1,0:T(8,128)(2,1)S(1)}, bf16[192,2048]{1,0:T(8,128)(2,1)S(1)}, u32[]{:S(2)}, u32[]{:S(2)}) collective-permute-start(bf16[192,2048]{1,0:T(8,128)(2,1)S(1)} %collective-permute-done.1), channel_id=1, source_target_pairs={{0,16},{16,32},{32,48},{48,64},{64,80},{80,96},{96,112},{112,0},{1... | collective-permute-start | bytes 2359304 | tf_op jit(solution)/shard_map/ppermute | solution.py:13
  79.5 80.3 %copy-start.14 = (bf16[192,2048]{1,0:T(8,128)(2,1)}, bf16[192,2048]{1,0:T(8,128)(2,1)S(1)}, u32[]{:S(2)}) copy-start(bf16[192,2048]{1,0:T(8,128)(2,1)S(1)} %collective-permute-done.3) | copy-start | bytes 2359300
  79.5 80.3 %collective-permute-start.5 = (bf16[192,2048]{1,0:T(8,128)(2,1)S(1)}, bf16[192,2048]{1,0:T(8,128)(2,1)}, u32[]{:S(2)}, u32[]{:S(2)}) collective-permute-start(bf16[192,2048]{1,0:T(8,128)(2,1)S(1)} %collective-permute-done.3), channel_id=1, source_target_pairs={{0,16},{16,32},{32,48},{48,64},{64,80},{80,96},{96,112},{112,0},{1... | collective-permute-start | bytes 2359304 | tf_op jit(solution)/shard_map/ppermute | solution.py:13
  85.3 41.4 %collective-permute-start = (bf16[192,512]{1,0:T(8,128)(2,1)}, bf16[192,512]{1,0:T(8,128)(2,1)S(1)}, u32[]{:S(2)}, u32[]{:S(2)}) collective-permute-start(bf16[192,512]{1,0:T(8,128)(2,1)} %fusion.6), channel_id=1, source_target_pairs={{0,16},{16,32},{32,48},{48,64},{64,80},{80,96},{96,112},{112,0},{1... | collective-permute-start | bytes 589832 | tf_op jit(solution)/shard_map/ppermute | solution.py:13
  126.7 0.7 copy-start.6
  127.4 13.0 %collective-permute-start.2 = (bf16[192,512]{1,0:T(8,128)(2,1)S(1)}, bf16[192,512]{1,0:T(8,128)(2,1)S(1)}, u32[]{:S(2)}, u32[]{:S(2)}) collective-permute-start(bf16[192,512]{1,0:T(8,128)(2,1)S(1)} %collective-permute-done), channel_id=1, source_target_pairs={{0,16},{16,32},{32,48},{48,64},{64,80},{80,96},{96,112},{112,0},{1... | collective-permute-start | bytes 589832 | tf_op jit(solution)/shard_map/ppermute | solution.py:13
  140.4 0.7 copy-start.9
  141.1 12.8 %collective-permute-start.4 = (bf16[192,512]{1,0:T(8,128)(2,1)S(1)}, bf16[192,512]{1,0:T(8,128)(2,1)}, u32[]{:S(2)}, u32[]{:S(2)}) collective-permute-start(bf16[192,512]{1,0:T(8,128)(2,1)S(1)} %collective-permute-done.2), channel_id=1, source_target_pairs={{0,16},{16,32},{32,48},{48,64},{64,80},{80,96},{96,112},{112,0},{1... | collective-permute-start | bytes 589832 | tf_op jit(solution)/shard_map/ppermute | solution.py:13
  153.8 131.6 %collective-permute-start.6 = (bf16[192,512]{1,0:T(8,128)(2,1)}, bf16[192,512]{1,0:T(8,128)(2,1)}, u32[]{:S(2)}, u32[]{:S(2)}) collective-permute-start(bf16[192,512]{1,0:T(8,128)(2,1)} %collective-permute-done.4), channel_id=1, source_target_pairs={{0,16},{16,32},{32,48},{48,64},{64,80},{80,96},{96,112},{112,0},{1... | collective-permute-start | bytes 589832 | tf_op jit(solution)/shard_map/ppermute | solution.py:13
  159.8 120.1 %collective-permute-start.7 = (bf16[192,2048]{1,0:T(8,128)(2,1)}, bf16[192,2048]{1,0:T(8,128)(2,1)}, u32[]{:S(2)}, u32[]{:S(2)}) collective-permute-start(bf16[192,2048]{1,0:T(8,128)(2,1)} %collective-permute-done.5), channel_id=1, source_target_pairs={{0,16},{16,32},{32,48},{48,64},{64,80},{80,96},{96,112},{112,0},{1... | collective-permute-start | bytes 2359304 | tf_op jit(solution)/shard_map/ppermute | solution.py:13
  263.3 9.2 %slice-start = ((s8[6291456]{0:T(1024)(128)(4,1)}), s8[4194304]{0:T(1024)(128)(4,1)S(1)}, s32[]{:S(2)}) async-start(s8[6291456]{0:T(1024)(128)(4,1)} %bitcast.36), calls=%async_computation.4 | async-start | bytes 8388608
  265.5 5.4 %copy-start = (bf16[1536,512]{1,0:T(8,128)(2,1)S(1)}, bf16[1536,512]{1,0:T(8,128)(2,1)}, u32[]{:S(2)}) copy-start(bf16[1536,512]{1,0:T(8,128)(2,1)} %all-gather.3.cloned.1.call-done) | copy-start | bytes 4718596
  265.5 5.4 %copy-start.7 = (bf16[192,512]{1,0:T(8,128)(2,1)S(1)}, bf16[192,512]{1,0:T(8,128)(2,1)}, u32[]{:S(2)}) copy-start(bf16[192,512]{1,0:T(8,128)(2,1)} %copy-done.6) | copy-start | bytes 589828
  265.5 7.1 %slice-start.1 = ((s8[6291456]{0:T(1024)(128)(4,1)}), s8[2097152]{0:T(1024)(128)(4,1)S(1)}, s32[]{:S(2)}) async-start(s8[6291456]{0:T(1024)(128)(4,1)} %bitcast.36), calls=%async_computation.5 | async-start | bytes 4194304
  270.8 1.7 copy-start.15
  272.5 2.2 copy-start.10
  312.1 1.8 copy-start.4
  312.1 1.8 copy-start.8
  313.9 1.1 copy-start.5
  313.9 1.1 copy-start.11
  315.0 1.1 copy-start.3
  316.1 1.6 copy-start.12
  321.3 13.9 %collective-permute-start.8 = (f32[192,512]{1,0:T(8,128)S(1)}, f32[192,512]{1,0:T(8,128)S(1)}, u32[]{:S(2)}, u32[]{:S(2)}) collective-permute-start(f32[192,512]{1,0:T(8,128)S(1)} %fusion.25), channel_id=1, source_target_pairs={{0,16},{16,32},{32,48},{48,64},{64,80},{80,96},{96,112},{112,0},{1... | collective-permute-start | bytes 1179656 | tf_op jit(solution)/shard_map/ppermute | solution.py:13
  335.7 22.7 %collective-permute-start.9 = (f32[192,512]{1,0:T(8,128)S(1)}, f32[192,512]{1,0:T(8,128)S(1)}, u32[]{:S(2)}, u32[]{:S(2)}) collective-permute-start(f32[192,512]{1,0:T(8,128)S(1)} %convolution_add_fusion.4), channel_id=1, source_target_pairs={{0,16},{16,32},{32,48},{48,64},{64,80},{80,96},{96,112},{112,0},{1... | collective-permute-start | bytes 1179656 | tf_op jit(solution)/shard_map/ppermute | solution.py:13
  358.4 22.4 %collective-permute-start.10 = (f32[192,512]{1,0:T(8,128)S(1)}, f32[192,512]{1,0:T(8,128)S(1)}, u32[]{:S(2)}, u32[]{:S(2)}) collective-permute-start(f32[192,512]{1,0:T(8,128)S(1)} %add.52), channel_id=1, source_target_pairs={{0,16},{16,32},{32,48},{48,64},{64,80},{80,96},{96,112},{112,0},{1... | collective-permute-start | bytes 1179656 | tf_op jit(solution)/shard_map/ppermute | solution.py:13
  380.8 19.7 %collective-permute-start.11 = (f32[192,512]{1,0:T(8,128)S(1)}, f32[192,512]{1,0:T(8,128)S(1)}, u32[]{:S(2)}, u32[]{:S(2)}) collective-permute-start(f32[192,512]{1,0:T(8,128)S(1)} %collective-permute-done.10), channel_id=1, source_target_pairs={{0,64},{16,80},{32,96},{48,112},{64,0},{80,16},{96,32},{112,48},{1... | collective-permute-start | bytes 1179656 | tf_op jit(solution)/shard_map/ppermute | solution.py:13
Sparse Core Ops, SparseCore 0:
  14.2 206.2 all-gather.4
  222.1 41.1 all-gather.2
  321.0 97.8 reduce-scatter.1
where the time goes:
time: 432 us; the launch traced here: 431 us
  waiting for transfers between devices  294 us (68%)
  starting transfers between devices  44.5 us (10%)
  matrix products  38.6 us (9%)
  blocking collectives  29.3 us (7%)
  between operations  13.4 us (3%)
  other arithmetic  8.63 us (2%)
    ppermute x12, waiting for transfers between devices, passed_along(): lax.ppermute(array, axis, [(i, (i + by) % length) for i in range(length)])  177 us
    all_gather x1, waiting for transfers between devices, body(): lax.all_gather(norm_t, 'rep', axis=0, tiled=True)  60.6 us
    ppermute x12, starting transfers between devices, passed_along(): lax.ppermute(array, axis, [(i, (i + by) % length) for i in range(length)])  44.4 us
    all_gather x1, waiting for transfers between devices, body(): lax.all_gather(norm_s, 'rep', axis=0, tiled=True)  38.1 us
    dot_general x10, matrix products, rows_product(): lax.dot_general(left, right, (((1,), (1,)), ((), ())), preferred_element_...  29.5 us
    psum x1, blocking collectives, body(): tile = lax.psum(partial_tile, 'sec').astype(jnp.bfloat16)  23.9 us
    reduce_scatter x1, waiting for transfers between devices, body(): lax.psum_scatter(row_total, 'rep', scatter_dimension=0, tiled=True)  18.3 us
  transfers between devices with their start and end apart: 15, of which 12 were waited for; matrix products, arithmetic and copies ran while one was open for 7% of the time, Pallas kernels for 0%

commit v1 on v0

v1 whole, which is shorter than its diff:
```python
import itertools

import jax
import jax.numpy as jnp
from jax import lax
from jax.sharding import PartitionSpec as P

AXES = ("loop", "rep", "sec")
X, Y, Z = 0, 1, 2
SIZE = 4
GATHER = (Y, X)
FIRST = (Z, Y)
SECOND = (X, Z)


def index_of(chip, core):
    x, y, z = chip
    return (((x // 2) * SIZE + z) * 8 + y * 2 + x % 2) * 2 + core


def shifted(array, axis_of_core, by):
    pairs = []
    for chip in itertools.product(range(SIZE), repeat=3):
        for core in range(2):
            target = list(chip)
            axis = axis_of_core[core]
            target[axis] = (target[axis] + by) % SIZE
            pairs.append((index_of(chip, core), index_of(target, core)))
    return lax.ppermute(array, AXES, pairs)


def other_core(array):
    return lax.ppermute(array, "sec", [(0, 1), (1, 0)])


def place_along(axis_of_core):
    loop, rep, core = (lax.axis_index(name) for name in AXES)
    place = ((loop // SIZE) * 2 + rep % 2, rep // 2, loop % SIZE)
    return jnp.where(core == 0, place[axis_of_core[0]], place[axis_of_core[1]])


def block(array, which, size, axis):
    return lax.dynamic_slice_in_dim(array, which * size, size, axis)


def reduce_scattered(array, axis_of_core):
    place = place_along(axis_of_core)
    size = array.shape[0] // SIZE
    total = block(array, place, size, 0)
    for by in (1, 3, 2):
        part = block(array, (place + by) % SIZE, size, 0).astype(jnp.bfloat16)
        total = total + shifted(part, axis_of_core, by).astype(jnp.float32)
    return total


def all_gathered(array, axis_of_core):
    place = place_along(axis_of_core)
    parts = [array] + [shifted(array, axis_of_core, -by) for by in (1, 2, 3)]
    around = jnp.concatenate(parts + parts, axis=0)
    size = array.shape[0]
    return lax.dynamic_slice_in_dim(around, ((SIZE - place) % SIZE) * size, SIZE * size, 0)


def cross(left, right):
    return lax.dot_general(
        left, right, (((0,), (0,)), ((), ())), preferred_element_type=jnp.float32
    )


def body(student, teacher):
    eps = 1e-06
    rows, half = student.shape
    wide = teacher.shape[1]
    width = 2 * half
    groups = lax.axis_size("loop") * lax.axis_size("rep")
    passages = rows * groups
    coef = 32.0 * width / (passages**0.5)
    level = passages / width
    s_own, t_own = student.astype(jnp.float32), teacher.astype(jnp.float32)
    s_far, t_far = (other_core(a).astype(jnp.float32) for a in (student, teacher))

    def inverse(own, far):
        total = jnp.sum(own * own, axis=1) + jnp.sum(far * far, axis=1)
        return lax.rsqrt(total + eps)[:, None]

    inv_s, inv_t = inverse(s_own, s_far), inverse(t_own, t_far)
    norm_s, norm_sf = ((a * inv_s).astype(jnp.bfloat16) for a in (s_own, s_far))
    norm_t, norm_tf = ((a * inv_t).astype(jnp.bfloat16) for a in (t_own, t_far))

    place = place_along(GATHER)
    ss, ts = half // SIZE, wide // SIZE

    def features(by):
        which = (place + by) % SIZE
        pieces = [block(a, which, ss, 1) for a in (norm_s, norm_sf)]
        pieces += [block(a, which, ts, 1) for a in (norm_t, norm_tf)]
        return jnp.concatenate(pieces + [norm_s], axis=1)

    packs = [features(0)] + [shifted(features(by), GATHER, by) for by in (1, 2, 3)]
    pack = jnp.concatenate(packs, axis=0)
    feats = 2 * (ss + ts)
    left, right = pack[:, :feats], pack[:, feats:]
    product = cross(left, right)
    row = lax.broadcasted_iota(jnp.int32, (2 * ss, half), 0)
    col = lax.broadcasted_iota(jnp.int32, (2 * ss, half), 1)
    on_diagonal = (row < ss) & (col == row + place * ss)
    share = level * SIZE / groups
    gram = jnp.concatenate(
        [product[: 2 * ss] - jnp.where(on_diagonal, share, 0.0), -product[2 * ss :]], axis=0
    )
    piece = reduce_scattered(reduce_scattered(gram, FIRST), SECOND).astype(jnp.bfloat16)
    weights = all_gathered(all_gathered(piece, SECOND), FIRST)
    partial = jnp.dot(left, weights, preferred_element_type=jnp.float32)
    norm_f = norm_s.astype(jnp.float32)
    grad_n = partial[:rows] + level * norm_f
    for by in (1, 2, 3):
        sent = partial[by * rows : (by + 1) * rows].astype(jnp.bfloat16)
        grad_n = grad_n + shifted(sent, GATHER, -by).astype(jnp.float32)
    grad_n = coef * grad_n
    inner = jnp.sum(grad_n * norm_f, axis=1)
    inner = inner + other_core(inner)
    return (grad_n - inner[:, None] * norm_f) * inv_s


def solution(mesh):
    placed = (P(("loop", "rep"), "sec"), P(("loop", "rep"), "sec"))
    return jax.shard_map(
        body, mesh=mesh, in_specs=placed, out_specs=P(("loop", "rep"), "sec"), check_vma=False
    )
```

time: 432 us -> 114 us (0.26)
  the two profiles are of different devices: /device:TPU:97 before, /device:TPU:1 now
where the time goes in v1:
time: 114 us
  waiting for transfers between devices  45.2 us (40%)
  starting transfers between devices  32 us (28%)
  local copies, waits for them, and re-layouts  22.7 us (20%)
  other arithmetic  9.77 us (9%)
  matrix products  3.71 us (3%)
    ppermute x18, waiting for transfers between devices, shifted(): return lax.ppermute(array, AXES, pairs)  44.4 us
    ppermute x18, starting transfers between devices, shifted(): return lax.ppermute(array, AXES, pairs)  21.6 us
    unnamed x27, local copies, waits for them, and re-layouts  19.3 us
    ppermute x3, starting transfers between devices, other_core(): return lax.ppermute(array, 'sec', [(0, 1), (1, 0)])  10.4 us
    reduce_sum x4, other arithmetic, inverse(): total = jnp.sum(own * own, axis=1) + jnp.sum(far * far, axis=1)  2.78 us
    dot_general x1, matrix products, body(): partial = jnp.dot(left, weights, preferred_element_type=jnp.float32)  2.48 us
    concatenate x2, local copies, waits for them, and re-layouts, all_gathered(): around = jnp.concatenate(parts + parts, axis=0)  2.37 us
  transfers between devices with their start and end apart: 21, of which 14 were waited for; matrix products, arithmetic and copies ran while one was open for 9% of the time, Pallas kernels for 0%

profile of v1, /device:TPU:1, one launch (start us, length us, event | category | flops | bytes accessed | tf_op | source)
XLA Modules:
  0.0 113.6 jit_solution(1764194402161228404)
XLA Ops:
  0.0 1.4 %collective-permute-start = (bf16[192,512]{1,0:T(8,128)(2,1)}, bf16[192,512]{1,0:T(8,128)(2,1)S(1)}, u32[]{:S(2)}, u32[]{:S(2)}) collective-permute-start(bf16[192,512]{1,0:T(8,128)(2,1)} %param.2), channel_id=1, source_target_pairs={{0,1},{1,0},{2,3},{3,2},{4,5},{5,4},{6,7},{7,6},{8,9},{9,8},{10,11... | collective-permute-start | bytes 589832 | tf_op jit(solution)/shard_map/ppermute | solution.py:33
  1.4 1.0 fusion.27
  2.6 1.4 %fusion.4 = f32[192]{0:T(256)S(1)} fusion(bf16[192,2048]{1,0:T(8,128)(2,1)} %param.3), kind=kLoop, calls=%fused_computation.18 | loop fusion | flops 1179456 | bytes 787200 | tf_op jit(solution)/shard_map/reduce_sum | solution.py:83
  4.1 1.1 fusion.30
  5.2 0.7 constant_dynamic-update-slice_fusion.2
  5.9 0.7 constant_dynamic-update-slice_fusion.1
  7.4 0.9 dynamic-slice_dynamic-update-slice_fusion.7
  8.3 0.8 dynamic-slice_dynamic-update-slice_fusion.6
  9.2 0.9 constant_dynamic-update-slice_fusion
  10.1 2.6 %collective-permute-start.4 = (bf16[192,1792]{1,0:T(8,128)(2,1)}, bf16[192,1792]{1,0:T(8,128)(2,1)S(1)}, u32[]{:S(2)}, u32[]{:S(2)}) collective-permute-start(bf16[192,1792]{1,0:T(8,128)(2,1)} %get-tuple-element.27), channel_id=1, source_target_pairs={{0,12},{1,67},{16,28},{17,83},{32,44},{33,99},{48,60},{49,115},{4,... | collective-permute-start | bytes 2064392 | tf_op jit(solution)/shard_map/ppermute | solution.py:29
  13.9 14.4 %collective-permute-done.4 = bf16[192,1792]{1,0:T(8,128)(2,1)S(1)} collective-permute-done((bf16[192,1792]{1,0:T(8,128)(2,1)}, bf16[192,1792]{1,0:T(8,128)(2,1)S(1)}, u32[]{:S(2)}, u32[]{:S(2)}) %collective-permute-start.4) | collective-permute-done | bytes 688160 | tf_op jit(solution)/shard_map/ppermute | solution.py:29
  28.3 3.6 %collective-permute-done.2 = bf16[192,1792]{1,0:T(8,128)(2,1)S(1)} collective-permute-done((bf16[192,1792]{1,0:T(8,128)(2,1)}, bf16[192,1792]{1,0:T(8,128)(2,1)S(1)}, u32[]{:S(2)}, u32[]{:S(2)}) %collective-permute-start.2) | collective-permute-done | bytes 688160 | tf_op jit(solution)/shard_map/ppermute | solution.py:29
  32.2 1.2 %fusion.2 = f32[1280,512]{1,0:T(8,128)S(1)} fusion(bf16[768,1792]{1,0:T(8,128)(2,1)S(1)} %pad_maximum_fusion, bf16[192,1792]{1,0:T(8,128)(2,1)S(1)} %collective-permute-done.4, bf16[192,1792]{1,0:T(8,128)(2,1)S(1)} %collective-permute-done.3, bf16[192,1792]{1,0:T(8,128)(2,1)S(1)} %collective-permute-done.2, bf16[192,1792]{1,0:T(8,128)(2,1)S(1)} %get-tuple-element.26), kind=kOutput, calls=%fused_computation.16 | convolution fusion | flops 1009778688 | bytes 7340032 | tf_op jit(solution)/shard_map/dot_general | solution.py:65
  34.1 1.4 %fusion.23 = (bf16[320,512]{1,0:T(8,128)(2,1)}, bf16[320,512]{1,0:T(8,128)(2,1)}, bf16[320,512]{1,0:T(8,128)(2,1)}) fusion(s32[]{:T(128)S(6)} %select_n.178, f32[1024,512]{1,0:T(8,128)S(1)} %slice_negate_fusion, f32[256,512]{1,0:T(8,128)S(1)} %slice_subtract_fusion, s32[]{:T(128)S(6)} %select_n.180, s32[]{:T(128)S(6)} %select_n.182), kind=kLoop, calls=%fused_computation.37 | loop fusion | flops 1966080 | bytes 3604492 | tf_op jit(solution)/shard_map/convert_element_type | solution.py:51
  35.5 1.0 collective-permute-start.5
  36.5 1.7 %collective-permute-start.6 = (bf16[320,512]{1,0:T(8,128)(2,1)}, bf16[320,512]{1,0:T(8,128)(2,1)S(1)}, u32[]{:S(2)}, u32[]{:S(2)}) collective-permute-start(bf16[320,512]{1,0:T(8,128)(2,1)} %get-tuple-element.10), channel_id=1, source_target_pairs={{0,48},{1,13},{16,0},{17,29},{32,16},{33,45},{48,32},{49,61},{4,52... | collective-permute-start | bytes 983048 | tf_op jit(solution)/shard_map/ppermute | solution.py:29
  38.2 1.4 %collective-permute-start.7 = (bf16[320,512]{1,0:T(8,128)(2,1)}, bf16[320,512]{1,0:T(8,128)(2,1)}, u32[]{:S(2)}, u32[]{:S(2)}) collective-permute-start(bf16[320,512]{1,0:T(8,128)(2,1)} %get-tuple-element.11), channel_id=1, source_target_pairs={{0,32},{1,9},{16,48},{17,25},{32,0},{33,41},{48,16},{49,57},{4,36}... | collective-permute-start | bytes 983048 | tf_op jit(solution)/shard_map/ppermute | solution.py:29
  39.6 3.6 %collective-permute-done.5 = bf16[320,512]{1,0:T(8,128)(2,1)S(1)} collective-permute-done((bf16[320,512]{1,0:T(8,128)(2,1)}, bf16[320,512]{1,0:T(8,128)(2,1)S(1)}, u32[]{:S(2)}, u32[]{:S(2)}) %collective-permute-start.5) | collective-permute-done | bytes 327712 | tf_op jit(solution)/shard_map/ppermute | solution.py:29
  43.2 2.9 %collective-permute-done.6 = bf16[320,512]{1,0:T(8,128)(2,1)S(1)} collective-permute-done((bf16[320,512]{1,0:T(8,128)(2,1)}, bf16[320,512]{1,0:T(8,128)(2,1)S(1)}, u32[]{:S(2)}, u32[]{:S(2)}) %collective-permute-start.6) | collective-permute-done | bytes 327712 | tf_op jit(solution)/shard_map/ppermute | solution.py:29
  46.1 0.7 copy-done.4
  47.4 1.4 %fusion.21 = f32[320,512]{1,0:T(8,128)S(1)} fusion(s32[]{:T(128)S(6)} %select_n.176, f32[1024,512]{1,0:T(8,128)S(1)} %slice_negate_fusion, f32[256,512]{1,0:T(8,128)S(1)} %slice_subtract_fusion, bf16[320,512]{1,0:T(8,128)(2,1)} %collective-permute-done.7, bf16[320,512]{1,0:T(8,128)(2,1)} %copy-done.4, bf16[320,512]{1,0:T(8,128)(2,1)} %copy-done.3), kind=kLoop, calls=%fused_computation.35 | loop fusion | flops 1146880 | bytes 4259844 | tf_op jit(solution)/shard_map/add | solution.py:52
  48.9 1.7 %collective-permute-start.8 = (bf16[80,512]{1,0:T(8,128)(2,1)S(1)}, bf16[80,512]{1,0:T(8,128)(2,1)S(1)}, u32[]{:S(2)}, u32[]{:S(2)}) collective-permute-start(bf16[80,512]{1,0:T(8,128)(2,1)S(1)} %get-tuple-element.23), channel_id=1, source_target_pairs={{0,2},{1,17},{16,18},{17,33},{32,34},{33,49},{48,50},{49,1},{4,6},... | collective-permute-start | bytes 245768 | tf_op jit(solution)/shard_map/ppermute | solution.py:29
  50.6 3.6 %collective-permute-start.10 = (bf16[80,512]{1,0:T(8,128)(2,1)S(1)}, bf16[80,512]{1,0:T(8,128)(2,1)S(1)}, u32[]{:S(2)}, u32[]{:S(2)}) collective-permute-start(bf16[80,512]{1,0:T(8,128)(2,1)S(1)} %get-tuple-element.24), channel_id=1, source_target_pairs={{0,64},{1,33},{16,80},{17,49},{32,96},{33,1},{48,112},{49,17},{4,6... | collective-permute-start | bytes 245768 | tf_op jit(solution)/shard_map/ppermute | solution.py:29
  54.9 2.1 %collective-permute-done.10 = bf16[80,512]{1,0:T(8,128)(2,1)S(1)} collective-permute-done((bf16[80,512]{1,0:T(8,128)(2,1)S(1)}, bf16[80,512]{1,0:T(8,128)(2,1)S(1)}, u32[]{:S(2)}, u32[]{:S(2)}) %collective-permute-start.10) | collective-permute-done | bytes 81952 | tf_op jit(solution)/shard_map/ppermute | solution.py:29
  56.9 0.9 collective-permute-done.9
  57.8 0.7 constant_dynamic-update-slice_fusion.19
  58.5 1.3 %collective-permute-start.11 = (bf16[80,512]{1,0:T(8,128)(2,1)S(1)}, bf16[80,512]{1,0:T(8,128)(2,1)S(1)}, u32[]{:S(2)}, u32[]{:S(2)}) collective-permute-start(bf16[80,512]{1,0:T(8,128)(2,1)S(1)} %get-tuple-element.8), channel_id=1, source_target_pairs={{0,66},{1,49},{16,82},{17,1},{32,98},{33,17},{48,114},{49,33},{4,7... | collective-permute-start | bytes 245768 | tf_op jit(solution)/shard_map/ppermute | solution.py:29
  60.0 1.2 %collective-permute-start.12 = (bf16[80,512]{1,0:T(8,128)(2,1)S(1)}, bf16[80,512]{1,0:T(8,128)(2,1)S(1)}, u32[]{:S(2)}, u32[]{:S(2)}) collective-permute-start(bf16[80,512]{1,0:T(8,128)(2,1)S(1)} %get-tuple-element.8), channel_id=1, source_target_pairs={{0,64},{1,33},{16,80},{17,49},{32,96},{33,1},{48,112},{49,17},{4,6... | collective-permute-start | bytes 245768 | tf_op jit(solution)/shard_map/ppermute | solution.py:29
  62.4 2.4 %collective-permute-done.12 = bf16[80,512]{1,0:T(8,128)(2,1)S(1)} collective-permute-done((bf16[80,512]{1,0:T(8,128)(2,1)S(1)}, bf16[80,512]{1,0:T(8,128)(2,1)S(1)}, u32[]{:S(2)}, u32[]{:S(2)}) %collective-permute-start.12) | collective-permute-done | bytes 81952 | tf_op jit(solution)/shard_map/ppermute | solution.py:29
  68.7 1.9 %constant_dynamic-update-slice_fusion.27 = (bf16[2560,512]{1,0:T(8,128)(2,1)}, bf16[320,512]{1,0:T(8,128)(2,1)S(1)}) fusion(bf16[640,512]{1,0:T(8,128)(2,1)} %constant_dynamic-update-slice_fusion.12, s32[]{:T(128)S(6)} %select_n.192), kind=kLoop, calls=%fused_computation.101 | loop fusion | bytes 983044
  70.6 2.3 %collective-permute-start.14 = (bf16[320,512]{1,0:T(8,128)(2,1)S(1)}, bf16[320,512]{1,0:T(8,128)(2,1)}, u32[]{:S(2)}, u32[]{:S(2)}) collective-permute-start(bf16[320,512]{1,0:T(8,128)(2,1)S(1)} %get-tuple-element.6), channel_id=1, source_target_pairs={{0,48},{1,13},{16,0},{17,29},{32,16},{33,45},{48,32},{49,61},{4,52... | collective-permute-start | bytes 983048 | tf_op jit(solution)/shard_map/ppermute | solution.py:29
  73.6 6.9 %collective-permute-done.14 = bf16[320,512]{1,0:T(8,128)(2,1)} collective-permute-done((bf16[320,512]{1,0:T(8,128)(2,1)S(1)}, bf16[320,512]{1,0:T(8,128)(2,1)}, u32[]{:S(2)}, u32[]{:S(2)}) %collective-permute-start.14) | collective-permute-done | bytes 327712 | tf_op jit(solution)/shard_map/ppermute | solution.py:29
  80.4 1.7 %constant_dynamic-update-slice_fusion.26 = bf16[2560,512]{1,0:T(8,128)(2,1)} fusion(bf16[2560,512]{1,0:T(8,128)(2,1)} %get-tuple-element.5, bf16[320,512]{1,0:T(8,128)(2,1)} %collective-permute-done.14), kind=kLoop, calls=%fused_computation.100 | loop fusion | bytes 655360
  82.2 1.7 %constant_dynamic-update-slice_fusion.25 = bf16[2560,512]{1,0:T(8,128)(2,1)} fusion(bf16[2560,512]{1,0:T(8,128)(2,1)} %constant_dynamic-update-slice_fusion.26, bf16[320,512]{1,0:T(8,128)(2,1)} %collective-permute-done.15), kind=kLoop, calls=%fused_computation.99 | loop fusion | bytes 655360
  83.9 1.7 %constant_dynamic-update-slice_fusion.24 = bf16[2560,512]{1,0:T(8,128)(2,1)} fusion(bf16[2560,512]{1,0:T(8,128)(2,1)} %constant_dynamic-update-slice_fusion.25, bf16[320,512]{1,0:T(8,128)(2,1)} %collective-permute-done.16), kind=kLoop, calls=%fused_computation.98 | loop fusion | bytes 655360
  85.6 0.8 constant_dynamic-update-slice_fusion.23
  86.4 1.7 %constant_dynamic-update-slice_fusion.22 = bf16[2560,512]{1,0:T(8,128)(2,1)} fusion(bf16[2560,512]{1,0:T(8,128)(2,1)} %constant_dynamic-update-slice_fusion.23, bf16[320,512]{1,0:T(8,128)(2,1)} %collective-permute-done.14), kind=kLoop, calls=%fused_computation.96 | loop fusion | bytes 655360
  88.1 1.7 %constant_dynamic-update-slice_fusion.21 = bf16[2560,512]{1,0:T(8,128)(2,1)} fusion(bf16[2560,512]{1,0:T(8,128)(2,1)} %constant_dynamic-update-slice_fusion.22, bf16[320,512]{1,0:T(8,128)(2,1)} %collective-permute-done.15), kind=kLoop, calls=%fused_computation.95 | loop fusion | bytes 655360
  89.8 1.7 %constant_dynamic-update-slice_fusion.20 = bf16[2560,512]{1,0:T(8,128)(2,1)} fusion(bf16[2560,512]{1,0:T(8,128)(2,1)} %constant_dynamic-update-slice_fusion.21, bf16[320,512]{1,0:T(8,128)(2,1)} %collective-permute-done.16), kind=kLoop, calls=%fused_computation.94 | loop fusion | bytes 655360 | tf_op jit(solution)/shard_map/concatenate | solution.py:59
  91.6 2.5 %fusion.42 = (bf16[768,512]{1,0:T(8,128)(2,1)S(1)}, f32[768,512]{1,0:T(8,128)S(1)}) fusion(bf16[2560,512]{1,0:T(8,128)(2,1)} %constant_dynamic-update-slice_fusion.20, s32[]{:T(128)S(6)} %select_n.194, bf16[768,1792]{1,0:T(8,128)(2,1)S(1)} %copy-done.2), kind=kOutput, calls=%fused_computation.110 | convolution fusion | flops 1007026176 | bytes 5636100 | tf_op jit(solution)/shard_map/dot_general | solution.py:113
  94.1 0.7 collective-permute-start.17
  94.8 0.8 collective-permute-start.19
  95.6 0.8 collective-permute-start.18
  96.5 2.2 %collective-permute-done.17 = bf16[192,512]{1,0:T(8,128)(2,1)S(1)} collective-permute-done((bf16[192,512]{1,0:T(8,128)(2,1)S(1)}, bf16[192,512]{1,0:T(8,128)(2,1)S(1)}, u32[]{:S(2)}, u32[]{:S(2)}) %collective-permute-start.17) | collective-permute-done | bytes 196640 | tf_op jit(solution)/shard_map/ppermute | solution.py:29
  98.7 3.9 %collective-permute-done.19 = bf16[192,512]{1,0:T(8,128)(2,1)S(1)} collective-permute-done((bf16[192,512]{1,0:T(8,128)(2,1)S(1)}, bf16[192,512]{1,0:T(8,128)(2,1)S(1)}, u32[]{:S(2)}, u32[]{:S(2)}) %collective-permute-start.19) | collective-permute-done | bytes 196640 | tf_op jit(solution)/shard_map/ppermute | solution.py:29
  102.9 9.0 %collective-permute-start.20 = (f32[192]{0:T(256)S(1)}, f32[192]{0:T(256)S(1)}, u32[]{:S(2)}, u32[]{:S(2)}) collective-permute-start(f32[192]{0:T(256)S(1)} %fusion.36), channel_id=1, source_target_pairs={{0,1},{1,0},{2,3},{3,2},{4,5},{5,4},{6,7},{7,6},{8,9},{9,8},{10,11... | collective-permute-start | bytes 2312 | tf_op jit(solution)/shard_map/ppermute | solution.py:33
  111.8 0.8 collective-permute-done.20
  112.7 0.9 fusion.38
  (47 shorter events, 10.5 us)
Async XLA Ops:
  0.0 6.9 %copy-start = (bf16[192,2048]{1,0:T(8,128)(2,1)S(1)}, bf16[192,2048]{1,0:T(8,128)(2,1)}, u32[]{:S(2)}) copy-start(bf16[192,2048]{1,0:T(8,128)(2,1)} %param.3) | copy-start | bytes 2359300
  0.0 4.0 %collective-permute-start = (bf16[192,512]{1,0:T(8,128)(2,1)}, bf16[192,512]{1,0:T(8,128)(2,1)S(1)}, u32[]{:S(2)}, u32[]{:S(2)}) collective-permute-start(bf16[192,512]{1,0:T(8,128)(2,1)} %param.2), channel_id=1, source_target_pairs={{0,1},{1,0},{2,3},{3,2},{4,5},{5,4},{6,7},{7,6},{8,9},{9,8},{10,11... | collective-permute-start | bytes 589832 | tf_op jit(solution)/shard_map/ppermute | solution.py:33
  1.4 5.2 %collective-permute-start.1 = (bf16[192,2048]{1,0:T(8,128)(2,1)}, bf16[192,2048]{1,0:T(8,128)(2,1)S(1)}, u32[]{:S(2)}, u32[]{:S(2)}) collective-permute-start(bf16[192,2048]{1,0:T(8,128)(2,1)} %param.3), channel_id=1, source_target_pairs={{0,1},{1,0},{2,3},{3,2},{4,5},{5,4},{6,7},{7,6},{8,9},{9,8},{10,11... | collective-permute-start | bytes 2359304 | tf_op jit(solution)/shard_map/ppermute | solution.py:33
  10.1 18.2 %collective-permute-start.4 = (bf16[192,1792]{1,0:T(8,128)(2,1)}, bf16[192,1792]{1,0:T(8,128)(2,1)S(1)}, u32[]{:S(2)}, u32[]{:S(2)}) collective-permute-start(bf16[192,1792]{1,0:T(8,128)(2,1)} %get-tuple-element.27), channel_id=1, source_target_pairs={{0,12},{1,67},{16,28},{17,83},{32,44},{33,99},{48,60},{49,115},{4,... | collective-permute-start | bytes 2064392 | tf_op jit(solution)/shard_map/ppermute | solution.py:29
  12.7 15.6 %collective-permute-start.3 = (bf16[192,1792]{1,0:T(8,128)(2,1)}, bf16[192,1792]{1,0:T(8,128)(2,1)S(1)}, u32[]{:S(2)}, u32[]{:S(2)}) collective-permute-start(bf16[192,1792]{1,0:T(8,128)(2,1)} %get-tuple-element.28), channel_id=1, source_target_pairs={{0,8},{1,65},{16,24},{17,81},{32,40},{33,97},{48,56},{49,113},{4,1... | collective-permute-start | bytes 2064392 | tf_op jit(solution)/shard_map/ppermute | solution.py:29
  13.2 18.6 %collective-permute-start.2 = (bf16[192,1792]{1,0:T(8,128)(2,1)}, bf16[192,1792]{1,0:T(8,128)(2,1)S(1)}, u32[]{:S(2)}, u32[]{:S(2)}) collective-permute-start(bf16[192,1792]{1,0:T(8,128)(2,1)} %get-tuple-element.29), channel_id=1, source_target_pairs={{0,4},{1,3},{16,20},{17,19},{32,36},{33,35},{48,52},{49,51},{4,8},... | collective-permute-start | bytes 2064392 | tf_op jit(solution)/shard_map/ppermute | solution.py:29
  32.1 1.5 %copy-start.1 = (bf16[768,1792]{1,0:T(8,128)(2,1)}, bf16[768,1792]{1,0:T(8,128)(2,1)S(1)}, u32[]{:S(2)}) copy-start(bf16[768,1792]{1,0:T(8,128)(2,1)S(1)} %pad_maximum_fusion) | copy-start | bytes 8257540
  35.5 7.6 %collective-permute-start.5 = (bf16[320,512]{1,0:T(8,128)(2,1)}, bf16[320,512]{1,0:T(8,128)(2,1)S(1)}, u32[]{:S(2)}, u32[]{:S(2)}) collective-permute-start(bf16[320,512]{1,0:T(8,128)(2,1)} %get-tuple-element.9), channel_id=1, source_target_pairs={{0,16},{1,5},{16,32},{17,21},{32,48},{33,37},{48,0},{49,53},{4,20}... | collective-permute-start | bytes 983048 | tf_op jit(solution)/shard_map/ppermute | solution.py:29
  36.5 9.6 %collective-permute-start.6 = (bf16[320,512]{1,0:T(8,128)(2,1)}, bf16[320,512]{1,0:T(8,128)(2,1)S(1)}, u32[]{:S(2)}, u32[]{:S(2)}) collective-permute-start(bf16[320,512]{1,0:T(8,128)(2,1)} %get-tuple-element.10), channel_id=1, source_target_pairs={{0,48},{1,13},{16,0},{17,29},{32,16},{33,45},{48,32},{49,61},{4,52... | collective-permute-start | bytes 983048 | tf_op jit(solution)/shard_map/ppermute | solution.py:29
  38.2 9.2 %collective-permute-start.7 = (bf16[320,512]{1,0:T(8,128)(2,1)}, bf16[320,512]{1,0:T(8,128)(2,1)}, u32[]{:S(2)}, u32[]{:S(2)}) collective-permute-start(bf16[320,512]{1,0:T(8,128)(2,1)} %get-tuple-element.11), channel_id=1, source_target_pairs={{0,32},{1,9},{16,48},{17,25},{32,0},{33,41},{48,16},{49,57},{4,36}... | collective-permute-start | bytes 983048 | tf_op jit(solution)/shard_map/ppermute | solution.py:29
  43.2 2.9 %copy-start.3 = (bf16[320,512]{1,0:T(8,128)(2,1)}, bf16[320,512]{1,0:T(8,128)(2,1)S(1)}, u32[]{:S(2)}) copy-start(bf16[320,512]{1,0:T(8,128)(2,1)S(1)} %collective-permute-done.5) | copy-start | bytes 983044
  46.1 0.7 copy-start.4
  48.9 6.0 %collective-permute-start.8 = (bf16[80,512]{1,0:T(8,128)(2,1)S(1)}, bf16[80,512]{1,0:T(8,128)(2,1)S(1)}, u32[]{:S(2)}, u32[]{:S(2)}) collective-permute-start(bf16[80,512]{1,0:T(8,128)(2,1)S(1)} %get-tuple-element.23), channel_id=1, source_target_pairs={{0,2},{1,17},{16,18},{17,33},{32,34},{33,49},{48,50},{49,1},{4,6},... | collective-permute-start | bytes 245768 | tf_op jit(solution)/shard_map/ppermute | solution.py:29
  50.6 6.3 %collective-permute-start.10 = (bf16[80,512]{1,0:T(8,128)(2,1)S(1)}, bf16[80,512]{1,0:T(8,128)(2,1)S(1)}, u32[]{:S(2)}, u32[]{:S(2)}) collective-permute-start(bf16[80,512]{1,0:T(8,128)(2,1)S(1)} %get-tuple-element.24), channel_id=1, source_target_pairs={{0,64},{1,33},{16,80},{17,49},{32,96},{33,1},{48,112},{49,17},{4,6... | collective-permute-start | bytes 245768 | tf_op jit(solution)/shard_map/ppermute | solution.py:29
  54.2 3.6 %collective-permute-start.9 = (bf16[80,512]{1,0:T(8,128)(2,1)S(1)}, bf16[80,512]{1,0:T(8,128)(2,1)S(1)}, u32[]{:S(2)}, u32[]{:S(2)}) collective-permute-start(bf16[80,512]{1,0:T(8,128)(2,1)S(1)} %get-tuple-element.25), channel_id=1, source_target_pairs={{0,66},{1,49},{16,82},{17,1},{32,98},{33,17},{48,114},{49,33},{4,7... | collective-permute-start | bytes 245768 | tf_op jit(solution)/shard_map/ppermute | solution.py:29
  58.5 3.3 %collective-permute-start.11 = (bf16[80,512]{1,0:T(8,128)(2,1)S(1)}, bf16[80,512]{1,0:T(8,128)(2,1)S(1)}, u32[]{:S(2)}, u32[]{:S(2)}) collective-permute-start(bf16[80,512]{1,0:T(8,128)(2,1)S(1)} %get-tuple-element.8), channel_id=1, source_target_pairs={{0,66},{1,49},{16,82},{17,1},{32,98},{33,17},{48,114},{49,33},{4,7... | collective-permute-start | bytes 245768 | tf_op jit(solution)/shard_map/ppermute | solution.py:29
  59.8 5.7 %collective-permute-start.13 = (bf16[80,512]{1,0:T(8,128)(2,1)S(1)}, bf16[80,512]{1,0:T(8,128)(2,1)S(1)}, u32[]{:S(2)}, u32[]{:S(2)}) collective-permute-start(bf16[80,512]{1,0:T(8,128)(2,1)S(1)} %get-tuple-element.8), channel_id=1, source_target_pairs={{0,2},{1,17},{16,18},{17,33},{32,34},{33,49},{48,50},{49,1},{4,6},... | collective-permute-start | bytes 245768 | tf_op jit(solution)/shard_map/ppermute | solution.py:29
  60.0 4.9 %collective-permute-start.12 = (bf16[80,512]{1,0:T(8,128)(2,1)S(1)}, bf16[80,512]{1,0:T(8,128)(2,1)S(1)}, u32[]{:S(2)}, u32[]{:S(2)}) collective-permute-start(bf16[80,512]{1,0:T(8,128)(2,1)S(1)} %get-tuple-element.8), channel_id=1, source_target_pairs={{0,64},{1,33},{16,80},{17,49},{32,96},{33,1},{48,112},{49,17},{4,6... | collective-permute-start | bytes 245768 | tf_op jit(solution)/shard_map/ppermute | solution.py:29
  68.7 22.8 %copy-start.2 = (bf16[768,1792]{1,0:T(8,128)(2,1)S(1)}, bf16[768,1792]{1,0:T(8,128)(2,1)}, u32[]{:S(2)}) copy-start(bf16[768,1792]{1,0:T(8,128)(2,1)} %copy-done.1) | copy-start | bytes 8257540
  70.6 9.8 %collective-permute-start.14 = (bf16[320,512]{1,0:T(8,128)(2,1)S(1)}, bf16[320,512]{1,0:T(8,128)(2,1)}, u32[]{:S(2)}, u32[]{:S(2)}) collective-permute-start(bf16[320,512]{1,0:T(8,128)(2,1)S(1)} %get-tuple-element.6), channel_id=1, source_target_pairs={{0,48},{1,13},{16,0},{17,29},{32,16},{33,45},{48,32},{49,61},{4,52... | collective-permute-start | bytes 983048 | tf_op jit(solution)/shard_map/ppermute | solution.py:29
  72.9 9.3 %collective-permute-start.15 = (bf16[320,512]{1,0:T(8,128)(2,1)S(1)}, bf16[320,512]{1,0:T(8,128)(2,1)}, u32[]{:S(2)}, u32[]{:S(2)}) collective-permute-start(bf16[320,512]{1,0:T(8,128)(2,1)S(1)} %get-tuple-element.6), channel_id=1, source_target_pairs={{0,32},{1,9},{16,48},{17,25},{32,0},{33,41},{48,16},{49,57},{4,36}... | collective-permute-start | bytes 983048 | tf_op jit(solution)/shard_map/ppermute | solution.py:29
  73.1 10.8 %collective-permute-start.16 = (bf16[320,512]{1,0:T(8,128)(2,1)S(1)}, bf16[320,512]{1,0:T(8,128)(2,1)}, u32[]{:S(2)}, u32[]{:S(2)}) collective-permute-start(bf16[320,512]{1,0:T(8,128)(2,1)S(1)} %get-tuple-element.6), channel_id=1, source_target_pairs={{0,16},{1,5},{16,32},{17,21},{32,48},{33,37},{48,0},{49,53},{4,20}... | collective-permute-start | bytes 983048 | tf_op jit(solution)/shard_map/ppermute | solution.py:29
  94.1 4.6 %collective-permute-start.17 = (bf16[192,512]{1,0:T(8,128)(2,1)S(1)}, bf16[192,512]{1,0:T(8,128)(2,1)S(1)}, u32[]{:S(2)}, u32[]{:S(2)}) collective-permute-start(bf16[192,512]{1,0:T(8,128)(2,1)S(1)} %get-tuple-element.12), channel_id=1, source_target_pairs={{0,12},{1,67},{16,28},{17,83},{32,44},{33,99},{48,60},{49,115},{4,... | collective-permute-start | bytes 589832 | tf_op jit(solution)/shard_map/ppermute | solution.py:29
  94.8 7.8 %collective-permute-start.19 = (bf16[192,512]{1,0:T(8,128)(2,1)S(1)}, bf16[192,512]{1,0:T(8,128)(2,1)S(1)}, u32[]{:S(2)}, u32[]{:S(2)}) collective-permute-start(bf16[192,512]{1,0:T(8,128)(2,1)S(1)} %get-tuple-element.13), channel_id=1, source_target_pairs={{0,4},{1,3},{16,20},{17,19},{32,36},{33,35},{48,52},{49,51},{4,8},... | collective-permute-start | bytes 589832 | tf_op jit(solution)/shard_map/ppermute | solution.py:29
  95.6 7.0 %collective-permute-start.18 = (bf16[192,512]{1,0:T(8,128)(2,1)S(1)}, bf16[192,512]{1,0:T(8,128)(2,1)S(1)}, u32[]{:S(2)}, u32[]{:S(2)}) collective-permute-start(bf16[192,512]{1,0:T(8,128)(2,1)S(1)} %get-tuple-element.14), channel_id=1, source_target_pairs={{0,8},{1,65},{16,24},{17,81},{32,40},{33,97},{48,56},{49,113},{4,1... | collective-permute-start | bytes 589832 | tf_op jit(solution)/shard_map/ppermute | solution.py:29
  102.9 9.8 %collective-permute-start.20 = (f32[192]{0:T(256)S(1)}, f32[192]{0:T(256)S(1)}, u32[]{:S(2)}, u32[]{:S(2)}) collective-permute-start(f32[192]{0:T(256)S(1)} %fusion.36), channel_id=1, source_target_pairs={{0,1},{1,0},{2,3},{3,2},{4,5},{5,4},{6,7},{7,6},{8,9},{9,8},{10,11... | collective-permute-start | bytes 2312 | tf_op jit(solution)/shard_map/ppermute | solution.py:33

commit v2 on v1

v2 whole, which is shorter than its diff:
```python
import functools
import itertools

import jax
import jax.numpy as jnp
from jax import lax
from jax.experimental import pallas as pl
from jax.experimental.pallas import tpu as pltpu
from jax.sharding import PartitionSpec as P

AXES = ("loop", "rep", "sec")
X, Y, Z = 0, 1, 2
SIZE = 4
GATHER = (Y, X)
FIRST = (Z, Y)
SECOND = (X, Z)
STRIP = 16
PARAMS = pltpu.CompilerParams(vmem_limit_bytes=40 * 1024 * 1024)
SCALAR = pl.BlockSpec(memory_space=pltpu.SMEM)
WHOLE = pl.BlockSpec(memory_space=pltpu.VMEM)


def index_of(chip, core):
    x, y, z = chip
    return (((x // 2) * SIZE + z) * 8 + y * 2 + x % 2) * 2 + core


def shifted(array, axis_of_core, by):
    pairs = []
    for chip in itertools.product(range(SIZE), repeat=3):
        for core in range(2):
            target = list(chip)
            axis = axis_of_core[core]
            target[axis] = (target[axis] + by) % SIZE
            pairs.append((index_of(chip, core), index_of(target, core)))
    return lax.ppermute(array, AXES, pairs)


def other_core(array):
    return lax.ppermute(array, "sec", [(0, 1), (1, 0)])


def place_along(axis_of_core):
    loop, rep, core = (lax.axis_index(name) for name in AXES)
    place = ((loop // SIZE) * 2 + rep % 2, rep // 2, loop % SIZE)
    return jnp.where(core == 0, place[axis_of_core[0]], place[axis_of_core[1]])


def pack_kernel(places, s_own, s_far, t_own, t_far, pack0, pack1, pack2, pack3, inv_out):
    packs = (pack0, pack1, pack2, pack3)
    rows, half = s_own.shape
    wide = t_own.shape[1]
    ss, ts = half // SIZE, wide // SIZE
    feats = 2 * (ss + ts)

    def inverse(own, far, at):
        a, b = own[at, :].astype(jnp.float32), far[at, :].astype(jnp.float32)
        total = jnp.sum(a * a, axis=1, keepdims=True) + jnp.sum(b * b, axis=1, keepdims=True)
        return lax.rsqrt(total + 1e-06)

    @pl.loop(0, rows // STRIP)
    def _(strip):
        at = pl.ds(pl.multiple_of(strip * STRIP, STRIP), STRIP)
        inv_s, inv_t = inverse(s_own, s_far, at), inverse(t_own, t_far, at)
        inv_out[at, :] = inv_s
        norm = (s_own[at, :].astype(jnp.float32) * inv_s).astype(jnp.bfloat16)
        for by in range(SIZE):
            which = lax.rem(places[0] + by, SIZE)
            pack = packs[by]
            start = 0
            for ref, size, inv in (
                (s_own, ss, inv_s),
                (s_far, ss, inv_s),
                (t_own, ts, inv_t),
                (t_far, ts, inv_t),
            ):
                piece = ref[at, pl.ds(pl.multiple_of(which * size, size), size)]
                pack[at, pl.ds(start, size)] = (piece.astype(jnp.float32) * inv).astype(
                    jnp.bfloat16
                )
                start += size
            pack[at, pl.ds(feats, half)] = norm


def gram_kernel(
    share, places, pack0, pack1, pack2, pack3, own, send1, send2, send3, whole, product
):
    rows = pack0.shape[0]
    half = product.shape[0]
    feats = product.shape[1]
    ss = half // SIZE
    for k, pack in enumerate((pack0, pack1, pack2, pack3)):
        whole[pl.ds(k * rows, rows), :] = pack[...]
    product[...] = lax.dot_general(
        whole[:, pl.ds(feats, half)],
        whole[:, pl.ds(0, feats)],
        (((0,), (0,)), ((), ())),
        preferred_element_type=jnp.float32,
    )
    diagonal = pl.ds(pl.multiple_of(places[0] * ss, ss), ss)
    row = lax.broadcasted_iota(jnp.int32, (ss, ss), 0)
    col = lax.broadcasted_iota(jnp.int32, (ss, ss), 1)
    product[diagonal, pl.ds(0, ss)] -= jnp.where(row == col, share, 0.0)
    for by, out in enumerate((own, send1, send2, send3)):
        which = lax.rem(places[1] + by, SIZE)
        block = pl.ds(pl.multiple_of(which * ss, ss), ss)
        out[:, pl.ds(0, 2 * ss)] = product[block, pl.ds(0, 2 * ss)].astype(out.dtype)
        out[:, pl.ds(2 * ss, feats - 2 * ss)] = -product[
            block, pl.ds(2 * ss, feats - 2 * ss)
        ].astype(out.dtype)


def apply_kernel(
    places, pack0, pack1, pack2, pack3, piece0, piece1, piece2, piece3, own, send1, send2, send3, weights
):
    ss, feats = piece0.shape
    for by, piece in enumerate((piece0, piece1, piece2, piece3)):
        which = lax.rem(places[1] + SIZE - by, SIZE)
        weights[pl.ds(pl.multiple_of(which * ss, ss), ss), :] = piece[...]
    for pack, out in ((pack0, own), (pack1, send1), (pack2, send2), (pack3, send3)):
        out[...] = lax.dot_general(
            pack[:, pl.ds(0, feats)],
            weights[...],
            (((1,), (1,)), ((), ())),
            preferred_element_type=jnp.float32,
        ).astype(out.dtype)


def shapes(*described):
    return [jax.ShapeDtypeStruct(shape, dtype) for shape, dtype in described]


def body(student, teacher):
    rows, half = student.shape
    wide = teacher.shape[1]
    width = 2 * half
    groups = lax.axis_size("loop") * lax.axis_size("rep")
    passages = rows * groups
    coef = 32.0 * width / (passages**0.5)
    level = passages / width
    ss = half // SIZE
    feats = width // SIZE + 2 * wide // SIZE
    bf16, f32 = jnp.bfloat16, jnp.float32
    places = jnp.stack([place_along(GATHER), place_along(FIRST)]).astype(jnp.int32)

    t_far, s_far = other_core(teacher), other_core(student)
    *packs, inv_s = pl.pallas_call(
        pack_kernel,
        out_shape=shapes(*[((rows, feats + half), bf16)] * SIZE, ((rows, 1), f32)),
        in_specs=[SCALAR] + [WHOLE] * 4,
        out_specs=[WHOLE] * 5,
        compiler_params=PARAMS,
        name="pack",
    )(places, student, s_far, teacher, t_far)
    arrived = [packs[0]] + [shifted(packs[by], GATHER, by) for by in (1, 2, 3)]

    own, *sends = pl.pallas_call(
        functools.partial(gram_kernel, level * SIZE / groups),
        out_shape=shapes(((ss, feats), f32), *[((ss, feats), bf16)] * 3),
        in_specs=[SCALAR] + [WHOLE] * 4,
        out_specs=[WHOLE] * 4,
        scratch_shapes=[
            pltpu.VMEM((SIZE * rows, feats + half), bf16),
            pltpu.VMEM((half, feats), f32),
        ],
        compiler_params=PARAMS,
        name="gram",
    )(places, *arrived)
    total = own
    for by in (1, 2, 3):
        total = total + shifted(sends[by - 1], FIRST, by).astype(f32)
    shared = total.astype(bf16)
    for by in (1, 2, 3):
        total = total + shifted(shared, SECOND, by).astype(f32)
    piece = total.astype(bf16)
    pieces = [piece] + [shifted(piece, FIRST, by) for by in (1, 2, 3)]

    grad_n, *parts = pl.pallas_call(
        apply_kernel,
        out_shape=shapes(((rows, half), f32), *[((rows, half), bf16)] * 3),
        in_specs=[SCALAR] + [WHOLE] * 8,
        out_specs=[WHOLE] * 4,
        scratch_shapes=[pltpu.VMEM((half, feats), bf16)],
        compiler_params=PARAMS,
        name="apply",
    )(places, *arrived, *pieces)
    norm_f = packs[0][:, feats:].astype(f32)
    grad_n = grad_n + level * norm_f
    for by in (1, 2, 3):
        grad_n = grad_n + shifted(parts[by - 1], GATHER, -by).astype(f32)
    grad_n = coef * grad_n
    inner = jnp.sum(grad_n * norm_f, axis=1)
    inner = inner + other_core(inner)
    return (grad_n - inner[:, None] * norm_f) * inv_s


def solution(mesh):
    placed = (P(("loop", "rep"), "sec"), P(("loop", "rep"), "sec"))
    return jax.shard_map(
        body, mesh=mesh, in_specs=placed, out_specs=P(("loop", "rep"), "sec"), check_vma=False
    )
```

time: 114 us -> 91.5 us (0.80)
  local copies, waits for them, and re-layouts: 22.7 us -> 2.06 us
  other arithmetic: 9.77 us -> 1.82 us
  waiting for transfers between devices: 45.2 us -> 52.6 us
  Pallas kernels: 0 us -> 6.57 us
  starting transfers between devices: 32 us -> 28.2 us
  matrix products: 3.71 us -> 0 us
    unnamed x27 -> x4, local copies, waits for them, and re-layouts: 19.3 us -> 2.06 us
    pallas_call x0 -> x3, Pallas kernels: none -> 6.57 us  [the longest x1 2.46 us: body(): pl.pallas_call(apply_kernel, out_shape=shapes(((rows, half), f32), *[((ro...]
    ppermute x18 -> x15, waiting for transfers between devices: 44.4 us -> 49.5 us  [shifted(): return lax.ppermute(array, AXES, pairs)]
    dot_general x2 -> x0, matrix products: 3.71 us -> none  [the longest x1 2.48 us: body(): partial = jnp.dot(left, weights, preferred_element_type=jnp.float32)]
    concatenate x3 -> x0, local copies, waits for them, and re-layouts: 3.28 us -> none  [the longest x2 2.37 us: all_gathered(): around = jnp.concatenate(parts + parts, axis=0)]
    ppermute x3, starting transfers between devices: 10.4 us -> 7.58 us  [other_core(): return lax.ppermute(array, 'sec', [(0, 1), (1, 0)])]
    reduce_sum x4 -> x0, other arithmetic: 2.78 us -> none  [inverse(): total = jnp.sum(own * own, axis=1) + jnp.sum(far * far, axis=1)]
    convert_element_type x3 -> x2, other arithmetic: 3.02 us -> 0.47 us  [the longest x1 0.31 us: body(): piece = total.astype(bf16)]
  transfers between devices with their start and end apart: 21 -> 18, of which waited for: 14 -> 14; matrix products, arithmetic and copies ran while one was open for 9% -> 0% of each run, Pallas kernels for 0% -> 0%
where the time goes in v2:
time: 91.5 us; the launch traced here: 91.3 us
  waiting for transfers between devices  52.6 us (57%)
  starting transfers between devices  28.2 us (31%)
  Pallas kernels  6.57 us (7%)
  local copies, waits for them, and re-layouts  2.06 us (2%)
  other arithmetic  1.82 us (2%)
    ppermute x15, waiting for transfers between devices, shifted(): return lax.ppermute(array, AXES, pairs)  49.5 us
    ppermute x15, starting transfers between devices, shifted(): return lax.ppermute(array, AXES, pairs)  20.6 us
    ppermute x3, starting transfers between devices, other_core(): return lax.ppermute(array, 'sec', [(0, 1), (1, 0)])  7.58 us
    ppermute x3, waiting for transfers between devices, other_core(): return lax.ppermute(array, 'sec', [(0, 1), (1, 0)])  3.04 us
    pallas_call x1, Pallas kernels, body(): pl.pallas_call(apply_kernel, out_shape=shapes(((rows, half), f32), *[((ro...  2.46 us
    pallas_call x1, Pallas kernels, body(): pl.pallas_call(pack_kernel, out_shape=shapes(*[((rows, feats + half), bf1...  2.18 us
    unnamed x4, local copies, waits for them, and re-layouts  2.06 us
    pallas_call x1, Pallas kernels, body(): pl.pallas_call(functools.partial(gram_kernel, level * SIZE / groups), out...  1.92 us
  transfers between devices with their start and end apart: 18, of which 14 were waited for; matrix products, arithmetic and copies ran while one was open for 0% of the time, Pallas kernels for 0%

profile of v2, /device:TPU:1, one launch (start us, length us, event | category | flops | bytes accessed | tf_op | source)
XLA Modules:
  0.0 91.3 jit_solution(13036572526602718952)
XLA Ops:
  0.0 1.4 %collective-permute-start.1 = (bf16[192,2048]{1,0:T(8,128)(2,1)}, bf16[192,2048]{1,0:T(8,128)(2,1)S(1)}, u32[]{:S(2)}, u32[]{:S(2)}) collective-permute-start(bf16[192,2048]{1,0:T(8,128)(2,1)} %t_own.1), channel_id=1, source_target_pairs={{0,1},{1,0},{2,3},{3,2},{4,5},{5,4},{6,7},{7,6},{8,9},{9,8},{10,11... | collective-permute-start | bytes 2359304 | tf_op jit(solution)/shard_map/ppermute | solution.py:40
  1.4 0.0 collective-permute-start
  1.4 0.1 pad_add_fusion.places
  1.5 2.3 %collective-permute-done.s_far = bf16[192,512]{1,0:T(8,128)(2,1)S(1)} collective-permute-done((bf16[192,512]{1,0:T(8,128)(2,1)}, bf16[192,512]{1,0:T(8,128)(2,1)S(1)}, u32[]{:S(2)}, u32[]{:S(2)}) %collective-permute-start) | collective-permute-done | bytes 196640 | tf_op jit(solution)/shard_map/ppermute | solution.py:40
  3.8 0.0 collective-permute-done.1.t_far
  3.8 0.0 copy-start
  3.8 1.1 %copy-done = bf16[192,2048]{1,0:T(8,128)(2,1)S(1)} copy-done((bf16[192,2048]{1,0:T(8,128)(2,1)S(1)}, bf16[192,2048]{1,0:T(8,128)(2,1)}, u32[]{:S(2)}) %copy-start) | copy-done | bytes 786456
  5.0 0.9 %copy-done.1 = bf16[192,512]{1,0:T(8,128)(2,1)S(1)} copy-done((bf16[192,512]{1,0:T(8,128)(2,1)S(1)}, bf16[192,512]{1,0:T(8,128)(2,1)}, u32[]{:S(2)}) %copy-start.1) | copy-done | bytes 196632
  5.9 2.2 %pack.1 = (bf16[192,1792]{1,0:T(8,128)(2,1)S(1)}, bf16[192,1792]{1,0:T(8,128)(2,1)S(1)}, bf16[192,1792]{1,0:T(8,128)(2,1)S(1)}, bf16[192,1792]{1,0:T(8,128)(2,1)S(1)}, f32[192,1]{1,0:T(8,128)S(1)}) custom-call(s32[2]{0:T(128)S(1)} %pad_add_fusion.places, bf16[192,512]{1,0:T(8,128)(2,1)S(1)} %copy-done.1, bf16[192,512]{1,0:T(8,128)(2,1)S(1)} %collective-permute-done.s_far, ...), custom_call_target="tpu_custom_call" | custom-call | tf_op jit(solution)/shard_map/pack/pallas_call | solution.py:147
  8.1 1.4 %collective-permute-start.2 = (bf16[192,1792]{1,0:T(8,128)(2,1)S(1)}, bf16[192,1792]{1,0:T(8,128)(2,1)S(1)}, u32[]{:S(2)}, u32[]{:S(2)}) collective-permute-start(bf16[192,1792]{1,0:T(8,128)(2,1)S(1)} %get-tuple-element.19), channel_id=1, source_target_pairs={{0,4},{1,3},{16,20},{17,19},{32,36},{33,35},{48,52},{49,51},{4,8},... | collective-permute-start | bytes 2064392 | tf_op jit(solution)/shard_map/ppermute | solution.py:36
  9.4 2.5 %collective-permute-start.3 = (bf16[192,1792]{1,0:T(8,128)(2,1)S(1)}, bf16[192,1792]{1,0:T(8,128)(2,1)S(1)}, u32[]{:S(2)}, u32[]{:S(2)}) collective-permute-start(bf16[192,1792]{1,0:T(8,128)(2,1)S(1)} %get-tuple-element.20), channel_id=1, source_target_pairs={{0,8},{1,65},{16,24},{17,81},{32,40},{33,97},{48,56},{49,113},{4,1... | collective-permute-start | bytes 2064392 | tf_op jit(solution)/shard_map/ppermute | solution.py:36
  11.9 1.2 %collective-permute-start.4 = (bf16[192,1792]{1,0:T(8,128)(2,1)S(1)}, bf16[192,1792]{1,0:T(8,128)(2,1)S(1)}, u32[]{:S(2)}, u32[]{:S(2)}) collective-permute-start(bf16[192,1792]{1,0:T(8,128)(2,1)S(1)} %get-tuple-element.21), channel_id=1, source_target_pairs={{0,12},{1,67},{16,28},{17,83},{32,44},{33,99},{48,60},{49,115},{4,... | collective-permute-start | bytes 2064392 | tf_op jit(solution)/shard_map/ppermute | solution.py:36
  13.0 6.4 %collective-permute-done.2.pack1 = bf16[192,1792]{1,0:T(8,128)(2,1)S(1)} collective-permute-done((bf16[192,1792]{1,0:T(8,128)(2,1)S(1)}, bf16[192,1792]{1,0:T(8,128)(2,1)S(1)}, u32[]{:S(2)}, u32[]{:S(2)}) %collective-permute-start.2) | collective-permute-done | bytes 688160 | tf_op jit(solution)/shard_map/ppermute | solution.py:36
  19.4 8.4 %collective-permute-done.3.pack2 = bf16[192,1792]{1,0:T(8,128)(2,1)S(1)} collective-permute-done((bf16[192,1792]{1,0:T(8,128)(2,1)S(1)}, bf16[192,1792]{1,0:T(8,128)(2,1)S(1)}, u32[]{:S(2)}, u32[]{:S(2)}) %collective-permute-start.3) | collective-permute-done | bytes 688160 | tf_op jit(solution)/shard_map/ppermute | solution.py:36
  27.9 0.0 collective-permute-done.4.pack3
  27.9 1.9 %gram.1 = (f32[128,1280]{1,0:T(8,128)S(1)}, bf16[128,1280]{1,0:T(8,128)(2,1)S(1)}, bf16[128,1280]{1,0:T(8,128)(2,1)S(1)}, bf16[128,1280]{1,0:T(8,128)(2,1)S(1)}) custom-call(s32[2]{0:T(128)S(1)} %pad_add_fusion.places, bf16[192,1792]{1,0:T(8,128)(2,1)S(1)} %get-tuple-element.18.pack0, bf16[192,1792]{1,0:T(8,128)(2,1)S(1)} %collective-permute-done.2.pack1, ...), custom_call_target="tpu_custom_call" | custom-call | tf_op jit(solution)/shard_map/gram/pallas_call | solution.py:157
  29.8 1.1 %collective-permute-start.5 = (bf16[128,1280]{1,0:T(8,128)(2,1)S(1)}, bf16[128,1280]{1,0:T(8,128)(2,1)S(1)}, u32[]{:S(2)}, u32[]{:S(2)}) collective-permute-start(bf16[128,1280]{1,0:T(8,128)(2,1)S(1)} %get-tuple-element.23), channel_id=1, source_target_pairs={{0,16},{1,5},{16,32},{17,21},{32,48},{33,37},{48,0},{49,53},{4,20}... | collective-permute-start | bytes 983048 | tf_op jit(solution)/shard_map/ppermute | solution.py:36
  30.9 2.6 %collective-permute-start.6 = (bf16[128,1280]{1,0:T(8,128)(2,1)S(1)}, bf16[128,1280]{1,0:T(8,128)(2,1)S(1)}, u32[]{:S(2)}, u32[]{:S(2)}) collective-permute-start(bf16[128,1280]{1,0:T(8,128)(2,1)S(1)} %get-tuple-element.24), channel_id=1, source_target_pairs={{0,32},{1,9},{16,48},{17,25},{32,0},{33,41},{48,16},{49,57},{4,36}... | collective-permute-start | bytes 983048 | tf_op jit(solution)/shard_map/ppermute | solution.py:36
  33.5 1.1 %collective-permute-start.7 = (bf16[128,1280]{1,0:T(8,128)(2,1)S(1)}, bf16[128,1280]{1,0:T(8,128)(2,1)S(1)}, u32[]{:S(2)}, u32[]{:S(2)}) collective-permute-start(bf16[128,1280]{1,0:T(8,128)(2,1)S(1)} %get-tuple-element.25), channel_id=1, source_target_pairs={{0,48},{1,13},{16,0},{17,29},{32,16},{33,45},{48,32},{49,61},{4,52... | collective-permute-start | bytes 983048 | tf_op jit(solution)/shard_map/ppermute | solution.py:36
  34.6 2.7 %collective-permute-done.5 = bf16[128,1280]{1,0:T(8,128)(2,1)S(1)} collective-permute-done((bf16[128,1280]{1,0:T(8,128)(2,1)S(1)}, bf16[128,1280]{1,0:T(8,128)(2,1)S(1)}, u32[]{:S(2)}, u32[]{:S(2)}) %collective-permute-start.5) | collective-permute-done | bytes 327712 | tf_op jit(solution)/shard_map/ppermute | solution.py:36
  37.3 4.5 %collective-permute-done.6 = bf16[128,1280]{1,0:T(8,128)(2,1)S(1)} collective-permute-done((bf16[128,1280]{1,0:T(8,128)(2,1)S(1)}, bf16[128,1280]{1,0:T(8,128)(2,1)S(1)}, u32[]{:S(2)}, u32[]{:S(2)}) %collective-permute-start.6) | collective-permute-done | bytes 327712 | tf_op jit(solution)/shard_map/ppermute | solution.py:36
  41.8 0.0 collective-permute-done.7
  41.8 0.2 fusion.8
  41.9 3.5 %collective-permute-start.10 = (bf16[128,1280]{1,0:T(8,128)(2,1)S(1)}, bf16[128,1280]{1,0:T(8,128)(2,1)S(1)}, u32[]{:S(2)}, u32[]{:S(2)}) collective-permute-start(bf16[128,1280]{1,0:T(8,128)(2,1)S(1)} %fusion.8), channel_id=1, source_target_pairs={{0,66},{1,49},{16,82},{17,1},{32,98},{33,17},{48,114},{49,33},{4,7... | collective-permute-start | bytes 983048 | tf_op jit(solution)/shard_map/ppermute | solution.py:36
  45.5 0.0 collective-permute-start.9
  45.5 0.7 collective-permute-start.8
  46.2 6.8 %collective-permute-done.10 = bf16[128,1280]{1,0:T(8,128)(2,1)S(1)} collective-permute-done((bf16[128,1280]{1,0:T(8,128)(2,1)S(1)}, bf16[128,1280]{1,0:T(8,128)(2,1)S(1)}, u32[]{:S(2)}, u32[]{:S(2)}) %collective-permute-start.10) | collective-permute-done | bytes 327712 | tf_op jit(solution)/shard_map/ppermute | solution.py:36
  53.0 0.2 collective-permute-done.9
  53.2 3.2 %collective-permute-done.8 = bf16[128,1280]{1,0:T(8,128)(2,1)S(1)} collective-permute-done((bf16[128,1280]{1,0:T(8,128)(2,1)S(1)}, bf16[128,1280]{1,0:T(8,128)(2,1)S(1)}, u32[]{:S(2)}, u32[]{:S(2)}) %collective-permute-start.8) | collective-permute-done | bytes 327712 | tf_op jit(solution)/shard_map/ppermute | solution.py:36
  56.4 0.3 add_convert_fusion.piece0
  56.7 2.4 %collective-permute-start.13 = (bf16[128,1280]{1,0:T(8,128)(2,1)S(1)}, bf16[128,1280]{1,0:T(8,128)(2,1)S(1)}, u32[]{:S(2)}, u32[]{:S(2)}) collective-permute-start(bf16[128,1280]{1,0:T(8,128)(2,1)S(1)} %add_convert_fusion.piece0), channel_id=1, source_target_pairs={{0,48},{1,13},{16,0},{17,29},{32,16},{33,45},{48,32},{49,61},{4,52... | collective-permute-start | bytes 983048 | tf_op jit(solution)/shard_map/ppermute | solution.py:36
  59.1 0.9 collective-permute-start.12
  60.0 0.3 collective-permute-start.11
  60.2 6.4 %collective-permute-done.13.piece3 = bf16[128,1280]{1,0:T(8,128)(2,1)S(1)} collective-permute-done((bf16[128,1280]{1,0:T(8,128)(2,1)S(1)}, bf16[128,1280]{1,0:T(8,128)(2,1)S(1)}, u32[]{:S(2)}, u32[]{:S(2)}) %collective-permute-start.13) | collective-permute-done | bytes 327712 | tf_op jit(solution)/shard_map/ppermute | solution.py:36
  66.6 0.0 collective-permute-done.12.piece2
  66.6 3.7 %collective-permute-done.11.piece1 = bf16[128,1280]{1,0:T(8,128)(2,1)S(1)} collective-permute-done((bf16[128,1280]{1,0:T(8,128)(2,1)S(1)}, bf16[128,1280]{1,0:T(8,128)(2,1)S(1)}, u32[]{:S(2)}, u32[]{:S(2)}) %collective-permute-start.11) | collective-permute-done | bytes 327712 | tf_op jit(solution)/shard_map/ppermute | solution.py:36
  70.3 2.5 %apply.1 = (f32[192,512]{1,0:T(8,128)S(1)}, bf16[192,512]{1,0:T(8,128)(2,1)S(1)}, bf16[192,512]{1,0:T(8,128)(2,1)S(1)}, bf16[192,512]{1,0:T(8,128)(2,1)S(1)}) custom-call(s32[2]{0:T(128)S(1)} %pad_add_fusion.places, bf16[192,1792]{1,0:T(8,128)(2,1)S(1)} %get-tuple-element.18.pack0, bf16[192,1792]{1,0:T(8,128)(2,1)S(1)} %collective-permute-done.2.pack1, ...), custom_call_target="tpu_custom_call" | custom-call | tf_op jit(solution)/shard_map/apply/pallas_call | solution.py:178
  72.8 2.2 %collective-permute-start.14 = (bf16[192,512]{1,0:T(8,128)(2,1)S(1)}, bf16[192,512]{1,0:T(8,128)(2,1)S(1)}, u32[]{:S(2)}, u32[]{:S(2)}) collective-permute-start(bf16[192,512]{1,0:T(8,128)(2,1)S(1)} %get-tuple-element.27), channel_id=1, source_target_pairs={{0,12},{1,67},{16,28},{17,83},{32,44},{33,99},{48,60},{49,115},{4,... | collective-permute-start | bytes 589832 | tf_op jit(solution)/shard_map/ppermute | solution.py:36
  75.0 0.7 collective-permute-start.15
  75.7 0.3 collective-permute-start.16
  76.0 3.8 %collective-permute-done.14 = bf16[192,512]{1,0:T(8,128)(2,1)S(1)} collective-permute-done((bf16[192,512]{1,0:T(8,128)(2,1)S(1)}, bf16[192,512]{1,0:T(8,128)(2,1)S(1)}, u32[]{:S(2)}, u32[]{:S(2)}) %collective-permute-start.14) | collective-permute-done | bytes 196640 | tf_op jit(solution)/shard_map/ppermute | solution.py:36
  79.7 1.4 %collective-permute-done.15 = bf16[192,512]{1,0:T(8,128)(2,1)S(1)} collective-permute-done((bf16[192,512]{1,0:T(8,128)(2,1)S(1)}, bf16[192,512]{1,0:T(8,128)(2,1)S(1)}, u32[]{:S(2)}, u32[]{:S(2)}) %collective-permute-start.15) | collective-permute-done | bytes 196640 | tf_op jit(solution)/shard_map/ppermute | solution.py:36
  81.2 2.0 %collective-permute-done.16 = bf16[192,512]{1,0:T(8,128)(2,1)S(1)} collective-permute-done((bf16[192,512]{1,0:T(8,128)(2,1)S(1)}, bf16[192,512]{1,0:T(8,128)(2,1)S(1)}, u32[]{:S(2)}, u32[]{:S(2)}) %collective-permute-start.16) | collective-permute-done | bytes 196640 | tf_op jit(solution)/shard_map/ppermute | solution.py:36
  83.2 0.2 fusion.5
  83.4 6.2 %collective-permute-start.17 = (f32[192]{0:T(256)S(1)}, f32[192]{0:T(256)S(1)}, u32[]{:S(2)}, u32[]{:S(2)}) collective-permute-start(f32[192]{0:T(256)S(1)} %fusion.5), channel_id=1, source_target_pairs={{0,1},{1,0},{2,3},{3,2},{4,5},{5,4},{6,7},{7,6},{8,9},{9,8},{10,11... | collective-permute-start | bytes 2312 | tf_op jit(solution)/shard_map/ppermute | solution.py:40
  89.6 0.1 reduce
  89.7 0.7 collective-permute-done.17
  90.4 0.9 %fusion.7 = f32[192,512]{1,0:T(8,128)} fusion(f32[192]{0:T(256)S(1)} %reduce, f32[192]{0:T(256)S(1)} %add.58, bf16[192,1792]{1,0:T(8,128)(2,1)S(1)} %get-tuple-element.18.pack0, bf16[192,512]{1,0:T(8,128)(2,1)S(1)} %collective-permute-done.16, bf16[192,512]{1,0:T(8,128)(2,1)S(1)} %collective-permute-done.15, ...), kind=kLoop, calls=%fused_computation.12 | loop fusion | flops 1277952 | bytes 1574400 | tf_op jit(solution)/shard_map/mul | solution.py:194
  (2 shorter events, 0.0 us)
Async XLA Ops:
  0.0 3.8 %collective-permute-start.1 = (bf16[192,2048]{1,0:T(8,128)(2,1)}, bf16[192,2048]{1,0:T(8,128)(2,1)S(1)}, u32[]{:S(2)}, u32[]{:S(2)}) collective-permute-start(bf16[192,2048]{1,0:T(8,128)(2,1)} %t_own.1), channel_id=1, source_target_pairs={{0,1},{1,0},{2,3},{3,2},{4,5},{5,4},{6,7},{7,6},{8,9},{9,8},{10,11... | collective-permute-start | bytes 2359304 | tf_op jit(solution)/shard_map/ppermute | solution.py:40
  1.4 2.4 %collective-permute-start = (bf16[192,512]{1,0:T(8,128)(2,1)}, bf16[192,512]{1,0:T(8,128)(2,1)S(1)}, u32[]{:S(2)}, u32[]{:S(2)}) collective-permute-start(bf16[192,512]{1,0:T(8,128)(2,1)} %s_own.1), channel_id=1, source_target_pairs={{0,1},{1,0},{2,3},{3,2},{4,5},{5,4},{6,7},{7,6},{8,9},{9,8},{10,11... | collective-permute-start | bytes 589832 | tf_op jit(solution)/shard_map/ppermute | solution.py:40
  3.8 1.1 %copy-start = (bf16[192,2048]{1,0:T(8,128)(2,1)S(1)}, bf16[192,2048]{1,0:T(8,128)(2,1)}, u32[]{:S(2)}) copy-start(bf16[192,2048]{1,0:T(8,128)(2,1)} %t_own.1) | copy-start | bytes 2359300
  5.0 0.9 %copy-start.1 = (bf16[192,512]{1,0:T(8,128)(2,1)S(1)}, bf16[192,512]{1,0:T(8,128)(2,1)}, u32[]{:S(2)}) copy-start(bf16[192,512]{1,0:T(8,128)(2,1)} %s_own.1) | copy-start | bytes 589828
  8.1 11.4 %collective-permute-start.2 = (bf16[192,1792]{1,0:T(8,128)(2,1)S(1)}, bf16[192,1792]{1,0:T(8,128)(2,1)S(1)}, u32[]{:S(2)}, u32[]{:S(2)}) collective-permute-start(bf16[192,1792]{1,0:T(8,128)(2,1)S(1)} %get-tuple-element.19), channel_id=1, source_target_pairs={{0,4},{1,3},{16,20},{17,19},{32,36},{33,35},{48,52},{49,51},{4,8},... | collective-permute-start | bytes 2064392 | tf_op jit(solution)/shard_map/ppermute | solution.py:36
  9.4 18.4 %collective-permute-start.3 = (bf16[192,1792]{1,0:T(8,128)(2,1)S(1)}, bf16[192,1792]{1,0:T(8,128)(2,1)S(1)}, u32[]{:S(2)}, u32[]{:S(2)}) collective-permute-start(bf16[192,1792]{1,0:T(8,128)(2,1)S(1)} %get-tuple-element.20), channel_id=1, source_target_pairs={{0,8},{1,65},{16,24},{17,81},{32,40},{33,97},{48,56},{49,113},{4,1... | collective-permute-start | bytes 2064392 | tf_op jit(solution)/shard_map/ppermute | solution.py:36
  11.9 16.0 %collective-permute-start.4 = (bf16[192,1792]{1,0:T(8,128)(2,1)S(1)}, bf16[192,1792]{1,0:T(8,128)(2,1)S(1)}, u32[]{:S(2)}, u32[]{:S(2)}) collective-permute-start(bf16[192,1792]{1,0:T(8,128)(2,1)S(1)} %get-tuple-element.21), channel_id=1, source_target_pairs={{0,12},{1,67},{16,28},{17,83},{32,44},{33,99},{48,60},{49,115},{4,... | collective-permute-start | bytes 2064392 | tf_op jit(solution)/shard_map/ppermute | solution.py:36
  29.8 7.5 %collective-permute-start.5 = (bf16[128,1280]{1,0:T(8,128)(2,1)S(1)}, bf16[128,1280]{1,0:T(8,128)(2,1)S(1)}, u32[]{:S(2)}, u32[]{:S(2)}) collective-permute-start(bf16[128,1280]{1,0:T(8,128)(2,1)S(1)} %get-tuple-element.23), channel_id=1, source_target_pairs={{0,16},{1,5},{16,32},{17,21},{32,48},{33,37},{48,0},{49,53},{4,20}... | collective-permute-start | bytes 983048 | tf_op jit(solution)/shard_map/ppermute | solution.py:36
  30.9 10.9 %collective-permute-start.6 = (bf16[128,1280]{1,0:T(8,128)(2,1)S(1)}, bf16[128,1280]{1,0:T(8,128)(2,1)S(1)}, u32[]{:S(2)}, u32[]{:S(2)}) collective-permute-start(bf16[128,1280]{1,0:T(8,128)(2,1)S(1)} %get-tuple-element.24), channel_id=1, source_target_pairs={{0,32},{1,9},{16,48},{17,25},{32,0},{33,41},{48,16},{49,57},{4,36}... | collective-permute-start | bytes 983048 | tf_op jit(solution)/shard_map/ppermute | solution.py:36
  33.5 8.3 %collective-permute-start.7 = (bf16[128,1280]{1,0:T(8,128)(2,1)S(1)}, bf16[128,1280]{1,0:T(8,128)(2,1)S(1)}, u32[]{:S(2)}, u32[]{:S(2)}) collective-permute-start(bf16[128,1280]{1,0:T(8,128)(2,1)S(1)} %get-tuple-element.25), channel_id=1, source_target_pairs={{0,48},{1,13},{16,0},{17,29},{32,16},{33,45},{48,32},{49,61},{4,52... | collective-permute-start | bytes 983048 | tf_op jit(solution)/shard_map/ppermute | solution.py:36
  41.9 11.1 %collective-permute-start.10 = (bf16[128,1280]{1,0:T(8,128)(2,1)S(1)}, bf16[128,1280]{1,0:T(8,128)(2,1)S(1)}, u32[]{:S(2)}, u32[]{:S(2)}) collective-permute-start(bf16[128,1280]{1,0:T(8,128)(2,1)S(1)} %fusion.8), channel_id=1, source_target_pairs={{0,66},{1,49},{16,82},{17,1},{32,98},{33,17},{48,114},{49,33},{4,7... | collective-permute-start | bytes 983048 | tf_op jit(solution)/shard_map/ppermute | solution.py:36
  45.5 7.8 %collective-permute-start.9 = (bf16[128,1280]{1,0:T(8,128)(2,1)S(1)}, bf16[128,1280]{1,0:T(8,128)(2,1)S(1)}, u32[]{:S(2)}, u32[]{:S(2)}) collective-permute-start(bf16[128,1280]{1,0:T(8,128)(2,1)S(1)} %fusion.8), channel_id=1, source_target_pairs={{0,64},{1,33},{16,80},{17,49},{32,96},{33,1},{48,112},{49,17},{4,6... | collective-permute-start | bytes 983048 | tf_op jit(solution)/shard_map/ppermute | solution.py:36
  45.5 10.9 %collective-permute-start.8 = (bf16[128,1280]{1,0:T(8,128)(2,1)S(1)}, bf16[128,1280]{1,0:T(8,128)(2,1)S(1)}, u32[]{:S(2)}, u32[]{:S(2)}) collective-permute-start(bf16[128,1280]{1,0:T(8,128)(2,1)S(1)} %fusion.8), channel_id=1, source_target_pairs={{0,2},{1,17},{16,18},{17,33},{32,34},{33,49},{48,50},{49,1},{4,6},... | collective-permute-start | bytes 983048 | tf_op jit(solution)/shard_map/ppermute | solution.py:36
  56.7 9.9 %collective-permute-start.13 = (bf16[128,1280]{1,0:T(8,128)(2,1)S(1)}, bf16[128,1280]{1,0:T(8,128)(2,1)S(1)}, u32[]{:S(2)}, u32[]{:S(2)}) collective-permute-start(bf16[128,1280]{1,0:T(8,128)(2,1)S(1)} %add_convert_fusion.piece0), channel_id=1, source_target_pairs={{0,48},{1,13},{16,0},{17,29},{32,16},{33,45},{48,32},{49,61},{4,52... | collective-permute-start | bytes 983048 | tf_op jit(solution)/shard_map/ppermute | solution.py:36
  59.1 7.5 %collective-permute-start.12 = (bf16[128,1280]{1,0:T(8,128)(2,1)S(1)}, bf16[128,1280]{1,0:T(8,128)(2,1)S(1)}, u32[]{:S(2)}, u32[]{:S(2)}) collective-permute-start(bf16[128,1280]{1,0:T(8,128)(2,1)S(1)} %add_convert_fusion.piece0), channel_id=1, source_target_pairs={{0,32},{1,9},{16,48},{17,25},{32,0},{33,41},{48,16},{49,57},{4,36}... | collective-permute-start | bytes 983048 | tf_op jit(solution)/shard_map/ppermute | solution.py:36
  60.0 10.4 %collective-permute-start.11 = (bf16[128,1280]{1,0:T(8,128)(2,1)S(1)}, bf16[128,1280]{1,0:T(8,128)(2,1)S(1)}, u32[]{:S(2)}, u32[]{:S(2)}) collective-permute-start(bf16[128,1280]{1,0:T(8,128)(2,1)S(1)} %add_convert_fusion.piece0), channel_id=1, source_target_pairs={{0,16},{1,5},{16,32},{17,21},{32,48},{33,37},{48,0},{49,53},{4,20}... | collective-permute-start | bytes 983048 | tf_op jit(solution)/shard_map/ppermute | solution.py:36
  72.8 6.9 %collective-permute-start.14 = (bf16[192,512]{1,0:T(8,128)(2,1)S(1)}, bf16[192,512]{1,0:T(8,128)(2,1)S(1)}, u32[]{:S(2)}, u32[]{:S(2)}) collective-permute-start(bf16[192,512]{1,0:T(8,128)(2,1)S(1)} %get-tuple-element.27), channel_id=1, source_target_pairs={{0,12},{1,67},{16,28},{17,83},{32,44},{33,99},{48,60},{49,115},{4,... | collective-permute-start | bytes 589832 | tf_op jit(solution)/shard_map/ppermute | solution.py:36
  75.0 6.1 %collective-permute-start.15 = (bf16[192,512]{1,0:T(8,128)(2,1)S(1)}, bf16[192,512]{1,0:T(8,128)(2,1)S(1)}, u32[]{:S(2)}, u32[]{:S(2)}) collective-permute-start(bf16[192,512]{1,0:T(8,128)(2,1)S(1)} %get-tuple-element.28), channel_id=1, source_target_pairs={{0,8},{1,65},{16,24},{17,81},{32,40},{33,97},{48,56},{49,113},{4,1... | collective-permute-start | bytes 589832 | tf_op jit(solution)/shard_map/ppermute | solution.py:36
  75.7 7.4 %collective-permute-start.16 = (bf16[192,512]{1,0:T(8,128)(2,1)S(1)}, bf16[192,512]{1,0:T(8,128)(2,1)S(1)}, u32[]{:S(2)}, u32[]{:S(2)}) collective-permute-start(bf16[192,512]{1,0:T(8,128)(2,1)S(1)} %get-tuple-element.29), channel_id=1, source_target_pairs={{0,4},{1,3},{16,20},{17,19},{32,36},{33,35},{48,52},{49,51},{4,8},... | collective-permute-start | bytes 589832 | tf_op jit(solution)/shard_map/ppermute | solution.py:36
  83.4 7.0 %collective-permute-start.17 = (f32[192]{0:T(256)S(1)}, f32[192]{0:T(256)S(1)}, u32[]{:S(2)}, u32[]{:S(2)}) collective-permute-start(f32[192]{0:T(256)S(1)} %fusion.5), channel_id=1, source_target_pairs={{0,1},{1,0},{2,3},{3,2},{4,5},{5,4},{6,7},{7,6},{8,9},{9,8},{10,11... | collective-permute-start | bytes 2312 | tf_op jit(solution)/shard_map/ppermute | solution.py:40

commit v3 on v1

v3 whole, which is shorter than its diff:
```python
import functools
import itertools

import jax
import jax.numpy as jnp
from jax import lax
from jax.experimental import pallas as pl
from jax.experimental.pallas import tpu as pltpu
from jax.sharding import PartitionSpec as P

AXES = ("loop", "rep", "sec")
X, Y, Z = 0, 1, 2
SIZE = 4
GATHER = (Y, X)
FIRST = (Z, Y)
SECOND = (X, Z)
STRIP = 32
PARAMS = pltpu.CompilerParams(vmem_limit_bytes=40 * 1024 * 1024)
SCALAR = pl.BlockSpec(memory_space=pltpu.SMEM)
WHOLE = pl.BlockSpec(memory_space=pltpu.VMEM)
BF16, F32 = jnp.bfloat16, jnp.float32


def index_of(chip, core):
    x, y, z = chip
    return (((x // 2) * SIZE + z) * 8 + y * 2 + x % 2) * 2 + core


def shifted(array, axis_of_core, by):
    pairs = []
    for chip in itertools.product(range(SIZE), repeat=3):
        for core in range(2):
            target = list(chip)
            axis = axis_of_core[core]
            target[axis] = (target[axis] + by) % SIZE
            pairs.append((index_of(chip, core), index_of(target, core)))
    return lax.ppermute(array, AXES, pairs)


def other_core(array):
    return lax.ppermute(array, "sec", [(0, 1), (1, 0)])


def place_along(axis_of_core):
    loop, rep, core = (lax.axis_index(name) for name in AXES)
    place = ((loop // SIZE) * 2 + rep % 2, rep // 2, loop % SIZE)
    return jnp.where(core == 0, place[axis_of_core[0]], place[axis_of_core[1]])


def scaled(piece, inv):
    return (piece.astype(F32) * inv).astype(BF16)


def part(places, by, size):
    return pl.ds(pl.multiple_of(lax.rem(places[0] + by, SIZE) * size, size), size)


def pack_own_kernel(places, s_own, s_far, t_own, t_far, *outs):
    half, wide = s_own.shape[1], t_own.shape[1]
    ts = wide // SIZE

    def inverse(own, far):
        a, b = own[...].astype(F32), far[...].astype(F32)
        total = jnp.sum(a * a, axis=1, keepdims=True) + jnp.sum(b * b, axis=1, keepdims=True)
        return lax.rsqrt(total + 1e-06)

    inv_s, inv_t = inverse(s_own, s_far), inverse(t_own, t_far)
    outs[SIZE][...] = inv_s
    outs[SIZE + 1][...] = inv_t
    norm = scaled(s_own[...], inv_s)
    for by in range(SIZE):
        outs[by][:, pl.ds(0, half)] = norm
        outs[by][:, pl.ds(half, ts)] = scaled(t_own[:, part(places, by, ts)], inv_t)


def pack_far_kernel(places, s_far, t_far, inv_s, inv_t, *outs):
    ss, ts = s_far.shape[1] // SIZE, t_far.shape[1] // SIZE
    for by in range(SIZE):
        outs[by][:, pl.ds(0, ss)] = scaled(s_far[:, part(places, by, ss)], inv_s[...])
        outs[by][:, pl.ds(ss, ts)] = scaled(t_far[:, part(places, by, ts)], inv_t[...])


def native_features(places, pack, half):
    ss = half // SIZE
    return pack[:, part(places, 0, ss)], pack[:, pl.ds(half, pack.shape[1] - half)]


def gram_kernel(share, native, places, *refs):
    count = SIZE if native else 2 * SIZE
    norms, packs = refs[:SIZE], refs[count - SIZE : count]
    outs, (left, right, product) = refs[count : count + SIZE], refs[count + SIZE :]
    half, feats = product.shape
    rows, ss = norms[0].shape[0], half // SIZE
    for k in range(SIZE):
        at = pl.ds(k * rows, rows)
        left[at, :] = norms[k][:, pl.ds(0, half)]
        if native:
            right[at, pl.ds(0, ss)], right[at, pl.ds(ss, feats - ss)] = native_features(
                places, packs[k], half
            )
        else:
            right[at, :] = packs[k][...]
    product[...] = lax.dot_general(
        left[...], right[...], (((0,), (0,)), ((), ())), preferred_element_type=F32
    )
    if native:
        row = lax.broadcasted_iota(jnp.int32, (ss, ss), 0)
        col = lax.broadcasted_iota(jnp.int32, (ss, ss), 1)
        product[part(places, 0, ss), pl.ds(0, ss)] -= jnp.where(row == col, share, 0.0)
    for by, out in enumerate(outs):
        which = lax.rem(places[1] + by, SIZE)
        block = pl.ds(pl.multiple_of(which * ss, ss), ss)
        rest = pl.ds(ss, feats - ss)
        out[:, pl.ds(0, ss)] = product[block, pl.ds(0, ss)].astype(out.dtype)
        out[:, rest] = -product[block, rest].astype(out.dtype)


def gather_weights(places, pieces, weights):
    ss = pieces[0].shape[0]
    for by, piece in enumerate(pieces):
        which = lax.rem(places[1] + SIZE - by, SIZE)
        weights[pl.ds(pl.multiple_of(which * ss, ss), ss), :] = piece[...]


def times(left, weights):
    return lax.dot_general(left, weights, (((1,), (1,)), ((), ())), preferred_element_type=F32)


def apply_native_kernel(places, *refs):
    packs, pieces, (out, left, weights) = refs[:SIZE], refs[SIZE : 2 * SIZE], refs[2 * SIZE :]
    half, feats = weights.shape
    rows, ss = packs[0].shape[0], half // SIZE
    gather_weights(places, pieces, weights)
    for k, pack in enumerate(packs):
        at = pl.ds(k * rows, rows)
        left[at, pl.ds(0, ss)], left[at, pl.ds(ss, feats - ss)] = native_features(
            places, pack, half
        )
    out[...] = times(left[...], weights[...])


def apply_far_kernel(first, count, places, *refs):
    packs, pieces, before = refs[:count], refs[count : count + SIZE], refs[count + SIZE]
    outs, weights = refs[count + SIZE + 1 : -1], refs[-1]
    rows = packs[0].shape[0]
    gather_weights(places, pieces, weights)
    for k, (pack, out) in enumerate(zip(packs, outs)):
        sofar = before[pl.ds((first + k) * rows, rows), :]
        out[...] = (times(pack[...], weights[...]) + sofar).astype(out.dtype)


def shapes(*described):
    return [jax.ShapeDtypeStruct(shape, dtype) for shape, dtype in described]


def kernel_call(kernel, name, outs, n_in, scratch=(), flops=0):
    return pl.pallas_call(
        kernel,
        out_shape=outs,
        in_specs=[SCALAR] + [WHOLE] * n_in,
        out_specs=[WHOLE] * len(outs),
        scratch_shapes=list(scratch),
        compiler_params=PARAMS,
        cost_estimate=pl.CostEstimate(flops=flops, bytes_accessed=4 << 20, transcendentals=0),
        name=name,
    )


def strip_call(kernel, name, widths_in, outs):
    rows = outs[0].shape[0]

    def spec(width):
        return pl.BlockSpec((STRIP, width), lambda i: (i, 0))

    return pl.pallas_call(
        kernel,
        out_shape=outs,
        grid=(rows // STRIP,),
        in_specs=[SCALAR] + [spec(w) for w in widths_in],
        out_specs=[spec(o.shape[1]) for o in outs],
        compiler_params=PARAMS,
        cost_estimate=pl.CostEstimate(flops=0, bytes_accessed=4 << 20, transcendentals=0),
        name=name,
    )


def body(student, teacher):
    rows, half = student.shape
    wide = teacher.shape[1]
    width = 2 * half
    groups = lax.axis_size("loop") * lax.axis_size("rep")
    passages = rows * groups
    coef = 32.0 * width / (passages**0.5)
    level = passages / width
    ss, ts = half // SIZE, wide // SIZE
    feats = ss + ts
    flops = 2 * SIZE * rows * half * feats
    places = jnp.stack([place_along(GATHER), place_along(FIRST)]).astype(jnp.int32)

    t_far, s_far = other_core(teacher), other_core(student)
    *near, inv_s, inv_t = strip_call(
        pack_own_kernel,
        "pack_own",
        (half, half, wide, wide),
        shapes(*[((rows, half + ts), BF16)] * SIZE, *[((rows, 1), F32)] * 2),
    )(places, student, s_far, teacher, t_far)
    far = strip_call(
        pack_far_kernel,
        "pack_far",
        (half, wide, 1, 1),
        shapes(*[((rows, feats), BF16)] * SIZE),
    )(places, s_far, t_far, inv_s, inv_t)
    norm_own = near[0][:, :half]
    near = [near[0]] + [shifted(near[by], GATHER, by) for by in (1, 2, 3)]
    far = [far[0]] + [shifted(far[by], GATHER, by) for by in (1, 2, 3)]

    def weights_of(native, packs, name):
        own, *sends = kernel_call(
            functools.partial(gram_kernel, level * SIZE / groups, native),
            name,
            shapes(((ss, feats), F32), *[((ss, feats), BF16)] * 3),
            len(packs),
            [
                pltpu.VMEM((SIZE * rows, half), BF16),
                pltpu.VMEM((SIZE * rows, feats), BF16),
                pltpu.VMEM((half, feats), F32),
            ],
            flops,
        )(places, *packs)
        total = own
        for by in (1, 2, 3):
            total = total + shifted(sends[by - 1], FIRST, by).astype(F32)
        shared = total.astype(BF16)
        for by in (1, 2, 3):
            total = total + shifted(shared, SECOND, by).astype(F32)
        piece = total.astype(BF16)
        return [piece] + [shifted(piece, FIRST, by) for by in (1, 2, 3)]

    near_weights = weights_of(True, near, "gram_native")
    far_weights = weights_of(False, near + far, "gram_far")

    sofar = kernel_call(
        apply_native_kernel,
        "apply_native",
        shapes(((SIZE * rows, half), F32)),
        2 * SIZE,
        [pltpu.VMEM((SIZE * rows, feats), BF16), pltpu.VMEM((half, feats), BF16)],
        flops,
    )(places, *near, *near_weights)[0]
    parts = kernel_call(
        functools.partial(apply_far_kernel, 1, SIZE - 1),
        "apply_sent",
        shapes(*[((rows, half), BF16)] * 3),
        2 * SIZE,
        [pltpu.VMEM((half, feats), BF16)],
        flops * 3 // 4,
    )(places, *far[1:], *far_weights, sofar)
    grad_n = kernel_call(
        functools.partial(apply_far_kernel, 0, 1),
        "apply_kept",
        shapes(((rows, half), F32)),
        SIZE + 2,
        [pltpu.VMEM((half, feats), BF16)],
        flops // 4,
    )(places, far[0], *far_weights, sofar)[0]
    norm_f = norm_own.astype(F32)
    grad_n = grad_n + level * norm_f
    for by in (1, 2, 3):
        grad_n = grad_n + shifted(parts[by - 1], GATHER, -by).astype(F32)
    grad_n = coef * grad_n
    inner = jnp.sum(grad_n * norm_f, axis=1)
    inner = inner + other_core(inner)
    return (grad_n - inner[:, None] * norm_f) * inv_s


def solution(mesh):
    placed = (P(("loop", "rep"), "sec"), P(("loop", "rep"), "sec"))
    return jax.shard_map(
        body, mesh=mesh, in_specs=placed, out_specs=P(("loop", "rep"), "sec"), check_vma=False
    )
```

time: 114 us -> 84.6 us (0.74)
  waiting for transfers between devices: 45.2 us -> 16 us
  starting transfers between devices: 32 us -> 54.6 us
  local copies, waits for them, and re-layouts: 22.7 us -> 2.06 us
  Pallas kernels: 0 us -> 9.81 us
  other arithmetic: 9.77 us -> 1.86 us
  matrix products: 3.71 us -> 0 us
    ppermute x18 -> x27, waiting for transfers between devices: 44.4 us -> 12.9 us  [shifted(): return lax.ppermute(array, AXES, pairs)]
    ppermute x18 -> x27, starting transfers between devices: 21.6 us -> 40.6 us  [shifted(): return lax.ppermute(array, AXES, pairs)]
    unnamed x27 -> x4, local copies, waits for them, and re-layouts: 19.3 us -> 2.06 us
    pallas_call x0 -> x7, Pallas kernels: none -> 9.81 us  [the longest x2 3.19 us: weights_of(): kernel_call(functools.partial(gram_kernel, level * SIZE / groups, native)...]
    dot_general x2 -> x0, matrix products: 3.71 us -> none  [the longest x1 2.48 us: body(): partial = jnp.dot(left, weights, preferred_element_type=jnp.float32)]
    ppermute x3, starting transfers between devices: 10.4 us -> 14 us  [other_core(): return lax.ppermute(array, 'sec', [(0, 1), (1, 0)])]
    concatenate x3 -> x0, local copies, waits for them, and re-layouts: 3.28 us -> none  [the longest x2 2.37 us: all_gathered(): around = jnp.concatenate(parts + parts, axis=0)]
    reduce_sum x4 -> x0, other arithmetic: 2.78 us -> none  [inverse(): total = jnp.sum(own * own, axis=1) + jnp.sum(far * far, axis=1)]
  transfers between devices with their start and end apart: 21 -> 30, of which waited for: 14 -> 10; matrix products, arithmetic and copies ran while one was open for 9% -> 1% of each run, Pallas kernels for 0% -> 8%
where the time goes in v3:
time: 84.6 us; the launch traced here: 84.4 us
  starting transfers between devices  54.6 us (65%)
  waiting for transfers between devices  16 us (19%)
  Pallas kernels  9.81 us (12%)
  local copies, waits for them, and re-layouts  2.06 us (2%)
  other arithmetic  1.86 us (2%)
    ppermute x27, starting transfers between devices, shifted(): return lax.ppermute(array, AXES, pairs)  40.6 us
    ppermute x3, starting transfers between devices, other_core(): return lax.ppermute(array, 'sec', [(0, 1), (1, 0)])  14 us
    ppermute x27, waiting for transfers between devices, shifted(): return lax.ppermute(array, AXES, pairs)  12.9 us
    pallas_call x2, Pallas kernels, weights_of(): kernel_call(functools.partial(gram_kernel, level * SIZE / groups, native)...  3.19 us
    ppermute x3, waiting for transfers between devices, other_core(): return lax.ppermute(array, 'sec', [(0, 1), (1, 0)])  3.04 us
    unnamed x4, local copies, waits for them, and re-layouts  2.06 us
  transfers between devices with their start and end apart: 30, of which 10 were waited for; matrix products, arithmetic and copies ran while one was open for 1% of the time, Pallas kernels for 8%

profile of v3, /device:TPU:1, one launch (start us, length us, event | category | flops | bytes accessed | tf_op | source)
XLA Modules:
  0.0 84.4 jit_solution(12515709815749132002)
XLA Ops:
  0.0 1.4 %collective-permute-start.1 = (bf16[192,2048]{1,0:T(8,128)(2,1)}, bf16[192,2048]{1,0:T(8,128)(2,1)S(1)}, u32[]{:S(2)}, u32[]{:S(2)}) collective-permute-start(bf16[192,2048]{1,0:T(8,128)(2,1)} %t_own.1), channel_id=1, source_target_pairs={{0,1},{1,0},{2,3},{3,2},{4,5},{5,4},{6,7},{7,6},{8,9},{9,8},{10,11... | collective-permute-start | bytes 2359304 | tf_op jit(solution)/shard_map/ppermute | solution.py:41
  1.5 2.3 %collective-permute-done.s_far = bf16[192,512]{1,0:T(8,128)(2,1)S(1)} collective-permute-done((bf16[192,512]{1,0:T(8,128)(2,1)}, bf16[192,512]{1,0:T(8,128)(2,1)S(1)}, u32[]{:S(2)}, u32[]{:S(2)}) %collective-permute-start) | collective-permute-done | bytes 196640 | tf_op jit(solution)/shard_map/ppermute | solution.py:41
  3.8 1.1 %copy-done = bf16[192,2048]{1,0:T(8,128)(2,1)S(1)} copy-done((bf16[192,2048]{1,0:T(8,128)(2,1)S(1)}, bf16[192,2048]{1,0:T(8,128)(2,1)}, u32[]{:S(2)}) %copy-start) | copy-done | bytes 786456
  5.0 0.9 %copy-done.1 = bf16[192,512]{1,0:T(8,128)(2,1)S(1)} copy-done((bf16[192,512]{1,0:T(8,128)(2,1)S(1)}, bf16[192,512]{1,0:T(8,128)(2,1)}, u32[]{:S(2)}) %copy-start.1) | copy-done | bytes 196632
  5.9 1.6 %pack_own.1 = (bf16[192,1024]{1,0:T(8,128)(2,1)S(1)}, bf16[192,1024]{1,0:T(8,128)(2,1)S(1)}, bf16[192,1024]{1,0:T(8,128)(2,1)S(1)}, bf16[192,1024]{1,0:T(8,128)(...) custom-call(s32[2]{0:T(128)S(1)} %pad_add_fusion.places, bf16[192,512]{1,0:T(8,128)(2,1)S(1)} %copy-done.1, ...), custom_call_target="tpu_custom_call" | custom-call | bytes 4194304 | tf_op jit(solution)/shard_map/pack_own/pallas_call | solution.py:201
  7.5 1.4 %collective-permute-start.2 = (bf16[192,1024]{1,0:T(8,128)(2,1)S(1)}, bf16[192,1024]{1,0:T(8,128)(2,1)S(1)}, u32[]{:S(2)}, u32[]{:S(2)}) collective-permute-start(bf16[192,1024]{1,0:T(8,128)(2,1)S(1)} %get-tuple-element.30), channel_id=1, source_target_pairs={{0,4},{1,3},{16,20},{17,19},{32,36},{33,35},{48,52},{49,51},{4,8},... | collective-permute-start | bytes 1179656 | tf_op jit(solution)/shard_map/ppermute | solution.py:37
  8.9 2.5 %collective-permute-start.3 = (bf16[192,1024]{1,0:T(8,128)(2,1)S(1)}, bf16[192,1024]{1,0:T(8,128)(2,1)S(1)}, u32[]{:S(2)}, u32[]{:S(2)}) collective-permute-start(bf16[192,1024]{1,0:T(8,128)(2,1)S(1)} %get-tuple-element.31), channel_id=1, source_target_pairs={{0,8},{1,65},{16,24},{17,81},{32,40},{33,97},{48,56},{49,113},{4,1... | collective-permute-start | bytes 1179656 | tf_op jit(solution)/shard_map/ppermute | solution.py:37
  11.3 1.2 %collective-permute-start.4 = (bf16[192,1024]{1,0:T(8,128)(2,1)S(1)}, bf16[192,1024]{1,0:T(8,128)(2,1)S(1)}, u32[]{:S(2)}, u32[]{:S(2)}) collective-permute-start(bf16[192,1024]{1,0:T(8,128)(2,1)S(1)} %get-tuple-element.32), channel_id=1, source_target_pairs={{0,12},{1,67},{16,28},{17,83},{32,44},{33,99},{48,60},{49,115},{4,... | collective-permute-start | bytes 1179656 | tf_op jit(solution)/shard_map/ppermute | solution.py:37
  12.5 1.3 %pack_far.1 = (bf16[192,640]{1,0:T(8,128)(2,1)S(1)}, bf16[192,640]{1,0:T(8,128)(2,1)S(1)}, bf16[192,640]{1,0:T(8,128)(2,1)S(1)}, bf16[192,640]{1,0:T(8,128)(2,1)S(1)}) custom-call(s32[2]{0:T(128)S(1)} %pad_add_fusion.places, bf16[192,512]{1,0:T(8,128)(2,1)S(1)} %collective-permute-done.s_far, bf16[192,2048]{1,0:T(8,128)(2,1)S(1)} %collective-permute-done.1.t_far, ...), custom_call_target="tpu_custom_call" | custom-call | bytes 4194304 | tf_op jit(solution)/shard_map/pack_far/pallas_call | solution.py:207
  13.7 0.4 collective-permute-start.5
  14.1 0.9 %collective-permute-start.6 = (bf16[192,640]{1,0:T(8,128)(2,1)S(1)}, bf16[192,640]{1,0:T(8,128)(2,1)S(1)}, u32[]{:S(2)}, u32[]{:S(2)}) collective-permute-start(bf16[192,640]{1,0:T(8,128)(2,1)S(1)} %get-tuple-element.34), channel_id=1, source_target_pairs={{0,8},{1,65},{16,24},{17,81},{32,40},{33,97},{48,56},{49,113},{4,1... | collective-permute-start | bytes 737288 | tf_op jit(solution)/shard_map/ppermute | solution.py:37
  15.0 0.7 collective-permute-done.2.refs_1_
  15.7 1.4 %collective-permute-start.7 = (bf16[192,640]{1,0:T(8,128)(2,1)S(1)}, bf16[192,640]{1,0:T(8,128)(2,1)S(1)}, u32[]{:S(2)}, u32[]{:S(2)}) collective-permute-start(bf16[192,640]{1,0:T(8,128)(2,1)S(1)} %get-tuple-element.35), channel_id=1, source_target_pairs={{0,12},{1,67},{16,28},{17,83},{32,44},{33,99},{48,60},{49,115},{4,... | collective-permute-start | bytes 737288 | tf_op jit(solution)/shard_map/ppermute | solution.py:37
  17.0 4.0 %collective-permute-done.3.refs_2_ = bf16[192,1024]{1,0:T(8,128)(2,1)S(1)} collective-permute-done((bf16[192,1024]{1,0:T(8,128)(2,1)S(1)}, bf16[192,1024]{1,0:T(8,128)(2,1)S(1)}, u32[]{:S(2)}, u32[]{:S(2)}) %collective-permute-start.3) | collective-permute-done | bytes 393248 | tf_op jit(solution)/shard_map/ppermute | solution.py:37
  21.0 1.6 %gram_native.1 = (f32[128,640]{1,0:T(8,128)S(1)}, bf16[128,640]{1,0:T(8,128)(2,1)S(1)}, bf16[128,640]{1,0:T(8,128)(2,1)S(1)}, bf16[128,640]{1,0:T(8,128)(2,1)S(1)}) custom-call(s32[2]{0:T(128)S(1)} %pad_add_fusion.places, bf16[192,1024]{1,0:T(8,128)(2,1)S(1)} %get-tuple-element.29.refs_0_, bf16[192,1024]{1,0:T(8,128)(2,1)S(1)} %collective-permute-done.2.refs_1_, ...), custom_call_target="tpu_custom_call" | custom-call | flops 503316480 | bytes 4194304 | tf_op jit(solution)/shard_map/gram_native/pallas_call | solution.py:218
  22.6 1.1 %collective-permute-start.17 = (bf16[128,640]{1,0:T(8,128)(2,1)S(1)}, bf16[128,640]{1,0:T(8,128)(2,1)S(1)}, u32[]{:S(2)}, u32[]{:S(2)}) collective-permute-start(bf16[128,640]{1,0:T(8,128)(2,1)S(1)} %get-tuple-element.41), channel_id=1, source_target_pairs={{0,16},{1,5},{16,32},{17,21},{32,48},{33,37},{48,0},{49,53},{4,20}... | collective-permute-start | bytes 491528 | tf_op jit(solution)/shard_map/ppermute | solution.py:37
  23.8 2.6 %collective-permute-start.18 = (bf16[128,640]{1,0:T(8,128)(2,1)S(1)}, bf16[128,640]{1,0:T(8,128)(2,1)S(1)}, u32[]{:S(2)}, u32[]{:S(2)}) collective-permute-start(bf16[128,640]{1,0:T(8,128)(2,1)S(1)} %get-tuple-element.42), channel_id=1, source_target_pairs={{0,32},{1,9},{16,48},{17,25},{32,0},{33,41},{48,16},{49,57},{4,36}... | collective-permute-start | bytes 491528 | tf_op jit(solution)/shard_map/ppermute | solution.py:37
  26.4 1.1 %collective-permute-start.19 = (bf16[128,640]{1,0:T(8,128)(2,1)S(1)}, bf16[128,640]{1,0:T(8,128)(2,1)S(1)}, u32[]{:S(2)}, u32[]{:S(2)}) collective-permute-start(bf16[128,640]{1,0:T(8,128)(2,1)S(1)} %get-tuple-element.43), channel_id=1, source_target_pairs={{0,48},{1,13},{16,0},{17,29},{32,16},{33,45},{48,32},{49,61},{4,52... | collective-permute-start | bytes 491528 | tf_op jit(solution)/shard_map/ppermute | solution.py:37
  27.5 1.6 %gram_far.1 = (f32[128,640]{1,0:T(8,128)S(1)}, bf16[128,640]{1,0:T(8,128)(2,1)S(1)}, bf16[128,640]{1,0:T(8,128)(2,1)S(1)}, bf16[128,640]{1,0:T(8,128)(2,1)S(1)}) custom-call(s32[2]{0:T(128)S(1)} %pad_add_fusion.places, bf16[192,1024]{1,0:T(8,128)(2,1)S(1)} %get-tuple-element.29.refs_0_, bf16[192,1024]{1,0:T(8,128)(2,1)S(1)} %collective-permute-done.2.refs_1_, ...), custom_call_target="tpu_custom_call" | custom-call | flops 503316480 | bytes 4194304 | tf_op jit(solution)/shard_map/gram_far/pallas_call | solution.py:218
  29.1 1.3 %collective-permute-start.10 = (bf16[128,640]{1,0:T(8,128)(2,1)S(1)}, bf16[128,640]{1,0:T(8,128)(2,1)S(1)}, u32[]{:S(2)}, u32[]{:S(2)}) collective-permute-start(bf16[128,640]{1,0:T(8,128)(2,1)S(1)} %get-tuple-element.39), channel_id=1, source_target_pairs={{0,48},{1,13},{16,0},{17,29},{32,16},{33,45},{48,32},{49,61},{4,52... | collective-permute-start | bytes 491528 | tf_op jit(solution)/shard_map/ppermute | solution.py:37
  30.6 1.4 %collective-permute-start.9 = (bf16[128,640]{1,0:T(8,128)(2,1)S(1)}, bf16[128,640]{1,0:T(8,128)(2,1)S(1)}, u32[]{:S(2)}, u32[]{:S(2)}) collective-permute-start(bf16[128,640]{1,0:T(8,128)(2,1)S(1)} %get-tuple-element.38), channel_id=1, source_target_pairs={{0,32},{1,9},{16,48},{17,25},{32,0},{33,41},{48,16},{49,57},{4,36}... | collective-permute-start | bytes 491528 | tf_op jit(solution)/shard_map/ppermute | solution.py:37
  32.1 1.7 %collective-permute-start.20 = (bf16[128,640]{1,0:T(8,128)(2,1)S(1)}, bf16[128,640]{1,0:T(8,128)(2,1)S(1)}, u32[]{:S(2)}, u32[]{:S(2)}) collective-permute-start(bf16[128,640]{1,0:T(8,128)(2,1)S(1)} %fusion.9), channel_id=1, source_target_pairs={{0,2},{1,17},{16,18},{17,33},{32,34},{33,49},{48,50},{49,1},{4,6},... | collective-permute-start | bytes 491528 | tf_op jit(solution)/shard_map/ppermute | solution.py:37
  33.8 3.3 %collective-permute-start.21 = (bf16[128,640]{1,0:T(8,128)(2,1)S(1)}, bf16[128,640]{1,0:T(8,128)(2,1)S(1)}, u32[]{:S(2)}, u32[]{:S(2)}) collective-permute-start(bf16[128,640]{1,0:T(8,128)(2,1)S(1)} %fusion.9), channel_id=1, source_target_pairs={{0,64},{1,33},{16,80},{17,49},{32,96},{33,1},{48,112},{49,17},{4,6... | collective-permute-start | bytes 491528 | tf_op jit(solution)/shard_map/ppermute | solution.py:37
  37.1 0.7 collective-permute-start.22
  38.0 1.3 %collective-permute-start.11 = (bf16[128,640]{1,0:T(8,128)(2,1)S(1)}, bf16[128,640]{1,0:T(8,128)(2,1)S(1)}, u32[]{:S(2)}, u32[]{:S(2)}) collective-permute-start(bf16[128,640]{1,0:T(8,128)(2,1)S(1)} %fusion.8), channel_id=1, source_target_pairs={{0,2},{1,17},{16,18},{17,33},{32,34},{33,49},{48,50},{49,1},{4,6},... | collective-permute-start | bytes 491528 | tf_op jit(solution)/shard_map/ppermute | solution.py:37
  39.3 3.6 %collective-permute-start.12 = (bf16[128,640]{1,0:T(8,128)(2,1)S(1)}, bf16[128,640]{1,0:T(8,128)(2,1)S(1)}, u32[]{:S(2)}, u32[]{:S(2)}) collective-permute-start(bf16[128,640]{1,0:T(8,128)(2,1)S(1)} %fusion.8), channel_id=1, source_target_pairs={{0,64},{1,33},{16,80},{17,49},{32,96},{33,1},{48,112},{49,17},{4,6... | collective-permute-start | bytes 491528 | tf_op jit(solution)/shard_map/ppermute | solution.py:37
  42.9 0.4 collective-permute-start.13
  43.3 0.3 collective-permute-done.21
  43.8 3.5 %collective-permute-start.23 = (bf16[128,640]{1,0:T(8,128)(2,1)S(1)}, bf16[128,640]{1,0:T(8,128)(2,1)S(1)}, u32[]{:S(2)}, u32[]{:S(2)}) collective-permute-start(bf16[128,640]{1,0:T(8,128)(2,1)S(1)} %add_convert_fusion.refs_4_), channel_id=1, source_target_pairs={{0,16},{1,5},{16,32},{17,21},{32,48},{33,37},{48,0},{49,53},{4,20}... | collective-permute-start | bytes 491528 | tf_op jit(solution)/shard_map/ppermute | solution.py:37
  47.4 2.5 %collective-permute-start.25 = (bf16[128,640]{1,0:T(8,128)(2,1)S(1)}, bf16[128,640]{1,0:T(8,128)(2,1)S(1)}, u32[]{:S(2)}, u32[]{:S(2)}) collective-permute-start(bf16[128,640]{1,0:T(8,128)(2,1)S(1)} %add_convert_fusion.refs_4_), channel_id=1, source_target_pairs={{0,48},{1,13},{16,0},{17,29},{32,16},{33,45},{48,32},{49,61},{4,52... | collective-permute-start | bytes 491528 | tf_op jit(solution)/shard_map/ppermute | solution.py:37
  50.0 0.7 collective-permute-start.14
  50.8 1.9 %collective-permute-start.15 = (bf16[128,640]{1,0:T(8,128)(2,1)S(1)}, bf16[128,640]{1,0:T(8,128)(2,1)S(1)}, u32[]{:S(2)}, u32[]{:S(2)}) collective-permute-start(bf16[128,640]{1,0:T(8,128)(2,1)S(1)} %add_convert_fusion.1.refs_1_.refs_3_), channel_id=1, source_target_pairs={{0,32},{1,9},{16,48},{17,25},{32,0},{33,41},{48,16},{49,57},{4,36}... | collective-permute-start | bytes 491528 | tf_op jit(solution)/shard_map/ppermute | solution.py:37
  52.6 2.0 %collective-permute-start.16 = (bf16[128,640]{1,0:T(8,128)(2,1)S(1)}, bf16[128,640]{1,0:T(8,128)(2,1)S(1)}, u32[]{:S(2)}, u32[]{:S(2)}) collective-permute-start(bf16[128,640]{1,0:T(8,128)(2,1)S(1)} %add_convert_fusion.1.refs_1_.refs_3_), channel_id=1, source_target_pairs={{0,48},{1,13},{16,0},{17,29},{32,16},{33,45},{48,32},{49,61},{4,52... | collective-permute-start | bytes 491528 | tf_op jit(solution)/shard_map/ppermute | solution.py:37
  54.6 1.4 %apply_native.1.refs_5_.refs_7_ = f32[768,512]{1,0:T(8,128)S(1)} custom-call(s32[2]{0:T(128)S(1)} %pad_add_fusion.places, bf16[192,1024]{1,0:T(8,128)(2,1)S(1)} %get-tuple-element.29.refs_0_, bf16[192,1024]{1,0:T(8,128)(2,1)S(1)} %collective-permute-done.2.refs_1_, bf16[192,1024]{1,0:T(8,128)(2,1)S(1)} %collective-permute-done.3.refs_2_, ...), custom_call_target="tpu_custom_call" | custom-call | flops 503316480 | bytes 4194304 | tf_op jit(solution)/shard_map/apply_native/pallas_call | solution.py:242
  56.0 1.5 %collective-permute-done.14.refs_2_.refs_4_ = bf16[128,640]{1,0:T(8,128)(2,1)S(1)} collective-permute-done((bf16[128,640]{1,0:T(8,128)(2,1)S(1)}, bf16[128,640]{1,0:T(8,128)(2,1)S(1)}, u32[]{:S(2)}, u32[]{:S(2)}) %collective-permute-start.14) | collective-permute-done | bytes 163872 | tf_op jit(solution)/shard_map/ppermute | solution.py:37
  57.5 0.6 collective-permute-done.16.refs_4_.refs_6_
  58.1 1.4 %apply_sent.1 = (bf16[192,512]{1,0:T(8,128)(2,1)S(1)}, bf16[192,512]{1,0:T(8,128)(2,1)S(1)}, bf16[192,512]{1,0:T(8,128)(2,1)S(1)}) custom-call(s32[2]{0:T(128)S(1)} %pad_add_fusion.places, bf16[192,640]{1,0:T(8,128)(2,1)S(1)} %collective-permute-done.5.refs_5_.refs_0_, bf16[192,640]{1,0:T(8,128)(2,1)S(1)} %collective-permute-done.6.refs_6_.refs_1_, ...), custom_call_target="tpu_custom_call" | custom-call | flops 377487360 | bytes 4194304 | tf_op jit(solution)/shard_map/apply_sent/pallas_call | solution.py:250
  59.5 2.1 %collective-permute-start.26 = (bf16[192,512]{1,0:T(8,128)(2,1)S(1)}, bf16[192,512]{1,0:T(8,128)(2,1)S(1)}, u32[]{:S(2)}, u32[]{:S(2)}) collective-permute-start(bf16[192,512]{1,0:T(8,128)(2,1)S(1)} %get-tuple-element.44), channel_id=1, source_target_pairs={{0,12},{1,67},{16,28},{17,83},{32,44},{33,99},{48,60},{49,115},{4,... | collective-permute-start | bytes 589832 | tf_op jit(solution)/shard_map/ppermute | solution.py:37
  61.7 0.7 collective-permute-start.27
  62.3 0.7 collective-permute-start.28
  63.0 1.0 %apply_kept.1 = f32[192,512]{1,0:T(8,128)S(1)} custom-call(s32[2]{0:T(128)S(1)} %pad_add_fusion.places, bf16[192,640]{1,0:T(8,128)(2,1)S(1)} %get-tuple-element.28.refs_4_.refs_0_, bf16[128,640]{1,0:T(8,128)(2,1)S(1)} %add_convert_fusion.1.refs_1_.refs_3_, bf16[128,640]{1,0:T(8,128)(2,1)S(1)} %collective-permute-done.14.refs_2_.refs_4_, ...), custom_call_target="tpu_custom_call" | custom-call | flops 125829120 | bytes 4194304 | tf_op jit(solution)/shard_map/apply_kept/pallas_call | solution.py:258
  64.0 2.4 %collective-permute-done.26 = bf16[192,512]{1,0:T(8,128)(2,1)S(1)} collective-permute-done((bf16[192,512]{1,0:T(8,128)(2,1)S(1)}, bf16[192,512]{1,0:T(8,128)(2,1)S(1)}, u32[]{:S(2)}, u32[]{:S(2)}) %collective-permute-start.26) | collective-permute-done | bytes 196640 | tf_op jit(solution)/shard_map/ppermute | solution.py:37
  66.4 1.4 %collective-permute-done.27 = bf16[192,512]{1,0:T(8,128)(2,1)S(1)} collective-permute-done((bf16[192,512]{1,0:T(8,128)(2,1)S(1)}, bf16[192,512]{1,0:T(8,128)(2,1)S(1)}, u32[]{:S(2)}, u32[]{:S(2)}) %collective-permute-start.27) | collective-permute-done | bytes 196640 | tf_op jit(solution)/shard_map/ppermute | solution.py:37
  67.8 2.0 %collective-permute-done.28 = bf16[192,512]{1,0:T(8,128)(2,1)S(1)} collective-permute-done((bf16[192,512]{1,0:T(8,128)(2,1)S(1)}, bf16[192,512]{1,0:T(8,128)(2,1)S(1)}, u32[]{:S(2)}, u32[]{:S(2)}) %collective-permute-start.28) | collective-permute-done | bytes 196640 | tf_op jit(solution)/shard_map/ppermute | solution.py:37
  69.8 0.2 fusion.5
  70.0 12.6 %collective-permute-start.29 = (f32[192]{0:T(256)S(1)}, f32[192]{0:T(256)S(1)}, u32[]{:S(2)}, u32[]{:S(2)}) collective-permute-start(f32[192]{0:T(256)S(1)} %fusion.5), channel_id=1, source_target_pairs={{0,1},{1,0},{2,3},{3,2},{4,5},{5,4},{6,7},{7,6},{8,9},{9,8},{10,11... | collective-permute-start | bytes 2312 | tf_op jit(solution)/shard_map/ppermute | solution.py:41
  82.8 0.7 collective-permute-done.29
  83.5 0.9 %fusion.7 = f32[192,512]{1,0:T(8,128)} fusion(f32[192]{0:T(256)S(1)} %reduce, f32[192]{0:T(256)S(1)} %add.82, bf16[192,1024]{1,0:T(8,128)(2,1)S(1)} %get-tuple-element.29.refs_0_, bf16[192,512]{1,0:T(8,128)(2,1)S(1)} %collective-permute-done.28, bf16[192,512]{1,0:T(8,128)(2,1)S(1)} %collective-permute-done.27, ...), kind=kLoop, calls=%fused_computation.10 | loop fusion | flops 1277952 | bytes 1574400 | tf_op jit(solution)/shard_map/mul | solution.py:273
  (32 shorter events, 1.0 us)
Async XLA Ops:
  0.0 3.8 %collective-permute-start.1 = (bf16[192,2048]{1,0:T(8,128)(2,1)}, bf16[192,2048]{1,0:T(8,128)(2,1)S(1)}, u32[]{:S(2)}, u32[]{:S(2)}) collective-permute-start(bf16[192,2048]{1,0:T(8,128)(2,1)} %t_own.1), channel_id=1, source_target_pairs={{0,1},{1,0},{2,3},{3,2},{4,5},{5,4},{6,7},{7,6},{8,9},{9,8},{10,11... | collective-permute-start | bytes 2359304 | tf_op jit(solution)/shard_map/ppermute | solution.py:41
  1.4 2.4 %collective-permute-start = (bf16[192,512]{1,0:T(8,128)(2,1)}, bf16[192,512]{1,0:T(8,128)(2,1)S(1)}, u32[]{:S(2)}, u32[]{:S(2)}) collective-permute-start(bf16[192,512]{1,0:T(8,128)(2,1)} %s_own.1), channel_id=1, source_target_pairs={{0,1},{1,0},{2,3},{3,2},{4,5},{5,4},{6,7},{7,6},{8,9},{9,8},{10,11... | collective-permute-start | bytes 589832 | tf_op jit(solution)/shard_map/ppermute | solution.py:41
  3.8 1.1 %copy-start = (bf16[192,2048]{1,0:T(8,128)(2,1)S(1)}, bf16[192,2048]{1,0:T(8,128)(2,1)}, u32[]{:S(2)}) copy-start(bf16[192,2048]{1,0:T(8,128)(2,1)} %t_own.1) | copy-start | bytes 2359300
  5.0 0.9 %copy-start.1 = (bf16[192,512]{1,0:T(8,128)(2,1)S(1)}, bf16[192,512]{1,0:T(8,128)(2,1)}, u32[]{:S(2)}) copy-start(bf16[192,512]{1,0:T(8,128)(2,1)} %s_own.1) | copy-start | bytes 589828
  7.5 8.2 %collective-permute-start.2 = (bf16[192,1024]{1,0:T(8,128)(2,1)S(1)}, bf16[192,1024]{1,0:T(8,128)(2,1)S(1)}, u32[]{:S(2)}, u32[]{:S(2)}) collective-permute-start(bf16[192,1024]{1,0:T(8,128)(2,1)S(1)} %get-tuple-element.30), channel_id=1, source_target_pairs={{0,4},{1,3},{16,20},{17,19},{32,36},{33,35},{48,52},{49,51},{4,8},... | collective-permute-start | bytes 1179656 | tf_op jit(solution)/shard_map/ppermute | solution.py:37
  8.9 12.2 %collective-permute-start.3 = (bf16[192,1024]{1,0:T(8,128)(2,1)S(1)}, bf16[192,1024]{1,0:T(8,128)(2,1)S(1)}, u32[]{:S(2)}, u32[]{:S(2)}) collective-permute-start(bf16[192,1024]{1,0:T(8,128)(2,1)S(1)} %get-tuple-element.31), channel_id=1, source_target_pairs={{0,8},{1,65},{16,24},{17,81},{32,40},{33,97},{48,56},{49,113},{4,1... | collective-permute-start | bytes 1179656 | tf_op jit(solution)/shard_map/ppermute | solution.py:37
  11.3 9.7 %collective-permute-start.4 = (bf16[192,1024]{1,0:T(8,128)(2,1)S(1)}, bf16[192,1024]{1,0:T(8,128)(2,1)S(1)}, u32[]{:S(2)}, u32[]{:S(2)}) collective-permute-start(bf16[192,1024]{1,0:T(8,128)(2,1)S(1)} %get-tuple-element.32), channel_id=1, source_target_pairs={{0,12},{1,67},{16,28},{17,83},{32,44},{33,99},{48,60},{49,115},{4,... | collective-permute-start | bytes 1179656 | tf_op jit(solution)/shard_map/ppermute | solution.py:37
  13.7 12.7 %collective-permute-start.5 = (bf16[192,640]{1,0:T(8,128)(2,1)S(1)}, bf16[192,640]{1,0:T(8,128)(2,1)S(1)}, u32[]{:S(2)}, u32[]{:S(2)}) collective-permute-start(bf16[192,640]{1,0:T(8,128)(2,1)S(1)} %get-tuple-element.33), channel_id=1, source_target_pairs={{0,4},{1,3},{16,20},{17,19},{32,36},{33,35},{48,52},{49,51},{4,8},... | collective-permute-start | bytes 737288 | tf_op jit(solution)/shard_map/ppermute | solution.py:37
  14.1 13.4 %collective-permute-start.6 = (bf16[192,640]{1,0:T(8,128)(2,1)S(1)}, bf16[192,640]{1,0:T(8,128)(2,1)S(1)}, u32[]{:S(2)}, u32[]{:S(2)}) collective-permute-start(bf16[192,640]{1,0:T(8,128)(2,1)S(1)} %get-tuple-element.34), channel_id=1, source_target_pairs={{0,8},{1,65},{16,24},{17,81},{32,40},{33,97},{48,56},{49,113},{4,1... | collective-permute-start | bytes 737288 | tf_op jit(solution)/shard_map/ppermute | solution.py:37
  15.7 11.8 %collective-permute-start.7 = (bf16[192,640]{1,0:T(8,128)(2,1)S(1)}, bf16[192,640]{1,0:T(8,128)(2,1)S(1)}, u32[]{:S(2)}, u32[]{:S(2)}) collective-permute-start(bf16[192,640]{1,0:T(8,128)(2,1)S(1)} %get-tuple-element.35), channel_id=1, source_target_pairs={{0,12},{1,67},{16,28},{17,83},{32,44},{33,99},{48,60},{49,115},{4,... | collective-permute-start | bytes 737288 | tf_op jit(solution)/shard_map/ppermute | solution.py:37
  22.6 7.9 %collective-permute-start.17 = (bf16[128,640]{1,0:T(8,128)(2,1)S(1)}, bf16[128,640]{1,0:T(8,128)(2,1)S(1)}, u32[]{:S(2)}, u32[]{:S(2)}) collective-permute-start(bf16[128,640]{1,0:T(8,128)(2,1)S(1)} %get-tuple-element.41), channel_id=1, source_target_pairs={{0,16},{1,5},{16,32},{17,21},{32,48},{33,37},{48,0},{49,53},{4,20}... | collective-permute-start | bytes 491528 | tf_op jit(solution)/shard_map/ppermute | solution.py:37
  23.8 8.2 %collective-permute-start.18 = (bf16[128,640]{1,0:T(8,128)(2,1)S(1)}, bf16[128,640]{1,0:T(8,128)(2,1)S(1)}, u32[]{:S(2)}, u32[]{:S(2)}) collective-permute-start(bf16[128,640]{1,0:T(8,128)(2,1)S(1)} %get-tuple-element.42), channel_id=1, source_target_pairs={{0,32},{1,9},{16,48},{17,25},{32,0},{33,41},{48,16},{49,57},{4,36}... | collective-permute-start | bytes 491528 | tf_op jit(solution)/shard_map/ppermute | solution.py:37
  26.4 5.6 %collective-permute-start.19 = (bf16[128,640]{1,0:T(8,128)(2,1)S(1)}, bf16[128,640]{1,0:T(8,128)(2,1)S(1)}, u32[]{:S(2)}, u32[]{:S(2)}) collective-permute-start(bf16[128,640]{1,0:T(8,128)(2,1)S(1)} %get-tuple-element.43), channel_id=1, source_target_pairs={{0,48},{1,13},{16,0},{17,29},{32,16},{33,45},{48,32},{49,61},{4,52... | collective-permute-start | bytes 491528 | tf_op jit(solution)/shard_map/ppermute | solution.py:37
  29.1 8.1 %collective-permute-start.10 = (bf16[128,640]{1,0:T(8,128)(2,1)S(1)}, bf16[128,640]{1,0:T(8,128)(2,1)S(1)}, u32[]{:S(2)}, u32[]{:S(2)}) collective-permute-start(bf16[128,640]{1,0:T(8,128)(2,1)S(1)} %get-tuple-element.39), channel_id=1, source_target_pairs={{0,48},{1,13},{16,0},{17,29},{32,16},{33,45},{48,32},{49,61},{4,52... | collective-permute-start | bytes 491528 | tf_op jit(solution)/shard_map/ppermute | solution.py:37
  30.4 7.5 %collective-permute-start.8 = (bf16[128,640]{1,0:T(8,128)(2,1)S(1)}, bf16[128,640]{1,0:T(8,128)(2,1)S(1)}, u32[]{:S(2)}, u32[]{:S(2)}) collective-permute-start(bf16[128,640]{1,0:T(8,128)(2,1)S(1)} %get-tuple-element.37), channel_id=1, source_target_pairs={{0,16},{1,5},{16,32},{17,21},{32,48},{33,37},{48,0},{49,53},{4,20}... | collective-permute-start | bytes 491528 | tf_op jit(solution)/shard_map/ppermute | solution.py:37
  30.6 7.3 %collective-permute-start.9 = (bf16[128,640]{1,0:T(8,128)(2,1)S(1)}, bf16[128,640]{1,0:T(8,128)(2,1)S(1)}, u32[]{:S(2)}, u32[]{:S(2)}) collective-permute-start(bf16[128,640]{1,0:T(8,128)(2,1)S(1)} %get-tuple-element.38), channel_id=1, source_target_pairs={{0,32},{1,9},{16,48},{17,25},{32,0},{33,41},{48,16},{49,57},{4,36}... | collective-permute-start | bytes 491528 | tf_op jit(solution)/shard_map/ppermute | solution.py:37
  32.1 10.8 %collective-permute-start.20 = (bf16[128,640]{1,0:T(8,128)(2,1)S(1)}, bf16[128,640]{1,0:T(8,128)(2,1)S(1)}, u32[]{:S(2)}, u32[]{:S(2)}) collective-permute-start(bf16[128,640]{1,0:T(8,128)(2,1)S(1)} %fusion.9), channel_id=1, source_target_pairs={{0,2},{1,17},{16,18},{17,33},{32,34},{33,49},{48,50},{49,1},{4,6},... | collective-permute-start | bytes 491528 | tf_op jit(solution)/shard_map/ppermute | solution.py:37
  33.8 9.9 %collective-permute-start.21 = (bf16[128,640]{1,0:T(8,128)(2,1)S(1)}, bf16[128,640]{1,0:T(8,128)(2,1)S(1)}, u32[]{:S(2)}, u32[]{:S(2)}) collective-permute-start(bf16[128,640]{1,0:T(8,128)(2,1)S(1)} %fusion.9), channel_id=1, source_target_pairs={{0,64},{1,33},{16,80},{17,49},{32,96},{33,1},{48,112},{49,17},{4,6... | collective-permute-start | bytes 491528 | tf_op jit(solution)/shard_map/ppermute | solution.py:37
  37.1 6.5 %collective-permute-start.22 = (bf16[128,640]{1,0:T(8,128)(2,1)S(1)}, bf16[128,640]{1,0:T(8,128)(2,1)S(1)}, u32[]{:S(2)}, u32[]{:S(2)}) collective-permute-start(bf16[128,640]{1,0:T(8,128)(2,1)S(1)} %fusion.9), channel_id=1, source_target_pairs={{0,66},{1,49},{16,82},{17,1},{32,98},{33,17},{48,114},{49,33},{4,7... | collective-permute-start | bytes 491528 | tf_op jit(solution)/shard_map/ppermute | solution.py:37
  38.0 9.4 %collective-permute-start.11 = (bf16[128,640]{1,0:T(8,128)(2,1)S(1)}, bf16[128,640]{1,0:T(8,128)(2,1)S(1)}, u32[]{:S(2)}, u32[]{:S(2)}) collective-permute-start(bf16[128,640]{1,0:T(8,128)(2,1)S(1)} %fusion.8), channel_id=1, source_target_pairs={{0,2},{1,17},{16,18},{17,33},{32,34},{33,49},{48,50},{49,1},{4,6},... | collective-permute-start | bytes 491528 | tf_op jit(solution)/shard_map/ppermute | solution.py:37
  39.3 10.5 %collective-permute-start.12 = (bf16[128,640]{1,0:T(8,128)(2,1)S(1)}, bf16[128,640]{1,0:T(8,128)(2,1)S(1)}, u32[]{:S(2)}, u32[]{:S(2)}) collective-permute-start(bf16[128,640]{1,0:T(8,128)(2,1)S(1)} %fusion.8), channel_id=1, source_target_pairs={{0,64},{1,33},{16,80},{17,49},{32,96},{33,1},{48,112},{49,17},{4,6... | collective-permute-start | bytes 491528 | tf_op jit(solution)/shard_map/ppermute | solution.py:37
  42.9 6.9 %collective-permute-start.13 = (bf16[128,640]{1,0:T(8,128)(2,1)S(1)}, bf16[128,640]{1,0:T(8,128)(2,1)S(1)}, u32[]{:S(2)}, u32[]{:S(2)}) collective-permute-start(bf16[128,640]{1,0:T(8,128)(2,1)S(1)} %fusion.8), channel_id=1, source_target_pairs={{0,66},{1,49},{16,82},{17,1},{32,98},{33,17},{48,114},{49,33},{4,7... | collective-permute-start | bytes 491528 | tf_op jit(solution)/shard_map/ppermute | solution.py:37
  43.8 8.8 %collective-permute-start.23 = (bf16[128,640]{1,0:T(8,128)(2,1)S(1)}, bf16[128,640]{1,0:T(8,128)(2,1)S(1)}, u32[]{:S(2)}, u32[]{:S(2)}) collective-permute-start(bf16[128,640]{1,0:T(8,128)(2,1)S(1)} %add_convert_fusion.refs_4_), channel_id=1, source_target_pairs={{0,16},{1,5},{16,32},{17,21},{32,48},{33,37},{48,0},{49,53},{4,20}... | collective-permute-start | bytes 491528 | tf_op jit(solution)/shard_map/ppermute | solution.py:37
  47.4 7.3 %collective-permute-start.24 = (bf16[128,640]{1,0:T(8,128)(2,1)S(1)}, bf16[128,640]{1,0:T(8,128)(2,1)S(1)}, u32[]{:S(2)}, u32[]{:S(2)}) collective-permute-start(bf16[128,640]{1,0:T(8,128)(2,1)S(1)} %add_convert_fusion.refs_4_), channel_id=1, source_target_pairs={{0,32},{1,9},{16,48},{17,25},{32,0},{33,41},{48,16},{49,57},{4,36}... | collective-permute-start | bytes 491528 | tf_op jit(solution)/shard_map/ppermute | solution.py:37
  47.4 7.3 %collective-permute-start.25 = (bf16[128,640]{1,0:T(8,128)(2,1)S(1)}, bf16[128,640]{1,0:T(8,128)(2,1)S(1)}, u32[]{:S(2)}, u32[]{:S(2)}) collective-permute-start(bf16[128,640]{1,0:T(8,128)(2,1)S(1)} %add_convert_fusion.refs_4_), channel_id=1, source_target_pairs={{0,48},{1,13},{16,0},{17,29},{32,16},{33,45},{48,32},{49,61},{4,52... | collective-permute-start | bytes 491528 | tf_op jit(solution)/shard_map/ppermute | solution.py:37
  50.0 7.5 %collective-permute-start.14 = (bf16[128,640]{1,0:T(8,128)(2,1)S(1)}, bf16[128,640]{1,0:T(8,128)(2,1)S(1)}, u32[]{:S(2)}, u32[]{:S(2)}) collective-permute-start(bf16[128,640]{1,0:T(8,128)(2,1)S(1)} %add_convert_fusion.1.refs_1_.refs_3_), channel_id=1, source_target_pairs={{0,16},{1,5},{16,32},{17,21},{32,48},{33,37},{48,0},{49,53},{4,20}... | collective-permute-start | bytes 491528 | tf_op jit(solution)/shard_map/ppermute | solution.py:37
  50.8 6.8 %collective-permute-start.15 = (bf16[128,640]{1,0:T(8,128)(2,1)S(1)}, bf16[128,640]{1,0:T(8,128)(2,1)S(1)}, u32[]{:S(2)}, u32[]{:S(2)}) collective-permute-start(bf16[128,640]{1,0:T(8,128)(2,1)S(1)} %add_convert_fusion.1.refs_1_.refs_3_), channel_id=1, source_target_pairs={{0,32},{1,9},{16,48},{17,25},{32,0},{33,41},{48,16},{49,57},{4,36}... | collective-permute-start | bytes 491528 | tf_op jit(solution)/shard_map/ppermute | solution.py:37
  52.6 5.5 %collective-permute-start.16 = (bf16[128,640]{1,0:T(8,128)(2,1)S(1)}, bf16[128,640]{1,0:T(8,128)(2,1)S(1)}, u32[]{:S(2)}, u32[]{:S(2)}) collective-permute-start(bf16[128,640]{1,0:T(8,128)(2,1)S(1)} %add_convert_fusion.1.refs_1_.refs_3_), channel_id=1, source_target_pairs={{0,48},{1,13},{16,0},{17,29},{32,16},{33,45},{48,32},{49,61},{4,52... | collective-permute-start | bytes 491528 | tf_op jit(solution)/shard_map/ppermute | solution.py:37
  59.5 6.9 %collective-permute-start.26 = (bf16[192,512]{1,0:T(8,128)(2,1)S(1)}, bf16[192,512]{1,0:T(8,128)(2,1)S(1)}, u32[]{:S(2)}, u32[]{:S(2)}) collective-permute-start(bf16[192,512]{1,0:T(8,128)(2,1)S(1)} %get-tuple-element.44), channel_id=1, source_target_pairs={{0,12},{1,67},{16,28},{17,83},{32,44},{33,99},{48,60},{49,115},{4,... | collective-permute-start | bytes 589832 | tf_op jit(solution)/shard_map/ppermute | solution.py:37
  61.7 6.1 %collective-permute-start.27 = (bf16[192,512]{1,0:T(8,128)(2,1)S(1)}, bf16[192,512]{1,0:T(8,128)(2,1)S(1)}, u32[]{:S(2)}, u32[]{:S(2)}) collective-permute-start(bf16[192,512]{1,0:T(8,128)(2,1)S(1)} %get-tuple-element.45), channel_id=1, source_target_pairs={{0,8},{1,65},{16,24},{17,81},{32,40},{33,97},{48,56},{49,113},{4,1... | collective-permute-start | bytes 589832 | tf_op jit(solution)/shard_map/ppermute | solution.py:37
  62.3 7.4 %collective-permute-start.28 = (bf16[192,512]{1,0:T(8,128)(2,1)S(1)}, bf16[192,512]{1,0:T(8,128)(2,1)S(1)}, u32[]{:S(2)}, u32[]{:S(2)}) collective-permute-start(bf16[192,512]{1,0:T(8,128)(2,1)S(1)} %get-tuple-element.46), channel_id=1, source_target_pairs={{0,4},{1,3},{16,20},{17,19},{32,36},{33,35},{48,52},{49,51},{4,8},... | collective-permute-start | bytes 589832 | tf_op jit(solution)/shard_map/ppermute | solution.py:37
  70.0 13.4 %collective-permute-start.29 = (f32[192]{0:T(256)S(1)}, f32[192]{0:T(256)S(1)}, u32[]{:S(2)}, u32[]{:S(2)}) collective-permute-start(f32[192]{0:T(256)S(1)} %fusion.5), channel_id=1, source_target_pairs={{0,1},{1,0},{2,3},{3,2},{4,5},{5,4},{6,7},{7,6},{8,9},{9,8},{10,11... | collective-permute-start | bytes 2312 | tf_op jit(solution)/shard_map/ppermute | solution.py:41

commit v4 on v3

--- a/solution.py
+++ b/solution.py
@@ -12,8 +12,9 @@
 X, Y, Z = 0, 1, 2
 SIZE = 4
 GATHER = (Y, X)
-FIRST = (Z, Y)
-SECOND = (X, Z)
+FIRST = ((Z, Z), (X, Y))
+SECOND = ((X, Y), (Z, Z))
+ORDER = (2, 1, 3)
 STRIP = 32
 PARAMS = pltpu.CompilerParams(vmem_limit_bytes=40 * 1024 * 1024)
 SCALAR = pl.BlockSpec(memory_space=pltpu.SMEM)
@@ -55,16 +56,21 @@
     return pl.ds(pl.multiple_of(lax.rem(places[0] + by, SIZE) * size, size), size)
 
 
-def pack_own_kernel(places, s_own, s_far, t_own, t_far, *outs):
+def squares(ref):
+    values = ref[...].astype(F32)
+    return jnp.sum(values * values, axis=1, keepdims=True)
+
+
+def sums_kernel(s_own, t_own, ssq_s, ssq_t):
+    ssq_s[...] = squares(s_own)
+    ssq_t[...] = squares(t_own)
+
+
+def pack_own_kernel(places, s_own, s_far, t_own, t_far, ssq_s, ssq_t, *outs):
     half, wide = s_own.shape[1], t_own.shape[1]
     ts = wide // SIZE
-
-    def inverse(own, far):
-        a, b = own[...].astype(F32), far[...].astype(F32)
-        total = jnp.sum(a * a, axis=1, keepdims=True) + jnp.sum(b * b, axis=1, keepdims=True)
-        return lax.rsqrt(total + 1e-06)
-
-    inv_s, inv_t = inverse(s_own, s_far), inverse(t_own, t_far)
+    inv_s = lax.rsqrt(ssq_s[...] + squares(s_far) + 1e-06)
+    inv_t = lax.rsqrt(ssq_t[...] + squares(t_far) + 1e-06)
     outs[SIZE][...] = inv_s
     outs[SIZE + 1][...] = inv_t
     norm = scaled(s_own[...], inv_s)
@@ -85,7 +91,8 @@
     return pack[:, part(places, 0, ss)], pack[:, pl.ds(half, pack.shape[1] - half)]
 
 
-def gram_kernel(share, native, places, *refs):
+def gram_kernel(share, chunk, places, *refs):
+    native = chunk == 0
     count = SIZE if native else 2 * SIZE
     norms, packs = refs[:SIZE], refs[count - SIZE : count]
     outs, (left, right, product) = refs[count : count + SIZE], refs[count + SIZE :]
@@ -108,17 +115,17 @@
         col = lax.broadcasted_iota(jnp.int32, (ss, ss), 1)
         product[part(places, 0, ss), pl.ds(0, ss)] -= jnp.where(row == col, share, 0.0)
     for by, out in enumerate(outs):
-        which = lax.rem(places[1] + by, SIZE)
+        which = lax.rem(places[1 + chunk] + by, SIZE)
         block = pl.ds(pl.multiple_of(which * ss, ss), ss)
         rest = pl.ds(ss, feats - ss)
         out[:, pl.ds(0, ss)] = product[block, pl.ds(0, ss)].astype(out.dtype)
         out[:, rest] = -product[block, rest].astype(out.dtype)
 
 
-def gather_weights(places, pieces, weights):
+def gather_weights(place, pieces, weights):
     ss = pieces[0].shape[0]
     for by, piece in enumerate(pieces):
-        which = lax.rem(places[1] + SIZE - by, SIZE)
+        which = lax.rem(place + SIZE - by, SIZE)
         weights[pl.ds(pl.multiple_of(which * ss, ss), ss), :] = piece[...]
 
 
@@ -130,7 +137,7 @@
     packs, pieces, (out, left, weights) = refs[:SIZE], refs[SIZE : 2 * SIZE], refs[2 * SIZE :]
     half, feats = weights.shape
     rows, ss = packs[0].shape[0], half // SIZE
-    gather_weights(places, pieces, weights)
+    gather_weights(places[1], pieces, weights)
     for k, pack in enumerate(packs):
         at = pl.ds(k * rows, rows)
         left[at, pl.ds(0, ss)], left[at, pl.ds(ss, feats - ss)] = native_features(
@@ -143,7 +150,7 @@
     packs, pieces, before = refs[:count], refs[count : count + SIZE], refs[count + SIZE]
     outs, weights = refs[count + SIZE + 1 : -1], refs[-1]
     rows = packs[0].shape[0]
-    gather_weights(places, pieces, weights)
+    gather_weights(places[2], pieces, weights)
     for k, (pack, out) in enumerate(zip(packs, outs)):
         sofar = before[pl.ds((first + k) * rows, rows), :]
         out[...] = (times(pack[...], weights[...]) + sofar).astype(out.dtype)
@@ -195,15 +202,24 @@
     ss, ts = half // SIZE, wide // SIZE
     feats = ss + ts
     flops = 2 * SIZE * rows * half * feats
-    places = jnp.stack([place_along(GATHER), place_along(FIRST)]).astype(jnp.int32)
+    places = jnp.stack([place_along(axes) for axes in (GATHER, *FIRST)]).astype(jnp.int32)
 
     t_far, s_far = other_core(teacher), other_core(student)
+    ssq_s, ssq_t = pl.pallas_call(
+        sums_kernel,
+        out_shape=shapes(*[((rows, 1), F32)] * 2),
+        in_specs=[WHOLE] * 2,
+        out_specs=[WHOLE] * 2,
+        compiler_params=PARAMS,
+        cost_estimate=pl.CostEstimate(flops=0, bytes_accessed=1 << 20, transcendentals=0),
+        name="sums",
+    )(student, teacher)
     *near, inv_s, inv_t = strip_call(
         pack_own_kernel,
         "pack_own",
-        (half, half, wide, wide),
+        (half, half, wide, wide, 1, 1),
         shapes(*[((rows, half + ts), BF16)] * SIZE, *[((rows, 1), F32)] * 2),
-    )(places, student, s_far, teacher, t_far)
+    )(places, student, s_far, teacher, t_far, ssq_s, ssq_t)
     far = strip_call(
         pack_far_kernel,
         "pack_far",
@@ -211,12 +227,22 @@
         shapes(*[((rows, feats), BF16)] * SIZE),
     )(places, s_far, t_far, inv_s, inv_t)
     norm_own = near[0][:, :half]
-    near = [near[0]] + [shifted(near[by], GATHER, by) for by in (1, 2, 3)]
-    far = [far[0]] + [shifted(far[by], GATHER, by) for by in (1, 2, 3)]
-
-    def weights_of(native, packs, name):
+
+    def exchanged(own, sent, axis_of_core, sign=1):
+        arrived = {by: shifted(sent(by), axis_of_core, sign * by) for by in ORDER}
+        return [own] + [arrived[by] for by in (1, 2, 3)]
+
+    def added(total, sent, axis_of_core, sign=1):
+        for array in exchanged(None, sent, axis_of_core, sign)[1:]:
+            total = total + array.astype(F32)
+        return total
+
+    near = exchanged(near[0], near.__getitem__, GATHER)
+    far = exchanged(far[0], far.__getitem__, GATHER)
+
+    def weights_of(chunk, packs, name):
         own, *sends = kernel_call(
-            functools.partial(gram_kernel, level * SIZE / groups, native),
+            functools.partial(gram_kernel, level * SIZE / groups, chunk),
             name,
             shapes(((ss, feats), F32), *[((ss, feats), BF16)] * 3),
             len(packs),
@@ -227,17 +253,13 @@
             ],
             flops,
         )(places, *packs)
-        total = own
-        for by in (1, 2, 3):
-            total = total + shifted(sends[by - 1], FIRST, by).astype(F32)
+        total = added(own, lambda by: sends[by - 1], FIRST[chunk])
         shared = total.astype(BF16)
-        for by in (1, 2, 3):
-            total = total + shifted(shared, SECOND, by).astype(F32)
-        piece = total.astype(BF16)
-        return [piece] + [shifted(piece, FIRST, by) for by in (1, 2, 3)]
-
-    near_weights = weights_of(True, near, "gram_native")
-    far_weights = weights_of(False, near + far, "gram_far")
+        piece = added(total, lambda by: shared, SECOND[chunk]).astype(BF16)
+        return exchanged(piece, lambda by: piece, FIRST[chunk])
+
+    near_weights = weights_of(0, near, "gram_native")
+    far_weights = weights_of(1, near + far, "gram_far")
 
     sofar = kernel_call(
         apply_native_kernel,
@@ -265,9 +287,7 @@
     )(places, far[0], *far_weights, sofar)[0]
     norm_f = norm_own.astype(F32)
     grad_n = grad_n + level * norm_f
-    for by in (1, 2, 3):
-        grad_n = grad_n + shifted(parts[by - 1], GATHER, -by).astype(F32)
-    grad_n = coef * grad_n
+    grad_n = coef * added(grad_n, lambda by: parts[by - 1], GATHER, -1)
     inner = jnp.sum(grad_n * norm_f, axis=1)
     inner = inner + other_core(inner)
     return (grad_n - inner[:, None] * norm_f) * inv_s

time: 84.6 us -> 82.1 us (0.970)
  starting transfers between devices: 54.6 us -> 45.4 us
  waiting for transfers between devices: 16 us -> 19.9 us
  local copies, waits for them, and re-layouts: 2.06 us -> 4.12 us
    ppermute x27, waiting for transfers between devices: 12.9 us -> 19.2 us  [shifted(): return lax.ppermute(array, AXES, pairs)]
    ppermute x27, starting transfers between devices: 40.6 us -> 35.3 us  [shifted(): return lax.ppermute(array, AXES, pairs)]
    ppermute x3, starting transfers between devices: 14 us -> 10.1 us  [other_core(): return lax.ppermute(array, 'sec', [(0, 1), (1, 0)])]
    ppermute x3, waiting for transfers between devices: 3.04 us -> 0.72 us  [other_core(): return lax.ppermute(array, 'sec', [(0, 1), (1, 0)])]
    unnamed x4 -> x8, local copies, waits for them, and re-layouts: 2.06 us -> 4.12 us
    pallas_call x3 -> x4, Pallas kernels: 4.78 us -> 5.43 us  [the longest x2 3.19 us: weights_of(): kernel_call(functools.partial(gram_kernel, level * SIZE / groups, chunk),...]
  transfers between devices with their start and end apart: 30 -> 30, of which waited for: 10 -> 13; matrix products, arithmetic and copies ran while one was open for 1% -> 1% of each run, Pallas kernels for 8% -> 9%
where the time goes in v4:
time: 82.1 us; the launch traced here: 81.9 us
  starting transfers between devices  45.4 us (55%)
  waiting for transfers between devices  19.9 us (24%)
  Pallas kernels  10.5 us (13%)
  local copies, waits for them, and re-layouts  4.12 us (5%)
  other arithmetic  1.85 us (2%)
    ppermute x27, starting transfers between devices, shifted(): return lax.ppermute(array, AXES, pairs)  35.3 us
    ppermute x27, waiting for transfers between devices, shifted(): return lax.ppermute(array, AXES, pairs)  19.2 us
    ppermute x3, starting transfers between devices, other_core(): return lax.ppermute(array, 'sec', [(0, 1), (1, 0)])  10.1 us
    unnamed x8, local copies, waits for them, and re-layouts  4.12 us
    pallas_call x2, Pallas kernels, weights_of(): kernel_call(functools.partial(gram_kernel, level * SIZE / groups, chunk),...  3.19 us
    pallas_call x1, Pallas kernels, body(): strip_call(pack_own_kernel, 'pack_own', (half, half, wide, wide, 1, 1), s...  1.97 us
  transfers between devices with their start and end apart: 30, of which 13 were waited for; matrix products, arithmetic and copies ran while one was open for 1% of the time, Pallas kernels for 9%

profile of v4, /device:TPU:1, one launch (start us, length us, event | category | flops | bytes accessed | tf_op | source)
XLA Modules:
  0.0 81.9 jit_solution(4900604371209958785)
XLA Ops:
  0.0 1.4 %collective-permute-start.1 = (bf16[192,2048]{1,0:T(8,128)(2,1)}, bf16[192,2048]{1,0:T(8,128)(2,1)S(1)}, u32[]{:S(2)}, u32[]{:S(2)}) collective-permute-start(bf16[192,2048]{1,0:T(8,128)(2,1)} %t_own.3), channel_id=1, source_target_pairs={{0,1},{1,0},{2,3},{3,2},{4,5},{5,4},{6,7},{7,6},{8,9},{9,8},{10,11... | collective-permute-start | bytes 2359304 | tf_op jit(solution)/shard_map/ppermute | solution.py:42
  1.4 1.1 %copy-done = bf16[192,2048]{1,0:T(8,128)(2,1)S(1)} copy-done((bf16[192,2048]{1,0:T(8,128)(2,1)S(1)}, bf16[192,2048]{1,0:T(8,128)(2,1)}, u32[]{:S(2)}) %copy-start) | copy-done | bytes 786456
  2.6 0.9 %copy-done.2 = bf16[192,512]{1,0:T(8,128)(2,1)S(1)} copy-done((bf16[192,512]{1,0:T(8,128)(2,1)S(1)}, bf16[192,512]{1,0:T(8,128)(2,1)}, u32[]{:S(2)}) %copy-start.2) | copy-done | bytes 196632
  3.8 1.1 %copy-done.1 = bf16[192,2048]{1,0:T(8,128)(2,1)S(1)} copy-done((bf16[192,2048]{1,0:T(8,128)(2,1)S(1)}, bf16[192,2048]{1,0:T(8,128)(2,1)}, u32[]{:S(2)}) %copy-start.1) | copy-done | bytes 786456
  5.0 0.9 %copy-done.3 = bf16[192,512]{1,0:T(8,128)(2,1)S(1)} copy-done((bf16[192,512]{1,0:T(8,128)(2,1)S(1)}, bf16[192,512]{1,0:T(8,128)(2,1)}, u32[]{:S(2)}) %copy-start.3) | copy-done | bytes 196632
  5.9 2.0 %pack_own.1 = (bf16[192,1024]{1,0:T(8,128)(2,1)S(1)}, bf16[192,1024]{1,0:T(8,128)(2,1)S(1)}, bf16[192,1024]{1,0:T(8,128)(2,1)S(1)}, bf16[192,1024]{1,0:T(8,128)(...) custom-call(s32[3]{0:T(128)S(1)} %pad_add_fusion.places, bf16[192,512]{1,0:T(8,128)(2,1)S(1)} %copy-done.3, ...), custom_call_target="tpu_custom_call" | custom-call | bytes 4194304 | tf_op jit(solution)/shard_map/pack_own/pallas_call | solution.py:217
  7.9 1.4 %collective-permute-start.2 = (bf16[192,1024]{1,0:T(8,128)(2,1)S(1)}, bf16[192,1024]{1,0:T(8,128)(2,1)S(1)}, u32[]{:S(2)}, u32[]{:S(2)}) collective-permute-start(bf16[192,1024]{1,0:T(8,128)(2,1)S(1)} %get-tuple-element.34), channel_id=1, source_target_pairs={{0,4},{1,3},{16,20},{17,19},{32,36},{33,35},{48,52},{49,51},{4,8},... | collective-permute-start | bytes 1179656 | tf_op jit(solution)/shard_map/ppermute | solution.py:38
  9.2 2.5 %collective-permute-start.3 = (bf16[192,1024]{1,0:T(8,128)(2,1)S(1)}, bf16[192,1024]{1,0:T(8,128)(2,1)S(1)}, u32[]{:S(2)}, u32[]{:S(2)}) collective-permute-start(bf16[192,1024]{1,0:T(8,128)(2,1)S(1)} %get-tuple-element.35), channel_id=1, source_target_pairs={{0,8},{1,65},{16,24},{17,81},{32,40},{33,97},{48,56},{49,113},{4,1... | collective-permute-start | bytes 1179656 | tf_op jit(solution)/shard_map/ppermute | solution.py:38
  11.7 1.2 %collective-permute-start.4 = (bf16[192,1024]{1,0:T(8,128)(2,1)S(1)}, bf16[192,1024]{1,0:T(8,128)(2,1)S(1)}, u32[]{:S(2)}, u32[]{:S(2)}) collective-permute-start(bf16[192,1024]{1,0:T(8,128)(2,1)S(1)} %get-tuple-element.36), channel_id=1, source_target_pairs={{0,12},{1,67},{16,28},{17,83},{32,44},{33,99},{48,60},{49,115},{4,... | collective-permute-start | bytes 1179656 | tf_op jit(solution)/shard_map/ppermute | solution.py:38
  12.9 1.3 %pack_far.1 = (bf16[192,640]{1,0:T(8,128)(2,1)S(1)}, bf16[192,640]{1,0:T(8,128)(2,1)S(1)}, bf16[192,640]{1,0:T(8,128)(2,1)S(1)}, bf16[192,640]{1,0:T(8,128)(2,1)S(1)}) custom-call(s32[3]{0:T(128)S(1)} %pad_add_fusion.places, bf16[192,512]{1,0:T(8,128)(2,1)S(1)} %collective-permute-done.s_far, bf16[192,2048]{1,0:T(8,128)(2,1)S(1)} %collective-permute-done.1.t_far, ...), custom_call_target="tpu_custom_call" | custom-call | bytes 4194304 | tf_op jit(solution)/shard_map/pack_far/pallas_call | solution.py:223
  14.5 0.9 %collective-permute-start.6 = (bf16[192,640]{1,0:T(8,128)(2,1)S(1)}, bf16[192,640]{1,0:T(8,128)(2,1)S(1)}, u32[]{:S(2)}, u32[]{:S(2)}) collective-permute-start(bf16[192,640]{1,0:T(8,128)(2,1)S(1)} %get-tuple-element.38), channel_id=1, source_target_pairs={{0,8},{1,65},{16,24},{17,81},{32,40},{33,97},{48,56},{49,113},{4,1... | collective-permute-start | bytes 737288 | tf_op jit(solution)/shard_map/ppermute | solution.py:38
  15.4 0.7 collective-permute-done.2.refs_1_
  16.1 1.4 %collective-permute-start.7 = (bf16[192,640]{1,0:T(8,128)(2,1)S(1)}, bf16[192,640]{1,0:T(8,128)(2,1)S(1)}, u32[]{:S(2)}, u32[]{:S(2)}) collective-permute-start(bf16[192,640]{1,0:T(8,128)(2,1)S(1)} %get-tuple-element.39), channel_id=1, source_target_pairs={{0,12},{1,67},{16,28},{17,83},{32,44},{33,99},{48,60},{49,115},{4,... | collective-permute-start | bytes 737288 | tf_op jit(solution)/shard_map/ppermute | solution.py:38
  17.4 4.0 %collective-permute-done.3.refs_2_ = bf16[192,1024]{1,0:T(8,128)(2,1)S(1)} collective-permute-done((bf16[192,1024]{1,0:T(8,128)(2,1)S(1)}, bf16[192,1024]{1,0:T(8,128)(2,1)S(1)}, u32[]{:S(2)}, u32[]{:S(2)}) %collective-permute-start.3) | collective-permute-done | bytes 393248 | tf_op jit(solution)/shard_map/ppermute | solution.py:38
  21.4 1.6 %gram_native.1 = (f32[128,640]{1,0:T(8,128)S(1)}, bf16[128,640]{1,0:T(8,128)(2,1)S(1)}, bf16[128,640]{1,0:T(8,128)(2,1)S(1)}, bf16[128,640]{1,0:T(8,128)(2,1)S(1)}) custom-call(s32[3]{0:T(128)S(1)} %pad_add_fusion.places, bf16[192,1024]{1,0:T(8,128)(2,1)S(1)} %get-tuple-element.33.refs_0_, bf16[192,1024]{1,0:T(8,128)(2,1)S(1)} %collective-permute-done.2.refs_1_, ...), custom_call_target="tpu_custom_call" | custom-call | flops 503316480 | bytes 4194304 | tf_op jit(solution)/shard_map/gram_native/pallas_call | solution.py:244
  23.0 1.7 %collective-permute-start.17 = (bf16[128,640]{1,0:T(8,128)(2,1)S(1)}, bf16[128,640]{1,0:T(8,128)(2,1)S(1)}, u32[]{:S(2)}, u32[]{:S(2)}) collective-permute-start(bf16[128,640]{1,0:T(8,128)(2,1)S(1)} %get-tuple-element.45), channel_id=1, source_target_pairs={{0,16},{1,17},{16,32},{17,33},{32,48},{33,49},{48,0},{49,1},{4,20}... | collective-permute-start | bytes 491528 | tf_op jit(solution)/shard_map/ppermute | solution.py:38
  24.7 3.3 %collective-permute-start.18 = (bf16[128,640]{1,0:T(8,128)(2,1)S(1)}, bf16[128,640]{1,0:T(8,128)(2,1)S(1)}, u32[]{:S(2)}, u32[]{:S(2)}) collective-permute-start(bf16[128,640]{1,0:T(8,128)(2,1)S(1)} %get-tuple-element.46), channel_id=1, source_target_pairs={{0,32},{1,33},{16,48},{17,49},{32,0},{33,1},{48,16},{49,17},{4,36}... | collective-permute-start | bytes 491528 | tf_op jit(solution)/shard_map/ppermute | solution.py:38
  28.1 0.7 collective-permute-start.19
  28.8 1.6 %gram_far.1 = (f32[128,640]{1,0:T(8,128)S(1)}, bf16[128,640]{1,0:T(8,128)(2,1)S(1)}, bf16[128,640]{1,0:T(8,128)(2,1)S(1)}, bf16[128,640]{1,0:T(8,128)(2,1)S(1)}) custom-call(s32[3]{0:T(128)S(1)} %pad_add_fusion.places, bf16[192,1024]{1,0:T(8,128)(2,1)S(1)} %get-tuple-element.33.refs_0_, bf16[192,1024]{1,0:T(8,128)(2,1)S(1)} %collective-permute-done.2.refs_1_, ...), custom_call_target="tpu_custom_call" | custom-call | flops 503316480 | bytes 4194304 | tf_op jit(solution)/shard_map/gram_far/pallas_call | solution.py:244
  30.4 2.6 %collective-permute-start.10 = (bf16[128,640]{1,0:T(8,128)(2,1)S(1)}, bf16[128,640]{1,0:T(8,128)(2,1)S(1)}, u32[]{:S(2)}, u32[]{:S(2)}) collective-permute-start(bf16[128,640]{1,0:T(8,128)(2,1)S(1)} %get-tuple-element.43), channel_id=1, source_target_pairs={{0,66},{1,13},{16,82},{17,29},{32,98},{33,45},{48,114},{49,61},{4,... | collective-permute-start | bytes 491528 | tf_op jit(solution)/shard_map/ppermute | solution.py:38
  33.0 1.6 %collective-permute-start.9 = (bf16[128,640]{1,0:T(8,128)(2,1)S(1)}, bf16[128,640]{1,0:T(8,128)(2,1)S(1)}, u32[]{:S(2)}, u32[]{:S(2)}) collective-permute-start(bf16[128,640]{1,0:T(8,128)(2,1)S(1)} %get-tuple-element.42), channel_id=1, source_target_pairs={{0,64},{1,9},{16,80},{17,25},{32,96},{33,41},{48,112},{49,57},{4,6... | collective-permute-start | bytes 491528 | tf_op jit(solution)/shard_map/ppermute | solution.py:38
  34.7 1.7 %collective-permute-start.20 = (bf16[128,640]{1,0:T(8,128)(2,1)S(1)}, bf16[128,640]{1,0:T(8,128)(2,1)S(1)}, u32[]{:S(2)}, u32[]{:S(2)}) collective-permute-start(bf16[128,640]{1,0:T(8,128)(2,1)S(1)} %fusion.9), channel_id=1, source_target_pairs={{0,2},{1,5},{16,18},{17,21},{32,34},{33,37},{48,50},{49,53},{4,6},... | collective-permute-start | bytes 491528 | tf_op jit(solution)/shard_map/ppermute | solution.py:38
  36.4 2.2 %collective-permute-start.21 = (bf16[128,640]{1,0:T(8,128)(2,1)S(1)}, bf16[128,640]{1,0:T(8,128)(2,1)S(1)}, u32[]{:S(2)}, u32[]{:S(2)}) collective-permute-start(bf16[128,640]{1,0:T(8,128)(2,1)S(1)} %fusion.9), channel_id=1, source_target_pairs={{0,64},{1,9},{16,80},{17,25},{32,96},{33,41},{48,112},{49,57},{4,6... | collective-permute-start | bytes 491528 | tf_op jit(solution)/shard_map/ppermute | solution.py:38
  38.6 0.6 collective-permute-start.22
  39.2 1.2 %collective-permute-done.8 = bf16[128,640]{1,0:T(8,128)(2,1)S(1)} collective-permute-done((bf16[128,640]{1,0:T(8,128)(2,1)S(1)}, bf16[128,640]{1,0:T(8,128)(2,1)S(1)}, u32[]{:S(2)}, u32[]{:S(2)}) %collective-permute-start.8) | collective-permute-done | bytes 163872 | tf_op jit(solution)/shard_map/ppermute | solution.py:38
  40.5 1.3 %collective-permute-start.11 = (bf16[128,640]{1,0:T(8,128)(2,1)S(1)}, bf16[128,640]{1,0:T(8,128)(2,1)S(1)}, u32[]{:S(2)}, u32[]{:S(2)}) collective-permute-start(bf16[128,640]{1,0:T(8,128)(2,1)S(1)} %fusion.8), channel_id=1, source_target_pairs={{0,16},{1,17},{16,32},{17,33},{32,48},{33,49},{48,0},{49,1},{4,20}... | collective-permute-start | bytes 491528 | tf_op jit(solution)/shard_map/ppermute | solution.py:38
  41.8 1.5 %collective-permute-start.12 = (bf16[128,640]{1,0:T(8,128)(2,1)S(1)}, bf16[128,640]{1,0:T(8,128)(2,1)S(1)}, u32[]{:S(2)}, u32[]{:S(2)}) collective-permute-start(bf16[128,640]{1,0:T(8,128)(2,1)S(1)} %fusion.8), channel_id=1, source_target_pairs={{0,32},{1,33},{16,48},{17,49},{32,0},{33,1},{48,16},{49,17},{4,36}... | collective-permute-start | bytes 491528 | tf_op jit(solution)/shard_map/ppermute | solution.py:38
  43.3 0.6 collective-permute-done.20
  44.5 1.1 %collective-permute-start.23 = (bf16[128,640]{1,0:T(8,128)(2,1)S(1)}, bf16[128,640]{1,0:T(8,128)(2,1)S(1)}, u32[]{:S(2)}, u32[]{:S(2)}) collective-permute-start(bf16[128,640]{1,0:T(8,128)(2,1)S(1)} %add_convert_fusion.refs_4_), channel_id=1, source_target_pairs={{0,16},{1,17},{16,32},{17,33},{32,48},{33,49},{48,0},{49,1},{4,20}... | collective-permute-start | bytes 491528 | tf_op jit(solution)/shard_map/ppermute | solution.py:38
  45.6 1.7 %collective-permute-start.24 = (bf16[128,640]{1,0:T(8,128)(2,1)S(1)}, bf16[128,640]{1,0:T(8,128)(2,1)S(1)}, u32[]{:S(2)}, u32[]{:S(2)}) collective-permute-start(bf16[128,640]{1,0:T(8,128)(2,1)S(1)} %add_convert_fusion.refs_4_), channel_id=1, source_target_pairs={{0,32},{1,33},{16,48},{17,49},{32,0},{33,1},{48,16},{49,17},{4,36}... | collective-permute-start | bytes 491528 | tf_op jit(solution)/shard_map/ppermute | solution.py:38
  47.3 0.8 collective-permute-start.25
  48.7 0.5 collective-permute-start.14
  49.3 2.2 %collective-permute-start.15 = (bf16[128,640]{1,0:T(8,128)(2,1)S(1)}, bf16[128,640]{1,0:T(8,128)(2,1)S(1)}, u32[]{:S(2)}, u32[]{:S(2)}) collective-permute-start(bf16[128,640]{1,0:T(8,128)(2,1)S(1)} %add_convert_fusion.1.refs_1_.refs_3_), channel_id=1, source_target_pairs={{0,64},{1,9},{16,80},{17,25},{32,96},{33,41},{48,112},{49,57},{4,6... | collective-permute-start | bytes 491528 | tf_op jit(solution)/shard_map/ppermute | solution.py:38
  51.5 3.8 %collective-permute-done.23.refs_5_ = bf16[128,640]{1,0:T(8,128)(2,1)S(1)} collective-permute-done((bf16[128,640]{1,0:T(8,128)(2,1)S(1)}, bf16[128,640]{1,0:T(8,128)(2,1)S(1)}, u32[]{:S(2)}, u32[]{:S(2)}) %collective-permute-start.23) | collective-permute-done | bytes 163872 | tf_op jit(solution)/shard_map/ppermute | solution.py:38
  55.3 0.5 collective-permute-done.25.refs_7_
  55.9 1.4 %apply_native.1.refs_5_.refs_7_ = f32[768,512]{1,0:T(8,128)S(1)} custom-call(s32[3]{0:T(128)S(1)} %pad_add_fusion.places, bf16[192,1024]{1,0:T(8,128)(2,1)S(1)} %get-tuple-element.33.refs_0_, bf16[192,1024]{1,0:T(8,128)(2,1)S(1)} %collective-permute-done.2.refs_1_, bf16[192,1024]{1,0:T(8,128)(2,1)S(1)} %collective-permute-done.3.refs_2_, ...), custom_call_target="tpu_custom_call" | custom-call | flops 503316480 | bytes 4194304 | tf_op jit(solution)/shard_map/apply_native/pallas_call | solution.py:264
  57.3 2.4 %collective-permute-done.16.refs_4_.refs_6_ = bf16[128,640]{1,0:T(8,128)(2,1)S(1)} collective-permute-done((bf16[128,640]{1,0:T(8,128)(2,1)S(1)}, bf16[128,640]{1,0:T(8,128)(2,1)S(1)}, u32[]{:S(2)}, u32[]{:S(2)}) %collective-permute-start.16) | collective-permute-done | bytes 163872 | tf_op jit(solution)/shard_map/ppermute | solution.py:38
  59.7 1.4 %apply_sent.1 = (bf16[192,512]{1,0:T(8,128)(2,1)S(1)}, bf16[192,512]{1,0:T(8,128)(2,1)S(1)}, bf16[192,512]{1,0:T(8,128)(2,1)S(1)}) custom-call(s32[3]{0:T(128)S(1)} %pad_add_fusion.places, bf16[192,640]{1,0:T(8,128)(2,1)S(1)} %collective-permute-done.5.refs_5_.refs_0_, bf16[192,640]{1,0:T(8,128)(2,1)S(1)} %collective-permute-done.6.refs_6_.refs_1_, ...), custom_call_target="tpu_custom_call" | custom-call | flops 377487360 | bytes 4194304 | tf_op jit(solution)/shard_map/apply_sent/pallas_call | solution.py:272
  61.1 2.0 %collective-permute-start.26 = (bf16[192,512]{1,0:T(8,128)(2,1)S(1)}, bf16[192,512]{1,0:T(8,128)(2,1)S(1)}, u32[]{:S(2)}, u32[]{:S(2)}) collective-permute-start(bf16[192,512]{1,0:T(8,128)(2,1)S(1)} %get-tuple-element.48), channel_id=1, source_target_pairs={{0,12},{1,67},{16,28},{17,83},{32,44},{33,99},{48,60},{49,115},{4,... | collective-permute-start | bytes 589832 | tf_op jit(solution)/shard_map/ppermute | solution.py:38
  63.1 0.9 %collective-permute-start.27 = (bf16[192,512]{1,0:T(8,128)(2,1)S(1)}, bf16[192,512]{1,0:T(8,128)(2,1)S(1)}, u32[]{:S(2)}, u32[]{:S(2)}) collective-permute-start(bf16[192,512]{1,0:T(8,128)(2,1)S(1)} %get-tuple-element.49), channel_id=1, source_target_pairs={{0,8},{1,65},{16,24},{17,81},{32,40},{33,97},{48,56},{49,113},{4,1... | collective-permute-start | bytes 589832 | tf_op jit(solution)/shard_map/ppermute | solution.py:38
  64.1 0.8 collective-permute-start.28
  64.8 1.0 %apply_kept.1 = f32[192,512]{1,0:T(8,128)S(1)} custom-call(s32[3]{0:T(128)S(1)} %pad_add_fusion.places, bf16[192,640]{1,0:T(8,128)(2,1)S(1)} %get-tuple-element.32.refs_4_.refs_0_, bf16[128,640]{1,0:T(8,128)(2,1)S(1)} %add_convert_fusion.1.refs_1_.refs_3_, bf16[128,640]{1,0:T(8,128)(2,1)S(1)} %collective-permute-done.14.refs_2_.refs_4_, ...), custom_call_target="tpu_custom_call" | custom-call | flops 125829120 | bytes 4194304 | tf_op jit(solution)/shard_map/apply_kept/pallas_call | solution.py:280
  65.8 1.5 %collective-permute-done.26 = bf16[192,512]{1,0:T(8,128)(2,1)S(1)} collective-permute-done((bf16[192,512]{1,0:T(8,128)(2,1)S(1)}, bf16[192,512]{1,0:T(8,128)(2,1)S(1)}, u32[]{:S(2)}, u32[]{:S(2)}) %collective-permute-start.26) | collective-permute-done | bytes 196640 | tf_op jit(solution)/shard_map/ppermute | solution.py:38
  67.3 1.9 %collective-permute-done.27 = bf16[192,512]{1,0:T(8,128)(2,1)S(1)} collective-permute-done((bf16[192,512]{1,0:T(8,128)(2,1)S(1)}, bf16[192,512]{1,0:T(8,128)(2,1)S(1)}, u32[]{:S(2)}, u32[]{:S(2)}) %collective-permute-start.27) | collective-permute-done | bytes 196640 | tf_op jit(solution)/shard_map/ppermute | solution.py:38
  69.2 2.0 %collective-permute-done.28 = bf16[192,512]{1,0:T(8,128)(2,1)S(1)} collective-permute-done((bf16[192,512]{1,0:T(8,128)(2,1)S(1)}, bf16[192,512]{1,0:T(8,128)(2,1)S(1)}, u32[]{:S(2)}, u32[]{:S(2)}) %collective-permute-start.28) | collective-permute-done | bytes 196640 | tf_op jit(solution)/shard_map/ppermute | solution.py:38
  71.5 8.6 %collective-permute-start.29 = (f32[192]{0:T(256)S(1)}, f32[192]{0:T(256)S(1)}, u32[]{:S(2)}, u32[]{:S(2)}) collective-permute-start(f32[192]{0:T(256)S(1)} %fusion.5), channel_id=1, source_target_pairs={{0,1},{1,0},{2,3},{3,2},{4,5},{5,4},{6,7},{7,6},{8,9},{9,8},{10,11... | collective-permute-start | bytes 2312 | tf_op jit(solution)/shard_map/ppermute | solution.py:42
  80.2 0.7 collective-permute-done.29
  81.0 0.9 %fusion.7 = f32[192,512]{1,0:T(8,128)} fusion(f32[192]{0:T(256)S(1)} %reduce, f32[192]{0:T(256)S(1)} %add.84, bf16[192,1024]{1,0:T(8,128)(2,1)S(1)} %get-tuple-element.33.refs_0_, bf16[192,512]{1,0:T(8,128)(2,1)S(1)} %collective-permute-done.28, bf16[192,512]{1,0:T(8,128)(2,1)S(1)} %collective-permute-done.27, ...), kind=kLoop, calls=%fused_computation.10 | loop fusion | flops 1277952 | bytes 1574400 | tf_op jit(solution)/shard_map/mul | solution.py:293
  (37 shorter events, 2.6 us)
Async XLA Ops:
  0.0 3.8 %collective-permute-start.1 = (bf16[192,2048]{1,0:T(8,128)(2,1)}, bf16[192,2048]{1,0:T(8,128)(2,1)S(1)}, u32[]{:S(2)}, u32[]{:S(2)}) collective-permute-start(bf16[192,2048]{1,0:T(8,128)(2,1)} %t_own.3), channel_id=1, source_target_pairs={{0,1},{1,0},{2,3},{3,2},{4,5},{5,4},{6,7},{7,6},{8,9},{9,8},{10,11... | collective-permute-start | bytes 2359304 | tf_op jit(solution)/shard_map/ppermute | solution.py:42
  1.4 2.4 %collective-permute-start = (bf16[192,512]{1,0:T(8,128)(2,1)}, bf16[192,512]{1,0:T(8,128)(2,1)S(1)}, u32[]{:S(2)}, u32[]{:S(2)}) collective-permute-start(bf16[192,512]{1,0:T(8,128)(2,1)} %s_own.3), channel_id=1, source_target_pairs={{0,1},{1,0},{2,3},{3,2},{4,5},{5,4},{6,7},{7,6},{8,9},{9,8},{10,11... | collective-permute-start | bytes 589832 | tf_op jit(solution)/shard_map/ppermute | solution.py:42
  1.4 1.1 %copy-start = (bf16[192,2048]{1,0:T(8,128)(2,1)S(1)}, bf16[192,2048]{1,0:T(8,128)(2,1)}, u32[]{:S(2)}) copy-start(bf16[192,2048]{1,0:T(8,128)(2,1)} %t_own.3) | copy-start | bytes 2359300
  2.6 0.9 %copy-start.2 = (bf16[192,512]{1,0:T(8,128)(2,1)S(1)}, bf16[192,512]{1,0:T(8,128)(2,1)}, u32[]{:S(2)}) copy-start(bf16[192,512]{1,0:T(8,128)(2,1)} %s_own.3) | copy-start | bytes 589828
  3.8 1.1 %copy-start.1 = (bf16[192,2048]{1,0:T(8,128)(2,1)S(1)}, bf16[192,2048]{1,0:T(8,128)(2,1)}, u32[]{:S(2)}) copy-start(bf16[192,2048]{1,0:T(8,128)(2,1)} %t_own.3) | copy-start | bytes 2359300
  5.0 0.9 %copy-start.3 = (bf16[192,512]{1,0:T(8,128)(2,1)S(1)}, bf16[192,512]{1,0:T(8,128)(2,1)}, u32[]{:S(2)}) copy-start(bf16[192,512]{1,0:T(8,128)(2,1)} %s_own.3) | copy-start | bytes 589828
  7.9 8.2 %collective-permute-start.2 = (bf16[192,1024]{1,0:T(8,128)(2,1)S(1)}, bf16[192,1024]{1,0:T(8,128)(2,1)S(1)}, u32[]{:S(2)}, u32[]{:S(2)}) collective-permute-start(bf16[192,1024]{1,0:T(8,128)(2,1)S(1)} %get-tuple-element.34), channel_id=1, source_target_pairs={{0,4},{1,3},{16,20},{17,19},{32,36},{33,35},{48,52},{49,51},{4,8},... | collective-permute-start | bytes 1179656 | tf_op jit(solution)/shard_map/ppermute | solution.py:38
  9.2 12.2 %collective-permute-start.3 = (bf16[192,1024]{1,0:T(8,128)(2,1)S(1)}, bf16[192,1024]{1,0:T(8,128)(2,1)S(1)}, u32[]{:S(2)}, u32[]{:S(2)}) collective-permute-start(bf16[192,1024]{1,0:T(8,128)(2,1)S(1)} %get-tuple-element.35), channel_id=1, source_target_pairs={{0,8},{1,65},{16,24},{17,81},{32,40},{33,97},{48,56},{49,113},{4,1... | collective-permute-start | bytes 1179656 | tf_op jit(solution)/shard_map/ppermute | solution.py:38
  11.7 9.7 %collective-permute-start.4 = (bf16[192,1024]{1,0:T(8,128)(2,1)S(1)}, bf16[192,1024]{1,0:T(8,128)(2,1)S(1)}, u32[]{:S(2)}, u32[]{:S(2)}) collective-permute-start(bf16[192,1024]{1,0:T(8,128)(2,1)S(1)} %get-tuple-element.36), channel_id=1, source_target_pairs={{0,12},{1,67},{16,28},{17,83},{32,44},{33,99},{48,60},{49,115},{4,... | collective-permute-start | bytes 1179656 | tf_op jit(solution)/shard_map/ppermute | solution.py:38
  14.1 13.9 %collective-permute-start.5 = (bf16[192,640]{1,0:T(8,128)(2,1)S(1)}, bf16[192,640]{1,0:T(8,128)(2,1)S(1)}, u32[]{:S(2)}, u32[]{:S(2)}) collective-permute-start(bf16[192,640]{1,0:T(8,128)(2,1)S(1)} %get-tuple-element.37), channel_id=1, source_target_pairs={{0,4},{1,3},{16,20},{17,19},{32,36},{33,35},{48,52},{49,51},{4,8},... | collective-permute-start | bytes 737288 | tf_op jit(solution)/shard_map/ppermute | solution.py:38
  14.5 14.3 %collective-permute-start.6 = (bf16[192,640]{1,0:T(8,128)(2,1)S(1)}, bf16[192,640]{1,0:T(8,128)(2,1)S(1)}, u32[]{:S(2)}, u32[]{:S(2)}) collective-permute-start(bf16[192,640]{1,0:T(8,128)(2,1)S(1)} %get-tuple-element.38), channel_id=1, source_target_pairs={{0,8},{1,65},{16,24},{17,81},{32,40},{33,97},{48,56},{49,113},{4,1... | collective-permute-start | bytes 737288 | tf_op jit(solution)/shard_map/ppermute | solution.py:38
  16.1 12.7 %collective-permute-start.7 = (bf16[192,640]{1,0:T(8,128)(2,1)S(1)}, bf16[192,640]{1,0:T(8,128)(2,1)S(1)}, u32[]{:S(2)}, u32[]{:S(2)}) collective-permute-start(bf16[192,640]{1,0:T(8,128)(2,1)S(1)} %get-tuple-element.39), channel_id=1, source_target_pairs={{0,12},{1,67},{16,28},{17,83},{32,44},{33,99},{48,60},{49,115},{4,... | collective-permute-start | bytes 737288 | tf_op jit(solution)/shard_map/ppermute | solution.py:38
  23.0 9.9 %collective-permute-start.17 = (bf16[128,640]{1,0:T(8,128)(2,1)S(1)}, bf16[128,640]{1,0:T(8,128)(2,1)S(1)}, u32[]{:S(2)}, u32[]{:S(2)}) collective-permute-start(bf16[128,640]{1,0:T(8,128)(2,1)S(1)} %get-tuple-element.45), channel_id=1, source_target_pairs={{0,16},{1,17},{16,32},{17,33},{32,48},{33,49},{48,0},{49,1},{4,20}... | collective-permute-start | bytes 491528 | tf_op jit(solution)/shard_map/ppermute | solution.py:38
  24.7 9.9 %collective-permute-start.18 = (bf16[128,640]{1,0:T(8,128)(2,1)S(1)}, bf16[128,640]{1,0:T(8,128)(2,1)S(1)}, u32[]{:S(2)}, u32[]{:S(2)}) collective-permute-start(bf16[128,640]{1,0:T(8,128)(2,1)S(1)} %get-tuple-element.46), channel_id=1, source_target_pairs={{0,32},{1,33},{16,48},{17,49},{32,0},{33,1},{48,16},{49,17},{4,36}... | collective-permute-start | bytes 491528 | tf_op jit(solution)/shard_map/ppermute | solution.py:38
  28.1 6.6 %collective-permute-start.19 = (bf16[128,640]{1,0:T(8,128)(2,1)S(1)}, bf16[128,640]{1,0:T(8,128)(2,1)S(1)}, u32[]{:S(2)}, u32[]{:S(2)}) collective-permute-start(bf16[128,640]{1,0:T(8,128)(2,1)S(1)} %get-tuple-element.47), channel_id=1, source_target_pairs={{0,48},{1,49},{16,0},{17,1},{32,16},{33,17},{48,32},{49,33},{4,52}... | collective-permute-start | bytes 491528 | tf_op jit(solution)/shard_map/ppermute | solution.py:38
  30.4 8.2 %collective-permute-start.10 = (bf16[128,640]{1,0:T(8,128)(2,1)S(1)}, bf16[128,640]{1,0:T(8,128)(2,1)S(1)}, u32[]{:S(2)}, u32[]{:S(2)}) collective-permute-start(bf16[128,640]{1,0:T(8,128)(2,1)S(1)} %get-tuple-element.43), channel_id=1, source_target_pairs={{0,66},{1,13},{16,82},{17,29},{32,98},{33,45},{48,114},{49,61},{4,... | collective-permute-start | bytes 491528 | tf_op jit(solution)/shard_map/ppermute | solution.py:38
  33.0 7.4 %collective-permute-start.8 = (bf16[128,640]{1,0:T(8,128)(2,1)S(1)}, bf16[128,640]{1,0:T(8,128)(2,1)S(1)}, u32[]{:S(2)}, u32[]{:S(2)}) collective-permute-start(bf16[128,640]{1,0:T(8,128)(2,1)S(1)} %get-tuple-element.41), channel_id=1, source_target_pairs={{0,2},{1,5},{16,18},{17,21},{32,34},{33,37},{48,50},{49,53},{4,6},... | collective-permute-start | bytes 491528 | tf_op jit(solution)/shard_map/ppermute | solution.py:38
  33.0 7.4 %collective-permute-start.9 = (bf16[128,640]{1,0:T(8,128)(2,1)S(1)}, bf16[128,640]{1,0:T(8,128)(2,1)S(1)}, u32[]{:S(2)}, u32[]{:S(2)}) collective-permute-start(bf16[128,640]{1,0:T(8,128)(2,1)S(1)} %get-tuple-element.42), channel_id=1, source_target_pairs={{0,64},{1,9},{16,80},{17,25},{32,96},{33,41},{48,112},{49,57},{4,6... | collective-permute-start | bytes 491528 | tf_op jit(solution)/shard_map/ppermute | solution.py:38
  34.7 9.2 %collective-permute-start.20 = (bf16[128,640]{1,0:T(8,128)(2,1)S(1)}, bf16[128,640]{1,0:T(8,128)(2,1)S(1)}, u32[]{:S(2)}, u32[]{:S(2)}) collective-permute-start(bf16[128,640]{1,0:T(8,128)(2,1)S(1)} %fusion.9), channel_id=1, source_target_pairs={{0,2},{1,5},{16,18},{17,21},{32,34},{33,37},{48,50},{49,53},{4,6},... | collective-permute-start | bytes 491528 | tf_op jit(solution)/shard_map/ppermute | solution.py:38
  36.4 7.9 %collective-permute-start.21 = (bf16[128,640]{1,0:T(8,128)(2,1)S(1)}, bf16[128,640]{1,0:T(8,128)(2,1)S(1)}, u32[]{:S(2)}, u32[]{:S(2)}) collective-permute-start(bf16[128,640]{1,0:T(8,128)(2,1)S(1)} %fusion.9), channel_id=1, source_target_pairs={{0,64},{1,9},{16,80},{17,25},{32,96},{33,41},{48,112},{49,57},{4,6... | collective-permute-start | bytes 491528 | tf_op jit(solution)/shard_map/ppermute | solution.py:38
  38.6 5.7 %collective-permute-start.22 = (bf16[128,640]{1,0:T(8,128)(2,1)S(1)}, bf16[128,640]{1,0:T(8,128)(2,1)S(1)}, u32[]{:S(2)}, u32[]{:S(2)}) collective-permute-start(bf16[128,640]{1,0:T(8,128)(2,1)S(1)} %fusion.9), channel_id=1, source_target_pairs={{0,66},{1,13},{16,82},{17,29},{32,98},{33,45},{48,114},{49,61},{4,... | collective-permute-start | bytes 491528 | tf_op jit(solution)/shard_map/ppermute | solution.py:38
  40.5 6.9 %collective-permute-start.11 = (bf16[128,640]{1,0:T(8,128)(2,1)S(1)}, bf16[128,640]{1,0:T(8,128)(2,1)S(1)}, u32[]{:S(2)}, u32[]{:S(2)}) collective-permute-start(bf16[128,640]{1,0:T(8,128)(2,1)S(1)} %fusion.8), channel_id=1, source_target_pairs={{0,16},{1,17},{16,32},{17,33},{32,48},{33,49},{48,0},{49,1},{4,20}... | collective-permute-start | bytes 491528 | tf_op jit(solution)/shard_map/ppermute | solution.py:38
  41.8 6.3 %collective-permute-start.12 = (bf16[128,640]{1,0:T(8,128)(2,1)S(1)}, bf16[128,640]{1,0:T(8,128)(2,1)S(1)}, u32[]{:S(2)}, u32[]{:S(2)}) collective-permute-start(bf16[128,640]{1,0:T(8,128)(2,1)S(1)} %fusion.8), channel_id=1, source_target_pairs={{0,32},{1,33},{16,48},{17,49},{32,0},{33,1},{48,16},{49,17},{4,36}... | collective-permute-start | bytes 491528 | tf_op jit(solution)/shard_map/ppermute | solution.py:38
  43.9 4.7 %collective-permute-start.13 = (bf16[128,640]{1,0:T(8,128)(2,1)S(1)}, bf16[128,640]{1,0:T(8,128)(2,1)S(1)}, u32[]{:S(2)}, u32[]{:S(2)}) collective-permute-start(bf16[128,640]{1,0:T(8,128)(2,1)S(1)} %fusion.8), channel_id=1, source_target_pairs={{0,48},{1,49},{16,0},{17,1},{32,16},{33,17},{48,32},{49,33},{4,52}... | collective-permute-start | bytes 491528 | tf_op jit(solution)/shard_map/ppermute | solution.py:38
  44.5 10.7 %collective-permute-start.23 = (bf16[128,640]{1,0:T(8,128)(2,1)S(1)}, bf16[128,640]{1,0:T(8,128)(2,1)S(1)}, u32[]{:S(2)}, u32[]{:S(2)}) collective-permute-start(bf16[128,640]{1,0:T(8,128)(2,1)S(1)} %add_convert_fusion.refs_4_), channel_id=1, source_target_pairs={{0,16},{1,17},{16,32},{17,33},{32,48},{33,49},{48,0},{49,1},{4,20}... | collective-permute-start | bytes 491528 | tf_op jit(solution)/shard_map/ppermute | solution.py:38
  45.6 9.7 %collective-permute-start.24 = (bf16[128,640]{1,0:T(8,128)(2,1)S(1)}, bf16[128,640]{1,0:T(8,128)(2,1)S(1)}, u32[]{:S(2)}, u32[]{:S(2)}) collective-permute-start(bf16[128,640]{1,0:T(8,128)(2,1)S(1)} %add_convert_fusion.refs_4_), channel_id=1, source_target_pairs={{0,32},{1,33},{16,48},{17,49},{32,0},{33,1},{48,16},{49,17},{4,36}... | collective-permute-start | bytes 491528 | tf_op jit(solution)/shard_map/ppermute | solution.py:38
  47.3 8.5 %collective-permute-start.25 = (bf16[128,640]{1,0:T(8,128)(2,1)S(1)}, bf16[128,640]{1,0:T(8,128)(2,1)S(1)}, u32[]{:S(2)}, u32[]{:S(2)}) collective-permute-start(bf16[128,640]{1,0:T(8,128)(2,1)S(1)} %add_convert_fusion.refs_4_), channel_id=1, source_target_pairs={{0,48},{1,49},{16,0},{17,1},{32,16},{33,17},{48,32},{49,33},{4,52}... | collective-permute-start | bytes 491528 | tf_op jit(solution)/shard_map/ppermute | solution.py:38
  48.7 8.6 %collective-permute-start.14 = (bf16[128,640]{1,0:T(8,128)(2,1)S(1)}, bf16[128,640]{1,0:T(8,128)(2,1)S(1)}, u32[]{:S(2)}, u32[]{:S(2)}) collective-permute-start(bf16[128,640]{1,0:T(8,128)(2,1)S(1)} %add_convert_fusion.1.refs_1_.refs_3_), channel_id=1, source_target_pairs={{0,2},{1,5},{16,18},{17,21},{32,34},{33,37},{48,50},{49,53},{4,6},... | collective-permute-start | bytes 491528 | tf_op jit(solution)/shard_map/ppermute | solution.py:38
  49.3 8.0 %collective-permute-start.15 = (bf16[128,640]{1,0:T(8,128)(2,1)S(1)}, bf16[128,640]{1,0:T(8,128)(2,1)S(1)}, u32[]{:S(2)}, u32[]{:S(2)}) collective-permute-start(bf16[128,640]{1,0:T(8,128)(2,1)S(1)} %add_convert_fusion.1.refs_1_.refs_3_), channel_id=1, source_target_pairs={{0,64},{1,9},{16,80},{17,25},{32,96},{33,41},{48,112},{49,57},{4,6... | collective-permute-start | bytes 491528 | tf_op jit(solution)/shard_map/ppermute | solution.py:38
  55.2 4.5 %collective-permute-start.16 = (bf16[128,640]{1,0:T(8,128)(2,1)S(1)}, bf16[128,640]{1,0:T(8,128)(2,1)S(1)}, u32[]{:S(2)}, u32[]{:S(2)}) collective-permute-start(bf16[128,640]{1,0:T(8,128)(2,1)S(1)} %add_convert_fusion.1.refs_1_.refs_3_), channel_id=1, source_target_pairs={{0,66},{1,13},{16,82},{17,29},{32,98},{33,45},{48,114},{49,61},{4,... | collective-permute-start | bytes 491528 | tf_op jit(solution)/shard_map/ppermute | solution.py:38
  61.1 6.2 %collective-permute-start.26 = (bf16[192,512]{1,0:T(8,128)(2,1)S(1)}, bf16[192,512]{1,0:T(8,128)(2,1)S(1)}, u32[]{:S(2)}, u32[]{:S(2)}) collective-permute-start(bf16[192,512]{1,0:T(8,128)(2,1)S(1)} %get-tuple-element.48), channel_id=1, source_target_pairs={{0,12},{1,67},{16,28},{17,83},{32,44},{33,99},{48,60},{49,115},{4,... | collective-permute-start | bytes 589832 | tf_op jit(solution)/shard_map/ppermute | solution.py:38
  63.1 6.1 %collective-permute-start.27 = (bf16[192,512]{1,0:T(8,128)(2,1)S(1)}, bf16[192,512]{1,0:T(8,128)(2,1)S(1)}, u32[]{:S(2)}, u32[]{:S(2)}) collective-permute-start(bf16[192,512]{1,0:T(8,128)(2,1)S(1)} %get-tuple-element.49), channel_id=1, source_target_pairs={{0,8},{1,65},{16,24},{17,81},{32,40},{33,97},{48,56},{49,113},{4,1... | collective-permute-start | bytes 589832 | tf_op jit(solution)/shard_map/ppermute | solution.py:38
  64.1 7.2 %collective-permute-start.28 = (bf16[192,512]{1,0:T(8,128)(2,1)S(1)}, bf16[192,512]{1,0:T(8,128)(2,1)S(1)}, u32[]{:S(2)}, u32[]{:S(2)}) collective-permute-start(bf16[192,512]{1,0:T(8,128)(2,1)S(1)} %get-tuple-element.50), channel_id=1, source_target_pairs={{0,4},{1,3},{16,20},{17,19},{32,36},{33,35},{48,52},{49,51},{4,8},... | collective-permute-start | bytes 589832 | tf_op jit(solution)/shard_map/ppermute | solution.py:38
  71.5 9.5 %collective-permute-start.29 = (f32[192]{0:T(256)S(1)}, f32[192]{0:T(256)S(1)}, u32[]{:S(2)}, u32[]{:S(2)}) collective-permute-start(f32[192]{0:T(256)S(1)} %fusion.5), channel_id=1, source_target_pairs={{0,1},{1,0},{2,3},{3,2},{4,5},{5,4},{6,7},{7,6},{8,9},{9,8},{10,11... | collective-permute-start | bytes 2312 | tf_op jit(solution)/shard_map/ppermute | solution.py:42

commit v5 on v1

v5 whole, which is shorter than its diff:
```python
import functools
import itertools

import jax
import jax.numpy as jnp
from jax import lax
from jax.experimental import pallas as pl
from jax.experimental.pallas import tpu as pltpu
from jax.sharding import PartitionSpec as P

AXES = ("loop", "rep", "sec")
X, Y, Z = 0, 1, 2
SIZE = 4
GATHER = (Y, X)
REDUCE = (X, Y)
GATHER_FLIP = (1, 3)
REDUCE_FLIP = (3, 1)
BIT_OF_Z = ((0, 1, 1, 0), (0, 0, 1, 1))
GROUP = 8
MESSAGES = ((0, 0), (2, 1), (2, 0), (1, 1), (3, 1), (1, 0), (3, 0), (0, 1))
EARLY = 3
RING_ORDER = (2, 1, 3)
STRIP = 64
LOADS = 4
PARAMS = pltpu.CompilerParams(vmem_limit_bytes=40 * 1024 * 1024)
SCALAR = pl.BlockSpec(memory_space=pltpu.SMEM)
WHOLE = pl.BlockSpec(memory_space=pltpu.VMEM)
BF16, F32 = jnp.bfloat16, jnp.float32


def index_of(chip, core):
    x, y, z = chip
    return (((x // 2) * SIZE + z) * 8 + y * 2 + x % 2) * 2 + core


def moved(array, axis_of_core, by, flip_of_core=(0, 0)):
    pairs = []
    for chip in itertools.product(range(SIZE), repeat=3):
        for core in range(2):
            target = list(chip)
            axis = axis_of_core[core]
            target[axis] = (target[axis] + by) % SIZE
            target[Z] ^= flip_of_core[core]
            pairs.append((index_of(chip, core), index_of(target, core)))
    return lax.ppermute(array, AXES, pairs)


def other_core(array):
    return lax.ppermute(array, "sec", [(0, 1), (1, 0)])


def places_here():
    loop, rep, core = (lax.axis_index(name) for name in AXES)
    place = ((loop // SIZE) * 2 + rep % 2, rep // 2, loop % SIZE)
    bits = []
    for table in BIT_OF_Z:
        bit = sum(jnp.where(place[Z] == z, value, 0) for z, value in enumerate(table))
        bits.append(bit)
    first = core == 0
    return jnp.stack(
        [
            jnp.where(first, place[GATHER[0]], place[GATHER[1]]),
            jnp.where(first, bits[0], bits[1]),
            jnp.where(first, place[REDUCE[0]], place[REDUCE[1]]),
        ]
    ).astype(jnp.int32)


def block(which, size):
    return pl.ds(pl.multiple_of(which * size, size), size)


def squares(values):
    values = values.astype(F32)
    return jnp.sum(values * values, axis=1, keepdims=True)


def load_kernel(s_from, t_from, s_own, t_own, ssq_s, ssq_t, arrived):
    rows = s_own.shape[0]
    step = rows // LOADS
    copies = []
    for i in range(LOADS):
        at = pl.ds(i * step, step)
        pair = [
            pltpu.make_async_copy(s_from.at[at, :], s_own.at[at, :], arrived.at[0, i]),
            pltpu.make_async_copy(t_from.at[at, :], t_own.at[at, :], arrived.at[1, i]),
        ]
        for copy in pair:
            copy.start()
        copies.append(pair)
    for i, pair in enumerate(copies):
        for copy in pair:
            copy.wait()
        at = pl.ds(i * step, step)
        ssq_s[at, :] = squares(s_own[at, :])
        ssq_t[at, :] = squares(t_own[at, :])


def inverse_kernel(s_far, t_far, ssq_s, ssq_t, inv_s, inv_t):
    inv_s[...] = lax.rsqrt(ssq_s[...] + squares(s_far[...]) + 1e-06)
    inv_t[...] = lax.rsqrt(ssq_t[...] + squares(t_far[...]) + 1e-06)


def scaled(piece, inv):
    return (piece.astype(F32) * inv).astype(BF16)


def pack_kernel(messages, places, s_own, s_far, t_own, t_far, first_s, first_t, *outs):
    rows, half = s_own.shape
    ss, ts = half // SIZE, t_own.shape[1] // GROUP
    if len(outs) > len(messages):
        inverse_kernel(s_far, t_far, first_s, first_t, *outs[len(messages) :])
        first_s, first_t = outs[len(messages) :]

    @pl.loop(0, rows // STRIP)
    def _(strip):
        at = pl.ds(pl.multiple_of(strip * STRIP, STRIP), STRIP)
        inv_s, inv_t = first_s[at, :], first_t[at, :]
        norm = scaled(s_own[at, :], inv_s)
        for (by, flip), out in zip(messages, outs):
            ring = lax.rem(places[0] + by, SIZE)
            bit = places[1] if flip == 0 else 1 - places[1]
            out[at, pl.ds(0, half)] = norm
            own, far = (ref[at, block(ring, ss)].astype(F32) for ref in (s_own, s_far))
            out[at, pl.ds(half, ss)] = (jnp.where(bit == 1, far, own) * inv_s).astype(BF16)
            which = block(ring + SIZE * bit, ts)
            out[at, pl.ds(half + ss, ts)] = scaled(t_own[at, which], inv_t)
            out[at, pl.ds(half + ss + ts, ts)] = scaled(t_far[at, which], inv_t)


def stacked(packs, left, right):
    rows, half = packs[0].shape[0], left.shape[1]
    for k, pack in enumerate(packs):
        at = pl.ds(k * rows, rows)
        left[at, :] = pack[:, pl.ds(0, half)]
        right[at, :] = pack[:, pl.ds(half, right.shape[1])]


def cross(left, right):
    return lax.dot_general(
        left[...], right[...], (((0,), (0,)), ((), ())), preferred_element_type=F32
    )


def gram_early_kernel(*refs):
    packs, (product, left, right) = refs[:-3], refs[-3:]
    stacked(packs, left, right)
    product[...] = cross(left, right)


def gram_late_kernel(share, places, *refs):
    packs, (before, *outs), (left, right, product) = refs[: -SIZE - 4], refs[-SIZE - 4 : -3], refs[-3:]
    half, feats = product.shape
    ss = half // SIZE
    stacked(packs, left, right)
    product[...] = before[...] + cross(left, right)
    row = lax.broadcasted_iota(jnp.int32, (ss, ss), 0)
    col = lax.broadcasted_iota(jnp.int32, (ss, ss), 1)
    on_diagonal = (row == col) & (places[1] == 0)
    product[block(places[0], ss), pl.ds(0, ss)] -= jnp.where(on_diagonal, share, 0.0)
    for by, out in enumerate(outs):
        at = block(lax.rem(places[2] + by, SIZE), ss)
        rest = pl.ds(ss, feats - ss)
        out[:, pl.ds(0, ss)] = product[at, pl.ds(0, ss)].astype(out.dtype)
        out[:, rest] = -product[at, rest].astype(out.dtype)


def apply_kernel(count, places, *refs):
    packs, pieces = refs[:count], refs[count : count + SIZE]
    outs, weights = refs[count + SIZE : -1], refs[-1]
    half, feats = weights.shape
    ss = half // SIZE
    for by, piece in enumerate(pieces):
        weights[block(lax.rem(places[2] + SIZE - by, SIZE), ss), :] = piece[...]
    for pack, out in zip(packs, outs):
        out[...] = lax.dot_general(
            pack[:, pl.ds(half, feats)],
            weights[...],
            (((1,), (1,)), ((), ())),
            preferred_element_type=F32,
        ).astype(out.dtype)


def shapes(*described):
    return [jax.ShapeDtypeStruct(shape, dtype) for shape, dtype in described]


def kernel_call(kernel, name, outs, args, scratch=(), flops=0, specs=None):
    return pl.pallas_call(
        kernel,
        out_shape=outs,
        in_specs=specs or [SCALAR] + [WHOLE] * (len(args) - 1),
        out_specs=[WHOLE] * len(outs),
        scratch_shapes=list(scratch),
        compiler_params=PARAMS,
        cost_estimate=pl.CostEstimate(flops=flops, bytes_accessed=4 << 20, transcendentals=0),
        name=name,
    )(*args)


def body(student, teacher):
    rows, half = student.shape
    wide = teacher.shape[1]
    width = 2 * half
    groups = lax.axis_size("loop") * lax.axis_size("rep")
    passages = rows * groups
    coef = 32.0 * width / (passages**0.5)
    level = passages / width
    ss, ts = half // SIZE, wide // GROUP
    feats = ss + 2 * ts
    flops = GROUP * rows * half * feats
    places = places_here()

    t_far, s_far = other_core(teacher), other_core(student)
    s_own, t_own, ssq_s, ssq_t = kernel_call(
        load_kernel,
        "load",
        shapes((student.shape, BF16), (teacher.shape, BF16), *[((rows, 1), F32)] * 2),
        (student, teacher),
        [pltpu.SemaphoreType.DMA((2, LOADS))],
        specs=[pl.BlockSpec(memory_space=pltpu.HBM)] * 2,
    )
    pack = ((rows, half + feats), BF16)
    *sent, inv_s, inv_t = kernel_call(
        functools.partial(pack_kernel, MESSAGES[1:EARLY]),
        "pack_early",
        shapes(*[pack] * (EARLY - 1), *[((rows, 1), F32)] * 2),
        (places, s_own, s_far, t_own, t_far, ssq_s, ssq_t),
    )
    late = MESSAGES[EARLY:] + MESSAGES[:1]
    sent += kernel_call(
        functools.partial(pack_kernel, late),
        "pack_late",
        shapes(*[pack] * len(late)),
        (places, s_own, s_far, t_own, t_far, inv_s, inv_t),
    )
    packs = [sent[-1]] + [
        moved(array, GATHER, by, [flip * f for f in GATHER_FLIP])
        for array, (by, flip) in zip(sent, MESSAGES[1:])
    ]
    norm_f = packs[0][:, :half].astype(F32)

    count = GROUP // 2
    operands = [pltpu.VMEM((count * rows, half), BF16), pltpu.VMEM((count * rows, feats), BF16)]
    product = pl.pallas_call(
        gram_early_kernel,
        out_shape=shapes(((half, feats), F32))[0],
        in_specs=[WHOLE] * count,
        out_specs=WHOLE,
        scratch_shapes=operands,
        compiler_params=PARAMS,
        cost_estimate=pl.CostEstimate(flops=flops, bytes_accessed=4 << 20, transcendentals=0),
        name="gram_early",
    )(*packs[:count])
    own, *sends = kernel_call(
        functools.partial(gram_late_kernel, level * GROUP / groups),
        "gram_late",
        shapes(((ss, feats), F32), *[((ss, feats), BF16)] * 3),
        (places, *packs[count:], product),
        operands + [pltpu.VMEM((half, feats), F32)],
        flops,
    )
    arrived = [moved(sends[by - 1], REDUCE, by) for by in RING_ORDER]
    total = own + sum(array.astype(F32) for array in arrived)
    total = total + moved(total.astype(BF16), REDUCE, 0, REDUCE_FLIP).astype(F32)
    piece = total.astype(BF16)
    arrived = {by: moved(piece, REDUCE, by) for by in RING_ORDER}
    pieces = [piece] + [arrived[by] for by in (1, 2, 3)]

    weights = [pltpu.VMEM((half, feats), BF16)]
    back = kernel_call(
        functools.partial(apply_kernel, EARLY),
        "apply_early",
        shapes(*[((rows, half), BF16)] * EARLY),
        (places, *packs[1 : EARLY + 1], *pieces),
        weights,
        flops * EARLY // GROUP,
    )
    rest = GROUP - 1 - EARLY
    *later, grad_n = kernel_call(
        functools.partial(apply_kernel, rest + 1),
        "apply_late",
        shapes(*[((rows, half), BF16)] * rest, ((rows, half), F32)),
        (places, *packs[EARLY + 1 :], packs[0], *pieces),
        weights,
        flops * (rest + 1) // GROUP,
    )
    grad_n = grad_n + level * norm_f
    for array, (by, flip) in zip(list(back) + later, MESSAGES[1:]):
        grad_n = grad_n + moved(array, GATHER, -by, [flip * f for f in GATHER_FLIP]).astype(F32)
    grad_n = coef * grad_n
    inner = jnp.sum(grad_n * norm_f, axis=1)
    inner = inner + other_core(inner)
    return (grad_n - inner[:, None] * norm_f) * inv_s


def solution(mesh):
    placed = (P(("loop", "rep"), "sec"), P(("loop", "rep"), "sec"))
    return jax.shard_map(
        body, mesh=mesh, in_specs=placed, out_specs=P(("loop", "rep"), "sec"), check_vma=False
    )
```

time: 114 us -> 89.4 us (0.78)
  local copies, waits for them, and re-layouts: 22.7 us -> 2.06 us
  waiting for transfers between devices: 45.2 us -> 35.1 us
  Pallas kernels: 0 us -> 9.62 us
  other arithmetic: 9.77 us -> 1.59 us
  starting transfers between devices: 32 us -> 39.6 us
  matrix products: 3.71 us -> 0 us
    unnamed x27 -> x4, local copies, waits for them, and re-layouts: 19.3 us -> 2.06 us
    ppermute x18 -> x21, starting transfers between devices: 21.6 us -> 34.5 us  [moved(): return lax.ppermute(array, AXES, pairs)]
    ppermute x18 -> x21, waiting for transfers between devices: 44.4 us -> 34.4 us  [moved(): return lax.ppermute(array, AXES, pairs)]
    pallas_call x0 -> x7, Pallas kernels: none -> 9.62 us  [the longest x6 8.78 us: kernel_call(): pl.pallas_call(kernel, out_shape=outs, in_specs=specs or [SCALAR] + [WHOL...]
    ppermute x3, starting transfers between devices: 10.4 us -> 5.05 us  [other_core(): return lax.ppermute(array, 'sec', [(0, 1), (1, 0)])]
    dot_general x2 -> x0, matrix products: 3.71 us -> none  [the longest x1 2.48 us: body(): partial = jnp.dot(left, weights, preferred_element_type=jnp.float32)]
    concatenate x3 -> x0, local copies, waits for them, and re-layouts: 3.28 us -> none  [the longest x2 2.37 us: all_gathered(): around = jnp.concatenate(parts + parts, axis=0)]
    convert_element_type x3 -> x2, other arithmetic: 3.02 us -> 0.18 us  [the longest x1 0.1 us: body(): piece = total.astype(BF16)]
  transfers between devices with their start and end apart: 21 -> 24, of which waited for: 14 -> 14; matrix products, arithmetic and copies ran while one was open for 9% -> 0% of each run, Pallas kernels for 0% -> 6%
where the time goes in v5:
time: 89.4 us; the launch traced here: 88.1 us
  starting transfers between devices  39.6 us (44%)
  waiting for transfers between devices  35.1 us (39%)
  Pallas kernels  9.62 us (11%)
  local copies, waits for them, and re-layouts  2.06 us (2%)
  other arithmetic  1.59 us (2%)
    ppermute x21, starting transfers between devices, moved(): return lax.ppermute(array, AXES, pairs)  34.5 us
    ppermute x21, waiting for transfers between devices, moved(): return lax.ppermute(array, AXES, pairs)  34.4 us
    pallas_call x6, Pallas kernels, kernel_call(): pl.pallas_call(kernel, out_shape=outs, in_specs=specs or [SCALAR] + [WHOL...  8.78 us
    ppermute x3, starting transfers between devices, other_core(): return lax.ppermute(array, 'sec', [(0, 1), (1, 0)])  5.05 us
    unnamed x4, local copies, waits for them, and re-layouts  2.06 us
  transfers between devices with their start and end apart: 24, of which 14 were waited for; matrix products, arithmetic and copies ran while one was open for 0% of the time, Pallas kernels for 6%

profile of v5, /device:TPU:1, one launch (start us, length us, event | category | flops | bytes accessed | tf_op | source)
XLA Modules:
  0.0 88.1 jit_solution(14773372905051685175)
XLA Ops:
  0.0 1.4 %collective-permute-start.1 = (bf16[192,2048]{1,0:T(8,128)(2,1)}, bf16[192,2048]{1,0:T(8,128)(2,1)S(1)}, u32[]{:S(2)}, u32[]{:S(2)}) collective-permute-start(bf16[192,2048]{1,0:T(8,128)(2,1)} %t_from.1), channel_id=1, source_target_pairs={{0,1},{1,0},{2,3},{3,2},{4,5},{5,4},{6,7},{7,6},{8,9},{9,8},{10,11... | collective-permute-start | bytes 2359304 | tf_op jit(solution)/shard_map/ppermute | solution.py:49
  1.4 1.1 %copy-done = bf16[192,2048]{1,0:T(8,128)(2,1)S(1)} copy-done((bf16[192,2048]{1,0:T(8,128)(2,1)S(1)}, bf16[192,2048]{1,0:T(8,128)(2,1)}, u32[]{:S(2)}) %copy-start) | copy-done | bytes 786456
  2.6 0.9 %copy-done.1 = bf16[192,512]{1,0:T(8,128)(2,1)S(1)} copy-done((bf16[192,512]{1,0:T(8,128)(2,1)S(1)}, bf16[192,512]{1,0:T(8,128)(2,1)}, u32[]{:S(2)}) %copy-start.1) | copy-done | bytes 196632
  3.5 1.8 %load.1 = (bf16[192,512]{1,0:T(8,128)(2,1)S(1)}, bf16[192,2048]{1,0:T(8,128)(2,1)S(1)}, f32[192,1]{1,0:T(8,128)S(1)}, f32[192,1]{1,0:T(8,128)S(1)}) custom-call(bf16[192,512]{1,0:T(8,128)(2,1)S(1)} %copy-done.1, bf16[192,2048]{1,0:T(8,128)(2,1)S(1)} %copy-done), custom_call_target="tpu_custom_call" | custom-call | bytes 4194304 | tf_op jit(solution)/shard_map/load/pallas_call | solution.py:189
  5.3 0.1 pad_add_fusion.places
  5.4 1.1 %pack_early.1 = (bf16[192,1152]{1,0:T(8,128)(2,1)S(1)}, bf16[192,1152]{1,0:T(8,128)(2,1)S(1)}, f32[192,1]{1,0:T(8,128)S(1)}, f32[192,1]{1,0:T(8,128)S(1)}) custom-call(s32[3]{0:T(128)S(1)} %pad_add_fusion.places, bf16[192,512]{1,0:T(8,128)(2,1)S(1)} %get-tuple-element.31.s_own, bf16[192,512]{1,0:T(8,128)(2,1)S(1)} %collective-permute-done.s_far, ...), custom_call_target="tpu_custom_call" | custom-call | bytes 4194304 | tf_op jit(solution)/shard_map/pack_early/pallas_call | solution.py:189
  6.6 6.4 %collective-permute-start.6 = (bf16[192,1152]{1,0:T(8,128)(2,1)S(1)}, bf16[192,1152]{1,0:T(8,128)(2,1)S(1)}, u32[]{:S(2)}, u32[]{:S(2)}) collective-permute-start(bf16[192,1152]{1,0:T(8,128)(2,1)S(1)} %get-tuple-element.42), channel_id=1, source_target_pairs={{0,24},{1,113},{16,8},{17,97},{32,56},{33,81},{48,40},{49,65},{4,2... | collective-permute-start | bytes 1327112 | tf_op jit(solution)/shard_map/ppermute | solution.py:45
  13.0 0.2 collective-permute-start.7
  13.2 1.1 %pack_late.1 = (bf16[192,1152]{1,0:T(8,128)(2,1)S(1)}, bf16[192,1152]{1,0:T(8,128)(2,1)S(1)}, bf16[192,1152]{1,0:T(8,128)(2,1)S(1)}, bf16[192,1152]{1,0:T(8,128)...) custom-call(s32[3]{0:T(128)S(1)} %pad_add_fusion.places, ...), custom_call_target="tpu_custom_call" | custom-call | bytes 4194304 | tf_op jit(solution)/shard_map/pack_late/pallas_call | solution.py:189
  14.3 0.2 collective-permute-start.8
  14.5 4.6 %collective-permute-start.2 = (bf16[192,1152]{1,0:T(8,128)(2,1)S(1)}, bf16[192,1152]{1,0:T(8,128)(2,1)S(1)}, u32[]{:S(2)}, u32[]{:S(2)}) collective-permute-start(bf16[192,1152]{1,0:T(8,128)(2,1)S(1)} %get-tuple-element.37), channel_id=1, source_target_pairs={{0,28},{1,115},{16,12},{17,99},{32,60},{33,83},{48,44},{49,67},{4,... | collective-permute-start | bytes 1327112 | tf_op jit(solution)/shard_map/ppermute | solution.py:45
  19.2 2.7 %collective-permute-start.4 = (bf16[192,1152]{1,0:T(8,128)(2,1)S(1)}, bf16[192,1152]{1,0:T(8,128)(2,1)S(1)}, u32[]{:S(2)}, u32[]{:S(2)}) collective-permute-start(bf16[192,1152]{1,0:T(8,128)(2,1)S(1)} %get-tuple-element.39), channel_id=1, source_target_pairs={{0,12},{1,67},{16,28},{17,83},{32,44},{33,99},{48,60},{49,115},{4,... | collective-permute-start | bytes 1327112 | tf_op jit(solution)/shard_map/ppermute | solution.py:45
  21.8 2.1 %collective-permute-done.7.refs_2_.refs_1_ = bf16[192,1152]{1,0:T(8,128)(2,1)S(1)} collective-permute-done((bf16[192,1152]{1,0:T(8,128)(2,1)S(1)}, bf16[192,1152]{1,0:T(8,128)(2,1)S(1)}, u32[]{:S(2)}, u32[]{:S(2)}) %collective-permute-start.7) | collective-permute-done | bytes 442400 | tf_op jit(solution)/shard_map/ppermute | solution.py:45
  24.0 7.5 %collective-permute-done.8.refs_3_.refs_2_ = bf16[192,1152]{1,0:T(8,128)(2,1)S(1)} collective-permute-done((bf16[192,1152]{1,0:T(8,128)(2,1)S(1)}, bf16[192,1152]{1,0:T(8,128)(2,1)S(1)}, u32[]{:S(2)}, u32[]{:S(2)}) %collective-permute-start.8) | collective-permute-done | bytes 442400 | tf_op jit(solution)/shard_map/ppermute | solution.py:45
  31.5 0.8 gram_early.1.refs_4_
  32.4 3.9 %collective-permute-done.3.refs_1_ = bf16[192,1152]{1,0:T(8,128)(2,1)S(1)} collective-permute-done((bf16[192,1152]{1,0:T(8,128)(2,1)S(1)}, bf16[192,1152]{1,0:T(8,128)(2,1)S(1)}, u32[]{:S(2)}, u32[]{:S(2)}) %collective-permute-start.3) | collective-permute-done | bytes 442400 | tf_op jit(solution)/shard_map/ppermute | solution.py:45
  36.3 1.6 %collective-permute-done.4.refs_2_ = bf16[192,1152]{1,0:T(8,128)(2,1)S(1)} collective-permute-done((bf16[192,1152]{1,0:T(8,128)(2,1)S(1)}, bf16[192,1152]{1,0:T(8,128)(2,1)S(1)}, u32[]{:S(2)}, u32[]{:S(2)}) %collective-permute-start.4) | collective-permute-done | bytes 442400 | tf_op jit(solution)/shard_map/ppermute | solution.py:45
  37.9 1.5 %gram_late.1 = (f32[128,640]{1,0:T(8,128)S(1)}, bf16[128,640]{1,0:T(8,128)(2,1)S(1)}, bf16[128,640]{1,0:T(8,128)(2,1)S(1)}, bf16[128,640]{1,0:T(8,128)(2,1)S(1)}) custom-call(s32[3]{0:T(128)S(1)} %pad_add_fusion.places, bf16[192,1152]{1,0:T(8,128)(2,1)S(1)} %collective-permute-done.2.refs_0_, bf16[192,1152]{1,0:T(8,128)(2,1)S(1)} %collective-permute-done.3.refs_1_, ...), custom_call_target="tpu_custom_call" | custom-call | flops 503316480 | bytes 4194304 | tf_op jit(solution)/shard_map/gram_late/pallas_call | solution.py:189
  39.4 3.0 %collective-permute-start.9 = (bf16[128,640]{1,0:T(8,128)(2,1)S(1)}, bf16[128,640]{1,0:T(8,128)(2,1)S(1)}, u32[]{:S(2)}, u32[]{:S(2)}) collective-permute-start(bf16[128,640]{1,0:T(8,128)(2,1)S(1)} %get-tuple-element.46), channel_id=1, source_target_pairs={{0,64},{1,9},{16,80},{17,25},{32,96},{33,41},{48,112},{49,57},{4,6... | collective-permute-start | bytes 491528 | tf_op jit(solution)/shard_map/ppermute | solution.py:45
  42.4 0.4 collective-permute-start.10
  42.8 2.3 %collective-permute-start.11 = (bf16[128,640]{1,0:T(8,128)(2,1)S(1)}, bf16[128,640]{1,0:T(8,128)(2,1)S(1)}, u32[]{:S(2)}, u32[]{:S(2)}) collective-permute-start(bf16[128,640]{1,0:T(8,128)(2,1)S(1)} %get-tuple-element.48), channel_id=1, source_target_pairs={{0,66},{1,13},{16,82},{17,29},{32,98},{33,45},{48,114},{49,61},{4,... | collective-permute-start | bytes 491528 | tf_op jit(solution)/shard_map/ppermute | solution.py:45
  45.1 0.4 collective-permute-done.9
  45.4 2.6 %collective-permute-done.10 = bf16[128,640]{1,0:T(8,128)(2,1)S(1)} collective-permute-done((bf16[128,640]{1,0:T(8,128)(2,1)S(1)}, bf16[128,640]{1,0:T(8,128)(2,1)S(1)}, u32[]{:S(2)}, u32[]{:S(2)}) %collective-permute-start.10) | collective-permute-done | bytes 163872 | tf_op jit(solution)/shard_map/ppermute | solution.py:45
  48.1 0.1 fusion.12
  48.1 0.1 collective-permute-start.12
  48.2 4.2 %collective-permute-done.12 = bf16[128,640]{1,0:T(8,128)(2,1)S(1)} collective-permute-done((bf16[128,640]{1,0:T(8,128)(2,1)S(1)}, bf16[128,640]{1,0:T(8,128)(2,1)S(1)}, u32[]{:S(2)}, u32[]{:S(2)}) %collective-permute-start.12) | collective-permute-done | bytes 163872 | tf_op jit(solution)/shard_map/ppermute | solution.py:45
  52.4 0.1 add_convert_fusion.refs_5_.refs_3_
  52.5 2.7 %collective-permute-start.15 = (bf16[128,640]{1,0:T(8,128)(2,1)S(1)}, bf16[128,640]{1,0:T(8,128)(2,1)S(1)}, u32[]{:S(2)}, u32[]{:S(2)}) collective-permute-start(bf16[128,640]{1,0:T(8,128)(2,1)S(1)} %add_convert_fusion.refs_5_.refs_3_), channel_id=1, source_target_pairs={{0,66},{1,13},{16,82},{17,29},{32,98},{33,45},{48,114},{49,61},{4,... | collective-permute-start | bytes 491528 | tf_op jit(solution)/shard_map/ppermute | solution.py:45
  55.2 0.7 collective-permute-start.13
  55.9 3.3 %collective-permute-done.15.refs_8_.refs_6_ = bf16[128,640]{1,0:T(8,128)(2,1)S(1)} collective-permute-done((bf16[128,640]{1,0:T(8,128)(2,1)S(1)}, bf16[128,640]{1,0:T(8,128)(2,1)S(1)}, u32[]{:S(2)}, u32[]{:S(2)}) %collective-permute-start.15) | collective-permute-done | bytes 163872 | tf_op jit(solution)/shard_map/ppermute | solution.py:45
  59.2 1.8 %collective-permute-done.14.refs_7_.refs_5_ = bf16[128,640]{1,0:T(8,128)(2,1)S(1)} collective-permute-done((bf16[128,640]{1,0:T(8,128)(2,1)S(1)}, bf16[128,640]{1,0:T(8,128)(2,1)S(1)}, u32[]{:S(2)}, u32[]{:S(2)}) %collective-permute-start.14) | collective-permute-done | bytes 163872 | tf_op jit(solution)/shard_map/ppermute | solution.py:45
  61.0 1.4 %collective-permute-done.13.refs_6_.refs_4_ = bf16[128,640]{1,0:T(8,128)(2,1)S(1)} collective-permute-done((bf16[128,640]{1,0:T(8,128)(2,1)S(1)}, bf16[128,640]{1,0:T(8,128)(2,1)S(1)}, u32[]{:S(2)}, u32[]{:S(2)}) %collective-permute-start.13) | collective-permute-done | bytes 163872 | tf_op jit(solution)/shard_map/ppermute | solution.py:45
  62.4 1.4 %apply_early.1 = (bf16[192,512]{1,0:T(8,128)(2,1)S(1)}, bf16[192,512]{1,0:T(8,128)(2,1)S(1)}, bf16[192,512]{1,0:T(8,128)(2,1)S(1)}) custom-call(s32[3]{0:T(128)S(1)} %pad_add_fusion.places, bf16[192,1152]{1,0:T(8,128)(2,1)S(1)} %collective-permute-done.6.refs_1_.refs_0_, bf16[192,1152]{1,0:T(8,128)(2,1)S(1)} %collective-permute-done.7.refs_2_.refs_1_, ...), custom_call_target="tpu_custom_call" | custom-call | flops 188743680 | bytes 4194304 | tf_op jit(solution)/shard_map/apply_early/pallas_call | solution.py:189
  63.8 4.0 %collective-permute-start.16 = (bf16[192,512]{1,0:T(8,128)(2,1)S(1)}, bf16[192,512]{1,0:T(8,128)(2,1)S(1)}, u32[]{:S(2)}, u32[]{:S(2)}) collective-permute-start(bf16[192,512]{1,0:T(8,128)(2,1)S(1)} %get-tuple-element.50), channel_id=1, source_target_pairs={{0,24},{1,113},{16,8},{17,97},{32,56},{33,81},{48,40},{49,65},{4,2... | collective-permute-start | bytes 589832 | tf_op jit(solution)/shard_map/ppermute | solution.py:45
  67.8 1.1 %collective-permute-start.17 = (bf16[192,512]{1,0:T(8,128)(2,1)S(1)}, bf16[192,512]{1,0:T(8,128)(2,1)S(1)}, u32[]{:S(2)}, u32[]{:S(2)}) collective-permute-start(bf16[192,512]{1,0:T(8,128)(2,1)S(1)} %get-tuple-element.51), channel_id=1, source_target_pairs={{0,8},{1,65},{16,24},{17,81},{32,40},{33,97},{48,56},{49,113},{4,1... | collective-permute-start | bytes 589832 | tf_op jit(solution)/shard_map/ppermute | solution.py:45
  68.9 0.8 collective-permute-start.18
  69.7 1.8 %apply_late.1 = (bf16[192,512]{1,0:T(8,128)(2,1)S(1)}, bf16[192,512]{1,0:T(8,128)(2,1)S(1)}, bf16[192,512]{1,0:T(8,128)(2,1)S(1)}, bf16[192,512]{1,0:T(8,128)(2,1)S(1)}, f32[192,512]{1,0:T(8,128)S(1)}) custom-call(s32[3]{0:T(128)S(1)} %pad_add_fusion.places, bf16[192,1152]{1,0:T(8,128)(2,1)S(1)} %collective-permute-done.2.refs_0_, ...), custom_call_target="tpu_custom_call" | custom-call | flops 314572800 | bytes 4194304 | tf_op jit(solution)/shard_map/apply_late/pallas_call | solution.py:189
  71.6 2.8 %collective-permute-start.19 = (bf16[192,512]{1,0:T(8,128)(2,1)S(1)}, bf16[192,512]{1,0:T(8,128)(2,1)S(1)}, u32[]{:S(2)}, u32[]{:S(2)}) collective-permute-start(bf16[192,512]{1,0:T(8,128)(2,1)S(1)} %get-tuple-element.53), channel_id=1, source_target_pairs={{0,20},{1,51},{16,4},{17,35},{32,52},{33,19},{48,36},{49,3},{4,24}... | collective-permute-start | bytes 589832 | tf_op jit(solution)/shard_map/ppermute | solution.py:45
  74.4 2.0 %collective-permute-start.20 = (bf16[192,512]{1,0:T(8,128)(2,1)S(1)}, bf16[192,512]{1,0:T(8,128)(2,1)S(1)}, u32[]{:S(2)}, u32[]{:S(2)}) collective-permute-start(bf16[192,512]{1,0:T(8,128)(2,1)S(1)} %get-tuple-element.54), channel_id=1, source_target_pairs={{0,12},{1,67},{16,28},{17,83},{32,44},{33,99},{48,60},{49,115},{4,... | collective-permute-start | bytes 589832 | tf_op jit(solution)/shard_map/ppermute | solution.py:45
  76.3 0.5 collective-permute-start.22
  76.8 2.7 %collective-permute-done.19 = bf16[192,512]{1,0:T(8,128)(2,1)S(1)} collective-permute-done((bf16[192,512]{1,0:T(8,128)(2,1)S(1)}, bf16[192,512]{1,0:T(8,128)(2,1)S(1)}, u32[]{:S(2)}, u32[]{:S(2)}) %collective-permute-start.19) | collective-permute-done | bytes 196640 | tf_op jit(solution)/shard_map/ppermute | solution.py:45
  79.5 2.9 %collective-permute-done.21 = bf16[192,512]{1,0:T(8,128)(2,1)S(1)} collective-permute-done((bf16[192,512]{1,0:T(8,128)(2,1)S(1)}, bf16[192,512]{1,0:T(8,128)(2,1)S(1)}, u32[]{:S(2)}, u32[]{:S(2)}) %collective-permute-start.21) | collective-permute-done | bytes 196640 | tf_op jit(solution)/shard_map/ppermute | solution.py:45
  82.4 0.1 collective-permute-done.22
  82.5 0.4 fusion.9
  82.8 3.6 %collective-permute-start.23 = (f32[192]{0:T(256)S(1)}, f32[192]{0:T(256)S(1)}, u32[]{:S(2)}, u32[]{:S(2)}) collective-permute-start(f32[192]{0:T(256)S(1)} %get-tuple-element.57), channel_id=1, source_target_pairs={{0,1},{1,0},{2,3},{3,2},{4,5},{5,4},{6,7},{7,6},{8,9},{9,8},{10,11... | collective-permute-start | bytes 2312 | tf_op jit(solution)/shard_map/ppermute | solution.py:49
  86.4 0.1 reduce
  86.5 0.7 collective-permute-done.23
  87.3 0.9 fusion.11
  (18 shorter events, 0.1 us)
Async XLA Ops:
  0.0 5.4 %collective-permute-start.1 = (bf16[192,2048]{1,0:T(8,128)(2,1)}, bf16[192,2048]{1,0:T(8,128)(2,1)S(1)}, u32[]{:S(2)}, u32[]{:S(2)}) collective-permute-start(bf16[192,2048]{1,0:T(8,128)(2,1)} %t_from.1), channel_id=1, source_target_pairs={{0,1},{1,0},{2,3},{3,2},{4,5},{5,4},{6,7},{7,6},{8,9},{9,8},{10,11... | collective-permute-start | bytes 2359304 | tf_op jit(solution)/shard_map/ppermute | solution.py:49
  1.4 4.0 %collective-permute-start = (bf16[192,512]{1,0:T(8,128)(2,1)}, bf16[192,512]{1,0:T(8,128)(2,1)S(1)}, u32[]{:S(2)}, u32[]{:S(2)}) collective-permute-start(bf16[192,512]{1,0:T(8,128)(2,1)} %s_from.1), channel_id=1, source_target_pairs={{0,1},{1,0},{2,3},{3,2},{4,5},{5,4},{6,7},{7,6},{8,9},{9,8},{10,11... | collective-permute-start | bytes 589832 | tf_op jit(solution)/shard_map/ppermute | solution.py:49
  1.4 1.1 %copy-start = (bf16[192,2048]{1,0:T(8,128)(2,1)S(1)}, bf16[192,2048]{1,0:T(8,128)(2,1)}, u32[]{:S(2)}) copy-start(bf16[192,2048]{1,0:T(8,128)(2,1)} %t_from.1) | copy-start | bytes 2359300
  2.6 0.9 %copy-start.1 = (bf16[192,512]{1,0:T(8,128)(2,1)S(1)}, bf16[192,512]{1,0:T(8,128)(2,1)}, u32[]{:S(2)}) copy-start(bf16[192,512]{1,0:T(8,128)(2,1)} %s_from.1) | copy-start | bytes 589828
  6.6 12.6 %collective-permute-start.6 = (bf16[192,1152]{1,0:T(8,128)(2,1)S(1)}, bf16[192,1152]{1,0:T(8,128)(2,1)S(1)}, u32[]{:S(2)}, u32[]{:S(2)}) collective-permute-start(bf16[192,1152]{1,0:T(8,128)(2,1)S(1)} %get-tuple-element.42), channel_id=1, source_target_pairs={{0,24},{1,113},{16,8},{17,97},{32,56},{33,81},{48,40},{49,65},{4,2... | collective-permute-start | bytes 1327112 | tf_op jit(solution)/shard_map/ppermute | solution.py:45
  13.0 11.0 %collective-permute-start.7 = (bf16[192,1152]{1,0:T(8,128)(2,1)S(1)}, bf16[192,1152]{1,0:T(8,128)(2,1)S(1)}, u32[]{:S(2)}, u32[]{:S(2)}) collective-permute-start(bf16[192,1152]{1,0:T(8,128)(2,1)S(1)} %get-tuple-element.43), channel_id=1, source_target_pairs={{0,8},{1,65},{16,24},{17,81},{32,40},{33,97},{48,56},{49,113},{4,1... | collective-permute-start | bytes 1327112 | tf_op jit(solution)/shard_map/ppermute | solution.py:45
  14.3 17.2 %collective-permute-start.8 = (bf16[192,1152]{1,0:T(8,128)(2,1)S(1)}, bf16[192,1152]{1,0:T(8,128)(2,1)S(1)}, u32[]{:S(2)}, u32[]{:S(2)}) collective-permute-start(bf16[192,1152]{1,0:T(8,128)(2,1)S(1)} %get-tuple-element.44), channel_id=1, source_target_pairs={{0,20},{1,51},{16,4},{17,35},{32,52},{33,19},{48,36},{49,3},{4,24}... | collective-permute-start | bytes 1327112 | tf_op jit(solution)/shard_map/ppermute | solution.py:45
  14.5 17.8 %collective-permute-start.2 = (bf16[192,1152]{1,0:T(8,128)(2,1)S(1)}, bf16[192,1152]{1,0:T(8,128)(2,1)S(1)}, u32[]{:S(2)}, u32[]{:S(2)}) collective-permute-start(bf16[192,1152]{1,0:T(8,128)(2,1)S(1)} %get-tuple-element.37), channel_id=1, source_target_pairs={{0,28},{1,115},{16,12},{17,99},{32,60},{33,83},{48,44},{49,67},{4,... | collective-permute-start | bytes 1327112 | tf_op jit(solution)/shard_map/ppermute | solution.py:45
  19.1 17.1 %collective-permute-start.3 = (bf16[192,1152]{1,0:T(8,128)(2,1)S(1)}, bf16[192,1152]{1,0:T(8,128)(2,1)S(1)}, u32[]{:S(2)}, u32[]{:S(2)}) collective-permute-start(bf16[192,1152]{1,0:T(8,128)(2,1)S(1)} %get-tuple-element.38), channel_id=1, source_target_pairs={{0,4},{1,3},{16,20},{17,19},{32,36},{33,35},{48,52},{49,51},{4,8},... | collective-permute-start | bytes 1327112 | tf_op jit(solution)/shard_map/ppermute | solution.py:45
  19.2 18.7 %collective-permute-start.4 = (bf16[192,1152]{1,0:T(8,128)(2,1)S(1)}, bf16[192,1152]{1,0:T(8,128)(2,1)S(1)}, u32[]{:S(2)}, u32[]{:S(2)}) collective-permute-start(bf16[192,1152]{1,0:T(8,128)(2,1)S(1)} %get-tuple-element.39), channel_id=1, source_target_pairs={{0,12},{1,67},{16,28},{17,83},{32,44},{33,99},{48,60},{49,115},{4,... | collective-permute-start | bytes 1327112 | tf_op jit(solution)/shard_map/ppermute | solution.py:45
  24.0 13.9 %collective-permute-start.5 = (bf16[192,1152]{1,0:T(8,128)(2,1)S(1)}, bf16[192,1152]{1,0:T(8,128)(2,1)S(1)}, u32[]{:S(2)}, u32[]{:S(2)}) collective-permute-start(bf16[192,1152]{1,0:T(8,128)(2,1)S(1)} %get-tuple-element.40), channel_id=1, source_target_pairs={{0,16},{1,49},{16,0},{17,33},{32,48},{33,17},{48,32},{49,1},{4,20}... | collective-permute-start | bytes 1327112 | tf_op jit(solution)/shard_map/ppermute | solution.py:45
  39.4 6.0 %collective-permute-start.9 = (bf16[128,640]{1,0:T(8,128)(2,1)S(1)}, bf16[128,640]{1,0:T(8,128)(2,1)S(1)}, u32[]{:S(2)}, u32[]{:S(2)}) collective-permute-start(bf16[128,640]{1,0:T(8,128)(2,1)S(1)} %get-tuple-element.46), channel_id=1, source_target_pairs={{0,64},{1,9},{16,80},{17,25},{32,96},{33,41},{48,112},{49,57},{4,6... | collective-permute-start | bytes 491528 | tf_op jit(solution)/shard_map/ppermute | solution.py:45
  42.4 5.7 %collective-permute-start.10 = (bf16[128,640]{1,0:T(8,128)(2,1)S(1)}, bf16[128,640]{1,0:T(8,128)(2,1)S(1)}, u32[]{:S(2)}, u32[]{:S(2)}) collective-permute-start(bf16[128,640]{1,0:T(8,128)(2,1)S(1)} %get-tuple-element.47), channel_id=1, source_target_pairs={{0,2},{1,5},{16,18},{17,21},{32,34},{33,37},{48,50},{49,53},{4,6},... | collective-permute-start | bytes 491528 | tf_op jit(solution)/shard_map/ppermute | solution.py:45
  42.8 5.3 %collective-permute-start.11 = (bf16[128,640]{1,0:T(8,128)(2,1)S(1)}, bf16[128,640]{1,0:T(8,128)(2,1)S(1)}, u32[]{:S(2)}, u32[]{:S(2)}) collective-permute-start(bf16[128,640]{1,0:T(8,128)(2,1)S(1)} %get-tuple-element.48), channel_id=1, source_target_pairs={{0,66},{1,13},{16,82},{17,29},{32,98},{33,45},{48,114},{49,61},{4,... | collective-permute-start | bytes 491528 | tf_op jit(solution)/shard_map/ppermute | solution.py:45
  48.1 4.2 %collective-permute-start.12 = (bf16[128,640]{1,0:T(8,128)(2,1)S(1)}, bf16[128,640]{1,0:T(8,128)(2,1)S(1)}, u32[]{:S(2)}, u32[]{:S(2)}) collective-permute-start(bf16[128,640]{1,0:T(8,128)(2,1)S(1)} %fusion.12), channel_id=1, source_target_pairs={{0,48},{1,17},{16,32},{17,1},{32,16},{33,49},{48,0},{49,33},{4,52}... | collective-permute-start | bytes 491528 | tf_op jit(solution)/shard_map/ppermute | solution.py:45
  52.5 6.8 %collective-permute-start.15 = (bf16[128,640]{1,0:T(8,128)(2,1)S(1)}, bf16[128,640]{1,0:T(8,128)(2,1)S(1)}, u32[]{:S(2)}, u32[]{:S(2)}) collective-permute-start(bf16[128,640]{1,0:T(8,128)(2,1)S(1)} %add_convert_fusion.refs_5_.refs_3_), channel_id=1, source_target_pairs={{0,66},{1,13},{16,82},{17,29},{32,98},{33,45},{48,114},{49,61},{4,... | collective-permute-start | bytes 491528 | tf_op jit(solution)/shard_map/ppermute | solution.py:45
  55.2 5.8 %collective-permute-start.14 = (bf16[128,640]{1,0:T(8,128)(2,1)S(1)}, bf16[128,640]{1,0:T(8,128)(2,1)S(1)}, u32[]{:S(2)}, u32[]{:S(2)}) collective-permute-start(bf16[128,640]{1,0:T(8,128)(2,1)S(1)} %add_convert_fusion.refs_5_.refs_3_), channel_id=1, source_target_pairs={{0,64},{1,9},{16,80},{17,25},{32,96},{33,41},{48,112},{49,57},{4,6... | collective-permute-start | bytes 491528 | tf_op jit(solution)/shard_map/ppermute | solution.py:45
  55.2 7.1 %collective-permute-start.13 = (bf16[128,640]{1,0:T(8,128)(2,1)S(1)}, bf16[128,640]{1,0:T(8,128)(2,1)S(1)}, u32[]{:S(2)}, u32[]{:S(2)}) collective-permute-start(bf16[128,640]{1,0:T(8,128)(2,1)S(1)} %add_convert_fusion.refs_5_.refs_3_), channel_id=1, source_target_pairs={{0,2},{1,5},{16,18},{17,21},{32,34},{33,37},{48,50},{49,53},{4,6},... | collective-permute-start | bytes 491528 | tf_op jit(solution)/shard_map/ppermute | solution.py:45
  63.8 12.6 %collective-permute-start.16 = (bf16[192,512]{1,0:T(8,128)(2,1)S(1)}, bf16[192,512]{1,0:T(8,128)(2,1)S(1)}, u32[]{:S(2)}, u32[]{:S(2)}) collective-permute-start(bf16[192,512]{1,0:T(8,128)(2,1)S(1)} %get-tuple-element.50), channel_id=1, source_target_pairs={{0,24},{1,113},{16,8},{17,97},{32,56},{33,81},{48,40},{49,65},{4,2... | collective-permute-start | bytes 589832 | tf_op jit(solution)/shard_map/ppermute | solution.py:45
  67.8 8.5 %collective-permute-start.17 = (bf16[192,512]{1,0:T(8,128)(2,1)S(1)}, bf16[192,512]{1,0:T(8,128)(2,1)S(1)}, u32[]{:S(2)}, u32[]{:S(2)}) collective-permute-start(bf16[192,512]{1,0:T(8,128)(2,1)S(1)} %get-tuple-element.51), channel_id=1, source_target_pairs={{0,8},{1,65},{16,24},{17,81},{32,40},{33,97},{48,56},{49,113},{4,1... | collective-permute-start | bytes 589832 | tf_op jit(solution)/shard_map/ppermute | solution.py:45
  68.9 7.9 %collective-permute-start.18 = (bf16[192,512]{1,0:T(8,128)(2,1)S(1)}, bf16[192,512]{1,0:T(8,128)(2,1)S(1)}, u32[]{:S(2)}, u32[]{:S(2)}) collective-permute-start(bf16[192,512]{1,0:T(8,128)(2,1)S(1)} %get-tuple-element.52), channel_id=1, source_target_pairs={{0,28},{1,115},{16,12},{17,99},{32,60},{33,83},{48,44},{49,67},{4,... | collective-permute-start | bytes 589832 | tf_op jit(solution)/shard_map/ppermute | solution.py:45
  71.6 7.9 %collective-permute-start.19 = (bf16[192,512]{1,0:T(8,128)(2,1)S(1)}, bf16[192,512]{1,0:T(8,128)(2,1)S(1)}, u32[]{:S(2)}, u32[]{:S(2)}) collective-permute-start(bf16[192,512]{1,0:T(8,128)(2,1)S(1)} %get-tuple-element.53), channel_id=1, source_target_pairs={{0,20},{1,51},{16,4},{17,35},{32,52},{33,19},{48,36},{49,3},{4,24}... | collective-permute-start | bytes 589832 | tf_op jit(solution)/shard_map/ppermute | solution.py:45
  74.4 5.1 %collective-permute-start.20 = (bf16[192,512]{1,0:T(8,128)(2,1)S(1)}, bf16[192,512]{1,0:T(8,128)(2,1)S(1)}, u32[]{:S(2)}, u32[]{:S(2)}) collective-permute-start(bf16[192,512]{1,0:T(8,128)(2,1)S(1)} %get-tuple-element.54), channel_id=1, source_target_pairs={{0,12},{1,67},{16,28},{17,83},{32,44},{33,99},{48,60},{49,115},{4,... | collective-permute-start | bytes 589832 | tf_op jit(solution)/shard_map/ppermute | solution.py:45
  76.3 6.0 %collective-permute-start.21 = (bf16[192,512]{1,0:T(8,128)(2,1)S(1)}, bf16[192,512]{1,0:T(8,128)(2,1)S(1)}, u32[]{:S(2)}, u32[]{:S(2)}) collective-permute-start(bf16[192,512]{1,0:T(8,128)(2,1)S(1)} %get-tuple-element.55), channel_id=1, source_target_pairs={{0,4},{1,3},{16,20},{17,19},{32,36},{33,35},{48,52},{49,51},{4,8},... | collective-permute-start | bytes 589832 | tf_op jit(solution)/shard_map/ppermute | solution.py:45
  76.3 6.1 %collective-permute-start.22 = (bf16[192,512]{1,0:T(8,128)(2,1)S(1)}, bf16[192,512]{1,0:T(8,128)(2,1)S(1)}, u32[]{:S(2)}, u32[]{:S(2)}) collective-permute-start(bf16[192,512]{1,0:T(8,128)(2,1)S(1)} %get-tuple-element.56), channel_id=1, source_target_pairs={{0,16},{1,49},{16,0},{17,33},{32,48},{33,17},{48,32},{49,1},{4,20}... | collective-permute-start | bytes 589832 | tf_op jit(solution)/shard_map/ppermute | solution.py:45
  82.8 4.4 %collective-permute-start.23 = (f32[192]{0:T(256)S(1)}, f32[192]{0:T(256)S(1)}, u32[]{:S(2)}, u32[]{:S(2)}) collective-permute-start(f32[192]{0:T(256)S(1)} %get-tuple-element.57), channel_id=1, source_target_pairs={{0,1},{1,0},{2,3},{3,2},{4,5},{5,4},{6,7},{7,6},{8,9},{9,8},{10,11... | collective-permute-start | bytes 2312 | tf_op jit(solution)/shard_map/ppermute | solution.py:49

commit v6 on v4

--- a/solution.py
+++ b/solution.py
@@ -12,8 +12,8 @@
 X, Y, Z = 0, 1, 2
 SIZE = 4
 GATHER = (Y, X)
-FIRST = ((Z, Z), (X, Y))
-SECOND = ((X, Y), (Z, Z))
+FIRST = ((X, Z), (Z, Y))
+SECOND = ((Z, Y), (X, Z))
 ORDER = (2, 1, 3)
 STRIP = 32
 PARAMS = pltpu.CompilerParams(vmem_limit_bytes=40 * 1024 * 1024)
@@ -56,34 +56,42 @@
     return pl.ds(pl.multiple_of(lax.rem(places[0] + by, SIZE) * size, size), size)
 
 
-def squares(ref):
-    values = ref[...].astype(F32)
+def squares(values):
+    values = values.astype(F32)
     return jnp.sum(values * values, axis=1, keepdims=True)
 
 
+def strips(rows):
+    return [pl.ds(start, STRIP) for start in range(0, rows, STRIP)]
+
+
 def sums_kernel(s_own, t_own, ssq_s, ssq_t):
-    ssq_s[...] = squares(s_own)
-    ssq_t[...] = squares(t_own)
+    for at in strips(s_own.shape[0]):
+        ssq_s[at, :] = squares(s_own[at, :])
+        ssq_t[at, :] = squares(t_own[at, :])
 
 
 def pack_own_kernel(places, s_own, s_far, t_own, t_far, ssq_s, ssq_t, *outs):
-    half, wide = s_own.shape[1], t_own.shape[1]
-    ts = wide // SIZE
-    inv_s = lax.rsqrt(ssq_s[...] + squares(s_far) + 1e-06)
-    inv_t = lax.rsqrt(ssq_t[...] + squares(t_far) + 1e-06)
-    outs[SIZE][...] = inv_s
-    outs[SIZE + 1][...] = inv_t
-    norm = scaled(s_own[...], inv_s)
-    for by in range(SIZE):
-        outs[by][:, pl.ds(0, half)] = norm
-        outs[by][:, pl.ds(half, ts)] = scaled(t_own[:, part(places, by, ts)], inv_t)
+    rows, half = s_own.shape
+    ts = t_own.shape[1] // SIZE
+    inv_s, inv_t = outs[SIZE:]
+    for at in strips(rows):
+        inv_s[at, :] = lax.rsqrt(ssq_s[at, :] + squares(s_far[at, :]) + 1e-06)
+        inv_t[at, :] = lax.rsqrt(ssq_t[at, :] + squares(t_far[at, :]) + 1e-06)
+    for at in strips(rows):
+        norm = scaled(s_own[at, :], inv_s[at, :])
+        for by in range(SIZE):
+            outs[by][at, pl.ds(0, half)] = norm
+            outs[by][at, pl.ds(half, ts)] = scaled(t_own[at, part(places, by, ts)], inv_t[at, :])
 
 
 def pack_far_kernel(places, s_far, t_far, inv_s, inv_t, *outs):
+    rows = s_far.shape[0]
     ss, ts = s_far.shape[1] // SIZE, t_far.shape[1] // SIZE
-    for by in range(SIZE):
-        outs[by][:, pl.ds(0, ss)] = scaled(s_far[:, part(places, by, ss)], inv_s[...])
-        outs[by][:, pl.ds(ss, ts)] = scaled(t_far[:, part(places, by, ts)], inv_t[...])
+    for at in strips(rows):
+        for by in range(SIZE):
+            outs[by][at, pl.ds(0, ss)] = scaled(s_far[at, part(places, by, ss)], inv_s[at, :])
+            outs[by][at, pl.ds(ss, ts)] = scaled(t_far[at, part(places, by, ts)], inv_t[at, :])
 
 
 def native_features(places, pack, half):
@@ -173,24 +181,6 @@
     )
 
 
-def strip_call(kernel, name, widths_in, outs):
-    rows = outs[0].shape[0]
-
-    def spec(width):
-        return pl.BlockSpec((STRIP, width), lambda i: (i, 0))
-
-    return pl.pallas_call(
-        kernel,
-        out_shape=outs,
-        grid=(rows // STRIP,),
-        in_specs=[SCALAR] + [spec(w) for w in widths_in],
-        out_specs=[spec(o.shape[1]) for o in outs],
-        compiler_params=PARAMS,
-        cost_estimate=pl.CostEstimate(flops=0, bytes_accessed=4 << 20, transcendentals=0),
-        name=name,
-    )
-
-
 def body(student, teacher):
     rows, half = student.shape
     wide = teacher.shape[1]
@@ -214,17 +204,14 @@
         cost_estimate=pl.CostEstimate(flops=0, bytes_accessed=1 << 20, transcendentals=0),
         name="sums",
     )(student, teacher)
-    *near, inv_s, inv_t = strip_call(
+    *near, inv_s, inv_t = kernel_call(
         pack_own_kernel,
         "pack_own",
-        (half, half, wide, wide, 1, 1),
         shapes(*[((rows, half + ts), BF16)] * SIZE, *[((rows, 1), F32)] * 2),
+        6,
     )(places, student, s_far, teacher, t_far, ssq_s, ssq_t)
-    far = strip_call(
-        pack_far_kernel,
-        "pack_far",
-        (half, wide, 1, 1),
-        shapes(*[((rows, feats), BF16)] * SIZE),
+    far = kernel_call(
+        pack_far_kernel, "pack_far", shapes(*[((rows, feats), BF16)] * SIZE), 4
     )(places, s_far, t_far, inv_s, inv_t)
     norm_own = near[0][:, :half]
 

time: 82.1 us -> 80.6 us (0.982)
  starting transfers between devices: 45.4 us -> 47.6 us
  local copies, waits for them, and re-layouts: 4.12 us -> 2.06 us
  Pallas kernels: 10.5 us -> 9.08 us
    ppermute x3, starting transfers between devices: 10.1 us -> 13.4 us  [other_core(): return lax.ppermute(array, 'sec', [(0, 1), (1, 0)])]
    unnamed x8 -> x4, local copies, waits for them, and re-layouts: 4.12 us -> 2.06 us
    pallas_call x2, Pallas kernels: 3.23 us -> 1.84 us  [the longest x1 1.03 us: body(): kernel_call(pack_own_kernel, 'pack_own', shapes(*[((rows, half + ts), BF1...]
    ppermute x27, starting transfers between devices: 35.3 us -> 34.2 us  [shifted(): return lax.ppermute(array, AXES, pairs)]
  transfers between devices with their start and end apart: 30 -> 30, of which waited for: 13 -> 12; matrix products, arithmetic and copies ran while one was open for 1% -> 1% of each run, Pallas kernels for 9% -> 8%
where the time goes in v6:
time: 80.6 us; the launch traced here: 80.4 us
  starting transfers between devices  47.6 us (59%)
  waiting for transfers between devices  19.7 us (24%)
  Pallas kernels  9.08 us (11%)
  local copies, waits for them, and re-layouts  2.06 us (3%)
  other arithmetic  1.85 us (2%)
    ppermute x27, starting transfers between devices, shifted(): return lax.ppermute(array, AXES, pairs)  34.2 us
    ppermute x27, waiting for transfers between devices, shifted(): return lax.ppermute(array, AXES, pairs)  19 us
    ppermute x3, starting transfers between devices, other_core(): return lax.ppermute(array, 'sec', [(0, 1), (1, 0)])  13.4 us
    pallas_call x2, Pallas kernels, weights_of(): kernel_call(functools.partial(gram_kernel, level * SIZE / groups, chunk),...  3.2 us
    unnamed x4, local copies, waits for them, and re-layouts  2.06 us
  transfers between devices with their start and end apart: 30, of which 12 were waited for; matrix products, arithmetic and copies ran while one was open for 1% of the time, Pallas kernels for 8%

profile of v6, /device:TPU:1, one launch (start us, length us, event | category | flops | bytes accessed | tf_op | source)
XLA Modules:
  0.0 80.4 jit_solution(1152719340333331267)
XLA Ops:
  0.0 1.4 %collective-permute-start.1 = (bf16[192,2048]{1,0:T(8,128)(2,1)}, bf16[192,2048]{1,0:T(8,128)(2,1)S(1)}, u32[]{:S(2)}, u32[]{:S(2)}) collective-permute-start(bf16[192,2048]{1,0:T(8,128)(2,1)} %t_own.3), channel_id=1, source_target_pairs={{0,1},{1,0},{2,3},{3,2},{4,5},{5,4},{6,7},{7,6},{8,9},{9,8},{10,11... | collective-permute-start | bytes 2359304 | tf_op jit(solution)/shard_map/ppermute | solution.py:42
  1.4 1.1 %copy-done = bf16[192,2048]{1,0:T(8,128)(2,1)S(1)} copy-done((bf16[192,2048]{1,0:T(8,128)(2,1)S(1)}, bf16[192,2048]{1,0:T(8,128)(2,1)}, u32[]{:S(2)}) %copy-start) | copy-done | bytes 786456
  2.6 0.9 %copy-done.1 = bf16[192,512]{1,0:T(8,128)(2,1)S(1)} copy-done((bf16[192,512]{1,0:T(8,128)(2,1)S(1)}, bf16[192,512]{1,0:T(8,128)(2,1)}, u32[]{:S(2)}) %copy-start.1) | copy-done | bytes 196632
  3.5 0.3 sums.1
  3.8 1.0 %pack_own.1 = (bf16[192,1024]{1,0:T(8,128)(2,1)S(1)}, bf16[192,1024]{1,0:T(8,128)(2,1)S(1)}, bf16[192,1024]{1,0:T(8,128)(2,1)S(1)}, bf16[192,1024]{1,0:T(8,128)(...) custom-call(s32[3]{0:T(128)S(1)} %pad_add_fusion.places, bf16[192,512]{1,0:T(8,128)(2,1)S(1)} %copy-done.1, ...), custom_call_target="tpu_custom_call" | custom-call | bytes 4194304 | tf_op jit(solution)/shard_map/pack_own/pallas_call | solution.py:207
  4.9 1.4 %collective-permute-start.2 = (bf16[192,1024]{1,0:T(8,128)(2,1)S(1)}, bf16[192,1024]{1,0:T(8,128)(2,1)S(1)}, u32[]{:S(2)}, u32[]{:S(2)}) collective-permute-start(bf16[192,1024]{1,0:T(8,128)(2,1)S(1)} %get-tuple-element.34), channel_id=1, source_target_pairs={{0,4},{1,3},{16,20},{17,19},{32,36},{33,35},{48,52},{49,51},{4,8},... | collective-permute-start | bytes 1179656 | tf_op jit(solution)/shard_map/ppermute | solution.py:38
  6.2 2.5 %collective-permute-start.3 = (bf16[192,1024]{1,0:T(8,128)(2,1)S(1)}, bf16[192,1024]{1,0:T(8,128)(2,1)S(1)}, u32[]{:S(2)}, u32[]{:S(2)}) collective-permute-start(bf16[192,1024]{1,0:T(8,128)(2,1)S(1)} %get-tuple-element.35), channel_id=1, source_target_pairs={{0,8},{1,65},{16,24},{17,81},{32,40},{33,97},{48,56},{49,113},{4,1... | collective-permute-start | bytes 1179656 | tf_op jit(solution)/shard_map/ppermute | solution.py:38
  8.7 1.2 %collective-permute-start.4 = (bf16[192,1024]{1,0:T(8,128)(2,1)S(1)}, bf16[192,1024]{1,0:T(8,128)(2,1)S(1)}, u32[]{:S(2)}, u32[]{:S(2)}) collective-permute-start(bf16[192,1024]{1,0:T(8,128)(2,1)S(1)} %get-tuple-element.36), channel_id=1, source_target_pairs={{0,12},{1,67},{16,28},{17,83},{32,44},{33,99},{48,60},{49,115},{4,... | collective-permute-start | bytes 1179656 | tf_op jit(solution)/shard_map/ppermute | solution.py:38
  9.8 0.8 %pack_far.1 = (bf16[192,640]{1,0:T(8,128)(2,1)S(1)}, bf16[192,640]{1,0:T(8,128)(2,1)S(1)}, bf16[192,640]{1,0:T(8,128)(2,1)S(1)}, bf16[192,640]{1,0:T(8,128)(2,1)S(1)}) custom-call(s32[3]{0:T(128)S(1)} %pad_add_fusion.places, bf16[192,512]{1,0:T(8,128)(2,1)S(1)} %collective-permute-done.s_far, bf16[192,2048]{1,0:T(8,128)(2,1)S(1)} %collective-permute-done.1.t_far, ...), custom_call_target="tpu_custom_call" | custom-call | bytes 4194304 | tf_op jit(solution)/shard_map/pack_far/pallas_call | solution.py:213
  10.7 0.4 collective-permute-start.5
  11.0 0.9 %collective-permute-start.6 = (bf16[192,640]{1,0:T(8,128)(2,1)S(1)}, bf16[192,640]{1,0:T(8,128)(2,1)S(1)}, u32[]{:S(2)}, u32[]{:S(2)}) collective-permute-start(bf16[192,640]{1,0:T(8,128)(2,1)S(1)} %get-tuple-element.38), channel_id=1, source_target_pairs={{0,8},{1,65},{16,24},{17,81},{32,40},{33,97},{48,56},{49,113},{4,1... | collective-permute-start | bytes 737288 | tf_op jit(solution)/shard_map/ppermute | solution.py:38
  11.9 1.2 %collective-permute-done.2.refs_1_ = bf16[192,1024]{1,0:T(8,128)(2,1)S(1)} collective-permute-done((bf16[192,1024]{1,0:T(8,128)(2,1)S(1)}, bf16[192,1024]{1,0:T(8,128)(2,1)S(1)}, u32[]{:S(2)}, u32[]{:S(2)}) %collective-permute-start.2) | collective-permute-done | bytes 393248 | tf_op jit(solution)/shard_map/ppermute | solution.py:38
  13.1 1.3 %collective-permute-start.7 = (bf16[192,640]{1,0:T(8,128)(2,1)S(1)}, bf16[192,640]{1,0:T(8,128)(2,1)S(1)}, u32[]{:S(2)}, u32[]{:S(2)}) collective-permute-start(bf16[192,640]{1,0:T(8,128)(2,1)S(1)} %get-tuple-element.39), channel_id=1, source_target_pairs={{0,12},{1,67},{16,28},{17,83},{32,44},{33,99},{48,60},{49,115},{4,... | collective-permute-start | bytes 737288 | tf_op jit(solution)/shard_map/ppermute | solution.py:38
  14.4 4.0 %collective-permute-done.3.refs_2_ = bf16[192,1024]{1,0:T(8,128)(2,1)S(1)} collective-permute-done((bf16[192,1024]{1,0:T(8,128)(2,1)S(1)}, bf16[192,1024]{1,0:T(8,128)(2,1)S(1)}, u32[]{:S(2)}, u32[]{:S(2)}) %collective-permute-start.3) | collective-permute-done | bytes 393248 | tf_op jit(solution)/shard_map/ppermute | solution.py:38
  18.4 1.6 %gram_native.1 = (f32[128,640]{1,0:T(8,128)S(1)}, bf16[128,640]{1,0:T(8,128)(2,1)S(1)}, bf16[128,640]{1,0:T(8,128)(2,1)S(1)}, bf16[128,640]{1,0:T(8,128)(2,1)S(1)}) custom-call(s32[3]{0:T(128)S(1)} %pad_add_fusion.places, bf16[192,1024]{1,0:T(8,128)(2,1)S(1)} %get-tuple-element.33.refs_0_, bf16[192,1024]{1,0:T(8,128)(2,1)S(1)} %collective-permute-done.2.refs_1_, ...), custom_call_target="tpu_custom_call" | custom-call | flops 503316480 | bytes 4194304 | tf_op jit(solution)/shard_map/gram_native/pallas_call | solution.py:231
  20.0 1.7 %collective-permute-start.17 = (bf16[128,640]{1,0:T(8,128)(2,1)S(1)}, bf16[128,640]{1,0:T(8,128)(2,1)S(1)}, u32[]{:S(2)}, u32[]{:S(2)}) collective-permute-start(bf16[128,640]{1,0:T(8,128)(2,1)S(1)} %get-tuple-element.45), channel_id=1, source_target_pairs={{0,2},{1,17},{16,18},{17,33},{32,34},{33,49},{48,50},{49,1},{4,6},... | collective-permute-start | bytes 491528 | tf_op jit(solution)/shard_map/ppermute | solution.py:38
  21.7 3.3 %collective-permute-start.18 = (bf16[128,640]{1,0:T(8,128)(2,1)S(1)}, bf16[128,640]{1,0:T(8,128)(2,1)S(1)}, u32[]{:S(2)}, u32[]{:S(2)}) collective-permute-start(bf16[128,640]{1,0:T(8,128)(2,1)S(1)} %get-tuple-element.46), channel_id=1, source_target_pairs={{0,64},{1,33},{16,80},{17,49},{32,96},{33,1},{48,112},{49,17},{4,6... | collective-permute-start | bytes 491528 | tf_op jit(solution)/shard_map/ppermute | solution.py:38
  25.1 0.7 collective-permute-start.19
  25.8 1.6 %gram_far.1 = (f32[128,640]{1,0:T(8,128)S(1)}, bf16[128,640]{1,0:T(8,128)(2,1)S(1)}, bf16[128,640]{1,0:T(8,128)(2,1)S(1)}, bf16[128,640]{1,0:T(8,128)(2,1)S(1)}) custom-call(s32[3]{0:T(128)S(1)} %pad_add_fusion.places, bf16[192,1024]{1,0:T(8,128)(2,1)S(1)} %get-tuple-element.33.refs_0_, bf16[192,1024]{1,0:T(8,128)(2,1)S(1)} %collective-permute-done.2.refs_1_, ...), custom_call_target="tpu_custom_call" | custom-call | flops 503316480 | bytes 4194304 | tf_op jit(solution)/shard_map/gram_far/pallas_call | solution.py:231
  27.4 2.6 %collective-permute-start.10 = (bf16[128,640]{1,0:T(8,128)(2,1)S(1)}, bf16[128,640]{1,0:T(8,128)(2,1)S(1)}, u32[]{:S(2)}, u32[]{:S(2)}) collective-permute-start(bf16[128,640]{1,0:T(8,128)(2,1)S(1)} %get-tuple-element.43), channel_id=1, source_target_pairs={{0,48},{1,13},{16,0},{17,29},{32,16},{33,45},{48,32},{49,61},{4,52... | collective-permute-start | bytes 491528 | tf_op jit(solution)/shard_map/ppermute | solution.py:38
  29.9 1.6 %collective-permute-start.9 = (bf16[128,640]{1,0:T(8,128)(2,1)S(1)}, bf16[128,640]{1,0:T(8,128)(2,1)S(1)}, u32[]{:S(2)}, u32[]{:S(2)}) collective-permute-start(bf16[128,640]{1,0:T(8,128)(2,1)S(1)} %get-tuple-element.42), channel_id=1, source_target_pairs={{0,32},{1,9},{16,48},{17,25},{32,0},{33,41},{48,16},{49,57},{4,36}... | collective-permute-start | bytes 491528 | tf_op jit(solution)/shard_map/ppermute | solution.py:38
  31.7 1.7 %collective-permute-start.20 = (bf16[128,640]{1,0:T(8,128)(2,1)S(1)}, bf16[128,640]{1,0:T(8,128)(2,1)S(1)}, u32[]{:S(2)}, u32[]{:S(2)}) collective-permute-start(bf16[128,640]{1,0:T(8,128)(2,1)S(1)} %fusion.9), channel_id=1, source_target_pairs={{0,16},{1,5},{16,32},{17,21},{32,48},{33,37},{48,0},{49,53},{4,20}... | collective-permute-start | bytes 491528 | tf_op jit(solution)/shard_map/ppermute | solution.py:38
  33.4 0.6 collective-permute-start.21
  34.0 1.9 %collective-permute-start.22 = (bf16[128,640]{1,0:T(8,128)(2,1)S(1)}, bf16[128,640]{1,0:T(8,128)(2,1)S(1)}, u32[]{:S(2)}, u32[]{:S(2)}) collective-permute-start(bf16[128,640]{1,0:T(8,128)(2,1)S(1)} %fusion.9), channel_id=1, source_target_pairs={{0,48},{1,13},{16,0},{17,29},{32,16},{33,45},{48,32},{49,61},{4,52... | collective-permute-start | bytes 491528 | tf_op jit(solution)/shard_map/ppermute | solution.py:38
  35.9 1.2 %collective-permute-done.8 = bf16[128,640]{1,0:T(8,128)(2,1)S(1)} collective-permute-done((bf16[128,640]{1,0:T(8,128)(2,1)S(1)}, bf16[128,640]{1,0:T(8,128)(2,1)S(1)}, u32[]{:S(2)}, u32[]{:S(2)}) %collective-permute-start.8) | collective-permute-done | bytes 163872 | tf_op jit(solution)/shard_map/ppermute | solution.py:38
  37.2 0.8 %collective-permute-start.11 = (bf16[128,640]{1,0:T(8,128)(2,1)S(1)}, bf16[128,640]{1,0:T(8,128)(2,1)S(1)}, u32[]{:S(2)}, u32[]{:S(2)}) collective-permute-start(bf16[128,640]{1,0:T(8,128)(2,1)S(1)} %fusion.8), channel_id=1, source_target_pairs={{0,2},{1,17},{16,18},{17,33},{32,34},{33,49},{48,50},{49,1},{4,6},... | collective-permute-start | bytes 491528 | tf_op jit(solution)/shard_map/ppermute | solution.py:38
  38.0 2.3 %collective-permute-start.12 = (bf16[128,640]{1,0:T(8,128)(2,1)S(1)}, bf16[128,640]{1,0:T(8,128)(2,1)S(1)}, u32[]{:S(2)}, u32[]{:S(2)}) collective-permute-start(bf16[128,640]{1,0:T(8,128)(2,1)S(1)} %fusion.8), channel_id=1, source_target_pairs={{0,64},{1,33},{16,80},{17,49},{32,96},{33,1},{48,112},{49,17},{4,6... | collective-permute-start | bytes 491528 | tf_op jit(solution)/shard_map/ppermute | solution.py:38
  40.3 0.6 collective-permute-done.20
  40.9 1.6 %collective-permute-start.13 = (bf16[128,640]{1,0:T(8,128)(2,1)S(1)}, bf16[128,640]{1,0:T(8,128)(2,1)S(1)}, u32[]{:S(2)}, u32[]{:S(2)}) collective-permute-start(bf16[128,640]{1,0:T(8,128)(2,1)S(1)} %fusion.8), channel_id=1, source_target_pairs={{0,66},{1,49},{16,82},{17,1},{32,98},{33,17},{48,114},{49,33},{4,7... | collective-permute-start | bytes 491528 | tf_op jit(solution)/shard_map/ppermute | solution.py:38
  42.7 1.2 %collective-permute-start.24 = (bf16[128,640]{1,0:T(8,128)(2,1)S(1)}, bf16[128,640]{1,0:T(8,128)(2,1)S(1)}, u32[]{:S(2)}, u32[]{:S(2)}) collective-permute-start(bf16[128,640]{1,0:T(8,128)(2,1)S(1)} %add_convert_fusion.refs_4_), channel_id=1, source_target_pairs={{0,64},{1,33},{16,80},{17,49},{32,96},{33,1},{48,112},{49,17},{4,6... | collective-permute-start | bytes 491528 | tf_op jit(solution)/shard_map/ppermute | solution.py:38
  43.9 4.2 %collective-permute-done.11 = bf16[128,640]{1,0:T(8,128)(2,1)S(1)} collective-permute-done((bf16[128,640]{1,0:T(8,128)(2,1)S(1)}, bf16[128,640]{1,0:T(8,128)(2,1)S(1)}, u32[]{:S(2)}, u32[]{:S(2)}) %collective-permute-start.11) | collective-permute-done | bytes 163872 | tf_op jit(solution)/shard_map/ppermute | solution.py:38
  48.3 2.6 %collective-permute-start.15 = (bf16[128,640]{1,0:T(8,128)(2,1)S(1)}, bf16[128,640]{1,0:T(8,128)(2,1)S(1)}, u32[]{:S(2)}, u32[]{:S(2)}) collective-permute-start(bf16[128,640]{1,0:T(8,128)(2,1)S(1)} %add_convert_fusion.1.refs_1_.refs_3_), channel_id=1, source_target_pairs={{0,32},{1,9},{16,48},{17,25},{32,0},{33,41},{48,16},{49,57},{4,36}... | collective-permute-start | bytes 491528 | tf_op jit(solution)/shard_map/ppermute | solution.py:38
  50.9 0.4 collective-permute-done.23.refs_5_
  51.3 1.9 %collective-permute-start.16 = (bf16[128,640]{1,0:T(8,128)(2,1)S(1)}, bf16[128,640]{1,0:T(8,128)(2,1)S(1)}, u32[]{:S(2)}, u32[]{:S(2)}) collective-permute-start(bf16[128,640]{1,0:T(8,128)(2,1)S(1)} %add_convert_fusion.1.refs_1_.refs_3_), channel_id=1, source_target_pairs={{0,48},{1,13},{16,0},{17,29},{32,16},{33,45},{48,32},{49,61},{4,52... | collective-permute-start | bytes 491528 | tf_op jit(solution)/shard_map/ppermute | solution.py:38
  53.2 1.4 %apply_native.1.refs_5_.refs_7_ = f32[768,512]{1,0:T(8,128)S(1)} custom-call(s32[3]{0:T(128)S(1)} %pad_add_fusion.places, bf16[192,1024]{1,0:T(8,128)(2,1)S(1)} %get-tuple-element.33.refs_0_, bf16[192,1024]{1,0:T(8,128)(2,1)S(1)} %collective-permute-done.2.refs_1_, bf16[192,1024]{1,0:T(8,128)(2,1)S(1)} %collective-permute-done.3.refs_2_, ...), custom_call_target="tpu_custom_call" | custom-call | flops 503316480 | bytes 4194304 | tf_op jit(solution)/shard_map/apply_native/pallas_call | solution.py:251
  54.6 1.1 %collective-permute-done.15.refs_3_.refs_5_ = bf16[128,640]{1,0:T(8,128)(2,1)S(1)} collective-permute-done((bf16[128,640]{1,0:T(8,128)(2,1)S(1)}, bf16[128,640]{1,0:T(8,128)(2,1)S(1)}, u32[]{:S(2)}, u32[]{:S(2)}) %collective-permute-start.15) | collective-permute-done | bytes 163872 | tf_op jit(solution)/shard_map/ppermute | solution.py:38
  55.7 0.6 collective-permute-done.16.refs_4_.refs_6_
  56.3 1.4 %apply_sent.1 = (bf16[192,512]{1,0:T(8,128)(2,1)S(1)}, bf16[192,512]{1,0:T(8,128)(2,1)S(1)}, bf16[192,512]{1,0:T(8,128)(2,1)S(1)}) custom-call(s32[3]{0:T(128)S(1)} %pad_add_fusion.places, bf16[192,640]{1,0:T(8,128)(2,1)S(1)} %collective-permute-done.5.refs_5_.refs_0_, bf16[192,640]{1,0:T(8,128)(2,1)S(1)} %collective-permute-done.6.refs_6_.refs_1_, ...), custom_call_target="tpu_custom_call" | custom-call | flops 377487360 | bytes 4194304 | tf_op jit(solution)/shard_map/apply_sent/pallas_call | solution.py:259
  57.7 0.6 collective-permute-start.26
  58.3 1.4 %collective-permute-start.27 = (bf16[192,512]{1,0:T(8,128)(2,1)S(1)}, bf16[192,512]{1,0:T(8,128)(2,1)S(1)}, u32[]{:S(2)}, u32[]{:S(2)}) collective-permute-start(bf16[192,512]{1,0:T(8,128)(2,1)S(1)} %get-tuple-element.49), channel_id=1, source_target_pairs={{0,8},{1,65},{16,24},{17,81},{32,40},{33,97},{48,56},{49,113},{4,1... | collective-permute-start | bytes 589832 | tf_op jit(solution)/shard_map/ppermute | solution.py:38
  59.7 1.0 %apply_kept.1 = f32[192,512]{1,0:T(8,128)S(1)} custom-call(s32[3]{0:T(128)S(1)} %pad_add_fusion.places, bf16[192,640]{1,0:T(8,128)(2,1)S(1)} %get-tuple-element.32.refs_4_.refs_0_, bf16[128,640]{1,0:T(8,128)(2,1)S(1)} %add_convert_fusion.1.refs_1_.refs_3_, bf16[128,640]{1,0:T(8,128)(2,1)S(1)} %collective-permute-done.14.refs_2_.refs_4_, ...), custom_call_target="tpu_custom_call" | custom-call | flops 125829120 | bytes 4194304 | tf_op jit(solution)/shard_map/apply_kept/pallas_call | solution.py:267
  60.7 1.8 %collective-permute-done.26 = bf16[192,512]{1,0:T(8,128)(2,1)S(1)} collective-permute-done((bf16[192,512]{1,0:T(8,128)(2,1)S(1)}, bf16[192,512]{1,0:T(8,128)(2,1)S(1)}, u32[]{:S(2)}, u32[]{:S(2)}) %collective-permute-start.26) | collective-permute-done | bytes 196640 | tf_op jit(solution)/shard_map/ppermute | solution.py:38
  62.5 1.9 %collective-permute-done.27 = bf16[192,512]{1,0:T(8,128)(2,1)S(1)} collective-permute-done((bf16[192,512]{1,0:T(8,128)(2,1)S(1)}, bf16[192,512]{1,0:T(8,128)(2,1)S(1)}, u32[]{:S(2)}, u32[]{:S(2)}) %collective-permute-start.27) | collective-permute-done | bytes 196640 | tf_op jit(solution)/shard_map/ppermute | solution.py:38
  64.4 2.0 %collective-permute-done.28 = bf16[192,512]{1,0:T(8,128)(2,1)S(1)} collective-permute-done((bf16[192,512]{1,0:T(8,128)(2,1)S(1)}, bf16[192,512]{1,0:T(8,128)(2,1)S(1)}, u32[]{:S(2)}, u32[]{:S(2)}) %collective-permute-start.28) | collective-permute-done | bytes 196640 | tf_op jit(solution)/shard_map/ppermute | solution.py:38
  66.4 0.2 fusion.5
  66.7 12.0 %collective-permute-start.29 = (f32[192]{0:T(256)S(1)}, f32[192]{0:T(256)S(1)}, u32[]{:S(2)}, u32[]{:S(2)}) collective-permute-start(f32[192]{0:T(256)S(1)} %fusion.5), channel_id=1, source_target_pairs={{0,1},{1,0},{2,3},{3,2},{4,5},{5,4},{6,7},{7,6},{8,9},{9,8},{10,11... | collective-permute-start | bytes 2312 | tf_op jit(solution)/shard_map/ppermute | solution.py:42
  78.7 0.7 collective-permute-done.29
  79.5 0.9 %fusion.7 = f32[192,512]{1,0:T(8,128)} fusion(f32[192]{0:T(256)S(1)} %reduce, f32[192]{0:T(256)S(1)} %add.85, bf16[192,1024]{1,0:T(8,128)(2,1)S(1)} %get-tuple-element.33.refs_0_, bf16[192,512]{1,0:T(8,128)(2,1)S(1)} %collective-permute-done.28, bf16[192,512]{1,0:T(8,128)(2,1)S(1)} %collective-permute-done.27, ...), kind=kLoop, calls=%fused_computation.10 | loop fusion | flops 1277952 | bytes 1574400 | tf_op jit(solution)/shard_map/mul | solution.py:280
  (33 shorter events, 0.9 us)
Async XLA Ops:
  0.0 3.8 %collective-permute-start.1 = (bf16[192,2048]{1,0:T(8,128)(2,1)}, bf16[192,2048]{1,0:T(8,128)(2,1)S(1)}, u32[]{:S(2)}, u32[]{:S(2)}) collective-permute-start(bf16[192,2048]{1,0:T(8,128)(2,1)} %t_own.3), channel_id=1, source_target_pairs={{0,1},{1,0},{2,3},{3,2},{4,5},{5,4},{6,7},{7,6},{8,9},{9,8},{10,11... | collective-permute-start | bytes 2359304 | tf_op jit(solution)/shard_map/ppermute | solution.py:42
  1.4 2.4 %collective-permute-start = (bf16[192,512]{1,0:T(8,128)(2,1)}, bf16[192,512]{1,0:T(8,128)(2,1)S(1)}, u32[]{:S(2)}, u32[]{:S(2)}) collective-permute-start(bf16[192,512]{1,0:T(8,128)(2,1)} %s_own.3), channel_id=1, source_target_pairs={{0,1},{1,0},{2,3},{3,2},{4,5},{5,4},{6,7},{7,6},{8,9},{9,8},{10,11... | collective-permute-start | bytes 589832 | tf_op jit(solution)/shard_map/ppermute | solution.py:42
  1.4 1.1 %copy-start = (bf16[192,2048]{1,0:T(8,128)(2,1)S(1)}, bf16[192,2048]{1,0:T(8,128)(2,1)}, u32[]{:S(2)}) copy-start(bf16[192,2048]{1,0:T(8,128)(2,1)} %t_own.3) | copy-start | bytes 2359300
  2.6 0.9 %copy-start.1 = (bf16[192,512]{1,0:T(8,128)(2,1)S(1)}, bf16[192,512]{1,0:T(8,128)(2,1)}, u32[]{:S(2)}) copy-start(bf16[192,512]{1,0:T(8,128)(2,1)} %s_own.3) | copy-start | bytes 589828
  4.9 8.2 %collective-permute-start.2 = (bf16[192,1024]{1,0:T(8,128)(2,1)S(1)}, bf16[192,1024]{1,0:T(8,128)(2,1)S(1)}, u32[]{:S(2)}, u32[]{:S(2)}) collective-permute-start(bf16[192,1024]{1,0:T(8,128)(2,1)S(1)} %get-tuple-element.34), channel_id=1, source_target_pairs={{0,4},{1,3},{16,20},{17,19},{32,36},{33,35},{48,52},{49,51},{4,8},... | collective-permute-start | bytes 1179656 | tf_op jit(solution)/shard_map/ppermute | solution.py:38
  6.2 12.2 %collective-permute-start.3 = (bf16[192,1024]{1,0:T(8,128)(2,1)S(1)}, bf16[192,1024]{1,0:T(8,128)(2,1)S(1)}, u32[]{:S(2)}, u32[]{:S(2)}) collective-permute-start(bf16[192,1024]{1,0:T(8,128)(2,1)S(1)} %get-tuple-element.35), channel_id=1, source_target_pairs={{0,8},{1,65},{16,24},{17,81},{32,40},{33,97},{48,56},{49,113},{4,1... | collective-permute-start | bytes 1179656 | tf_op jit(solution)/shard_map/ppermute | solution.py:38
  8.7 9.7 %collective-permute-start.4 = (bf16[192,1024]{1,0:T(8,128)(2,1)S(1)}, bf16[192,1024]{1,0:T(8,128)(2,1)S(1)}, u32[]{:S(2)}, u32[]{:S(2)}) collective-permute-start(bf16[192,1024]{1,0:T(8,128)(2,1)S(1)} %get-tuple-element.36), channel_id=1, source_target_pairs={{0,12},{1,67},{16,28},{17,83},{32,44},{33,99},{48,60},{49,115},{4,... | collective-permute-start | bytes 1179656 | tf_op jit(solution)/shard_map/ppermute | solution.py:38
  10.7 14.4 %collective-permute-start.5 = (bf16[192,640]{1,0:T(8,128)(2,1)S(1)}, bf16[192,640]{1,0:T(8,128)(2,1)S(1)}, u32[]{:S(2)}, u32[]{:S(2)}) collective-permute-start(bf16[192,640]{1,0:T(8,128)(2,1)S(1)} %get-tuple-element.37), channel_id=1, source_target_pairs={{0,4},{1,3},{16,20},{17,19},{32,36},{33,35},{48,52},{49,51},{4,8},... | collective-permute-start | bytes 737288 | tf_op jit(solution)/shard_map/ppermute | solution.py:38
  11.0 14.7 %collective-permute-start.6 = (bf16[192,640]{1,0:T(8,128)(2,1)S(1)}, bf16[192,640]{1,0:T(8,128)(2,1)S(1)}, u32[]{:S(2)}, u32[]{:S(2)}) collective-permute-start(bf16[192,640]{1,0:T(8,128)(2,1)S(1)} %get-tuple-element.38), channel_id=1, source_target_pairs={{0,8},{1,65},{16,24},{17,81},{32,40},{33,97},{48,56},{49,113},{4,1... | collective-permute-start | bytes 737288 | tf_op jit(solution)/shard_map/ppermute | solution.py:38
  13.1 12.7 %collective-permute-start.7 = (bf16[192,640]{1,0:T(8,128)(2,1)S(1)}, bf16[192,640]{1,0:T(8,128)(2,1)S(1)}, u32[]{:S(2)}, u32[]{:S(2)}) collective-permute-start(bf16[192,640]{1,0:T(8,128)(2,1)S(1)} %get-tuple-element.39), channel_id=1, source_target_pairs={{0,12},{1,67},{16,28},{17,83},{32,44},{33,99},{48,60},{49,115},{4,... | collective-permute-start | bytes 737288 | tf_op jit(solution)/shard_map/ppermute | solution.py:38
  20.0 9.9 %collective-permute-start.17 = (bf16[128,640]{1,0:T(8,128)(2,1)S(1)}, bf16[128,640]{1,0:T(8,128)(2,1)S(1)}, u32[]{:S(2)}, u32[]{:S(2)}) collective-permute-start(bf16[128,640]{1,0:T(8,128)(2,1)S(1)} %get-tuple-element.45), channel_id=1, source_target_pairs={{0,2},{1,17},{16,18},{17,33},{32,34},{33,49},{48,50},{49,1},{4,6},... | collective-permute-start | bytes 491528 | tf_op jit(solution)/shard_map/ppermute | solution.py:38
  21.7 9.8 %collective-permute-start.18 = (bf16[128,640]{1,0:T(8,128)(2,1)S(1)}, bf16[128,640]{1,0:T(8,128)(2,1)S(1)}, u32[]{:S(2)}, u32[]{:S(2)}) collective-permute-start(bf16[128,640]{1,0:T(8,128)(2,1)S(1)} %get-tuple-element.46), channel_id=1, source_target_pairs={{0,64},{1,33},{16,80},{17,49},{32,96},{33,1},{48,112},{49,17},{4,6... | collective-permute-start | bytes 491528 | tf_op jit(solution)/shard_map/ppermute | solution.py:38
  25.1 6.5 %collective-permute-start.19 = (bf16[128,640]{1,0:T(8,128)(2,1)S(1)}, bf16[128,640]{1,0:T(8,128)(2,1)S(1)}, u32[]{:S(2)}, u32[]{:S(2)}) collective-permute-start(bf16[128,640]{1,0:T(8,128)(2,1)S(1)} %get-tuple-element.47), channel_id=1, source_target_pairs={{0,66},{1,49},{16,82},{17,1},{32,98},{33,17},{48,114},{49,33},{4,7... | collective-permute-start | bytes 491528 | tf_op jit(solution)/shard_map/ppermute | solution.py:38
  27.4 6.6 %collective-permute-start.10 = (bf16[128,640]{1,0:T(8,128)(2,1)S(1)}, bf16[128,640]{1,0:T(8,128)(2,1)S(1)}, u32[]{:S(2)}, u32[]{:S(2)}) collective-permute-start(bf16[128,640]{1,0:T(8,128)(2,1)S(1)} %get-tuple-element.43), channel_id=1, source_target_pairs={{0,48},{1,13},{16,0},{17,29},{32,16},{33,45},{48,32},{49,61},{4,52... | collective-permute-start | bytes 491528 | tf_op jit(solution)/shard_map/ppermute | solution.py:38
  29.9 7.1 %collective-permute-start.8 = (bf16[128,640]{1,0:T(8,128)(2,1)S(1)}, bf16[128,640]{1,0:T(8,128)(2,1)S(1)}, u32[]{:S(2)}, u32[]{:S(2)}) collective-permute-start(bf16[128,640]{1,0:T(8,128)(2,1)S(1)} %get-tuple-element.41), channel_id=1, source_target_pairs={{0,16},{1,5},{16,32},{17,21},{32,48},{33,37},{48,0},{49,53},{4,20}... | collective-permute-start | bytes 491528 | tf_op jit(solution)/shard_map/ppermute | solution.py:38
  29.9 7.1 %collective-permute-start.9 = (bf16[128,640]{1,0:T(8,128)(2,1)S(1)}, bf16[128,640]{1,0:T(8,128)(2,1)S(1)}, u32[]{:S(2)}, u32[]{:S(2)}) collective-permute-start(bf16[128,640]{1,0:T(8,128)(2,1)S(1)} %get-tuple-element.42), channel_id=1, source_target_pairs={{0,32},{1,9},{16,48},{17,25},{32,0},{33,41},{48,16},{49,57},{4,36}... | collective-permute-start | bytes 491528 | tf_op jit(solution)/shard_map/ppermute | solution.py:38
  31.7 9.2 %collective-permute-start.20 = (bf16[128,640]{1,0:T(8,128)(2,1)S(1)}, bf16[128,640]{1,0:T(8,128)(2,1)S(1)}, u32[]{:S(2)}, u32[]{:S(2)}) collective-permute-start(bf16[128,640]{1,0:T(8,128)(2,1)S(1)} %fusion.9), channel_id=1, source_target_pairs={{0,16},{1,5},{16,32},{17,21},{32,48},{33,37},{48,0},{49,53},{4,20}... | collective-permute-start | bytes 491528 | tf_op jit(solution)/shard_map/ppermute | solution.py:38
  33.4 9.1 %collective-permute-start.21 = (bf16[128,640]{1,0:T(8,128)(2,1)S(1)}, bf16[128,640]{1,0:T(8,128)(2,1)S(1)}, u32[]{:S(2)}, u32[]{:S(2)}) collective-permute-start(bf16[128,640]{1,0:T(8,128)(2,1)S(1)} %fusion.9), channel_id=1, source_target_pairs={{0,32},{1,9},{16,48},{17,25},{32,0},{33,41},{48,16},{49,57},{4,36}... | collective-permute-start | bytes 491528 | tf_op jit(solution)/shard_map/ppermute | solution.py:38
  34.0 8.5 %collective-permute-start.22 = (bf16[128,640]{1,0:T(8,128)(2,1)S(1)}, bf16[128,640]{1,0:T(8,128)(2,1)S(1)}, u32[]{:S(2)}, u32[]{:S(2)}) collective-permute-start(bf16[128,640]{1,0:T(8,128)(2,1)S(1)} %fusion.9), channel_id=1, source_target_pairs={{0,48},{1,13},{16,0},{17,29},{32,16},{33,45},{48,32},{49,61},{4,52... | collective-permute-start | bytes 491528 | tf_op jit(solution)/shard_map/ppermute | solution.py:38
  37.2 10.9 %collective-permute-start.11 = (bf16[128,640]{1,0:T(8,128)(2,1)S(1)}, bf16[128,640]{1,0:T(8,128)(2,1)S(1)}, u32[]{:S(2)}, u32[]{:S(2)}) collective-permute-start(bf16[128,640]{1,0:T(8,128)(2,1)S(1)} %fusion.8), channel_id=1, source_target_pairs={{0,2},{1,17},{16,18},{17,33},{32,34},{33,49},{48,50},{49,1},{4,6},... | collective-permute-start | bytes 491528 | tf_op jit(solution)/shard_map/ppermute | solution.py:38
  38.0 10.1 %collective-permute-start.12 = (bf16[128,640]{1,0:T(8,128)(2,1)S(1)}, bf16[128,640]{1,0:T(8,128)(2,1)S(1)}, u32[]{:S(2)}, u32[]{:S(2)}) collective-permute-start(bf16[128,640]{1,0:T(8,128)(2,1)S(1)} %fusion.8), channel_id=1, source_target_pairs={{0,64},{1,33},{16,80},{17,49},{32,96},{33,1},{48,112},{49,17},{4,6... | collective-permute-start | bytes 491528 | tf_op jit(solution)/shard_map/ppermute | solution.py:38
  40.9 7.2 %collective-permute-start.13 = (bf16[128,640]{1,0:T(8,128)(2,1)S(1)}, bf16[128,640]{1,0:T(8,128)(2,1)S(1)}, u32[]{:S(2)}, u32[]{:S(2)}) collective-permute-start(bf16[128,640]{1,0:T(8,128)(2,1)S(1)} %fusion.8), channel_id=1, source_target_pairs={{0,66},{1,49},{16,82},{17,1},{32,98},{33,17},{48,114},{49,33},{4,7... | collective-permute-start | bytes 491528 | tf_op jit(solution)/shard_map/ppermute | solution.py:38
  42.6 8.6 %collective-permute-start.23 = (bf16[128,640]{1,0:T(8,128)(2,1)S(1)}, bf16[128,640]{1,0:T(8,128)(2,1)S(1)}, u32[]{:S(2)}, u32[]{:S(2)}) collective-permute-start(bf16[128,640]{1,0:T(8,128)(2,1)S(1)} %add_convert_fusion.refs_4_), channel_id=1, source_target_pairs={{0,2},{1,17},{16,18},{17,33},{32,34},{33,49},{48,50},{49,1},{4,6},... | collective-permute-start | bytes 491528 | tf_op jit(solution)/shard_map/ppermute | solution.py:38
  42.7 10.4 %collective-permute-start.24 = (bf16[128,640]{1,0:T(8,128)(2,1)S(1)}, bf16[128,640]{1,0:T(8,128)(2,1)S(1)}, u32[]{:S(2)}, u32[]{:S(2)}) collective-permute-start(bf16[128,640]{1,0:T(8,128)(2,1)S(1)} %add_convert_fusion.refs_4_), channel_id=1, source_target_pairs={{0,64},{1,33},{16,80},{17,49},{32,96},{33,1},{48,112},{49,17},{4,6... | collective-permute-start | bytes 491528 | tf_op jit(solution)/shard_map/ppermute | solution.py:38
  48.0 5.1 %collective-permute-start.25 = (bf16[128,640]{1,0:T(8,128)(2,1)S(1)}, bf16[128,640]{1,0:T(8,128)(2,1)S(1)}, u32[]{:S(2)}, u32[]{:S(2)}) collective-permute-start(bf16[128,640]{1,0:T(8,128)(2,1)S(1)} %add_convert_fusion.refs_4_), channel_id=1, source_target_pairs={{0,66},{1,49},{16,82},{17,1},{32,98},{33,17},{48,114},{49,33},{4,7... | collective-permute-start | bytes 491528 | tf_op jit(solution)/shard_map/ppermute | solution.py:38
  48.2 6.4 %collective-permute-start.14 = (bf16[128,640]{1,0:T(8,128)(2,1)S(1)}, bf16[128,640]{1,0:T(8,128)(2,1)S(1)}, u32[]{:S(2)}, u32[]{:S(2)}) collective-permute-start(bf16[128,640]{1,0:T(8,128)(2,1)S(1)} %add_convert_fusion.1.refs_1_.refs_3_), channel_id=1, source_target_pairs={{0,16},{1,5},{16,32},{17,21},{32,48},{33,37},{48,0},{49,53},{4,20}... | collective-permute-start | bytes 491528 | tf_op jit(solution)/shard_map/ppermute | solution.py:38
  48.3 7.4 %collective-permute-start.15 = (bf16[128,640]{1,0:T(8,128)(2,1)S(1)}, bf16[128,640]{1,0:T(8,128)(2,1)S(1)}, u32[]{:S(2)}, u32[]{:S(2)}) collective-permute-start(bf16[128,640]{1,0:T(8,128)(2,1)S(1)} %add_convert_fusion.1.refs_1_.refs_3_), channel_id=1, source_target_pairs={{0,32},{1,9},{16,48},{17,25},{32,0},{33,41},{48,16},{49,57},{4,36}... | collective-permute-start | bytes 491528 | tf_op jit(solution)/shard_map/ppermute | solution.py:38
  51.3 5.0 %collective-permute-start.16 = (bf16[128,640]{1,0:T(8,128)(2,1)S(1)}, bf16[128,640]{1,0:T(8,128)(2,1)S(1)}, u32[]{:S(2)}, u32[]{:S(2)}) collective-permute-start(bf16[128,640]{1,0:T(8,128)(2,1)S(1)} %add_convert_fusion.1.refs_1_.refs_3_), channel_id=1, source_target_pairs={{0,48},{1,13},{16,0},{17,29},{32,16},{33,45},{48,32},{49,61},{4,52... | collective-permute-start | bytes 491528 | tf_op jit(solution)/shard_map/ppermute | solution.py:38
  57.7 4.8 %collective-permute-start.26 = (bf16[192,512]{1,0:T(8,128)(2,1)S(1)}, bf16[192,512]{1,0:T(8,128)(2,1)S(1)}, u32[]{:S(2)}, u32[]{:S(2)}) collective-permute-start(bf16[192,512]{1,0:T(8,128)(2,1)S(1)} %get-tuple-element.48), channel_id=1, source_target_pairs={{0,12},{1,67},{16,28},{17,83},{32,44},{33,99},{48,60},{49,115},{4,... | collective-permute-start | bytes 589832 | tf_op jit(solution)/shard_map/ppermute | solution.py:38
  58.3 6.1 %collective-permute-start.27 = (bf16[192,512]{1,0:T(8,128)(2,1)S(1)}, bf16[192,512]{1,0:T(8,128)(2,1)S(1)}, u32[]{:S(2)}, u32[]{:S(2)}) collective-permute-start(bf16[192,512]{1,0:T(8,128)(2,1)S(1)} %get-tuple-element.49), channel_id=1, source_target_pairs={{0,8},{1,65},{16,24},{17,81},{32,40},{33,97},{48,56},{49,113},{4,1... | collective-permute-start | bytes 589832 | tf_op jit(solution)/shard_map/ppermute | solution.py:38
  59.7 6.7 %collective-permute-start.28 = (bf16[192,512]{1,0:T(8,128)(2,1)S(1)}, bf16[192,512]{1,0:T(8,128)(2,1)S(1)}, u32[]{:S(2)}, u32[]{:S(2)}) collective-permute-start(bf16[192,512]{1,0:T(8,128)(2,1)S(1)} %get-tuple-element.50), channel_id=1, source_target_pairs={{0,4},{1,3},{16,20},{17,19},{32,36},{33,35},{48,52},{49,51},{4,8},... | collective-permute-start | bytes 589832 | tf_op jit(solution)/shard_map/ppermute | solution.py:38
  66.7 12.8 %collective-permute-start.29 = (f32[192]{0:T(256)S(1)}, f32[192]{0:T(256)S(1)}, u32[]{:S(2)}, u32[]{:S(2)}) collective-permute-start(f32[192]{0:T(256)S(1)} %fusion.5), channel_id=1, source_target_pairs={{0,1},{1,0},{2,3},{3,2},{4,5},{5,4},{6,7},{7,6},{8,9},{9,8},{10,11... | collective-permute-start | bytes 2312 | tf_op jit(solution)/shard_map/ppermute | solution.py:42

commit v7 on v6

--- a/solution.py
+++ b/solution.py
@@ -15,6 +15,7 @@
 FIRST = ((X, Z), (Z, Y))
 SECOND = ((Z, Y), (X, Z))
 ORDER = (2, 1, 3)
+PAIRS = ((1, 3), (3, 1))
 STRIP = 32
 PARAMS = pltpu.CompilerParams(vmem_limit_bytes=40 * 1024 * 1024)
 SCALAR = pl.BlockSpec(memory_space=pltpu.SMEM)
@@ -27,15 +28,23 @@
     return (((x // 2) * SIZE + z) * 8 + y * 2 + x % 2) * 2 + core
 
 
-def shifted(array, axis_of_core, by):
+def moved(array, axis_of_core, place_of):
     pairs = []
     for chip in itertools.product(range(SIZE), repeat=3):
         for core in range(2):
             target = list(chip)
             axis = axis_of_core[core]
-            target[axis] = (target[axis] + by) % SIZE
+            target[axis] = place_of(target[axis])
             pairs.append((index_of(chip, core), index_of(target, core)))
     return lax.ppermute(array, AXES, pairs)
+
+
+def shifted(array, axis_of_core, by):
+    return moved(array, axis_of_core, lambda place: (place + by) % SIZE)
+
+
+def paired(array, axis_of_core, mask):
+    return moved(array, axis_of_core, lambda place: place ^ mask)
 
 
 def other_core(array):
@@ -241,8 +250,9 @@
             flops,
         )(places, *packs)
         total = added(own, lambda by: sends[by - 1], FIRST[chunk])
-        shared = total.astype(BF16)
-        piece = added(total, lambda by: shared, SECOND[chunk]).astype(BF16)
+        for mask in PAIRS[chunk]:
+            total = total + paired(total.astype(BF16), SECOND[chunk], mask).astype(F32)
+        piece = total.astype(BF16)
         return exchanged(piece, lambda by: piece, FIRST[chunk])
 
     near_weights = weights_of(0, near, "gram_native")
@@ -256,25 +266,21 @@
         [pltpu.VMEM((SIZE * rows, feats), BF16), pltpu.VMEM((half, feats), BF16)],
         flops,
     )(places, *near, *near_weights)[0]
-    parts = kernel_call(
-        functools.partial(apply_far_kernel, 1, SIZE - 1),
-        "apply_sent",
-        shapes(*[((rows, half), BF16)] * 3),
-        2 * SIZE,
-        [pltpu.VMEM((half, feats), BF16)],
-        flops * 3 // 4,
-    )(places, *far[1:], *far_weights, sofar)
-    grad_n = kernel_call(
-        functools.partial(apply_far_kernel, 0, 1),
-        "apply_kept",
-        shapes(((rows, half), F32)),
-        SIZE + 2,
-        [pltpu.VMEM((half, feats), BF16)],
-        flops // 4,
-    )(places, far[0], *far_weights, sofar)[0]
+    def last_product(by, dtype, name):
+        return kernel_call(
+            functools.partial(apply_far_kernel, by, 1),
+            name,
+            shapes(((rows, half), dtype)),
+            SIZE + 2,
+            [pltpu.VMEM((half, feats), BF16)],
+            flops // 4,
+        )(places, far[by], *far_weights, sofar)[0]
+
+    parts = {by: last_product(by, BF16, "apply_sent") for by in ORDER}
+    grad_n = last_product(0, F32, "apply_kept")
     norm_f = norm_own.astype(F32)
     grad_n = grad_n + level * norm_f
-    grad_n = coef * added(grad_n, lambda by: parts[by - 1], GATHER, -1)
+    grad_n = coef * added(grad_n, parts.__getitem__, GATHER, -1)
     inner = jnp.sum(grad_n * norm_f, axis=1)
     inner = inner + other_core(inner)
     return (grad_n - inner[:, None] * norm_f) * inv_s

time: 80.6 us -> 82 us (1.017)
  Pallas kernels: 9.08 us -> 10.5 us
    pallas_call x2 -> x4, Pallas kernels: 2.36 us -> 3.82 us  [last_product(): kernel_call(functools.partial(apply_far_kernel, by, 1), name, shapes(((ro...]
    ppermute x3, starting transfers between devices: 13.4 us -> 12 us  [other_core(): return lax.ppermute(array, 'sec', [(0, 1), (1, 0)])]
    ppermute x27 -> x25, starting transfers between devices: 34.2 us -> 35.1 us  [moved(): return lax.ppermute(array, AXES, pairs)]
    ppermute x27 -> x25, waiting for transfers between devices: 19 us -> 19.6 us  [moved(): return lax.ppermute(array, AXES, pairs)]
  transfers between devices with their start and end apart: 30 -> 28, of which waited for: 12 -> 11; matrix products, arithmetic and copies ran while one was open for 1% -> 1% of each run, Pallas kernels for 8% -> 10%
where the time goes in v7:
time: 82 us; the launch traced here: 81.8 us
  starting transfers between devices  47.1 us (57%)
  waiting for transfers between devices  20.3 us (25%)
  Pallas kernels  10.5 us (13%)
  local copies, waits for them, and re-layouts  2.06 us (3%)
  other arithmetic  1.72 us (2%)
    ppermute x25, starting transfers between devices, moved(): return lax.ppermute(array, AXES, pairs)  35.1 us
    ppermute x25, waiting for transfers between devices, moved(): return lax.ppermute(array, AXES, pairs)  19.6 us
    ppermute x3, starting transfers between devices, other_core(): return lax.ppermute(array, 'sec', [(0, 1), (1, 0)])  12 us
    pallas_call x4, Pallas kernels, last_product(): kernel_call(functools.partial(apply_far_kernel, by, 1), name, shapes(((ro...  3.82 us
    pallas_call x2, Pallas kernels, weights_of(): kernel_call(functools.partial(gram_kernel, level * SIZE / groups, chunk),...  3.19 us
    unnamed x4, local copies, waits for them, and re-layouts  2.06 us
  transfers between devices with their start and end apart: 28, of which 11 were waited for; matrix products, arithmetic and copies ran while one was open for 1% of the time, Pallas kernels for 10%

profile of v7, /device:TPU:1, one launch (start us, length us, event | category | flops | bytes accessed | tf_op | source)
XLA Modules:
  0.0 81.8 jit_solution(308168152755478993)
XLA Ops:
  0.0 1.4 %collective-permute-start.1 = (bf16[192,2048]{1,0:T(8,128)(2,1)}, bf16[192,2048]{1,0:T(8,128)(2,1)S(1)}, u32[]{:S(2)}, u32[]{:S(2)}) collective-permute-start(bf16[192,2048]{1,0:T(8,128)(2,1)} %t_own.3), channel_id=1, source_target_pairs={{0,1},{1,0},{2,3},{3,2},{4,5},{5,4},{6,7},{7,6},{8,9},{9,8},{10,11... | collective-permute-start | bytes 2359304 | tf_op jit(solution)/shard_map/ppermute | solution.py:51
  1.4 1.1 %copy-done = bf16[192,2048]{1,0:T(8,128)(2,1)S(1)} copy-done((bf16[192,2048]{1,0:T(8,128)(2,1)S(1)}, bf16[192,2048]{1,0:T(8,128)(2,1)}, u32[]{:S(2)}) %copy-start) | copy-done | bytes 786456
  2.6 0.9 %copy-done.1 = bf16[192,512]{1,0:T(8,128)(2,1)S(1)} copy-done((bf16[192,512]{1,0:T(8,128)(2,1)S(1)}, bf16[192,512]{1,0:T(8,128)(2,1)}, u32[]{:S(2)}) %copy-start.1) | copy-done | bytes 196632
  3.5 0.3 sums.1
  3.8 1.0 %pack_own.1 = (bf16[192,1024]{1,0:T(8,128)(2,1)S(1)}, bf16[192,1024]{1,0:T(8,128)(2,1)S(1)}, bf16[192,1024]{1,0:T(8,128)(2,1)S(1)}, bf16[192,1024]{1,0:T(8,128)(...) custom-call(s32[3]{0:T(128)S(1)} %pad_add_fusion.places, bf16[192,512]{1,0:T(8,128)(2,1)S(1)} %copy-done.1, ...), custom_call_target="tpu_custom_call" | custom-call | bytes 4194304 | tf_op jit(solution)/shard_map/pack_own/pallas_call | solution.py:216
  4.9 1.4 %collective-permute-start.2 = (bf16[192,1024]{1,0:T(8,128)(2,1)S(1)}, bf16[192,1024]{1,0:T(8,128)(2,1)S(1)}, u32[]{:S(2)}, u32[]{:S(2)}) collective-permute-start(bf16[192,1024]{1,0:T(8,128)(2,1)S(1)} %get-tuple-element.31), channel_id=1, source_target_pairs={{0,4},{1,3},{16,20},{17,19},{32,36},{33,35},{48,52},{49,51},{4,8},... | collective-permute-start | bytes 1179656 | tf_op jit(solution)/shard_map/ppermute | solution.py:39
  6.2 2.5 %collective-permute-start.3 = (bf16[192,1024]{1,0:T(8,128)(2,1)S(1)}, bf16[192,1024]{1,0:T(8,128)(2,1)S(1)}, u32[]{:S(2)}, u32[]{:S(2)}) collective-permute-start(bf16[192,1024]{1,0:T(8,128)(2,1)S(1)} %get-tuple-element.32), channel_id=1, source_target_pairs={{0,8},{1,65},{16,24},{17,81},{32,40},{33,97},{48,56},{49,113},{4,1... | collective-permute-start | bytes 1179656 | tf_op jit(solution)/shard_map/ppermute | solution.py:39
  8.7 1.2 %collective-permute-start.4 = (bf16[192,1024]{1,0:T(8,128)(2,1)S(1)}, bf16[192,1024]{1,0:T(8,128)(2,1)S(1)}, u32[]{:S(2)}, u32[]{:S(2)}) collective-permute-start(bf16[192,1024]{1,0:T(8,128)(2,1)S(1)} %get-tuple-element.33), channel_id=1, source_target_pairs={{0,12},{1,67},{16,28},{17,83},{32,44},{33,99},{48,60},{49,115},{4,... | collective-permute-start | bytes 1179656 | tf_op jit(solution)/shard_map/ppermute | solution.py:39
  9.8 0.8 pack_far.1
  10.7 0.4 collective-permute-start.5
  11.0 0.9 %collective-permute-start.6 = (bf16[192,640]{1,0:T(8,128)(2,1)S(1)}, bf16[192,640]{1,0:T(8,128)(2,1)S(1)}, u32[]{:S(2)}, u32[]{:S(2)}) collective-permute-start(bf16[192,640]{1,0:T(8,128)(2,1)S(1)} %get-tuple-element.35), channel_id=1, source_target_pairs={{0,8},{1,65},{16,24},{17,81},{32,40},{33,97},{48,56},{49,113},{4,1... | collective-permute-start | bytes 737288 | tf_op jit(solution)/shard_map/ppermute | solution.py:39
  11.9 1.2 %collective-permute-done.2.refs_1_ = bf16[192,1024]{1,0:T(8,128)(2,1)S(1)} collective-permute-done((bf16[192,1024]{1,0:T(8,128)(2,1)S(1)}, bf16[192,1024]{1,0:T(8,128)(2,1)S(1)}, u32[]{:S(2)}, u32[]{:S(2)}) %collective-permute-start.2) | collective-permute-done | bytes 393248 | tf_op jit(solution)/shard_map/ppermute | solution.py:39
  13.1 1.3 %collective-permute-start.7 = (bf16[192,640]{1,0:T(8,128)(2,1)S(1)}, bf16[192,640]{1,0:T(8,128)(2,1)S(1)}, u32[]{:S(2)}, u32[]{:S(2)}) collective-permute-start(bf16[192,640]{1,0:T(8,128)(2,1)S(1)} %get-tuple-element.36), channel_id=1, source_target_pairs={{0,12},{1,67},{16,28},{17,83},{32,44},{33,99},{48,60},{49,115},{4,... | collective-permute-start | bytes 737288 | tf_op jit(solution)/shard_map/ppermute | solution.py:39
  14.4 4.0 %collective-permute-done.3.refs_2_ = bf16[192,1024]{1,0:T(8,128)(2,1)S(1)} collective-permute-done((bf16[192,1024]{1,0:T(8,128)(2,1)S(1)}, bf16[192,1024]{1,0:T(8,128)(2,1)S(1)}, u32[]{:S(2)}, u32[]{:S(2)}) %collective-permute-start.3) | collective-permute-done | bytes 393248 | tf_op jit(solution)/shard_map/ppermute | solution.py:39
  18.4 1.6 %gram_native.1 = (f32[128,640]{1,0:T(8,128)S(1)}, bf16[128,640]{1,0:T(8,128)(2,1)S(1)}, bf16[128,640]{1,0:T(8,128)(2,1)S(1)}, bf16[128,640]{1,0:T(8,128)(2,1)S(1)}) custom-call(s32[3]{0:T(128)S(1)} %pad_add_fusion.places, bf16[192,1024]{1,0:T(8,128)(2,1)S(1)} %get-tuple-element.30.refs_0_, bf16[192,1024]{1,0:T(8,128)(2,1)S(1)} %collective-permute-done.2.refs_1_, ...), custom_call_target="tpu_custom_call" | custom-call | flops 503316480 | bytes 4194304 | tf_op jit(solution)/shard_map/gram_native/pallas_call | solution.py:240
  20.0 1.7 %collective-permute-start.16 = (bf16[128,640]{1,0:T(8,128)(2,1)S(1)}, bf16[128,640]{1,0:T(8,128)(2,1)S(1)}, u32[]{:S(2)}, u32[]{:S(2)}) collective-permute-start(bf16[128,640]{1,0:T(8,128)(2,1)S(1)} %get-tuple-element.42), channel_id=1, source_target_pairs={{0,2},{1,17},{16,18},{17,33},{32,34},{33,49},{48,50},{49,1},{4,6},... | collective-permute-start | bytes 491528 | tf_op jit(solution)/shard_map/ppermute | solution.py:39
  21.7 3.3 %collective-permute-start.17 = (bf16[128,640]{1,0:T(8,128)(2,1)S(1)}, bf16[128,640]{1,0:T(8,128)(2,1)S(1)}, u32[]{:S(2)}, u32[]{:S(2)}) collective-permute-start(bf16[128,640]{1,0:T(8,128)(2,1)S(1)} %get-tuple-element.43), channel_id=1, source_target_pairs={{0,64},{1,33},{16,80},{17,49},{32,96},{33,1},{48,112},{49,17},{4,6... | collective-permute-start | bytes 491528 | tf_op jit(solution)/shard_map/ppermute | solution.py:39
  25.1 0.7 collective-permute-start.18
  25.8 1.6 %gram_far.1 = (f32[128,640]{1,0:T(8,128)S(1)}, bf16[128,640]{1,0:T(8,128)(2,1)S(1)}, bf16[128,640]{1,0:T(8,128)(2,1)S(1)}, bf16[128,640]{1,0:T(8,128)(2,1)S(1)}) custom-call(s32[3]{0:T(128)S(1)} %pad_add_fusion.places, bf16[192,1024]{1,0:T(8,128)(2,1)S(1)} %get-tuple-element.30.refs_0_, bf16[192,1024]{1,0:T(8,128)(2,1)S(1)} %collective-permute-done.2.refs_1_, ...), custom_call_target="tpu_custom_call" | custom-call | flops 503316480 | bytes 4194304 | tf_op jit(solution)/shard_map/gram_far/pallas_call | solution.py:240
  27.4 2.6 %collective-permute-start.10 = (bf16[128,640]{1,0:T(8,128)(2,1)S(1)}, bf16[128,640]{1,0:T(8,128)(2,1)S(1)}, u32[]{:S(2)}, u32[]{:S(2)}) collective-permute-start(bf16[128,640]{1,0:T(8,128)(2,1)S(1)} %get-tuple-element.40), channel_id=1, source_target_pairs={{0,48},{1,13},{16,0},{17,29},{32,16},{33,45},{48,32},{49,61},{4,52... | collective-permute-start | bytes 491528 | tf_op jit(solution)/shard_map/ppermute | solution.py:39
  29.9 1.6 %collective-permute-start.9 = (bf16[128,640]{1,0:T(8,128)(2,1)S(1)}, bf16[128,640]{1,0:T(8,128)(2,1)S(1)}, u32[]{:S(2)}, u32[]{:S(2)}) collective-permute-start(bf16[128,640]{1,0:T(8,128)(2,1)S(1)} %get-tuple-element.39), channel_id=1, source_target_pairs={{0,32},{1,9},{16,48},{17,25},{32,0},{33,41},{48,16},{49,57},{4,36}... | collective-permute-start | bytes 491528 | tf_op jit(solution)/shard_map/ppermute | solution.py:39
  31.7 1.7 %collective-permute-start.19 = (bf16[128,640]{1,0:T(8,128)(2,1)S(1)}, bf16[128,640]{1,0:T(8,128)(2,1)S(1)}, u32[]{:S(2)}, u32[]{:S(2)}) collective-permute-start(bf16[128,640]{1,0:T(8,128)(2,1)S(1)} %get-tuple-element.45), channel_id=1, source_target_pairs={{0,16},{1,5},{16,0},{17,21},{32,48},{33,37},{48,32},{49,53},{4,20}... | collective-permute-start | bytes 491528 | tf_op jit(solution)/shard_map/ppermute | solution.py:39
  33.4 3.7 %collective-permute-done.8 = bf16[128,640]{1,0:T(8,128)(2,1)S(1)} collective-permute-done((bf16[128,640]{1,0:T(8,128)(2,1)S(1)}, bf16[128,640]{1,0:T(8,128)(2,1)S(1)}, u32[]{:S(2)}, u32[]{:S(2)}) %collective-permute-start.8) | collective-permute-done | bytes 163872 | tf_op jit(solution)/shard_map/ppermute | solution.py:39
  37.2 2.0 %collective-permute-start.11 = (bf16[128,640]{1,0:T(8,128)(2,1)S(1)}, bf16[128,640]{1,0:T(8,128)(2,1)S(1)}, u32[]{:S(2)}, u32[]{:S(2)}) collective-permute-start(bf16[128,640]{1,0:T(8,128)(2,1)S(1)} %get-tuple-element.47), channel_id=1, source_target_pairs={{0,66},{1,49},{16,82},{17,33},{32,98},{33,17},{48,114},{49,1},{4,7... | collective-permute-start | bytes 491528 | tf_op jit(solution)/shard_map/ppermute | solution.py:39
  39.2 1.0 %collective-permute-start.20 = (bf16[128,640]{1,0:T(8,128)(2,1)S(1)}, bf16[128,640]{1,0:T(8,128)(2,1)S(1)}, u32[]{:S(2)}, u32[]{:S(2)}) collective-permute-start(bf16[128,640]{1,0:T(8,128)(2,1)S(1)} %fusion.9), channel_id=1, source_target_pairs={{0,48},{1,13},{16,32},{17,29},{32,16},{33,45},{48,0},{49,61},{4,52... | collective-permute-start | bytes 491528 | tf_op jit(solution)/shard_map/ppermute | solution.py:39
  40.2 2.4 %collective-permute-done.11 = bf16[128,640]{1,0:T(8,128)(2,1)S(1)} collective-permute-done((bf16[128,640]{1,0:T(8,128)(2,1)S(1)}, bf16[128,640]{1,0:T(8,128)(2,1)S(1)}, u32[]{:S(2)}, u32[]{:S(2)}) %collective-permute-start.11) | collective-permute-done | bytes 163872 | tf_op jit(solution)/shard_map/ppermute | solution.py:39
  42.8 1.9 %collective-permute-done.20 = bf16[128,640]{1,0:T(8,128)(2,1)S(1)} collective-permute-done((bf16[128,640]{1,0:T(8,128)(2,1)S(1)}, bf16[128,640]{1,0:T(8,128)(2,1)S(1)}, u32[]{:S(2)}, u32[]{:S(2)}) %collective-permute-start.20) | collective-permute-done | bytes 163872 | tf_op jit(solution)/shard_map/ppermute | solution.py:39
  44.8 2.0 %collective-permute-start.22 = (bf16[128,640]{1,0:T(8,128)(2,1)S(1)}, bf16[128,640]{1,0:T(8,128)(2,1)S(1)}, u32[]{:S(2)}, u32[]{:S(2)}) collective-permute-start(bf16[128,640]{1,0:T(8,128)(2,1)S(1)} %add_convert_fusion.refs_4_), channel_id=1, source_target_pairs={{0,64},{1,33},{16,80},{17,49},{32,96},{33,1},{48,112},{49,17},{4,6... | collective-permute-start | bytes 491528 | tf_op jit(solution)/shard_map/ppermute | solution.py:39
  46.7 1.3 %collective-permute-start.23 = (bf16[128,640]{1,0:T(8,128)(2,1)S(1)}, bf16[128,640]{1,0:T(8,128)(2,1)S(1)}, u32[]{:S(2)}, u32[]{:S(2)}) collective-permute-start(bf16[128,640]{1,0:T(8,128)(2,1)S(1)} %add_convert_fusion.refs_4_), channel_id=1, source_target_pairs={{0,66},{1,49},{16,82},{17,1},{32,98},{33,17},{48,114},{49,33},{4,7... | collective-permute-start | bytes 491528 | tf_op jit(solution)/shard_map/ppermute | solution.py:39
  48.1 0.4 collective-permute-start.13
  48.4 2.3 %collective-permute-start.14 = (bf16[128,640]{1,0:T(8,128)(2,1)S(1)}, bf16[128,640]{1,0:T(8,128)(2,1)S(1)}, u32[]{:S(2)}, u32[]{:S(2)}) collective-permute-start(bf16[128,640]{1,0:T(8,128)(2,1)S(1)} %add_convert_fusion.1.refs_1_), channel_id=1, source_target_pairs={{0,32},{1,9},{16,48},{17,25},{32,0},{33,41},{48,16},{49,57},{4,36}... | collective-permute-start | bytes 491528 | tf_op jit(solution)/shard_map/ppermute | solution.py:39
  50.7 2.9 %collective-permute-start.15 = (bf16[128,640]{1,0:T(8,128)(2,1)S(1)}, bf16[128,640]{1,0:T(8,128)(2,1)S(1)}, u32[]{:S(2)}, u32[]{:S(2)}) collective-permute-start(bf16[128,640]{1,0:T(8,128)(2,1)S(1)} %add_convert_fusion.1.refs_1_), channel_id=1, source_target_pairs={{0,48},{1,13},{16,0},{17,29},{32,16},{33,45},{48,32},{49,61},{4,52... | collective-permute-start | bytes 491528 | tf_op jit(solution)/shard_map/ppermute | solution.py:39
  53.6 1.4 %apply_native.1.refs_5_ = f32[768,512]{1,0:T(8,128)S(1)} custom-call(s32[3]{0:T(128)S(1)} %pad_add_fusion.places, bf16[192,1024]{1,0:T(8,128)(2,1)S(1)} %get-tuple-element.30.refs_0_, bf16[192,1024]{1,0:T(8,128)(2,1)S(1)} %collective-permute-done.2.refs_1_, bf16[192,1024]{1,0:T(8,128)(2,1)S(1)} %collective-permute-done.3.refs_2_, ...), custom_call_target="tpu_custom_call" | custom-call | flops 503316480 | bytes 4194304 | tf_op jit(solution)/shard_map/apply_native/pallas_call | solution.py:261
  55.1 0.2 collective-permute-done.13.refs_2_
  55.3 0.9 %collective-permute-done.15.refs_4_ = bf16[128,640]{1,0:T(8,128)(2,1)S(1)} collective-permute-done((bf16[128,640]{1,0:T(8,128)(2,1)S(1)}, bf16[128,640]{1,0:T(8,128)(2,1)S(1)}, u32[]{:S(2)}, u32[]{:S(2)}) %collective-permute-start.15) | collective-permute-done | bytes 163872 | tf_op jit(solution)/shard_map/ppermute | solution.py:39
  56.2 1.0 %apply_sent.3 = bf16[192,512]{1,0:T(8,128)(2,1)S(1)} custom-call(s32[3]{0:T(128)S(1)} %pad_add_fusion.places, bf16[192,640]{1,0:T(8,128)(2,1)S(1)} %collective-permute-done.5.refs_5_.refs_0_, bf16[128,640]{1,0:T(8,128)(2,1)S(1)} %add_convert_fusion.1.refs_1_, bf16[128,640]{1,0:T(8,128)(2,1)S(1)} %collective-permute-done.13.refs_2_, ...), custom_call_target="tpu_custom_call" | custom-call | flops 125829120 | bytes 4194304 | tf_op jit(solution)/shard_map/apply_sent/pallas_call | solution.py:270
  57.1 3.0 %collective-permute-start.24 = (bf16[192,512]{1,0:T(8,128)(2,1)S(1)}, bf16[192,512]{1,0:T(8,128)(2,1)S(1)}, u32[]{:S(2)}, u32[]{:S(2)}) collective-permute-start(bf16[192,512]{1,0:T(8,128)(2,1)S(1)} %apply_sent.3), channel_id=1, source_target_pairs={{0,12},{1,67},{16,28},{17,83},{32,44},{33,99},{48,60},{49,115},{4,... | collective-permute-start | bytes 589832 | tf_op jit(solution)/shard_map/ppermute | solution.py:39
  60.1 1.0 %apply_sent.4 = bf16[192,512]{1,0:T(8,128)(2,1)S(1)} custom-call(s32[3]{0:T(128)S(1)} %pad_add_fusion.places, bf16[192,640]{1,0:T(8,128)(2,1)S(1)} %collective-permute-done.6.refs_6_.refs_0_, bf16[128,640]{1,0:T(8,128)(2,1)S(1)} %add_convert_fusion.1.refs_1_, bf16[128,640]{1,0:T(8,128)(2,1)S(1)} %collective-permute-done.13.refs_2_, ...), custom_call_target="tpu_custom_call" | custom-call | flops 125829120 | bytes 4194304 | tf_op jit(solution)/shard_map/apply_sent/pallas_call | solution.py:270
  61.2 1.0 %apply_sent.5 = bf16[192,512]{1,0:T(8,128)(2,1)S(1)} custom-call(s32[3]{0:T(128)S(1)} %pad_add_fusion.places, bf16[192,640]{1,0:T(8,128)(2,1)S(1)} %collective-permute-done.7.refs_7_.refs_0_, bf16[128,640]{1,0:T(8,128)(2,1)S(1)} %add_convert_fusion.1.refs_1_, bf16[128,640]{1,0:T(8,128)(2,1)S(1)} %collective-permute-done.13.refs_2_, ...), custom_call_target="tpu_custom_call" | custom-call | flops 125829120 | bytes 4194304 | tf_op jit(solution)/shard_map/apply_sent/pallas_call | solution.py:270
  62.2 0.9 %collective-permute-start.26 = (bf16[192,512]{1,0:T(8,128)(2,1)S(1)}, bf16[192,512]{1,0:T(8,128)(2,1)S(1)}, u32[]{:S(2)}, u32[]{:S(2)}) collective-permute-start(bf16[192,512]{1,0:T(8,128)(2,1)S(1)} %apply_sent.5), channel_id=1, source_target_pairs={{0,4},{1,3},{16,20},{17,19},{32,36},{33,35},{48,52},{49,51},{4,8},... | collective-permute-start | bytes 589832 | tf_op jit(solution)/shard_map/ppermute | solution.py:39
  63.0 1.0 %apply_kept.1 = f32[192,512]{1,0:T(8,128)S(1)} custom-call(s32[3]{0:T(128)S(1)} %pad_add_fusion.places, bf16[192,640]{1,0:T(8,128)(2,1)S(1)} %get-tuple-element.29.refs_4_.refs_0_, bf16[128,640]{1,0:T(8,128)(2,1)S(1)} %add_convert_fusion.1.refs_1_, bf16[128,640]{1,0:T(8,128)(2,1)S(1)} %collective-permute-done.13.refs_2_, ...), custom_call_target="tpu_custom_call" | custom-call | flops 125829120 | bytes 4194304 | tf_op jit(solution)/shard_map/apply_kept/pallas_call | solution.py:270
  64.0 0.8 %collective-permute-done.24 = bf16[192,512]{1,0:T(8,128)(2,1)S(1)} collective-permute-done((bf16[192,512]{1,0:T(8,128)(2,1)S(1)}, bf16[192,512]{1,0:T(8,128)(2,1)S(1)}, u32[]{:S(2)}, u32[]{:S(2)}) %collective-permute-start.24) | collective-permute-done | bytes 196640 | tf_op jit(solution)/shard_map/ppermute | solution.py:39
  64.8 2.4 %collective-permute-done.25 = bf16[192,512]{1,0:T(8,128)(2,1)S(1)} collective-permute-done((bf16[192,512]{1,0:T(8,128)(2,1)S(1)}, bf16[192,512]{1,0:T(8,128)(2,1)S(1)}, u32[]{:S(2)}, u32[]{:S(2)}) %collective-permute-start.25) | collective-permute-done | bytes 196640 | tf_op jit(solution)/shard_map/ppermute | solution.py:39
  67.3 2.0 %collective-permute-done.26 = bf16[192,512]{1,0:T(8,128)(2,1)S(1)} collective-permute-done((bf16[192,512]{1,0:T(8,128)(2,1)S(1)}, bf16[192,512]{1,0:T(8,128)(2,1)S(1)}, u32[]{:S(2)}, u32[]{:S(2)}) %collective-permute-start.26) | collective-permute-done | bytes 196640 | tf_op jit(solution)/shard_map/ppermute | solution.py:39
  69.3 0.2 fusion.5
  69.5 10.5 %collective-permute-start.27 = (f32[192]{0:T(256)S(1)}, f32[192]{0:T(256)S(1)}, u32[]{:S(2)}, u32[]{:S(2)}) collective-permute-start(f32[192]{0:T(256)S(1)} %fusion.5), channel_id=1, source_target_pairs={{0,1},{1,0},{2,3},{3,2},{4,5},{5,4},{6,7},{7,6},{8,9},{9,8},{10,11... | collective-permute-start | bytes 2312 | tf_op jit(solution)/shard_map/ppermute | solution.py:51
  80.2 0.7 collective-permute-done.27
  80.9 0.9 %fusion.7 = f32[192,512]{1,0:T(8,128)} fusion(f32[192]{0:T(256)S(1)} %reduce, f32[192]{0:T(256)S(1)} %add.77, bf16[192,1024]{1,0:T(8,128)(2,1)S(1)} %get-tuple-element.30.refs_0_, bf16[192,512]{1,0:T(8,128)(2,1)S(1)} %collective-permute-done.26, bf16[192,512]{1,0:T(8,128)(2,1)S(1)} %collective-permute-done.25, ...), kind=kLoop, calls=%fused_computation.10 | loop fusion | flops 1277952 | bytes 1574400 | tf_op jit(solution)/shard_map/mul | solution.py:286
  (33 shorter events, 0.9 us)
Async XLA Ops:
  0.0 3.8 %collective-permute-start.1 = (bf16[192,2048]{1,0:T(8,128)(2,1)}, bf16[192,2048]{1,0:T(8,128)(2,1)S(1)}, u32[]{:S(2)}, u32[]{:S(2)}) collective-permute-start(bf16[192,2048]{1,0:T(8,128)(2,1)} %t_own.3), channel_id=1, source_target_pairs={{0,1},{1,0},{2,3},{3,2},{4,5},{5,4},{6,7},{7,6},{8,9},{9,8},{10,11... | collective-permute-start | bytes 2359304 | tf_op jit(solution)/shard_map/ppermute | solution.py:51
  1.4 2.4 %collective-permute-start = (bf16[192,512]{1,0:T(8,128)(2,1)}, bf16[192,512]{1,0:T(8,128)(2,1)S(1)}, u32[]{:S(2)}, u32[]{:S(2)}) collective-permute-start(bf16[192,512]{1,0:T(8,128)(2,1)} %s_own.3), channel_id=1, source_target_pairs={{0,1},{1,0},{2,3},{3,2},{4,5},{5,4},{6,7},{7,6},{8,9},{9,8},{10,11... | collective-permute-start | bytes 589832 | tf_op jit(solution)/shard_map/ppermute | solution.py:51
  1.4 1.1 %copy-start = (bf16[192,2048]{1,0:T(8,128)(2,1)S(1)}, bf16[192,2048]{1,0:T(8,128)(2,1)}, u32[]{:S(2)}) copy-start(bf16[192,2048]{1,0:T(8,128)(2,1)} %t_own.3) | copy-start | bytes 2359300
  2.6 0.9 %copy-start.1 = (bf16[192,512]{1,0:T(8,128)(2,1)S(1)}, bf16[192,512]{1,0:T(8,128)(2,1)}, u32[]{:S(2)}) copy-start(bf16[192,512]{1,0:T(8,128)(2,1)} %s_own.3) | copy-start | bytes 589828
  4.9 8.2 %collective-permute-start.2 = (bf16[192,1024]{1,0:T(8,128)(2,1)S(1)}, bf16[192,1024]{1,0:T(8,128)(2,1)S(1)}, u32[]{:S(2)}, u32[]{:S(2)}) collective-permute-start(bf16[192,1024]{1,0:T(8,128)(2,1)S(1)} %get-tuple-element.31), channel_id=1, source_target_pairs={{0,4},{1,3},{16,20},{17,19},{32,36},{33,35},{48,52},{49,51},{4,8},... | collective-permute-start | bytes 1179656 | tf_op jit(solution)/shard_map/ppermute | solution.py:39
  6.2 12.2 %collective-permute-start.3 = (bf16[192,1024]{1,0:T(8,128)(2,1)S(1)}, bf16[192,1024]{1,0:T(8,128)(2,1)S(1)}, u32[]{:S(2)}, u32[]{:S(2)}) collective-permute-start(bf16[192,1024]{1,0:T(8,128)(2,1)S(1)} %get-tuple-element.32), channel_id=1, source_target_pairs={{0,8},{1,65},{16,24},{17,81},{32,40},{33,97},{48,56},{49,113},{4,1... | collective-permute-start | bytes 1179656 | tf_op jit(solution)/shard_map/ppermute | solution.py:39
  8.7 9.7 %collective-permute-start.4 = (bf16[192,1024]{1,0:T(8,128)(2,1)S(1)}, bf16[192,1024]{1,0:T(8,128)(2,1)S(1)}, u32[]{:S(2)}, u32[]{:S(2)}) collective-permute-start(bf16[192,1024]{1,0:T(8,128)(2,1)S(1)} %get-tuple-element.33), channel_id=1, source_target_pairs={{0,12},{1,67},{16,28},{17,83},{32,44},{33,99},{48,60},{49,115},{4,... | collective-permute-start | bytes 1179656 | tf_op jit(solution)/shard_map/ppermute | solution.py:39
  10.7 14.4 %collective-permute-start.5 = (bf16[192,640]{1,0:T(8,128)(2,1)S(1)}, bf16[192,640]{1,0:T(8,128)(2,1)S(1)}, u32[]{:S(2)}, u32[]{:S(2)}) collective-permute-start(bf16[192,640]{1,0:T(8,128)(2,1)S(1)} %get-tuple-element.34), channel_id=1, source_target_pairs={{0,4},{1,3},{16,20},{17,19},{32,36},{33,35},{48,52},{49,51},{4,8},... | collective-permute-start | bytes 737288 | tf_op jit(solution)/shard_map/ppermute | solution.py:39
  11.0 14.7 %collective-permute-start.6 = (bf16[192,640]{1,0:T(8,128)(2,1)S(1)}, bf16[192,640]{1,0:T(8,128)(2,1)S(1)}, u32[]{:S(2)}, u32[]{:S(2)}) collective-permute-start(bf16[192,640]{1,0:T(8,128)(2,1)S(1)} %get-tuple-element.35), channel_id=1, source_target_pairs={{0,8},{1,65},{16,24},{17,81},{32,40},{33,97},{48,56},{49,113},{4,1... | collective-permute-start | bytes 737288 | tf_op jit(solution)/shard_map/ppermute | solution.py:39
  13.1 12.7 %collective-permute-start.7 = (bf16[192,640]{1,0:T(8,128)(2,1)S(1)}, bf16[192,640]{1,0:T(8,128)(2,1)S(1)}, u32[]{:S(2)}, u32[]{:S(2)}) collective-permute-start(bf16[192,640]{1,0:T(8,128)(2,1)S(1)} %get-tuple-element.36), channel_id=1, source_target_pairs={{0,12},{1,67},{16,28},{17,83},{32,44},{33,99},{48,60},{49,115},{4,... | collective-permute-start | bytes 737288 | tf_op jit(solution)/shard_map/ppermute | solution.py:39
  20.0 9.9 %collective-permute-start.16 = (bf16[128,640]{1,0:T(8,128)(2,1)S(1)}, bf16[128,640]{1,0:T(8,128)(2,1)S(1)}, u32[]{:S(2)}, u32[]{:S(2)}) collective-permute-start(bf16[128,640]{1,0:T(8,128)(2,1)S(1)} %get-tuple-element.42), channel_id=1, source_target_pairs={{0,2},{1,17},{16,18},{17,33},{32,34},{33,49},{48,50},{49,1},{4,6},... | collective-permute-start | bytes 491528 | tf_op jit(solution)/shard_map/ppermute | solution.py:39
  21.7 9.8 %collective-permute-start.17 = (bf16[128,640]{1,0:T(8,128)(2,1)S(1)}, bf16[128,640]{1,0:T(8,128)(2,1)S(1)}, u32[]{:S(2)}, u32[]{:S(2)}) collective-permute-start(bf16[128,640]{1,0:T(8,128)(2,1)S(1)} %get-tuple-element.43), channel_id=1, source_target_pairs={{0,64},{1,33},{16,80},{17,49},{32,96},{33,1},{48,112},{49,17},{4,6... | collective-permute-start | bytes 491528 | tf_op jit(solution)/shard_map/ppermute | solution.py:39
  25.1 6.5 %collective-permute-start.18 = (bf16[128,640]{1,0:T(8,128)(2,1)S(1)}, bf16[128,640]{1,0:T(8,128)(2,1)S(1)}, u32[]{:S(2)}, u32[]{:S(2)}) collective-permute-start(bf16[128,640]{1,0:T(8,128)(2,1)S(1)} %get-tuple-element.44), channel_id=1, source_target_pairs={{0,66},{1,49},{16,82},{17,1},{32,98},{33,17},{48,114},{49,33},{4,7... | collective-permute-start | bytes 491528 | tf_op jit(solution)/shard_map/ppermute | solution.py:39
  27.4 6.0 %collective-permute-start.10 = (bf16[128,640]{1,0:T(8,128)(2,1)S(1)}, bf16[128,640]{1,0:T(8,128)(2,1)S(1)}, u32[]{:S(2)}, u32[]{:S(2)}) collective-permute-start(bf16[128,640]{1,0:T(8,128)(2,1)S(1)} %get-tuple-element.40), channel_id=1, source_target_pairs={{0,48},{1,13},{16,0},{17,29},{32,16},{33,45},{48,32},{49,61},{4,52... | collective-permute-start | bytes 491528 | tf_op jit(solution)/shard_map/ppermute | solution.py:39
  29.9 7.1 %collective-permute-start.8 = (bf16[128,640]{1,0:T(8,128)(2,1)S(1)}, bf16[128,640]{1,0:T(8,128)(2,1)S(1)}, u32[]{:S(2)}, u32[]{:S(2)}) collective-permute-start(bf16[128,640]{1,0:T(8,128)(2,1)S(1)} %get-tuple-element.38), channel_id=1, source_target_pairs={{0,16},{1,5},{16,32},{17,21},{32,48},{33,37},{48,0},{49,53},{4,20}... | collective-permute-start | bytes 491528 | tf_op jit(solution)/shard_map/ppermute | solution.py:39
  29.9 7.1 %collective-permute-start.9 = (bf16[128,640]{1,0:T(8,128)(2,1)S(1)}, bf16[128,640]{1,0:T(8,128)(2,1)S(1)}, u32[]{:S(2)}, u32[]{:S(2)}) collective-permute-start(bf16[128,640]{1,0:T(8,128)(2,1)S(1)} %get-tuple-element.39), channel_id=1, source_target_pairs={{0,32},{1,9},{16,48},{17,25},{32,0},{33,41},{48,16},{49,57},{4,36}... | collective-permute-start | bytes 491528 | tf_op jit(solution)/shard_map/ppermute | solution.py:39
  31.7 7.5 %collective-permute-start.19 = (bf16[128,640]{1,0:T(8,128)(2,1)S(1)}, bf16[128,640]{1,0:T(8,128)(2,1)S(1)}, u32[]{:S(2)}, u32[]{:S(2)}) collective-permute-start(bf16[128,640]{1,0:T(8,128)(2,1)S(1)} %get-tuple-element.45), channel_id=1, source_target_pairs={{0,16},{1,5},{16,0},{17,21},{32,48},{33,37},{48,32},{49,53},{4,20}... | collective-permute-start | bytes 491528 | tf_op jit(solution)/shard_map/ppermute | solution.py:39
  37.2 5.5 %collective-permute-start.11 = (bf16[128,640]{1,0:T(8,128)(2,1)S(1)}, bf16[128,640]{1,0:T(8,128)(2,1)S(1)}, u32[]{:S(2)}, u32[]{:S(2)}) collective-permute-start(bf16[128,640]{1,0:T(8,128)(2,1)S(1)} %get-tuple-element.47), channel_id=1, source_target_pairs={{0,66},{1,49},{16,82},{17,33},{32,98},{33,17},{48,114},{49,1},{4,7... | collective-permute-start | bytes 491528 | tf_op jit(solution)/shard_map/ppermute | solution.py:39
  39.2 5.5 %collective-permute-start.20 = (bf16[128,640]{1,0:T(8,128)(2,1)S(1)}, bf16[128,640]{1,0:T(8,128)(2,1)S(1)}, u32[]{:S(2)}, u32[]{:S(2)}) collective-permute-start(bf16[128,640]{1,0:T(8,128)(2,1)S(1)} %fusion.9), channel_id=1, source_target_pairs={{0,48},{1,13},{16,32},{17,29},{32,16},{33,45},{48,0},{49,61},{4,52... | collective-permute-start | bytes 491528 | tf_op jit(solution)/shard_map/ppermute | solution.py:39
  42.7 5.4 %collective-permute-start.12 = (bf16[128,640]{1,0:T(8,128)(2,1)S(1)}, bf16[128,640]{1,0:T(8,128)(2,1)S(1)}, u32[]{:S(2)}, u32[]{:S(2)}) collective-permute-start(bf16[128,640]{1,0:T(8,128)(2,1)S(1)} %fusion.8), channel_id=1, source_target_pairs={{0,2},{1,17},{16,18},{17,1},{32,34},{33,49},{48,50},{49,33},{4,6},... | collective-permute-start | bytes 491528 | tf_op jit(solution)/shard_map/ppermute | solution.py:39
  44.7 6.0 %collective-permute-start.21 = (bf16[128,640]{1,0:T(8,128)(2,1)S(1)}, bf16[128,640]{1,0:T(8,128)(2,1)S(1)}, u32[]{:S(2)}, u32[]{:S(2)}) collective-permute-start(bf16[128,640]{1,0:T(8,128)(2,1)S(1)} %add_convert_fusion.refs_4_), channel_id=1, source_target_pairs={{0,2},{1,17},{16,18},{17,33},{32,34},{33,49},{48,50},{49,1},{4,6},... | collective-permute-start | bytes 491528 | tf_op jit(solution)/shard_map/ppermute | solution.py:39
  44.8 8.9 %collective-permute-start.22 = (bf16[128,640]{1,0:T(8,128)(2,1)S(1)}, bf16[128,640]{1,0:T(8,128)(2,1)S(1)}, u32[]{:S(2)}, u32[]{:S(2)}) collective-permute-start(bf16[128,640]{1,0:T(8,128)(2,1)S(1)} %add_convert_fusion.refs_4_), channel_id=1, source_target_pairs={{0,64},{1,33},{16,80},{17,49},{32,96},{33,1},{48,112},{49,17},{4,6... | collective-permute-start | bytes 491528 | tf_op jit(solution)/shard_map/ppermute | solution.py:39
  46.7 6.9 %collective-permute-start.23 = (bf16[128,640]{1,0:T(8,128)(2,1)S(1)}, bf16[128,640]{1,0:T(8,128)(2,1)S(1)}, u32[]{:S(2)}, u32[]{:S(2)}) collective-permute-start(bf16[128,640]{1,0:T(8,128)(2,1)S(1)} %add_convert_fusion.refs_4_), channel_id=1, source_target_pairs={{0,66},{1,49},{16,82},{17,1},{32,98},{33,17},{48,114},{49,33},{4,7... | collective-permute-start | bytes 491528 | tf_op jit(solution)/shard_map/ppermute | solution.py:39
  48.1 7.2 %collective-permute-start.13 = (bf16[128,640]{1,0:T(8,128)(2,1)S(1)}, bf16[128,640]{1,0:T(8,128)(2,1)S(1)}, u32[]{:S(2)}, u32[]{:S(2)}) collective-permute-start(bf16[128,640]{1,0:T(8,128)(2,1)S(1)} %add_convert_fusion.1.refs_1_), channel_id=1, source_target_pairs={{0,16},{1,5},{16,32},{17,21},{32,48},{33,37},{48,0},{49,53},{4,20}... | collective-permute-start | bytes 491528 | tf_op jit(solution)/shard_map/ppermute | solution.py:39
  48.4 6.9 %collective-permute-start.14 = (bf16[128,640]{1,0:T(8,128)(2,1)S(1)}, bf16[128,640]{1,0:T(8,128)(2,1)S(1)}, u32[]{:S(2)}, u32[]{:S(2)}) collective-permute-start(bf16[128,640]{1,0:T(8,128)(2,1)S(1)} %add_convert_fusion.1.refs_1_), channel_id=1, source_target_pairs={{0,32},{1,9},{16,48},{17,25},{32,0},{33,41},{48,16},{49,57},{4,36}... | collective-permute-start | bytes 491528 | tf_op jit(solution)/shard_map/ppermute | solution.py:39
  50.7 5.5 %collective-permute-start.15 = (bf16[128,640]{1,0:T(8,128)(2,1)S(1)}, bf16[128,640]{1,0:T(8,128)(2,1)S(1)}, u32[]{:S(2)}, u32[]{:S(2)}) collective-permute-start(bf16[128,640]{1,0:T(8,128)(2,1)S(1)} %add_convert_fusion.1.refs_1_), channel_id=1, source_target_pairs={{0,48},{1,13},{16,0},{17,29},{32,16},{33,45},{48,32},{49,61},{4,52... | collective-permute-start | bytes 491528 | tf_op jit(solution)/shard_map/ppermute | solution.py:39
  57.1 7.7 %collective-permute-start.24 = (bf16[192,512]{1,0:T(8,128)(2,1)S(1)}, bf16[192,512]{1,0:T(8,128)(2,1)S(1)}, u32[]{:S(2)}, u32[]{:S(2)}) collective-permute-start(bf16[192,512]{1,0:T(8,128)(2,1)S(1)} %apply_sent.3), channel_id=1, source_target_pairs={{0,12},{1,67},{16,28},{17,83},{32,44},{33,99},{48,60},{49,115},{4,... | collective-permute-start | bytes 589832 | tf_op jit(solution)/shard_map/ppermute | solution.py:39
  61.1 6.2 %collective-permute-start.25 = (bf16[192,512]{1,0:T(8,128)(2,1)S(1)}, bf16[192,512]{1,0:T(8,128)(2,1)S(1)}, u32[]{:S(2)}, u32[]{:S(2)}) collective-permute-start(bf16[192,512]{1,0:T(8,128)(2,1)S(1)} %apply_sent.4), channel_id=1, source_target_pairs={{0,8},{1,65},{16,24},{17,81},{32,40},{33,97},{48,56},{49,113},{4,1... | collective-permute-start | bytes 589832 | tf_op jit(solution)/shard_map/ppermute | solution.py:39
  62.2 7.1 %collective-permute-start.26 = (bf16[192,512]{1,0:T(8,128)(2,1)S(1)}, bf16[192,512]{1,0:T(8,128)(2,1)S(1)}, u32[]{:S(2)}, u32[]{:S(2)}) collective-permute-start(bf16[192,512]{1,0:T(8,128)(2,1)S(1)} %apply_sent.5), channel_id=1, source_target_pairs={{0,4},{1,3},{16,20},{17,19},{32,36},{33,35},{48,52},{49,51},{4,8},... | collective-permute-start | bytes 589832 | tf_op jit(solution)/shard_map/ppermute | solution.py:39
  69.5 11.4 %collective-permute-start.27 = (f32[192]{0:T(256)S(1)}, f32[192]{0:T(256)S(1)}, u32[]{:S(2)}, u32[]{:S(2)}) collective-permute-start(f32[192]{0:T(256)S(1)} %fusion.5), channel_id=1, source_target_pairs={{0,1},{1,0},{2,3},{3,2},{4,5},{5,4},{6,7},{7,6},{8,9},{9,8},{10,11... | collective-permute-start | bytes 2312 | tf_op jit(solution)/shard_map/ppermute | solution.py:51

commit v8 on v6

--- a/solution.py
+++ b/solution.py
@@ -16,6 +16,7 @@
 SECOND = ((Z, Y), (X, Z))
 ORDER = (2, 1, 3)
 STRIP = 32
+LANES = 128
 PARAMS = pltpu.CompilerParams(vmem_limit_bytes=40 * 1024 * 1024)
 SCALAR = pl.BlockSpec(memory_space=pltpu.SMEM)
 WHOLE = pl.BlockSpec(memory_space=pltpu.VMEM)
@@ -71,18 +72,25 @@
         ssq_t[at, :] = squares(t_own[at, :])
 
 
-def pack_own_kernel(places, s_own, s_far, t_own, t_far, ssq_s, ssq_t, *outs):
-    rows, half = s_own.shape
-    ts = t_own.shape[1] // SIZE
+def pack_own_kernel(places, s_far, t_own, t_far, ssq_s, ssq_t, *outs):
+    rows, wide = t_own.shape
+    ts = wide // SIZE
     inv_s, inv_t = outs[SIZE:]
+    lane = lax.broadcasted_iota(jnp.int32, (STRIP, LANES), 1)
     for at in strips(rows):
-        inv_s[at, :] = lax.rsqrt(ssq_s[at, :] + squares(s_far[at, :]) + 1e-06)
+        inv = lax.rsqrt(ssq_s[at, :] + squares(s_far[at, :]) + 1e-06)
+        inv_s[at, :] = inv
         inv_t[at, :] = lax.rsqrt(ssq_t[at, :] + squares(t_far[at, :]) + 1e-06)
+        terms = jnp.zeros((STRIP, LANES), F32)
+        for i in range(3):
+            term = inv.astype(BF16).astype(F32)
+            terms = jnp.where(lane == i, term, terms)
+            inv = inv - term
+        for by in range(SIZE):
+            outs[by][at, pl.ds(ts, LANES)] = terms.astype(BF16)
     for at in strips(rows):
-        norm = scaled(s_own[at, :], inv_s[at, :])
         for by in range(SIZE):
-            outs[by][at, pl.ds(0, half)] = norm
-            outs[by][at, pl.ds(half, ts)] = scaled(t_own[at, part(places, by, ts)], inv_t[at, :])
+            outs[by][at, pl.ds(0, ts)] = scaled(t_own[at, part(places, by, ts)], inv_t[at, :])
 
 
 def pack_far_kernel(places, s_far, t_far, inv_s, inv_t, *outs):
@@ -94,40 +102,49 @@
             outs[by][at, pl.ds(ss, ts)] = scaled(t_far[at, part(places, by, ts)], inv_t[at, :])
 
 
-def native_features(places, pack, half):
+def emit(place, product, outs):
+    half, feats = product.shape
     ss = half // SIZE
-    return pack[:, part(places, 0, ss)], pack[:, pl.ds(half, pack.shape[1] - half)]
-
-
-def gram_kernel(share, chunk, places, *refs):
-    native = chunk == 0
-    count = SIZE if native else 2 * SIZE
-    norms, packs = refs[:SIZE], refs[count - SIZE : count]
-    outs, (left, right, product) = refs[count : count + SIZE], refs[count + SIZE :]
+    rest = pl.ds(ss, feats - ss)
+    for by, out in enumerate(outs):
+        block = pl.ds(pl.multiple_of(lax.rem(place + by, SIZE) * ss, ss), ss)
+        out[:, pl.ds(0, ss)] = product[block, pl.ds(0, ss)].astype(out.dtype)
+        out[:, rest] = -product[block, rest].astype(out.dtype)
+
+
+def cross(left, right):
+    return lax.dot_general(
+        left[...], right[...], (((0,), (0,)), ((), ())), preferred_element_type=F32
+    )
+
+
+def gram_native_kernel(share, places, *refs):
+    students, packs = refs[:SIZE], refs[SIZE : 2 * SIZE]
+    outs, (left, right, product) = refs[2 * SIZE : 3 * SIZE], refs[3 * SIZE :]
     half, feats = product.shape
-    rows, ss = norms[0].shape[0], half // SIZE
+    rows, ss = students[0].shape[0], half // SIZE
+    ts = feats - ss
     for k in range(SIZE):
         at = pl.ds(k * rows, rows)
-        left[at, :] = norms[k][:, pl.ds(0, half)]
-        if native:
-            right[at, pl.ds(0, ss)], right[at, pl.ds(ss, feats - ss)] = native_features(
-                places, packs[k], half
-            )
-        else:
-            right[at, :] = packs[k][...]
-    product[...] = lax.dot_general(
-        left[...], right[...], (((0,), (0,)), ((), ())), preferred_element_type=F32
-    )
-    if native:
-        row = lax.broadcasted_iota(jnp.int32, (ss, ss), 0)
-        col = lax.broadcasted_iota(jnp.int32, (ss, ss), 1)
-        product[part(places, 0, ss), pl.ds(0, ss)] -= jnp.where(row == col, share, 0.0)
-    for by, out in enumerate(outs):
-        which = lax.rem(places[1 + chunk] + by, SIZE)
-        block = pl.ds(pl.multiple_of(which * ss, ss), ss)
-        rest = pl.ds(ss, feats - ss)
-        out[:, pl.ds(0, ss)] = product[block, pl.ds(0, ss)].astype(out.dtype)
-        out[:, rest] = -product[block, rest].astype(out.dtype)
+        terms = packs[k][:, pl.ds(ts, LANES)].astype(F32)
+        inv = (terms[:, 0:1] + terms[:, 1:2]) + terms[:, 2:3]
+        left[at, :] = scaled(students[k][...], inv)
+        right[at, pl.ds(0, ss)] = left[at, part(places, 0, ss)]
+        right[at, pl.ds(ss, ts)] = packs[k][:, pl.ds(0, ts)]
+    product[...] = cross(left, right)
+    row = lax.broadcasted_iota(jnp.int32, (ss, ss), 0)
+    col = lax.broadcasted_iota(jnp.int32, (ss, ss), 1)
+    product[part(places, 0, ss), pl.ds(0, ss)] -= jnp.where(row == col, share, 0.0)
+    emit(places[1], product, outs)
+
+
+def gram_far_kernel(places, left, *refs):
+    packs, outs, (right, product) = refs[:SIZE], refs[SIZE : 2 * SIZE], refs[2 * SIZE :]
+    rows = packs[0].shape[0]
+    for k, pack in enumerate(packs):
+        right[pl.ds(k * rows, rows), :] = pack[...]
+    product[...] = cross(left, right)
+    emit(places[2], product, outs)
 
 
 def gather_weights(place, pieces, weights):
@@ -141,16 +158,9 @@
     return lax.dot_general(left, weights, (((1,), (1,)), ((), ())), preferred_element_type=F32)
 
 
-def apply_native_kernel(places, *refs):
-    packs, pieces, (out, left, weights) = refs[:SIZE], refs[SIZE : 2 * SIZE], refs[2 * SIZE :]
-    half, feats = weights.shape
-    rows, ss = packs[0].shape[0], half // SIZE
+def apply_native_kernel(places, left, *refs):
+    pieces, (out, weights) = refs[:SIZE], refs[SIZE:]
     gather_weights(places[1], pieces, weights)
-    for k, pack in enumerate(packs):
-        at = pl.ds(k * rows, rows)
-        left[at, pl.ds(0, ss)], left[at, pl.ds(ss, feats - ss)] = native_features(
-            places, pack, half
-        )
     out[...] = times(left[...], weights[...])
 
 
@@ -207,13 +217,12 @@
     *near, inv_s, inv_t = kernel_call(
         pack_own_kernel,
         "pack_own",
-        shapes(*[((rows, half + ts), BF16)] * SIZE, *[((rows, 1), F32)] * 2),
-        6,
-    )(places, student, s_far, teacher, t_far, ssq_s, ssq_t)
+        shapes(*[((rows, ts + LANES), BF16)] * SIZE, *[((rows, 1), F32)] * 2),
+        5,
+    )(places, s_far, teacher, t_far, ssq_s, ssq_t)
     far = kernel_call(
         pack_far_kernel, "pack_far", shapes(*[((rows, feats), BF16)] * SIZE), 4
     )(places, s_far, t_far, inv_s, inv_t)
-    norm_own = near[0][:, :half]
 
     def exchanged(own, sent, axis_of_core, sign=1):
         arrived = {by: shifted(sent(by), axis_of_core, sign * by) for by in ORDER}
@@ -224,38 +233,47 @@
             total = total + array.astype(F32)
         return total
 
+    students = exchanged(student, lambda by: student, GATHER)
     near = exchanged(near[0], near.__getitem__, GATHER)
     far = exchanged(far[0], far.__getitem__, GATHER)
 
-    def weights_of(chunk, packs, name):
-        own, *sends = kernel_call(
-            functools.partial(gram_kernel, level * SIZE / groups, chunk),
-            name,
-            shapes(((ss, feats), F32), *[((ss, feats), BF16)] * 3),
-            len(packs),
-            [
-                pltpu.VMEM((SIZE * rows, half), BF16),
-                pltpu.VMEM((SIZE * rows, feats), BF16),
-                pltpu.VMEM((half, feats), F32),
-            ],
-            flops,
-        )(places, *packs)
+    blocks = shapes(((ss, feats), F32), *[((ss, feats), BF16)] * 3)
+    product = pltpu.VMEM((half, feats), F32)
+    stacked = shapes(((SIZE * rows, half), BF16), ((SIZE * rows, feats), BF16))
+    *near_blocks, norms, native = kernel_call(
+        functools.partial(gram_native_kernel, level * SIZE / groups),
+        "gram_native",
+        blocks + stacked,
+        2 * SIZE,
+        [product],
+        flops,
+    )(places, *students, *near)
+    far_blocks = kernel_call(
+        gram_far_kernel,
+        "gram_far",
+        blocks,
+        SIZE + 1,
+        [pltpu.VMEM((SIZE * rows, feats), BF16), product],
+        flops,
+    )(places, norms, *far)
+
+    def weights_of(chunk, own, *sends):
         total = added(own, lambda by: sends[by - 1], FIRST[chunk])
         shared = total.astype(BF16)
         piece = added(total, lambda by: shared, SECOND[chunk]).astype(BF16)
         return exchanged(piece, lambda by: piece, FIRST[chunk])
 
-    near_weights = weights_of(0, near, "gram_native")
-    far_weights = weights_of(1, near + far, "gram_far")
+    near_weights = weights_of(0, *near_blocks)
+    far_weights = weights_of(1, *far_blocks)
 
     sofar = kernel_call(
         apply_native_kernel,
         "apply_native",
         shapes(((SIZE * rows, half), F32)),
-        2 * SIZE,
-        [pltpu.VMEM((SIZE * rows, feats), BF16), pltpu.VMEM((half, feats), BF16)],
+        SIZE + 1,
+        [pltpu.VMEM((half, feats), BF16)],
         flops,
-    )(places, *near, *near_weights)[0]
+    )(places, native, *near_weights)[0]
     parts = kernel_call(
         functools.partial(apply_far_kernel, 1, SIZE - 1),
         "apply_sent",
@@ -272,7 +290,7 @@
         [pltpu.VMEM((half, feats), BF16)],
         flops // 4,
     )(places, far[0], *far_weights, sofar)[0]
-    norm_f = norm_own.astype(F32)
+    norm_f = norms[:rows].astype(F32)
     grad_n = grad_n + level * norm_f
     grad_n = coef * added(grad_n, lambda by: parts[by - 1], GATHER, -1)
     inner = jnp.sum(grad_n * norm_f, axis=1)

time: 80.6 us -> 83.9 us (1.041)
  starting transfers between devices: 47.6 us -> 49.4 us
  local copies, waits for them, and re-layouts: 2.06 us -> 3.19 us
    ppermute x27 -> x30, starting transfers between devices: 34.2 us -> 39.1 us  [shifted(): return lax.ppermute(array, AXES, pairs)]
    ppermute x3, starting transfers between devices: 13.4 us -> 10.3 us  [other_core(): return lax.ppermute(array, 'sec', [(0, 1), (1, 0)])]
    unnamed x4 -> x8, local copies, waits for them, and re-layouts: 2.06 us -> 3.19 us
    ppermute x27 -> x30, waiting for transfers between devices: 19 us -> 18.9 us  [shifted(): return lax.ppermute(array, AXES, pairs)]
  transfers between devices with their start and end apart: 30 -> 33, of which waited for: 12 -> 13; matrix products, arithmetic and copies ran while one was open for 1% -> 1% of each run, Pallas kernels for 8% -> 10%
where the time goes in v8:
time: 83.9 us; the launch traced here: 83.7 us
  starting transfers between devices  49.4 us (59%)
  waiting for transfers between devices  19.6 us (23%)
  Pallas kernels  9.51 us (11%)
  local copies, waits for them, and re-layouts  3.19 us (4%)
  other arithmetic  1.85 us (2%)
    ppermute x30, starting transfers between devices, shifted(): return lax.ppermute(array, AXES, pairs)  39.1 us
    ppermute x30, waiting for transfers between devices, shifted(): return lax.ppermute(array, AXES, pairs)  18.9 us
    ppermute x3, starting transfers between devices, other_core(): return lax.ppermute(array, 'sec', [(0, 1), (1, 0)])  10.3 us
    unnamed x8, local copies, waits for them, and re-layouts  3.19 us
    pallas_call x1, Pallas kernels, body(): kernel_call(functools.partial(gram_native_kernel, level * SIZE / groups),...  2.09 us
  transfers between devices with their start and end apart: 33, of which 13 were waited for; matrix products, arithmetic and copies ran while one was open for 1% of the time, Pallas kernels for 10%

profile of v8, /device:TPU:1, one launch (start us, length us, event | category | flops | bytes accessed | tf_op | source)
XLA Modules:
  0.0 83.7 jit_solution(11103062043145706823)
XLA Ops:
  0.0 1.4 %collective-permute-start.1 = (bf16[192,2048]{1,0:T(8,128)(2,1)}, bf16[192,2048]{1,0:T(8,128)(2,1)S(1)}, u32[]{:S(2)}, u32[]{:S(2)}) collective-permute-start(bf16[192,2048]{1,0:T(8,128)(2,1)} %t_own.3), channel_id=1, source_target_pairs={{0,1},{1,0},{2,3},{3,2},{4,5},{5,4},{6,7},{7,6},{8,9},{9,8},{10,11... | collective-permute-start | bytes 2359304 | tf_op jit(solution)/shard_map/ppermute | solution.py:43
  1.4 2.8 %collective-permute-start.3 = (bf16[192,512]{1,0:T(8,128)(2,1)}, bf16[192,512]{1,0:T(8,128)(2,1)S(1)}, u32[]{:S(2)}, u32[]{:S(2)}) collective-permute-start(bf16[192,512]{1,0:T(8,128)(2,1)} %refs_0_.1), channel_id=1, source_target_pairs={{0,8},{1,65},{16,24},{17,81},{32,40},{33,97},{48,56},{49,113},{4,1... | collective-permute-start | bytes 589832 | tf_op jit(solution)/shard_map/ppermute | solution.py:39
  4.6 1.1 %copy-done = bf16[192,2048]{1,0:T(8,128)(2,1)S(1)} copy-done((bf16[192,2048]{1,0:T(8,128)(2,1)S(1)}, bf16[192,2048]{1,0:T(8,128)(2,1)}, u32[]{:S(2)}) %copy-start) | copy-done | bytes 786456
  5.7 0.9 %copy-done.2 = bf16[192,512]{1,0:T(8,128)(2,1)S(1)} copy-done((bf16[192,512]{1,0:T(8,128)(2,1)S(1)}, bf16[192,512]{1,0:T(8,128)(2,1)}, u32[]{:S(2)}) %copy-start.2) | copy-done | bytes 196632
  7.0 1.1 %copy-done.1 = bf16[192,2048]{1,0:T(8,128)(2,1)S(1)} copy-done((bf16[192,2048]{1,0:T(8,128)(2,1)S(1)}, bf16[192,2048]{1,0:T(8,128)(2,1)}, u32[]{:S(2)}) %copy-start.1) | copy-done | bytes 786456
  8.1 1.0 %pack_own.1 = (bf16[192,640]{1,0:T(8,128)(2,1)S(1)}, bf16[192,640]{1,0:T(8,128)(2,1)S(1)}, bf16[192,640]{1,0:T(8,128)(2,1)S(1)}, bf16[192,640]{1,0:T(8,128)(2,1)...) custom-call(s32[3]{0:T(128)S(1)} %pad_add_fusion.places, bf16[192,512]{1,0:T(8,128)(2,1)S(1)} %collective-permute-done.s_far, ...), custom_call_target="tpu_custom_call" | custom-call | bytes 4194304 | tf_op jit(solution)/shard_map/pack_own/pallas_call | solution.py:217
  9.3 2.7 %collective-permute-start.4 = (bf16[192,512]{1,0:T(8,128)(2,1)S(1)}, bf16[192,512]{1,0:T(8,128)(2,1)S(1)}, u32[]{:S(2)}, u32[]{:S(2)}) collective-permute-start(bf16[192,512]{1,0:T(8,128)(2,1)S(1)} %copy-done.3), channel_id=1, source_target_pairs={{0,12},{1,67},{16,28},{17,83},{32,44},{33,99},{48,60},{49,115},{4,... | collective-permute-start | bytes 589832 | tf_op jit(solution)/shard_map/ppermute | solution.py:39
  11.9 0.9 %collective-permute-start.6 = (bf16[192,640]{1,0:T(8,128)(2,1)S(1)}, bf16[192,640]{1,0:T(8,128)(2,1)S(1)}, u32[]{:S(2)}, u32[]{:S(2)}) collective-permute-start(bf16[192,640]{1,0:T(8,128)(2,1)S(1)} %get-tuple-element.37), channel_id=1, source_target_pairs={{0,8},{1,65},{16,24},{17,81},{32,40},{33,97},{48,56},{49,113},{4,1... | collective-permute-start | bytes 737288 | tf_op jit(solution)/shard_map/ppermute | solution.py:39
  12.8 0.4 collective-permute-start.7
  13.2 0.8 pack_far.1
  14.0 1.1 %collective-permute-start.8 = (bf16[192,640]{1,0:T(8,128)(2,1)S(1)}, bf16[192,640]{1,0:T(8,128)(2,1)S(1)}, u32[]{:S(2)}, u32[]{:S(2)}) collective-permute-start(bf16[192,640]{1,0:T(8,128)(2,1)S(1)} %get-tuple-element.40), channel_id=1, source_target_pairs={{0,4},{1,3},{16,20},{17,19},{32,36},{33,35},{48,52},{49,51},{4,8},... | collective-permute-start | bytes 737288 | tf_op jit(solution)/shard_map/ppermute | solution.py:39
  15.2 2.0 %collective-permute-done.4.refs_3_ = bf16[192,512]{1,0:T(8,128)(2,1)S(1)} collective-permute-done((bf16[192,512]{1,0:T(8,128)(2,1)S(1)}, bf16[192,512]{1,0:T(8,128)(2,1)S(1)}, u32[]{:S(2)}, u32[]{:S(2)}) %collective-permute-start.4) | collective-permute-done | bytes 196640 | tf_op jit(solution)/shard_map/ppermute | solution.py:39
  17.2 0.4 collective-permute-start.9
  17.6 2.7 %collective-permute-start.10 = (bf16[192,640]{1,0:T(8,128)(2,1)S(1)}, bf16[192,640]{1,0:T(8,128)(2,1)S(1)}, u32[]{:S(2)}, u32[]{:S(2)}) collective-permute-start(bf16[192,640]{1,0:T(8,128)(2,1)S(1)} %get-tuple-element.42), channel_id=1, source_target_pairs={{0,12},{1,67},{16,28},{17,83},{32,44},{33,99},{48,60},{49,115},{4,... | collective-permute-start | bytes 737288 | tf_op jit(solution)/shard_map/ppermute | solution.py:39
  20.3 2.1 %gram_native.1 = (f32[128,640]{1,0:T(8,128)S(1)}, bf16[128,640]{1,0:T(8,128)(2,1)S(1)}, bf16[128,640]{1,0:T(8,128)(2,1)S(1)}, bf16[128,640]{1,0:T(8,128)(2,1)S(1...) custom-call(s32[3]{0:T(128)S(1)} %pad_add_fusion.places, bf16[192,512]{1,0:T(8,128)(2,1)S(1)} %copy-done.3, ...), custom_call_target="tpu_custom_call" | custom-call | flops 503316480 | bytes 4194304 | tf_op jit(solution)/shard_map/gram_native/pallas_call | solution.py:243
  22.4 1.7 %collective-permute-start.20 = (bf16[128,640]{1,0:T(8,128)(2,1)S(1)}, bf16[128,640]{1,0:T(8,128)(2,1)S(1)}, u32[]{:S(2)}, u32[]{:S(2)}) collective-permute-start(bf16[128,640]{1,0:T(8,128)(2,1)S(1)} %get-tuple-element.49), channel_id=1, source_target_pairs={{0,2},{1,17},{16,18},{17,33},{32,34},{33,49},{48,50},{49,1},{4,6},... | collective-permute-start | bytes 491528 | tf_op jit(solution)/shard_map/ppermute | solution.py:39
  24.1 3.3 %collective-permute-start.21 = (bf16[128,640]{1,0:T(8,128)(2,1)S(1)}, bf16[128,640]{1,0:T(8,128)(2,1)S(1)}, u32[]{:S(2)}, u32[]{:S(2)}) collective-permute-start(bf16[128,640]{1,0:T(8,128)(2,1)S(1)} %get-tuple-element.50), channel_id=1, source_target_pairs={{0,64},{1,33},{16,80},{17,49},{32,96},{33,1},{48,112},{49,17},{4,6... | collective-permute-start | bytes 491528 | tf_op jit(solution)/shard_map/ppermute | solution.py:39
  27.4 0.7 collective-permute-start.22
  28.1 1.6 %gram_far.1 = (f32[128,640]{1,0:T(8,128)S(1)}, bf16[128,640]{1,0:T(8,128)(2,1)S(1)}, bf16[128,640]{1,0:T(8,128)(2,1)S(1)}, bf16[128,640]{1,0:T(8,128)(2,1)S(1)}) custom-call(s32[3]{0:T(128)S(1)} %pad_add_fusion.places, bf16[768,512]{1,0:T(8,128)(2,1)S(1)} %get-tuple-element.39.left, bf16[192,640]{1,0:T(8,128)(2,1)S(1)} %get-tuple-element.34.refs_0_, ...), custom_call_target="tpu_custom_call" | custom-call | flops 503316480 | bytes 4194304 | tf_op jit(solution)/shard_map/gram_far/pallas_call | solution.py:251
  29.7 1.5 %collective-permute-start.11 = (bf16[128,640]{1,0:T(8,128)(2,1)S(1)}, bf16[128,640]{1,0:T(8,128)(2,1)S(1)}, u32[]{:S(2)}, u32[]{:S(2)}) collective-permute-start(bf16[128,640]{1,0:T(8,128)(2,1)S(1)} %get-tuple-element.44), channel_id=1, source_target_pairs={{0,16},{1,5},{16,32},{17,21},{32,48},{33,37},{48,0},{49,53},{4,20}... | collective-permute-start | bytes 491528 | tf_op jit(solution)/shard_map/ppermute | solution.py:39
  31.2 2.8 %collective-permute-start.12 = (bf16[128,640]{1,0:T(8,128)(2,1)S(1)}, bf16[128,640]{1,0:T(8,128)(2,1)S(1)}, u32[]{:S(2)}, u32[]{:S(2)}) collective-permute-start(bf16[128,640]{1,0:T(8,128)(2,1)S(1)} %get-tuple-element.45), channel_id=1, source_target_pairs={{0,32},{1,9},{16,48},{17,25},{32,0},{33,41},{48,16},{49,57},{4,36}... | collective-permute-start | bytes 491528 | tf_op jit(solution)/shard_map/ppermute | solution.py:39
  34.0 0.9 %collective-permute-start.13 = (bf16[128,640]{1,0:T(8,128)(2,1)S(1)}, bf16[128,640]{1,0:T(8,128)(2,1)S(1)}, u32[]{:S(2)}, u32[]{:S(2)}) collective-permute-start(bf16[128,640]{1,0:T(8,128)(2,1)S(1)} %get-tuple-element.46), channel_id=1, source_target_pairs={{0,48},{1,13},{16,0},{17,29},{32,16},{33,45},{48,32},{49,61},{4,52... | collective-permute-start | bytes 491528 | tf_op jit(solution)/shard_map/ppermute | solution.py:39
  35.0 0.4 collective-permute-start.25
  35.4 2.1 %collective-permute-start.24 = (bf16[128,640]{1,0:T(8,128)(2,1)S(1)}, bf16[128,640]{1,0:T(8,128)(2,1)S(1)}, u32[]{:S(2)}, u32[]{:S(2)}) collective-permute-start(bf16[128,640]{1,0:T(8,128)(2,1)S(1)} %fusion.9), channel_id=1, source_target_pairs={{0,32},{1,9},{16,48},{17,25},{32,0},{33,41},{48,16},{49,57},{4,36}... | collective-permute-start | bytes 491528 | tf_op jit(solution)/shard_map/ppermute | solution.py:39
  37.4 1.0 %collective-permute-done.12 = bf16[128,640]{1,0:T(8,128)(2,1)S(1)} collective-permute-done((bf16[128,640]{1,0:T(8,128)(2,1)S(1)}, bf16[128,640]{1,0:T(8,128)(2,1)S(1)}, u32[]{:S(2)}, u32[]{:S(2)}) %collective-permute-start.12) | collective-permute-done | bytes 163872 | tf_op jit(solution)/shard_map/ppermute | solution.py:39
  38.5 3.4 %collective-permute-start.16 = (bf16[128,640]{1,0:T(8,128)(2,1)S(1)}, bf16[128,640]{1,0:T(8,128)(2,1)S(1)}, u32[]{:S(2)}, u32[]{:S(2)}) collective-permute-start(bf16[128,640]{1,0:T(8,128)(2,1)S(1)} %fusion.8), channel_id=1, source_target_pairs={{0,66},{1,49},{16,82},{17,1},{32,98},{33,17},{48,114},{49,33},{4,7... | collective-permute-start | bytes 491528 | tf_op jit(solution)/shard_map/ppermute | solution.py:39
  41.9 0.7 collective-permute-start.14
  43.1 3.2 %collective-permute-start.28 = (bf16[128,640]{1,0:T(8,128)(2,1)S(1)}, bf16[128,640]{1,0:T(8,128)(2,1)S(1)}, u32[]{:S(2)}, u32[]{:S(2)}) collective-permute-start(bf16[128,640]{1,0:T(8,128)(2,1)S(1)} %add_convert_fusion.refs_0_), channel_id=1, source_target_pairs={{0,66},{1,49},{16,82},{17,1},{32,98},{33,17},{48,114},{49,33},{4,7... | collective-permute-start | bytes 491528 | tf_op jit(solution)/shard_map/ppermute | solution.py:39
  46.7 0.5 collective-permute-start.26
  47.2 1.6 %collective-permute-done.15 = bf16[128,640]{1,0:T(8,128)(2,1)S(1)} collective-permute-done((bf16[128,640]{1,0:T(8,128)(2,1)S(1)}, bf16[128,640]{1,0:T(8,128)(2,1)S(1)}, u32[]{:S(2)}, u32[]{:S(2)}) %collective-permute-start.15) | collective-permute-done | bytes 163872 | tf_op jit(solution)/shard_map/ppermute | solution.py:39
  48.8 2.2 %collective-permute-done.14 = bf16[128,640]{1,0:T(8,128)(2,1)S(1)} collective-permute-done((bf16[128,640]{1,0:T(8,128)(2,1)S(1)}, bf16[128,640]{1,0:T(8,128)(2,1)S(1)}, u32[]{:S(2)}, u32[]{:S(2)}) %collective-permute-start.14) | collective-permute-done | bytes 163872 | tf_op jit(solution)/shard_map/ppermute | solution.py:39
  51.2 2.6 %collective-permute-start.19 = (bf16[128,640]{1,0:T(8,128)(2,1)S(1)}, bf16[128,640]{1,0:T(8,128)(2,1)S(1)}, u32[]{:S(2)}, u32[]{:S(2)}) collective-permute-start(bf16[128,640]{1,0:T(8,128)(2,1)S(1)} %add_convert_fusion.1.refs_1_.refs_3_), channel_id=1, source_target_pairs={{0,48},{1,13},{16,0},{17,29},{32,16},{33,45},{48,32},{49,61},{4,52... | collective-permute-start | bytes 491528 | tf_op jit(solution)/shard_map/ppermute | solution.py:39
  53.7 0.7 collective-permute-start.18
  54.4 0.5 collective-permute-start.17
  54.9 1.4 %apply_native.1.refs_5_.refs_7_ = f32[768,512]{1,0:T(8,128)S(1)} custom-call(s32[3]{0:T(128)S(1)} %pad_add_fusion.places, bf16[768,640]{1,0:T(8,128)(2,1)S(1)} %get-tuple-element.47.left, bf16[128,640]{1,0:T(8,128)(2,1)S(1)} %add_convert_fusion.refs_0_, bf16[128,640]{1,0:T(8,128)(2,1)S(1)} %collective-permute-done.26.refs_1_, ...), custom_call_target="tpu_custom_call" | custom-call | flops 503316480 | bytes 4194304 | tf_op jit(solution)/shard_map/apply_native/pallas_call | solution.py:269
  56.3 1.5 %collective-permute-done.19.refs_4_.refs_6_ = bf16[128,640]{1,0:T(8,128)(2,1)S(1)} collective-permute-done((bf16[128,640]{1,0:T(8,128)(2,1)S(1)}, bf16[128,640]{1,0:T(8,128)(2,1)S(1)}, u32[]{:S(2)}, u32[]{:S(2)}) %collective-permute-start.19) | collective-permute-done | bytes 163872 | tf_op jit(solution)/shard_map/ppermute | solution.py:39
  57.8 1.9 %collective-permute-done.18.refs_3_.refs_5_ = bf16[128,640]{1,0:T(8,128)(2,1)S(1)} collective-permute-done((bf16[128,640]{1,0:T(8,128)(2,1)S(1)}, bf16[128,640]{1,0:T(8,128)(2,1)S(1)}, u32[]{:S(2)}, u32[]{:S(2)}) %collective-permute-start.18) | collective-permute-done | bytes 163872 | tf_op jit(solution)/shard_map/ppermute | solution.py:39
  59.7 1.8 %collective-permute-done.17.refs_2_.refs_4_ = bf16[128,640]{1,0:T(8,128)(2,1)S(1)} collective-permute-done((bf16[128,640]{1,0:T(8,128)(2,1)S(1)}, bf16[128,640]{1,0:T(8,128)(2,1)S(1)}, u32[]{:S(2)}, u32[]{:S(2)}) %collective-permute-start.17) | collective-permute-done | bytes 163872 | tf_op jit(solution)/shard_map/ppermute | solution.py:39
  61.5 1.4 %apply_sent.1 = (bf16[192,512]{1,0:T(8,128)(2,1)S(1)}, bf16[192,512]{1,0:T(8,128)(2,1)S(1)}, bf16[192,512]{1,0:T(8,128)(2,1)S(1)}) custom-call(s32[3]{0:T(128)S(1)} %pad_add_fusion.places, bf16[192,640]{1,0:T(8,128)(2,1)S(1)} %collective-permute-done.8.refs_1_.refs_0_, bf16[192,640]{1,0:T(8,128)(2,1)S(1)} %collective-permute-done.9.refs_2_.refs_1_, ...), custom_call_target="tpu_custom_call" | custom-call | flops 377487360 | bytes 4194304 | tf_op jit(solution)/shard_map/apply_sent/pallas_call | solution.py:277
  62.9 1.8 %collective-permute-start.29 = (bf16[192,512]{1,0:T(8,128)(2,1)S(1)}, bf16[192,512]{1,0:T(8,128)(2,1)S(1)}, u32[]{:S(2)}, u32[]{:S(2)}) collective-permute-start(bf16[192,512]{1,0:T(8,128)(2,1)S(1)} %get-tuple-element.52), channel_id=1, source_target_pairs={{0,12},{1,67},{16,28},{17,83},{32,44},{33,99},{48,60},{49,115},{4,... | collective-permute-start | bytes 589832 | tf_op jit(solution)/shard_map/ppermute | solution.py:39
  64.7 0.8 collective-permute-start.30
  65.4 1.0 %apply_kept.1 = f32[192,512]{1,0:T(8,128)S(1)} custom-call(s32[3]{0:T(128)S(1)} %pad_add_fusion.places, bf16[192,640]{1,0:T(8,128)(2,1)S(1)} %get-tuple-element.34.refs_0_, bf16[128,640]{1,0:T(8,128)(2,1)S(1)} %add_convert_fusion.1.refs_1_.refs_3_, bf16[128,640]{1,0:T(8,128)(2,1)S(1)} %collective-permute-done.17.refs_2_.refs_4_, ...), custom_call_target="tpu_custom_call" | custom-call | flops 125829120 | bytes 4194304 | tf_op jit(solution)/shard_map/apply_kept/pallas_call | solution.py:285
  66.4 3.0 %collective-permute-done.29 = bf16[192,512]{1,0:T(8,128)(2,1)S(1)} collective-permute-done((bf16[192,512]{1,0:T(8,128)(2,1)S(1)}, bf16[192,512]{1,0:T(8,128)(2,1)S(1)}, u32[]{:S(2)}, u32[]{:S(2)}) %collective-permute-start.29) | collective-permute-done | bytes 196640 | tf_op jit(solution)/shard_map/ppermute | solution.py:39
  69.4 1.4 %collective-permute-done.30 = bf16[192,512]{1,0:T(8,128)(2,1)S(1)} collective-permute-done((bf16[192,512]{1,0:T(8,128)(2,1)S(1)}, bf16[192,512]{1,0:T(8,128)(2,1)S(1)}, u32[]{:S(2)}, u32[]{:S(2)}) %collective-permute-start.30) | collective-permute-done | bytes 196640 | tf_op jit(solution)/shard_map/ppermute | solution.py:39
  70.8 2.0 %collective-permute-done.31 = bf16[192,512]{1,0:T(8,128)(2,1)S(1)} collective-permute-done((bf16[192,512]{1,0:T(8,128)(2,1)S(1)}, bf16[192,512]{1,0:T(8,128)(2,1)S(1)}, u32[]{:S(2)}, u32[]{:S(2)}) %collective-permute-start.31) | collective-permute-done | bytes 196640 | tf_op jit(solution)/shard_map/ppermute | solution.py:39
  73.1 8.9 %collective-permute-start.32 = (f32[192]{0:T(256)S(1)}, f32[192]{0:T(256)S(1)}, u32[]{:S(2)}, u32[]{:S(2)}) collective-permute-start(f32[192]{0:T(256)S(1)} %fusion.5), channel_id=1, source_target_pairs={{0,1},{1,0},{2,3},{3,2},{4,5},{5,4},{6,7},{7,6},{8,9},{9,8},{10,11... | collective-permute-start | bytes 2312 | tf_op jit(solution)/shard_map/ppermute | solution.py:43
  82.1 0.7 collective-permute-done.32
  82.8 0.9 %fusion.7 = f32[192,512]{1,0:T(8,128)} fusion(f32[192]{0:T(256)S(1)} %reduce, f32[192]{0:T(256)S(1)} %add.85, bf16[768,512]{1,0:T(8,128)(2,1)S(1)} %get-tuple-element.39.left, bf16[192,512]{1,0:T(8,128)(2,1)S(1)} %collective-permute-done.31, bf16[192,512]{1,0:T(8,128)(2,1)S(1)} %collective-permute-done.30, bf16[192,512]{1,0:T(8,128)(2,1)S(1)} %collective-permute-done.29, ...), kind=kLoop, calls=%fused_computation.10 | loop fusion | flops 1277952 | bytes 1574400 | tf_op jit(solution)/shard_map/mul | solution.py:298
  (43 shorter events, 2.3 us)
Async XLA Ops:
  0.0 7.0 %collective-permute-start.1 = (bf16[192,2048]{1,0:T(8,128)(2,1)}, bf16[192,2048]{1,0:T(8,128)(2,1)S(1)}, u32[]{:S(2)}, u32[]{:S(2)}) collective-permute-start(bf16[192,2048]{1,0:T(8,128)(2,1)} %t_own.3), channel_id=1, source_target_pairs={{0,1},{1,0},{2,3},{3,2},{4,5},{5,4},{6,7},{7,6},{8,9},{9,8},{10,11... | collective-permute-start | bytes 2359304 | tf_op jit(solution)/shard_map/ppermute | solution.py:43
  1.4 5.6 %collective-permute-start = (bf16[192,512]{1,0:T(8,128)(2,1)}, bf16[192,512]{1,0:T(8,128)(2,1)S(1)}, u32[]{:S(2)}, u32[]{:S(2)}) collective-permute-start(bf16[192,512]{1,0:T(8,128)(2,1)} %refs_0_.1), channel_id=1, source_target_pairs={{0,1},{1,0},{2,3},{3,2},{4,5},{5,4},{6,7},{7,6},{8,9},{9,8},{10,11... | collective-permute-start | bytes 589832 | tf_op jit(solution)/shard_map/ppermute | solution.py:43
  1.4 11.4 %collective-permute-start.3 = (bf16[192,512]{1,0:T(8,128)(2,1)}, bf16[192,512]{1,0:T(8,128)(2,1)S(1)}, u32[]{:S(2)}, u32[]{:S(2)}) collective-permute-start(bf16[192,512]{1,0:T(8,128)(2,1)} %refs_0_.1), channel_id=1, source_target_pairs={{0,8},{1,65},{16,24},{17,81},{32,40},{33,97},{48,56},{49,113},{4,1... | collective-permute-start | bytes 589832 | tf_op jit(solution)/shard_map/ppermute | solution.py:39
  4.3 9.8 %collective-permute-start.2 = (bf16[192,512]{1,0:T(8,128)(2,1)}, bf16[192,512]{1,0:T(8,128)(2,1)S(1)}, u32[]{:S(2)}, u32[]{:S(2)}) collective-permute-start(bf16[192,512]{1,0:T(8,128)(2,1)} %refs_0_.1), channel_id=1, source_target_pairs={{0,4},{1,3},{16,20},{17,19},{32,36},{33,35},{48,52},{49,51},{4,8},... | collective-permute-start | bytes 589832 | tf_op jit(solution)/shard_map/ppermute | solution.py:39
  4.6 1.1 %copy-start = (bf16[192,2048]{1,0:T(8,128)(2,1)S(1)}, bf16[192,2048]{1,0:T(8,128)(2,1)}, u32[]{:S(2)}) copy-start(bf16[192,2048]{1,0:T(8,128)(2,1)} %t_own.3) | copy-start | bytes 2359300
  5.7 0.9 %copy-start.2 = (bf16[192,512]{1,0:T(8,128)(2,1)S(1)}, bf16[192,512]{1,0:T(8,128)(2,1)}, u32[]{:S(2)}) copy-start(bf16[192,512]{1,0:T(8,128)(2,1)} %refs_0_.1) | copy-start | bytes 589828
  6.6 2.6 %copy-start.3 = (bf16[192,512]{1,0:T(8,128)(2,1)S(1)}, bf16[192,512]{1,0:T(8,128)(2,1)}, u32[]{:S(2)}) copy-start(bf16[192,512]{1,0:T(8,128)(2,1)} %refs_0_.1) | copy-start | bytes 589828
  7.0 1.1 %copy-start.1 = (bf16[192,2048]{1,0:T(8,128)(2,1)S(1)}, bf16[192,2048]{1,0:T(8,128)(2,1)}, u32[]{:S(2)}) copy-start(bf16[192,2048]{1,0:T(8,128)(2,1)} %t_own.3) | copy-start | bytes 2359300
  9.2 8.4 %collective-permute-start.5 = (bf16[192,640]{1,0:T(8,128)(2,1)S(1)}, bf16[192,640]{1,0:T(8,128)(2,1)S(1)}, u32[]{:S(2)}, u32[]{:S(2)}) collective-permute-start(bf16[192,640]{1,0:T(8,128)(2,1)S(1)} %get-tuple-element.36), channel_id=1, source_target_pairs={{0,4},{1,3},{16,20},{17,19},{32,36},{33,35},{48,52},{49,51},{4,8},... | collective-permute-start | bytes 737288 | tf_op jit(solution)/shard_map/ppermute | solution.py:39
  9.3 7.9 %collective-permute-start.4 = (bf16[192,512]{1,0:T(8,128)(2,1)S(1)}, bf16[192,512]{1,0:T(8,128)(2,1)S(1)}, u32[]{:S(2)}, u32[]{:S(2)}) collective-permute-start(bf16[192,512]{1,0:T(8,128)(2,1)S(1)} %copy-done.3), channel_id=1, source_target_pairs={{0,12},{1,67},{16,28},{17,83},{32,44},{33,99},{48,60},{49,115},{4,... | collective-permute-start | bytes 589832 | tf_op jit(solution)/shard_map/ppermute | solution.py:39
  11.9 8.4 %collective-permute-start.6 = (bf16[192,640]{1,0:T(8,128)(2,1)S(1)}, bf16[192,640]{1,0:T(8,128)(2,1)S(1)}, u32[]{:S(2)}, u32[]{:S(2)}) collective-permute-start(bf16[192,640]{1,0:T(8,128)(2,1)S(1)} %get-tuple-element.37), channel_id=1, source_target_pairs={{0,8},{1,65},{16,24},{17,81},{32,40},{33,97},{48,56},{49,113},{4,1... | collective-permute-start | bytes 737288 | tf_op jit(solution)/shard_map/ppermute | solution.py:39
  12.8 7.5 %collective-permute-start.7 = (bf16[192,640]{1,0:T(8,128)(2,1)S(1)}, bf16[192,640]{1,0:T(8,128)(2,1)S(1)}, u32[]{:S(2)}, u32[]{:S(2)}) collective-permute-start(bf16[192,640]{1,0:T(8,128)(2,1)S(1)} %get-tuple-element.38), channel_id=1, source_target_pairs={{0,12},{1,67},{16,28},{17,83},{32,44},{33,99},{48,60},{49,115},{4,... | collective-permute-start | bytes 737288 | tf_op jit(solution)/shard_map/ppermute | solution.py:39
  14.0 13.4 %collective-permute-start.8 = (bf16[192,640]{1,0:T(8,128)(2,1)S(1)}, bf16[192,640]{1,0:T(8,128)(2,1)S(1)}, u32[]{:S(2)}, u32[]{:S(2)}) collective-permute-start(bf16[192,640]{1,0:T(8,128)(2,1)S(1)} %get-tuple-element.40), channel_id=1, source_target_pairs={{0,4},{1,3},{16,20},{17,19},{32,36},{33,35},{48,52},{49,51},{4,8},... | collective-permute-start | bytes 737288 | tf_op jit(solution)/shard_map/ppermute | solution.py:39
  17.2 11.0 %collective-permute-start.9 = (bf16[192,640]{1,0:T(8,128)(2,1)S(1)}, bf16[192,640]{1,0:T(8,128)(2,1)S(1)}, u32[]{:S(2)}, u32[]{:S(2)}) collective-permute-start(bf16[192,640]{1,0:T(8,128)(2,1)S(1)} %get-tuple-element.41), channel_id=1, source_target_pairs={{0,8},{1,65},{16,24},{17,81},{32,40},{33,97},{48,56},{49,113},{4,1... | collective-permute-start | bytes 737288 | tf_op jit(solution)/shard_map/ppermute | solution.py:39
  17.6 10.5 %collective-permute-start.10 = (bf16[192,640]{1,0:T(8,128)(2,1)S(1)}, bf16[192,640]{1,0:T(8,128)(2,1)S(1)}, u32[]{:S(2)}, u32[]{:S(2)}) collective-permute-start(bf16[192,640]{1,0:T(8,128)(2,1)S(1)} %get-tuple-element.42), channel_id=1, source_target_pairs={{0,12},{1,67},{16,28},{17,83},{32,44},{33,99},{48,60},{49,115},{4,... | collective-permute-start | bytes 737288 | tf_op jit(solution)/shard_map/ppermute | solution.py:39
  22.4 11.6 %collective-permute-start.20 = (bf16[128,640]{1,0:T(8,128)(2,1)S(1)}, bf16[128,640]{1,0:T(8,128)(2,1)S(1)}, u32[]{:S(2)}, u32[]{:S(2)}) collective-permute-start(bf16[128,640]{1,0:T(8,128)(2,1)S(1)} %get-tuple-element.49), channel_id=1, source_target_pairs={{0,2},{1,17},{16,18},{17,33},{32,34},{33,49},{48,50},{49,1},{4,6},... | collective-permute-start | bytes 491528 | tf_op jit(solution)/shard_map/ppermute | solution.py:39
  24.1 10.8 %collective-permute-start.21 = (bf16[128,640]{1,0:T(8,128)(2,1)S(1)}, bf16[128,640]{1,0:T(8,128)(2,1)S(1)}, u32[]{:S(2)}, u32[]{:S(2)}) collective-permute-start(bf16[128,640]{1,0:T(8,128)(2,1)S(1)} %get-tuple-element.50), channel_id=1, source_target_pairs={{0,64},{1,33},{16,80},{17,49},{32,96},{33,1},{48,112},{49,17},{4,6... | collective-permute-start | bytes 491528 | tf_op jit(solution)/shard_map/ppermute | solution.py:39
  27.4 7.5 %collective-permute-start.22 = (bf16[128,640]{1,0:T(8,128)(2,1)S(1)}, bf16[128,640]{1,0:T(8,128)(2,1)S(1)}, u32[]{:S(2)}, u32[]{:S(2)}) collective-permute-start(bf16[128,640]{1,0:T(8,128)(2,1)S(1)} %get-tuple-element.51), channel_id=1, source_target_pairs={{0,66},{1,49},{16,82},{17,1},{32,98},{33,17},{48,114},{49,33},{4,7... | collective-permute-start | bytes 491528 | tf_op jit(solution)/shard_map/ppermute | solution.py:39
  29.7 7.7 %collective-permute-start.11 = (bf16[128,640]{1,0:T(8,128)(2,1)S(1)}, bf16[128,640]{1,0:T(8,128)(2,1)S(1)}, u32[]{:S(2)}, u32[]{:S(2)}) collective-permute-start(bf16[128,640]{1,0:T(8,128)(2,1)S(1)} %get-tuple-element.44), channel_id=1, source_target_pairs={{0,16},{1,5},{16,32},{17,21},{32,48},{33,37},{48,0},{49,53},{4,20}... | collective-permute-start | bytes 491528 | tf_op jit(solution)/shard_map/ppermute | solution.py:39
  31.2 7.2 %collective-permute-start.12 = (bf16[128,640]{1,0:T(8,128)(2,1)S(1)}, bf16[128,640]{1,0:T(8,128)(2,1)S(1)}, u32[]{:S(2)}, u32[]{:S(2)}) collective-permute-start(bf16[128,640]{1,0:T(8,128)(2,1)S(1)} %get-tuple-element.45), channel_id=1, source_target_pairs={{0,32},{1,9},{16,48},{17,25},{32,0},{33,41},{48,16},{49,57},{4,36}... | collective-permute-start | bytes 491528 | tf_op jit(solution)/shard_map/ppermute | solution.py:39
  34.0 4.5 %collective-permute-start.13 = (bf16[128,640]{1,0:T(8,128)(2,1)S(1)}, bf16[128,640]{1,0:T(8,128)(2,1)S(1)}, u32[]{:S(2)}, u32[]{:S(2)}) collective-permute-start(bf16[128,640]{1,0:T(8,128)(2,1)S(1)} %get-tuple-element.46), channel_id=1, source_target_pairs={{0,48},{1,13},{16,0},{17,29},{32,16},{33,45},{48,32},{49,61},{4,52... | collective-permute-start | bytes 491528 | tf_op jit(solution)/shard_map/ppermute | solution.py:39
  35.0 6.9 %collective-permute-start.25 = (bf16[128,640]{1,0:T(8,128)(2,1)S(1)}, bf16[128,640]{1,0:T(8,128)(2,1)S(1)}, u32[]{:S(2)}, u32[]{:S(2)}) collective-permute-start(bf16[128,640]{1,0:T(8,128)(2,1)S(1)} %fusion.9), channel_id=1, source_target_pairs={{0,48},{1,13},{16,0},{17,29},{32,16},{33,45},{48,32},{49,61},{4,52... | collective-permute-start | bytes 491528 | tf_op jit(solution)/shard_map/ppermute | solution.py:39
  35.4 7.3 %collective-permute-start.24 = (bf16[128,640]{1,0:T(8,128)(2,1)S(1)}, bf16[128,640]{1,0:T(8,128)(2,1)S(1)}, u32[]{:S(2)}, u32[]{:S(2)}) collective-permute-start(bf16[128,640]{1,0:T(8,128)(2,1)S(1)} %fusion.9), channel_id=1, source_target_pairs={{0,32},{1,9},{16,48},{17,25},{32,0},{33,41},{48,16},{49,57},{4,36}... | collective-permute-start | bytes 491528 | tf_op jit(solution)/shard_map/ppermute | solution.py:39
  37.4 5.5 %collective-permute-start.23 = (bf16[128,640]{1,0:T(8,128)(2,1)S(1)}, bf16[128,640]{1,0:T(8,128)(2,1)S(1)}, u32[]{:S(2)}, u32[]{:S(2)}) collective-permute-start(bf16[128,640]{1,0:T(8,128)(2,1)S(1)} %fusion.9), channel_id=1, source_target_pairs={{0,16},{1,5},{16,32},{17,21},{32,48},{33,37},{48,0},{49,53},{4,20}... | collective-permute-start | bytes 491528 | tf_op jit(solution)/shard_map/ppermute | solution.py:39
  38.5 8.1 %collective-permute-start.16 = (bf16[128,640]{1,0:T(8,128)(2,1)S(1)}, bf16[128,640]{1,0:T(8,128)(2,1)S(1)}, u32[]{:S(2)}, u32[]{:S(2)}) collective-permute-start(bf16[128,640]{1,0:T(8,128)(2,1)S(1)} %fusion.8), channel_id=1, source_target_pairs={{0,66},{1,49},{16,82},{17,1},{32,98},{33,17},{48,114},{49,33},{4,7... | collective-permute-start | bytes 491528 | tf_op jit(solution)/shard_map/ppermute | solution.py:39
  41.9 6.8 %collective-permute-start.15 = (bf16[128,640]{1,0:T(8,128)(2,1)S(1)}, bf16[128,640]{1,0:T(8,128)(2,1)S(1)}, u32[]{:S(2)}, u32[]{:S(2)}) collective-permute-start(bf16[128,640]{1,0:T(8,128)(2,1)S(1)} %fusion.8), channel_id=1, source_target_pairs={{0,64},{1,33},{16,80},{17,49},{32,96},{33,1},{48,112},{49,17},{4,6... | collective-permute-start | bytes 491528 | tf_op jit(solution)/shard_map/ppermute | solution.py:39
  41.9 9.1 %collective-permute-start.14 = (bf16[128,640]{1,0:T(8,128)(2,1)S(1)}, bf16[128,640]{1,0:T(8,128)(2,1)S(1)}, u32[]{:S(2)}, u32[]{:S(2)}) collective-permute-start(bf16[128,640]{1,0:T(8,128)(2,1)S(1)} %fusion.8), channel_id=1, source_target_pairs={{0,2},{1,17},{16,18},{17,33},{32,34},{33,49},{48,50},{49,1},{4,6},... | collective-permute-start | bytes 491528 | tf_op jit(solution)/shard_map/ppermute | solution.py:39
  43.1 11.3 %collective-permute-start.28 = (bf16[128,640]{1,0:T(8,128)(2,1)S(1)}, bf16[128,640]{1,0:T(8,128)(2,1)S(1)}, u32[]{:S(2)}, u32[]{:S(2)}) collective-permute-start(bf16[128,640]{1,0:T(8,128)(2,1)S(1)} %add_convert_fusion.refs_0_), channel_id=1, source_target_pairs={{0,66},{1,49},{16,82},{17,1},{32,98},{33,17},{48,114},{49,33},{4,7... | collective-permute-start | bytes 491528 | tf_op jit(solution)/shard_map/ppermute | solution.py:39
  46.3 8.6 %collective-permute-start.27 = (bf16[128,640]{1,0:T(8,128)(2,1)S(1)}, bf16[128,640]{1,0:T(8,128)(2,1)S(1)}, u32[]{:S(2)}, u32[]{:S(2)}) collective-permute-start(bf16[128,640]{1,0:T(8,128)(2,1)S(1)} %add_convert_fusion.refs_0_), channel_id=1, source_target_pairs={{0,64},{1,33},{16,80},{17,49},{32,96},{33,1},{48,112},{49,17},{4,6... | collective-permute-start | bytes 491528 | tf_op jit(solution)/shard_map/ppermute | solution.py:39
  46.7 8.2 %collective-permute-start.26 = (bf16[128,640]{1,0:T(8,128)(2,1)S(1)}, bf16[128,640]{1,0:T(8,128)(2,1)S(1)}, u32[]{:S(2)}, u32[]{:S(2)}) collective-permute-start(bf16[128,640]{1,0:T(8,128)(2,1)S(1)} %add_convert_fusion.refs_0_), channel_id=1, source_target_pairs={{0,2},{1,17},{16,18},{17,33},{32,34},{33,49},{48,50},{49,1},{4,6},... | collective-permute-start | bytes 491528 | tf_op jit(solution)/shard_map/ppermute | solution.py:39
  51.2 6.6 %collective-permute-start.19 = (bf16[128,640]{1,0:T(8,128)(2,1)S(1)}, bf16[128,640]{1,0:T(8,128)(2,1)S(1)}, u32[]{:S(2)}, u32[]{:S(2)}) collective-permute-start(bf16[128,640]{1,0:T(8,128)(2,1)S(1)} %add_convert_fusion.1.refs_1_.refs_3_), channel_id=1, source_target_pairs={{0,48},{1,13},{16,0},{17,29},{32,16},{33,45},{48,32},{49,61},{4,52... | collective-permute-start | bytes 491528 | tf_op jit(solution)/shard_map/ppermute | solution.py:39
  53.7 6.0 %collective-permute-start.18 = (bf16[128,640]{1,0:T(8,128)(2,1)S(1)}, bf16[128,640]{1,0:T(8,128)(2,1)S(1)}, u32[]{:S(2)}, u32[]{:S(2)}) collective-permute-start(bf16[128,640]{1,0:T(8,128)(2,1)S(1)} %add_convert_fusion.1.refs_1_.refs_3_), channel_id=1, source_target_pairs={{0,32},{1,9},{16,48},{17,25},{32,0},{33,41},{48,16},{49,57},{4,36}... | collective-permute-start | bytes 491528 | tf_op jit(solution)/shard_map/ppermute | solution.py:39
  54.4 7.1 %collective-permute-start.17 = (bf16[128,640]{1,0:T(8,128)(2,1)S(1)}, bf16[128,640]{1,0:T(8,128)(2,1)S(1)}, u32[]{:S(2)}, u32[]{:S(2)}) collective-permute-start(bf16[128,640]{1,0:T(8,128)(2,1)S(1)} %add_convert_fusion.1.refs_1_.refs_3_), channel_id=1, source_target_pairs={{0,16},{1,5},{16,32},{17,21},{32,48},{33,37},{48,0},{49,53},{4,20}... | collective-permute-start | bytes 491528 | tf_op jit(solution)/shard_map/ppermute | solution.py:39
  62.9 6.5 %collective-permute-start.29 = (bf16[192,512]{1,0:T(8,128)(2,1)S(1)}, bf16[192,512]{1,0:T(8,128)(2,1)S(1)}, u32[]{:S(2)}, u32[]{:S(2)}) collective-permute-start(bf16[192,512]{1,0:T(8,128)(2,1)S(1)} %get-tuple-element.52), channel_id=1, source_target_pairs={{0,12},{1,67},{16,28},{17,83},{32,44},{33,99},{48,60},{49,115},{4,... | collective-permute-start | bytes 589832 | tf_op jit(solution)/shard_map/ppermute | solution.py:39
  64.7 6.1 %collective-permute-start.30 = (bf16[192,512]{1,0:T(8,128)(2,1)S(1)}, bf16[192,512]{1,0:T(8,128)(2,1)S(1)}, u32[]{:S(2)}, u32[]{:S(2)}) collective-permute-start(bf16[192,512]{1,0:T(8,128)(2,1)S(1)} %get-tuple-element.53), channel_id=1, source_target_pairs={{0,8},{1,65},{16,24},{17,81},{32,40},{33,97},{48,56},{49,113},{4,1... | collective-permute-start | bytes 589832 | tf_op jit(solution)/shard_map/ppermute | solution.py:39
  65.4 7.4 %collective-permute-start.31 = (bf16[192,512]{1,0:T(8,128)(2,1)S(1)}, bf16[192,512]{1,0:T(8,128)(2,1)S(1)}, u32[]{:S(2)}, u32[]{:S(2)}) collective-permute-start(bf16[192,512]{1,0:T(8,128)(2,1)S(1)} %get-tuple-element.54), channel_id=1, source_target_pairs={{0,4},{1,3},{16,20},{17,19},{32,36},{33,35},{48,52},{49,51},{4,8},... | collective-permute-start | bytes 589832 | tf_op jit(solution)/shard_map/ppermute | solution.py:39
  73.1 9.7 %collective-permute-start.32 = (f32[192]{0:T(256)S(1)}, f32[192]{0:T(256)S(1)}, u32[]{:S(2)}, u32[]{:S(2)}) collective-permute-start(f32[192]{0:T(256)S(1)} %fusion.5), channel_id=1, source_target_pairs={{0,1},{1,0},{2,3},{3,2},{4,5},{5,4},{6,7},{7,6},{8,9},{9,8},{10,11... | collective-permute-start | bytes 2312 | tf_op jit(solution)/shard_map/ppermute | solution.py:43

commit v9 on v6

--- a/solution.py
+++ b/solution.py
@@ -99,35 +99,60 @@
     return pack[:, part(places, 0, ss)], pack[:, pl.ds(half, pack.shape[1] - half)]
 
 
-def gram_kernel(share, chunk, places, *refs):
-    native = chunk == 0
-    count = SIZE if native else 2 * SIZE
-    norms, packs = refs[:SIZE], refs[count - SIZE : count]
-    outs, (left, right, product) = refs[count : count + SIZE], refs[count + SIZE :]
-    half, feats = product.shape
-    rows, ss = norms[0].shape[0], half // SIZE
-    for k in range(SIZE):
+def stack(places, norms, packs, left, right, native):
+    rows = norms[0].shape[0]
+    half, feats = left.shape[1], right.shape[1]
+    ss = half // SIZE
+    for k, (norm, pack) in enumerate(zip(norms, packs)):
         at = pl.ds(k * rows, rows)
-        left[at, :] = norms[k][:, pl.ds(0, half)]
+        left[at, :] = norm[:, pl.ds(0, half)]
         if native:
             right[at, pl.ds(0, ss)], right[at, pl.ds(ss, feats - ss)] = native_features(
-                places, packs[k], half
+                places, pack, half
             )
         else:
-            right[at, :] = packs[k][...]
-    product[...] = lax.dot_general(
+            right[at, :] = pack[...]
+
+
+def cross(left, right):
+    return lax.dot_general(
         left[...], right[...], (((0,), (0,)), ((), ())), preferred_element_type=F32
     )
-    if native:
-        row = lax.broadcasted_iota(jnp.int32, (ss, ss), 0)
-        col = lax.broadcasted_iota(jnp.int32, (ss, ss), 1)
-        product[part(places, 0, ss), pl.ds(0, ss)] -= jnp.where(row == col, share, 0.0)
+
+
+def emit(place, product, outs):
+    half, feats = product.shape
+    ss = half // SIZE
+    rest = pl.ds(ss, feats - ss)
     for by, out in enumerate(outs):
-        which = lax.rem(places[1 + chunk] + by, SIZE)
-        block = pl.ds(pl.multiple_of(which * ss, ss), ss)
-        rest = pl.ds(ss, feats - ss)
+        block = pl.ds(pl.multiple_of(lax.rem(place + by, SIZE) * ss, ss), ss)
         out[:, pl.ds(0, ss)] = product[block, pl.ds(0, ss)].astype(out.dtype)
         out[:, rest] = -product[block, rest].astype(out.dtype)
+
+
+def gram_early_kernel(places, *refs):
+    packs, (product, left, right) = refs[:-3], refs[-3:]
+    stack(places, packs, packs, left, right, True)
+    product[...] = cross(left, right)
+
+
+def gram_native_kernel(share, places, pack, before, *refs):
+    outs, (left, right, product) = refs[:SIZE], refs[SIZE:]
+    ss = left.shape[1] // SIZE
+    stack(places, [pack], [pack], left, right, True)
+    product[...] = before[...] + cross(left, right)
+    row = lax.broadcasted_iota(jnp.int32, (ss, ss), 0)
+    col = lax.broadcasted_iota(jnp.int32, (ss, ss), 1)
+    product[part(places, 0, ss), pl.ds(0, ss)] -= jnp.where(row == col, share, 0.0)
+    emit(places[1], product, outs)
+
+
+def gram_far_kernel(places, *refs):
+    norms, packs, outs = refs[:SIZE], refs[SIZE : 2 * SIZE], refs[2 * SIZE : 3 * SIZE]
+    left, right, product = refs[3 * SIZE :]
+    stack(places, norms, packs, left, right, False)
+    product[...] = cross(left, right)
+    emit(places[2], product, outs)
 
 
 def gather_weights(place, pieces, weights):
@@ -154,14 +179,35 @@
     out[...] = times(left[...], weights[...])
 
 
-def apply_far_kernel(first, count, places, *refs):
-    packs, pieces, before = refs[:count], refs[count : count + SIZE], refs[count + SIZE]
-    outs, weights = refs[count + SIZE + 1 : -1], refs[-1]
-    rows = packs[0].shape[0]
+def apply_early_kernel(places, far1, far2, far3, piece0, piece1, piece2, before, *refs):
+    outs, (left, weights) = refs[: SIZE - 1], refs[SIZE - 1 :]
+    rows = far1.shape[0]
+    last = jnp.zeros(piece0.shape, piece0.dtype)
+    gather_weights(places[2], (piece0, piece1, piece2, last), weights)
+    for k, pack in enumerate((far1, far2, far3)):
+        left[pl.ds(k * rows, rows), :] = pack[...]
+    product = times(left[...], weights[...])
+    for k, out in enumerate(outs):
+        sofar = before[pl.ds((k + 1) * rows, rows), :]
+        out[...] = (product[k * rows : (k + 1) * rows] + sofar).astype(out.dtype)
+
+
+def apply_sent_kernel(places, far1, far2, far3, piece, before, early1, early2, early3, *outs):
+    rows, ss = far1.shape[0], piece.shape[0]
+    which = lax.rem(places[2] + 1, SIZE)
+    block = pl.ds(pl.multiple_of(which * ss, ss), ss)
+    for k, (pack, early, out) in enumerate(
+        zip((far1, far2, far3), (early1, early2, early3), outs)
+    ):
+        out[...] = early[...]
+        sofar = before[pl.ds((k + 1) * rows, rows), block]
+        out[:, block] = (times(pack[...], piece[...]) + sofar).astype(out.dtype)
+
+
+def apply_kept_kernel(places, pack, *refs):
+    pieces, (before, out, weights) = refs[:SIZE], refs[SIZE:]
     gather_weights(places[2], pieces, weights)
-    for k, (pack, out) in enumerate(zip(packs, outs)):
-        sofar = before[pl.ds((first + k) * rows, rows), :]
-        out[...] = (times(pack[...], weights[...]) + sofar).astype(out.dtype)
+    out[...] = times(pack[...], weights[...]) + before[pl.ds(0, pack.shape[0]), :]
 
 
 def shapes(*described):
@@ -227,26 +273,35 @@
     near = exchanged(near[0], near.__getitem__, GATHER)
     far = exchanged(far[0], far.__getitem__, GATHER)
 
-    def weights_of(chunk, packs, name):
-        own, *sends = kernel_call(
-            functools.partial(gram_kernel, level * SIZE / groups, chunk),
-            name,
-            shapes(((ss, feats), F32), *[((ss, feats), BF16)] * 3),
-            len(packs),
-            [
-                pltpu.VMEM((SIZE * rows, half), BF16),
-                pltpu.VMEM((SIZE * rows, feats), BF16),
-                pltpu.VMEM((half, feats), F32),
-            ],
-            flops,
-        )(places, *packs)
+    blocks = shapes(((ss, feats), F32), *[((ss, feats), BF16)] * 3)
+    product = pltpu.VMEM((half, feats), F32)
+
+    def operands(count):
+        return [pltpu.VMEM((count * rows, half), BF16), pltpu.VMEM((count * rows, feats), BF16)]
+
+    early = kernel_call(
+        gram_early_kernel, "gram_early", shapes(((half, feats), F32)), 3, operands(3), flops
+    )(places, *near[:3])[0]
+    near_blocks = kernel_call(
+        functools.partial(gram_native_kernel, level * SIZE / groups),
+        "gram_native",
+        blocks,
+        2,
+        operands(1) + [product],
+        flops // 4,
+    )(places, near[3], early)
+    far_blocks = kernel_call(
+        gram_far_kernel, "gram_far", blocks, 2 * SIZE, operands(SIZE) + [product], flops
+    )(places, *near, *far)
+
+    def weights_of(chunk, own, *sends):
         total = added(own, lambda by: sends[by - 1], FIRST[chunk])
         shared = total.astype(BF16)
         piece = added(total, lambda by: shared, SECOND[chunk]).astype(BF16)
         return exchanged(piece, lambda by: piece, FIRST[chunk])
 
-    near_weights = weights_of(0, near, "gram_native")
-    far_weights = weights_of(1, near + far, "gram_far")
+    near_weights = weights_of(0, *near_blocks)
+    far_weights = weights_of(1, *far_blocks)
 
     sofar = kernel_call(
         apply_native_kernel,
@@ -256,21 +311,21 @@
         [pltpu.VMEM((SIZE * rows, feats), BF16), pltpu.VMEM((half, feats), BF16)],
         flops,
     )(places, *near, *near_weights)[0]
-    parts = kernel_call(
-        functools.partial(apply_far_kernel, 1, SIZE - 1),
-        "apply_sent",
-        shapes(*[((rows, half), BF16)] * 3),
-        2 * SIZE,
-        [pltpu.VMEM((half, feats), BF16)],
+    messages = shapes(*[((rows, half), BF16)] * 3)
+    weights = pltpu.VMEM((half, feats), BF16)
+    most = kernel_call(
+        apply_early_kernel,
+        "apply_early",
+        messages,
+        7,
+        [pltpu.VMEM((3 * rows, feats), BF16), weights],
         flops * 3 // 4,
-    )(places, *far[1:], *far_weights, sofar)
+    )(places, *far[1:], *far_weights[:3], sofar)
+    parts = kernel_call(apply_sent_kernel, "apply_sent", messages, 8, (), flops // 4)(
+        places, *far[1:], far_weights[3], sofar, *most
+    )
     grad_n = kernel_call(
-        functools.partial(apply_far_kernel, 0, 1),
-        "apply_kept",
-        shapes(((rows, half), F32)),
-        SIZE + 2,
-        [pltpu.VMEM((half, feats), BF16)],
-        flops // 4,
+        apply_kept_kernel, "apply_kept", shapes(((rows, half), F32)), SIZE + 2, [weights], flops // 4
     )(places, far[0], *far_weights, sofar)[0]
     norm_f = norm_own.astype(F32)
     grad_n = grad_n + level * norm_f

time: 80.6 us -> 77.5 us (0.962)
  starting transfers between devices: 47.6 us -> 44.8 us
  waiting for transfers between devices: 19.7 us -> 17.9 us
  Pallas kernels: 9.08 us -> 10.6 us
    ppermute x3, starting transfers between devices: 13.4 us -> 8.5 us  [other_core(): return lax.ppermute(array, 'sec', [(0, 1), (1, 0)])]
    ppermute x27, starting transfers between devices: 34.2 us -> 36.3 us  [shifted(): return lax.ppermute(array, AXES, pairs)]
    ppermute x27, waiting for transfers between devices: 19 us -> 17.1 us  [shifted(): return lax.ppermute(array, AXES, pairs)]
    pallas_call x4 -> x6, Pallas kernels: 5.56 us -> 7.12 us  [the longest x1 1.57 us: body(): kernel_call(gram_far_kernel, 'gram_far', blocks, 2 * SIZE, operands(SIZE)...]
  transfers between devices with their start and end apart: 30 -> 30, of which waited for: 12 -> 14; matrix products, arithmetic and copies ran while one was open for 1% -> 1% of each run, Pallas kernels for 8% -> 11%
where the time goes in v9:
time: 77.5 us; the launch traced here: 77.3 us
  starting transfers between devices  44.8 us (58%)
  waiting for transfers between devices  17.9 us (23%)
  Pallas kernels  10.6 us (14%)
  local copies, waits for them, and re-layouts  2.06 us (3%)
  other arithmetic  1.86 us (2%)
    ppermute x27, starting transfers between devices, shifted(): return lax.ppermute(array, AXES, pairs)  36.3 us
    ppermute x27, waiting for transfers between devices, shifted(): return lax.ppermute(array, AXES, pairs)  17.1 us
    ppermute x3, starting transfers between devices, other_core(): return lax.ppermute(array, 'sec', [(0, 1), (1, 0)])  8.5 us
    unnamed x4, local copies, waits for them, and re-layouts  2.06 us
    pallas_call x1, Pallas kernels, body(): kernel_call(gram_far_kernel, 'gram_far', blocks, 2 * SIZE, operands(SIZE)...  1.57 us
  transfers between devices with their start and end apart: 30, of which 14 were waited for; matrix products, arithmetic and copies ran while one was open for 1% of the time, Pallas kernels for 11%

profile of v9, /device:TPU:1, one launch (start us, length us, event | category | flops | bytes accessed | tf_op | source)
XLA Modules:
  0.0 77.3 jit_solution(10740107189782965979)
XLA Ops:
  0.0 1.4 %collective-permute-start.1 = (bf16[192,2048]{1,0:T(8,128)(2,1)}, bf16[192,2048]{1,0:T(8,128)(2,1)S(1)}, u32[]{:S(2)}, u32[]{:S(2)}) collective-permute-start(bf16[192,2048]{1,0:T(8,128)(2,1)} %t_own.3), channel_id=1, source_target_pairs={{0,1},{1,0},{2,3},{3,2},{4,5},{5,4},{6,7},{7,6},{8,9},{9,8},{10,11... | collective-permute-start | bytes 2359304 | tf_op jit(solution)/shard_map/ppermute | solution.py:42
  1.4 1.1 %copy-done = bf16[192,2048]{1,0:T(8,128)(2,1)S(1)} copy-done((bf16[192,2048]{1,0:T(8,128)(2,1)S(1)}, bf16[192,2048]{1,0:T(8,128)(2,1)}, u32[]{:S(2)}) %copy-start) | copy-done | bytes 786456
  2.6 0.9 %copy-done.1 = bf16[192,512]{1,0:T(8,128)(2,1)S(1)} copy-done((bf16[192,512]{1,0:T(8,128)(2,1)S(1)}, bf16[192,512]{1,0:T(8,128)(2,1)}, u32[]{:S(2)}) %copy-start.1) | copy-done | bytes 196632
  3.8 1.0 %pack_own.1 = (bf16[192,1024]{1,0:T(8,128)(2,1)S(1)}, bf16[192,1024]{1,0:T(8,128)(2,1)S(1)}, bf16[192,1024]{1,0:T(8,128)(2,1)S(1)}, bf16[192,1024]{1,0:T(8,128)(...) custom-call(s32[3]{0:T(128)S(1)} %pad_add_fusion.places, bf16[192,512]{1,0:T(8,128)(2,1)S(1)} %copy-done.1, ...), custom_call_target="tpu_custom_call" | custom-call | bytes 4194304 | tf_op jit(solution)/shard_map/pack_own/pallas_call | solution.py:253
  4.9 1.4 %collective-permute-start.2 = (bf16[192,1024]{1,0:T(8,128)(2,1)S(1)}, bf16[192,1024]{1,0:T(8,128)(2,1)S(1)}, u32[]{:S(2)}, u32[]{:S(2)}) collective-permute-start(bf16[192,1024]{1,0:T(8,128)(2,1)S(1)} %get-tuple-element.37), channel_id=1, source_target_pairs={{0,4},{1,3},{16,20},{17,19},{32,36},{33,35},{48,52},{49,51},{4,8},... | collective-permute-start | bytes 1179656 | tf_op jit(solution)/shard_map/ppermute | solution.py:38
  6.2 2.5 %collective-permute-start.3 = (bf16[192,1024]{1,0:T(8,128)(2,1)S(1)}, bf16[192,1024]{1,0:T(8,128)(2,1)S(1)}, u32[]{:S(2)}, u32[]{:S(2)}) collective-permute-start(bf16[192,1024]{1,0:T(8,128)(2,1)S(1)} %get-tuple-element.38), channel_id=1, source_target_pairs={{0,8},{1,65},{16,24},{17,81},{32,40},{33,97},{48,56},{49,113},{4,1... | collective-permute-start | bytes 1179656 | tf_op jit(solution)/shard_map/ppermute | solution.py:38
  8.7 1.2 %collective-permute-start.4 = (bf16[192,1024]{1,0:T(8,128)(2,1)S(1)}, bf16[192,1024]{1,0:T(8,128)(2,1)S(1)}, u32[]{:S(2)}, u32[]{:S(2)}) collective-permute-start(bf16[192,1024]{1,0:T(8,128)(2,1)S(1)} %get-tuple-element.39), channel_id=1, source_target_pairs={{0,12},{1,67},{16,28},{17,83},{32,44},{33,99},{48,60},{49,115},{4,... | collective-permute-start | bytes 1179656 | tf_op jit(solution)/shard_map/ppermute | solution.py:38
  9.8 0.8 %pack_far.1 = (bf16[192,640]{1,0:T(8,128)(2,1)S(1)}, bf16[192,640]{1,0:T(8,128)(2,1)S(1)}, bf16[192,640]{1,0:T(8,128)(2,1)S(1)}, bf16[192,640]{1,0:T(8,128)(2,1)S(1)}) custom-call(s32[3]{0:T(128)S(1)} %pad_add_fusion.places, bf16[192,512]{1,0:T(8,128)(2,1)S(1)} %collective-permute-done.s_far, bf16[192,2048]{1,0:T(8,128)(2,1)S(1)} %collective-permute-done.1.t_far, ...), custom_call_target="tpu_custom_call" | custom-call | bytes 4194304 | tf_op jit(solution)/shard_map/pack_far/pallas_call | solution.py:259
  10.7 0.4 collective-permute-start.5
  11.0 0.9 %collective-permute-start.6 = (bf16[192,640]{1,0:T(8,128)(2,1)S(1)}, bf16[192,640]{1,0:T(8,128)(2,1)S(1)}, u32[]{:S(2)}, u32[]{:S(2)}) collective-permute-start(bf16[192,640]{1,0:T(8,128)(2,1)S(1)} %get-tuple-element.41), channel_id=1, source_target_pairs={{0,8},{1,65},{16,24},{17,81},{32,40},{33,97},{48,56},{49,113},{4,1... | collective-permute-start | bytes 737288 | tf_op jit(solution)/shard_map/ppermute | solution.py:38
  11.9 1.2 %collective-permute-done.2.refs_1_ = bf16[192,1024]{1,0:T(8,128)(2,1)S(1)} collective-permute-done((bf16[192,1024]{1,0:T(8,128)(2,1)S(1)}, bf16[192,1024]{1,0:T(8,128)(2,1)S(1)}, u32[]{:S(2)}, u32[]{:S(2)}) %collective-permute-start.2) | collective-permute-done | bytes 393248 | tf_op jit(solution)/shard_map/ppermute | solution.py:38
  13.1 1.4 %collective-permute-start.7 = (bf16[192,640]{1,0:T(8,128)(2,1)S(1)}, bf16[192,640]{1,0:T(8,128)(2,1)S(1)}, u32[]{:S(2)}, u32[]{:S(2)}) collective-permute-start(bf16[192,640]{1,0:T(8,128)(2,1)S(1)} %get-tuple-element.42), channel_id=1, source_target_pairs={{0,12},{1,67},{16,28},{17,83},{32,44},{33,99},{48,60},{49,115},{4,... | collective-permute-start | bytes 737288 | tf_op jit(solution)/shard_map/ppermute | solution.py:38
  14.4 4.0 %collective-permute-done.3.refs_2_ = bf16[192,1024]{1,0:T(8,128)(2,1)S(1)} collective-permute-done((bf16[192,1024]{1,0:T(8,128)(2,1)S(1)}, bf16[192,1024]{1,0:T(8,128)(2,1)S(1)}, u32[]{:S(2)}, u32[]{:S(2)}) %collective-permute-start.3) | collective-permute-done | bytes 393248 | tf_op jit(solution)/shard_map/ppermute | solution.py:38
  18.4 1.4 %gram_early.1.before = f32[512,640]{1,0:T(8,128)S(1)} custom-call(s32[3]{0:T(128)S(1)} %pad_add_fusion.places, bf16[192,1024]{1,0:T(8,128)(2,1)S(1)} %get-tuple-element.36.refs_0_, bf16[192,1024]{1,0:T(8,128)(2,1)S(1)} %collective-permute-done.2.refs_1_, bf16[192,1024]{1,0:T(8,128)(2,1)S(1)} %collective-permute-done.3.refs_2_), custom_call_target="tpu_custom_call" | custom-call | flops 503316480 | bytes 4194304 | tf_op jit(solution)/shard_map/gram_early/pallas_call | solution.py:282
  19.8 1.1 %gram_native.1 = (f32[128,640]{1,0:T(8,128)S(1)}, bf16[128,640]{1,0:T(8,128)(2,1)S(1)}, bf16[128,640]{1,0:T(8,128)(2,1)S(1)}, bf16[128,640]{1,0:T(8,128)(2,1)S(1)}) custom-call(s32[3]{0:T(128)S(1)} %pad_add_fusion.places, bf16[192,1024]{1,0:T(8,128)(2,1)S(1)} %collective-permute-done.4.refs_3_.pack, f32[512,640]{1,0:T(8,128)S(1)} %gram_early.1.before), custom_call_target="tpu_custom_call" | custom-call | flops 125829120 | bytes 4194304 | tf_op jit(solution)/shard_map/gram_native/pallas_call | solution.py:285
  20.9 3.8 %collective-permute-start.19 = (bf16[128,640]{1,0:T(8,128)(2,1)S(1)}, bf16[128,640]{1,0:T(8,128)(2,1)S(1)}, u32[]{:S(2)}, u32[]{:S(2)}) collective-permute-start(bf16[128,640]{1,0:T(8,128)(2,1)S(1)} %get-tuple-element.50), channel_id=1, source_target_pairs={{0,66},{1,49},{16,82},{17,1},{32,98},{33,17},{48,114},{49,33},{4,7... | collective-permute-start | bytes 491528 | tf_op jit(solution)/shard_map/ppermute | solution.py:38
  24.7 0.7 collective-permute-start.17
  25.4 1.6 %gram_far.1 = (f32[128,640]{1,0:T(8,128)S(1)}, bf16[128,640]{1,0:T(8,128)(2,1)S(1)}, bf16[128,640]{1,0:T(8,128)(2,1)S(1)}, bf16[128,640]{1,0:T(8,128)(2,1)S(1)}) custom-call(s32[3]{0:T(128)S(1)} %pad_add_fusion.places, bf16[192,1024]{1,0:T(8,128)(2,1)S(1)} %get-tuple-element.36.refs_0_, bf16[192,1024]{1,0:T(8,128)(2,1)S(1)} %collective-permute-done.2.refs_1_, ...), custom_call_target="tpu_custom_call" | custom-call | flops 503316480 | bytes 4194304 | tf_op jit(solution)/shard_map/gram_far/pallas_call | solution.py:293
  27.0 2.6 %collective-permute-start.10 = (bf16[128,640]{1,0:T(8,128)(2,1)S(1)}, bf16[128,640]{1,0:T(8,128)(2,1)S(1)}, u32[]{:S(2)}, u32[]{:S(2)}) collective-permute-start(bf16[128,640]{1,0:T(8,128)(2,1)S(1)} %get-tuple-element.46), channel_id=1, source_target_pairs={{0,48},{1,13},{16,0},{17,29},{32,16},{33,45},{48,32},{49,61},{4,52... | collective-permute-start | bytes 491528 | tf_op jit(solution)/shard_map/ppermute | solution.py:38
  29.9 0.7 collective-permute-start.8
  30.7 1.4 %collective-permute-done.17 = bf16[128,640]{1,0:T(8,128)(2,1)S(1)} collective-permute-done((bf16[128,640]{1,0:T(8,128)(2,1)S(1)}, bf16[128,640]{1,0:T(8,128)(2,1)S(1)}, u32[]{:S(2)}, u32[]{:S(2)}) %collective-permute-start.17) | collective-permute-done | bytes 163872 | tf_op jit(solution)/shard_map/ppermute | solution.py:38
  32.2 2.4 %collective-permute-start.22 = (bf16[128,640]{1,0:T(8,128)(2,1)S(1)}, bf16[128,640]{1,0:T(8,128)(2,1)S(1)}, u32[]{:S(2)}, u32[]{:S(2)}) collective-permute-start(bf16[128,640]{1,0:T(8,128)(2,1)S(1)} %fusion.9), channel_id=1, source_target_pairs={{0,48},{1,13},{16,0},{17,29},{32,16},{33,45},{48,32},{49,61},{4,52... | collective-permute-start | bytes 491528 | tf_op jit(solution)/shard_map/ppermute | solution.py:38
  34.7 0.5 collective-permute-start.21
  35.1 0.5 collective-permute-start.20
  35.7 1.6 %collective-permute-done.8 = bf16[128,640]{1,0:T(8,128)(2,1)S(1)} collective-permute-done((bf16[128,640]{1,0:T(8,128)(2,1)S(1)}, bf16[128,640]{1,0:T(8,128)(2,1)S(1)}, u32[]{:S(2)}, u32[]{:S(2)}) %collective-permute-start.8) | collective-permute-done | bytes 163872 | tf_op jit(solution)/shard_map/ppermute | solution.py:38
  37.4 2.1 %collective-permute-start.13 = (bf16[128,640]{1,0:T(8,128)(2,1)S(1)}, bf16[128,640]{1,0:T(8,128)(2,1)S(1)}, u32[]{:S(2)}, u32[]{:S(2)}) collective-permute-start(bf16[128,640]{1,0:T(8,128)(2,1)S(1)} %fusion.8), channel_id=1, source_target_pairs={{0,66},{1,49},{16,82},{17,1},{32,98},{33,17},{48,114},{49,33},{4,7... | collective-permute-start | bytes 491528 | tf_op jit(solution)/shard_map/ppermute | solution.py:38
  39.4 1.5 %collective-permute-start.12 = (bf16[128,640]{1,0:T(8,128)(2,1)S(1)}, bf16[128,640]{1,0:T(8,128)(2,1)S(1)}, u32[]{:S(2)}, u32[]{:S(2)}) collective-permute-start(bf16[128,640]{1,0:T(8,128)(2,1)S(1)} %fusion.8), channel_id=1, source_target_pairs={{0,64},{1,33},{16,80},{17,49},{32,96},{33,1},{48,112},{49,17},{4,6... | collective-permute-start | bytes 491528 | tf_op jit(solution)/shard_map/ppermute | solution.py:38
  40.9 1.2 %collective-permute-done.20 = bf16[128,640]{1,0:T(8,128)(2,1)S(1)} collective-permute-done((bf16[128,640]{1,0:T(8,128)(2,1)S(1)}, bf16[128,640]{1,0:T(8,128)(2,1)S(1)}, u32[]{:S(2)}, u32[]{:S(2)}) %collective-permute-start.20) | collective-permute-done | bytes 163872 | tf_op jit(solution)/shard_map/ppermute | solution.py:38
  42.3 0.6 collective-permute-start.23
  42.8 2.2 %collective-permute-start.24 = (bf16[128,640]{1,0:T(8,128)(2,1)S(1)}, bf16[128,640]{1,0:T(8,128)(2,1)S(1)}, u32[]{:S(2)}, u32[]{:S(2)}) collective-permute-start(bf16[128,640]{1,0:T(8,128)(2,1)S(1)} %add_convert_fusion.refs_4_), channel_id=1, source_target_pairs={{0,64},{1,33},{16,80},{17,49},{32,96},{33,1},{48,112},{49,17},{4,6... | collective-permute-start | bytes 491528 | tf_op jit(solution)/shard_map/ppermute | solution.py:38
  45.0 0.9 %collective-permute-done.13 = bf16[128,640]{1,0:T(8,128)(2,1)S(1)} collective-permute-done((bf16[128,640]{1,0:T(8,128)(2,1)S(1)}, bf16[128,640]{1,0:T(8,128)(2,1)S(1)}, u32[]{:S(2)}, u32[]{:S(2)}) %collective-permute-start.13) | collective-permute-done | bytes 163872 | tf_op jit(solution)/shard_map/ppermute | solution.py:38
  45.9 3.4 %collective-permute-start.25 = (bf16[128,640]{1,0:T(8,128)(2,1)S(1)}, bf16[128,640]{1,0:T(8,128)(2,1)S(1)}, u32[]{:S(2)}, u32[]{:S(2)}) collective-permute-start(bf16[128,640]{1,0:T(8,128)(2,1)S(1)} %add_convert_fusion.refs_4_), channel_id=1, source_target_pairs={{0,66},{1,49},{16,82},{17,1},{32,98},{33,17},{48,114},{49,33},{4,7... | collective-permute-start | bytes 491528 | tf_op jit(solution)/shard_map/ppermute | solution.py:38
  49.3 0.6 collective-permute-done.11
  50.0 1.2 %collective-permute-start.14 = (bf16[128,640]{1,0:T(8,128)(2,1)S(1)}, bf16[128,640]{1,0:T(8,128)(2,1)S(1)}, u32[]{:S(2)}, u32[]{:S(2)}) collective-permute-start(bf16[128,640]{1,0:T(8,128)(2,1)S(1)} %add_convert_fusion.1.refs_0_.piece0), channel_id=1, source_target_pairs={{0,16},{1,5},{16,32},{17,21},{32,48},{33,37},{48,0},{49,53},{4,20}... | collective-permute-start | bytes 491528 | tf_op jit(solution)/shard_map/ppermute | solution.py:38
  51.2 1.9 %collective-permute-start.15 = (bf16[128,640]{1,0:T(8,128)(2,1)S(1)}, bf16[128,640]{1,0:T(8,128)(2,1)S(1)}, u32[]{:S(2)}, u32[]{:S(2)}) collective-permute-start(bf16[128,640]{1,0:T(8,128)(2,1)S(1)} %add_convert_fusion.1.refs_0_.piece0), channel_id=1, source_target_pairs={{0,32},{1,9},{16,48},{17,25},{32,0},{33,41},{48,16},{49,57},{4,36}... | collective-permute-start | bytes 491528 | tf_op jit(solution)/shard_map/ppermute | solution.py:38
  53.1 1.1 %collective-permute-start.16 = (bf16[128,640]{1,0:T(8,128)(2,1)S(1)}, bf16[128,640]{1,0:T(8,128)(2,1)S(1)}, u32[]{:S(2)}, u32[]{:S(2)}) collective-permute-start(bf16[128,640]{1,0:T(8,128)(2,1)S(1)} %add_convert_fusion.1.refs_0_.piece0), channel_id=1, source_target_pairs={{0,48},{1,13},{16,0},{17,29},{32,16},{33,45},{48,32},{49,61},{4,52... | collective-permute-start | bytes 491528 | tf_op jit(solution)/shard_map/ppermute | solution.py:38
  54.2 1.4 %apply_native.1.refs_4_.before = f32[768,512]{1,0:T(8,128)S(1)} custom-call(s32[3]{0:T(128)S(1)} %pad_add_fusion.places, bf16[192,1024]{1,0:T(8,128)(2,1)S(1)} %get-tuple-element.36.refs_0_, bf16[192,1024]{1,0:T(8,128)(2,1)S(1)} %collective-permute-done.2.refs_1_, bf16[192,1024]{1,0:T(8,128)(2,1)S(1)} %collective-permute-done.3.refs_2_, ...), custom_call_target="tpu_custom_call" | custom-call | flops 503316480 | bytes 4194304 | tf_op jit(solution)/shard_map/apply_native/pallas_call | solution.py:306
  55.8 1.8 %collective-permute-done.15.refs_2_.piece2 = bf16[128,640]{1,0:T(8,128)(2,1)S(1)} collective-permute-done((bf16[128,640]{1,0:T(8,128)(2,1)S(1)}, bf16[128,640]{1,0:T(8,128)(2,1)S(1)}, u32[]{:S(2)}, u32[]{:S(2)}) %collective-permute-start.15) | collective-permute-done | bytes 163872 | tf_op jit(solution)/shard_map/ppermute | solution.py:38
  57.5 1.2 %apply_early.1 = (bf16[192,512]{1,0:T(8,128)(2,1)S(1)}, bf16[192,512]{1,0:T(8,128)(2,1)S(1)}, bf16[192,512]{1,0:T(8,128)(2,1)S(1)}) custom-call(s32[3]{0:T(128)S(1)} %pad_add_fusion.places, bf16[192,640]{1,0:T(8,128)(2,1)S(1)} %collective-permute-done.5.refs_5_.far1, bf16[192,640]{1,0:T(8,128)(2,1)S(1)} %collective-permute-done.6.refs_6_.far2, ...), custom_call_target="tpu_custom_call" | custom-call | flops 377487360 | bytes 4194304 | tf_op jit(solution)/shard_map/apply_early/pallas_call | solution.py:316
  58.8 0.9 %apply_sent.1 = (bf16[192,512]{1,0:T(8,128)(2,1)S(1)}, bf16[192,512]{1,0:T(8,128)(2,1)S(1)}, bf16[192,512]{1,0:T(8,128)(2,1)S(1)}) custom-call(s32[3]{0:T(128)S(1)} %pad_add_fusion.places, bf16[192,640]{1,0:T(8,128)(2,1)S(1)} %collective-permute-done.5.refs_5_.far1, bf16[192,640]{1,0:T(8,128)(2,1)S(1)} %collective-permute-done.6.refs_6_.far2, ...), custom_call_target="tpu_custom_call" | custom-call | flops 125829120 | bytes 4194304 | tf_op jit(solution)/shard_map/apply_sent/pallas_call | solution.py:324
  59.7 0.8 %collective-permute-start.28 = (bf16[192,512]{1,0:T(8,128)(2,1)S(1)}, bf16[192,512]{1,0:T(8,128)(2,1)S(1)}, u32[]{:S(2)}, u32[]{:S(2)}) collective-permute-start(bf16[192,512]{1,0:T(8,128)(2,1)S(1)} %get-tuple-element.56), channel_id=1, source_target_pairs={{0,4},{1,3},{16,20},{17,19},{32,36},{33,35},{48,52},{49,51},{4,8},... | collective-permute-start | bytes 589832 | tf_op jit(solution)/shard_map/ppermute | solution.py:38
  60.5 2.4 %collective-permute-start.27 = (bf16[192,512]{1,0:T(8,128)(2,1)S(1)}, bf16[192,512]{1,0:T(8,128)(2,1)S(1)}, u32[]{:S(2)}, u32[]{:S(2)}) collective-permute-start(bf16[192,512]{1,0:T(8,128)(2,1)S(1)} %get-tuple-element.55), channel_id=1, source_target_pairs={{0,8},{1,65},{16,24},{17,81},{32,40},{33,97},{48,56},{49,113},{4,1... | collective-permute-start | bytes 589832 | tf_op jit(solution)/shard_map/ppermute | solution.py:38
  63.0 1.0 %apply_kept.1 = f32[192,512]{1,0:T(8,128)S(1)} custom-call(s32[3]{0:T(128)S(1)} %pad_add_fusion.places, bf16[192,640]{1,0:T(8,128)(2,1)S(1)} %get-tuple-element.35.refs_4_.pack, bf16[128,640]{1,0:T(8,128)(2,1)S(1)} %add_convert_fusion.1.refs_0_.piece0, bf16[128,640]{1,0:T(8,128)(2,1)S(1)} %collective-permute-done.14.refs_1_.piece1, ...), custom_call_target="tpu_custom_call" | custom-call | flops 125829120 | bytes 4194304 | tf_op jit(solution)/shard_map/apply_kept/pallas_call | solution.py:327
  64.0 1.6 %collective-permute-done.28 = bf16[192,512]{1,0:T(8,128)(2,1)S(1)} collective-permute-done((bf16[192,512]{1,0:T(8,128)(2,1)S(1)}, bf16[192,512]{1,0:T(8,128)(2,1)S(1)}, u32[]{:S(2)}, u32[]{:S(2)}) %collective-permute-start.28) | collective-permute-done | bytes 196640 | tf_op jit(solution)/shard_map/ppermute | solution.py:38
  65.5 2.5 %collective-permute-done.27 = bf16[192,512]{1,0:T(8,128)(2,1)S(1)} collective-permute-done((bf16[192,512]{1,0:T(8,128)(2,1)S(1)}, bf16[192,512]{1,0:T(8,128)(2,1)S(1)}, u32[]{:S(2)}, u32[]{:S(2)}) %collective-permute-start.27) | collective-permute-done | bytes 196640 | tf_op jit(solution)/shard_map/ppermute | solution.py:38
  68.5 7.1 %collective-permute-start.29 = (f32[192]{0:T(256)S(1)}, f32[192]{0:T(256)S(1)}, u32[]{:S(2)}, u32[]{:S(2)}) collective-permute-start(f32[192]{0:T(256)S(1)} %fusion.5), channel_id=1, source_target_pairs={{0,1},{1,0},{2,3},{3,2},{4,5},{5,4},{6,7},{7,6},{8,9},{9,8},{10,11... | collective-permute-start | bytes 2312 | tf_op jit(solution)/shard_map/ppermute | solution.py:42
  75.7 0.7 collective-permute-done.29
  76.4 0.9 %fusion.7 = f32[192,512]{1,0:T(8,128)} fusion(f32[192]{0:T(256)S(1)} %reduce, f32[192]{0:T(256)S(1)} %add.85, bf16[192,1024]{1,0:T(8,128)(2,1)S(1)} %get-tuple-element.36.refs_0_, bf16[192,512]{1,0:T(8,128)(2,1)S(1)} %collective-permute-done.28, bf16[192,512]{1,0:T(8,128)(2,1)S(1)} %collective-permute-done.27, ...), kind=kLoop, calls=%fused_computation.10 | loop fusion | flops 1277952 | bytes 1574400 | tf_op jit(solution)/shard_map/mul | solution.py:335
  (35 shorter events, 2.3 us)
Async XLA Ops:
  0.0 3.8 %collective-permute-start.1 = (bf16[192,2048]{1,0:T(8,128)(2,1)}, bf16[192,2048]{1,0:T(8,128)(2,1)S(1)}, u32[]{:S(2)}, u32[]{:S(2)}) collective-permute-start(bf16[192,2048]{1,0:T(8,128)(2,1)} %t_own.3), channel_id=1, source_target_pairs={{0,1},{1,0},{2,3},{3,2},{4,5},{5,4},{6,7},{7,6},{8,9},{9,8},{10,11... | collective-permute-start | bytes 2359304 | tf_op jit(solution)/shard_map/ppermute | solution.py:42
  1.4 2.4 %collective-permute-start = (bf16[192,512]{1,0:T(8,128)(2,1)}, bf16[192,512]{1,0:T(8,128)(2,1)S(1)}, u32[]{:S(2)}, u32[]{:S(2)}) collective-permute-start(bf16[192,512]{1,0:T(8,128)(2,1)} %s_own.3), channel_id=1, source_target_pairs={{0,1},{1,0},{2,3},{3,2},{4,5},{5,4},{6,7},{7,6},{8,9},{9,8},{10,11... | collective-permute-start | bytes 589832 | tf_op jit(solution)/shard_map/ppermute | solution.py:42
  1.4 1.1 %copy-start = (bf16[192,2048]{1,0:T(8,128)(2,1)S(1)}, bf16[192,2048]{1,0:T(8,128)(2,1)}, u32[]{:S(2)}) copy-start(bf16[192,2048]{1,0:T(8,128)(2,1)} %t_own.3) | copy-start | bytes 2359300
  2.6 0.9 %copy-start.1 = (bf16[192,512]{1,0:T(8,128)(2,1)S(1)}, bf16[192,512]{1,0:T(8,128)(2,1)}, u32[]{:S(2)}) copy-start(bf16[192,512]{1,0:T(8,128)(2,1)} %s_own.3) | copy-start | bytes 589828
  4.9 8.2 %collective-permute-start.2 = (bf16[192,1024]{1,0:T(8,128)(2,1)S(1)}, bf16[192,1024]{1,0:T(8,128)(2,1)S(1)}, u32[]{:S(2)}, u32[]{:S(2)}) collective-permute-start(bf16[192,1024]{1,0:T(8,128)(2,1)S(1)} %get-tuple-element.37), channel_id=1, source_target_pairs={{0,4},{1,3},{16,20},{17,19},{32,36},{33,35},{48,52},{49,51},{4,8},... | collective-permute-start | bytes 1179656 | tf_op jit(solution)/shard_map/ppermute | solution.py:38
  6.2 12.2 %collective-permute-start.3 = (bf16[192,1024]{1,0:T(8,128)(2,1)S(1)}, bf16[192,1024]{1,0:T(8,128)(2,1)S(1)}, u32[]{:S(2)}, u32[]{:S(2)}) collective-permute-start(bf16[192,1024]{1,0:T(8,128)(2,1)S(1)} %get-tuple-element.38), channel_id=1, source_target_pairs={{0,8},{1,65},{16,24},{17,81},{32,40},{33,97},{48,56},{49,113},{4,1... | collective-permute-start | bytes 1179656 | tf_op jit(solution)/shard_map/ppermute | solution.py:38
  8.7 11.1 %collective-permute-start.4 = (bf16[192,1024]{1,0:T(8,128)(2,1)S(1)}, bf16[192,1024]{1,0:T(8,128)(2,1)S(1)}, u32[]{:S(2)}, u32[]{:S(2)}) collective-permute-start(bf16[192,1024]{1,0:T(8,128)(2,1)S(1)} %get-tuple-element.39), channel_id=1, source_target_pairs={{0,12},{1,67},{16,28},{17,83},{32,44},{33,99},{48,60},{49,115},{4,... | collective-permute-start | bytes 1179656 | tf_op jit(solution)/shard_map/ppermute | solution.py:38
  10.7 14.0 %collective-permute-start.5 = (bf16[192,640]{1,0:T(8,128)(2,1)S(1)}, bf16[192,640]{1,0:T(8,128)(2,1)S(1)}, u32[]{:S(2)}, u32[]{:S(2)}) collective-permute-start(bf16[192,640]{1,0:T(8,128)(2,1)S(1)} %get-tuple-element.40), channel_id=1, source_target_pairs={{0,4},{1,3},{16,20},{17,19},{32,36},{33,35},{48,52},{49,51},{4,8},... | collective-permute-start | bytes 737288 | tf_op jit(solution)/shard_map/ppermute | solution.py:38
  11.0 14.4 %collective-permute-start.6 = (bf16[192,640]{1,0:T(8,128)(2,1)S(1)}, bf16[192,640]{1,0:T(8,128)(2,1)S(1)}, u32[]{:S(2)}, u32[]{:S(2)}) collective-permute-start(bf16[192,640]{1,0:T(8,128)(2,1)S(1)} %get-tuple-element.41), channel_id=1, source_target_pairs={{0,8},{1,65},{16,24},{17,81},{32,40},{33,97},{48,56},{49,113},{4,1... | collective-permute-start | bytes 737288 | tf_op jit(solution)/shard_map/ppermute | solution.py:38
  13.1 12.3 %collective-permute-start.7 = (bf16[192,640]{1,0:T(8,128)(2,1)S(1)}, bf16[192,640]{1,0:T(8,128)(2,1)S(1)}, u32[]{:S(2)}, u32[]{:S(2)}) collective-permute-start(bf16[192,640]{1,0:T(8,128)(2,1)S(1)} %get-tuple-element.42), channel_id=1, source_target_pairs={{0,12},{1,67},{16,28},{17,83},{32,44},{33,99},{48,60},{49,115},{4,... | collective-permute-start | bytes 737288 | tf_op jit(solution)/shard_map/ppermute | solution.py:38
  20.9 9.0 %collective-permute-start.19 = (bf16[128,640]{1,0:T(8,128)(2,1)S(1)}, bf16[128,640]{1,0:T(8,128)(2,1)S(1)}, u32[]{:S(2)}, u32[]{:S(2)}) collective-permute-start(bf16[128,640]{1,0:T(8,128)(2,1)S(1)} %get-tuple-element.50), channel_id=1, source_target_pairs={{0,66},{1,49},{16,82},{17,1},{32,98},{33,17},{48,114},{49,33},{4,7... | collective-permute-start | bytes 491528 | tf_op jit(solution)/shard_map/ppermute | solution.py:38
  24.7 6.0 %collective-permute-start.18 = (bf16[128,640]{1,0:T(8,128)(2,1)S(1)}, bf16[128,640]{1,0:T(8,128)(2,1)S(1)}, u32[]{:S(2)}, u32[]{:S(2)}) collective-permute-start(bf16[128,640]{1,0:T(8,128)(2,1)S(1)} %get-tuple-element.49), channel_id=1, source_target_pairs={{0,64},{1,33},{16,80},{17,49},{32,96},{33,1},{48,112},{49,17},{4,6... | collective-permute-start | bytes 491528 | tf_op jit(solution)/shard_map/ppermute | solution.py:38
  24.7 7.4 %collective-permute-start.17 = (bf16[128,640]{1,0:T(8,128)(2,1)S(1)}, bf16[128,640]{1,0:T(8,128)(2,1)S(1)}, u32[]{:S(2)}, u32[]{:S(2)}) collective-permute-start(bf16[128,640]{1,0:T(8,128)(2,1)S(1)} %get-tuple-element.48), channel_id=1, source_target_pairs={{0,2},{1,17},{16,18},{17,33},{32,34},{33,49},{48,50},{49,1},{4,6},... | collective-permute-start | bytes 491528 | tf_op jit(solution)/shard_map/ppermute | solution.py:38
  27.0 8.2 %collective-permute-start.10 = (bf16[128,640]{1,0:T(8,128)(2,1)S(1)}, bf16[128,640]{1,0:T(8,128)(2,1)S(1)}, u32[]{:S(2)}, u32[]{:S(2)}) collective-permute-start(bf16[128,640]{1,0:T(8,128)(2,1)S(1)} %get-tuple-element.46), channel_id=1, source_target_pairs={{0,48},{1,13},{16,0},{17,29},{32,16},{33,45},{48,32},{49,61},{4,52... | collective-permute-start | bytes 491528 | tf_op jit(solution)/shard_map/ppermute | solution.py:38
  29.6 6.1 %collective-permute-start.9 = (bf16[128,640]{1,0:T(8,128)(2,1)S(1)}, bf16[128,640]{1,0:T(8,128)(2,1)S(1)}, u32[]{:S(2)}, u32[]{:S(2)}) collective-permute-start(bf16[128,640]{1,0:T(8,128)(2,1)S(1)} %get-tuple-element.45), channel_id=1, source_target_pairs={{0,32},{1,9},{16,48},{17,25},{32,0},{33,41},{48,16},{49,57},{4,36}... | collective-permute-start | bytes 491528 | tf_op jit(solution)/shard_map/ppermute | solution.py:38
  29.9 7.4 %collective-permute-start.8 = (bf16[128,640]{1,0:T(8,128)(2,1)S(1)}, bf16[128,640]{1,0:T(8,128)(2,1)S(1)}, u32[]{:S(2)}, u32[]{:S(2)}) collective-permute-start(bf16[128,640]{1,0:T(8,128)(2,1)S(1)} %get-tuple-element.44), channel_id=1, source_target_pairs={{0,16},{1,5},{16,32},{17,21},{32,48},{33,37},{48,0},{49,53},{4,20}... | collective-permute-start | bytes 491528 | tf_op jit(solution)/shard_map/ppermute | solution.py:38
  32.2 8.7 %collective-permute-start.22 = (bf16[128,640]{1,0:T(8,128)(2,1)S(1)}, bf16[128,640]{1,0:T(8,128)(2,1)S(1)}, u32[]{:S(2)}, u32[]{:S(2)}) collective-permute-start(bf16[128,640]{1,0:T(8,128)(2,1)S(1)} %fusion.9), channel_id=1, source_target_pairs={{0,48},{1,13},{16,0},{17,29},{32,16},{33,45},{48,32},{49,61},{4,52... | collective-permute-start | bytes 491528 | tf_op jit(solution)/shard_map/ppermute | solution.py:38
  34.7 6.2 %collective-permute-start.21 = (bf16[128,640]{1,0:T(8,128)(2,1)S(1)}, bf16[128,640]{1,0:T(8,128)(2,1)S(1)}, u32[]{:S(2)}, u32[]{:S(2)}) collective-permute-start(bf16[128,640]{1,0:T(8,128)(2,1)S(1)} %fusion.9), channel_id=1, source_target_pairs={{0,32},{1,9},{16,48},{17,25},{32,0},{33,41},{48,16},{49,57},{4,36}... | collective-permute-start | bytes 491528 | tf_op jit(solution)/shard_map/ppermute | solution.py:38
  35.1 6.9 %collective-permute-start.20 = (bf16[128,640]{1,0:T(8,128)(2,1)S(1)}, bf16[128,640]{1,0:T(8,128)(2,1)S(1)}, u32[]{:S(2)}, u32[]{:S(2)}) collective-permute-start(bf16[128,640]{1,0:T(8,128)(2,1)S(1)} %fusion.9), channel_id=1, source_target_pairs={{0,16},{1,5},{16,32},{17,21},{32,48},{33,37},{48,0},{49,53},{4,20}... | collective-permute-start | bytes 491528 | tf_op jit(solution)/shard_map/ppermute | solution.py:38
  37.4 8.5 %collective-permute-start.13 = (bf16[128,640]{1,0:T(8,128)(2,1)S(1)}, bf16[128,640]{1,0:T(8,128)(2,1)S(1)}, u32[]{:S(2)}, u32[]{:S(2)}) collective-permute-start(bf16[128,640]{1,0:T(8,128)(2,1)S(1)} %fusion.8), channel_id=1, source_target_pairs={{0,66},{1,49},{16,82},{17,1},{32,98},{33,17},{48,114},{49,33},{4,7... | collective-permute-start | bytes 491528 | tf_op jit(solution)/shard_map/ppermute | solution.py:38
  39.4 9.9 %collective-permute-start.12 = (bf16[128,640]{1,0:T(8,128)(2,1)S(1)}, bf16[128,640]{1,0:T(8,128)(2,1)S(1)}, u32[]{:S(2)}, u32[]{:S(2)}) collective-permute-start(bf16[128,640]{1,0:T(8,128)(2,1)S(1)} %fusion.8), channel_id=1, source_target_pairs={{0,64},{1,33},{16,80},{17,49},{32,96},{33,1},{48,112},{49,17},{4,6... | collective-permute-start | bytes 491528 | tf_op jit(solution)/shard_map/ppermute | solution.py:38
  40.9 9.0 %collective-permute-start.11 = (bf16[128,640]{1,0:T(8,128)(2,1)S(1)}, bf16[128,640]{1,0:T(8,128)(2,1)S(1)}, u32[]{:S(2)}, u32[]{:S(2)}) collective-permute-start(bf16[128,640]{1,0:T(8,128)(2,1)S(1)} %fusion.8), channel_id=1, source_target_pairs={{0,2},{1,17},{16,18},{17,33},{32,34},{33,49},{48,50},{49,1},{4,6},... | collective-permute-start | bytes 491528 | tf_op jit(solution)/shard_map/ppermute | solution.py:38
  42.3 10.8 %collective-permute-start.23 = (bf16[128,640]{1,0:T(8,128)(2,1)S(1)}, bf16[128,640]{1,0:T(8,128)(2,1)S(1)}, u32[]{:S(2)}, u32[]{:S(2)}) collective-permute-start(bf16[128,640]{1,0:T(8,128)(2,1)S(1)} %add_convert_fusion.refs_4_), channel_id=1, source_target_pairs={{0,2},{1,17},{16,18},{17,33},{32,34},{33,49},{48,50},{49,1},{4,6},... | collective-permute-start | bytes 491528 | tf_op jit(solution)/shard_map/ppermute | solution.py:38
  42.8 11.3 %collective-permute-start.24 = (bf16[128,640]{1,0:T(8,128)(2,1)S(1)}, bf16[128,640]{1,0:T(8,128)(2,1)S(1)}, u32[]{:S(2)}, u32[]{:S(2)}) collective-permute-start(bf16[128,640]{1,0:T(8,128)(2,1)S(1)} %add_convert_fusion.refs_4_), channel_id=1, source_target_pairs={{0,64},{1,33},{16,80},{17,49},{32,96},{33,1},{48,112},{49,17},{4,6... | collective-permute-start | bytes 491528 | tf_op jit(solution)/shard_map/ppermute | solution.py:38
  45.9 8.3 %collective-permute-start.25 = (bf16[128,640]{1,0:T(8,128)(2,1)S(1)}, bf16[128,640]{1,0:T(8,128)(2,1)S(1)}, u32[]{:S(2)}, u32[]{:S(2)}) collective-permute-start(bf16[128,640]{1,0:T(8,128)(2,1)S(1)} %add_convert_fusion.refs_4_), channel_id=1, source_target_pairs={{0,66},{1,49},{16,82},{17,1},{32,98},{33,17},{48,114},{49,33},{4,7... | collective-permute-start | bytes 491528 | tf_op jit(solution)/shard_map/ppermute | solution.py:38
  50.0 5.7 %collective-permute-start.14 = (bf16[128,640]{1,0:T(8,128)(2,1)S(1)}, bf16[128,640]{1,0:T(8,128)(2,1)S(1)}, u32[]{:S(2)}, u32[]{:S(2)}) collective-permute-start(bf16[128,640]{1,0:T(8,128)(2,1)S(1)} %add_convert_fusion.1.refs_0_.piece0), channel_id=1, source_target_pairs={{0,16},{1,5},{16,32},{17,21},{32,48},{33,37},{48,0},{49,53},{4,20}... | collective-permute-start | bytes 491528 | tf_op jit(solution)/shard_map/ppermute | solution.py:38
  51.2 6.4 %collective-permute-start.15 = (bf16[128,640]{1,0:T(8,128)(2,1)S(1)}, bf16[128,640]{1,0:T(8,128)(2,1)S(1)}, u32[]{:S(2)}, u32[]{:S(2)}) collective-permute-start(bf16[128,640]{1,0:T(8,128)(2,1)S(1)} %add_convert_fusion.1.refs_0_.piece0), channel_id=1, source_target_pairs={{0,32},{1,9},{16,48},{17,25},{32,0},{33,41},{48,16},{49,57},{4,36}... | collective-permute-start | bytes 491528 | tf_op jit(solution)/shard_map/ppermute | solution.py:38
  53.1 5.7 %collective-permute-start.16 = (bf16[128,640]{1,0:T(8,128)(2,1)S(1)}, bf16[128,640]{1,0:T(8,128)(2,1)S(1)}, u32[]{:S(2)}, u32[]{:S(2)}) collective-permute-start(bf16[128,640]{1,0:T(8,128)(2,1)S(1)} %add_convert_fusion.1.refs_0_.piece0), channel_id=1, source_target_pairs={{0,48},{1,13},{16,0},{17,29},{32,16},{33,45},{48,32},{49,61},{4,52... | collective-permute-start | bytes 491528 | tf_op jit(solution)/shard_map/ppermute | solution.py:38
  59.7 5.8 %collective-permute-start.28 = (bf16[192,512]{1,0:T(8,128)(2,1)S(1)}, bf16[192,512]{1,0:T(8,128)(2,1)S(1)}, u32[]{:S(2)}, u32[]{:S(2)}) collective-permute-start(bf16[192,512]{1,0:T(8,128)(2,1)S(1)} %get-tuple-element.56), channel_id=1, source_target_pairs={{0,4},{1,3},{16,20},{17,19},{32,36},{33,35},{48,52},{49,51},{4,8},... | collective-permute-start | bytes 589832 | tf_op jit(solution)/shard_map/ppermute | solution.py:38
  60.5 7.5 %collective-permute-start.27 = (bf16[192,512]{1,0:T(8,128)(2,1)S(1)}, bf16[192,512]{1,0:T(8,128)(2,1)S(1)}, u32[]{:S(2)}, u32[]{:S(2)}) collective-permute-start(bf16[192,512]{1,0:T(8,128)(2,1)S(1)} %get-tuple-element.55), channel_id=1, source_target_pairs={{0,8},{1,65},{16,24},{17,81},{32,40},{33,97},{48,56},{49,113},{4,1... | collective-permute-start | bytes 589832 | tf_op jit(solution)/shard_map/ppermute | solution.py:38
  62.9 5.4 %collective-permute-start.26 = (bf16[192,512]{1,0:T(8,128)(2,1)S(1)}, bf16[192,512]{1,0:T(8,128)(2,1)S(1)}, u32[]{:S(2)}, u32[]{:S(2)}) collective-permute-start(bf16[192,512]{1,0:T(8,128)(2,1)S(1)} %get-tuple-element.54), channel_id=1, source_target_pairs={{0,12},{1,67},{16,28},{17,83},{32,44},{33,99},{48,60},{49,115},{4,... | collective-permute-start | bytes 589832 | tf_op jit(solution)/shard_map/ppermute | solution.py:38
  68.5 7.9 %collective-permute-start.29 = (f32[192]{0:T(256)S(1)}, f32[192]{0:T(256)S(1)}, u32[]{:S(2)}, u32[]{:S(2)}) collective-permute-start(f32[192]{0:T(256)S(1)} %fusion.5), channel_id=1, source_target_pairs={{0,1},{1,0},{2,3},{3,2},{4,5},{5,4},{6,7},{7,6},{8,9},{9,8},{10,11... | collective-permute-start | bytes 2312 | tf_op jit(solution)/shard_map/ppermute | solution.py:42

commit v10 on v9

--- a/solution.py
+++ b/solution.py
@@ -99,13 +99,17 @@
     return pack[:, part(places, 0, ss)], pack[:, pl.ds(half, pack.shape[1] - half)]
 
 
-def stack(places, norms, packs, left, right, native):
+def stack(places, chunk, norms, packs, left, right):
+    native = chunk == 0
     rows = norms[0].shape[0]
     half, feats = left.shape[1], right.shape[1]
     ss = half // SIZE
     for k, (norm, pack) in enumerate(zip(norms, packs)):
         at = pl.ds(k * rows, rows)
-        left[at, :] = norm[:, pl.ds(0, half)]
+        for by in range(SIZE):
+            which = lax.rem(places[1 + chunk] + by, SIZE)
+            block = pl.ds(pl.multiple_of(which * ss, ss), ss)
+            left[at, pl.ds(by * ss, ss)] = norm[:, block]
         if native:
             right[at, pl.ds(0, ss)], right[at, pl.ds(ss, feats - ss)] = native_features(
                 places, pack, half
@@ -120,39 +124,38 @@
     )
 
 
-def emit(place, product, outs):
+def emit(product, outs):
     half, feats = product.shape
     ss = half // SIZE
-    rest = pl.ds(ss, feats - ss)
     for by, out in enumerate(outs):
-        block = pl.ds(pl.multiple_of(lax.rem(place + by, SIZE) * ss, ss), ss)
-        out[:, pl.ds(0, ss)] = product[block, pl.ds(0, ss)].astype(out.dtype)
-        out[:, rest] = -product[block, rest].astype(out.dtype)
-
-
-def gram_early_kernel(places, *refs):
+        rows = product[by * ss : (by + 1) * ss]
+        out[:, pl.ds(0, ss)] = rows[:, :ss].astype(out.dtype)
+        out[:, pl.ds(ss, feats - ss)] = -rows[:, ss:].astype(out.dtype)
+
+
+def gram_early_kernel(share, places, *refs):
     packs, (product, left, right) = refs[:-3], refs[-3:]
-    stack(places, packs, packs, left, right, True)
+    stack(places, 0, packs, packs, left, right)
     product[...] = cross(left, right)
-
-
-def gram_native_kernel(share, places, pack, before, *refs):
-    outs, (left, right, product) = refs[:SIZE], refs[SIZE:]
-    ss = left.shape[1] // SIZE
-    stack(places, [pack], [pack], left, right, True)
-    product[...] = before[...] + cross(left, right)
+    ss = product.shape[0] // SIZE
     row = lax.broadcasted_iota(jnp.int32, (ss, ss), 0)
     col = lax.broadcasted_iota(jnp.int32, (ss, ss), 1)
-    product[part(places, 0, ss), pl.ds(0, ss)] -= jnp.where(row == col, share, 0.0)
-    emit(places[1], product, outs)
+    by = lax.rem(places[0] + SIZE - places[1], SIZE)
+    block = pl.ds(pl.multiple_of(by * ss, ss), ss)
+    product[block, pl.ds(0, ss)] -= jnp.where(row == col, share, 0.0)
+
+
+def gram_native_kernel(places, pack, before, *refs):
+    outs, (left, right) = refs[:SIZE], refs[SIZE:]
+    stack(places, 0, [pack], [pack], left, right)
+    emit(before[...] + cross(left, right), outs)
 
 
 def gram_far_kernel(places, *refs):
     norms, packs, outs = refs[:SIZE], refs[SIZE : 2 * SIZE], refs[2 * SIZE : 3 * SIZE]
-    left, right, product = refs[3 * SIZE :]
-    stack(places, norms, packs, left, right, False)
-    product[...] = cross(left, right)
-    emit(places[2], product, outs)
+    left, right = refs[3 * SIZE :]
+    stack(places, 1, norms, packs, left, right)
+    emit(cross(left, right), outs)
 
 
 def gather_weights(place, pieces, weights):
@@ -192,16 +195,14 @@
         out[...] = (product[k * rows : (k + 1) * rows] + sofar).astype(out.dtype)
 
 
-def apply_sent_kernel(places, far1, far2, far3, piece, before, early1, early2, early3, *outs):
-    rows, ss = far1.shape[0], piece.shape[0]
+def apply_sent_kernel(places, left, piece, before, early1, early2, early3, *outs):
+    rows, ss = outs[0].shape[0], piece.shape[0]
     which = lax.rem(places[2] + 1, SIZE)
     block = pl.ds(pl.multiple_of(which * ss, ss), ss)
-    for k, (pack, early, out) in enumerate(
-        zip((far1, far2, far3), (early1, early2, early3), outs)
-    ):
-        out[...] = early[...]
+    product = times(left[...], piece[...])
+    for k, out in enumerate(outs):
         sofar = before[pl.ds((k + 1) * rows, rows), block]
-        out[:, block] = (times(pack[...], piece[...]) + sofar).astype(out.dtype)
+        out[:, block] = (product[k * rows : (k + 1) * rows] + sofar).astype(out.dtype)
 
 
 def apply_kept_kernel(places, pack, *refs):
@@ -214,13 +215,14 @@
     return [jax.ShapeDtypeStruct(shape, dtype) for shape, dtype in described]
 
 
-def kernel_call(kernel, name, outs, n_in, scratch=(), flops=0):
+def kernel_call(kernel, name, outs, n_in, scratch=(), flops=0, aliases=None):
     return pl.pallas_call(
         kernel,
         out_shape=outs,
         in_specs=[SCALAR] + [WHOLE] * n_in,
         out_specs=[WHOLE] * len(outs),
         scratch_shapes=list(scratch),
+        input_output_aliases=aliases or {},
         compiler_params=PARAMS,
         cost_estimate=pl.CostEstimate(flops=flops, bytes_accessed=4 << 20, transcendentals=0),
         name=name,
@@ -274,24 +276,23 @@
     far = exchanged(far[0], far.__getitem__, GATHER)
 
     blocks = shapes(((ss, feats), F32), *[((ss, feats), BF16)] * 3)
-    product = pltpu.VMEM((half, feats), F32)
 
     def operands(count):
         return [pltpu.VMEM((count * rows, half), BF16), pltpu.VMEM((count * rows, feats), BF16)]
 
     early = kernel_call(
-        gram_early_kernel, "gram_early", shapes(((half, feats), F32)), 3, operands(3), flops
+        functools.partial(gram_early_kernel, level * SIZE / groups),
+        "gram_early",
+        shapes(((half, feats), F32)),
+        3,
+        operands(3),
+        flops,
     )(places, *near[:3])[0]
     near_blocks = kernel_call(
-        functools.partial(gram_native_kernel, level * SIZE / groups),
-        "gram_native",
-        blocks,
-        2,
-        operands(1) + [product],
-        flops // 4,
+        gram_native_kernel, "gram_native", blocks, 2, operands(1), flops // 4
     )(places, near[3], early)
     far_blocks = kernel_call(
-        gram_far_kernel, "gram_far", blocks, 2 * SIZE, operands(SIZE) + [product], flops
+        gram_far_kernel, "gram_far", blocks, 2 * SIZE, operands(SIZE), flops
     )(places, *near, *far)
 
     def weights_of(chunk, own, *sends):
@@ -313,17 +314,23 @@
     )(places, *near, *near_weights)[0]
     messages = shapes(*[((rows, half), BF16)] * 3)
     weights = pltpu.VMEM((half, feats), BF16)
-    most = kernel_call(
+    *most, stacked = kernel_call(
         apply_early_kernel,
         "apply_early",
-        messages,
+        messages + shapes(((3 * rows, feats), BF16)),
         7,
-        [pltpu.VMEM((3 * rows, feats), BF16), weights],
+        [weights],
         flops * 3 // 4,
     )(places, *far[1:], *far_weights[:3], sofar)
-    parts = kernel_call(apply_sent_kernel, "apply_sent", messages, 8, (), flops // 4)(
-        places, *far[1:], far_weights[3], sofar, *most
-    )
+    parts = kernel_call(
+        apply_sent_kernel,
+        "apply_sent",
+        messages,
+        6,
+        (),
+        flops // 4,
+        {4 + k: k for k in range(3)},
+    )(places, stacked, far_weights[3], sofar, *most)
     grad_n = kernel_call(
         apply_kept_kernel, "apply_kept", shapes(((rows, half), F32)), SIZE + 2, [weights], flops // 4
     )(places, far[0], *far_weights, sofar)[0]

time: 77.5 us -> 77.6 us (level)
  no operation moved by 1% of the time
where the time goes in v10:
time: 77.6 us; the launch traced here: 77.5 us
  starting transfers between devices  44.5 us (57%)
  waiting for transfers between devices  18.3 us (24%)
  Pallas kernels  10.6 us (14%)
  local copies, waits for them, and re-layouts  2.06 us (3%)
  other arithmetic  1.83 us (2%)
    ppermute x27, starting transfers between devices, shifted(): return lax.ppermute(array, AXES, pairs)  35.9 us
    ppermute x27, waiting for transfers between devices, shifted(): return lax.ppermute(array, AXES, pairs)  17.6 us
    ppermute x3, starting transfers between devices, other_core(): return lax.ppermute(array, 'sec', [(0, 1), (1, 0)])  8.6 us
    unnamed x4, local copies, waits for them, and re-layouts  2.06 us
  transfers between devices with their start and end apart: 30, of which 14 were waited for; matrix products, arithmetic and copies ran while one was open for 1% of the time, Pallas kernels for 11%

profile of v10, /device:TPU:1, one launch (start us, length us, event | category | flops | bytes accessed | tf_op | source)
XLA Modules:
  0.0 77.5 jit_solution(12304473216563242853)
XLA Ops:
  0.0 1.4 %collective-permute-start.1 = (bf16[192,2048]{1,0:T(8,128)(2,1)}, bf16[192,2048]{1,0:T(8,128)(2,1)S(1)}, u32[]{:S(2)}, u32[]{:S(2)}) collective-permute-start(bf16[192,2048]{1,0:T(8,128)(2,1)} %t_own.3), channel_id=1, source_target_pairs={{0,1},{1,0},{2,3},{3,2},{4,5},{5,4},{6,7},{7,6},{8,9},{9,8},{10,11... | collective-permute-start | bytes 2359304 | tf_op jit(solution)/shard_map/ppermute | solution.py:42
  1.4 1.1 %copy-done = bf16[192,2048]{1,0:T(8,128)(2,1)S(1)} copy-done((bf16[192,2048]{1,0:T(8,128)(2,1)S(1)}, bf16[192,2048]{1,0:T(8,128)(2,1)}, u32[]{:S(2)}) %copy-start) | copy-done | bytes 786456
  2.6 0.9 %copy-done.1 = bf16[192,512]{1,0:T(8,128)(2,1)S(1)} copy-done((bf16[192,512]{1,0:T(8,128)(2,1)S(1)}, bf16[192,512]{1,0:T(8,128)(2,1)}, u32[]{:S(2)}) %copy-start.1) | copy-done | bytes 196632
  3.8 1.0 %pack_own.1 = (bf16[192,1024]{1,0:T(8,128)(2,1)S(1)}, bf16[192,1024]{1,0:T(8,128)(2,1)S(1)}, bf16[192,1024]{1,0:T(8,128)(2,1)S(1)}, bf16[192,1024]{1,0:T(8,128)(...) custom-call(s32[3]{0:T(128)S(1)} %pad_add_fusion.places, bf16[192,512]{1,0:T(8,128)(2,1)S(1)} %copy-done.1, ...), custom_call_target="tpu_custom_call" | custom-call | bytes 4194304 | tf_op jit(solution)/shard_map/pack_own/pallas_call | solution.py:255
  4.9 1.4 %collective-permute-start.2 = (bf16[192,1024]{1,0:T(8,128)(2,1)S(1)}, bf16[192,1024]{1,0:T(8,128)(2,1)S(1)}, u32[]{:S(2)}, u32[]{:S(2)}) collective-permute-start(bf16[192,1024]{1,0:T(8,128)(2,1)S(1)} %get-tuple-element.38), channel_id=1, source_target_pairs={{0,4},{1,3},{16,20},{17,19},{32,36},{33,35},{48,52},{49,51},{4,8},... | collective-permute-start | bytes 1179656 | tf_op jit(solution)/shard_map/ppermute | solution.py:38
  6.2 2.5 %collective-permute-start.3 = (bf16[192,1024]{1,0:T(8,128)(2,1)S(1)}, bf16[192,1024]{1,0:T(8,128)(2,1)S(1)}, u32[]{:S(2)}, u32[]{:S(2)}) collective-permute-start(bf16[192,1024]{1,0:T(8,128)(2,1)S(1)} %get-tuple-element.39), channel_id=1, source_target_pairs={{0,8},{1,65},{16,24},{17,81},{32,40},{33,97},{48,56},{49,113},{4,1... | collective-permute-start | bytes 1179656 | tf_op jit(solution)/shard_map/ppermute | solution.py:38
  8.7 1.2 %collective-permute-start.4 = (bf16[192,1024]{1,0:T(8,128)(2,1)S(1)}, bf16[192,1024]{1,0:T(8,128)(2,1)S(1)}, u32[]{:S(2)}, u32[]{:S(2)}) collective-permute-start(bf16[192,1024]{1,0:T(8,128)(2,1)S(1)} %get-tuple-element.40), channel_id=1, source_target_pairs={{0,12},{1,67},{16,28},{17,83},{32,44},{33,99},{48,60},{49,115},{4,... | collective-permute-start | bytes 1179656 | tf_op jit(solution)/shard_map/ppermute | solution.py:38
  9.8 0.8 %pack_far.1 = (bf16[192,640]{1,0:T(8,128)(2,1)S(1)}, bf16[192,640]{1,0:T(8,128)(2,1)S(1)}, bf16[192,640]{1,0:T(8,128)(2,1)S(1)}, bf16[192,640]{1,0:T(8,128)(2,1)S(1)}) custom-call(s32[3]{0:T(128)S(1)} %pad_add_fusion.places, bf16[192,512]{1,0:T(8,128)(2,1)S(1)} %collective-permute-done.s_far, bf16[192,2048]{1,0:T(8,128)(2,1)S(1)} %collective-permute-done.1.t_far, ...), custom_call_target="tpu_custom_call" | custom-call | bytes 4194304 | tf_op jit(solution)/shard_map/pack_far/pallas_call | solution.py:261
  10.7 0.4 collective-permute-start.5
  11.0 0.9 %collective-permute-start.6 = (bf16[192,640]{1,0:T(8,128)(2,1)S(1)}, bf16[192,640]{1,0:T(8,128)(2,1)S(1)}, u32[]{:S(2)}, u32[]{:S(2)}) collective-permute-start(bf16[192,640]{1,0:T(8,128)(2,1)S(1)} %get-tuple-element.42), channel_id=1, source_target_pairs={{0,8},{1,65},{16,24},{17,81},{32,40},{33,97},{48,56},{49,113},{4,1... | collective-permute-start | bytes 737288 | tf_op jit(solution)/shard_map/ppermute | solution.py:38
  11.9 1.2 %collective-permute-done.2.refs_1_ = bf16[192,1024]{1,0:T(8,128)(2,1)S(1)} collective-permute-done((bf16[192,1024]{1,0:T(8,128)(2,1)S(1)}, bf16[192,1024]{1,0:T(8,128)(2,1)S(1)}, u32[]{:S(2)}, u32[]{:S(2)}) %collective-permute-start.2) | collective-permute-done | bytes 393248 | tf_op jit(solution)/shard_map/ppermute | solution.py:38
  13.1 1.4 %collective-permute-start.7 = (bf16[192,640]{1,0:T(8,128)(2,1)S(1)}, bf16[192,640]{1,0:T(8,128)(2,1)S(1)}, u32[]{:S(2)}, u32[]{:S(2)}) collective-permute-start(bf16[192,640]{1,0:T(8,128)(2,1)S(1)} %get-tuple-element.43), channel_id=1, source_target_pairs={{0,12},{1,67},{16,28},{17,83},{32,44},{33,99},{48,60},{49,115},{4,... | collective-permute-start | bytes 737288 | tf_op jit(solution)/shard_map/ppermute | solution.py:38
  14.4 4.0 %collective-permute-done.3.refs_2_ = bf16[192,1024]{1,0:T(8,128)(2,1)S(1)} collective-permute-done((bf16[192,1024]{1,0:T(8,128)(2,1)S(1)}, bf16[192,1024]{1,0:T(8,128)(2,1)S(1)}, u32[]{:S(2)}, u32[]{:S(2)}) %collective-permute-start.3) | collective-permute-done | bytes 393248 | tf_op jit(solution)/shard_map/ppermute | solution.py:38
  18.4 1.5 %gram_early.1.before = f32[512,640]{1,0:T(8,128)S(1)} custom-call(s32[3]{0:T(128)S(1)} %pad_add_fusion.places, bf16[192,1024]{1,0:T(8,128)(2,1)S(1)} %get-tuple-element.37.refs_0_, bf16[192,1024]{1,0:T(8,128)(2,1)S(1)} %collective-permute-done.2.refs_1_, bf16[192,1024]{1,0:T(8,128)(2,1)S(1)} %collective-permute-done.3.refs_2_), custom_call_target="tpu_custom_call" | custom-call | flops 503316480 | bytes 4194304 | tf_op jit(solution)/shard_map/gram_early/pallas_call | solution.py:283
  19.9 1.0 %gram_native.1 = (f32[128,640]{1,0:T(8,128)S(1)}, bf16[128,640]{1,0:T(8,128)(2,1)S(1)}, bf16[128,640]{1,0:T(8,128)(2,1)S(1)}, bf16[128,640]{1,0:T(8,128)(2,1)S(1)}) custom-call(s32[3]{0:T(128)S(1)} %pad_add_fusion.places, bf16[192,1024]{1,0:T(8,128)(2,1)S(1)} %collective-permute-done.4.refs_3_.pack, f32[512,640]{1,0:T(8,128)S(1)} %gram_early.1.before), custom_call_target="tpu_custom_call" | custom-call | flops 125829120 | bytes 4194304 | tf_op jit(solution)/shard_map/gram_native/pallas_call | solution.py:291
  20.9 3.8 %collective-permute-start.19 = (bf16[128,640]{1,0:T(8,128)(2,1)S(1)}, bf16[128,640]{1,0:T(8,128)(2,1)S(1)}, u32[]{:S(2)}, u32[]{:S(2)}) collective-permute-start(bf16[128,640]{1,0:T(8,128)(2,1)S(1)} %get-tuple-element.51), channel_id=1, source_target_pairs={{0,66},{1,49},{16,82},{17,1},{32,98},{33,17},{48,114},{49,33},{4,7... | collective-permute-start | bytes 491528 | tf_op jit(solution)/shard_map/ppermute | solution.py:38
  24.8 0.7 collective-permute-start.17
  25.5 1.5 %gram_far.1 = (f32[128,640]{1,0:T(8,128)S(1)}, bf16[128,640]{1,0:T(8,128)(2,1)S(1)}, bf16[128,640]{1,0:T(8,128)(2,1)S(1)}, bf16[128,640]{1,0:T(8,128)(2,1)S(1)}) custom-call(s32[3]{0:T(128)S(1)} %pad_add_fusion.places, bf16[192,1024]{1,0:T(8,128)(2,1)S(1)} %get-tuple-element.37.refs_0_, bf16[192,1024]{1,0:T(8,128)(2,1)S(1)} %collective-permute-done.2.refs_1_, ...), custom_call_target="tpu_custom_call" | custom-call | flops 503316480 | bytes 4194304 | tf_op jit(solution)/shard_map/gram_far/pallas_call | solution.py:294
  27.0 2.6 %collective-permute-start.10 = (bf16[128,640]{1,0:T(8,128)(2,1)S(1)}, bf16[128,640]{1,0:T(8,128)(2,1)S(1)}, u32[]{:S(2)}, u32[]{:S(2)}) collective-permute-start(bf16[128,640]{1,0:T(8,128)(2,1)S(1)} %get-tuple-element.47), channel_id=1, source_target_pairs={{0,48},{1,13},{16,0},{17,29},{32,16},{33,45},{48,32},{49,61},{4,52... | collective-permute-start | bytes 491528 | tf_op jit(solution)/shard_map/ppermute | solution.py:38
  29.9 0.7 collective-permute-start.8
  30.8 1.4 %collective-permute-done.17 = bf16[128,640]{1,0:T(8,128)(2,1)S(1)} collective-permute-done((bf16[128,640]{1,0:T(8,128)(2,1)S(1)}, bf16[128,640]{1,0:T(8,128)(2,1)S(1)}, u32[]{:S(2)}, u32[]{:S(2)}) %collective-permute-start.17) | collective-permute-done | bytes 163872 | tf_op jit(solution)/shard_map/ppermute | solution.py:38
  32.3 2.4 %collective-permute-start.22 = (bf16[128,640]{1,0:T(8,128)(2,1)S(1)}, bf16[128,640]{1,0:T(8,128)(2,1)S(1)}, u32[]{:S(2)}, u32[]{:S(2)}) collective-permute-start(bf16[128,640]{1,0:T(8,128)(2,1)S(1)} %fusion.9), channel_id=1, source_target_pairs={{0,48},{1,13},{16,0},{17,29},{32,16},{33,45},{48,32},{49,61},{4,52... | collective-permute-start | bytes 491528 | tf_op jit(solution)/shard_map/ppermute | solution.py:38
  34.7 0.5 collective-permute-start.21
  35.2 0.4 collective-permute-start.20
  35.6 1.7 %collective-permute-done.8 = bf16[128,640]{1,0:T(8,128)(2,1)S(1)} collective-permute-done((bf16[128,640]{1,0:T(8,128)(2,1)S(1)}, bf16[128,640]{1,0:T(8,128)(2,1)S(1)}, u32[]{:S(2)}, u32[]{:S(2)}) %collective-permute-start.8) | collective-permute-done | bytes 163872 | tf_op jit(solution)/shard_map/ppermute | solution.py:38
  37.4 2.0 %collective-permute-start.13 = (bf16[128,640]{1,0:T(8,128)(2,1)S(1)}, bf16[128,640]{1,0:T(8,128)(2,1)S(1)}, u32[]{:S(2)}, u32[]{:S(2)}) collective-permute-start(bf16[128,640]{1,0:T(8,128)(2,1)S(1)} %fusion.8), channel_id=1, source_target_pairs={{0,66},{1,49},{16,82},{17,1},{32,98},{33,17},{48,114},{49,33},{4,7... | collective-permute-start | bytes 491528 | tf_op jit(solution)/shard_map/ppermute | solution.py:38
  39.4 1.5 %collective-permute-start.12 = (bf16[128,640]{1,0:T(8,128)(2,1)S(1)}, bf16[128,640]{1,0:T(8,128)(2,1)S(1)}, u32[]{:S(2)}, u32[]{:S(2)}) collective-permute-start(bf16[128,640]{1,0:T(8,128)(2,1)S(1)} %fusion.8), channel_id=1, source_target_pairs={{0,64},{1,33},{16,80},{17,49},{32,96},{33,1},{48,112},{49,17},{4,6... | collective-permute-start | bytes 491528 | tf_op jit(solution)/shard_map/ppermute | solution.py:38
  40.9 1.3 %collective-permute-done.20 = bf16[128,640]{1,0:T(8,128)(2,1)S(1)} collective-permute-done((bf16[128,640]{1,0:T(8,128)(2,1)S(1)}, bf16[128,640]{1,0:T(8,128)(2,1)S(1)}, u32[]{:S(2)}, u32[]{:S(2)}) %collective-permute-start.20) | collective-permute-done | bytes 163872 | tf_op jit(solution)/shard_map/ppermute | solution.py:38
  42.3 0.4 collective-permute-start.23
  42.7 2.3 %collective-permute-start.24 = (bf16[128,640]{1,0:T(8,128)(2,1)S(1)}, bf16[128,640]{1,0:T(8,128)(2,1)S(1)}, u32[]{:S(2)}, u32[]{:S(2)}) collective-permute-start(bf16[128,640]{1,0:T(8,128)(2,1)S(1)} %add_convert_fusion.refs_4_), channel_id=1, source_target_pairs={{0,64},{1,33},{16,80},{17,49},{32,96},{33,1},{48,112},{49,17},{4,6... | collective-permute-start | bytes 491528 | tf_op jit(solution)/shard_map/ppermute | solution.py:38
  45.0 1.0 %collective-permute-done.13 = bf16[128,640]{1,0:T(8,128)(2,1)S(1)} collective-permute-done((bf16[128,640]{1,0:T(8,128)(2,1)S(1)}, bf16[128,640]{1,0:T(8,128)(2,1)S(1)}, u32[]{:S(2)}, u32[]{:S(2)}) %collective-permute-start.13) | collective-permute-done | bytes 163872 | tf_op jit(solution)/shard_map/ppermute | solution.py:38
  45.9 3.4 %collective-permute-start.25 = (bf16[128,640]{1,0:T(8,128)(2,1)S(1)}, bf16[128,640]{1,0:T(8,128)(2,1)S(1)}, u32[]{:S(2)}, u32[]{:S(2)}) collective-permute-start(bf16[128,640]{1,0:T(8,128)(2,1)S(1)} %add_convert_fusion.refs_4_), channel_id=1, source_target_pairs={{0,66},{1,49},{16,82},{17,1},{32,98},{33,17},{48,114},{49,33},{4,7... | collective-permute-start | bytes 491528 | tf_op jit(solution)/shard_map/ppermute | solution.py:38
  49.4 0.5 collective-permute-done.11
  50.0 1.0 %collective-permute-start.14 = (bf16[128,640]{1,0:T(8,128)(2,1)S(1)}, bf16[128,640]{1,0:T(8,128)(2,1)S(1)}, u32[]{:S(2)}, u32[]{:S(2)}) collective-permute-start(bf16[128,640]{1,0:T(8,128)(2,1)S(1)} %add_convert_fusion.1.refs_0_.piece0), channel_id=1, source_target_pairs={{0,16},{1,5},{16,32},{17,21},{32,48},{33,37},{48,0},{49,53},{4,20}... | collective-permute-start | bytes 491528 | tf_op jit(solution)/shard_map/ppermute | solution.py:38
  51.0 2.1 %collective-permute-start.15 = (bf16[128,640]{1,0:T(8,128)(2,1)S(1)}, bf16[128,640]{1,0:T(8,128)(2,1)S(1)}, u32[]{:S(2)}, u32[]{:S(2)}) collective-permute-start(bf16[128,640]{1,0:T(8,128)(2,1)S(1)} %add_convert_fusion.1.refs_0_.piece0), channel_id=1, source_target_pairs={{0,32},{1,9},{16,48},{17,25},{32,0},{33,41},{48,16},{49,57},{4,36}... | collective-permute-start | bytes 491528 | tf_op jit(solution)/shard_map/ppermute | solution.py:38
  53.1 0.9 %collective-permute-start.16 = (bf16[128,640]{1,0:T(8,128)(2,1)S(1)}, bf16[128,640]{1,0:T(8,128)(2,1)S(1)}, u32[]{:S(2)}, u32[]{:S(2)}) collective-permute-start(bf16[128,640]{1,0:T(8,128)(2,1)S(1)} %add_convert_fusion.1.refs_0_.piece0), channel_id=1, source_target_pairs={{0,48},{1,13},{16,0},{17,29},{32,16},{33,45},{48,32},{49,61},{4,52... | collective-permute-start | bytes 491528 | tf_op jit(solution)/shard_map/ppermute | solution.py:38
  54.0 1.4 %apply_native.1.refs_4_.before = f32[768,512]{1,0:T(8,128)S(1)} custom-call(s32[3]{0:T(128)S(1)} %pad_add_fusion.places, bf16[192,1024]{1,0:T(8,128)(2,1)S(1)} %get-tuple-element.37.refs_0_, bf16[192,1024]{1,0:T(8,128)(2,1)S(1)} %collective-permute-done.2.refs_1_, bf16[192,1024]{1,0:T(8,128)(2,1)S(1)} %collective-permute-done.3.refs_2_, ...), custom_call_target="tpu_custom_call" | custom-call | flops 503316480 | bytes 4194304 | tf_op jit(solution)/shard_map/apply_native/pallas_call | solution.py:307
  55.8 1.8 %collective-permute-done.15.refs_2_.piece2 = bf16[128,640]{1,0:T(8,128)(2,1)S(1)} collective-permute-done((bf16[128,640]{1,0:T(8,128)(2,1)S(1)}, bf16[128,640]{1,0:T(8,128)(2,1)S(1)}, u32[]{:S(2)}, u32[]{:S(2)}) %collective-permute-start.15) | collective-permute-done | bytes 163872 | tf_op jit(solution)/shard_map/ppermute | solution.py:38
  57.6 1.3 %apply_early.1 = (bf16[192,512]{1,0:T(8,128)(2,1)S(1)}, bf16[192,512]{1,0:T(8,128)(2,1)S(1)}, bf16[192,512]{1,0:T(8,128)(2,1)S(1)}, bf16[576,640]{1,0:T(8,128)(2,1)S(1)}) custom-call(s32[3]{0:T(128)S(1)} %pad_add_fusion.places, bf16[192,640]{1,0:T(8,128)(2,1)S(1)} %collective-permute-done.5.refs_5_.far1, ...), custom_call_target="tpu_custom_call" | custom-call | flops 377487360 | bytes 4194304 | tf_op jit(solution)/shard_map/apply_early/pallas_call | solution.py:317
  58.9 0.9 %apply_sent.1 = (bf16[192,512]{1,0:T(8,128)(2,1)S(1)}, bf16[192,512]{1,0:T(8,128)(2,1)S(1)}, bf16[192,512]{1,0:T(8,128)(2,1)S(1)}) custom-call(s32[3]{0:T(128)S(1)} %pad_add_fusion.places, bf16[576,640]{1,0:T(8,128)(2,1)S(1)} %get-tuple-element.52.left, ...), custom_call_target="tpu_custom_call", output_to_operand_aliasing={{0}: (4, {}), {1}: (5, {}), {2}: (6, {})} | custom-call | flops 125829120 | bytes 4194304 | tf_op jit(solution)/shard_map/apply_sent/pallas_call | solution.py:325
  59.8 0.8 %collective-permute-start.28 = (bf16[192,512]{1,0:T(8,128)(2,1)S(1)}, bf16[192,512]{1,0:T(8,128)(2,1)S(1)}, u32[]{:S(2)}, u32[]{:S(2)}) collective-permute-start(bf16[192,512]{1,0:T(8,128)(2,1)S(1)} %get-tuple-element.58), channel_id=1, source_target_pairs={{0,4},{1,3},{16,20},{17,19},{32,36},{33,35},{48,52},{49,51},{4,8},... | collective-permute-start | bytes 589832 | tf_op jit(solution)/shard_map/ppermute | solution.py:38
  60.5 2.3 %collective-permute-start.27 = (bf16[192,512]{1,0:T(8,128)(2,1)S(1)}, bf16[192,512]{1,0:T(8,128)(2,1)S(1)}, u32[]{:S(2)}, u32[]{:S(2)}) collective-permute-start(bf16[192,512]{1,0:T(8,128)(2,1)S(1)} %get-tuple-element.57), channel_id=1, source_target_pairs={{0,8},{1,65},{16,24},{17,81},{32,40},{33,97},{48,56},{49,113},{4,1... | collective-permute-start | bytes 589832 | tf_op jit(solution)/shard_map/ppermute | solution.py:38
  63.0 1.0 %apply_kept.1 = f32[192,512]{1,0:T(8,128)S(1)} custom-call(s32[3]{0:T(128)S(1)} %pad_add_fusion.places, bf16[192,640]{1,0:T(8,128)(2,1)S(1)} %get-tuple-element.36.refs_4_.pack, bf16[128,640]{1,0:T(8,128)(2,1)S(1)} %add_convert_fusion.1.refs_0_.piece0, bf16[128,640]{1,0:T(8,128)(2,1)S(1)} %collective-permute-done.14.refs_1_.piece1, ...), custom_call_target="tpu_custom_call" | custom-call | flops 125829120 | bytes 4194304 | tf_op jit(solution)/shard_map/apply_kept/pallas_call | solution.py:334
  64.0 1.6 %collective-permute-done.28 = bf16[192,512]{1,0:T(8,128)(2,1)S(1)} collective-permute-done((bf16[192,512]{1,0:T(8,128)(2,1)S(1)}, bf16[192,512]{1,0:T(8,128)(2,1)S(1)}, u32[]{:S(2)}, u32[]{:S(2)}) %collective-permute-start.28) | collective-permute-done | bytes 196640 | tf_op jit(solution)/shard_map/ppermute | solution.py:38
  65.6 2.5 %collective-permute-done.27 = bf16[192,512]{1,0:T(8,128)(2,1)S(1)} collective-permute-done((bf16[192,512]{1,0:T(8,128)(2,1)S(1)}, bf16[192,512]{1,0:T(8,128)(2,1)S(1)}, u32[]{:S(2)}, u32[]{:S(2)}) %collective-permute-start.27) | collective-permute-done | bytes 196640 | tf_op jit(solution)/shard_map/ppermute | solution.py:38
  68.5 7.2 %collective-permute-start.29 = (f32[192]{0:T(256)S(1)}, f32[192]{0:T(256)S(1)}, u32[]{:S(2)}, u32[]{:S(2)}) collective-permute-start(f32[192]{0:T(256)S(1)} %fusion.5), channel_id=1, source_target_pairs={{0,1},{1,0},{2,3},{3,2},{4,5},{5,4},{6,7},{7,6},{8,9},{9,8},{10,11... | collective-permute-start | bytes 2312 | tf_op jit(solution)/shard_map/ppermute | solution.py:42
  75.8 0.7 collective-permute-done.29
  76.5 0.9 %fusion.7 = f32[192,512]{1,0:T(8,128)} fusion(f32[192]{0:T(256)S(1)} %reduce, f32[192]{0:T(256)S(1)} %add.85, bf16[192,1024]{1,0:T(8,128)(2,1)S(1)} %get-tuple-element.37.refs_0_, bf16[192,512]{1,0:T(8,128)(2,1)S(1)} %collective-permute-done.28, bf16[192,512]{1,0:T(8,128)(2,1)S(1)} %collective-permute-done.27, ...), kind=kLoop, calls=%fused_computation.10 | loop fusion | flops 1277952 | bytes 1574400 | tf_op jit(solution)/shard_map/mul | solution.py:342
  (35 shorter events, 2.5 us)
Async XLA Ops:
  0.0 3.8 %collective-permute-start.1 = (bf16[192,2048]{1,0:T(8,128)(2,1)}, bf16[192,2048]{1,0:T(8,128)(2,1)S(1)}, u32[]{:S(2)}, u32[]{:S(2)}) collective-permute-start(bf16[192,2048]{1,0:T(8,128)(2,1)} %t_own.3), channel_id=1, source_target_pairs={{0,1},{1,0},{2,3},{3,2},{4,5},{5,4},{6,7},{7,6},{8,9},{9,8},{10,11... | collective-permute-start | bytes 2359304 | tf_op jit(solution)/shard_map/ppermute | solution.py:42
  1.4 2.4 %collective-permute-start = (bf16[192,512]{1,0:T(8,128)(2,1)}, bf16[192,512]{1,0:T(8,128)(2,1)S(1)}, u32[]{:S(2)}, u32[]{:S(2)}) collective-permute-start(bf16[192,512]{1,0:T(8,128)(2,1)} %s_own.3), channel_id=1, source_target_pairs={{0,1},{1,0},{2,3},{3,2},{4,5},{5,4},{6,7},{7,6},{8,9},{9,8},{10,11... | collective-permute-start | bytes 589832 | tf_op jit(solution)/shard_map/ppermute | solution.py:42
  1.4 1.1 %copy-start = (bf16[192,2048]{1,0:T(8,128)(2,1)S(1)}, bf16[192,2048]{1,0:T(8,128)(2,1)}, u32[]{:S(2)}) copy-start(bf16[192,2048]{1,0:T(8,128)(2,1)} %t_own.3) | copy-start | bytes 2359300
  2.6 0.9 %copy-start.1 = (bf16[192,512]{1,0:T(8,128)(2,1)S(1)}, bf16[192,512]{1,0:T(8,128)(2,1)}, u32[]{:S(2)}) copy-start(bf16[192,512]{1,0:T(8,128)(2,1)} %s_own.3) | copy-start | bytes 589828
  4.9 8.2 %collective-permute-start.2 = (bf16[192,1024]{1,0:T(8,128)(2,1)S(1)}, bf16[192,1024]{1,0:T(8,128)(2,1)S(1)}, u32[]{:S(2)}, u32[]{:S(2)}) collective-permute-start(bf16[192,1024]{1,0:T(8,128)(2,1)S(1)} %get-tuple-element.38), channel_id=1, source_target_pairs={{0,4},{1,3},{16,20},{17,19},{32,36},{33,35},{48,52},{49,51},{4,8},... | collective-permute-start | bytes 1179656 | tf_op jit(solution)/shard_map/ppermute | solution.py:38
  6.2 12.2 %collective-permute-start.3 = (bf16[192,1024]{1,0:T(8,128)(2,1)S(1)}, bf16[192,1024]{1,0:T(8,128)(2,1)S(1)}, u32[]{:S(2)}, u32[]{:S(2)}) collective-permute-start(bf16[192,1024]{1,0:T(8,128)(2,1)S(1)} %get-tuple-element.39), channel_id=1, source_target_pairs={{0,8},{1,65},{16,24},{17,81},{32,40},{33,97},{48,56},{49,113},{4,1... | collective-permute-start | bytes 1179656 | tf_op jit(solution)/shard_map/ppermute | solution.py:38
  8.7 11.2 %collective-permute-start.4 = (bf16[192,1024]{1,0:T(8,128)(2,1)S(1)}, bf16[192,1024]{1,0:T(8,128)(2,1)S(1)}, u32[]{:S(2)}, u32[]{:S(2)}) collective-permute-start(bf16[192,1024]{1,0:T(8,128)(2,1)S(1)} %get-tuple-element.40), channel_id=1, source_target_pairs={{0,12},{1,67},{16,28},{17,83},{32,44},{33,99},{48,60},{49,115},{4,... | collective-permute-start | bytes 1179656 | tf_op jit(solution)/shard_map/ppermute | solution.py:38
  10.7 14.1 %collective-permute-start.5 = (bf16[192,640]{1,0:T(8,128)(2,1)S(1)}, bf16[192,640]{1,0:T(8,128)(2,1)S(1)}, u32[]{:S(2)}, u32[]{:S(2)}) collective-permute-start(bf16[192,640]{1,0:T(8,128)(2,1)S(1)} %get-tuple-element.41), channel_id=1, source_target_pairs={{0,4},{1,3},{16,20},{17,19},{32,36},{33,35},{48,52},{49,51},{4,8},... | collective-permute-start | bytes 737288 | tf_op jit(solution)/shard_map/ppermute | solution.py:38
  11.0 14.4 %collective-permute-start.6 = (bf16[192,640]{1,0:T(8,128)(2,1)S(1)}, bf16[192,640]{1,0:T(8,128)(2,1)S(1)}, u32[]{:S(2)}, u32[]{:S(2)}) collective-permute-start(bf16[192,640]{1,0:T(8,128)(2,1)S(1)} %get-tuple-element.42), channel_id=1, source_target_pairs={{0,8},{1,65},{16,24},{17,81},{32,40},{33,97},{48,56},{49,113},{4,1... | collective-permute-start | bytes 737288 | tf_op jit(solution)/shard_map/ppermute | solution.py:38
  13.1 12.4 %collective-permute-start.7 = (bf16[192,640]{1,0:T(8,128)(2,1)S(1)}, bf16[192,640]{1,0:T(8,128)(2,1)S(1)}, u32[]{:S(2)}, u32[]{:S(2)}) collective-permute-start(bf16[192,640]{1,0:T(8,128)(2,1)S(1)} %get-tuple-element.43), channel_id=1, source_target_pairs={{0,12},{1,67},{16,28},{17,83},{32,44},{33,99},{48,60},{49,115},{4,... | collective-permute-start | bytes 737288 | tf_op jit(solution)/shard_map/ppermute | solution.py:38
  20.9 9.0 %collective-permute-start.19 = (bf16[128,640]{1,0:T(8,128)(2,1)S(1)}, bf16[128,640]{1,0:T(8,128)(2,1)S(1)}, u32[]{:S(2)}, u32[]{:S(2)}) collective-permute-start(bf16[128,640]{1,0:T(8,128)(2,1)S(1)} %get-tuple-element.51), channel_id=1, source_target_pairs={{0,66},{1,49},{16,82},{17,1},{32,98},{33,17},{48,114},{49,33},{4,7... | collective-permute-start | bytes 491528 | tf_op jit(solution)/shard_map/ppermute | solution.py:38
  24.8 6.0 %collective-permute-start.18 = (bf16[128,640]{1,0:T(8,128)(2,1)S(1)}, bf16[128,640]{1,0:T(8,128)(2,1)S(1)}, u32[]{:S(2)}, u32[]{:S(2)}) collective-permute-start(bf16[128,640]{1,0:T(8,128)(2,1)S(1)} %get-tuple-element.50), channel_id=1, source_target_pairs={{0,64},{1,33},{16,80},{17,49},{32,96},{33,1},{48,112},{49,17},{4,6... | collective-permute-start | bytes 491528 | tf_op jit(solution)/shard_map/ppermute | solution.py:38
  24.8 7.4 %collective-permute-start.17 = (bf16[128,640]{1,0:T(8,128)(2,1)S(1)}, bf16[128,640]{1,0:T(8,128)(2,1)S(1)}, u32[]{:S(2)}, u32[]{:S(2)}) collective-permute-start(bf16[128,640]{1,0:T(8,128)(2,1)S(1)} %get-tuple-element.49), channel_id=1, source_target_pairs={{0,2},{1,17},{16,18},{17,33},{32,34},{33,49},{48,50},{49,1},{4,6},... | collective-permute-start | bytes 491528 | tf_op jit(solution)/shard_map/ppermute | solution.py:38
  27.0 8.2 %collective-permute-start.10 = (bf16[128,640]{1,0:T(8,128)(2,1)S(1)}, bf16[128,640]{1,0:T(8,128)(2,1)S(1)}, u32[]{:S(2)}, u32[]{:S(2)}) collective-permute-start(bf16[128,640]{1,0:T(8,128)(2,1)S(1)} %get-tuple-element.47), channel_id=1, source_target_pairs={{0,48},{1,13},{16,0},{17,29},{32,16},{33,45},{48,32},{49,61},{4,52... | collective-permute-start | bytes 491528 | tf_op jit(solution)/shard_map/ppermute | solution.py:38
  29.6 6.1 %collective-permute-start.9 = (bf16[128,640]{1,0:T(8,128)(2,1)S(1)}, bf16[128,640]{1,0:T(8,128)(2,1)S(1)}, u32[]{:S(2)}, u32[]{:S(2)}) collective-permute-start(bf16[128,640]{1,0:T(8,128)(2,1)S(1)} %get-tuple-element.46), channel_id=1, source_target_pairs={{0,32},{1,9},{16,48},{17,25},{32,0},{33,41},{48,16},{49,57},{4,36}... | collective-permute-start | bytes 491528 | tf_op jit(solution)/shard_map/ppermute | solution.py:38
  29.9 7.4 %collective-permute-start.8 = (bf16[128,640]{1,0:T(8,128)(2,1)S(1)}, bf16[128,640]{1,0:T(8,128)(2,1)S(1)}, u32[]{:S(2)}, u32[]{:S(2)}) collective-permute-start(bf16[128,640]{1,0:T(8,128)(2,1)S(1)} %get-tuple-element.45), channel_id=1, source_target_pairs={{0,16},{1,5},{16,32},{17,21},{32,48},{33,37},{48,0},{49,53},{4,20}... | collective-permute-start | bytes 491528 | tf_op jit(solution)/shard_map/ppermute | solution.py:38
  32.3 8.6 %collective-permute-start.22 = (bf16[128,640]{1,0:T(8,128)(2,1)S(1)}, bf16[128,640]{1,0:T(8,128)(2,1)S(1)}, u32[]{:S(2)}, u32[]{:S(2)}) collective-permute-start(bf16[128,640]{1,0:T(8,128)(2,1)S(1)} %fusion.9), channel_id=1, source_target_pairs={{0,48},{1,13},{16,0},{17,29},{32,16},{33,45},{48,32},{49,61},{4,52... | collective-permute-start | bytes 491528 | tf_op jit(solution)/shard_map/ppermute | solution.py:38
  34.7 6.2 %collective-permute-start.21 = (bf16[128,640]{1,0:T(8,128)(2,1)S(1)}, bf16[128,640]{1,0:T(8,128)(2,1)S(1)}, u32[]{:S(2)}, u32[]{:S(2)}) collective-permute-start(bf16[128,640]{1,0:T(8,128)(2,1)S(1)} %fusion.9), channel_id=1, source_target_pairs={{0,32},{1,9},{16,48},{17,25},{32,0},{33,41},{48,16},{49,57},{4,36}... | collective-permute-start | bytes 491528 | tf_op jit(solution)/shard_map/ppermute | solution.py:38
  35.2 6.9 %collective-permute-start.20 = (bf16[128,640]{1,0:T(8,128)(2,1)S(1)}, bf16[128,640]{1,0:T(8,128)(2,1)S(1)}, u32[]{:S(2)}, u32[]{:S(2)}) collective-permute-start(bf16[128,640]{1,0:T(8,128)(2,1)S(1)} %fusion.9), channel_id=1, source_target_pairs={{0,16},{1,5},{16,32},{17,21},{32,48},{33,37},{48,0},{49,53},{4,20}... | collective-permute-start | bytes 491528 | tf_op jit(solution)/shard_map/ppermute | solution.py:38
  37.4 8.6 %collective-permute-start.13 = (bf16[128,640]{1,0:T(8,128)(2,1)S(1)}, bf16[128,640]{1,0:T(8,128)(2,1)S(1)}, u32[]{:S(2)}, u32[]{:S(2)}) collective-permute-start(bf16[128,640]{1,0:T(8,128)(2,1)S(1)} %fusion.8), channel_id=1, source_target_pairs={{0,66},{1,49},{16,82},{17,1},{32,98},{33,17},{48,114},{49,33},{4,7... | collective-permute-start | bytes 491528 | tf_op jit(solution)/shard_map/ppermute | solution.py:38
  39.4 10.0 %collective-permute-start.12 = (bf16[128,640]{1,0:T(8,128)(2,1)S(1)}, bf16[128,640]{1,0:T(8,128)(2,1)S(1)}, u32[]{:S(2)}, u32[]{:S(2)}) collective-permute-start(bf16[128,640]{1,0:T(8,128)(2,1)S(1)} %fusion.8), channel_id=1, source_target_pairs={{0,64},{1,33},{16,80},{17,49},{32,96},{33,1},{48,112},{49,17},{4,6... | collective-permute-start | bytes 491528 | tf_op jit(solution)/shard_map/ppermute | solution.py:38
  40.9 9.0 %collective-permute-start.11 = (bf16[128,640]{1,0:T(8,128)(2,1)S(1)}, bf16[128,640]{1,0:T(8,128)(2,1)S(1)}, u32[]{:S(2)}, u32[]{:S(2)}) collective-permute-start(bf16[128,640]{1,0:T(8,128)(2,1)S(1)} %fusion.8), channel_id=1, source_target_pairs={{0,2},{1,17},{16,18},{17,33},{32,34},{33,49},{48,50},{49,1},{4,6},... | collective-permute-start | bytes 491528 | tf_op jit(solution)/shard_map/ppermute | solution.py:38
  42.3 10.8 %collective-permute-start.23 = (bf16[128,640]{1,0:T(8,128)(2,1)S(1)}, bf16[128,640]{1,0:T(8,128)(2,1)S(1)}, u32[]{:S(2)}, u32[]{:S(2)}) collective-permute-start(bf16[128,640]{1,0:T(8,128)(2,1)S(1)} %add_convert_fusion.refs_4_), channel_id=1, source_target_pairs={{0,2},{1,17},{16,18},{17,33},{32,34},{33,49},{48,50},{49,1},{4,6},... | collective-permute-start | bytes 491528 | tf_op jit(solution)/shard_map/ppermute | solution.py:38
  42.7 11.3 %collective-permute-start.24 = (bf16[128,640]{1,0:T(8,128)(2,1)S(1)}, bf16[128,640]{1,0:T(8,128)(2,1)S(1)}, u32[]{:S(2)}, u32[]{:S(2)}) collective-permute-start(bf16[128,640]{1,0:T(8,128)(2,1)S(1)} %add_convert_fusion.refs_4_), channel_id=1, source_target_pairs={{0,64},{1,33},{16,80},{17,49},{32,96},{33,1},{48,112},{49,17},{4,6... | collective-permute-start | bytes 491528 | tf_op jit(solution)/shard_map/ppermute | solution.py:38
  45.9 8.1 %collective-permute-start.25 = (bf16[128,640]{1,0:T(8,128)(2,1)S(1)}, bf16[128,640]{1,0:T(8,128)(2,1)S(1)}, u32[]{:S(2)}, u32[]{:S(2)}) collective-permute-start(bf16[128,640]{1,0:T(8,128)(2,1)S(1)} %add_convert_fusion.refs_4_), channel_id=1, source_target_pairs={{0,66},{1,49},{16,82},{17,1},{32,98},{33,17},{48,114},{49,33},{4,7... | collective-permute-start | bytes 491528 | tf_op jit(solution)/shard_map/ppermute | solution.py:38
  50.0 5.7 %collective-permute-start.14 = (bf16[128,640]{1,0:T(8,128)(2,1)S(1)}, bf16[128,640]{1,0:T(8,128)(2,1)S(1)}, u32[]{:S(2)}, u32[]{:S(2)}) collective-permute-start(bf16[128,640]{1,0:T(8,128)(2,1)S(1)} %add_convert_fusion.1.refs_0_.piece0), channel_id=1, source_target_pairs={{0,16},{1,5},{16,32},{17,21},{32,48},{33,37},{48,0},{49,53},{4,20}... | collective-permute-start | bytes 491528 | tf_op jit(solution)/shard_map/ppermute | solution.py:38
  51.0 6.5 %collective-permute-start.15 = (bf16[128,640]{1,0:T(8,128)(2,1)S(1)}, bf16[128,640]{1,0:T(8,128)(2,1)S(1)}, u32[]{:S(2)}, u32[]{:S(2)}) collective-permute-start(bf16[128,640]{1,0:T(8,128)(2,1)S(1)} %add_convert_fusion.1.refs_0_.piece0), channel_id=1, source_target_pairs={{0,32},{1,9},{16,48},{17,25},{32,0},{33,41},{48,16},{49,57},{4,36}... | collective-permute-start | bytes 491528 | tf_op jit(solution)/shard_map/ppermute | solution.py:38
  53.1 5.7 %collective-permute-start.16 = (bf16[128,640]{1,0:T(8,128)(2,1)S(1)}, bf16[128,640]{1,0:T(8,128)(2,1)S(1)}, u32[]{:S(2)}, u32[]{:S(2)}) collective-permute-start(bf16[128,640]{1,0:T(8,128)(2,1)S(1)} %add_convert_fusion.1.refs_0_.piece0), channel_id=1, source_target_pairs={{0,48},{1,13},{16,0},{17,29},{32,16},{33,45},{48,32},{49,61},{4,52... | collective-permute-start | bytes 491528 | tf_op jit(solution)/shard_map/ppermute | solution.py:38
  59.8 5.8 %collective-permute-start.28 = (bf16[192,512]{1,0:T(8,128)(2,1)S(1)}, bf16[192,512]{1,0:T(8,128)(2,1)S(1)}, u32[]{:S(2)}, u32[]{:S(2)}) collective-permute-start(bf16[192,512]{1,0:T(8,128)(2,1)S(1)} %get-tuple-element.58), channel_id=1, source_target_pairs={{0,4},{1,3},{16,20},{17,19},{32,36},{33,35},{48,52},{49,51},{4,8},... | collective-permute-start | bytes 589832 | tf_op jit(solution)/shard_map/ppermute | solution.py:38
  60.5 7.5 %collective-permute-start.27 = (bf16[192,512]{1,0:T(8,128)(2,1)S(1)}, bf16[192,512]{1,0:T(8,128)(2,1)S(1)}, u32[]{:S(2)}, u32[]{:S(2)}) collective-permute-start(bf16[192,512]{1,0:T(8,128)(2,1)S(1)} %get-tuple-element.57), channel_id=1, source_target_pairs={{0,8},{1,65},{16,24},{17,81},{32,40},{33,97},{48,56},{49,113},{4,1... | collective-permute-start | bytes 589832 | tf_op jit(solution)/shard_map/ppermute | solution.py:38
  62.9 5.4 %collective-permute-start.26 = (bf16[192,512]{1,0:T(8,128)(2,1)S(1)}, bf16[192,512]{1,0:T(8,128)(2,1)S(1)}, u32[]{:S(2)}, u32[]{:S(2)}) collective-permute-start(bf16[192,512]{1,0:T(8,128)(2,1)S(1)} %get-tuple-element.56), channel_id=1, source_target_pairs={{0,12},{1,67},{16,28},{17,83},{32,44},{33,99},{48,60},{49,115},{4,... | collective-permute-start | bytes 589832 | tf_op jit(solution)/shard_map/ppermute | solution.py:38
  68.5 8.0 %collective-permute-start.29 = (f32[192]{0:T(256)S(1)}, f32[192]{0:T(256)S(1)}, u32[]{:S(2)}, u32[]{:S(2)}) collective-permute-start(f32[192]{0:T(256)S(1)} %fusion.5), channel_id=1, source_target_pairs={{0,1},{1,0},{2,3},{3,2},{4,5},{5,4},{6,7},{7,6},{8,9},{9,8},{10,11... | collective-permute-start | bytes 2312 | tf_op jit(solution)/shard_map/ppermute | solution.py:42

commit v11 on v10

--- a/solution.py
+++ b/solution.py
@@ -17,7 +17,6 @@
 ORDER = (2, 1, 3)
 STRIP = 32
 PARAMS = pltpu.CompilerParams(vmem_limit_bytes=40 * 1024 * 1024)
-SCALAR = pl.BlockSpec(memory_space=pltpu.SMEM)
 WHOLE = pl.BlockSpec(memory_space=pltpu.VMEM)
 BF16, F32 = jnp.bfloat16, jnp.float32
 
@@ -42,10 +41,10 @@
     return lax.ppermute(array, "sec", [(0, 1), (1, 0)])
 
 
-def place_along(axis_of_core):
+def places_here():
     loop, rep, core = (lax.axis_index(name) for name in AXES)
-    place = ((loop // SIZE) * 2 + rep % 2, rep // 2, loop % SIZE)
-    return jnp.where(core == 0, place[axis_of_core[0]], place[axis_of_core[1]])
+    chip = (lax.div(loop, SIZE) * 2 + lax.rem(rep, 2), lax.div(rep, 2), lax.rem(loop, SIZE))
+    return [jnp.where(core == 0, chip[axes[0]], chip[axes[1]]) for axes in (GATHER, *FIRST)]
 
 
 def scaled(piece, inv):
@@ -71,7 +70,8 @@
         ssq_t[at, :] = squares(t_own[at, :])
 
 
-def pack_own_kernel(places, s_own, s_far, t_own, t_far, ssq_s, ssq_t, *outs):
+def pack_own_kernel(s_own, s_far, t_own, t_far, ssq_s, ssq_t, *outs):
+    places = places_here()
     rows, half = s_own.shape
     ts = t_own.shape[1] // SIZE
     inv_s, inv_t = outs[SIZE:]
@@ -85,7 +85,8 @@
             outs[by][at, pl.ds(half, ts)] = scaled(t_own[at, part(places, by, ts)], inv_t[at, :])
 
 
-def pack_far_kernel(places, s_far, t_far, inv_s, inv_t, *outs):
+def pack_far_kernel(s_far, t_far, inv_s, inv_t, *outs):
+    places = places_here()
     rows = s_far.shape[0]
     ss, ts = s_far.shape[1] // SIZE, t_far.shape[1] // SIZE
     for at in strips(rows):
@@ -133,7 +134,8 @@
         out[:, pl.ds(ss, feats - ss)] = -rows[:, ss:].astype(out.dtype)
 
 
-def gram_early_kernel(share, places, *refs):
+def gram_early_kernel(share, *refs):
+    places = places_here()
     packs, (product, left, right) = refs[:-3], refs[-3:]
     stack(places, 0, packs, packs, left, right)
     product[...] = cross(left, right)
@@ -145,13 +147,15 @@
     product[block, pl.ds(0, ss)] -= jnp.where(row == col, share, 0.0)
 
 
-def gram_native_kernel(places, pack, before, *refs):
+def gram_native_kernel(pack, before, *refs):
+    places = places_here()
     outs, (left, right) = refs[:SIZE], refs[SIZE:]
     stack(places, 0, [pack], [pack], left, right)
     emit(before[...] + cross(left, right), outs)
 
 
-def gram_far_kernel(places, *refs):
+def gram_far_kernel(*refs):
+    places = places_here()
     norms, packs, outs = refs[:SIZE], refs[SIZE : 2 * SIZE], refs[2 * SIZE : 3 * SIZE]
     left, right = refs[3 * SIZE :]
     stack(places, 1, norms, packs, left, right)
@@ -169,7 +173,8 @@
     return lax.dot_general(left, weights, (((1,), (1,)), ((), ())), preferred_element_type=F32)
 
 
-def apply_native_kernel(places, *refs):
+def apply_native_kernel(*refs):
+    places = places_here()
     packs, pieces, (out, left, weights) = refs[:SIZE], refs[SIZE : 2 * SIZE], refs[2 * SIZE :]
     half, feats = weights.shape
     rows, ss = packs[0].shape[0], half // SIZE
@@ -182,7 +187,8 @@
     out[...] = times(left[...], weights[...])
 
 
-def apply_early_kernel(places, far1, far2, far3, piece0, piece1, piece2, before, *refs):
+def apply_early_kernel(far1, far2, far3, piece0, piece1, piece2, before, *refs):
+    places = places_here()
     outs, (left, weights) = refs[: SIZE - 1], refs[SIZE - 1 :]
     rows = far1.shape[0]
     last = jnp.zeros(piece0.shape, piece0.dtype)
@@ -195,7 +201,8 @@
         out[...] = (product[k * rows : (k + 1) * rows] + sofar).astype(out.dtype)
 
 
-def apply_sent_kernel(places, left, piece, before, early1, early2, early3, *outs):
+def apply_sent_kernel(left, piece, before, early1, early2, early3, *outs):
+    places = places_here()
     rows, ss = outs[0].shape[0], piece.shape[0]
     which = lax.rem(places[2] + 1, SIZE)
     block = pl.ds(pl.multiple_of(which * ss, ss), ss)
@@ -205,7 +212,8 @@
         out[:, block] = (product[k * rows : (k + 1) * rows] + sofar).astype(out.dtype)
 
 
-def apply_kept_kernel(places, pack, *refs):
+def apply_kept_kernel(pack, *refs):
+    places = places_here()
     pieces, (before, out, weights) = refs[:SIZE], refs[SIZE:]
     gather_weights(places[2], pieces, weights)
     out[...] = times(pack[...], weights[...]) + before[pl.ds(0, pack.shape[0]), :]
@@ -219,7 +227,7 @@
     return pl.pallas_call(
         kernel,
         out_shape=outs,
-        in_specs=[SCALAR] + [WHOLE] * n_in,
+        in_specs=[WHOLE] * n_in,
         out_specs=[WHOLE] * len(outs),
         scratch_shapes=list(scratch),
         input_output_aliases=aliases or {},
@@ -240,27 +248,20 @@
     ss, ts = half // SIZE, wide // SIZE
     feats = ss + ts
     flops = 2 * SIZE * rows * half * feats
-    places = jnp.stack([place_along(axes) for axes in (GATHER, *FIRST)]).astype(jnp.int32)
 
     t_far, s_far = other_core(teacher), other_core(student)
-    ssq_s, ssq_t = pl.pallas_call(
-        sums_kernel,
-        out_shape=shapes(*[((rows, 1), F32)] * 2),
-        in_specs=[WHOLE] * 2,
-        out_specs=[WHOLE] * 2,
-        compiler_params=PARAMS,
-        cost_estimate=pl.CostEstimate(flops=0, bytes_accessed=1 << 20, transcendentals=0),
-        name="sums",
-    )(student, teacher)
+    ssq_s, ssq_t = kernel_call(sums_kernel, "sums", shapes(*[((rows, 1), F32)] * 2), 2)(
+        student, teacher
+    )
     *near, inv_s, inv_t = kernel_call(
         pack_own_kernel,
         "pack_own",
         shapes(*[((rows, half + ts), BF16)] * SIZE, *[((rows, 1), F32)] * 2),
         6,
-    )(places, student, s_far, teacher, t_far, ssq_s, ssq_t)
+    )(student, s_far, teacher, t_far, ssq_s, ssq_t)
     far = kernel_call(
         pack_far_kernel, "pack_far", shapes(*[((rows, feats), BF16)] * SIZE), 4
-    )(places, s_far, t_far, inv_s, inv_t)
+    )(s_far, t_far, inv_s, inv_t)
     norm_own = near[0][:, :half]
 
     def exchanged(own, sent, axis_of_core, sign=1):
@@ -287,13 +288,13 @@
         3,
         operands(3),
         flops,
-    )(places, *near[:3])[0]
+    )(*near[:3])[0]
     near_blocks = kernel_call(
         gram_native_kernel, "gram_native", blocks, 2, operands(1), flops // 4
-    )(places, near[3], early)
+    )(near[3], early)
     far_blocks = kernel_call(
         gram_far_kernel, "gram_far", blocks, 2 * SIZE, operands(SIZE), flops
-    )(places, *near, *far)
+    )(*near, *far)
 
     def weights_of(chunk, own, *sends):
         total = added(own, lambda by: sends[by - 1], FIRST[chunk])
@@ -311,7 +312,7 @@
         2 * SIZE,
         [pltpu.VMEM((SIZE * rows, feats), BF16), pltpu.VMEM((half, feats), BF16)],
         flops,
-    )(places, *near, *near_weights)[0]
+    )(*near, *near_weights)[0]
     messages = shapes(*[((rows, half), BF16)] * 3)
     weights = pltpu.VMEM((half, feats), BF16)
     *most, stacked = kernel_call(
@@ -321,7 +322,7 @@
         7,
         [weights],
         flops * 3 // 4,
-    )(places, *far[1:], *far_weights[:3], sofar)
+    )(*far[1:], *far_weights[:3], sofar)
     parts = kernel_call(
         apply_sent_kernel,
         "apply_sent",
@@ -329,11 +330,11 @@
         6,
         (),
         flops // 4,
-        {4 + k: k for k in range(3)},
-    )(places, stacked, far_weights[3], sofar, *most)
+        {3 + k: k for k in range(3)},
+    )(stacked, far_weights[3], sofar, *most)
     grad_n = kernel_call(
         apply_kept_kernel, "apply_kept", shapes(((rows, half), F32)), SIZE + 2, [weights], flops // 4
-    )(places, far[0], *far_weights, sofar)[0]
+    )(far[0], *far_weights, sofar)[0]
     norm_f = norm_own.astype(F32)
     grad_n = grad_n + level * norm_f
     grad_n = coef * added(grad_n, lambda by: parts[by - 1], GATHER, -1)

time: 77.6 us -> 74.3 us (0.957)
  Pallas kernels: 10.6 us -> 5.8 us
  starting transfers between devices: 44.5 us -> 45.5 us
    ppermute x27, starting transfers between devices: 35.9 us -> 37.4 us  [shifted(): return lax.ppermute(array, AXES, pairs)]
  transfers between devices with their start and end apart: 30 -> 30, of which waited for: 14 -> 15; matrix products, arithmetic and copies ran while one was open for 1% -> 1% of each run, Pallas kernels for 11% -> 7%
where the time goes in v11:
time: 74.3 us; the launch traced here: 74.2 us
  starting transfers between devices  45.5 us (61%)
  waiting for transfers between devices  19 us (26%)
  Pallas kernels  5.8 us (8%)
  local copies, waits for them, and re-layouts  2.06 us (3%)
  other arithmetic  1.7 us (2%)
    ppermute x27, starting transfers between devices, shifted(): return lax.ppermute(array, AXES, pairs)  37.4 us
    ppermute x27, waiting for transfers between devices, shifted(): return lax.ppermute(array, AXES, pairs)  18.2 us
    ppermute x3, starting transfers between devices, other_core(): return lax.ppermute(array, 'sec', [(0, 1), (1, 0)])  8.09 us
    unnamed x4, local copies, waits for them, and re-layouts  2.06 us
  transfers between devices with their start and end apart: 30, of which 15 were waited for; matrix products, arithmetic and copies ran while one was open for 1% of the time, Pallas kernels for 7%

profile of v11, /device:TPU:1, one launch (start us, length us, event | category | flops | bytes accessed | tf_op | source)
XLA Modules:
  0.0 74.2 jit_solution(17572958542882568001)
XLA Ops:
  0.0 1.4 %collective-permute-start.1 = (bf16[192,2048]{1,0:T(8,128)(2,1)}, bf16[192,2048]{1,0:T(8,128)(2,1)S(1)}, u32[]{:S(2)}, u32[]{:S(2)}) collective-permute-start(bf16[192,2048]{1,0:T(8,128)(2,1)} %t_own.3), channel_id=1, source_target_pairs={{0,1},{1,0},{2,3},{3,2},{4,5},{5,4},{6,7},{7,6},{8,9},{9,8},{10,11... | collective-permute-start | bytes 2359304 | tf_op jit(solution)/shard_map/ppermute | solution.py:41
  1.4 1.1 %copy-done = bf16[192,2048]{1,0:T(8,128)(2,1)S(1)} copy-done((bf16[192,2048]{1,0:T(8,128)(2,1)S(1)}, bf16[192,2048]{1,0:T(8,128)(2,1)}, u32[]{:S(2)}) %copy-start) | copy-done | bytes 786456
  2.6 0.9 %copy-done.1 = bf16[192,512]{1,0:T(8,128)(2,1)S(1)} copy-done((bf16[192,512]{1,0:T(8,128)(2,1)S(1)}, bf16[192,512]{1,0:T(8,128)(2,1)}, u32[]{:S(2)}) %copy-start.1) | copy-done | bytes 196632
  3.8 0.5 pack_own.1
  4.3 1.4 %collective-permute-start.2 = (bf16[192,1024]{1,0:T(8,128)(2,1)S(1)}, bf16[192,1024]{1,0:T(8,128)(2,1)S(1)}, u32[]{:S(2)}, u32[]{:S(2)}) collective-permute-start(bf16[192,1024]{1,0:T(8,128)(2,1)S(1)} %get-tuple-element.38), channel_id=1, source_target_pairs={{0,4},{1,3},{16,20},{17,19},{32,36},{33,35},{48,52},{49,51},{4,8},... | collective-permute-start | bytes 1179656 | tf_op jit(solution)/shard_map/ppermute | solution.py:37
  5.7 2.5 %collective-permute-start.3 = (bf16[192,1024]{1,0:T(8,128)(2,1)S(1)}, bf16[192,1024]{1,0:T(8,128)(2,1)S(1)}, u32[]{:S(2)}, u32[]{:S(2)}) collective-permute-start(bf16[192,1024]{1,0:T(8,128)(2,1)S(1)} %get-tuple-element.39), channel_id=1, source_target_pairs={{0,8},{1,65},{16,24},{17,81},{32,40},{33,97},{48,56},{49,113},{4,1... | collective-permute-start | bytes 1179656 | tf_op jit(solution)/shard_map/ppermute | solution.py:37
  8.1 1.2 %collective-permute-start.4 = (bf16[192,1024]{1,0:T(8,128)(2,1)S(1)}, bf16[192,1024]{1,0:T(8,128)(2,1)S(1)}, u32[]{:S(2)}, u32[]{:S(2)}) collective-permute-start(bf16[192,1024]{1,0:T(8,128)(2,1)S(1)} %get-tuple-element.40), channel_id=1, source_target_pairs={{0,12},{1,67},{16,28},{17,83},{32,44},{33,99},{48,60},{49,115},{4,... | collective-permute-start | bytes 1179656 | tf_op jit(solution)/shard_map/ppermute | solution.py:37
  9.6 0.4 collective-permute-start.5
  10.0 0.9 %collective-permute-start.6 = (bf16[192,640]{1,0:T(8,128)(2,1)S(1)}, bf16[192,640]{1,0:T(8,128)(2,1)S(1)}, u32[]{:S(2)}, u32[]{:S(2)}) collective-permute-start(bf16[192,640]{1,0:T(8,128)(2,1)S(1)} %get-tuple-element.42), channel_id=1, source_target_pairs={{0,8},{1,65},{16,24},{17,81},{32,40},{33,97},{48,56},{49,113},{4,1... | collective-permute-start | bytes 737288 | tf_op jit(solution)/shard_map/ppermute | solution.py:37
  10.8 1.7 %collective-permute-done.2.refs_1_ = bf16[192,1024]{1,0:T(8,128)(2,1)S(1)} collective-permute-done((bf16[192,1024]{1,0:T(8,128)(2,1)S(1)}, bf16[192,1024]{1,0:T(8,128)(2,1)S(1)}, u32[]{:S(2)}, u32[]{:S(2)}) %collective-permute-start.2) | collective-permute-done | bytes 393248 | tf_op jit(solution)/shard_map/ppermute | solution.py:37
  12.5 1.4 %collective-permute-start.7 = (bf16[192,640]{1,0:T(8,128)(2,1)S(1)}, bf16[192,640]{1,0:T(8,128)(2,1)S(1)}, u32[]{:S(2)}, u32[]{:S(2)}) collective-permute-start(bf16[192,640]{1,0:T(8,128)(2,1)S(1)} %get-tuple-element.43), channel_id=1, source_target_pairs={{0,12},{1,67},{16,28},{17,83},{32,44},{33,99},{48,60},{49,115},{4,... | collective-permute-start | bytes 737288 | tf_op jit(solution)/shard_map/ppermute | solution.py:37
  13.9 4.0 %collective-permute-done.3.refs_2_ = bf16[192,1024]{1,0:T(8,128)(2,1)S(1)} collective-permute-done((bf16[192,1024]{1,0:T(8,128)(2,1)S(1)}, bf16[192,1024]{1,0:T(8,128)(2,1)S(1)}, u32[]{:S(2)}, u32[]{:S(2)}) %collective-permute-start.3) | collective-permute-done | bytes 393248 | tf_op jit(solution)/shard_map/ppermute | solution.py:37
  17.9 1.0 %gram_early.1.before = f32[512,640]{1,0:T(8,128)S(1)} custom-call(bf16[192,1024]{1,0:T(8,128)(2,1)S(1)} %get-tuple-element.37.refs_0_, bf16[192,1024]{1,0:T(8,128)(2,1)S(1)} %collective-permute-done.2.refs_1_, bf16[192,1024]{1,0:T(8,128)(2,1)S(1)} %collective-permute-done.3.refs_2_), custom_call_target="tpu_custom_call" | custom-call | flops 503316480 | bytes 4194304 | tf_op jit(solution)/shard_map/gram_early/pallas_call | solution.py:284
  18.9 0.5 gram_native.1
  19.3 3.8 %collective-permute-start.19 = (bf16[128,640]{1,0:T(8,128)(2,1)S(1)}, bf16[128,640]{1,0:T(8,128)(2,1)S(1)}, u32[]{:S(2)}, u32[]{:S(2)}) collective-permute-start(bf16[128,640]{1,0:T(8,128)(2,1)S(1)} %get-tuple-element.51), channel_id=1, source_target_pairs={{0,66},{1,49},{16,82},{17,1},{32,98},{33,17},{48,114},{49,33},{4,7... | collective-permute-start | bytes 491528 | tf_op jit(solution)/shard_map/ppermute | solution.py:37
  23.2 0.7 collective-permute-start.17
  23.9 1.0 %gram_far.1 = (f32[128,640]{1,0:T(8,128)S(1)}, bf16[128,640]{1,0:T(8,128)(2,1)S(1)}, bf16[128,640]{1,0:T(8,128)(2,1)S(1)}, bf16[128,640]{1,0:T(8,128)(2,1)S(1)}) custom-call(bf16[192,1024]{1,0:T(8,128)(2,1)S(1)} %get-tuple-element.37.refs_0_, bf16[192,1024]{1,0:T(8,128)(2,1)S(1)} %collective-permute-done.2.refs_1_, ...), custom_call_target="tpu_custom_call" | custom-call | flops 503316480 | bytes 4194304 | tf_op jit(solution)/shard_map/gram_far/pallas_call | solution.py:295
  24.8 2.6 %collective-permute-start.10 = (bf16[128,640]{1,0:T(8,128)(2,1)S(1)}, bf16[128,640]{1,0:T(8,128)(2,1)S(1)}, u32[]{:S(2)}, u32[]{:S(2)}) collective-permute-start(bf16[128,640]{1,0:T(8,128)(2,1)S(1)} %get-tuple-element.47), channel_id=1, source_target_pairs={{0,48},{1,13},{16,0},{17,29},{32,16},{33,45},{48,32},{49,61},{4,52... | collective-permute-start | bytes 491528 | tf_op jit(solution)/shard_map/ppermute | solution.py:37
  27.7 0.7 collective-permute-start.8
  28.4 0.7 collective-permute-done.18
  29.2 1.4 %collective-permute-done.17 = bf16[128,640]{1,0:T(8,128)(2,1)S(1)} collective-permute-done((bf16[128,640]{1,0:T(8,128)(2,1)S(1)}, bf16[128,640]{1,0:T(8,128)(2,1)S(1)}, u32[]{:S(2)}, u32[]{:S(2)}) %collective-permute-start.17) | collective-permute-done | bytes 163872 | tf_op jit(solution)/shard_map/ppermute | solution.py:37
  30.7 2.3 %collective-permute-start.22 = (bf16[128,640]{1,0:T(8,128)(2,1)S(1)}, bf16[128,640]{1,0:T(8,128)(2,1)S(1)}, u32[]{:S(2)}, u32[]{:S(2)}) collective-permute-start(bf16[128,640]{1,0:T(8,128)(2,1)S(1)} %fusion.9), channel_id=1, source_target_pairs={{0,48},{1,13},{16,0},{17,29},{32,16},{33,45},{48,32},{49,61},{4,52... | collective-permute-start | bytes 491528 | tf_op jit(solution)/shard_map/ppermute | solution.py:37
  33.0 0.6 collective-permute-start.21
  33.6 0.7 collective-permute-start.20
  34.3 0.8 %collective-permute-done.8 = bf16[128,640]{1,0:T(8,128)(2,1)S(1)} collective-permute-done((bf16[128,640]{1,0:T(8,128)(2,1)S(1)}, bf16[128,640]{1,0:T(8,128)(2,1)S(1)}, u32[]{:S(2)}, u32[]{:S(2)}) %collective-permute-start.8) | collective-permute-done | bytes 163872 | tf_op jit(solution)/shard_map/ppermute | solution.py:37
  35.2 3.1 %collective-permute-start.13 = (bf16[128,640]{1,0:T(8,128)(2,1)S(1)}, bf16[128,640]{1,0:T(8,128)(2,1)S(1)}, u32[]{:S(2)}, u32[]{:S(2)}) collective-permute-start(bf16[128,640]{1,0:T(8,128)(2,1)S(1)} %fusion.8), channel_id=1, source_target_pairs={{0,66},{1,49},{16,82},{17,1},{32,98},{33,17},{48,114},{49,33},{4,7... | collective-permute-start | bytes 491528 | tf_op jit(solution)/shard_map/ppermute | solution.py:37
  38.3 0.4 collective-permute-start.12
  39.0 1.5 %collective-permute-done.20 = bf16[128,640]{1,0:T(8,128)(2,1)S(1)} collective-permute-done((bf16[128,640]{1,0:T(8,128)(2,1)S(1)}, bf16[128,640]{1,0:T(8,128)(2,1)S(1)}, u32[]{:S(2)}, u32[]{:S(2)}) %collective-permute-start.20) | collective-permute-done | bytes 163872 | tf_op jit(solution)/shard_map/ppermute | solution.py:37
  40.6 0.6 collective-permute-start.23
  41.2 2.1 %collective-permute-start.24 = (bf16[128,640]{1,0:T(8,128)(2,1)S(1)}, bf16[128,640]{1,0:T(8,128)(2,1)S(1)}, u32[]{:S(2)}, u32[]{:S(2)}) collective-permute-start(bf16[128,640]{1,0:T(8,128)(2,1)S(1)} %add_convert_fusion.refs_4_), channel_id=1, source_target_pairs={{0,64},{1,33},{16,80},{17,49},{32,96},{33,1},{48,112},{49,17},{4,6... | collective-permute-start | bytes 491528 | tf_op jit(solution)/shard_map/ppermute | solution.py:37
  43.3 1.0 %collective-permute-done.13 = bf16[128,640]{1,0:T(8,128)(2,1)S(1)} collective-permute-done((bf16[128,640]{1,0:T(8,128)(2,1)S(1)}, bf16[128,640]{1,0:T(8,128)(2,1)S(1)}, u32[]{:S(2)}, u32[]{:S(2)}) %collective-permute-start.13) | collective-permute-done | bytes 163872 | tf_op jit(solution)/shard_map/ppermute | solution.py:37
  44.2 3.4 %collective-permute-start.25 = (bf16[128,640]{1,0:T(8,128)(2,1)S(1)}, bf16[128,640]{1,0:T(8,128)(2,1)S(1)}, u32[]{:S(2)}, u32[]{:S(2)}) collective-permute-start(bf16[128,640]{1,0:T(8,128)(2,1)S(1)} %add_convert_fusion.refs_4_), channel_id=1, source_target_pairs={{0,66},{1,49},{16,82},{17,1},{32,98},{33,17},{48,114},{49,33},{4,7... | collective-permute-start | bytes 491528 | tf_op jit(solution)/shard_map/ppermute | solution.py:37
  48.1 1.8 %collective-permute-start.14 = (bf16[128,640]{1,0:T(8,128)(2,1)S(1)}, bf16[128,640]{1,0:T(8,128)(2,1)S(1)}, u32[]{:S(2)}, u32[]{:S(2)}) collective-permute-start(bf16[128,640]{1,0:T(8,128)(2,1)S(1)} %add_convert_fusion.1.refs_0_.piece0), channel_id=1, source_target_pairs={{0,16},{1,5},{16,32},{17,21},{32,48},{33,37},{48,0},{49,53},{4,20}... | collective-permute-start | bytes 491528 | tf_op jit(solution)/shard_map/ppermute | solution.py:37
  49.9 1.6 %collective-permute-start.15 = (bf16[128,640]{1,0:T(8,128)(2,1)S(1)}, bf16[128,640]{1,0:T(8,128)(2,1)S(1)}, u32[]{:S(2)}, u32[]{:S(2)}) collective-permute-start(bf16[128,640]{1,0:T(8,128)(2,1)S(1)} %add_convert_fusion.1.refs_0_.piece0), channel_id=1, source_target_pairs={{0,32},{1,9},{16,48},{17,25},{32,0},{33,41},{48,16},{49,57},{4,36}... | collective-permute-start | bytes 491528 | tf_op jit(solution)/shard_map/ppermute | solution.py:37
  51.4 1.4 %collective-permute-start.16 = (bf16[128,640]{1,0:T(8,128)(2,1)S(1)}, bf16[128,640]{1,0:T(8,128)(2,1)S(1)}, u32[]{:S(2)}, u32[]{:S(2)}) collective-permute-start(bf16[128,640]{1,0:T(8,128)(2,1)S(1)} %add_convert_fusion.1.refs_0_.piece0), channel_id=1, source_target_pairs={{0,48},{1,13},{16,0},{17,29},{32,16},{33,45},{48,32},{49,61},{4,52... | collective-permute-start | bytes 491528 | tf_op jit(solution)/shard_map/ppermute | solution.py:37
  52.9 0.9 %apply_native.1.refs_4_.before = f32[768,512]{1,0:T(8,128)S(1)} custom-call(bf16[192,1024]{1,0:T(8,128)(2,1)S(1)} %get-tuple-element.37.refs_0_, bf16[192,1024]{1,0:T(8,128)(2,1)S(1)} %collective-permute-done.2.refs_1_, bf16[192,1024]{1,0:T(8,128)(2,1)S(1)} %collective-permute-done.3.refs_2_, bf16[192,1024]{1,0:T(8,128)(2,1)S(1)} %collective-permute-done.4.refs_3_.pack, ...), custom_call_target="tpu_custom_call" | custom-call | flops 503316480 | bytes 4194304 | tf_op jit(solution)/shard_map/apply_native/pallas_call | solution.py:308
  53.8 2.1 %collective-permute-done.15.refs_2_.piece2 = bf16[128,640]{1,0:T(8,128)(2,1)S(1)} collective-permute-done((bf16[128,640]{1,0:T(8,128)(2,1)S(1)}, bf16[128,640]{1,0:T(8,128)(2,1)S(1)}, u32[]{:S(2)}, u32[]{:S(2)}) %collective-permute-start.15) | collective-permute-done | bytes 163872 | tf_op jit(solution)/shard_map/ppermute | solution.py:37
  55.9 0.7 apply_early.1
  56.6 0.4 apply_sent.1
  57.1 2.6 %collective-permute-start.27 = (bf16[192,512]{1,0:T(8,128)(2,1)S(1)}, bf16[192,512]{1,0:T(8,128)(2,1)S(1)}, u32[]{:S(2)}, u32[]{:S(2)}) collective-permute-start(bf16[192,512]{1,0:T(8,128)(2,1)S(1)} %get-tuple-element.57), channel_id=1, source_target_pairs={{0,8},{1,65},{16,24},{17,81},{32,40},{33,97},{48,56},{49,113},{4,1... | collective-permute-start | bytes 589832 | tf_op jit(solution)/shard_map/ppermute | solution.py:37
  59.6 0.8 %collective-permute-start.26 = (bf16[192,512]{1,0:T(8,128)(2,1)S(1)}, bf16[192,512]{1,0:T(8,128)(2,1)S(1)}, u32[]{:S(2)}, u32[]{:S(2)}) collective-permute-start(bf16[192,512]{1,0:T(8,128)(2,1)S(1)} %get-tuple-element.56), channel_id=1, source_target_pairs={{0,12},{1,67},{16,28},{17,83},{32,44},{33,99},{48,60},{49,115},{4,... | collective-permute-start | bytes 589832 | tf_op jit(solution)/shard_map/ppermute | solution.py:37
  60.4 0.4 apply_kept.1
  60.8 2.0 %collective-permute-done.28 = bf16[192,512]{1,0:T(8,128)(2,1)S(1)} collective-permute-done((bf16[192,512]{1,0:T(8,128)(2,1)S(1)}, bf16[192,512]{1,0:T(8,128)(2,1)S(1)}, u32[]{:S(2)}, u32[]{:S(2)}) %collective-permute-start.28) | collective-permute-done | bytes 196640 | tf_op jit(solution)/shard_map/ppermute | solution.py:37
  62.8 2.1 %collective-permute-done.27 = bf16[192,512]{1,0:T(8,128)(2,1)S(1)} collective-permute-done((bf16[192,512]{1,0:T(8,128)(2,1)S(1)}, bf16[192,512]{1,0:T(8,128)(2,1)S(1)}, u32[]{:S(2)}, u32[]{:S(2)}) %collective-permute-start.27) | collective-permute-done | bytes 196640 | tf_op jit(solution)/shard_map/ppermute | solution.py:37
  64.9 0.6 collective-permute-done.26
  65.7 6.7 %collective-permute-start.29 = (f32[192]{0:T(256)S(1)}, f32[192]{0:T(256)S(1)}, u32[]{:S(2)}, u32[]{:S(2)}) collective-permute-start(f32[192]{0:T(256)S(1)} %fusion.5), channel_id=1, source_target_pairs={{0,1},{1,0},{2,3},{3,2},{4,5},{5,4},{6,7},{7,6},{8,9},{9,8},{10,11... | collective-permute-start | bytes 2312 | tf_op jit(solution)/shard_map/ppermute | solution.py:41
  72.5 0.7 collective-permute-done.29
  73.2 0.9 %fusion.7 = f32[192,512]{1,0:T(8,128)} fusion(f32[192]{0:T(256)S(1)} %reduce, f32[192]{0:T(256)S(1)} %add.67, bf16[192,1024]{1,0:T(8,128)(2,1)S(1)} %get-tuple-element.37.refs_0_, bf16[192,512]{1,0:T(8,128)(2,1)S(1)} %collective-permute-done.28, bf16[192,512]{1,0:T(8,128)(2,1)S(1)} %collective-permute-done.27, ...), kind=kLoop, calls=%fused_computation.10 | loop fusion | flops 1277952 | bytes 1574400 | tf_op jit(solution)/shard_map/mul | solution.py:343
  (34 shorter events, 2.4 us)
Async XLA Ops:
  0.0 3.8 %collective-permute-start.1 = (bf16[192,2048]{1,0:T(8,128)(2,1)}, bf16[192,2048]{1,0:T(8,128)(2,1)S(1)}, u32[]{:S(2)}, u32[]{:S(2)}) collective-permute-start(bf16[192,2048]{1,0:T(8,128)(2,1)} %t_own.3), channel_id=1, source_target_pairs={{0,1},{1,0},{2,3},{3,2},{4,5},{5,4},{6,7},{7,6},{8,9},{9,8},{10,11... | collective-permute-start | bytes 2359304 | tf_op jit(solution)/shard_map/ppermute | solution.py:41
  1.4 2.4 %collective-permute-start = (bf16[192,512]{1,0:T(8,128)(2,1)}, bf16[192,512]{1,0:T(8,128)(2,1)S(1)}, u32[]{:S(2)}, u32[]{:S(2)}) collective-permute-start(bf16[192,512]{1,0:T(8,128)(2,1)} %s_own.3), channel_id=1, source_target_pairs={{0,1},{1,0},{2,3},{3,2},{4,5},{5,4},{6,7},{7,6},{8,9},{9,8},{10,11... | collective-permute-start | bytes 589832 | tf_op jit(solution)/shard_map/ppermute | solution.py:41
  1.4 1.1 %copy-start = (bf16[192,2048]{1,0:T(8,128)(2,1)S(1)}, bf16[192,2048]{1,0:T(8,128)(2,1)}, u32[]{:S(2)}) copy-start(bf16[192,2048]{1,0:T(8,128)(2,1)} %t_own.3) | copy-start | bytes 2359300
  2.6 0.9 %copy-start.1 = (bf16[192,512]{1,0:T(8,128)(2,1)S(1)}, bf16[192,512]{1,0:T(8,128)(2,1)}, u32[]{:S(2)}) copy-start(bf16[192,512]{1,0:T(8,128)(2,1)} %s_own.3) | copy-start | bytes 589828
  4.3 8.2 %collective-permute-start.2 = (bf16[192,1024]{1,0:T(8,128)(2,1)S(1)}, bf16[192,1024]{1,0:T(8,128)(2,1)S(1)}, u32[]{:S(2)}, u32[]{:S(2)}) collective-permute-start(bf16[192,1024]{1,0:T(8,128)(2,1)S(1)} %get-tuple-element.38), channel_id=1, source_target_pairs={{0,4},{1,3},{16,20},{17,19},{32,36},{33,35},{48,52},{49,51},{4,8},... | collective-permute-start | bytes 1179656 | tf_op jit(solution)/shard_map/ppermute | solution.py:37
  5.7 12.2 %collective-permute-start.3 = (bf16[192,1024]{1,0:T(8,128)(2,1)S(1)}, bf16[192,1024]{1,0:T(8,128)(2,1)S(1)}, u32[]{:S(2)}, u32[]{:S(2)}) collective-permute-start(bf16[192,1024]{1,0:T(8,128)(2,1)S(1)} %get-tuple-element.39), channel_id=1, source_target_pairs={{0,8},{1,65},{16,24},{17,81},{32,40},{33,97},{48,56},{49,113},{4,1... | collective-permute-start | bytes 1179656 | tf_op jit(solution)/shard_map/ppermute | solution.py:37
  8.1 10.7 %collective-permute-start.4 = (bf16[192,1024]{1,0:T(8,128)(2,1)S(1)}, bf16[192,1024]{1,0:T(8,128)(2,1)S(1)}, u32[]{:S(2)}, u32[]{:S(2)}) collective-permute-start(bf16[192,1024]{1,0:T(8,128)(2,1)S(1)} %get-tuple-element.40), channel_id=1, source_target_pairs={{0,12},{1,67},{16,28},{17,83},{32,44},{33,99},{48,60},{49,115},{4,... | collective-permute-start | bytes 1179656 | tf_op jit(solution)/shard_map/ppermute | solution.py:37
  9.6 13.6 %collective-permute-start.5 = (bf16[192,640]{1,0:T(8,128)(2,1)S(1)}, bf16[192,640]{1,0:T(8,128)(2,1)S(1)}, u32[]{:S(2)}, u32[]{:S(2)}) collective-permute-start(bf16[192,640]{1,0:T(8,128)(2,1)S(1)} %get-tuple-element.41), channel_id=1, source_target_pairs={{0,4},{1,3},{16,20},{17,19},{32,36},{33,35},{48,52},{49,51},{4,8},... | collective-permute-start | bytes 737288 | tf_op jit(solution)/shard_map/ppermute | solution.py:37
  10.0 13.9 %collective-permute-start.6 = (bf16[192,640]{1,0:T(8,128)(2,1)S(1)}, bf16[192,640]{1,0:T(8,128)(2,1)S(1)}, u32[]{:S(2)}, u32[]{:S(2)}) collective-permute-start(bf16[192,640]{1,0:T(8,128)(2,1)S(1)} %get-tuple-element.42), channel_id=1, source_target_pairs={{0,8},{1,65},{16,24},{17,81},{32,40},{33,97},{48,56},{49,113},{4,1... | collective-permute-start | bytes 737288 | tf_op jit(solution)/shard_map/ppermute | solution.py:37
  12.5 11.3 %collective-permute-start.7 = (bf16[192,640]{1,0:T(8,128)(2,1)S(1)}, bf16[192,640]{1,0:T(8,128)(2,1)S(1)}, u32[]{:S(2)}, u32[]{:S(2)}) collective-permute-start(bf16[192,640]{1,0:T(8,128)(2,1)S(1)} %get-tuple-element.43), channel_id=1, source_target_pairs={{0,12},{1,67},{16,28},{17,83},{32,44},{33,99},{48,60},{49,115},{4,... | collective-permute-start | bytes 737288 | tf_op jit(solution)/shard_map/ppermute | solution.py:37
  19.3 8.4 %collective-permute-start.19 = (bf16[128,640]{1,0:T(8,128)(2,1)S(1)}, bf16[128,640]{1,0:T(8,128)(2,1)S(1)}, u32[]{:S(2)}, u32[]{:S(2)}) collective-permute-start(bf16[128,640]{1,0:T(8,128)(2,1)S(1)} %get-tuple-element.51), channel_id=1, source_target_pairs={{0,66},{1,49},{16,82},{17,1},{32,98},{33,17},{48,114},{49,33},{4,7... | collective-permute-start | bytes 491528 | tf_op jit(solution)/shard_map/ppermute | solution.py:37
  23.2 6.0 %collective-permute-start.18 = (bf16[128,640]{1,0:T(8,128)(2,1)S(1)}, bf16[128,640]{1,0:T(8,128)(2,1)S(1)}, u32[]{:S(2)}, u32[]{:S(2)}) collective-permute-start(bf16[128,640]{1,0:T(8,128)(2,1)S(1)} %get-tuple-element.50), channel_id=1, source_target_pairs={{0,64},{1,33},{16,80},{17,49},{32,96},{33,1},{48,112},{49,17},{4,6... | collective-permute-start | bytes 491528 | tf_op jit(solution)/shard_map/ppermute | solution.py:37
  23.2 7.4 %collective-permute-start.17 = (bf16[128,640]{1,0:T(8,128)(2,1)S(1)}, bf16[128,640]{1,0:T(8,128)(2,1)S(1)}, u32[]{:S(2)}, u32[]{:S(2)}) collective-permute-start(bf16[128,640]{1,0:T(8,128)(2,1)S(1)} %get-tuple-element.49), channel_id=1, source_target_pairs={{0,2},{1,17},{16,18},{17,33},{32,34},{33,49},{48,50},{49,1},{4,6},... | collective-permute-start | bytes 491528 | tf_op jit(solution)/shard_map/ppermute | solution.py:37
  24.8 8.8 %collective-permute-start.10 = (bf16[128,640]{1,0:T(8,128)(2,1)S(1)}, bf16[128,640]{1,0:T(8,128)(2,1)S(1)}, u32[]{:S(2)}, u32[]{:S(2)}) collective-permute-start(bf16[128,640]{1,0:T(8,128)(2,1)S(1)} %get-tuple-element.47), channel_id=1, source_target_pairs={{0,48},{1,13},{16,0},{17,29},{32,16},{33,45},{48,32},{49,61},{4,52... | collective-permute-start | bytes 491528 | tf_op jit(solution)/shard_map/ppermute | solution.py:37
  27.4 6.9 %collective-permute-start.9 = (bf16[128,640]{1,0:T(8,128)(2,1)S(1)}, bf16[128,640]{1,0:T(8,128)(2,1)S(1)}, u32[]{:S(2)}, u32[]{:S(2)}) collective-permute-start(bf16[128,640]{1,0:T(8,128)(2,1)S(1)} %get-tuple-element.46), channel_id=1, source_target_pairs={{0,32},{1,9},{16,48},{17,25},{32,0},{33,41},{48,16},{49,57},{4,36}... | collective-permute-start | bytes 491528 | tf_op jit(solution)/shard_map/ppermute | solution.py:37
  27.7 7.4 %collective-permute-start.8 = (bf16[128,640]{1,0:T(8,128)(2,1)S(1)}, bf16[128,640]{1,0:T(8,128)(2,1)S(1)}, u32[]{:S(2)}, u32[]{:S(2)}) collective-permute-start(bf16[128,640]{1,0:T(8,128)(2,1)S(1)} %get-tuple-element.45), channel_id=1, source_target_pairs={{0,16},{1,5},{16,32},{17,21},{32,48},{33,37},{48,0},{49,53},{4,20}... | collective-permute-start | bytes 491528 | tf_op jit(solution)/shard_map/ppermute | solution.py:37
  30.7 8.0 %collective-permute-start.22 = (bf16[128,640]{1,0:T(8,128)(2,1)S(1)}, bf16[128,640]{1,0:T(8,128)(2,1)S(1)}, u32[]{:S(2)}, u32[]{:S(2)}) collective-permute-start(bf16[128,640]{1,0:T(8,128)(2,1)S(1)} %fusion.9), channel_id=1, source_target_pairs={{0,48},{1,13},{16,0},{17,29},{32,16},{33,45},{48,32},{49,61},{4,52... | collective-permute-start | bytes 491528 | tf_op jit(solution)/shard_map/ppermute | solution.py:37
  33.0 5.9 %collective-permute-start.21 = (bf16[128,640]{1,0:T(8,128)(2,1)S(1)}, bf16[128,640]{1,0:T(8,128)(2,1)S(1)}, u32[]{:S(2)}, u32[]{:S(2)}) collective-permute-start(bf16[128,640]{1,0:T(8,128)(2,1)S(1)} %fusion.9), channel_id=1, source_target_pairs={{0,32},{1,9},{16,48},{17,25},{32,0},{33,41},{48,16},{49,57},{4,36}... | collective-permute-start | bytes 491528 | tf_op jit(solution)/shard_map/ppermute | solution.py:37
  33.6 6.9 %collective-permute-start.20 = (bf16[128,640]{1,0:T(8,128)(2,1)S(1)}, bf16[128,640]{1,0:T(8,128)(2,1)S(1)}, u32[]{:S(2)}, u32[]{:S(2)}) collective-permute-start(bf16[128,640]{1,0:T(8,128)(2,1)S(1)} %fusion.9), channel_id=1, source_target_pairs={{0,16},{1,5},{16,32},{17,21},{32,48},{33,37},{48,0},{49,53},{4,20}... | collective-permute-start | bytes 491528 | tf_op jit(solution)/shard_map/ppermute | solution.py:37
  35.2 9.0 %collective-permute-start.13 = (bf16[128,640]{1,0:T(8,128)(2,1)S(1)}, bf16[128,640]{1,0:T(8,128)(2,1)S(1)}, u32[]{:S(2)}, u32[]{:S(2)}) collective-permute-start(bf16[128,640]{1,0:T(8,128)(2,1)S(1)} %fusion.8), channel_id=1, source_target_pairs={{0,66},{1,49},{16,82},{17,1},{32,98},{33,17},{48,114},{49,33},{4,7... | collective-permute-start | bytes 491528 | tf_op jit(solution)/shard_map/ppermute | solution.py:37
  38.3 9.4 %collective-permute-start.12 = (bf16[128,640]{1,0:T(8,128)(2,1)S(1)}, bf16[128,640]{1,0:T(8,128)(2,1)S(1)}, u32[]{:S(2)}, u32[]{:S(2)}) collective-permute-start(bf16[128,640]{1,0:T(8,128)(2,1)S(1)} %fusion.8), channel_id=1, source_target_pairs={{0,64},{1,33},{16,80},{17,49},{32,96},{33,1},{48,112},{49,17},{4,6... | collective-permute-start | bytes 491528 | tf_op jit(solution)/shard_map/ppermute | solution.py:37
  38.7 9.2 %collective-permute-start.11 = (bf16[128,640]{1,0:T(8,128)(2,1)S(1)}, bf16[128,640]{1,0:T(8,128)(2,1)S(1)}, u32[]{:S(2)}, u32[]{:S(2)}) collective-permute-start(bf16[128,640]{1,0:T(8,128)(2,1)S(1)} %fusion.8), channel_id=1, source_target_pairs={{0,2},{1,17},{16,18},{17,33},{32,34},{33,49},{48,50},{49,1},{4,6},... | collective-permute-start | bytes 491528 | tf_op jit(solution)/shard_map/ppermute | solution.py:37
  40.6 10.8 %collective-permute-start.23 = (bf16[128,640]{1,0:T(8,128)(2,1)S(1)}, bf16[128,640]{1,0:T(8,128)(2,1)S(1)}, u32[]{:S(2)}, u32[]{:S(2)}) collective-permute-start(bf16[128,640]{1,0:T(8,128)(2,1)S(1)} %add_convert_fusion.refs_4_), channel_id=1, source_target_pairs={{0,2},{1,17},{16,18},{17,33},{32,34},{33,49},{48,50},{49,1},{4,6},... | collective-permute-start | bytes 491528 | tf_op jit(solution)/shard_map/ppermute | solution.py:37
  41.2 11.7 %collective-permute-start.24 = (bf16[128,640]{1,0:T(8,128)(2,1)S(1)}, bf16[128,640]{1,0:T(8,128)(2,1)S(1)}, u32[]{:S(2)}, u32[]{:S(2)}) collective-permute-start(bf16[128,640]{1,0:T(8,128)(2,1)S(1)} %add_convert_fusion.refs_4_), channel_id=1, source_target_pairs={{0,64},{1,33},{16,80},{17,49},{32,96},{33,1},{48,112},{49,17},{4,6... | collective-permute-start | bytes 491528 | tf_op jit(solution)/shard_map/ppermute | solution.py:37
  44.2 8.6 %collective-permute-start.25 = (bf16[128,640]{1,0:T(8,128)(2,1)S(1)}, bf16[128,640]{1,0:T(8,128)(2,1)S(1)}, u32[]{:S(2)}, u32[]{:S(2)}) collective-permute-start(bf16[128,640]{1,0:T(8,128)(2,1)S(1)} %add_convert_fusion.refs_4_), channel_id=1, source_target_pairs={{0,66},{1,49},{16,82},{17,1},{32,98},{33,17},{48,114},{49,33},{4,7... | collective-permute-start | bytes 491528 | tf_op jit(solution)/shard_map/ppermute | solution.py:37
  48.1 5.7 %collective-permute-start.14 = (bf16[128,640]{1,0:T(8,128)(2,1)S(1)}, bf16[128,640]{1,0:T(8,128)(2,1)S(1)}, u32[]{:S(2)}, u32[]{:S(2)}) collective-permute-start(bf16[128,640]{1,0:T(8,128)(2,1)S(1)} %add_convert_fusion.1.refs_0_.piece0), channel_id=1, source_target_pairs={{0,16},{1,5},{16,32},{17,21},{32,48},{33,37},{48,0},{49,53},{4,20}... | collective-permute-start | bytes 491528 | tf_op jit(solution)/shard_map/ppermute | solution.py:37
  49.9 6.0 %collective-permute-start.15 = (bf16[128,640]{1,0:T(8,128)(2,1)S(1)}, bf16[128,640]{1,0:T(8,128)(2,1)S(1)}, u32[]{:S(2)}, u32[]{:S(2)}) collective-permute-start(bf16[128,640]{1,0:T(8,128)(2,1)S(1)} %add_convert_fusion.1.refs_0_.piece0), channel_id=1, source_target_pairs={{0,32},{1,9},{16,48},{17,25},{32,0},{33,41},{48,16},{49,57},{4,36}... | collective-permute-start | bytes 491528 | tf_op jit(solution)/shard_map/ppermute | solution.py:37
  51.4 5.2 %collective-permute-start.16 = (bf16[128,640]{1,0:T(8,128)(2,1)S(1)}, bf16[128,640]{1,0:T(8,128)(2,1)S(1)}, u32[]{:S(2)}, u32[]{:S(2)}) collective-permute-start(bf16[128,640]{1,0:T(8,128)(2,1)S(1)} %add_convert_fusion.1.refs_0_.piece0), channel_id=1, source_target_pairs={{0,48},{1,13},{16,0},{17,29},{32,16},{33,45},{48,32},{49,61},{4,52... | collective-permute-start | bytes 491528 | tf_op jit(solution)/shard_map/ppermute | solution.py:37
  57.0 5.8 %collective-permute-start.28 = (bf16[192,512]{1,0:T(8,128)(2,1)S(1)}, bf16[192,512]{1,0:T(8,128)(2,1)S(1)}, u32[]{:S(2)}, u32[]{:S(2)}) collective-permute-start(bf16[192,512]{1,0:T(8,128)(2,1)S(1)} %get-tuple-element.58), channel_id=1, source_target_pairs={{0,4},{1,3},{16,20},{17,19},{32,36},{33,35},{48,52},{49,51},{4,8},... | collective-permute-start | bytes 589832 | tf_op jit(solution)/shard_map/ppermute | solution.py:37
  57.1 7.8 %collective-permute-start.27 = (bf16[192,512]{1,0:T(8,128)(2,1)S(1)}, bf16[192,512]{1,0:T(8,128)(2,1)S(1)}, u32[]{:S(2)}, u32[]{:S(2)}) collective-permute-start(bf16[192,512]{1,0:T(8,128)(2,1)S(1)} %get-tuple-element.57), channel_id=1, source_target_pairs={{0,8},{1,65},{16,24},{17,81},{32,40},{33,97},{48,56},{49,113},{4,1... | collective-permute-start | bytes 589832 | tf_op jit(solution)/shard_map/ppermute | solution.py:37
  59.6 5.9 %collective-permute-start.26 = (bf16[192,512]{1,0:T(8,128)(2,1)S(1)}, bf16[192,512]{1,0:T(8,128)(2,1)S(1)}, u32[]{:S(2)}, u32[]{:S(2)}) collective-permute-start(bf16[192,512]{1,0:T(8,128)(2,1)S(1)} %get-tuple-element.56), channel_id=1, source_target_pairs={{0,12},{1,67},{16,28},{17,83},{32,44},{33,99},{48,60},{49,115},{4,... | collective-permute-start | bytes 589832 | tf_op jit(solution)/shard_map/ppermute | solution.py:37
  65.7 7.5 %collective-permute-start.29 = (f32[192]{0:T(256)S(1)}, f32[192]{0:T(256)S(1)}, u32[]{:S(2)}, u32[]{:S(2)}) collective-permute-start(f32[192]{0:T(256)S(1)} %fusion.5), channel_id=1, source_target_pairs={{0,1},{1,0},{2,3},{3,2},{4,5},{5,4},{6,7},{7,6},{8,9},{9,8},{10,11... | collective-permute-start | bytes 2312 | tf_op jit(solution)/shard_map/ppermute | solution.py:41

commit v12 on v11

--- a/solution.py
+++ b/solution.py
@@ -154,12 +154,19 @@
     emit(before[...] + cross(left, right), outs)
 
 
-def gram_far_kernel(*refs):
-    places = places_here()
-    norms, packs, outs = refs[:SIZE], refs[SIZE : 2 * SIZE], refs[2 * SIZE : 3 * SIZE]
-    left, right = refs[3 * SIZE :]
-    stack(places, 1, norms, packs, left, right)
-    emit(cross(left, right), outs)
+def gram_far_early_kernel(*refs):
+    places = places_here()
+    count = len(refs) // 2 - 1
+    product, left, right = refs[2 * count :]
+    stack(places, 1, refs[:count], refs[count : 2 * count], left, right)
+    product[...] = cross(left, right)
+
+
+def gram_far_kernel(norm, pack, before, *refs):
+    places = places_here()
+    outs, (left, right) = refs[:SIZE], refs[SIZE:]
+    stack(places, 1, [norm], [pack], left, right)
+    emit(before[...] + cross(left, right), outs)
 
 
 def gather_weights(place, pieces, weights):
@@ -259,9 +266,6 @@
         shapes(*[((rows, half + ts), BF16)] * SIZE, *[((rows, 1), F32)] * 2),
         6,
     )(student, s_far, teacher, t_far, ssq_s, ssq_t)
-    far = kernel_call(
-        pack_far_kernel, "pack_far", shapes(*[((rows, feats), BF16)] * SIZE), 4
-    )(s_far, t_far, inv_s, inv_t)
     norm_own = near[0][:, :half]
 
     def exchanged(own, sent, axis_of_core, sign=1):
@@ -274,6 +278,10 @@
         return total
 
     near = exchanged(near[0], near.__getitem__, GATHER)
+    near[1], t_far = lax.optimization_barrier((near[1], t_far))
+    far = kernel_call(
+        pack_far_kernel, "pack_far", shapes(*[((rows, feats), BF16)] * SIZE), 4
+    )(s_far, t_far, inv_s, inv_t)
     far = exchanged(far[0], far.__getitem__, GATHER)
 
     blocks = shapes(((ss, feats), F32), *[((ss, feats), BF16)] * 3)
@@ -292,9 +300,12 @@
     near_blocks = kernel_call(
         gram_native_kernel, "gram_native", blocks, 2, operands(1), flops // 4
     )(near[3], early)
+    early = kernel_call(
+        gram_far_early_kernel, "gram_far_early", shapes(((half, feats), F32)), 6, operands(3), flops
+    )(*near[:3], *far[:3])[0]
     far_blocks = kernel_call(
-        gram_far_kernel, "gram_far", blocks, 2 * SIZE, operands(SIZE), flops
-    )(*near, *far)
+        gram_far_kernel, "gram_far", blocks, 3, operands(1), flops // 4
+    )(near[3], far[3], early)
 
     def weights_of(chunk, own, *sends):
         total = added(own, lambda by: sends[by - 1], FIRST[chunk])

time: 74.3 us -> 81.3 us (1.094)
  starting transfers between devices: 45.5 us -> 50.2 us
  waiting for transfers between devices: 19 us -> 20.2 us
    ppermute x3, starting transfers between devices: 8.09 us -> 12.1 us  [other_core(): return lax.ppermute(array, 'sec', [(0, 1), (1, 0)])]
    ppermute x27, waiting for transfers between devices: 18.2 us -> 19.5 us  [shifted(): return lax.ppermute(array, AXES, pairs)]
  transfers between devices with their start and end apart: 30 -> 30, of which waited for: 15 -> 11; matrix products, arithmetic and copies ran while one was open for 1% -> 1% of each run, Pallas kernels for 7% -> 7%
where the time goes in v12:
time: 81.3 us; the launch traced here: 80.6 us
  starting transfers between devices  50.2 us (62%)
  waiting for transfers between devices  20.2 us (25%)
  Pallas kernels  6.21 us (8%)
  local copies, waits for them, and re-layouts  2.06 us (3%)
  other arithmetic  1.7 us (2%)
    ppermute x27, starting transfers between devices, shifted(): return lax.ppermute(array, AXES, pairs)  38.1 us
    ppermute x27, waiting for transfers between devices, shifted(): return lax.ppermute(array, AXES, pairs)  19.5 us
    ppermute x3, starting transfers between devices, other_core(): return lax.ppermute(array, 'sec', [(0, 1), (1, 0)])  12.1 us
    unnamed x4, local copies, waits for them, and re-layouts  2.06 us
  transfers between devices with their start and end apart: 30, of which 11 were waited for; matrix products, arithmetic and copies ran while one was open for 1% of the time, Pallas kernels for 7%

profile of v12, /device:TPU:1, one launch (start us, length us, event | category | flops | bytes accessed | tf_op | source)
XLA Modules:
  0.0 80.6 jit_solution(17185120673378859100)
XLA Ops:
  0.0 1.4 %collective-permute-start.1 = (bf16[192,2048]{1,0:T(8,128)(2,1)}, bf16[192,2048]{1,0:T(8,128)(2,1)S(1)}, u32[]{:S(2)}, u32[]{:S(2)}) collective-permute-start(bf16[192,2048]{1,0:T(8,128)(2,1)} %t_own.3), channel_id=1, source_target_pairs={{0,1},{1,0},{2,3},{3,2},{4,5},{5,4},{6,7},{7,6},{8,9},{9,8},{10,11... | collective-permute-start | bytes 2359304 | tf_op jit(solution)/shard_map/ppermute | solution.py:41
  1.4 1.1 %copy-done = bf16[192,2048]{1,0:T(8,128)(2,1)S(1)} copy-done((bf16[192,2048]{1,0:T(8,128)(2,1)S(1)}, bf16[192,2048]{1,0:T(8,128)(2,1)}, u32[]{:S(2)}) %copy-start) | copy-done | bytes 786456
  2.6 0.9 %copy-done.1 = bf16[192,512]{1,0:T(8,128)(2,1)S(1)} copy-done((bf16[192,512]{1,0:T(8,128)(2,1)S(1)}, bf16[192,512]{1,0:T(8,128)(2,1)}, u32[]{:S(2)}) %copy-start.1) | copy-done | bytes 196632
  3.8 0.5 pack_own.1
  4.3 1.4 %collective-permute-start.2 = (bf16[192,1024]{1,0:T(8,128)(2,1)S(1)}, bf16[192,1024]{1,0:T(8,128)(2,1)S(1)}, u32[]{:S(2)}, u32[]{:S(2)}) collective-permute-start(bf16[192,1024]{1,0:T(8,128)(2,1)S(1)} %get-tuple-element.36), channel_id=1, source_target_pairs={{0,4},{1,3},{16,20},{17,19},{32,36},{33,35},{48,52},{49,51},{4,8},... | collective-permute-start | bytes 1179656 | tf_op jit(solution)/shard_map/ppermute | solution.py:37
  5.7 2.5 %collective-permute-start.5 = (bf16[192,1024]{1,0:T(8,128)(2,1)S(1)}, bf16[192,1024]{1,0:T(8,128)(2,1)S(1)}, u32[]{:S(2)}, u32[]{:S(2)}) collective-permute-start(bf16[192,1024]{1,0:T(8,128)(2,1)S(1)} %get-tuple-element.45), channel_id=1, source_target_pairs={{0,8},{1,65},{16,24},{17,81},{32,40},{33,97},{48,56},{49,113},{4,1... | collective-permute-start | bytes 1179656 | tf_op jit(solution)/shard_map/ppermute | solution.py:37
  8.1 1.2 %collective-permute-start.3 = (bf16[192,1024]{1,0:T(8,128)(2,1)S(1)}, bf16[192,1024]{1,0:T(8,128)(2,1)S(1)}, u32[]{:S(2)}, u32[]{:S(2)}) collective-permute-start(bf16[192,1024]{1,0:T(8,128)(2,1)S(1)} %get-tuple-element.41), channel_id=1, source_target_pairs={{0,12},{1,67},{16,28},{17,83},{32,44},{33,99},{48,60},{49,115},{4,... | collective-permute-start | bytes 1179656 | tf_op jit(solution)/shard_map/ppermute | solution.py:37
  9.3 3.2 %collective-permute-done.2.refs_1_ = bf16[192,1024]{1,0:T(8,128)(2,1)S(1)} collective-permute-done((bf16[192,1024]{1,0:T(8,128)(2,1)S(1)}, bf16[192,1024]{1,0:T(8,128)(2,1)S(1)}, u32[]{:S(2)}, u32[]{:S(2)}) %collective-permute-start.2) | collective-permute-done | bytes 393248 | tf_op jit(solution)/shard_map/ppermute | solution.py:37
  12.5 0.3 pack_far.1
  13.0 2.5 %collective-permute-start.7 = (bf16[192,640]{1,0:T(8,128)(2,1)S(1)}, bf16[192,640]{1,0:T(8,128)(2,1)S(1)}, u32[]{:S(2)}, u32[]{:S(2)}) collective-permute-start(bf16[192,640]{1,0:T(8,128)(2,1)S(1)} %get-tuple-element.47), channel_id=1, source_target_pairs={{0,8},{1,65},{16,24},{17,81},{32,40},{33,97},{48,56},{49,113},{4,1... | collective-permute-start | bytes 737288 | tf_op jit(solution)/shard_map/ppermute | solution.py:37
  15.4 1.2 %collective-permute-start.4 = (bf16[192,640]{1,0:T(8,128)(2,1)S(1)}, bf16[192,640]{1,0:T(8,128)(2,1)S(1)}, u32[]{:S(2)}, u32[]{:S(2)}) collective-permute-start(bf16[192,640]{1,0:T(8,128)(2,1)S(1)} %get-tuple-element.42), channel_id=1, source_target_pairs={{0,12},{1,67},{16,28},{17,83},{32,44},{33,99},{48,60},{49,115},{4,... | collective-permute-start | bytes 737288 | tf_op jit(solution)/shard_map/ppermute | solution.py:37
  16.6 1.2 %collective-permute-done.5.refs_2_ = bf16[192,1024]{1,0:T(8,128)(2,1)S(1)} collective-permute-done((bf16[192,1024]{1,0:T(8,128)(2,1)S(1)}, bf16[192,1024]{1,0:T(8,128)(2,1)S(1)}, u32[]{:S(2)}, u32[]{:S(2)}) %collective-permute-start.5) | collective-permute-done | bytes 393248 | tf_op jit(solution)/shard_map/ppermute | solution.py:37
  17.8 1.0 %gram_early.1.before = f32[512,640]{1,0:T(8,128)S(1)} custom-call(bf16[192,1024]{1,0:T(8,128)(2,1)S(1)} %get-tuple-element.43.refs_0_, bf16[192,1024]{1,0:T(8,128)(2,1)S(1)} %collective-permute-done.2.refs_1_, bf16[192,1024]{1,0:T(8,128)(2,1)S(1)} %collective-permute-done.5.refs_2_), custom_call_target="tpu_custom_call" | custom-call | flops 503316480 | bytes 4194304 | tf_op jit(solution)/shard_map/gram_early/pallas_call | solution.py:292
  18.8 0.5 gram_native.1
  19.3 3.8 %collective-permute-start.19 = (bf16[128,640]{1,0:T(8,128)(2,1)S(1)}, bf16[128,640]{1,0:T(8,128)(2,1)S(1)}, u32[]{:S(2)}, u32[]{:S(2)}) collective-permute-start(bf16[128,640]{1,0:T(8,128)(2,1)S(1)} %get-tuple-element.55), channel_id=1, source_target_pairs={{0,66},{1,49},{16,82},{17,1},{32,98},{33,17},{48,114},{49,33},{4,7... | collective-permute-start | bytes 491528 | tf_op jit(solution)/shard_map/ppermute | solution.py:37
  23.1 0.7 collective-permute-start.17
  23.8 0.9 %gram_far_early.1.before = f32[512,640]{1,0:T(8,128)S(1)} custom-call(bf16[192,1024]{1,0:T(8,128)(2,1)S(1)} %get-tuple-element.43.refs_0_, bf16[192,1024]{1,0:T(8,128)(2,1)S(1)} %collective-permute-done.2.refs_1_, bf16[192,1024]{1,0:T(8,128)(2,1)S(1)} %collective-permute-done.5.refs_2_, bf16[192,640]{1,0:T(8,128)(2,1)S(1)} %get-tuple-element.40.refs_3_.pack, ...), custom_call_target="tpu_custom_call" | custom-call | flops 503316480 | bytes 4194304 | tf_op jit(solution)/shard_map/gram_far_early/pallas_call | solution.py:303
  24.7 0.5 gram_far.1
  25.2 2.6 %collective-permute-start.10 = (bf16[128,640]{1,0:T(8,128)(2,1)S(1)}, bf16[128,640]{1,0:T(8,128)(2,1)S(1)}, u32[]{:S(2)}, u32[]{:S(2)}) collective-permute-start(bf16[128,640]{1,0:T(8,128)(2,1)S(1)} %get-tuple-element.51), channel_id=1, source_target_pairs={{0,48},{1,13},{16,0},{17,29},{32,16},{33,45},{48,32},{49,61},{4,52... | collective-permute-start | bytes 491528 | tf_op jit(solution)/shard_map/ppermute | solution.py:37
  27.8 0.4 collective-permute-start.9
  28.1 0.7 collective-permute-start.8
  28.9 1.4 %collective-permute-done.17 = bf16[128,640]{1,0:T(8,128)(2,1)S(1)} collective-permute-done((bf16[128,640]{1,0:T(8,128)(2,1)S(1)}, bf16[128,640]{1,0:T(8,128)(2,1)S(1)}, u32[]{:S(2)}, u32[]{:S(2)}) %collective-permute-start.17) | collective-permute-done | bytes 163872 | tf_op jit(solution)/shard_map/ppermute | solution.py:37
  30.3 2.9 %collective-permute-start.22 = (bf16[128,640]{1,0:T(8,128)(2,1)S(1)}, bf16[128,640]{1,0:T(8,128)(2,1)S(1)}, u32[]{:S(2)}, u32[]{:S(2)}) collective-permute-start(bf16[128,640]{1,0:T(8,128)(2,1)S(1)} %fusion.9), channel_id=1, source_target_pairs={{0,48},{1,13},{16,0},{17,29},{32,16},{33,45},{48,32},{49,61},{4,52... | collective-permute-start | bytes 491528 | tf_op jit(solution)/shard_map/ppermute | solution.py:37
  33.2 0.4 collective-permute-start.21
  33.6 0.4 collective-permute-start.20
  34.0 1.5 %collective-permute-done.8 = bf16[128,640]{1,0:T(8,128)(2,1)S(1)} collective-permute-done((bf16[128,640]{1,0:T(8,128)(2,1)S(1)}, bf16[128,640]{1,0:T(8,128)(2,1)S(1)}, u32[]{:S(2)}, u32[]{:S(2)}) %collective-permute-start.8) | collective-permute-done | bytes 163872 | tf_op jit(solution)/shard_map/ppermute | solution.py:37
  35.6 3.0 %collective-permute-start.13 = (bf16[128,640]{1,0:T(8,128)(2,1)S(1)}, bf16[128,640]{1,0:T(8,128)(2,1)S(1)}, u32[]{:S(2)}, u32[]{:S(2)}) collective-permute-start(bf16[128,640]{1,0:T(8,128)(2,1)S(1)} %fusion.8), channel_id=1, source_target_pairs={{0,66},{1,49},{16,82},{17,1},{32,98},{33,17},{48,114},{49,33},{4,7... | collective-permute-start | bytes 491528 | tf_op jit(solution)/shard_map/ppermute | solution.py:37
  38.6 0.5 collective-permute-start.12
  39.3 1.6 %collective-permute-done.20 = bf16[128,640]{1,0:T(8,128)(2,1)S(1)} collective-permute-done((bf16[128,640]{1,0:T(8,128)(2,1)S(1)}, bf16[128,640]{1,0:T(8,128)(2,1)S(1)}, u32[]{:S(2)}, u32[]{:S(2)}) %collective-permute-start.20) | collective-permute-done | bytes 163872 | tf_op jit(solution)/shard_map/ppermute | solution.py:37
  41.1 0.4 collective-permute-start.23
  41.5 2.0 %collective-permute-start.24 = (bf16[128,640]{1,0:T(8,128)(2,1)S(1)}, bf16[128,640]{1,0:T(8,128)(2,1)S(1)}, u32[]{:S(2)}, u32[]{:S(2)}) collective-permute-start(bf16[128,640]{1,0:T(8,128)(2,1)S(1)} %add_convert_fusion.refs_4_), channel_id=1, source_target_pairs={{0,64},{1,33},{16,80},{17,49},{32,96},{33,1},{48,112},{49,17},{4,6... | collective-permute-start | bytes 491528 | tf_op jit(solution)/shard_map/ppermute | solution.py:37
  43.6 1.1 %collective-permute-start.25 = (bf16[128,640]{1,0:T(8,128)(2,1)S(1)}, bf16[128,640]{1,0:T(8,128)(2,1)S(1)}, u32[]{:S(2)}, u32[]{:S(2)}) collective-permute-start(bf16[128,640]{1,0:T(8,128)(2,1)S(1)} %add_convert_fusion.refs_4_), channel_id=1, source_target_pairs={{0,66},{1,49},{16,82},{17,1},{32,98},{33,17},{48,114},{49,33},{4,7... | collective-permute-start | bytes 491528 | tf_op jit(solution)/shard_map/ppermute | solution.py:37
  44.6 5.1 %collective-permute-done.11 = bf16[128,640]{1,0:T(8,128)(2,1)S(1)} collective-permute-done((bf16[128,640]{1,0:T(8,128)(2,1)S(1)}, bf16[128,640]{1,0:T(8,128)(2,1)S(1)}, u32[]{:S(2)}, u32[]{:S(2)}) %collective-permute-start.11) | collective-permute-done | bytes 163872 | tf_op jit(solution)/shard_map/ppermute | solution.py:37
  50.2 3.1 %collective-permute-start.15 = (bf16[128,640]{1,0:T(8,128)(2,1)S(1)}, bf16[128,640]{1,0:T(8,128)(2,1)S(1)}, u32[]{:S(2)}, u32[]{:S(2)}) collective-permute-start(bf16[128,640]{1,0:T(8,128)(2,1)S(1)} %add_convert_fusion.1.refs_0_.piece0), channel_id=1, source_target_pairs={{0,32},{1,9},{16,48},{17,25},{32,0},{33,41},{48,16},{49,57},{4,36}... | collective-permute-start | bytes 491528 | tf_op jit(solution)/shard_map/ppermute | solution.py:37
  53.3 2.0 %collective-permute-start.16 = (bf16[128,640]{1,0:T(8,128)(2,1)S(1)}, bf16[128,640]{1,0:T(8,128)(2,1)S(1)}, u32[]{:S(2)}, u32[]{:S(2)}) collective-permute-start(bf16[128,640]{1,0:T(8,128)(2,1)S(1)} %add_convert_fusion.1.refs_0_.piece0), channel_id=1, source_target_pairs={{0,48},{1,13},{16,0},{17,29},{32,16},{33,45},{48,32},{49,61},{4,52... | collective-permute-start | bytes 491528 | tf_op jit(solution)/shard_map/ppermute | solution.py:37
  55.3 0.9 %apply_native.1.refs_4_.before = f32[768,512]{1,0:T(8,128)S(1)} custom-call(bf16[192,1024]{1,0:T(8,128)(2,1)S(1)} %get-tuple-element.43.refs_0_, bf16[192,1024]{1,0:T(8,128)(2,1)S(1)} %collective-permute-done.2.refs_1_, bf16[192,1024]{1,0:T(8,128)(2,1)S(1)} %collective-permute-done.5.refs_2_, bf16[192,1024]{1,0:T(8,128)(2,1)S(1)} %collective-permute-done.3.norm.pack.refs_3_, ...), custom_call_target="tpu_custom_call" | custom-call | flops 503316480 | bytes 4194304 | tf_op jit(solution)/shard_map/apply_native/pallas_call | solution.py:319
  56.2 1.5 %collective-permute-done.15.refs_2_.piece2 = bf16[128,640]{1,0:T(8,128)(2,1)S(1)} collective-permute-done((bf16[128,640]{1,0:T(8,128)(2,1)S(1)}, bf16[128,640]{1,0:T(8,128)(2,1)S(1)}, u32[]{:S(2)}, u32[]{:S(2)}) %collective-permute-start.15) | collective-permute-done | bytes 163872 | tf_op jit(solution)/shard_map/ppermute | solution.py:37
  57.7 0.7 apply_early.1
  58.4 0.4 apply_sent.1
  58.8 2.3 %collective-permute-start.28 = (bf16[192,512]{1,0:T(8,128)(2,1)S(1)}, bf16[192,512]{1,0:T(8,128)(2,1)S(1)}, u32[]{:S(2)}, u32[]{:S(2)}) collective-permute-start(bf16[192,512]{1,0:T(8,128)(2,1)S(1)} %get-tuple-element.62), channel_id=1, source_target_pairs={{0,4},{1,3},{16,20},{17,19},{32,36},{33,35},{48,52},{49,51},{4,8},... | collective-permute-start | bytes 589832 | tf_op jit(solution)/shard_map/ppermute | solution.py:37
  61.0 1.7 %collective-permute-start.27 = (bf16[192,512]{1,0:T(8,128)(2,1)S(1)}, bf16[192,512]{1,0:T(8,128)(2,1)S(1)}, u32[]{:S(2)}, u32[]{:S(2)}) collective-permute-start(bf16[192,512]{1,0:T(8,128)(2,1)S(1)} %get-tuple-element.61), channel_id=1, source_target_pairs={{0,8},{1,65},{16,24},{17,81},{32,40},{33,97},{48,56},{49,113},{4,1... | collective-permute-start | bytes 589832 | tf_op jit(solution)/shard_map/ppermute | solution.py:37
  62.7 0.9 %collective-permute-start.26 = (bf16[192,512]{1,0:T(8,128)(2,1)S(1)}, bf16[192,512]{1,0:T(8,128)(2,1)S(1)}, u32[]{:S(2)}, u32[]{:S(2)}) collective-permute-start(bf16[192,512]{1,0:T(8,128)(2,1)S(1)} %get-tuple-element.60), channel_id=1, source_target_pairs={{0,12},{1,67},{16,28},{17,83},{32,44},{33,99},{48,60},{49,115},{4,... | collective-permute-start | bytes 589832 | tf_op jit(solution)/shard_map/ppermute | solution.py:37
  63.6 0.4 apply_kept.1
  64.1 0.8 collective-permute-done.28
  64.9 3.0 %collective-permute-done.27 = bf16[192,512]{1,0:T(8,128)(2,1)S(1)} collective-permute-done((bf16[192,512]{1,0:T(8,128)(2,1)S(1)}, bf16[192,512]{1,0:T(8,128)(2,1)S(1)}, u32[]{:S(2)}, u32[]{:S(2)}) %collective-permute-start.27) | collective-permute-done | bytes 196640 | tf_op jit(solution)/shard_map/ppermute | solution.py:37
  68.1 10.7 %collective-permute-start.29 = (f32[192]{0:T(256)S(1)}, f32[192]{0:T(256)S(1)}, u32[]{:S(2)}, u32[]{:S(2)}) collective-permute-start(f32[192]{0:T(256)S(1)} %fusion.5), channel_id=1, source_target_pairs={{0,1},{1,0},{2,3},{3,2},{4,5},{5,4},{6,7},{7,6},{8,9},{9,8},{10,11... | collective-permute-start | bytes 2312 | tf_op jit(solution)/shard_map/ppermute | solution.py:41
  78.9 0.7 collective-permute-done.29
  79.7 0.9 %fusion.7 = f32[192,512]{1,0:T(8,128)} fusion(f32[192]{0:T(256)S(1)} %reduce, f32[192]{0:T(256)S(1)} %add.67, bf16[192,1024]{1,0:T(8,128)(2,1)S(1)} %get-tuple-element.43.refs_0_, bf16[192,512]{1,0:T(8,128)(2,1)S(1)} %collective-permute-done.28, bf16[192,512]{1,0:T(8,128)(2,1)S(1)} %collective-permute-done.27, ...), kind=kLoop, calls=%fused_computation.10 | loop fusion | flops 1277952 | bytes 1574400 | tf_op jit(solution)/shard_map/mul | solution.py:354
  (35 shorter events, 1.8 us)
Async XLA Ops:
  0.0 3.8 %collective-permute-start.1 = (bf16[192,2048]{1,0:T(8,128)(2,1)}, bf16[192,2048]{1,0:T(8,128)(2,1)S(1)}, u32[]{:S(2)}, u32[]{:S(2)}) collective-permute-start(bf16[192,2048]{1,0:T(8,128)(2,1)} %t_own.3), channel_id=1, source_target_pairs={{0,1},{1,0},{2,3},{3,2},{4,5},{5,4},{6,7},{7,6},{8,9},{9,8},{10,11... | collective-permute-start | bytes 2359304 | tf_op jit(solution)/shard_map/ppermute | solution.py:41
  1.4 2.4 %collective-permute-start = (bf16[192,512]{1,0:T(8,128)(2,1)}, bf16[192,512]{1,0:T(8,128)(2,1)S(1)}, u32[]{:S(2)}, u32[]{:S(2)}) collective-permute-start(bf16[192,512]{1,0:T(8,128)(2,1)} %s_own.3), channel_id=1, source_target_pairs={{0,1},{1,0},{2,3},{3,2},{4,5},{5,4},{6,7},{7,6},{8,9},{9,8},{10,11... | collective-permute-start | bytes 589832 | tf_op jit(solution)/shard_map/ppermute | solution.py:41
  1.4 1.1 %copy-start = (bf16[192,2048]{1,0:T(8,128)(2,1)S(1)}, bf16[192,2048]{1,0:T(8,128)(2,1)}, u32[]{:S(2)}) copy-start(bf16[192,2048]{1,0:T(8,128)(2,1)} %t_own.3) | copy-start | bytes 2359300
  2.6 0.9 %copy-start.1 = (bf16[192,512]{1,0:T(8,128)(2,1)S(1)}, bf16[192,512]{1,0:T(8,128)(2,1)}, u32[]{:S(2)}) copy-start(bf16[192,512]{1,0:T(8,128)(2,1)} %s_own.3) | copy-start | bytes 589828
  4.3 8.2 %collective-permute-start.2 = (bf16[192,1024]{1,0:T(8,128)(2,1)S(1)}, bf16[192,1024]{1,0:T(8,128)(2,1)S(1)}, u32[]{:S(2)}, u32[]{:S(2)}) collective-permute-start(bf16[192,1024]{1,0:T(8,128)(2,1)S(1)} %get-tuple-element.36), channel_id=1, source_target_pairs={{0,4},{1,3},{16,20},{17,19},{32,36},{33,35},{48,52},{49,51},{4,8},... | collective-permute-start | bytes 1179656 | tf_op jit(solution)/shard_map/ppermute | solution.py:37
  5.7 12.1 %collective-permute-start.5 = (bf16[192,1024]{1,0:T(8,128)(2,1)S(1)}, bf16[192,1024]{1,0:T(8,128)(2,1)S(1)}, u32[]{:S(2)}, u32[]{:S(2)}) collective-permute-start(bf16[192,1024]{1,0:T(8,128)(2,1)S(1)} %get-tuple-element.45), channel_id=1, source_target_pairs={{0,8},{1,65},{16,24},{17,81},{32,40},{33,97},{48,56},{49,113},{4,1... | collective-permute-start | bytes 1179656 | tf_op jit(solution)/shard_map/ppermute | solution.py:37
  8.1 10.7 %collective-permute-start.3 = (bf16[192,1024]{1,0:T(8,128)(2,1)S(1)}, bf16[192,1024]{1,0:T(8,128)(2,1)S(1)}, u32[]{:S(2)}, u32[]{:S(2)}) collective-permute-start(bf16[192,1024]{1,0:T(8,128)(2,1)S(1)} %get-tuple-element.41), channel_id=1, source_target_pairs={{0,12},{1,67},{16,28},{17,83},{32,44},{33,99},{48,60},{49,115},{4,... | collective-permute-start | bytes 1179656 | tf_op jit(solution)/shard_map/ppermute | solution.py:37
  12.8 10.3 %collective-permute-start.6 = (bf16[192,640]{1,0:T(8,128)(2,1)S(1)}, bf16[192,640]{1,0:T(8,128)(2,1)S(1)}, u32[]{:S(2)}, u32[]{:S(2)}) collective-permute-start(bf16[192,640]{1,0:T(8,128)(2,1)S(1)} %get-tuple-element.46), channel_id=1, source_target_pairs={{0,4},{1,3},{16,20},{17,19},{32,36},{33,35},{48,52},{49,51},{4,8},... | collective-permute-start | bytes 737288 | tf_op jit(solution)/shard_map/ppermute | solution.py:37
  13.0 10.8 %collective-permute-start.7 = (bf16[192,640]{1,0:T(8,128)(2,1)S(1)}, bf16[192,640]{1,0:T(8,128)(2,1)S(1)}, u32[]{:S(2)}, u32[]{:S(2)}) collective-permute-start(bf16[192,640]{1,0:T(8,128)(2,1)S(1)} %get-tuple-element.47), channel_id=1, source_target_pairs={{0,8},{1,65},{16,24},{17,81},{32,40},{33,97},{48,56},{49,113},{4,1... | collective-permute-start | bytes 737288 | tf_op jit(solution)/shard_map/ppermute | solution.py:37
  15.4 9.3 %collective-permute-start.4 = (bf16[192,640]{1,0:T(8,128)(2,1)S(1)}, bf16[192,640]{1,0:T(8,128)(2,1)S(1)}, u32[]{:S(2)}, u32[]{:S(2)}) collective-permute-start(bf16[192,640]{1,0:T(8,128)(2,1)S(1)} %get-tuple-element.42), channel_id=1, source_target_pairs={{0,12},{1,67},{16,28},{17,83},{32,44},{33,99},{48,60},{49,115},{4,... | collective-permute-start | bytes 737288 | tf_op jit(solution)/shard_map/ppermute | solution.py:37
  19.3 8.9 %collective-permute-start.19 = (bf16[128,640]{1,0:T(8,128)(2,1)S(1)}, bf16[128,640]{1,0:T(8,128)(2,1)S(1)}, u32[]{:S(2)}, u32[]{:S(2)}) collective-permute-start(bf16[128,640]{1,0:T(8,128)(2,1)S(1)} %get-tuple-element.55), channel_id=1, source_target_pairs={{0,66},{1,49},{16,82},{17,1},{32,98},{33,17},{48,114},{49,33},{4,7... | collective-permute-start | bytes 491528 | tf_op jit(solution)/shard_map/ppermute | solution.py:37
  23.1 5.8 %collective-permute-start.18 = (bf16[128,640]{1,0:T(8,128)(2,1)S(1)}, bf16[128,640]{1,0:T(8,128)(2,1)S(1)}, u32[]{:S(2)}, u32[]{:S(2)}) collective-permute-start(bf16[128,640]{1,0:T(8,128)(2,1)S(1)} %get-tuple-element.54), channel_id=1, source_target_pairs={{0,64},{1,33},{16,80},{17,49},{32,96},{33,1},{48,112},{49,17},{4,6... | collective-permute-start | bytes 491528 | tf_op jit(solution)/shard_map/ppermute | solution.py:37
  23.1 7.1 %collective-permute-start.17 = (bf16[128,640]{1,0:T(8,128)(2,1)S(1)}, bf16[128,640]{1,0:T(8,128)(2,1)S(1)}, u32[]{:S(2)}, u32[]{:S(2)}) collective-permute-start(bf16[128,640]{1,0:T(8,128)(2,1)S(1)} %get-tuple-element.53), channel_id=1, source_target_pairs={{0,2},{1,17},{16,18},{17,33},{32,34},{33,49},{48,50},{49,1},{4,6},... | collective-permute-start | bytes 491528 | tf_op jit(solution)/shard_map/ppermute | solution.py:37
  25.2 8.4 %collective-permute-start.10 = (bf16[128,640]{1,0:T(8,128)(2,1)S(1)}, bf16[128,640]{1,0:T(8,128)(2,1)S(1)}, u32[]{:S(2)}, u32[]{:S(2)}) collective-permute-start(bf16[128,640]{1,0:T(8,128)(2,1)S(1)} %get-tuple-element.51), channel_id=1, source_target_pairs={{0,48},{1,13},{16,0},{17,29},{32,16},{33,45},{48,32},{49,61},{4,52... | collective-permute-start | bytes 491528 | tf_op jit(solution)/shard_map/ppermute | solution.py:37
  27.8 6.2 %collective-permute-start.9 = (bf16[128,640]{1,0:T(8,128)(2,1)S(1)}, bf16[128,640]{1,0:T(8,128)(2,1)S(1)}, u32[]{:S(2)}, u32[]{:S(2)}) collective-permute-start(bf16[128,640]{1,0:T(8,128)(2,1)S(1)} %get-tuple-element.50), channel_id=1, source_target_pairs={{0,32},{1,9},{16,48},{17,25},{32,0},{33,41},{48,16},{49,57},{4,36}... | collective-permute-start | bytes 491528 | tf_op jit(solution)/shard_map/ppermute | solution.py:37
  28.1 7.4 %collective-permute-start.8 = (bf16[128,640]{1,0:T(8,128)(2,1)S(1)}, bf16[128,640]{1,0:T(8,128)(2,1)S(1)}, u32[]{:S(2)}, u32[]{:S(2)}) collective-permute-start(bf16[128,640]{1,0:T(8,128)(2,1)S(1)} %get-tuple-element.49), channel_id=1, source_target_pairs={{0,16},{1,5},{16,32},{17,21},{32,48},{33,37},{48,0},{49,53},{4,20}... | collective-permute-start | bytes 491528 | tf_op jit(solution)/shard_map/ppermute | solution.py:37
  30.3 8.8 %collective-permute-start.22 = (bf16[128,640]{1,0:T(8,128)(2,1)S(1)}, bf16[128,640]{1,0:T(8,128)(2,1)S(1)}, u32[]{:S(2)}, u32[]{:S(2)}) collective-permute-start(bf16[128,640]{1,0:T(8,128)(2,1)S(1)} %fusion.9), channel_id=1, source_target_pairs={{0,48},{1,13},{16,0},{17,29},{32,16},{33,45},{48,32},{49,61},{4,52... | collective-permute-start | bytes 491528 | tf_op jit(solution)/shard_map/ppermute | solution.py:37
  33.2 6.1 %collective-permute-start.21 = (bf16[128,640]{1,0:T(8,128)(2,1)S(1)}, bf16[128,640]{1,0:T(8,128)(2,1)S(1)}, u32[]{:S(2)}, u32[]{:S(2)}) collective-permute-start(bf16[128,640]{1,0:T(8,128)(2,1)S(1)} %fusion.9), channel_id=1, source_target_pairs={{0,32},{1,9},{16,48},{17,25},{32,0},{33,41},{48,16},{49,57},{4,36}... | collective-permute-start | bytes 491528 | tf_op jit(solution)/shard_map/ppermute | solution.py:37
  33.6 7.4 %collective-permute-start.20 = (bf16[128,640]{1,0:T(8,128)(2,1)S(1)}, bf16[128,640]{1,0:T(8,128)(2,1)S(1)}, u32[]{:S(2)}, u32[]{:S(2)}) collective-permute-start(bf16[128,640]{1,0:T(8,128)(2,1)S(1)} %fusion.9), channel_id=1, source_target_pairs={{0,16},{1,5},{16,32},{17,21},{32,48},{33,37},{48,0},{49,53},{4,20}... | collective-permute-start | bytes 491528 | tf_op jit(solution)/shard_map/ppermute | solution.py:37
  35.6 8.0 %collective-permute-start.13 = (bf16[128,640]{1,0:T(8,128)(2,1)S(1)}, bf16[128,640]{1,0:T(8,128)(2,1)S(1)}, u32[]{:S(2)}, u32[]{:S(2)}) collective-permute-start(bf16[128,640]{1,0:T(8,128)(2,1)S(1)} %fusion.8), channel_id=1, source_target_pairs={{0,66},{1,49},{16,82},{17,1},{32,98},{33,17},{48,114},{49,33},{4,7... | collective-permute-start | bytes 491528 | tf_op jit(solution)/shard_map/ppermute | solution.py:37
  38.6 6.0 %collective-permute-start.12 = (bf16[128,640]{1,0:T(8,128)(2,1)S(1)}, bf16[128,640]{1,0:T(8,128)(2,1)S(1)}, u32[]{:S(2)}, u32[]{:S(2)}) collective-permute-start(bf16[128,640]{1,0:T(8,128)(2,1)S(1)} %fusion.8), channel_id=1, source_target_pairs={{0,64},{1,33},{16,80},{17,49},{32,96},{33,1},{48,112},{49,17},{4,6... | collective-permute-start | bytes 491528 | tf_op jit(solution)/shard_map/ppermute | solution.py:37
  39.1 10.6 %collective-permute-start.11 = (bf16[128,640]{1,0:T(8,128)(2,1)S(1)}, bf16[128,640]{1,0:T(8,128)(2,1)S(1)}, u32[]{:S(2)}, u32[]{:S(2)}) collective-permute-start(bf16[128,640]{1,0:T(8,128)(2,1)S(1)} %fusion.8), channel_id=1, source_target_pairs={{0,2},{1,17},{16,18},{17,33},{32,34},{33,49},{48,50},{49,1},{4,6},... | collective-permute-start | bytes 491528 | tf_op jit(solution)/shard_map/ppermute | solution.py:37
  41.1 12.2 %collective-permute-start.23 = (bf16[128,640]{1,0:T(8,128)(2,1)S(1)}, bf16[128,640]{1,0:T(8,128)(2,1)S(1)}, u32[]{:S(2)}, u32[]{:S(2)}) collective-permute-start(bf16[128,640]{1,0:T(8,128)(2,1)S(1)} %add_convert_fusion.refs_4_), channel_id=1, source_target_pairs={{0,2},{1,17},{16,18},{17,33},{32,34},{33,49},{48,50},{49,1},{4,6},... | collective-permute-start | bytes 491528 | tf_op jit(solution)/shard_map/ppermute | solution.py:37
  41.5 13.8 %collective-permute-start.24 = (bf16[128,640]{1,0:T(8,128)(2,1)S(1)}, bf16[128,640]{1,0:T(8,128)(2,1)S(1)}, u32[]{:S(2)}, u32[]{:S(2)}) collective-permute-start(bf16[128,640]{1,0:T(8,128)(2,1)S(1)} %add_convert_fusion.refs_4_), channel_id=1, source_target_pairs={{0,64},{1,33},{16,80},{17,49},{32,96},{33,1},{48,112},{49,17},{4,6... | collective-permute-start | bytes 491528 | tf_op jit(solution)/shard_map/ppermute | solution.py:37
  43.6 11.7 %collective-permute-start.25 = (bf16[128,640]{1,0:T(8,128)(2,1)S(1)}, bf16[128,640]{1,0:T(8,128)(2,1)S(1)}, u32[]{:S(2)}, u32[]{:S(2)}) collective-permute-start(bf16[128,640]{1,0:T(8,128)(2,1)S(1)} %add_convert_fusion.refs_4_), channel_id=1, source_target_pairs={{0,66},{1,49},{16,82},{17,1},{32,98},{33,17},{48,114},{49,33},{4,7... | collective-permute-start | bytes 491528 | tf_op jit(solution)/shard_map/ppermute | solution.py:37
  49.9 6.2 %collective-permute-start.14 = (bf16[128,640]{1,0:T(8,128)(2,1)S(1)}, bf16[128,640]{1,0:T(8,128)(2,1)S(1)}, u32[]{:S(2)}, u32[]{:S(2)}) collective-permute-start(bf16[128,640]{1,0:T(8,128)(2,1)S(1)} %add_convert_fusion.1.refs_0_.piece0), channel_id=1, source_target_pairs={{0,16},{1,5},{16,32},{17,21},{32,48},{33,37},{48,0},{49,53},{4,20}... | collective-permute-start | bytes 491528 | tf_op jit(solution)/shard_map/ppermute | solution.py:37
  50.2 7.5 %collective-permute-start.15 = (bf16[128,640]{1,0:T(8,128)(2,1)S(1)}, bf16[128,640]{1,0:T(8,128)(2,1)S(1)}, u32[]{:S(2)}, u32[]{:S(2)}) collective-permute-start(bf16[128,640]{1,0:T(8,128)(2,1)S(1)} %add_convert_fusion.1.refs_0_.piece0), channel_id=1, source_target_pairs={{0,32},{1,9},{16,48},{17,25},{32,0},{33,41},{48,16},{49,57},{4,36}... | collective-permute-start | bytes 491528 | tf_op jit(solution)/shard_map/ppermute | solution.py:37
  53.3 5.1 %collective-permute-start.16 = (bf16[128,640]{1,0:T(8,128)(2,1)S(1)}, bf16[128,640]{1,0:T(8,128)(2,1)S(1)}, u32[]{:S(2)}, u32[]{:S(2)}) collective-permute-start(bf16[128,640]{1,0:T(8,128)(2,1)S(1)} %add_convert_fusion.1.refs_0_.piece0), channel_id=1, source_target_pairs={{0,48},{1,13},{16,0},{17,29},{32,16},{33,45},{48,32},{49,61},{4,52... | collective-permute-start | bytes 491528 | tf_op jit(solution)/shard_map/ppermute | solution.py:37
  58.8 6.1 %collective-permute-start.28 = (bf16[192,512]{1,0:T(8,128)(2,1)S(1)}, bf16[192,512]{1,0:T(8,128)(2,1)S(1)}, u32[]{:S(2)}, u32[]{:S(2)}) collective-permute-start(bf16[192,512]{1,0:T(8,128)(2,1)S(1)} %get-tuple-element.62), channel_id=1, source_target_pairs={{0,4},{1,3},{16,20},{17,19},{32,36},{33,35},{48,52},{49,51},{4,8},... | collective-permute-start | bytes 589832 | tf_op jit(solution)/shard_map/ppermute | solution.py:37
  61.0 6.8 %collective-permute-start.27 = (bf16[192,512]{1,0:T(8,128)(2,1)S(1)}, bf16[192,512]{1,0:T(8,128)(2,1)S(1)}, u32[]{:S(2)}, u32[]{:S(2)}) collective-permute-start(bf16[192,512]{1,0:T(8,128)(2,1)S(1)} %get-tuple-element.61), channel_id=1, source_target_pairs={{0,8},{1,65},{16,24},{17,81},{32,40},{33,97},{48,56},{49,113},{4,1... | collective-permute-start | bytes 589832 | tf_op jit(solution)/shard_map/ppermute | solution.py:37
  62.7 5.2 %collective-permute-start.26 = (bf16[192,512]{1,0:T(8,128)(2,1)S(1)}, bf16[192,512]{1,0:T(8,128)(2,1)S(1)}, u32[]{:S(2)}, u32[]{:S(2)}) collective-permute-start(bf16[192,512]{1,0:T(8,128)(2,1)S(1)} %get-tuple-element.60), channel_id=1, source_target_pairs={{0,12},{1,67},{16,28},{17,83},{32,44},{33,99},{48,60},{49,115},{4,... | collective-permute-start | bytes 589832 | tf_op jit(solution)/shard_map/ppermute | solution.py:37
  68.1 11.5 %collective-permute-start.29 = (f32[192]{0:T(256)S(1)}, f32[192]{0:T(256)S(1)}, u32[]{:S(2)}, u32[]{:S(2)}) collective-permute-start(f32[192]{0:T(256)S(1)} %fusion.5), channel_id=1, source_target_pairs={{0,1},{1,0},{2,3},{3,2},{4,5},{5,4},{6,7},{7,6},{8,9},{9,8},{10,11... | collective-permute-start | bytes 2312 | tf_op jit(solution)/shard_map/ppermute | solution.py:41

commit v13 on v12

--- a/solution.py
+++ b/solution.py
@@ -14,7 +14,7 @@
 GATHER = (Y, X)
 FIRST = ((X, Z), (Z, Y))
 SECOND = ((Z, Y), (X, Z))
-ORDER = (2, 1, 3)
+ORDER = (1, 3, 2)
 STRIP = 32
 PARAMS = pltpu.CompilerParams(vmem_limit_bytes=40 * 1024 * 1024)
 WHOLE = pl.BlockSpec(memory_space=pltpu.VMEM)
@@ -278,7 +278,6 @@
         return total
 
     near = exchanged(near[0], near.__getitem__, GATHER)
-    near[1], t_far = lax.optimization_barrier((near[1], t_far))
     far = kernel_call(
         pack_far_kernel, "pack_far", shapes(*[((rows, feats), BF16)] * SIZE), 4
     )(s_far, t_far, inv_s, inv_t)
@@ -289,6 +288,7 @@
     def operands(count):
         return [pltpu.VMEM((count * rows, half), BF16), pltpu.VMEM((count * rows, feats), BF16)]
 
+    first, last = (0, 1, 3), 2
     early = kernel_call(
         functools.partial(gram_early_kernel, level * SIZE / groups),
         "gram_early",
@@ -296,16 +296,16 @@
         3,
         operands(3),
         flops,
-    )(*near[:3])[0]
+    )(*[near[by] for by in first])[0]
     near_blocks = kernel_call(
         gram_native_kernel, "gram_native", blocks, 2, operands(1), flops // 4
-    )(near[3], early)
+    )(near[last], early)
     early = kernel_call(
         gram_far_early_kernel, "gram_far_early", shapes(((half, feats), F32)), 6, operands(3), flops
-    )(*near[:3], *far[:3])[0]
+    )(*[near[by] for by in first], *[far[by] for by in first])[0]
     far_blocks = kernel_call(
         gram_far_kernel, "gram_far", blocks, 3, operands(1), flops // 4
-    )(near[3], far[3], early)
+    )(near[last], far[last], early)
 
     def weights_of(chunk, own, *sends):
         total = added(own, lambda by: sends[by - 1], FIRST[chunk])

time: 81.3 us -> 77.1 us (0.948)
  starting transfers between devices: 50.2 us -> 45.8 us
    ppermute x3, starting transfers between devices: 12.1 us -> 9.44 us  [other_core(): return lax.ppermute(array, 'sec', [(0, 1), (1, 0)])]
    ppermute x27, starting transfers between devices: 38.1 us -> 36.4 us  [shifted(): return lax.ppermute(array, AXES, pairs)]
  transfers between devices with their start and end apart: 30 -> 30, of which waited for: 11 -> 12; matrix products, arithmetic and copies ran while one was open for 1% -> 1% of each run, Pallas kernels for 7% -> 7%
where the time goes in v13:
time: 77.1 us; the launch traced here: 76.9 us
  starting transfers between devices  45.8 us (59%)
  waiting for transfers between devices  21 us (27%)
  Pallas kernels  6.2 us (8%)
  local copies, waits for them, and re-layouts  2.06 us (3%)
  other arithmetic  1.7 us (2%)
    ppermute x27, starting transfers between devices, shifted(): return lax.ppermute(array, AXES, pairs)  36.4 us
    ppermute x27, waiting for transfers between devices, shifted(): return lax.ppermute(array, AXES, pairs)  20.2 us
    ppermute x3, starting transfers between devices, other_core(): return lax.ppermute(array, 'sec', [(0, 1), (1, 0)])  9.44 us
    unnamed x4, local copies, waits for them, and re-layouts  2.06 us
  transfers between devices with their start and end apart: 30, of which 12 were waited for; matrix products, arithmetic and copies ran while one was open for 1% of the time, Pallas kernels for 7%

profile of v13, /device:TPU:1, one launch (start us, length us, event | category | flops | bytes accessed | tf_op | source)
XLA Modules:
  0.0 76.9 jit_solution(6033302859361746472)
XLA Ops:
  0.0 1.4 %collective-permute-start.1 = (bf16[192,2048]{1,0:T(8,128)(2,1)}, bf16[192,2048]{1,0:T(8,128)(2,1)S(1)}, u32[]{:S(2)}, u32[]{:S(2)}) collective-permute-start(bf16[192,2048]{1,0:T(8,128)(2,1)} %t_own.3), channel_id=1, source_target_pairs={{0,1},{1,0},{2,3},{3,2},{4,5},{5,4},{6,7},{7,6},{8,9},{9,8},{10,11... | collective-permute-start | bytes 2359304 | tf_op jit(solution)/shard_map/ppermute | solution.py:41
  1.4 1.1 %copy-done = bf16[192,2048]{1,0:T(8,128)(2,1)S(1)} copy-done((bf16[192,2048]{1,0:T(8,128)(2,1)S(1)}, bf16[192,2048]{1,0:T(8,128)(2,1)}, u32[]{:S(2)}) %copy-start) | copy-done | bytes 786456
  2.6 0.9 %copy-done.1 = bf16[192,512]{1,0:T(8,128)(2,1)S(1)} copy-done((bf16[192,512]{1,0:T(8,128)(2,1)S(1)}, bf16[192,512]{1,0:T(8,128)(2,1)}, u32[]{:S(2)}) %copy-start.1) | copy-done | bytes 196632
  3.5 0.3 sums.1
  3.8 0.5 pack_own.1
  4.3 1.4 %collective-permute-start.4 = (bf16[192,1024]{1,0:T(8,128)(2,1)S(1)}, bf16[192,1024]{1,0:T(8,128)(2,1)S(1)}, u32[]{:S(2)}, u32[]{:S(2)}) collective-permute-start(bf16[192,1024]{1,0:T(8,128)(2,1)S(1)} %get-tuple-element.40), channel_id=1, source_target_pairs={{0,4},{1,3},{16,20},{17,19},{32,36},{33,35},{48,52},{49,51},{4,8},... | collective-permute-start | bytes 1179656 | tf_op jit(solution)/shard_map/ppermute | solution.py:37
  5.7 1.4 %collective-permute-start.5 = (bf16[192,1024]{1,0:T(8,128)(2,1)S(1)}, bf16[192,1024]{1,0:T(8,128)(2,1)S(1)}, u32[]{:S(2)}, u32[]{:S(2)}) collective-permute-start(bf16[192,1024]{1,0:T(8,128)(2,1)S(1)} %get-tuple-element.41), channel_id=1, source_target_pairs={{0,12},{1,67},{16,28},{17,83},{32,44},{33,99},{48,60},{49,115},{4,... | collective-permute-start | bytes 1179656 | tf_op jit(solution)/shard_map/ppermute | solution.py:37
  7.1 1.6 %collective-permute-start.2 = (bf16[192,1024]{1,0:T(8,128)(2,1)S(1)}, bf16[192,1024]{1,0:T(8,128)(2,1)S(1)}, u32[]{:S(2)}, u32[]{:S(2)}) collective-permute-start(bf16[192,1024]{1,0:T(8,128)(2,1)S(1)} %get-tuple-element.37), channel_id=1, source_target_pairs={{0,8},{1,65},{16,24},{17,81},{32,40},{33,97},{48,56},{49,113},{4,1... | collective-permute-start | bytes 1179656 | tf_op jit(solution)/shard_map/ppermute | solution.py:37
  8.7 0.3 pack_far.1
  9.0 0.4 collective-permute-start.6
  9.3 2.4 %collective-permute-start.7 = (bf16[192,640]{1,0:T(8,128)(2,1)S(1)}, bf16[192,640]{1,0:T(8,128)(2,1)S(1)}, u32[]{:S(2)}, u32[]{:S(2)}) collective-permute-start(bf16[192,640]{1,0:T(8,128)(2,1)S(1)} %get-tuple-element.43), channel_id=1, source_target_pairs={{0,12},{1,67},{16,28},{17,83},{32,44},{33,99},{48,60},{49,115},{4,... | collective-permute-start | bytes 737288 | tf_op jit(solution)/shard_map/ppermute | solution.py:37
  11.7 0.8 %collective-permute-done.4.refs_1_ = bf16[192,1024]{1,0:T(8,128)(2,1)S(1)} collective-permute-done((bf16[192,1024]{1,0:T(8,128)(2,1)S(1)}, bf16[192,1024]{1,0:T(8,128)(2,1)S(1)}, u32[]{:S(2)}, u32[]{:S(2)}) %collective-permute-start.4) | collective-permute-done | bytes 393248 | tf_op jit(solution)/shard_map/ppermute | solution.py:37
  12.5 1.6 %collective-permute-start.3 = (bf16[192,640]{1,0:T(8,128)(2,1)S(1)}, bf16[192,640]{1,0:T(8,128)(2,1)S(1)}, u32[]{:S(2)}, u32[]{:S(2)}) collective-permute-start(bf16[192,640]{1,0:T(8,128)(2,1)S(1)} %get-tuple-element.38), channel_id=1, source_target_pairs={{0,8},{1,65},{16,24},{17,81},{32,40},{33,97},{48,56},{49,113},{4,1... | collective-permute-start | bytes 737288 | tf_op jit(solution)/shard_map/ppermute | solution.py:37
  14.2 1.0 %gram_early.1.before = f32[512,640]{1,0:T(8,128)S(1)} custom-call(bf16[192,1024]{1,0:T(8,128)(2,1)S(1)} %get-tuple-element.39.refs_0_, bf16[192,1024]{1,0:T(8,128)(2,1)S(1)} %collective-permute-done.4.refs_1_, bf16[192,1024]{1,0:T(8,128)(2,1)S(1)} %collective-permute-done.5.refs_2_.refs_3_), custom_call_target="tpu_custom_call" | custom-call | flops 503316480 | bytes 4194304 | tf_op jit(solution)/shard_map/gram_early/pallas_call | solution.py:292
  15.1 2.7 %collective-permute-done.2.norm.pack.refs_2_ = bf16[192,1024]{1,0:T(8,128)(2,1)S(1)} collective-permute-done((bf16[192,1024]{1,0:T(8,128)(2,1)S(1)}, bf16[192,1024]{1,0:T(8,128)(2,1)S(1)}, u32[]{:S(2)}, u32[]{:S(2)}) %collective-permute-start.2) | collective-permute-done | bytes 393248 | tf_op jit(solution)/shard_map/ppermute | solution.py:37
  17.9 0.5 gram_native.1
  18.3 3.8 %collective-permute-start.19 = (bf16[128,640]{1,0:T(8,128)(2,1)S(1)}, bf16[128,640]{1,0:T(8,128)(2,1)S(1)}, u32[]{:S(2)}, u32[]{:S(2)}) collective-permute-start(bf16[128,640]{1,0:T(8,128)(2,1)S(1)} %get-tuple-element.51), channel_id=1, source_target_pairs={{0,66},{1,49},{16,82},{17,1},{32,98},{33,17},{48,114},{49,33},{4,7... | collective-permute-start | bytes 491528 | tf_op jit(solution)/shard_map/ppermute | solution.py:37
  22.2 0.7 collective-permute-start.17
  22.9 0.9 %gram_far_early.1.before = f32[512,640]{1,0:T(8,128)S(1)} custom-call(bf16[192,1024]{1,0:T(8,128)(2,1)S(1)} %get-tuple-element.39.refs_0_, bf16[192,1024]{1,0:T(8,128)(2,1)S(1)} %collective-permute-done.4.refs_1_, bf16[192,1024]{1,0:T(8,128)(2,1)S(1)} %collective-permute-done.5.refs_2_.refs_3_, bf16[192,640]{1,0:T(8,128)(2,1)S(1)} %get-tuple-element.36.refs_3_.pack, ...), custom_call_target="tpu_custom_call" | custom-call | flops 503316480 | bytes 4194304 | tf_op jit(solution)/shard_map/gram_far_early/pallas_call | solution.py:303
  23.8 0.5 gram_far.1
  24.2 2.7 %collective-permute-start.10 = (bf16[128,640]{1,0:T(8,128)(2,1)S(1)}, bf16[128,640]{1,0:T(8,128)(2,1)S(1)}, u32[]{:S(2)}, u32[]{:S(2)}) collective-permute-start(bf16[128,640]{1,0:T(8,128)(2,1)S(1)} %get-tuple-element.47), channel_id=1, source_target_pairs={{0,48},{1,13},{16,0},{17,29},{32,16},{33,45},{48,32},{49,61},{4,52... | collective-permute-start | bytes 491528 | tf_op jit(solution)/shard_map/ppermute | solution.py:37
  27.1 0.7 collective-permute-start.8
  27.9 1.7 %collective-permute-done.17 = bf16[128,640]{1,0:T(8,128)(2,1)S(1)} collective-permute-done((bf16[128,640]{1,0:T(8,128)(2,1)S(1)}, bf16[128,640]{1,0:T(8,128)(2,1)S(1)}, u32[]{:S(2)}, u32[]{:S(2)}) %collective-permute-start.17) | collective-permute-done | bytes 163872 | tf_op jit(solution)/shard_map/ppermute | solution.py:37
  29.7 2.7 %collective-permute-start.22 = (bf16[128,640]{1,0:T(8,128)(2,1)S(1)}, bf16[128,640]{1,0:T(8,128)(2,1)S(1)}, u32[]{:S(2)}, u32[]{:S(2)}) collective-permute-start(bf16[128,640]{1,0:T(8,128)(2,1)S(1)} %fusion.9), channel_id=1, source_target_pairs={{0,48},{1,13},{16,0},{17,29},{32,16},{33,45},{48,32},{49,61},{4,52... | collective-permute-start | bytes 491528 | tf_op jit(solution)/shard_map/ppermute | solution.py:37
  32.6 0.7 collective-permute-start.20
  33.3 1.0 %collective-permute-done.8 = bf16[128,640]{1,0:T(8,128)(2,1)S(1)} collective-permute-done((bf16[128,640]{1,0:T(8,128)(2,1)S(1)}, bf16[128,640]{1,0:T(8,128)(2,1)S(1)}, u32[]{:S(2)}, u32[]{:S(2)}) %collective-permute-start.8) | collective-permute-done | bytes 163872 | tf_op jit(solution)/shard_map/ppermute | solution.py:37
  34.4 3.4 %collective-permute-start.13 = (bf16[128,640]{1,0:T(8,128)(2,1)S(1)}, bf16[128,640]{1,0:T(8,128)(2,1)S(1)}, u32[]{:S(2)}, u32[]{:S(2)}) collective-permute-start(bf16[128,640]{1,0:T(8,128)(2,1)S(1)} %fusion.8), channel_id=1, source_target_pairs={{0,66},{1,49},{16,82},{17,1},{32,98},{33,17},{48,114},{49,33},{4,7... | collective-permute-start | bytes 491528 | tf_op jit(solution)/shard_map/ppermute | solution.py:37
  37.8 0.5 collective-permute-start.12
  38.5 1.3 %collective-permute-done.20 = bf16[128,640]{1,0:T(8,128)(2,1)S(1)} collective-permute-done((bf16[128,640]{1,0:T(8,128)(2,1)S(1)}, bf16[128,640]{1,0:T(8,128)(2,1)S(1)}, u32[]{:S(2)}, u32[]{:S(2)}) %collective-permute-start.20) | collective-permute-done | bytes 163872 | tf_op jit(solution)/shard_map/ppermute | solution.py:37
  39.9 0.8 %collective-permute-start.23 = (bf16[128,640]{1,0:T(8,128)(2,1)S(1)}, bf16[128,640]{1,0:T(8,128)(2,1)S(1)}, u32[]{:S(2)}, u32[]{:S(2)}) collective-permute-start(bf16[128,640]{1,0:T(8,128)(2,1)S(1)} %add_convert_fusion.refs_4_), channel_id=1, source_target_pairs={{0,2},{1,17},{16,18},{17,33},{32,34},{33,49},{48,50},{49,1},{4,6},... | collective-permute-start | bytes 491528 | tf_op jit(solution)/shard_map/ppermute | solution.py:37
  40.6 2.2 %collective-permute-start.24 = (bf16[128,640]{1,0:T(8,128)(2,1)S(1)}, bf16[128,640]{1,0:T(8,128)(2,1)S(1)}, u32[]{:S(2)}, u32[]{:S(2)}) collective-permute-start(bf16[128,640]{1,0:T(8,128)(2,1)S(1)} %add_convert_fusion.refs_4_), channel_id=1, source_target_pairs={{0,64},{1,33},{16,80},{17,49},{32,96},{33,1},{48,112},{49,17},{4,6... | collective-permute-start | bytes 491528 | tf_op jit(solution)/shard_map/ppermute | solution.py:37
  42.8 3.8 %collective-permute-done.13 = bf16[128,640]{1,0:T(8,128)(2,1)S(1)} collective-permute-done((bf16[128,640]{1,0:T(8,128)(2,1)S(1)}, bf16[128,640]{1,0:T(8,128)(2,1)S(1)}, u32[]{:S(2)}, u32[]{:S(2)}) %collective-permute-start.13) | collective-permute-done | bytes 163872 | tf_op jit(solution)/shard_map/ppermute | solution.py:37
  46.6 3.1 %collective-permute-start.25 = (bf16[128,640]{1,0:T(8,128)(2,1)S(1)}, bf16[128,640]{1,0:T(8,128)(2,1)S(1)}, u32[]{:S(2)}, u32[]{:S(2)}) collective-permute-start(bf16[128,640]{1,0:T(8,128)(2,1)S(1)} %add_convert_fusion.refs_4_), channel_id=1, source_target_pairs={{0,66},{1,49},{16,82},{17,1},{32,98},{33,17},{48,114},{49,33},{4,7... | collective-permute-start | bytes 491528 | tf_op jit(solution)/shard_map/ppermute | solution.py:37
  49.9 0.3 collective-permute-start.14
  50.2 2.4 %collective-permute-start.15 = (bf16[128,640]{1,0:T(8,128)(2,1)S(1)}, bf16[128,640]{1,0:T(8,128)(2,1)S(1)}, u32[]{:S(2)}, u32[]{:S(2)}) collective-permute-start(bf16[128,640]{1,0:T(8,128)(2,1)S(1)} %add_convert_fusion.1.refs_0_.piece0), channel_id=1, source_target_pairs={{0,32},{1,9},{16,48},{17,25},{32,0},{33,41},{48,16},{49,57},{4,36}... | collective-permute-start | bytes 491528 | tf_op jit(solution)/shard_map/ppermute | solution.py:37
  52.6 0.2 collective-permute-start.16
  52.8 0.9 %apply_native.1.refs_4_.before = f32[768,512]{1,0:T(8,128)S(1)} custom-call(bf16[192,1024]{1,0:T(8,128)(2,1)S(1)} %get-tuple-element.39.refs_0_, bf16[192,1024]{1,0:T(8,128)(2,1)S(1)} %collective-permute-done.4.refs_1_, bf16[192,1024]{1,0:T(8,128)(2,1)S(1)} %collective-permute-done.2.norm.pack.refs_2_, ...), custom_call_target="tpu_custom_call" | custom-call | flops 503316480 | bytes 4194304 | tf_op jit(solution)/shard_map/apply_native/pallas_call | solution.py:319
  53.7 3.6 %collective-permute-done.14.refs_1_.piece1 = bf16[128,640]{1,0:T(8,128)(2,1)S(1)} collective-permute-done((bf16[128,640]{1,0:T(8,128)(2,1)S(1)}, bf16[128,640]{1,0:T(8,128)(2,1)S(1)}, u32[]{:S(2)}, u32[]{:S(2)}) %collective-permute-start.14) | collective-permute-done | bytes 163872 | tf_op jit(solution)/shard_map/ppermute | solution.py:37
  57.3 0.7 apply_early.1
  58.0 0.4 apply_sent.1
  58.5 0.9 %collective-permute-start.27 = (bf16[192,512]{1,0:T(8,128)(2,1)S(1)}, bf16[192,512]{1,0:T(8,128)(2,1)S(1)}, u32[]{:S(2)}, u32[]{:S(2)}) collective-permute-start(bf16[192,512]{1,0:T(8,128)(2,1)S(1)} %get-tuple-element.57), channel_id=1, source_target_pairs={{0,8},{1,65},{16,24},{17,81},{32,40},{33,97},{48,56},{49,113},{4,1... | collective-permute-start | bytes 589832 | tf_op jit(solution)/shard_map/ppermute | solution.py:37
  59.3 1.9 %collective-permute-start.26 = (bf16[192,512]{1,0:T(8,128)(2,1)S(1)}, bf16[192,512]{1,0:T(8,128)(2,1)S(1)}, u32[]{:S(2)}, u32[]{:S(2)}) collective-permute-start(bf16[192,512]{1,0:T(8,128)(2,1)S(1)} %get-tuple-element.56), channel_id=1, source_target_pairs={{0,12},{1,67},{16,28},{17,83},{32,44},{33,99},{48,60},{49,115},{4,... | collective-permute-start | bytes 589832 | tf_op jit(solution)/shard_map/ppermute | solution.py:37
  61.2 0.4 apply_kept.1
  61.7 4.6 %collective-permute-done.28 = bf16[192,512]{1,0:T(8,128)(2,1)S(1)} collective-permute-done((bf16[192,512]{1,0:T(8,128)(2,1)S(1)}, bf16[192,512]{1,0:T(8,128)(2,1)S(1)}, u32[]{:S(2)}, u32[]{:S(2)}) %collective-permute-start.28) | collective-permute-done | bytes 196640 | tf_op jit(solution)/shard_map/ppermute | solution.py:37
  66.3 0.6 collective-permute-done.26
  67.1 8.0 %collective-permute-start.29 = (f32[192]{0:T(256)S(1)}, f32[192]{0:T(256)S(1)}, u32[]{:S(2)}, u32[]{:S(2)}) collective-permute-start(f32[192]{0:T(256)S(1)} %fusion.5), channel_id=1, source_target_pairs={{0,1},{1,0},{2,3},{3,2},{4,5},{5,4},{6,7},{7,6},{8,9},{9,8},{10,11... | collective-permute-start | bytes 2312 | tf_op jit(solution)/shard_map/ppermute | solution.py:41
  75.3 0.7 collective-permute-done.29
  76.0 0.9 %fusion.7 = f32[192,512]{1,0:T(8,128)} fusion(f32[192]{0:T(256)S(1)} %reduce, f32[192]{0:T(256)S(1)} %add.67, bf16[192,1024]{1,0:T(8,128)(2,1)S(1)} %get-tuple-element.39.refs_0_, bf16[192,512]{1,0:T(8,128)(2,1)S(1)} %collective-permute-done.28, bf16[192,512]{1,0:T(8,128)(2,1)S(1)} %collective-permute-done.27, ...), kind=kLoop, calls=%fused_computation.10 | loop fusion | flops 1277952 | bytes 1574400 | tf_op jit(solution)/shard_map/mul | solution.py:354
  (35 shorter events, 1.5 us)
Async XLA Ops:
  0.0 3.8 %collective-permute-start.1 = (bf16[192,2048]{1,0:T(8,128)(2,1)}, bf16[192,2048]{1,0:T(8,128)(2,1)S(1)}, u32[]{:S(2)}, u32[]{:S(2)}) collective-permute-start(bf16[192,2048]{1,0:T(8,128)(2,1)} %t_own.3), channel_id=1, source_target_pairs={{0,1},{1,0},{2,3},{3,2},{4,5},{5,4},{6,7},{7,6},{8,9},{9,8},{10,11... | collective-permute-start | bytes 2359304 | tf_op jit(solution)/shard_map/ppermute | solution.py:41
  1.4 2.4 %collective-permute-start = (bf16[192,512]{1,0:T(8,128)(2,1)}, bf16[192,512]{1,0:T(8,128)(2,1)S(1)}, u32[]{:S(2)}, u32[]{:S(2)}) collective-permute-start(bf16[192,512]{1,0:T(8,128)(2,1)} %s_own.3), channel_id=1, source_target_pairs={{0,1},{1,0},{2,3},{3,2},{4,5},{5,4},{6,7},{7,6},{8,9},{9,8},{10,11... | collective-permute-start | bytes 589832 | tf_op jit(solution)/shard_map/ppermute | solution.py:41
  1.4 1.1 %copy-start = (bf16[192,2048]{1,0:T(8,128)(2,1)S(1)}, bf16[192,2048]{1,0:T(8,128)(2,1)}, u32[]{:S(2)}) copy-start(bf16[192,2048]{1,0:T(8,128)(2,1)} %t_own.3) | copy-start | bytes 2359300
  2.6 0.9 %copy-start.1 = (bf16[192,512]{1,0:T(8,128)(2,1)S(1)}, bf16[192,512]{1,0:T(8,128)(2,1)}, u32[]{:S(2)}) copy-start(bf16[192,512]{1,0:T(8,128)(2,1)} %s_own.3) | copy-start | bytes 589828
  4.3 8.2 %collective-permute-start.4 = (bf16[192,1024]{1,0:T(8,128)(2,1)S(1)}, bf16[192,1024]{1,0:T(8,128)(2,1)S(1)}, u32[]{:S(2)}, u32[]{:S(2)}) collective-permute-start(bf16[192,1024]{1,0:T(8,128)(2,1)S(1)} %get-tuple-element.40), channel_id=1, source_target_pairs={{0,4},{1,3},{16,20},{17,19},{32,36},{33,35},{48,52},{49,51},{4,8},... | collective-permute-start | bytes 1179656 | tf_op jit(solution)/shard_map/ppermute | solution.py:37
  5.7 8.5 %collective-permute-start.5 = (bf16[192,1024]{1,0:T(8,128)(2,1)S(1)}, bf16[192,1024]{1,0:T(8,128)(2,1)S(1)}, u32[]{:S(2)}, u32[]{:S(2)}) collective-permute-start(bf16[192,1024]{1,0:T(8,128)(2,1)S(1)} %get-tuple-element.41), channel_id=1, source_target_pairs={{0,12},{1,67},{16,28},{17,83},{32,44},{33,99},{48,60},{49,115},{4,... | collective-permute-start | bytes 1179656 | tf_op jit(solution)/shard_map/ppermute | solution.py:37
  7.1 10.8 %collective-permute-start.2 = (bf16[192,1024]{1,0:T(8,128)(2,1)S(1)}, bf16[192,1024]{1,0:T(8,128)(2,1)S(1)}, u32[]{:S(2)}, u32[]{:S(2)}) collective-permute-start(bf16[192,1024]{1,0:T(8,128)(2,1)S(1)} %get-tuple-element.37), channel_id=1, source_target_pairs={{0,8},{1,65},{16,24},{17,81},{32,40},{33,97},{48,56},{49,113},{4,1... | collective-permute-start | bytes 1179656 | tf_op jit(solution)/shard_map/ppermute | solution.py:37
  9.0 13.2 %collective-permute-start.6 = (bf16[192,640]{1,0:T(8,128)(2,1)S(1)}, bf16[192,640]{1,0:T(8,128)(2,1)S(1)}, u32[]{:S(2)}, u32[]{:S(2)}) collective-permute-start(bf16[192,640]{1,0:T(8,128)(2,1)S(1)} %get-tuple-element.42), channel_id=1, source_target_pairs={{0,4},{1,3},{16,20},{17,19},{32,36},{33,35},{48,52},{49,51},{4,8},... | collective-permute-start | bytes 737288 | tf_op jit(solution)/shard_map/ppermute | solution.py:37
  9.3 13.5 %collective-permute-start.7 = (bf16[192,640]{1,0:T(8,128)(2,1)S(1)}, bf16[192,640]{1,0:T(8,128)(2,1)S(1)}, u32[]{:S(2)}, u32[]{:S(2)}) collective-permute-start(bf16[192,640]{1,0:T(8,128)(2,1)S(1)} %get-tuple-element.43), channel_id=1, source_target_pairs={{0,12},{1,67},{16,28},{17,83},{32,44},{33,99},{48,60},{49,115},{4,... | collective-permute-start | bytes 737288 | tf_op jit(solution)/shard_map/ppermute | solution.py:37
  12.5 11.2 %collective-permute-start.3 = (bf16[192,640]{1,0:T(8,128)(2,1)S(1)}, bf16[192,640]{1,0:T(8,128)(2,1)S(1)}, u32[]{:S(2)}, u32[]{:S(2)}) collective-permute-start(bf16[192,640]{1,0:T(8,128)(2,1)S(1)} %get-tuple-element.38), channel_id=1, source_target_pairs={{0,8},{1,65},{16,24},{17,81},{32,40},{33,97},{48,56},{49,113},{4,1... | collective-permute-start | bytes 737288 | tf_op jit(solution)/shard_map/ppermute | solution.py:37
  18.3 8.8 %collective-permute-start.19 = (bf16[128,640]{1,0:T(8,128)(2,1)S(1)}, bf16[128,640]{1,0:T(8,128)(2,1)S(1)}, u32[]{:S(2)}, u32[]{:S(2)}) collective-permute-start(bf16[128,640]{1,0:T(8,128)(2,1)S(1)} %get-tuple-element.51), channel_id=1, source_target_pairs={{0,66},{1,49},{16,82},{17,1},{32,98},{33,17},{48,114},{49,33},{4,7... | collective-permute-start | bytes 491528 | tf_op jit(solution)/shard_map/ppermute | solution.py:37
  22.1 5.8 %collective-permute-start.18 = (bf16[128,640]{1,0:T(8,128)(2,1)S(1)}, bf16[128,640]{1,0:T(8,128)(2,1)S(1)}, u32[]{:S(2)}, u32[]{:S(2)}) collective-permute-start(bf16[128,640]{1,0:T(8,128)(2,1)S(1)} %get-tuple-element.50), channel_id=1, source_target_pairs={{0,64},{1,33},{16,80},{17,49},{32,96},{33,1},{48,112},{49,17},{4,6... | collective-permute-start | bytes 491528 | tf_op jit(solution)/shard_map/ppermute | solution.py:37
  22.2 7.4 %collective-permute-start.17 = (bf16[128,640]{1,0:T(8,128)(2,1)S(1)}, bf16[128,640]{1,0:T(8,128)(2,1)S(1)}, u32[]{:S(2)}, u32[]{:S(2)}) collective-permute-start(bf16[128,640]{1,0:T(8,128)(2,1)S(1)} %get-tuple-element.49), channel_id=1, source_target_pairs={{0,2},{1,17},{16,18},{17,33},{32,34},{33,49},{48,50},{49,1},{4,6},... | collective-permute-start | bytes 491528 | tf_op jit(solution)/shard_map/ppermute | solution.py:37
  24.2 8.4 %collective-permute-start.10 = (bf16[128,640]{1,0:T(8,128)(2,1)S(1)}, bf16[128,640]{1,0:T(8,128)(2,1)S(1)}, u32[]{:S(2)}, u32[]{:S(2)}) collective-permute-start(bf16[128,640]{1,0:T(8,128)(2,1)S(1)} %get-tuple-element.47), channel_id=1, source_target_pairs={{0,48},{1,13},{16,0},{17,29},{32,16},{33,45},{48,32},{49,61},{4,52... | collective-permute-start | bytes 491528 | tf_op jit(solution)/shard_map/ppermute | solution.py:37
  27.0 6.3 %collective-permute-start.9 = (bf16[128,640]{1,0:T(8,128)(2,1)S(1)}, bf16[128,640]{1,0:T(8,128)(2,1)S(1)}, u32[]{:S(2)}, u32[]{:S(2)}) collective-permute-start(bf16[128,640]{1,0:T(8,128)(2,1)S(1)} %get-tuple-element.46), channel_id=1, source_target_pairs={{0,32},{1,9},{16,48},{17,25},{32,0},{33,41},{48,16},{49,57},{4,36}... | collective-permute-start | bytes 491528 | tf_op jit(solution)/shard_map/ppermute | solution.py:37
  27.1 7.1 %collective-permute-start.8 = (bf16[128,640]{1,0:T(8,128)(2,1)S(1)}, bf16[128,640]{1,0:T(8,128)(2,1)S(1)}, u32[]{:S(2)}, u32[]{:S(2)}) collective-permute-start(bf16[128,640]{1,0:T(8,128)(2,1)S(1)} %get-tuple-element.45), channel_id=1, source_target_pairs={{0,16},{1,5},{16,32},{17,21},{32,48},{33,37},{48,0},{49,53},{4,20}... | collective-permute-start | bytes 491528 | tf_op jit(solution)/shard_map/ppermute | solution.py:37
  29.7 8.6 %collective-permute-start.22 = (bf16[128,640]{1,0:T(8,128)(2,1)S(1)}, bf16[128,640]{1,0:T(8,128)(2,1)S(1)}, u32[]{:S(2)}, u32[]{:S(2)}) collective-permute-start(bf16[128,640]{1,0:T(8,128)(2,1)S(1)} %fusion.9), channel_id=1, source_target_pairs={{0,48},{1,13},{16,0},{17,29},{32,16},{33,45},{48,32},{49,61},{4,52... | collective-permute-start | bytes 491528 | tf_op jit(solution)/shard_map/ppermute | solution.py:37
  32.4 6.0 %collective-permute-start.21 = (bf16[128,640]{1,0:T(8,128)(2,1)S(1)}, bf16[128,640]{1,0:T(8,128)(2,1)S(1)}, u32[]{:S(2)}, u32[]{:S(2)}) collective-permute-start(bf16[128,640]{1,0:T(8,128)(2,1)S(1)} %fusion.9), channel_id=1, source_target_pairs={{0,32},{1,9},{16,48},{17,25},{32,0},{33,41},{48,16},{49,57},{4,36}... | collective-permute-start | bytes 491528 | tf_op jit(solution)/shard_map/ppermute | solution.py:37
  32.6 7.1 %collective-permute-start.20 = (bf16[128,640]{1,0:T(8,128)(2,1)S(1)}, bf16[128,640]{1,0:T(8,128)(2,1)S(1)}, u32[]{:S(2)}, u32[]{:S(2)}) collective-permute-start(bf16[128,640]{1,0:T(8,128)(2,1)S(1)} %fusion.9), channel_id=1, source_target_pairs={{0,16},{1,5},{16,32},{17,21},{32,48},{33,37},{48,0},{49,53},{4,20}... | collective-permute-start | bytes 491528 | tf_op jit(solution)/shard_map/ppermute | solution.py:37
  34.4 12.3 %collective-permute-start.13 = (bf16[128,640]{1,0:T(8,128)(2,1)S(1)}, bf16[128,640]{1,0:T(8,128)(2,1)S(1)}, u32[]{:S(2)}, u32[]{:S(2)}) collective-permute-start(bf16[128,640]{1,0:T(8,128)(2,1)S(1)} %fusion.8), channel_id=1, source_target_pairs={{0,66},{1,49},{16,82},{17,1},{32,98},{33,17},{48,114},{49,33},{4,7... | collective-permute-start | bytes 491528 | tf_op jit(solution)/shard_map/ppermute | solution.py:37
  37.8 12.0 %collective-permute-start.12 = (bf16[128,640]{1,0:T(8,128)(2,1)S(1)}, bf16[128,640]{1,0:T(8,128)(2,1)S(1)}, u32[]{:S(2)}, u32[]{:S(2)}) collective-permute-start(bf16[128,640]{1,0:T(8,128)(2,1)S(1)} %fusion.8), channel_id=1, source_target_pairs={{0,64},{1,33},{16,80},{17,49},{32,96},{33,1},{48,112},{49,17},{4,6... | collective-permute-start | bytes 491528 | tf_op jit(solution)/shard_map/ppermute | solution.py:37
  38.3 11.4 %collective-permute-start.11 = (bf16[128,640]{1,0:T(8,128)(2,1)S(1)}, bf16[128,640]{1,0:T(8,128)(2,1)S(1)}, u32[]{:S(2)}, u32[]{:S(2)}) collective-permute-start(bf16[128,640]{1,0:T(8,128)(2,1)S(1)} %fusion.8), channel_id=1, source_target_pairs={{0,2},{1,17},{16,18},{17,33},{32,34},{33,49},{48,50},{49,1},{4,6},... | collective-permute-start | bytes 491528 | tf_op jit(solution)/shard_map/ppermute | solution.py:37
  39.9 12.7 %collective-permute-start.23 = (bf16[128,640]{1,0:T(8,128)(2,1)S(1)}, bf16[128,640]{1,0:T(8,128)(2,1)S(1)}, u32[]{:S(2)}, u32[]{:S(2)}) collective-permute-start(bf16[128,640]{1,0:T(8,128)(2,1)S(1)} %add_convert_fusion.refs_4_), channel_id=1, source_target_pairs={{0,2},{1,17},{16,18},{17,33},{32,34},{33,49},{48,50},{49,1},{4,6},... | collective-permute-start | bytes 491528 | tf_op jit(solution)/shard_map/ppermute | solution.py:37
  40.6 12.2 %collective-permute-start.24 = (bf16[128,640]{1,0:T(8,128)(2,1)S(1)}, bf16[128,640]{1,0:T(8,128)(2,1)S(1)}, u32[]{:S(2)}, u32[]{:S(2)}) collective-permute-start(bf16[128,640]{1,0:T(8,128)(2,1)S(1)} %add_convert_fusion.refs_4_), channel_id=1, source_target_pairs={{0,64},{1,33},{16,80},{17,49},{32,96},{33,1},{48,112},{49,17},{4,6... | collective-permute-start | bytes 491528 | tf_op jit(solution)/shard_map/ppermute | solution.py:37
  46.6 6.2 %collective-permute-start.25 = (bf16[128,640]{1,0:T(8,128)(2,1)S(1)}, bf16[128,640]{1,0:T(8,128)(2,1)S(1)}, u32[]{:S(2)}, u32[]{:S(2)}) collective-permute-start(bf16[128,640]{1,0:T(8,128)(2,1)S(1)} %add_convert_fusion.refs_4_), channel_id=1, source_target_pairs={{0,66},{1,49},{16,82},{17,1},{32,98},{33,17},{48,114},{49,33},{4,7... | collective-permute-start | bytes 491528 | tf_op jit(solution)/shard_map/ppermute | solution.py:37
  49.9 7.4 %collective-permute-start.14 = (bf16[128,640]{1,0:T(8,128)(2,1)S(1)}, bf16[128,640]{1,0:T(8,128)(2,1)S(1)}, u32[]{:S(2)}, u32[]{:S(2)}) collective-permute-start(bf16[128,640]{1,0:T(8,128)(2,1)S(1)} %add_convert_fusion.1.refs_0_.piece0), channel_id=1, source_target_pairs={{0,16},{1,5},{16,32},{17,21},{32,48},{33,37},{48,0},{49,53},{4,20}... | collective-permute-start | bytes 491528 | tf_op jit(solution)/shard_map/ppermute | solution.py:37
  50.2 7.1 %collective-permute-start.15 = (bf16[128,640]{1,0:T(8,128)(2,1)S(1)}, bf16[128,640]{1,0:T(8,128)(2,1)S(1)}, u32[]{:S(2)}, u32[]{:S(2)}) collective-permute-start(bf16[128,640]{1,0:T(8,128)(2,1)S(1)} %add_convert_fusion.1.refs_0_.piece0), channel_id=1, source_target_pairs={{0,32},{1,9},{16,48},{17,25},{32,0},{33,41},{48,16},{49,57},{4,36}... | collective-permute-start | bytes 491528 | tf_op jit(solution)/shard_map/ppermute | solution.py:37
  52.6 5.4 %collective-permute-start.16 = (bf16[128,640]{1,0:T(8,128)(2,1)S(1)}, bf16[128,640]{1,0:T(8,128)(2,1)S(1)}, u32[]{:S(2)}, u32[]{:S(2)}) collective-permute-start(bf16[128,640]{1,0:T(8,128)(2,1)S(1)} %add_convert_fusion.1.refs_0_.piece0), channel_id=1, source_target_pairs={{0,48},{1,13},{16,0},{17,29},{32,16},{33,45},{48,32},{49,61},{4,52... | collective-permute-start | bytes 491528 | tf_op jit(solution)/shard_map/ppermute | solution.py:37
  58.4 7.9 %collective-permute-start.28 = (bf16[192,512]{1,0:T(8,128)(2,1)S(1)}, bf16[192,512]{1,0:T(8,128)(2,1)S(1)}, u32[]{:S(2)}, u32[]{:S(2)}) collective-permute-start(bf16[192,512]{1,0:T(8,128)(2,1)S(1)} %get-tuple-element.58), channel_id=1, source_target_pairs={{0,4},{1,3},{16,20},{17,19},{32,36},{33,35},{48,52},{49,51},{4,8},... | collective-permute-start | bytes 589832 | tf_op jit(solution)/shard_map/ppermute | solution.py:37
  58.5 7.8 %collective-permute-start.27 = (bf16[192,512]{1,0:T(8,128)(2,1)S(1)}, bf16[192,512]{1,0:T(8,128)(2,1)S(1)}, u32[]{:S(2)}, u32[]{:S(2)}) collective-permute-start(bf16[192,512]{1,0:T(8,128)(2,1)S(1)} %get-tuple-element.57), channel_id=1, source_target_pairs={{0,8},{1,65},{16,24},{17,81},{32,40},{33,97},{48,56},{49,113},{4,1... | collective-permute-start | bytes 589832 | tf_op jit(solution)/shard_map/ppermute | solution.py:37
  59.3 7.6 %collective-permute-start.26 = (bf16[192,512]{1,0:T(8,128)(2,1)S(1)}, bf16[192,512]{1,0:T(8,128)(2,1)S(1)}, u32[]{:S(2)}, u32[]{:S(2)}) collective-permute-start(bf16[192,512]{1,0:T(8,128)(2,1)S(1)} %get-tuple-element.56), channel_id=1, source_target_pairs={{0,12},{1,67},{16,28},{17,83},{32,44},{33,99},{48,60},{49,115},{4,... | collective-permute-start | bytes 589832 | tf_op jit(solution)/shard_map/ppermute | solution.py:37
  67.1 8.8 %collective-permute-start.29 = (f32[192]{0:T(256)S(1)}, f32[192]{0:T(256)S(1)}, u32[]{:S(2)}, u32[]{:S(2)}) collective-permute-start(f32[192]{0:T(256)S(1)} %fusion.5), channel_id=1, source_target_pairs={{0,1},{1,0},{2,3},{3,2},{4,5},{5,4},{6,7},{7,6},{8,9},{9,8},{10,11... | collective-permute-start | bytes 2312 | tf_op jit(solution)/shard_map/ppermute | solution.py:41

commit v14 on v13

--- a/solution.py
+++ b/solution.py
@@ -12,9 +12,11 @@
 X, Y, Z = 0, 1, 2
 SIZE = 4
 GATHER = (Y, X)
-FIRST = ((X, Z), (Z, Y))
-SECOND = ((Z, Y), (X, Z))
-ORDER = (1, 3, 2)
+FIRST = ((X, Z), (Z, Z))
+SECOND = ((Z, Y), (X, Y))
+ORDER = (2, 1, 3)
+SUM = (1, 3, 2)
+LAST = 3
 STRIP = 32
 PARAMS = pltpu.CompilerParams(vmem_limit_bytes=40 * 1024 * 1024)
 WHOLE = pl.BlockSpec(memory_space=pltpu.VMEM)
@@ -198,8 +200,9 @@
     places = places_here()
     outs, (left, weights) = refs[: SIZE - 1], refs[SIZE - 1 :]
     rows = far1.shape[0]
-    last = jnp.zeros(piece0.shape, piece0.dtype)
-    gather_weights(places[2], (piece0, piece1, piece2, last), weights)
+    pieces = [piece0, piece1, piece2]
+    pieces.insert(LAST, jnp.zeros(piece0.shape, piece0.dtype))
+    gather_weights(places[2], pieces, weights)
     for k, pack in enumerate((far1, far2, far3)):
         left[pl.ds(k * rows, rows), :] = pack[...]
     product = times(left[...], weights[...])
@@ -211,7 +214,7 @@
 def apply_sent_kernel(left, piece, before, early1, early2, early3, *outs):
     places = places_here()
     rows, ss = outs[0].shape[0], piece.shape[0]
-    which = lax.rem(places[2] + 1, SIZE)
+    which = lax.rem(places[2] + SIZE - LAST, SIZE)
     block = pl.ds(pl.multiple_of(which * ss, ss), ss)
     product = times(left[...], piece[...])
     for k, out in enumerate(outs):
@@ -273,8 +276,9 @@
         return [own] + [arrived[by] for by in (1, 2, 3)]
 
     def added(total, sent, axis_of_core, sign=1):
-        for array in exchanged(None, sent, axis_of_core, sign)[1:]:
-            total = total + array.astype(F32)
+        arrived = exchanged(None, sent, axis_of_core, sign)
+        for by in SUM:
+            total = total + arrived[by].astype(F32)
         return total
 
     near = exchanged(near[0], near.__getitem__, GATHER)
@@ -288,7 +292,7 @@
     def operands(count):
         return [pltpu.VMEM((count * rows, half), BF16), pltpu.VMEM((count * rows, feats), BF16)]
 
-    first, last = (0, 1, 3), 2
+    first = [by for by in range(SIZE) if by != LAST]
     early = kernel_call(
         functools.partial(gram_early_kernel, level * SIZE / groups),
         "gram_early",
@@ -299,13 +303,13 @@
     )(*[near[by] for by in first])[0]
     near_blocks = kernel_call(
         gram_native_kernel, "gram_native", blocks, 2, operands(1), flops // 4
-    )(near[last], early)
+    )(near[LAST], early)
     early = kernel_call(
         gram_far_early_kernel, "gram_far_early", shapes(((half, feats), F32)), 6, operands(3), flops
     )(*[near[by] for by in first], *[far[by] for by in first])[0]
     far_blocks = kernel_call(
         gram_far_kernel, "gram_far", blocks, 3, operands(1), flops // 4
-    )(near[last], far[last], early)
+    )(near[LAST], far[LAST], early)
 
     def weights_of(chunk, own, *sends):
         total = added(own, lambda by: sends[by - 1], FIRST[chunk])
@@ -333,7 +337,7 @@
         7,
         [weights],
         flops * 3 // 4,
-    )(*far[1:], *far_weights[:3], sofar)
+    )(*far[1:], *[far_weights[by] for by in range(SIZE) if by != LAST], sofar)
     parts = kernel_call(
         apply_sent_kernel,
         "apply_sent",
@@ -342,7 +346,7 @@
         (),
         flops // 4,
         {3 + k: k for k in range(3)},
-    )(stacked, far_weights[3], sofar, *most)
+    )(stacked, far_weights[LAST], sofar, *most)
     grad_n = kernel_call(
         apply_kept_kernel, "apply_kept", shapes(((rows, half), F32)), SIZE + 2, [weights], flops // 4
     )(far[0], *far_weights, sofar)[0]

time: 77.1 us -> 71.6 us (0.929)
  waiting for transfers between devices: 21 us -> 15.8 us
    ppermute x27, waiting for transfers between devices: 20.2 us -> 15.1 us  [shifted(): return lax.ppermute(array, AXES, pairs)]
    ppermute x3, starting transfers between devices: 9.44 us -> 6.78 us  [other_core(): return lax.ppermute(array, 'sec', [(0, 1), (1, 0)])]
    ppermute x27, starting transfers between devices: 36.4 us -> 38.7 us  [shifted(): return lax.ppermute(array, AXES, pairs)]
  transfers between devices with their start and end apart: 30 -> 30, of which waited for: 12 -> 9; matrix products, arithmetic and copies ran while one was open for 1% -> 1% of each run, Pallas kernels for 7% -> 7%
where the time goes in v14:
time: 71.6 us; the launch traced here: 71.5 us
  starting transfers between devices  45.5 us (64%)
  waiting for transfers between devices  15.8 us (22%)
  Pallas kernels  6.19 us (9%)
  local copies, waits for them, and re-layouts  2.06 us (3%)
  other arithmetic  1.7 us (2%)
    ppermute x27, starting transfers between devices, shifted(): return lax.ppermute(array, AXES, pairs)  38.7 us
    ppermute x27, waiting for transfers between devices, shifted(): return lax.ppermute(array, AXES, pairs)  15.1 us
    ppermute x3, starting transfers between devices, other_core(): return lax.ppermute(array, 'sec', [(0, 1), (1, 0)])  6.78 us
    unnamed x4, local copies, waits for them, and re-layouts  2.06 us
  transfers between devices with their start and end apart: 30, of which 9 were waited for; matrix products, arithmetic and copies ran while one was open for 1% of the time, Pallas kernels for 7%

profile of v14, /device:TPU:1, one launch (start us, length us, event | category | flops | bytes accessed | tf_op | source)
XLA Modules:
  0.0 71.5 jit_solution(13898048810237980699)
XLA Ops:
  0.0 1.4 %collective-permute-start.1 = (bf16[192,2048]{1,0:T(8,128)(2,1)}, bf16[192,2048]{1,0:T(8,128)(2,1)S(1)}, u32[]{:S(2)}, u32[]{:S(2)}) collective-permute-start(bf16[192,2048]{1,0:T(8,128)(2,1)} %t_own.3), channel_id=1, source_target_pairs={{0,1},{1,0},{2,3},{3,2},{4,5},{5,4},{6,7},{7,6},{8,9},{9,8},{10,11... | collective-permute-start | bytes 2359304 | tf_op jit(solution)/shard_map/ppermute | solution.py:43
  1.4 1.1 %copy-done = bf16[192,2048]{1,0:T(8,128)(2,1)S(1)} copy-done((bf16[192,2048]{1,0:T(8,128)(2,1)S(1)}, bf16[192,2048]{1,0:T(8,128)(2,1)}, u32[]{:S(2)}) %copy-start) | copy-done | bytes 786456
  2.6 0.9 %copy-done.1 = bf16[192,512]{1,0:T(8,128)(2,1)S(1)} copy-done((bf16[192,512]{1,0:T(8,128)(2,1)S(1)}, bf16[192,512]{1,0:T(8,128)(2,1)}, u32[]{:S(2)}) %copy-start.1) | copy-done | bytes 196632
  3.5 0.3 sums.1
  3.8 0.5 pack_own.1
  4.3 1.4 %collective-permute-start.4 = (bf16[192,1024]{1,0:T(8,128)(2,1)S(1)}, bf16[192,1024]{1,0:T(8,128)(2,1)S(1)}, u32[]{:S(2)}, u32[]{:S(2)}) collective-permute-start(bf16[192,1024]{1,0:T(8,128)(2,1)S(1)} %get-tuple-element.40), channel_id=1, source_target_pairs={{0,4},{1,3},{16,20},{17,19},{32,36},{33,35},{48,52},{49,51},{4,8},... | collective-permute-start | bytes 1179656 | tf_op jit(solution)/shard_map/ppermute | solution.py:39
  5.7 2.5 %collective-permute-start.5 = (bf16[192,1024]{1,0:T(8,128)(2,1)S(1)}, bf16[192,1024]{1,0:T(8,128)(2,1)S(1)}, u32[]{:S(2)}, u32[]{:S(2)}) collective-permute-start(bf16[192,1024]{1,0:T(8,128)(2,1)S(1)} %get-tuple-element.41), channel_id=1, source_target_pairs={{0,8},{1,65},{16,24},{17,81},{32,40},{33,97},{48,56},{49,113},{4,1... | collective-permute-start | bytes 1179656 | tf_op jit(solution)/shard_map/ppermute | solution.py:39
  8.1 1.2 %collective-permute-start.2 = (bf16[192,1024]{1,0:T(8,128)(2,1)S(1)}, bf16[192,1024]{1,0:T(8,128)(2,1)S(1)}, u32[]{:S(2)}, u32[]{:S(2)}) collective-permute-start(bf16[192,1024]{1,0:T(8,128)(2,1)S(1)} %get-tuple-element.37), channel_id=1, source_target_pairs={{0,12},{1,67},{16,28},{17,83},{32,44},{33,99},{48,60},{49,115},{4,... | collective-permute-start | bytes 1179656 | tf_op jit(solution)/shard_map/ppermute | solution.py:39
  9.3 0.3 pack_far.1
  9.6 0.4 collective-permute-start.6
  10.0 0.9 %collective-permute-start.7 = (bf16[192,640]{1,0:T(8,128)(2,1)S(1)}, bf16[192,640]{1,0:T(8,128)(2,1)S(1)}, u32[]{:S(2)}, u32[]{:S(2)}) collective-permute-start(bf16[192,640]{1,0:T(8,128)(2,1)S(1)} %get-tuple-element.43), channel_id=1, source_target_pairs={{0,8},{1,65},{16,24},{17,81},{32,40},{33,97},{48,56},{49,113},{4,1... | collective-permute-start | bytes 737288 | tf_op jit(solution)/shard_map/ppermute | solution.py:39
  10.8 1.7 %collective-permute-done.4.refs_1_ = bf16[192,1024]{1,0:T(8,128)(2,1)S(1)} collective-permute-done((bf16[192,1024]{1,0:T(8,128)(2,1)S(1)}, bf16[192,1024]{1,0:T(8,128)(2,1)S(1)}, u32[]{:S(2)}, u32[]{:S(2)}) %collective-permute-start.4) | collective-permute-done | bytes 393248 | tf_op jit(solution)/shard_map/ppermute | solution.py:39
  12.5 1.4 %collective-permute-start.3 = (bf16[192,640]{1,0:T(8,128)(2,1)S(1)}, bf16[192,640]{1,0:T(8,128)(2,1)S(1)}, u32[]{:S(2)}, u32[]{:S(2)}) collective-permute-start(bf16[192,640]{1,0:T(8,128)(2,1)S(1)} %get-tuple-element.38), channel_id=1, source_target_pairs={{0,12},{1,67},{16,28},{17,83},{32,44},{33,99},{48,60},{49,115},{4,... | collective-permute-start | bytes 737288 | tf_op jit(solution)/shard_map/ppermute | solution.py:39
  13.9 4.0 %collective-permute-done.5.refs_2_ = bf16[192,1024]{1,0:T(8,128)(2,1)S(1)} collective-permute-done((bf16[192,1024]{1,0:T(8,128)(2,1)S(1)}, bf16[192,1024]{1,0:T(8,128)(2,1)S(1)}, u32[]{:S(2)}, u32[]{:S(2)}) %collective-permute-start.5) | collective-permute-done | bytes 393248 | tf_op jit(solution)/shard_map/ppermute | solution.py:39
  17.9 1.0 %gram_early.1.before = f32[512,640]{1,0:T(8,128)S(1)} custom-call(bf16[192,1024]{1,0:T(8,128)(2,1)S(1)} %get-tuple-element.39.refs_0_, bf16[192,1024]{1,0:T(8,128)(2,1)S(1)} %collective-permute-done.4.refs_1_, bf16[192,1024]{1,0:T(8,128)(2,1)S(1)} %collective-permute-done.5.refs_2_), custom_call_target="tpu_custom_call" | custom-call | flops 503316480 | bytes 4194304 | tf_op jit(solution)/shard_map/gram_early/pallas_call | solution.py:296
  18.9 0.5 gram_native.1
  19.3 3.7 %collective-permute-start.19 = (bf16[128,640]{1,0:T(8,128)(2,1)S(1)}, bf16[128,640]{1,0:T(8,128)(2,1)S(1)}, u32[]{:S(2)}, u32[]{:S(2)}) collective-permute-start(bf16[128,640]{1,0:T(8,128)(2,1)S(1)} %get-tuple-element.51), channel_id=1, source_target_pairs={{0,64},{1,33},{16,80},{17,49},{32,96},{33,1},{48,112},{49,17},{4,6... | collective-permute-start | bytes 491528 | tf_op jit(solution)/shard_map/ppermute | solution.py:39
  23.0 0.4 collective-permute-start.18
  23.4 1.0 %collective-permute-start.17 = (bf16[128,640]{1,0:T(8,128)(2,1)S(1)}, bf16[128,640]{1,0:T(8,128)(2,1)S(1)}, u32[]{:S(2)}, u32[]{:S(2)}) collective-permute-start(bf16[128,640]{1,0:T(8,128)(2,1)S(1)} %get-tuple-element.49), channel_id=1, source_target_pairs={{0,2},{1,17},{16,18},{17,33},{32,34},{33,49},{48,50},{49,1},{4,6},... | collective-permute-start | bytes 491528 | tf_op jit(solution)/shard_map/ppermute | solution.py:39
  24.5 0.9 %gram_far_early.1.before = f32[512,640]{1,0:T(8,128)S(1)} custom-call(bf16[192,1024]{1,0:T(8,128)(2,1)S(1)} %get-tuple-element.39.refs_0_, bf16[192,1024]{1,0:T(8,128)(2,1)S(1)} %collective-permute-done.4.refs_1_, bf16[192,1024]{1,0:T(8,128)(2,1)S(1)} %collective-permute-done.5.refs_2_, bf16[192,640]{1,0:T(8,128)(2,1)S(1)} %get-tuple-element.36.refs_3_.pack, ...), custom_call_target="tpu_custom_call" | custom-call | flops 503316480 | bytes 4194304 | tf_op jit(solution)/shard_map/gram_far_early/pallas_call | solution.py:307
  25.4 0.5 gram_far.1
  25.8 2.3 %collective-permute-start.10 = (bf16[128,640]{1,0:T(8,128)(2,1)S(1)}, bf16[128,640]{1,0:T(8,128)(2,1)S(1)}, u32[]{:S(2)}, u32[]{:S(2)}) collective-permute-start(bf16[128,640]{1,0:T(8,128)(2,1)S(1)} %get-tuple-element.47), channel_id=1, source_target_pairs={{0,32},{1,33},{16,48},{17,49},{32,0},{33,1},{48,16},{49,17},{4,36}... | collective-permute-start | bytes 491528 | tf_op jit(solution)/shard_map/ppermute | solution.py:39
  28.2 0.9 %collective-permute-start.9 = (bf16[128,640]{1,0:T(8,128)(2,1)S(1)}, bf16[128,640]{1,0:T(8,128)(2,1)S(1)}, u32[]{:S(2)}, u32[]{:S(2)}) collective-permute-start(bf16[128,640]{1,0:T(8,128)(2,1)S(1)} %get-tuple-element.46), channel_id=1, source_target_pairs={{0,48},{1,49},{16,0},{17,1},{32,16},{33,17},{48,32},{49,33},{4,52}... | collective-permute-start | bytes 491528 | tf_op jit(solution)/shard_map/ppermute | solution.py:39
  29.1 0.6 collective-permute-start.8
  29.7 2.7 %collective-permute-start.22 = (bf16[128,640]{1,0:T(8,128)(2,1)S(1)}, bf16[128,640]{1,0:T(8,128)(2,1)S(1)}, u32[]{:S(2)}, u32[]{:S(2)}) collective-permute-start(bf16[128,640]{1,0:T(8,128)(2,1)S(1)} %fusion.9), channel_id=1, source_target_pairs={{0,32},{1,9},{16,48},{17,25},{32,0},{33,41},{48,16},{49,57},{4,36}... | collective-permute-start | bytes 491528 | tf_op jit(solution)/shard_map/ppermute | solution.py:39
  32.4 0.8 %collective-permute-start.21 = (bf16[128,640]{1,0:T(8,128)(2,1)S(1)}, bf16[128,640]{1,0:T(8,128)(2,1)S(1)}, u32[]{:S(2)}, u32[]{:S(2)}) collective-permute-start(bf16[128,640]{1,0:T(8,128)(2,1)S(1)} %fusion.9), channel_id=1, source_target_pairs={{0,48},{1,13},{16,0},{17,29},{32,16},{33,45},{48,32},{49,61},{4,52... | collective-permute-start | bytes 491528 | tf_op jit(solution)/shard_map/ppermute | solution.py:39
  33.2 0.7 collective-permute-start.20
  33.9 2.1 %collective-permute-done.8 = bf16[128,640]{1,0:T(8,128)(2,1)S(1)} collective-permute-done((bf16[128,640]{1,0:T(8,128)(2,1)S(1)}, bf16[128,640]{1,0:T(8,128)(2,1)S(1)}, u32[]{:S(2)}, u32[]{:S(2)}) %collective-permute-start.8) | collective-permute-done | bytes 163872 | tf_op jit(solution)/shard_map/ppermute | solution.py:39
  36.0 2.8 %collective-permute-start.13 = (bf16[128,640]{1,0:T(8,128)(2,1)S(1)}, bf16[128,640]{1,0:T(8,128)(2,1)S(1)}, u32[]{:S(2)}, u32[]{:S(2)}) collective-permute-start(bf16[128,640]{1,0:T(8,128)(2,1)S(1)} %fusion.8), channel_id=1, source_target_pairs={{0,64},{1,9},{16,80},{17,25},{32,96},{33,41},{48,112},{49,57},{4,6... | collective-permute-start | bytes 491528 | tf_op jit(solution)/shard_map/ppermute | solution.py:39
  38.8 0.8 %collective-permute-start.12 = (bf16[128,640]{1,0:T(8,128)(2,1)S(1)}, bf16[128,640]{1,0:T(8,128)(2,1)S(1)}, u32[]{:S(2)}, u32[]{:S(2)}) collective-permute-start(bf16[128,640]{1,0:T(8,128)(2,1)S(1)} %fusion.8), channel_id=1, source_target_pairs={{0,66},{1,13},{16,82},{17,29},{32,98},{33,45},{48,114},{49,61},{4,... | collective-permute-start | bytes 491528 | tf_op jit(solution)/shard_map/ppermute | solution.py:39
  39.7 0.7 collective-permute-start.11
  40.5 1.1 %collective-permute-start.23 = (bf16[128,640]{1,0:T(8,128)(2,1)S(1)}, bf16[128,640]{1,0:T(8,128)(2,1)S(1)}, u32[]{:S(2)}, u32[]{:S(2)}) collective-permute-start(bf16[128,640]{1,0:T(8,128)(2,1)S(1)} %add_convert_fusion.refs_4_), channel_id=1, source_target_pairs={{0,2},{1,17},{16,18},{17,33},{32,34},{33,49},{48,50},{49,1},{4,6},... | collective-permute-start | bytes 491528 | tf_op jit(solution)/shard_map/ppermute | solution.py:39
  41.6 2.9 %collective-permute-start.24 = (bf16[128,640]{1,0:T(8,128)(2,1)S(1)}, bf16[128,640]{1,0:T(8,128)(2,1)S(1)}, u32[]{:S(2)}, u32[]{:S(2)}) collective-permute-start(bf16[128,640]{1,0:T(8,128)(2,1)S(1)} %add_convert_fusion.refs_4_), channel_id=1, source_target_pairs={{0,64},{1,33},{16,80},{17,49},{32,96},{33,1},{48,112},{49,17},{4,6... | collective-permute-start | bytes 491528 | tf_op jit(solution)/shard_map/ppermute | solution.py:39
  44.5 0.7 collective-permute-done.11
  45.4 1.0 %collective-permute-start.14 = (bf16[128,640]{1,0:T(8,128)(2,1)S(1)}, bf16[128,640]{1,0:T(8,128)(2,1)S(1)}, u32[]{:S(2)}, u32[]{:S(2)}) collective-permute-start(bf16[128,640]{1,0:T(8,128)(2,1)S(1)} %add_convert_fusion.1.refs_0_.piece0), channel_id=1, source_target_pairs={{0,16},{1,17},{16,32},{17,33},{32,48},{33,49},{48,0},{49,1},{4,20}... | collective-permute-start | bytes 491528 | tf_op jit(solution)/shard_map/ppermute | solution.py:39
  46.3 2.6 %collective-permute-start.15 = (bf16[128,640]{1,0:T(8,128)(2,1)S(1)}, bf16[128,640]{1,0:T(8,128)(2,1)S(1)}, u32[]{:S(2)}, u32[]{:S(2)}) collective-permute-start(bf16[128,640]{1,0:T(8,128)(2,1)S(1)} %add_convert_fusion.1.refs_0_.piece0), channel_id=1, source_target_pairs={{0,32},{1,33},{16,48},{17,49},{32,0},{33,1},{48,16},{49,17},{4,36}... | collective-permute-start | bytes 491528 | tf_op jit(solution)/shard_map/ppermute | solution.py:39
  49.0 0.9 %apply_native.1.refs_4_.before = f32[768,512]{1,0:T(8,128)S(1)} custom-call(bf16[192,1024]{1,0:T(8,128)(2,1)S(1)} %get-tuple-element.39.refs_0_, bf16[192,1024]{1,0:T(8,128)(2,1)S(1)} %collective-permute-done.4.refs_1_, bf16[192,1024]{1,0:T(8,128)(2,1)S(1)} %collective-permute-done.5.refs_2_, bf16[192,1024]{1,0:T(8,128)(2,1)S(1)} %collective-permute-done.2.norm.pack.refs_3_, ...), custom_call_target="tpu_custom_call" | custom-call | flops 503316480 | bytes 4194304 | tf_op jit(solution)/shard_map/apply_native/pallas_call | solution.py:323
  49.8 1.5 %collective-permute-done.14.refs_1_.piece1 = bf16[128,640]{1,0:T(8,128)(2,1)S(1)} collective-permute-done((bf16[128,640]{1,0:T(8,128)(2,1)S(1)}, bf16[128,640]{1,0:T(8,128)(2,1)S(1)}, u32[]{:S(2)}, u32[]{:S(2)}) %collective-permute-start.14) | collective-permute-done | bytes 163872 | tf_op jit(solution)/shard_map/ppermute | solution.py:39
  51.3 2.2 %collective-permute-done.15.refs_2_.piece2 = bf16[128,640]{1,0:T(8,128)(2,1)S(1)} collective-permute-done((bf16[128,640]{1,0:T(8,128)(2,1)S(1)}, bf16[128,640]{1,0:T(8,128)(2,1)S(1)}, u32[]{:S(2)}, u32[]{:S(2)}) %collective-permute-start.15) | collective-permute-done | bytes 163872 | tf_op jit(solution)/shard_map/ppermute | solution.py:39
  53.5 0.7 apply_early.1
  54.3 0.4 apply_sent.1
  54.6 3.4 %collective-permute-start.28 = (bf16[192,512]{1,0:T(8,128)(2,1)S(1)}, bf16[192,512]{1,0:T(8,128)(2,1)S(1)}, u32[]{:S(2)}, u32[]{:S(2)}) collective-permute-start(bf16[192,512]{1,0:T(8,128)(2,1)S(1)} %get-tuple-element.58), channel_id=1, source_target_pairs={{0,8},{1,65},{16,24},{17,81},{32,40},{33,97},{48,56},{49,113},{4,1... | collective-permute-start | bytes 589832 | tf_op jit(solution)/shard_map/ppermute | solution.py:39
  58.1 2.7 %collective-permute-start.26 = (bf16[192,512]{1,0:T(8,128)(2,1)S(1)}, bf16[192,512]{1,0:T(8,128)(2,1)S(1)}, u32[]{:S(2)}, u32[]{:S(2)}) collective-permute-start(bf16[192,512]{1,0:T(8,128)(2,1)S(1)} %get-tuple-element.56), channel_id=1, source_target_pairs={{0,12},{1,67},{16,28},{17,83},{32,44},{33,99},{48,60},{49,115},{4,... | collective-permute-start | bytes 589832 | tf_op jit(solution)/shard_map/ppermute | solution.py:39
  60.7 0.4 apply_kept.1
  61.2 2.9 %collective-permute-done.27 = bf16[192,512]{1,0:T(8,128)(2,1)S(1)} collective-permute-done((bf16[192,512]{1,0:T(8,128)(2,1)S(1)}, bf16[192,512]{1,0:T(8,128)(2,1)S(1)}, u32[]{:S(2)}, u32[]{:S(2)}) %collective-permute-start.27) | collective-permute-done | bytes 196640 | tf_op jit(solution)/shard_map/ppermute | solution.py:39
  64.3 5.4 %collective-permute-start.29 = (f32[192]{0:T(256)S(1)}, f32[192]{0:T(256)S(1)}, u32[]{:S(2)}, u32[]{:S(2)}) collective-permute-start(f32[192]{0:T(256)S(1)} %fusion.5), channel_id=1, source_target_pairs={{0,1},{1,0},{2,3},{3,2},{4,5},{5,4},{6,7},{7,6},{8,9},{9,8},{10,11... | collective-permute-start | bytes 2312 | tf_op jit(solution)/shard_map/ppermute | solution.py:43
  69.8 0.7 collective-permute-done.29
  70.5 0.9 %fusion.7 = f32[192,512]{1,0:T(8,128)} fusion(f32[192]{0:T(256)S(1)} %reduce, f32[192]{0:T(256)S(1)} %add.67, bf16[192,1024]{1,0:T(8,128)(2,1)S(1)} %get-tuple-element.39.refs_0_, bf16[192,512]{1,0:T(8,128)(2,1)S(1)} %collective-permute-done.28, bf16[192,512]{1,0:T(8,128)(2,1)S(1)} %collective-permute-done.27, ...), kind=kLoop, calls=%fused_computation.10 | loop fusion | flops 1277952 | bytes 1574400 | tf_op jit(solution)/shard_map/mul | solution.py:358
  (35 shorter events, 1.0 us)
Async XLA Ops:
  0.0 3.8 %collective-permute-start.1 = (bf16[192,2048]{1,0:T(8,128)(2,1)}, bf16[192,2048]{1,0:T(8,128)(2,1)S(1)}, u32[]{:S(2)}, u32[]{:S(2)}) collective-permute-start(bf16[192,2048]{1,0:T(8,128)(2,1)} %t_own.3), channel_id=1, source_target_pairs={{0,1},{1,0},{2,3},{3,2},{4,5},{5,4},{6,7},{7,6},{8,9},{9,8},{10,11... | collective-permute-start | bytes 2359304 | tf_op jit(solution)/shard_map/ppermute | solution.py:43
  1.4 2.4 %collective-permute-start = (bf16[192,512]{1,0:T(8,128)(2,1)}, bf16[192,512]{1,0:T(8,128)(2,1)S(1)}, u32[]{:S(2)}, u32[]{:S(2)}) collective-permute-start(bf16[192,512]{1,0:T(8,128)(2,1)} %s_own.3), channel_id=1, source_target_pairs={{0,1},{1,0},{2,3},{3,2},{4,5},{5,4},{6,7},{7,6},{8,9},{9,8},{10,11... | collective-permute-start | bytes 589832 | tf_op jit(solution)/shard_map/ppermute | solution.py:43
  1.4 1.1 %copy-start = (bf16[192,2048]{1,0:T(8,128)(2,1)S(1)}, bf16[192,2048]{1,0:T(8,128)(2,1)}, u32[]{:S(2)}) copy-start(bf16[192,2048]{1,0:T(8,128)(2,1)} %t_own.3) | copy-start | bytes 2359300
  2.6 0.9 %copy-start.1 = (bf16[192,512]{1,0:T(8,128)(2,1)S(1)}, bf16[192,512]{1,0:T(8,128)(2,1)}, u32[]{:S(2)}) copy-start(bf16[192,512]{1,0:T(8,128)(2,1)} %s_own.3) | copy-start | bytes 589828
  4.3 8.2 %collective-permute-start.4 = (bf16[192,1024]{1,0:T(8,128)(2,1)S(1)}, bf16[192,1024]{1,0:T(8,128)(2,1)S(1)}, u32[]{:S(2)}, u32[]{:S(2)}) collective-permute-start(bf16[192,1024]{1,0:T(8,128)(2,1)S(1)} %get-tuple-element.40), channel_id=1, source_target_pairs={{0,4},{1,3},{16,20},{17,19},{32,36},{33,35},{48,52},{49,51},{4,8},... | collective-permute-start | bytes 1179656 | tf_op jit(solution)/shard_map/ppermute | solution.py:39
  5.7 12.2 %collective-permute-start.5 = (bf16[192,1024]{1,0:T(8,128)(2,1)S(1)}, bf16[192,1024]{1,0:T(8,128)(2,1)S(1)}, u32[]{:S(2)}, u32[]{:S(2)}) collective-permute-start(bf16[192,1024]{1,0:T(8,128)(2,1)S(1)} %get-tuple-element.41), channel_id=1, source_target_pairs={{0,8},{1,65},{16,24},{17,81},{32,40},{33,97},{48,56},{49,113},{4,1... | collective-permute-start | bytes 1179656 | tf_op jit(solution)/shard_map/ppermute | solution.py:39
  8.1 10.7 %collective-permute-start.2 = (bf16[192,1024]{1,0:T(8,128)(2,1)S(1)}, bf16[192,1024]{1,0:T(8,128)(2,1)S(1)}, u32[]{:S(2)}, u32[]{:S(2)}) collective-permute-start(bf16[192,1024]{1,0:T(8,128)(2,1)S(1)} %get-tuple-element.37), channel_id=1, source_target_pairs={{0,12},{1,67},{16,28},{17,83},{32,44},{33,99},{48,60},{49,115},{4,... | collective-permute-start | bytes 1179656 | tf_op jit(solution)/shard_map/ppermute | solution.py:39
  9.6 13.9 %collective-permute-start.6 = (bf16[192,640]{1,0:T(8,128)(2,1)S(1)}, bf16[192,640]{1,0:T(8,128)(2,1)S(1)}, u32[]{:S(2)}, u32[]{:S(2)}) collective-permute-start(bf16[192,640]{1,0:T(8,128)(2,1)S(1)} %get-tuple-element.42), channel_id=1, source_target_pairs={{0,4},{1,3},{16,20},{17,19},{32,36},{33,35},{48,52},{49,51},{4,8},... | collective-permute-start | bytes 737288 | tf_op jit(solution)/shard_map/ppermute | solution.py:39
  10.0 14.5 %collective-permute-start.7 = (bf16[192,640]{1,0:T(8,128)(2,1)S(1)}, bf16[192,640]{1,0:T(8,128)(2,1)S(1)}, u32[]{:S(2)}, u32[]{:S(2)}) collective-permute-start(bf16[192,640]{1,0:T(8,128)(2,1)S(1)} %get-tuple-element.43), channel_id=1, source_target_pairs={{0,8},{1,65},{16,24},{17,81},{32,40},{33,97},{48,56},{49,113},{4,1... | collective-permute-start | bytes 737288 | tf_op jit(solution)/shard_map/ppermute | solution.py:39
  12.5 12.8 %collective-permute-start.3 = (bf16[192,640]{1,0:T(8,128)(2,1)S(1)}, bf16[192,640]{1,0:T(8,128)(2,1)S(1)}, u32[]{:S(2)}, u32[]{:S(2)}) collective-permute-start(bf16[192,640]{1,0:T(8,128)(2,1)S(1)} %get-tuple-element.38), channel_id=1, source_target_pairs={{0,12},{1,67},{16,28},{17,83},{32,44},{33,99},{48,60},{49,115},{4,... | collective-permute-start | bytes 737288 | tf_op jit(solution)/shard_map/ppermute | solution.py:39
  19.3 9.7 %collective-permute-start.19 = (bf16[128,640]{1,0:T(8,128)(2,1)S(1)}, bf16[128,640]{1,0:T(8,128)(2,1)S(1)}, u32[]{:S(2)}, u32[]{:S(2)}) collective-permute-start(bf16[128,640]{1,0:T(8,128)(2,1)S(1)} %get-tuple-element.51), channel_id=1, source_target_pairs={{0,64},{1,33},{16,80},{17,49},{32,96},{33,1},{48,112},{49,17},{4,6... | collective-permute-start | bytes 491528 | tf_op jit(solution)/shard_map/ppermute | solution.py:39
  23.0 6.6 %collective-permute-start.18 = (bf16[128,640]{1,0:T(8,128)(2,1)S(1)}, bf16[128,640]{1,0:T(8,128)(2,1)S(1)}, u32[]{:S(2)}, u32[]{:S(2)}) collective-permute-start(bf16[128,640]{1,0:T(8,128)(2,1)S(1)} %get-tuple-element.50), channel_id=1, source_target_pairs={{0,66},{1,49},{16,82},{17,1},{32,98},{33,17},{48,114},{49,33},{4,7... | collective-permute-start | bytes 491528 | tf_op jit(solution)/shard_map/ppermute | solution.py:39
  23.4 6.2 %collective-permute-start.17 = (bf16[128,640]{1,0:T(8,128)(2,1)S(1)}, bf16[128,640]{1,0:T(8,128)(2,1)S(1)}, u32[]{:S(2)}, u32[]{:S(2)}) collective-permute-start(bf16[128,640]{1,0:T(8,128)(2,1)S(1)} %get-tuple-element.49), channel_id=1, source_target_pairs={{0,2},{1,17},{16,18},{17,33},{32,34},{33,49},{48,50},{49,1},{4,6},... | collective-permute-start | bytes 491528 | tf_op jit(solution)/shard_map/ppermute | solution.py:39
  25.8 7.4 %collective-permute-start.10 = (bf16[128,640]{1,0:T(8,128)(2,1)S(1)}, bf16[128,640]{1,0:T(8,128)(2,1)S(1)}, u32[]{:S(2)}, u32[]{:S(2)}) collective-permute-start(bf16[128,640]{1,0:T(8,128)(2,1)S(1)} %get-tuple-element.47), channel_id=1, source_target_pairs={{0,32},{1,33},{16,48},{17,49},{32,0},{33,1},{48,16},{49,17},{4,36}... | collective-permute-start | bytes 491528 | tf_op jit(solution)/shard_map/ppermute | solution.py:39
  28.2 5.7 %collective-permute-start.9 = (bf16[128,640]{1,0:T(8,128)(2,1)S(1)}, bf16[128,640]{1,0:T(8,128)(2,1)S(1)}, u32[]{:S(2)}, u32[]{:S(2)}) collective-permute-start(bf16[128,640]{1,0:T(8,128)(2,1)S(1)} %get-tuple-element.46), channel_id=1, source_target_pairs={{0,48},{1,49},{16,0},{17,1},{32,16},{33,17},{48,32},{49,33},{4,52}... | collective-permute-start | bytes 491528 | tf_op jit(solution)/shard_map/ppermute | solution.py:39
  29.1 6.9 %collective-permute-start.8 = (bf16[128,640]{1,0:T(8,128)(2,1)S(1)}, bf16[128,640]{1,0:T(8,128)(2,1)S(1)}, u32[]{:S(2)}, u32[]{:S(2)}) collective-permute-start(bf16[128,640]{1,0:T(8,128)(2,1)S(1)} %get-tuple-element.45), channel_id=1, source_target_pairs={{0,16},{1,17},{16,32},{17,33},{32,48},{33,49},{48,0},{49,1},{4,20}... | collective-permute-start | bytes 491528 | tf_op jit(solution)/shard_map/ppermute | solution.py:39
  29.7 9.9 %collective-permute-start.22 = (bf16[128,640]{1,0:T(8,128)(2,1)S(1)}, bf16[128,640]{1,0:T(8,128)(2,1)S(1)}, u32[]{:S(2)}, u32[]{:S(2)}) collective-permute-start(bf16[128,640]{1,0:T(8,128)(2,1)S(1)} %fusion.9), channel_id=1, source_target_pairs={{0,32},{1,9},{16,48},{17,25},{32,0},{33,41},{48,16},{49,57},{4,36}... | collective-permute-start | bytes 491528 | tf_op jit(solution)/shard_map/ppermute | solution.py:39
  32.4 7.9 %collective-permute-start.21 = (bf16[128,640]{1,0:T(8,128)(2,1)S(1)}, bf16[128,640]{1,0:T(8,128)(2,1)S(1)}, u32[]{:S(2)}, u32[]{:S(2)}) collective-permute-start(bf16[128,640]{1,0:T(8,128)(2,1)S(1)} %fusion.9), channel_id=1, source_target_pairs={{0,48},{1,13},{16,0},{17,29},{32,16},{33,45},{48,32},{49,61},{4,52... | collective-permute-start | bytes 491528 | tf_op jit(solution)/shard_map/ppermute | solution.py:39
  33.2 7.1 %collective-permute-start.20 = (bf16[128,640]{1,0:T(8,128)(2,1)S(1)}, bf16[128,640]{1,0:T(8,128)(2,1)S(1)}, u32[]{:S(2)}, u32[]{:S(2)}) collective-permute-start(bf16[128,640]{1,0:T(8,128)(2,1)S(1)} %fusion.9), channel_id=1, source_target_pairs={{0,16},{1,5},{16,32},{17,21},{32,48},{33,37},{48,0},{49,53},{4,20}... | collective-permute-start | bytes 491528 | tf_op jit(solution)/shard_map/ppermute | solution.py:39
  36.0 8.5 %collective-permute-start.13 = (bf16[128,640]{1,0:T(8,128)(2,1)S(1)}, bf16[128,640]{1,0:T(8,128)(2,1)S(1)}, u32[]{:S(2)}, u32[]{:S(2)}) collective-permute-start(bf16[128,640]{1,0:T(8,128)(2,1)S(1)} %fusion.8), channel_id=1, source_target_pairs={{0,64},{1,9},{16,80},{17,25},{32,96},{33,41},{48,112},{49,57},{4,6... | collective-permute-start | bytes 491528 | tf_op jit(solution)/shard_map/ppermute | solution.py:39
  38.8 5.7 %collective-permute-start.12 = (bf16[128,640]{1,0:T(8,128)(2,1)S(1)}, bf16[128,640]{1,0:T(8,128)(2,1)S(1)}, u32[]{:S(2)}, u32[]{:S(2)}) collective-permute-start(bf16[128,640]{1,0:T(8,128)(2,1)S(1)} %fusion.8), channel_id=1, source_target_pairs={{0,66},{1,13},{16,82},{17,29},{32,98},{33,45},{48,114},{49,61},{4,... | collective-permute-start | bytes 491528 | tf_op jit(solution)/shard_map/ppermute | solution.py:39
  39.7 5.6 %collective-permute-start.11 = (bf16[128,640]{1,0:T(8,128)(2,1)S(1)}, bf16[128,640]{1,0:T(8,128)(2,1)S(1)}, u32[]{:S(2)}, u32[]{:S(2)}) collective-permute-start(bf16[128,640]{1,0:T(8,128)(2,1)S(1)} %fusion.8), channel_id=1, source_target_pairs={{0,2},{1,5},{16,18},{17,21},{32,34},{33,37},{48,50},{49,53},{4,6},... | collective-permute-start | bytes 491528 | tf_op jit(solution)/shard_map/ppermute | solution.py:39
  40.5 8.5 %collective-permute-start.23 = (bf16[128,640]{1,0:T(8,128)(2,1)S(1)}, bf16[128,640]{1,0:T(8,128)(2,1)S(1)}, u32[]{:S(2)}, u32[]{:S(2)}) collective-permute-start(bf16[128,640]{1,0:T(8,128)(2,1)S(1)} %add_convert_fusion.refs_4_), channel_id=1, source_target_pairs={{0,2},{1,17},{16,18},{17,33},{32,34},{33,49},{48,50},{49,1},{4,6},... | collective-permute-start | bytes 491528 | tf_op jit(solution)/shard_map/ppermute | solution.py:39
  41.6 7.3 %collective-permute-start.24 = (bf16[128,640]{1,0:T(8,128)(2,1)S(1)}, bf16[128,640]{1,0:T(8,128)(2,1)S(1)}, u32[]{:S(2)}, u32[]{:S(2)}) collective-permute-start(bf16[128,640]{1,0:T(8,128)(2,1)S(1)} %add_convert_fusion.refs_4_), channel_id=1, source_target_pairs={{0,64},{1,33},{16,80},{17,49},{32,96},{33,1},{48,112},{49,17},{4,6... | collective-permute-start | bytes 491528 | tf_op jit(solution)/shard_map/ppermute | solution.py:39
  44.5 4.5 %collective-permute-start.25 = (bf16[128,640]{1,0:T(8,128)(2,1)S(1)}, bf16[128,640]{1,0:T(8,128)(2,1)S(1)}, u32[]{:S(2)}, u32[]{:S(2)}) collective-permute-start(bf16[128,640]{1,0:T(8,128)(2,1)S(1)} %add_convert_fusion.refs_4_), channel_id=1, source_target_pairs={{0,66},{1,49},{16,82},{17,1},{32,98},{33,17},{48,114},{49,33},{4,7... | collective-permute-start | bytes 491528 | tf_op jit(solution)/shard_map/ppermute | solution.py:39
  45.4 5.9 %collective-permute-start.14 = (bf16[128,640]{1,0:T(8,128)(2,1)S(1)}, bf16[128,640]{1,0:T(8,128)(2,1)S(1)}, u32[]{:S(2)}, u32[]{:S(2)}) collective-permute-start(bf16[128,640]{1,0:T(8,128)(2,1)S(1)} %add_convert_fusion.1.refs_0_.piece0), channel_id=1, source_target_pairs={{0,16},{1,17},{16,32},{17,33},{32,48},{33,49},{48,0},{49,1},{4,20}... | collective-permute-start | bytes 491528 | tf_op jit(solution)/shard_map/ppermute | solution.py:39
  46.3 7.2 %collective-permute-start.15 = (bf16[128,640]{1,0:T(8,128)(2,1)S(1)}, bf16[128,640]{1,0:T(8,128)(2,1)S(1)}, u32[]{:S(2)}, u32[]{:S(2)}) collective-permute-start(bf16[128,640]{1,0:T(8,128)(2,1)S(1)} %add_convert_fusion.1.refs_0_.piece0), channel_id=1, source_target_pairs={{0,32},{1,33},{16,48},{17,49},{32,0},{33,1},{48,16},{49,17},{4,36}... | collective-permute-start | bytes 491528 | tf_op jit(solution)/shard_map/ppermute | solution.py:39
  48.9 5.3 %collective-permute-start.16 = (bf16[128,640]{1,0:T(8,128)(2,1)S(1)}, bf16[128,640]{1,0:T(8,128)(2,1)S(1)}, u32[]{:S(2)}, u32[]{:S(2)}) collective-permute-start(bf16[128,640]{1,0:T(8,128)(2,1)S(1)} %add_convert_fusion.1.refs_0_.piece0), channel_id=1, source_target_pairs={{0,48},{1,49},{16,0},{17,1},{32,16},{33,17},{48,32},{49,33},{4,52}... | collective-permute-start | bytes 491528 | tf_op jit(solution)/shard_map/ppermute | solution.py:39
  54.6 6.5 %collective-permute-start.28 = (bf16[192,512]{1,0:T(8,128)(2,1)S(1)}, bf16[192,512]{1,0:T(8,128)(2,1)S(1)}, u32[]{:S(2)}, u32[]{:S(2)}) collective-permute-start(bf16[192,512]{1,0:T(8,128)(2,1)S(1)} %get-tuple-element.58), channel_id=1, source_target_pairs={{0,8},{1,65},{16,24},{17,81},{32,40},{33,97},{48,56},{49,113},{4,1... | collective-permute-start | bytes 589832 | tf_op jit(solution)/shard_map/ppermute | solution.py:39
  58.1 6.0 %collective-permute-start.27 = (bf16[192,512]{1,0:T(8,128)(2,1)S(1)}, bf16[192,512]{1,0:T(8,128)(2,1)S(1)}, u32[]{:S(2)}, u32[]{:S(2)}) collective-permute-start(bf16[192,512]{1,0:T(8,128)(2,1)S(1)} %get-tuple-element.57), channel_id=1, source_target_pairs={{0,4},{1,3},{16,20},{17,19},{32,36},{33,35},{48,52},{49,51},{4,8},... | collective-permute-start | bytes 589832 | tf_op jit(solution)/shard_map/ppermute | solution.py:39
  58.1 6.0 %collective-permute-start.26 = (bf16[192,512]{1,0:T(8,128)(2,1)S(1)}, bf16[192,512]{1,0:T(8,128)(2,1)S(1)}, u32[]{:S(2)}, u32[]{:S(2)}) collective-permute-start(bf16[192,512]{1,0:T(8,128)(2,1)S(1)} %get-tuple-element.56), channel_id=1, source_target_pairs={{0,12},{1,67},{16,28},{17,83},{32,44},{33,99},{48,60},{49,115},{4,... | collective-permute-start | bytes 589832 | tf_op jit(solution)/shard_map/ppermute | solution.py:39
  64.3 6.2 %collective-permute-start.29 = (f32[192]{0:T(256)S(1)}, f32[192]{0:T(256)S(1)}, u32[]{:S(2)}, u32[]{:S(2)}) collective-permute-start(f32[192]{0:T(256)S(1)} %fusion.5), channel_id=1, source_target_pairs={{0,1},{1,0},{2,3},{3,2},{4,5},{5,4},{6,7},{7,6},{8,9},{9,8},{10,11... | collective-permute-start | bytes 2312 | tf_op jit(solution)/shard_map/ppermute | solution.py:43

commit v15 on v14

--- a/solution.py
+++ b/solution.py
@@ -16,6 +16,7 @@
 SECOND = ((Z, Y), (X, Y))
 ORDER = (2, 1, 3)
 SUM = (1, 3, 2)
+BACK = (1, 2, 3)
 LAST = 3
 STRIP = 32
 PARAMS = pltpu.CompilerParams(vmem_limit_bytes=40 * 1024 * 1024)
@@ -275,9 +276,9 @@
         arrived = {by: shifted(sent(by), axis_of_core, sign * by) for by in ORDER}
         return [own] + [arrived[by] for by in (1, 2, 3)]
 
-    def added(total, sent, axis_of_core, sign=1):
+    def added(total, sent, axis_of_core, sign=1, order=SUM):
         arrived = exchanged(None, sent, axis_of_core, sign)
-        for by in SUM:
+        for by in order:
             total = total + arrived[by].astype(F32)
         return total
 
@@ -352,7 +353,7 @@
     )(far[0], *far_weights, sofar)[0]
     norm_f = norm_own.astype(F32)
     grad_n = grad_n + level * norm_f
-    grad_n = coef * added(grad_n, lambda by: parts[by - 1], GATHER, -1)
+    grad_n = coef * added(grad_n, lambda by: parts[by - 1], GATHER, -1, BACK)
     inner = jnp.sum(grad_n * norm_f, axis=1)
     inner = inner + other_core(inner)
     return (grad_n - inner[:, None] * norm_f) * inv_s

time: 71.6 us -> 70.8 us (0.989)
  transfers between devices with their start and end apart: 30 -> 30, of which waited for: 9 -> 10; matrix products, arithmetic and copies ran while one was open for 1% -> 1% of each run, Pallas kernels for 7% -> 8%
where the time goes in v15:
time: 70.8 us; the launch traced here: 70.7 us
  starting transfers between devices  44.8 us (63%)
  waiting for transfers between devices  15.8 us (22%)
  Pallas kernels  6.19 us (9%)
  local copies, waits for them, and re-layouts  2.06 us (3%)
  other arithmetic  1.7 us (2%)
    ppermute x27, starting transfers between devices, shifted(): return lax.ppermute(array, AXES, pairs)  38.1 us
    ppermute x27, waiting for transfers between devices, shifted(): return lax.ppermute(array, AXES, pairs)  15 us
    ppermute x3, starting transfers between devices, other_core(): return lax.ppermute(array, 'sec', [(0, 1), (1, 0)])  6.69 us
    unnamed x4, local copies, waits for them, and re-layouts  2.06 us
  transfers between devices with their start and end apart: 30, of which 10 were waited for; matrix products, arithmetic and copies ran while one was open for 1% of the time, Pallas kernels for 8%

profile of v15, /device:TPU:1, one launch (start us, length us, event | category | flops | bytes accessed | tf_op | source)
XLA Modules:
  0.0 70.7 jit_solution(10455209393815621712)
XLA Ops:
  0.0 1.4 %collective-permute-start.1 = (bf16[192,2048]{1,0:T(8,128)(2,1)}, bf16[192,2048]{1,0:T(8,128)(2,1)S(1)}, u32[]{:S(2)}, u32[]{:S(2)}) collective-permute-start(bf16[192,2048]{1,0:T(8,128)(2,1)} %t_own.3), channel_id=1, source_target_pairs={{0,1},{1,0},{2,3},{3,2},{4,5},{5,4},{6,7},{7,6},{8,9},{9,8},{10,11... | collective-permute-start | bytes 2359304 | tf_op jit(solution)/shard_map/ppermute | solution.py:44
  1.4 1.1 %copy-done = bf16[192,2048]{1,0:T(8,128)(2,1)S(1)} copy-done((bf16[192,2048]{1,0:T(8,128)(2,1)S(1)}, bf16[192,2048]{1,0:T(8,128)(2,1)}, u32[]{:S(2)}) %copy-start) | copy-done | bytes 786456
  2.6 0.9 %copy-done.1 = bf16[192,512]{1,0:T(8,128)(2,1)S(1)} copy-done((bf16[192,512]{1,0:T(8,128)(2,1)S(1)}, bf16[192,512]{1,0:T(8,128)(2,1)}, u32[]{:S(2)}) %copy-start.1) | copy-done | bytes 196632
  3.8 0.5 pack_own.1
  4.3 1.4 %collective-permute-start.4 = (bf16[192,1024]{1,0:T(8,128)(2,1)S(1)}, bf16[192,1024]{1,0:T(8,128)(2,1)S(1)}, u32[]{:S(2)}, u32[]{:S(2)}) collective-permute-start(bf16[192,1024]{1,0:T(8,128)(2,1)S(1)} %get-tuple-element.40), channel_id=1, source_target_pairs={{0,4},{1,3},{16,20},{17,19},{32,36},{33,35},{48,52},{49,51},{4,8},... | collective-permute-start | bytes 1179656 | tf_op jit(solution)/shard_map/ppermute | solution.py:40
  5.7 2.5 %collective-permute-start.5 = (bf16[192,1024]{1,0:T(8,128)(2,1)S(1)}, bf16[192,1024]{1,0:T(8,128)(2,1)S(1)}, u32[]{:S(2)}, u32[]{:S(2)}) collective-permute-start(bf16[192,1024]{1,0:T(8,128)(2,1)S(1)} %get-tuple-element.41), channel_id=1, source_target_pairs={{0,8},{1,65},{16,24},{17,81},{32,40},{33,97},{48,56},{49,113},{4,1... | collective-permute-start | bytes 1179656 | tf_op jit(solution)/shard_map/ppermute | solution.py:40
  8.1 1.2 %collective-permute-start.2 = (bf16[192,1024]{1,0:T(8,128)(2,1)S(1)}, bf16[192,1024]{1,0:T(8,128)(2,1)S(1)}, u32[]{:S(2)}, u32[]{:S(2)}) collective-permute-start(bf16[192,1024]{1,0:T(8,128)(2,1)S(1)} %get-tuple-element.37), channel_id=1, source_target_pairs={{0,12},{1,67},{16,28},{17,83},{32,44},{33,99},{48,60},{49,115},{4,... | collective-permute-start | bytes 1179656 | tf_op jit(solution)/shard_map/ppermute | solution.py:40
  9.3 0.3 pack_far.1
  9.6 0.4 collective-permute-start.6
  10.0 0.9 %collective-permute-start.7 = (bf16[192,640]{1,0:T(8,128)(2,1)S(1)}, bf16[192,640]{1,0:T(8,128)(2,1)S(1)}, u32[]{:S(2)}, u32[]{:S(2)}) collective-permute-start(bf16[192,640]{1,0:T(8,128)(2,1)S(1)} %get-tuple-element.43), channel_id=1, source_target_pairs={{0,8},{1,65},{16,24},{17,81},{32,40},{33,97},{48,56},{49,113},{4,1... | collective-permute-start | bytes 737288 | tf_op jit(solution)/shard_map/ppermute | solution.py:40
  10.8 1.7 %collective-permute-done.4.refs_1_ = bf16[192,1024]{1,0:T(8,128)(2,1)S(1)} collective-permute-done((bf16[192,1024]{1,0:T(8,128)(2,1)S(1)}, bf16[192,1024]{1,0:T(8,128)(2,1)S(1)}, u32[]{:S(2)}, u32[]{:S(2)}) %collective-permute-start.4) | collective-permute-done | bytes 393248 | tf_op jit(solution)/shard_map/ppermute | solution.py:40
  12.5 1.4 %collective-permute-start.3 = (bf16[192,640]{1,0:T(8,128)(2,1)S(1)}, bf16[192,640]{1,0:T(8,128)(2,1)S(1)}, u32[]{:S(2)}, u32[]{:S(2)}) collective-permute-start(bf16[192,640]{1,0:T(8,128)(2,1)S(1)} %get-tuple-element.38), channel_id=1, source_target_pairs={{0,12},{1,67},{16,28},{17,83},{32,44},{33,99},{48,60},{49,115},{4,... | collective-permute-start | bytes 737288 | tf_op jit(solution)/shard_map/ppermute | solution.py:40
  13.9 4.0 %collective-permute-done.5.refs_2_ = bf16[192,1024]{1,0:T(8,128)(2,1)S(1)} collective-permute-done((bf16[192,1024]{1,0:T(8,128)(2,1)S(1)}, bf16[192,1024]{1,0:T(8,128)(2,1)S(1)}, u32[]{:S(2)}, u32[]{:S(2)}) %collective-permute-start.5) | collective-permute-done | bytes 393248 | tf_op jit(solution)/shard_map/ppermute | solution.py:40
  17.9 1.0 %gram_early.1.before = f32[512,640]{1,0:T(8,128)S(1)} custom-call(bf16[192,1024]{1,0:T(8,128)(2,1)S(1)} %get-tuple-element.39.refs_0_, bf16[192,1024]{1,0:T(8,128)(2,1)S(1)} %collective-permute-done.4.refs_1_, bf16[192,1024]{1,0:T(8,128)(2,1)S(1)} %collective-permute-done.5.refs_2_), custom_call_target="tpu_custom_call" | custom-call | flops 503316480 | bytes 4194304 | tf_op jit(solution)/shard_map/gram_early/pallas_call | solution.py:297
  18.9 0.5 gram_native.1
  19.3 3.7 %collective-permute-start.19 = (bf16[128,640]{1,0:T(8,128)(2,1)S(1)}, bf16[128,640]{1,0:T(8,128)(2,1)S(1)}, u32[]{:S(2)}, u32[]{:S(2)}) collective-permute-start(bf16[128,640]{1,0:T(8,128)(2,1)S(1)} %get-tuple-element.51), channel_id=1, source_target_pairs={{0,64},{1,33},{16,80},{17,49},{32,96},{33,1},{48,112},{49,17},{4,6... | collective-permute-start | bytes 491528 | tf_op jit(solution)/shard_map/ppermute | solution.py:40
  23.0 0.4 collective-permute-start.18
  23.4 1.0 %collective-permute-start.17 = (bf16[128,640]{1,0:T(8,128)(2,1)S(1)}, bf16[128,640]{1,0:T(8,128)(2,1)S(1)}, u32[]{:S(2)}, u32[]{:S(2)}) collective-permute-start(bf16[128,640]{1,0:T(8,128)(2,1)S(1)} %get-tuple-element.49), channel_id=1, source_target_pairs={{0,2},{1,17},{16,18},{17,33},{32,34},{33,49},{48,50},{49,1},{4,6},... | collective-permute-start | bytes 491528 | tf_op jit(solution)/shard_map/ppermute | solution.py:40
  24.5 0.9 %gram_far_early.1.before = f32[512,640]{1,0:T(8,128)S(1)} custom-call(bf16[192,1024]{1,0:T(8,128)(2,1)S(1)} %get-tuple-element.39.refs_0_, bf16[192,1024]{1,0:T(8,128)(2,1)S(1)} %collective-permute-done.4.refs_1_, bf16[192,1024]{1,0:T(8,128)(2,1)S(1)} %collective-permute-done.5.refs_2_, bf16[192,640]{1,0:T(8,128)(2,1)S(1)} %get-tuple-element.36.refs_3_.pack, ...), custom_call_target="tpu_custom_call" | custom-call | flops 503316480 | bytes 4194304 | tf_op jit(solution)/shard_map/gram_far_early/pallas_call | solution.py:308
  25.4 0.5 gram_far.1
  25.8 2.3 %collective-permute-start.10 = (bf16[128,640]{1,0:T(8,128)(2,1)S(1)}, bf16[128,640]{1,0:T(8,128)(2,1)S(1)}, u32[]{:S(2)}, u32[]{:S(2)}) collective-permute-start(bf16[128,640]{1,0:T(8,128)(2,1)S(1)} %get-tuple-element.47), channel_id=1, source_target_pairs={{0,32},{1,33},{16,48},{17,49},{32,0},{33,1},{48,16},{49,17},{4,36}... | collective-permute-start | bytes 491528 | tf_op jit(solution)/shard_map/ppermute | solution.py:40
  28.2 0.9 %collective-permute-start.9 = (bf16[128,640]{1,0:T(8,128)(2,1)S(1)}, bf16[128,640]{1,0:T(8,128)(2,1)S(1)}, u32[]{:S(2)}, u32[]{:S(2)}) collective-permute-start(bf16[128,640]{1,0:T(8,128)(2,1)S(1)} %get-tuple-element.46), channel_id=1, source_target_pairs={{0,48},{1,49},{16,0},{17,1},{32,16},{33,17},{48,32},{49,33},{4,52}... | collective-permute-start | bytes 491528 | tf_op jit(solution)/shard_map/ppermute | solution.py:40
  29.1 0.6 collective-permute-start.8
  29.7 2.7 %collective-permute-start.22 = (bf16[128,640]{1,0:T(8,128)(2,1)S(1)}, bf16[128,640]{1,0:T(8,128)(2,1)S(1)}, u32[]{:S(2)}, u32[]{:S(2)}) collective-permute-start(bf16[128,640]{1,0:T(8,128)(2,1)S(1)} %fusion.9), channel_id=1, source_target_pairs={{0,32},{1,9},{16,48},{17,25},{32,0},{33,41},{48,16},{49,57},{4,36}... | collective-permute-start | bytes 491528 | tf_op jit(solution)/shard_map/ppermute | solution.py:40
  32.4 0.8 %collective-permute-start.21 = (bf16[128,640]{1,0:T(8,128)(2,1)S(1)}, bf16[128,640]{1,0:T(8,128)(2,1)S(1)}, u32[]{:S(2)}, u32[]{:S(2)}) collective-permute-start(bf16[128,640]{1,0:T(8,128)(2,1)S(1)} %fusion.9), channel_id=1, source_target_pairs={{0,48},{1,13},{16,0},{17,29},{32,16},{33,45},{48,32},{49,61},{4,52... | collective-permute-start | bytes 491528 | tf_op jit(solution)/shard_map/ppermute | solution.py:40
  33.2 0.7 collective-permute-start.20
  33.9 2.1 %collective-permute-done.8 = bf16[128,640]{1,0:T(8,128)(2,1)S(1)} collective-permute-done((bf16[128,640]{1,0:T(8,128)(2,1)S(1)}, bf16[128,640]{1,0:T(8,128)(2,1)S(1)}, u32[]{:S(2)}, u32[]{:S(2)}) %collective-permute-start.8) | collective-permute-done | bytes 163872 | tf_op jit(solution)/shard_map/ppermute | solution.py:40
  36.0 2.8 %collective-permute-start.13 = (bf16[128,640]{1,0:T(8,128)(2,1)S(1)}, bf16[128,640]{1,0:T(8,128)(2,1)S(1)}, u32[]{:S(2)}, u32[]{:S(2)}) collective-permute-start(bf16[128,640]{1,0:T(8,128)(2,1)S(1)} %fusion.8), channel_id=1, source_target_pairs={{0,64},{1,9},{16,80},{17,25},{32,96},{33,41},{48,112},{49,57},{4,6... | collective-permute-start | bytes 491528 | tf_op jit(solution)/shard_map/ppermute | solution.py:40
  38.8 0.8 %collective-permute-start.12 = (bf16[128,640]{1,0:T(8,128)(2,1)S(1)}, bf16[128,640]{1,0:T(8,128)(2,1)S(1)}, u32[]{:S(2)}, u32[]{:S(2)}) collective-permute-start(bf16[128,640]{1,0:T(8,128)(2,1)S(1)} %fusion.8), channel_id=1, source_target_pairs={{0,66},{1,13},{16,82},{17,29},{32,98},{33,45},{48,114},{49,61},{4,... | collective-permute-start | bytes 491528 | tf_op jit(solution)/shard_map/ppermute | solution.py:40
  39.7 0.7 collective-permute-start.11
  40.5 1.1 %collective-permute-start.23 = (bf16[128,640]{1,0:T(8,128)(2,1)S(1)}, bf16[128,640]{1,0:T(8,128)(2,1)S(1)}, u32[]{:S(2)}, u32[]{:S(2)}) collective-permute-start(bf16[128,640]{1,0:T(8,128)(2,1)S(1)} %add_convert_fusion.refs_4_), channel_id=1, source_target_pairs={{0,2},{1,17},{16,18},{17,33},{32,34},{33,49},{48,50},{49,1},{4,6},... | collective-permute-start | bytes 491528 | tf_op jit(solution)/shard_map/ppermute | solution.py:40
  41.6 2.9 %collective-permute-start.24 = (bf16[128,640]{1,0:T(8,128)(2,1)S(1)}, bf16[128,640]{1,0:T(8,128)(2,1)S(1)}, u32[]{:S(2)}, u32[]{:S(2)}) collective-permute-start(bf16[128,640]{1,0:T(8,128)(2,1)S(1)} %add_convert_fusion.refs_4_), channel_id=1, source_target_pairs={{0,64},{1,33},{16,80},{17,49},{32,96},{33,1},{48,112},{49,17},{4,6... | collective-permute-start | bytes 491528 | tf_op jit(solution)/shard_map/ppermute | solution.py:40
  44.5 0.7 collective-permute-done.11
  45.4 1.0 %collective-permute-start.14 = (bf16[128,640]{1,0:T(8,128)(2,1)S(1)}, bf16[128,640]{1,0:T(8,128)(2,1)S(1)}, u32[]{:S(2)}, u32[]{:S(2)}) collective-permute-start(bf16[128,640]{1,0:T(8,128)(2,1)S(1)} %add_convert_fusion.1.refs_0_.piece0), channel_id=1, source_target_pairs={{0,16},{1,17},{16,32},{17,33},{32,48},{33,49},{48,0},{49,1},{4,20}... | collective-permute-start | bytes 491528 | tf_op jit(solution)/shard_map/ppermute | solution.py:40
  46.3 2.6 %collective-permute-start.15 = (bf16[128,640]{1,0:T(8,128)(2,1)S(1)}, bf16[128,640]{1,0:T(8,128)(2,1)S(1)}, u32[]{:S(2)}, u32[]{:S(2)}) collective-permute-start(bf16[128,640]{1,0:T(8,128)(2,1)S(1)} %add_convert_fusion.1.refs_0_.piece0), channel_id=1, source_target_pairs={{0,32},{1,33},{16,48},{17,49},{32,0},{33,1},{48,16},{49,17},{4,36}... | collective-permute-start | bytes 491528 | tf_op jit(solution)/shard_map/ppermute | solution.py:40
  49.0 0.9 %apply_native.1.refs_4_.before = f32[768,512]{1,0:T(8,128)S(1)} custom-call(bf16[192,1024]{1,0:T(8,128)(2,1)S(1)} %get-tuple-element.39.refs_0_, bf16[192,1024]{1,0:T(8,128)(2,1)S(1)} %collective-permute-done.4.refs_1_, bf16[192,1024]{1,0:T(8,128)(2,1)S(1)} %collective-permute-done.5.refs_2_, bf16[192,1024]{1,0:T(8,128)(2,1)S(1)} %collective-permute-done.2.norm.pack.refs_3_, ...), custom_call_target="tpu_custom_call" | custom-call | flops 503316480 | bytes 4194304 | tf_op jit(solution)/shard_map/apply_native/pallas_call | solution.py:324
  49.8 1.5 %collective-permute-done.14.refs_1_.piece1 = bf16[128,640]{1,0:T(8,128)(2,1)S(1)} collective-permute-done((bf16[128,640]{1,0:T(8,128)(2,1)S(1)}, bf16[128,640]{1,0:T(8,128)(2,1)S(1)}, u32[]{:S(2)}, u32[]{:S(2)}) %collective-permute-start.14) | collective-permute-done | bytes 163872 | tf_op jit(solution)/shard_map/ppermute | solution.py:40
  51.3 2.2 %collective-permute-done.15.refs_2_.piece2 = bf16[128,640]{1,0:T(8,128)(2,1)S(1)} collective-permute-done((bf16[128,640]{1,0:T(8,128)(2,1)S(1)}, bf16[128,640]{1,0:T(8,128)(2,1)S(1)}, u32[]{:S(2)}, u32[]{:S(2)}) %collective-permute-start.15) | collective-permute-done | bytes 163872 | tf_op jit(solution)/shard_map/ppermute | solution.py:40
  53.5 0.7 %apply_early.1 = (bf16[192,512]{1,0:T(8,128)(2,1)S(1)}, bf16[192,512]{1,0:T(8,128)(2,1)S(1)}, bf16[192,512]{1,0:T(8,128)(2,1)S(1)}, bf16[576,640]{1,0:T(8,128)(2,1)S(1)}) custom-call(bf16[192,640]{1,0:T(8,128)(2,1)S(1)} %collective-permute-done.6.refs_4_.far1, bf16[192,640]{1,0:T(8,128)(2,1)S(1)} %collective-permute-done.7.refs_5_.far2, ...), custom_call_target="tpu_custom_call" | custom-call | flops 377487360 | bytes 4194304 | tf_op jit(solution)/shard_map/apply_early/pallas_call | solution.py:334
  54.3 0.4 apply_sent.1
  54.6 0.8 %collective-permute-start.28 = (bf16[192,512]{1,0:T(8,128)(2,1)S(1)}, bf16[192,512]{1,0:T(8,128)(2,1)S(1)}, u32[]{:S(2)}, u32[]{:S(2)}) collective-permute-start(bf16[192,512]{1,0:T(8,128)(2,1)S(1)} %get-tuple-element.58), channel_id=1, source_target_pairs={{0,4},{1,3},{16,20},{17,19},{32,36},{33,35},{48,52},{49,51},{4,8},... | collective-permute-start | bytes 589832 | tf_op jit(solution)/shard_map/ppermute | solution.py:40
  55.4 2.7 %collective-permute-start.27 = (bf16[192,512]{1,0:T(8,128)(2,1)S(1)}, bf16[192,512]{1,0:T(8,128)(2,1)S(1)}, u32[]{:S(2)}, u32[]{:S(2)}) collective-permute-start(bf16[192,512]{1,0:T(8,128)(2,1)S(1)} %get-tuple-element.57), channel_id=1, source_target_pairs={{0,8},{1,65},{16,24},{17,81},{32,40},{33,97},{48,56},{49,113},{4,1... | collective-permute-start | bytes 589832 | tf_op jit(solution)/shard_map/ppermute | solution.py:40
  58.1 2.0 %collective-permute-start.26 = (bf16[192,512]{1,0:T(8,128)(2,1)S(1)}, bf16[192,512]{1,0:T(8,128)(2,1)S(1)}, u32[]{:S(2)}, u32[]{:S(2)}) collective-permute-start(bf16[192,512]{1,0:T(8,128)(2,1)S(1)} %get-tuple-element.56), channel_id=1, source_target_pairs={{0,12},{1,67},{16,28},{17,83},{32,44},{33,99},{48,60},{49,115},{4,... | collective-permute-start | bytes 589832 | tf_op jit(solution)/shard_map/ppermute | solution.py:40
  60.1 0.4 apply_kept.1
  60.6 2.7 %collective-permute-done.27 = bf16[192,512]{1,0:T(8,128)(2,1)S(1)} collective-permute-done((bf16[192,512]{1,0:T(8,128)(2,1)S(1)}, bf16[192,512]{1,0:T(8,128)(2,1)S(1)}, u32[]{:S(2)}, u32[]{:S(2)}) %collective-permute-start.27) | collective-permute-done | bytes 196640 | tf_op jit(solution)/shard_map/ppermute | solution.py:40
  63.6 5.3 %collective-permute-start.29 = (f32[192]{0:T(256)S(1)}, f32[192]{0:T(256)S(1)}, u32[]{:S(2)}, u32[]{:S(2)}) collective-permute-start(f32[192]{0:T(256)S(1)} %fusion.5), channel_id=1, source_target_pairs={{0,1},{1,0},{2,3},{3,2},{4,5},{5,4},{6,7},{7,6},{8,9},{9,8},{10,11... | collective-permute-start | bytes 2312 | tf_op jit(solution)/shard_map/ppermute | solution.py:44
  69.0 0.7 %collective-permute-done.29 = f32[192]{0:T(256)S(1)} collective-permute-done((f32[192]{0:T(256)S(1)}, f32[192]{0:T(256)S(1)}, u32[]{:S(2)}, u32[]{:S(2)}) %collective-permute-start.29) | collective-permute-done | bytes 800 | tf_op jit(solution)/shard_map/ppermute | solution.py:44
  69.7 0.9 %fusion.7 = f32[192,512]{1,0:T(8,128)} fusion(f32[192]{0:T(256)S(1)} %reduce, f32[192]{0:T(256)S(1)} %add.67, bf16[192,1024]{1,0:T(8,128)(2,1)S(1)} %get-tuple-element.39.refs_0_, bf16[192,512]{1,0:T(8,128)(2,1)S(1)} %collective-permute-done.28, bf16[192,512]{1,0:T(8,128)(2,1)S(1)} %collective-permute-done.27, ...), kind=kLoop, calls=%fused_computation.10 | loop fusion | flops 1277952 | bytes 1574400 | tf_op jit(solution)/shard_map/mul | solution.py:359
  (35 shorter events, 1.4 us)
Async XLA Ops:
  0.0 3.8 %collective-permute-start.1 = (bf16[192,2048]{1,0:T(8,128)(2,1)}, bf16[192,2048]{1,0:T(8,128)(2,1)S(1)}, u32[]{:S(2)}, u32[]{:S(2)}) collective-permute-start(bf16[192,2048]{1,0:T(8,128)(2,1)} %t_own.3), channel_id=1, source_target_pairs={{0,1},{1,0},{2,3},{3,2},{4,5},{5,4},{6,7},{7,6},{8,9},{9,8},{10,11... | collective-permute-start | bytes 2359304 | tf_op jit(solution)/shard_map/ppermute | solution.py:44
  1.4 2.4 %collective-permute-start = (bf16[192,512]{1,0:T(8,128)(2,1)}, bf16[192,512]{1,0:T(8,128)(2,1)S(1)}, u32[]{:S(2)}, u32[]{:S(2)}) collective-permute-start(bf16[192,512]{1,0:T(8,128)(2,1)} %s_own.3), channel_id=1, source_target_pairs={{0,1},{1,0},{2,3},{3,2},{4,5},{5,4},{6,7},{7,6},{8,9},{9,8},{10,11... | collective-permute-start | bytes 589832 | tf_op jit(solution)/shard_map/ppermute | solution.py:44
  1.4 1.1 %copy-start = (bf16[192,2048]{1,0:T(8,128)(2,1)S(1)}, bf16[192,2048]{1,0:T(8,128)(2,1)}, u32[]{:S(2)}) copy-start(bf16[192,2048]{1,0:T(8,128)(2,1)} %t_own.3) | copy-start | bytes 2359300
  2.6 0.9 %copy-start.1 = (bf16[192,512]{1,0:T(8,128)(2,1)S(1)}, bf16[192,512]{1,0:T(8,128)(2,1)}, u32[]{:S(2)}) copy-start(bf16[192,512]{1,0:T(8,128)(2,1)} %s_own.3) | copy-start | bytes 589828
  4.3 8.2 %collective-permute-start.4 = (bf16[192,1024]{1,0:T(8,128)(2,1)S(1)}, bf16[192,1024]{1,0:T(8,128)(2,1)S(1)}, u32[]{:S(2)}, u32[]{:S(2)}) collective-permute-start(bf16[192,1024]{1,0:T(8,128)(2,1)S(1)} %get-tuple-element.40), channel_id=1, source_target_pairs={{0,4},{1,3},{16,20},{17,19},{32,36},{33,35},{48,52},{49,51},{4,8},... | collective-permute-start | bytes 1179656 | tf_op jit(solution)/shard_map/ppermute | solution.py:40
  5.7 12.2 %collective-permute-start.5 = (bf16[192,1024]{1,0:T(8,128)(2,1)S(1)}, bf16[192,1024]{1,0:T(8,128)(2,1)S(1)}, u32[]{:S(2)}, u32[]{:S(2)}) collective-permute-start(bf16[192,1024]{1,0:T(8,128)(2,1)S(1)} %get-tuple-element.41), channel_id=1, source_target_pairs={{0,8},{1,65},{16,24},{17,81},{32,40},{33,97},{48,56},{49,113},{4,1... | collective-permute-start | bytes 1179656 | tf_op jit(solution)/shard_map/ppermute | solution.py:40
  8.1 10.7 %collective-permute-start.2 = (bf16[192,1024]{1,0:T(8,128)(2,1)S(1)}, bf16[192,1024]{1,0:T(8,128)(2,1)S(1)}, u32[]{:S(2)}, u32[]{:S(2)}) collective-permute-start(bf16[192,1024]{1,0:T(8,128)(2,1)S(1)} %get-tuple-element.37), channel_id=1, source_target_pairs={{0,12},{1,67},{16,28},{17,83},{32,44},{33,99},{48,60},{49,115},{4,... | collective-permute-start | bytes 1179656 | tf_op jit(solution)/shard_map/ppermute | solution.py:40
  9.6 13.9 %collective-permute-start.6 = (bf16[192,640]{1,0:T(8,128)(2,1)S(1)}, bf16[192,640]{1,0:T(8,128)(2,1)S(1)}, u32[]{:S(2)}, u32[]{:S(2)}) collective-permute-start(bf16[192,640]{1,0:T(8,128)(2,1)S(1)} %get-tuple-element.42), channel_id=1, source_target_pairs={{0,4},{1,3},{16,20},{17,19},{32,36},{33,35},{48,52},{49,51},{4,8},... | collective-permute-start | bytes 737288 | tf_op jit(solution)/shard_map/ppermute | solution.py:40
  10.0 14.5 %collective-permute-start.7 = (bf16[192,640]{1,0:T(8,128)(2,1)S(1)}, bf16[192,640]{1,0:T(8,128)(2,1)S(1)}, u32[]{:S(2)}, u32[]{:S(2)}) collective-permute-start(bf16[192,640]{1,0:T(8,128)(2,1)S(1)} %get-tuple-element.43), channel_id=1, source_target_pairs={{0,8},{1,65},{16,24},{17,81},{32,40},{33,97},{48,56},{49,113},{4,1... | collective-permute-start | bytes 737288 | tf_op jit(solution)/shard_map/ppermute | solution.py:40
  12.5 12.8 %collective-permute-start.3 = (bf16[192,640]{1,0:T(8,128)(2,1)S(1)}, bf16[192,640]{1,0:T(8,128)(2,1)S(1)}, u32[]{:S(2)}, u32[]{:S(2)}) collective-permute-start(bf16[192,640]{1,0:T(8,128)(2,1)S(1)} %get-tuple-element.38), channel_id=1, source_target_pairs={{0,12},{1,67},{16,28},{17,83},{32,44},{33,99},{48,60},{49,115},{4,... | collective-permute-start | bytes 737288 | tf_op jit(solution)/shard_map/ppermute | solution.py:40
  19.3 9.7 %collective-permute-start.19 = (bf16[128,640]{1,0:T(8,128)(2,1)S(1)}, bf16[128,640]{1,0:T(8,128)(2,1)S(1)}, u32[]{:S(2)}, u32[]{:S(2)}) collective-permute-start(bf16[128,640]{1,0:T(8,128)(2,1)S(1)} %get-tuple-element.51), channel_id=1, source_target_pairs={{0,64},{1,33},{16,80},{17,49},{32,96},{33,1},{48,112},{49,17},{4,6... | collective-permute-start | bytes 491528 | tf_op jit(solution)/shard_map/ppermute | solution.py:40
  23.0 6.6 %collective-permute-start.18 = (bf16[128,640]{1,0:T(8,128)(2,1)S(1)}, bf16[128,640]{1,0:T(8,128)(2,1)S(1)}, u32[]{:S(2)}, u32[]{:S(2)}) collective-permute-start(bf16[128,640]{1,0:T(8,128)(2,1)S(1)} %get-tuple-element.50), channel_id=1, source_target_pairs={{0,66},{1,49},{16,82},{17,1},{32,98},{33,17},{48,114},{49,33},{4,7... | collective-permute-start | bytes 491528 | tf_op jit(solution)/shard_map/ppermute | solution.py:40
  23.4 6.2 %collective-permute-start.17 = (bf16[128,640]{1,0:T(8,128)(2,1)S(1)}, bf16[128,640]{1,0:T(8,128)(2,1)S(1)}, u32[]{:S(2)}, u32[]{:S(2)}) collective-permute-start(bf16[128,640]{1,0:T(8,128)(2,1)S(1)} %get-tuple-element.49), channel_id=1, source_target_pairs={{0,2},{1,17},{16,18},{17,33},{32,34},{33,49},{48,50},{49,1},{4,6},... | collective-permute-start | bytes 491528 | tf_op jit(solution)/shard_map/ppermute | solution.py:40
  25.8 7.4 %collective-permute-start.10 = (bf16[128,640]{1,0:T(8,128)(2,1)S(1)}, bf16[128,640]{1,0:T(8,128)(2,1)S(1)}, u32[]{:S(2)}, u32[]{:S(2)}) collective-permute-start(bf16[128,640]{1,0:T(8,128)(2,1)S(1)} %get-tuple-element.47), channel_id=1, source_target_pairs={{0,32},{1,33},{16,48},{17,49},{32,0},{33,1},{48,16},{49,17},{4,36}... | collective-permute-start | bytes 491528 | tf_op jit(solution)/shard_map/ppermute | solution.py:40
  28.2 5.7 %collective-permute-start.9 = (bf16[128,640]{1,0:T(8,128)(2,1)S(1)}, bf16[128,640]{1,0:T(8,128)(2,1)S(1)}, u32[]{:S(2)}, u32[]{:S(2)}) collective-permute-start(bf16[128,640]{1,0:T(8,128)(2,1)S(1)} %get-tuple-element.46), channel_id=1, source_target_pairs={{0,48},{1,49},{16,0},{17,1},{32,16},{33,17},{48,32},{49,33},{4,52}... | collective-permute-start | bytes 491528 | tf_op jit(solution)/shard_map/ppermute | solution.py:40
  29.1 6.9 %collective-permute-start.8 = (bf16[128,640]{1,0:T(8,128)(2,1)S(1)}, bf16[128,640]{1,0:T(8,128)(2,1)S(1)}, u32[]{:S(2)}, u32[]{:S(2)}) collective-permute-start(bf16[128,640]{1,0:T(8,128)(2,1)S(1)} %get-tuple-element.45), channel_id=1, source_target_pairs={{0,16},{1,17},{16,32},{17,33},{32,48},{33,49},{48,0},{49,1},{4,20}... | collective-permute-start | bytes 491528 | tf_op jit(solution)/shard_map/ppermute | solution.py:40
  29.7 9.9 %collective-permute-start.22 = (bf16[128,640]{1,0:T(8,128)(2,1)S(1)}, bf16[128,640]{1,0:T(8,128)(2,1)S(1)}, u32[]{:S(2)}, u32[]{:S(2)}) collective-permute-start(bf16[128,640]{1,0:T(8,128)(2,1)S(1)} %fusion.9), channel_id=1, source_target_pairs={{0,32},{1,9},{16,48},{17,25},{32,0},{33,41},{48,16},{49,57},{4,36}... | collective-permute-start | bytes 491528 | tf_op jit(solution)/shard_map/ppermute | solution.py:40
  32.4 7.9 %collective-permute-start.21 = (bf16[128,640]{1,0:T(8,128)(2,1)S(1)}, bf16[128,640]{1,0:T(8,128)(2,1)S(1)}, u32[]{:S(2)}, u32[]{:S(2)}) collective-permute-start(bf16[128,640]{1,0:T(8,128)(2,1)S(1)} %fusion.9), channel_id=1, source_target_pairs={{0,48},{1,13},{16,0},{17,29},{32,16},{33,45},{48,32},{49,61},{4,52... | collective-permute-start | bytes 491528 | tf_op jit(solution)/shard_map/ppermute | solution.py:40
  33.2 7.1 %collective-permute-start.20 = (bf16[128,640]{1,0:T(8,128)(2,1)S(1)}, bf16[128,640]{1,0:T(8,128)(2,1)S(1)}, u32[]{:S(2)}, u32[]{:S(2)}) collective-permute-start(bf16[128,640]{1,0:T(8,128)(2,1)S(1)} %fusion.9), channel_id=1, source_target_pairs={{0,16},{1,5},{16,32},{17,21},{32,48},{33,37},{48,0},{49,53},{4,20}... | collective-permute-start | bytes 491528 | tf_op jit(solution)/shard_map/ppermute | solution.py:40
  36.0 8.5 %collective-permute-start.13 = (bf16[128,640]{1,0:T(8,128)(2,1)S(1)}, bf16[128,640]{1,0:T(8,128)(2,1)S(1)}, u32[]{:S(2)}, u32[]{:S(2)}) collective-permute-start(bf16[128,640]{1,0:T(8,128)(2,1)S(1)} %fusion.8), channel_id=1, source_target_pairs={{0,64},{1,9},{16,80},{17,25},{32,96},{33,41},{48,112},{49,57},{4,6... | collective-permute-start | bytes 491528 | tf_op jit(solution)/shard_map/ppermute | solution.py:40
  38.8 5.7 %collective-permute-start.12 = (bf16[128,640]{1,0:T(8,128)(2,1)S(1)}, bf16[128,640]{1,0:T(8,128)(2,1)S(1)}, u32[]{:S(2)}, u32[]{:S(2)}) collective-permute-start(bf16[128,640]{1,0:T(8,128)(2,1)S(1)} %fusion.8), channel_id=1, source_target_pairs={{0,66},{1,13},{16,82},{17,29},{32,98},{33,45},{48,114},{49,61},{4,... | collective-permute-start | bytes 491528 | tf_op jit(solution)/shard_map/ppermute | solution.py:40
  39.7 5.6 %collective-permute-start.11 = (bf16[128,640]{1,0:T(8,128)(2,1)S(1)}, bf16[128,640]{1,0:T(8,128)(2,1)S(1)}, u32[]{:S(2)}, u32[]{:S(2)}) collective-permute-start(bf16[128,640]{1,0:T(8,128)(2,1)S(1)} %fusion.8), channel_id=1, source_target_pairs={{0,2},{1,5},{16,18},{17,21},{32,34},{33,37},{48,50},{49,53},{4,6},... | collective-permute-start | bytes 491528 | tf_op jit(solution)/shard_map/ppermute | solution.py:40
  40.5 8.5 %collective-permute-start.23 = (bf16[128,640]{1,0:T(8,128)(2,1)S(1)}, bf16[128,640]{1,0:T(8,128)(2,1)S(1)}, u32[]{:S(2)}, u32[]{:S(2)}) collective-permute-start(bf16[128,640]{1,0:T(8,128)(2,1)S(1)} %add_convert_fusion.refs_4_), channel_id=1, source_target_pairs={{0,2},{1,17},{16,18},{17,33},{32,34},{33,49},{48,50},{49,1},{4,6},... | collective-permute-start | bytes 491528 | tf_op jit(solution)/shard_map/ppermute | solution.py:40
  41.6 7.3 %collective-permute-start.24 = (bf16[128,640]{1,0:T(8,128)(2,1)S(1)}, bf16[128,640]{1,0:T(8,128)(2,1)S(1)}, u32[]{:S(2)}, u32[]{:S(2)}) collective-permute-start(bf16[128,640]{1,0:T(8,128)(2,1)S(1)} %add_convert_fusion.refs_4_), channel_id=1, source_target_pairs={{0,64},{1,33},{16,80},{17,49},{32,96},{33,1},{48,112},{49,17},{4,6... | collective-permute-start | bytes 491528 | tf_op jit(solution)/shard_map/ppermute | solution.py:40
  44.5 4.5 %collective-permute-start.25 = (bf16[128,640]{1,0:T(8,128)(2,1)S(1)}, bf16[128,640]{1,0:T(8,128)(2,1)S(1)}, u32[]{:S(2)}, u32[]{:S(2)}) collective-permute-start(bf16[128,640]{1,0:T(8,128)(2,1)S(1)} %add_convert_fusion.refs_4_), channel_id=1, source_target_pairs={{0,66},{1,49},{16,82},{17,1},{32,98},{33,17},{48,114},{49,33},{4,7... | collective-permute-start | bytes 491528 | tf_op jit(solution)/shard_map/ppermute | solution.py:40
  45.4 5.9 %collective-permute-start.14 = (bf16[128,640]{1,0:T(8,128)(2,1)S(1)}, bf16[128,640]{1,0:T(8,128)(2,1)S(1)}, u32[]{:S(2)}, u32[]{:S(2)}) collective-permute-start(bf16[128,640]{1,0:T(8,128)(2,1)S(1)} %add_convert_fusion.1.refs_0_.piece0), channel_id=1, source_target_pairs={{0,16},{1,17},{16,32},{17,33},{32,48},{33,49},{48,0},{49,1},{4,20}... | collective-permute-start | bytes 491528 | tf_op jit(solution)/shard_map/ppermute | solution.py:40
  46.3 7.2 %collective-permute-start.15 = (bf16[128,640]{1,0:T(8,128)(2,1)S(1)}, bf16[128,640]{1,0:T(8,128)(2,1)S(1)}, u32[]{:S(2)}, u32[]{:S(2)}) collective-permute-start(bf16[128,640]{1,0:T(8,128)(2,1)S(1)} %add_convert_fusion.1.refs_0_.piece0), channel_id=1, source_target_pairs={{0,32},{1,33},{16,48},{17,49},{32,0},{33,1},{48,16},{49,17},{4,36}... | collective-permute-start | bytes 491528 | tf_op jit(solution)/shard_map/ppermute | solution.py:40
  48.9 5.3 %collective-permute-start.16 = (bf16[128,640]{1,0:T(8,128)(2,1)S(1)}, bf16[128,640]{1,0:T(8,128)(2,1)S(1)}, u32[]{:S(2)}, u32[]{:S(2)}) collective-permute-start(bf16[128,640]{1,0:T(8,128)(2,1)S(1)} %add_convert_fusion.1.refs_0_.piece0), channel_id=1, source_target_pairs={{0,48},{1,49},{16,0},{17,1},{32,16},{33,17},{48,32},{49,33},{4,52}... | collective-permute-start | bytes 491528 | tf_op jit(solution)/shard_map/ppermute | solution.py:40
  54.6 5.9 %collective-permute-start.28 = (bf16[192,512]{1,0:T(8,128)(2,1)S(1)}, bf16[192,512]{1,0:T(8,128)(2,1)S(1)}, u32[]{:S(2)}, u32[]{:S(2)}) collective-permute-start(bf16[192,512]{1,0:T(8,128)(2,1)S(1)} %get-tuple-element.58), channel_id=1, source_target_pairs={{0,4},{1,3},{16,20},{17,19},{32,36},{33,35},{48,52},{49,51},{4,8},... | collective-permute-start | bytes 589832 | tf_op jit(solution)/shard_map/ppermute | solution.py:40
  55.4 7.8 %collective-permute-start.27 = (bf16[192,512]{1,0:T(8,128)(2,1)S(1)}, bf16[192,512]{1,0:T(8,128)(2,1)S(1)}, u32[]{:S(2)}, u32[]{:S(2)}) collective-permute-start(bf16[192,512]{1,0:T(8,128)(2,1)S(1)} %get-tuple-element.57), channel_id=1, source_target_pairs={{0,8},{1,65},{16,24},{17,81},{32,40},{33,97},{48,56},{49,113},{4,1... | collective-permute-start | bytes 589832 | tf_op jit(solution)/shard_map/ppermute | solution.py:40
  58.1 5.3 %collective-permute-start.26 = (bf16[192,512]{1,0:T(8,128)(2,1)S(1)}, bf16[192,512]{1,0:T(8,128)(2,1)S(1)}, u32[]{:S(2)}, u32[]{:S(2)}) collective-permute-start(bf16[192,512]{1,0:T(8,128)(2,1)S(1)} %get-tuple-element.56), channel_id=1, source_target_pairs={{0,12},{1,67},{16,28},{17,83},{32,44},{33,99},{48,60},{49,115},{4,... | collective-permute-start | bytes 589832 | tf_op jit(solution)/shard_map/ppermute | solution.py:40
  63.6 6.1 %collective-permute-start.29 = (f32[192]{0:T(256)S(1)}, f32[192]{0:T(256)S(1)}, u32[]{:S(2)}, u32[]{:S(2)}) collective-permute-start(f32[192]{0:T(256)S(1)} %fusion.5), channel_id=1, source_target_pairs={{0,1},{1,0},{2,3},{3,2},{4,5},{5,4},{6,7},{7,6},{8,9},{9,8},{10,11... | collective-permute-start | bytes 2312 | tf_op jit(solution)/shard_map/ppermute | solution.py:44

commit v16 on v15

--- a/solution.py
+++ b/solution.py
@@ -218,7 +218,8 @@
     which = lax.rem(places[2] + SIZE - LAST, SIZE)
     block = pl.ds(pl.multiple_of(which * ss, ss), ss)
     product = times(left[...], piece[...])
-    for k, out in enumerate(outs):
+    for k, (early, out) in enumerate(zip((early1, early2, early3), outs)):
+        out[...] = early[...]
         sofar = before[pl.ds((k + 1) * rows, rows), block]
         out[:, block] = (product[k * rows : (k + 1) * rows] + sofar).astype(out.dtype)
 
@@ -234,14 +235,13 @@
     return [jax.ShapeDtypeStruct(shape, dtype) for shape, dtype in described]
 
 
-def kernel_call(kernel, name, outs, n_in, scratch=(), flops=0, aliases=None):
+def kernel_call(kernel, name, outs, n_in, scratch=(), flops=0):
     return pl.pallas_call(
         kernel,
         out_shape=outs,
         in_specs=[WHOLE] * n_in,
         out_specs=[WHOLE] * len(outs),
         scratch_shapes=list(scratch),
-        input_output_aliases=aliases or {},
         compiler_params=PARAMS,
         cost_estimate=pl.CostEstimate(flops=flops, bytes_accessed=4 << 20, transcendentals=0),
         name=name,
@@ -346,7 +346,6 @@
         6,
         (),
         flops // 4,
-        {3 + k: k for k in range(3)},
     )(stacked, far_weights[LAST], sofar, *most)
     grad_n = kernel_call(
         apply_kept_kernel, "apply_kept", shapes(((rows, half), F32)), SIZE + 2, [weights], flops // 4

time: 70.8 us -> 70.8 us (level)
  no operation moved by 1% of the time
where the time goes in v16:
time: 70.8 us; the launch traced here: 70.7 us
  starting transfers between devices  44.8 us (63%)
  waiting for transfers between devices  15.8 us (22%)
  Pallas kernels  6.19 us (9%)
  local copies, waits for them, and re-layouts  2.06 us (3%)
  other arithmetic  1.7 us (2%)
    ppermute x27, starting transfers between devices, shifted(): return lax.ppermute(array, AXES, pairs)  38.1 us
    ppermute x27, waiting for transfers between devices, shifted(): return lax.ppermute(array, AXES, pairs)  15 us
    ppermute x3, starting transfers between devices, other_core(): return lax.ppermute(array, 'sec', [(0, 1), (1, 0)])  6.69 us
    unnamed x4, local copies, waits for them, and re-layouts  2.06 us
  transfers between devices with their start and end apart: 30, of which 10 were waited for; matrix products, arithmetic and copies ran while one was open for 1% of the time, Pallas kernels for 8%

profile of v16, /device:TPU:1, one launch (start us, length us, event | category | flops | bytes accessed | tf_op | source)
XLA Modules:
  0.0 70.7 jit_solution(2879398203831545195)
XLA Ops:
  0.0 1.4 %collective-permute-start.1 = (bf16[192,2048]{1,0:T(8,128)(2,1)}, bf16[192,2048]{1,0:T(8,128)(2,1)S(1)}, u32[]{:S(2)}, u32[]{:S(2)}) collective-permute-start(bf16[192,2048]{1,0:T(8,128)(2,1)} %t_own.3), channel_id=1, source_target_pairs={{0,1},{1,0},{2,3},{3,2},{4,5},{5,4},{6,7},{7,6},{8,9},{9,8},{10,11... | collective-permute-start | bytes 2359304 | tf_op jit(solution)/shard_map/ppermute | solution.py:44
  1.4 1.1 %copy-done = bf16[192,2048]{1,0:T(8,128)(2,1)S(1)} copy-done((bf16[192,2048]{1,0:T(8,128)(2,1)S(1)}, bf16[192,2048]{1,0:T(8,128)(2,1)}, u32[]{:S(2)}) %copy-start) | copy-done | bytes 786456
  2.6 0.9 %copy-done.1 = bf16[192,512]{1,0:T(8,128)(2,1)S(1)} copy-done((bf16[192,512]{1,0:T(8,128)(2,1)S(1)}, bf16[192,512]{1,0:T(8,128)(2,1)}, u32[]{:S(2)}) %copy-start.1) | copy-done | bytes 196632
  3.8 0.5 pack_own.1
  4.3 1.4 %collective-permute-start.4 = (bf16[192,1024]{1,0:T(8,128)(2,1)S(1)}, bf16[192,1024]{1,0:T(8,128)(2,1)S(1)}, u32[]{:S(2)}, u32[]{:S(2)}) collective-permute-start(bf16[192,1024]{1,0:T(8,128)(2,1)S(1)} %get-tuple-element.40), channel_id=1, source_target_pairs={{0,4},{1,3},{16,20},{17,19},{32,36},{33,35},{48,52},{49,51},{4,8},... | collective-permute-start | bytes 1179656 | tf_op jit(solution)/shard_map/ppermute | solution.py:40
  5.7 2.5 %collective-permute-start.5 = (bf16[192,1024]{1,0:T(8,128)(2,1)S(1)}, bf16[192,1024]{1,0:T(8,128)(2,1)S(1)}, u32[]{:S(2)}, u32[]{:S(2)}) collective-permute-start(bf16[192,1024]{1,0:T(8,128)(2,1)S(1)} %get-tuple-element.41), channel_id=1, source_target_pairs={{0,8},{1,65},{16,24},{17,81},{32,40},{33,97},{48,56},{49,113},{4,1... | collective-permute-start | bytes 1179656 | tf_op jit(solution)/shard_map/ppermute | solution.py:40
  8.1 1.2 %collective-permute-start.2 = (bf16[192,1024]{1,0:T(8,128)(2,1)S(1)}, bf16[192,1024]{1,0:T(8,128)(2,1)S(1)}, u32[]{:S(2)}, u32[]{:S(2)}) collective-permute-start(bf16[192,1024]{1,0:T(8,128)(2,1)S(1)} %get-tuple-element.37), channel_id=1, source_target_pairs={{0,12},{1,67},{16,28},{17,83},{32,44},{33,99},{48,60},{49,115},{4,... | collective-permute-start | bytes 1179656 | tf_op jit(solution)/shard_map/ppermute | solution.py:40
  9.3 0.3 pack_far.1
  9.6 0.4 collective-permute-start.6
  10.0 0.9 %collective-permute-start.7 = (bf16[192,640]{1,0:T(8,128)(2,1)S(1)}, bf16[192,640]{1,0:T(8,128)(2,1)S(1)}, u32[]{:S(2)}, u32[]{:S(2)}) collective-permute-start(bf16[192,640]{1,0:T(8,128)(2,1)S(1)} %get-tuple-element.43), channel_id=1, source_target_pairs={{0,8},{1,65},{16,24},{17,81},{32,40},{33,97},{48,56},{49,113},{4,1... | collective-permute-start | bytes 737288 | tf_op jit(solution)/shard_map/ppermute | solution.py:40
  10.8 1.7 %collective-permute-done.4.refs_1_ = bf16[192,1024]{1,0:T(8,128)(2,1)S(1)} collective-permute-done((bf16[192,1024]{1,0:T(8,128)(2,1)S(1)}, bf16[192,1024]{1,0:T(8,128)(2,1)S(1)}, u32[]{:S(2)}, u32[]{:S(2)}) %collective-permute-start.4) | collective-permute-done | bytes 393248 | tf_op jit(solution)/shard_map/ppermute | solution.py:40
  12.5 1.4 %collective-permute-start.3 = (bf16[192,640]{1,0:T(8,128)(2,1)S(1)}, bf16[192,640]{1,0:T(8,128)(2,1)S(1)}, u32[]{:S(2)}, u32[]{:S(2)}) collective-permute-start(bf16[192,640]{1,0:T(8,128)(2,1)S(1)} %get-tuple-element.38), channel_id=1, source_target_pairs={{0,12},{1,67},{16,28},{17,83},{32,44},{33,99},{48,60},{49,115},{4,... | collective-permute-start | bytes 737288 | tf_op jit(solution)/shard_map/ppermute | solution.py:40
  13.9 4.0 %collective-permute-done.5.refs_2_ = bf16[192,1024]{1,0:T(8,128)(2,1)S(1)} collective-permute-done((bf16[192,1024]{1,0:T(8,128)(2,1)S(1)}, bf16[192,1024]{1,0:T(8,128)(2,1)S(1)}, u32[]{:S(2)}, u32[]{:S(2)}) %collective-permute-start.5) | collective-permute-done | bytes 393248 | tf_op jit(solution)/shard_map/ppermute | solution.py:40
  17.9 1.0 %gram_early.1.before = f32[512,640]{1,0:T(8,128)S(1)} custom-call(bf16[192,1024]{1,0:T(8,128)(2,1)S(1)} %get-tuple-element.39.refs_0_, bf16[192,1024]{1,0:T(8,128)(2,1)S(1)} %collective-permute-done.4.refs_1_, bf16[192,1024]{1,0:T(8,128)(2,1)S(1)} %collective-permute-done.5.refs_2_), custom_call_target="tpu_custom_call" | custom-call | flops 503316480 | bytes 4194304 | tf_op jit(solution)/shard_map/gram_early/pallas_call | solution.py:297
  18.9 0.5 gram_native.1
  19.3 3.7 %collective-permute-start.19 = (bf16[128,640]{1,0:T(8,128)(2,1)S(1)}, bf16[128,640]{1,0:T(8,128)(2,1)S(1)}, u32[]{:S(2)}, u32[]{:S(2)}) collective-permute-start(bf16[128,640]{1,0:T(8,128)(2,1)S(1)} %get-tuple-element.51), channel_id=1, source_target_pairs={{0,64},{1,33},{16,80},{17,49},{32,96},{33,1},{48,112},{49,17},{4,6... | collective-permute-start | bytes 491528 | tf_op jit(solution)/shard_map/ppermute | solution.py:40
  23.0 0.4 collective-permute-start.18
  23.4 1.0 %collective-permute-start.17 = (bf16[128,640]{1,0:T(8,128)(2,1)S(1)}, bf16[128,640]{1,0:T(8,128)(2,1)S(1)}, u32[]{:S(2)}, u32[]{:S(2)}) collective-permute-start(bf16[128,640]{1,0:T(8,128)(2,1)S(1)} %get-tuple-element.49), channel_id=1, source_target_pairs={{0,2},{1,17},{16,18},{17,33},{32,34},{33,49},{48,50},{49,1},{4,6},... | collective-permute-start | bytes 491528 | tf_op jit(solution)/shard_map/ppermute | solution.py:40
  24.5 0.9 %gram_far_early.1.before = f32[512,640]{1,0:T(8,128)S(1)} custom-call(bf16[192,1024]{1,0:T(8,128)(2,1)S(1)} %get-tuple-element.39.refs_0_, bf16[192,1024]{1,0:T(8,128)(2,1)S(1)} %collective-permute-done.4.refs_1_, bf16[192,1024]{1,0:T(8,128)(2,1)S(1)} %collective-permute-done.5.refs_2_, bf16[192,640]{1,0:T(8,128)(2,1)S(1)} %get-tuple-element.36.refs_3_.pack, ...), custom_call_target="tpu_custom_call" | custom-call | flops 503316480 | bytes 4194304 | tf_op jit(solution)/shard_map/gram_far_early/pallas_call | solution.py:308
  25.4 0.5 gram_far.1
  25.8 2.3 %collective-permute-start.10 = (bf16[128,640]{1,0:T(8,128)(2,1)S(1)}, bf16[128,640]{1,0:T(8,128)(2,1)S(1)}, u32[]{:S(2)}, u32[]{:S(2)}) collective-permute-start(bf16[128,640]{1,0:T(8,128)(2,1)S(1)} %get-tuple-element.47), channel_id=1, source_target_pairs={{0,32},{1,33},{16,48},{17,49},{32,0},{33,1},{48,16},{49,17},{4,36}... | collective-permute-start | bytes 491528 | tf_op jit(solution)/shard_map/ppermute | solution.py:40
  28.2 0.9 %collective-permute-start.9 = (bf16[128,640]{1,0:T(8,128)(2,1)S(1)}, bf16[128,640]{1,0:T(8,128)(2,1)S(1)}, u32[]{:S(2)}, u32[]{:S(2)}) collective-permute-start(bf16[128,640]{1,0:T(8,128)(2,1)S(1)} %get-tuple-element.46), channel_id=1, source_target_pairs={{0,48},{1,49},{16,0},{17,1},{32,16},{33,17},{48,32},{49,33},{4,52}... | collective-permute-start | bytes 491528 | tf_op jit(solution)/shard_map/ppermute | solution.py:40
  29.1 0.6 collective-permute-start.8
  29.7 2.7 %collective-permute-start.22 = (bf16[128,640]{1,0:T(8,128)(2,1)S(1)}, bf16[128,640]{1,0:T(8,128)(2,1)S(1)}, u32[]{:S(2)}, u32[]{:S(2)}) collective-permute-start(bf16[128,640]{1,0:T(8,128)(2,1)S(1)} %fusion.9), channel_id=1, source_target_pairs={{0,32},{1,9},{16,48},{17,25},{32,0},{33,41},{48,16},{49,57},{4,36}... | collective-permute-start | bytes 491528 | tf_op jit(solution)/shard_map/ppermute | solution.py:40
  32.4 0.8 %collective-permute-start.21 = (bf16[128,640]{1,0:T(8,128)(2,1)S(1)}, bf16[128,640]{1,0:T(8,128)(2,1)S(1)}, u32[]{:S(2)}, u32[]{:S(2)}) collective-permute-start(bf16[128,640]{1,0:T(8,128)(2,1)S(1)} %fusion.9), channel_id=1, source_target_pairs={{0,48},{1,13},{16,0},{17,29},{32,16},{33,45},{48,32},{49,61},{4,52... | collective-permute-start | bytes 491528 | tf_op jit(solution)/shard_map/ppermute | solution.py:40
  33.2 0.7 collective-permute-start.20
  33.9 2.1 %collective-permute-done.8 = bf16[128,640]{1,0:T(8,128)(2,1)S(1)} collective-permute-done((bf16[128,640]{1,0:T(8,128)(2,1)S(1)}, bf16[128,640]{1,0:T(8,128)(2,1)S(1)}, u32[]{:S(2)}, u32[]{:S(2)}) %collective-permute-start.8) | collective-permute-done | bytes 163872 | tf_op jit(solution)/shard_map/ppermute | solution.py:40
  36.0 2.8 %collective-permute-start.13 = (bf16[128,640]{1,0:T(8,128)(2,1)S(1)}, bf16[128,640]{1,0:T(8,128)(2,1)S(1)}, u32[]{:S(2)}, u32[]{:S(2)}) collective-permute-start(bf16[128,640]{1,0:T(8,128)(2,1)S(1)} %fusion.8), channel_id=1, source_target_pairs={{0,64},{1,9},{16,80},{17,25},{32,96},{33,41},{48,112},{49,57},{4,6... | collective-permute-start | bytes 491528 | tf_op jit(solution)/shard_map/ppermute | solution.py:40
  38.8 0.8 %collective-permute-start.12 = (bf16[128,640]{1,0:T(8,128)(2,1)S(1)}, bf16[128,640]{1,0:T(8,128)(2,1)S(1)}, u32[]{:S(2)}, u32[]{:S(2)}) collective-permute-start(bf16[128,640]{1,0:T(8,128)(2,1)S(1)} %fusion.8), channel_id=1, source_target_pairs={{0,66},{1,13},{16,82},{17,29},{32,98},{33,45},{48,114},{49,61},{4,... | collective-permute-start | bytes 491528 | tf_op jit(solution)/shard_map/ppermute | solution.py:40
  39.7 0.7 collective-permute-start.11
  40.5 1.1 %collective-permute-start.23 = (bf16[128,640]{1,0:T(8,128)(2,1)S(1)}, bf16[128,640]{1,0:T(8,128)(2,1)S(1)}, u32[]{:S(2)}, u32[]{:S(2)}) collective-permute-start(bf16[128,640]{1,0:T(8,128)(2,1)S(1)} %add_convert_fusion.refs_4_), channel_id=1, source_target_pairs={{0,2},{1,17},{16,18},{17,33},{32,34},{33,49},{48,50},{49,1},{4,6},... | collective-permute-start | bytes 491528 | tf_op jit(solution)/shard_map/ppermute | solution.py:40
  41.6 2.9 %collective-permute-start.24 = (bf16[128,640]{1,0:T(8,128)(2,1)S(1)}, bf16[128,640]{1,0:T(8,128)(2,1)S(1)}, u32[]{:S(2)}, u32[]{:S(2)}) collective-permute-start(bf16[128,640]{1,0:T(8,128)(2,1)S(1)} %add_convert_fusion.refs_4_), channel_id=1, source_target_pairs={{0,64},{1,33},{16,80},{17,49},{32,96},{33,1},{48,112},{49,17},{4,6... | collective-permute-start | bytes 491528 | tf_op jit(solution)/shard_map/ppermute | solution.py:40
  44.5 0.7 collective-permute-done.11
  45.4 1.0 %collective-permute-start.14 = (bf16[128,640]{1,0:T(8,128)(2,1)S(1)}, bf16[128,640]{1,0:T(8,128)(2,1)S(1)}, u32[]{:S(2)}, u32[]{:S(2)}) collective-permute-start(bf16[128,640]{1,0:T(8,128)(2,1)S(1)} %add_convert_fusion.1.refs_0_.piece0), channel_id=1, source_target_pairs={{0,16},{1,17},{16,32},{17,33},{32,48},{33,49},{48,0},{49,1},{4,20}... | collective-permute-start | bytes 491528 | tf_op jit(solution)/shard_map/ppermute | solution.py:40
  46.3 2.6 %collective-permute-start.15 = (bf16[128,640]{1,0:T(8,128)(2,1)S(1)}, bf16[128,640]{1,0:T(8,128)(2,1)S(1)}, u32[]{:S(2)}, u32[]{:S(2)}) collective-permute-start(bf16[128,640]{1,0:T(8,128)(2,1)S(1)} %add_convert_fusion.1.refs_0_.piece0), channel_id=1, source_target_pairs={{0,32},{1,33},{16,48},{17,49},{32,0},{33,1},{48,16},{49,17},{4,36}... | collective-permute-start | bytes 491528 | tf_op jit(solution)/shard_map/ppermute | solution.py:40
  49.0 0.9 %apply_native.1.refs_4_.before = f32[768,512]{1,0:T(8,128)S(1)} custom-call(bf16[192,1024]{1,0:T(8,128)(2,1)S(1)} %get-tuple-element.39.refs_0_, bf16[192,1024]{1,0:T(8,128)(2,1)S(1)} %collective-permute-done.4.refs_1_, bf16[192,1024]{1,0:T(8,128)(2,1)S(1)} %collective-permute-done.5.refs_2_, bf16[192,1024]{1,0:T(8,128)(2,1)S(1)} %collective-permute-done.2.norm.pack.refs_3_, ...), custom_call_target="tpu_custom_call" | custom-call | flops 503316480 | bytes 4194304 | tf_op jit(solution)/shard_map/apply_native/pallas_call | solution.py:324
  49.8 1.5 %collective-permute-done.14.refs_1_.piece1 = bf16[128,640]{1,0:T(8,128)(2,1)S(1)} collective-permute-done((bf16[128,640]{1,0:T(8,128)(2,1)S(1)}, bf16[128,640]{1,0:T(8,128)(2,1)S(1)}, u32[]{:S(2)}, u32[]{:S(2)}) %collective-permute-start.14) | collective-permute-done | bytes 163872 | tf_op jit(solution)/shard_map/ppermute | solution.py:40
  51.3 2.2 %collective-permute-done.15.refs_2_.piece2 = bf16[128,640]{1,0:T(8,128)(2,1)S(1)} collective-permute-done((bf16[128,640]{1,0:T(8,128)(2,1)S(1)}, bf16[128,640]{1,0:T(8,128)(2,1)S(1)}, u32[]{:S(2)}, u32[]{:S(2)}) %collective-permute-start.15) | collective-permute-done | bytes 163872 | tf_op jit(solution)/shard_map/ppermute | solution.py:40
  53.5 0.7 %apply_early.1 = (bf16[192,512]{1,0:T(8,128)(2,1)S(1)}, bf16[192,512]{1,0:T(8,128)(2,1)S(1)}, bf16[192,512]{1,0:T(8,128)(2,1)S(1)}, bf16[576,640]{1,0:T(8,128)(2,1)S(1)}) custom-call(bf16[192,640]{1,0:T(8,128)(2,1)S(1)} %collective-permute-done.6.refs_4_.far1, bf16[192,640]{1,0:T(8,128)(2,1)S(1)} %collective-permute-done.7.refs_5_.far2, ...), custom_call_target="tpu_custom_call" | custom-call | flops 377487360 | bytes 4194304 | tf_op jit(solution)/shard_map/apply_early/pallas_call | solution.py:334
  54.3 0.4 apply_sent.1
  54.6 0.8 %collective-permute-start.28 = (bf16[192,512]{1,0:T(8,128)(2,1)S(1)}, bf16[192,512]{1,0:T(8,128)(2,1)S(1)}, u32[]{:S(2)}, u32[]{:S(2)}) collective-permute-start(bf16[192,512]{1,0:T(8,128)(2,1)S(1)} %get-tuple-element.58), channel_id=1, source_target_pairs={{0,4},{1,3},{16,20},{17,19},{32,36},{33,35},{48,52},{49,51},{4,8},... | collective-permute-start | bytes 589832 | tf_op jit(solution)/shard_map/ppermute | solution.py:40
  55.4 2.7 %collective-permute-start.27 = (bf16[192,512]{1,0:T(8,128)(2,1)S(1)}, bf16[192,512]{1,0:T(8,128)(2,1)S(1)}, u32[]{:S(2)}, u32[]{:S(2)}) collective-permute-start(bf16[192,512]{1,0:T(8,128)(2,1)S(1)} %get-tuple-element.57), channel_id=1, source_target_pairs={{0,8},{1,65},{16,24},{17,81},{32,40},{33,97},{48,56},{49,113},{4,1... | collective-permute-start | bytes 589832 | tf_op jit(solution)/shard_map/ppermute | solution.py:40
  58.1 2.0 %collective-permute-start.26 = (bf16[192,512]{1,0:T(8,128)(2,1)S(1)}, bf16[192,512]{1,0:T(8,128)(2,1)S(1)}, u32[]{:S(2)}, u32[]{:S(2)}) collective-permute-start(bf16[192,512]{1,0:T(8,128)(2,1)S(1)} %get-tuple-element.56), channel_id=1, source_target_pairs={{0,12},{1,67},{16,28},{17,83},{32,44},{33,99},{48,60},{49,115},{4,... | collective-permute-start | bytes 589832 | tf_op jit(solution)/shard_map/ppermute | solution.py:40
  60.1 0.4 apply_kept.1
  60.6 2.7 %collective-permute-done.27 = bf16[192,512]{1,0:T(8,128)(2,1)S(1)} collective-permute-done((bf16[192,512]{1,0:T(8,128)(2,1)S(1)}, bf16[192,512]{1,0:T(8,128)(2,1)S(1)}, u32[]{:S(2)}, u32[]{:S(2)}) %collective-permute-start.27) | collective-permute-done | bytes 196640 | tf_op jit(solution)/shard_map/ppermute | solution.py:40
  63.6 5.3 %collective-permute-start.29 = (f32[192]{0:T(256)S(1)}, f32[192]{0:T(256)S(1)}, u32[]{:S(2)}, u32[]{:S(2)}) collective-permute-start(f32[192]{0:T(256)S(1)} %fusion.5), channel_id=1, source_target_pairs={{0,1},{1,0},{2,3},{3,2},{4,5},{5,4},{6,7},{7,6},{8,9},{9,8},{10,11... | collective-permute-start | bytes 2312 | tf_op jit(solution)/shard_map/ppermute | solution.py:44
  69.0 0.7 %collective-permute-done.29 = f32[192]{0:T(256)S(1)} collective-permute-done((f32[192]{0:T(256)S(1)}, f32[192]{0:T(256)S(1)}, u32[]{:S(2)}, u32[]{:S(2)}) %collective-permute-start.29) | collective-permute-done | bytes 800 | tf_op jit(solution)/shard_map/ppermute | solution.py:44
  69.7 0.9 %fusion.7 = f32[192,512]{1,0:T(8,128)} fusion(f32[192]{0:T(256)S(1)} %reduce, f32[192]{0:T(256)S(1)} %add.67, bf16[192,1024]{1,0:T(8,128)(2,1)S(1)} %get-tuple-element.39.refs_0_, bf16[192,512]{1,0:T(8,128)(2,1)S(1)} %collective-permute-done.28, bf16[192,512]{1,0:T(8,128)(2,1)S(1)} %collective-permute-done.27, ...), kind=kLoop, calls=%fused_computation.10 | loop fusion | flops 1277952 | bytes 1574400 | tf_op jit(solution)/shard_map/mul | solution.py:358
  (35 shorter events, 1.4 us)
Async XLA Ops:
  0.0 3.8 %collective-permute-start.1 = (bf16[192,2048]{1,0:T(8,128)(2,1)}, bf16[192,2048]{1,0:T(8,128)(2,1)S(1)}, u32[]{:S(2)}, u32[]{:S(2)}) collective-permute-start(bf16[192,2048]{1,0:T(8,128)(2,1)} %t_own.3), channel_id=1, source_target_pairs={{0,1},{1,0},{2,3},{3,2},{4,5},{5,4},{6,7},{7,6},{8,9},{9,8},{10,11... | collective-permute-start | bytes 2359304 | tf_op jit(solution)/shard_map/ppermute | solution.py:44
  1.4 2.4 %collective-permute-start = (bf16[192,512]{1,0:T(8,128)(2,1)}, bf16[192,512]{1,0:T(8,128)(2,1)S(1)}, u32[]{:S(2)}, u32[]{:S(2)}) collective-permute-start(bf16[192,512]{1,0:T(8,128)(2,1)} %s_own.3), channel_id=1, source_target_pairs={{0,1},{1,0},{2,3},{3,2},{4,5},{5,4},{6,7},{7,6},{8,9},{9,8},{10,11... | collective-permute-start | bytes 589832 | tf_op jit(solution)/shard_map/ppermute | solution.py:44
  1.4 1.1 %copy-start = (bf16[192,2048]{1,0:T(8,128)(2,1)S(1)}, bf16[192,2048]{1,0:T(8,128)(2,1)}, u32[]{:S(2)}) copy-start(bf16[192,2048]{1,0:T(8,128)(2,1)} %t_own.3) | copy-start | bytes 2359300
  2.6 0.9 %copy-start.1 = (bf16[192,512]{1,0:T(8,128)(2,1)S(1)}, bf16[192,512]{1,0:T(8,128)(2,1)}, u32[]{:S(2)}) copy-start(bf16[192,512]{1,0:T(8,128)(2,1)} %s_own.3) | copy-start | bytes 589828
  4.3 8.2 %collective-permute-start.4 = (bf16[192,1024]{1,0:T(8,128)(2,1)S(1)}, bf16[192,1024]{1,0:T(8,128)(2,1)S(1)}, u32[]{:S(2)}, u32[]{:S(2)}) collective-permute-start(bf16[192,1024]{1,0:T(8,128)(2,1)S(1)} %get-tuple-element.40), channel_id=1, source_target_pairs={{0,4},{1,3},{16,20},{17,19},{32,36},{33,35},{48,52},{49,51},{4,8},... | collective-permute-start | bytes 1179656 | tf_op jit(solution)/shard_map/ppermute | solution.py:40
  5.7 12.2 %collective-permute-start.5 = (bf16[192,1024]{1,0:T(8,128)(2,1)S(1)}, bf16[192,1024]{1,0:T(8,128)(2,1)S(1)}, u32[]{:S(2)}, u32[]{:S(2)}) collective-permute-start(bf16[192,1024]{1,0:T(8,128)(2,1)S(1)} %get-tuple-element.41), channel_id=1, source_target_pairs={{0,8},{1,65},{16,24},{17,81},{32,40},{33,97},{48,56},{49,113},{4,1... | collective-permute-start | bytes 1179656 | tf_op jit(solution)/shard_map/ppermute | solution.py:40
  8.1 10.7 %collective-permute-start.2 = (bf16[192,1024]{1,0:T(8,128)(2,1)S(1)}, bf16[192,1024]{1,0:T(8,128)(2,1)S(1)}, u32[]{:S(2)}, u32[]{:S(2)}) collective-permute-start(bf16[192,1024]{1,0:T(8,128)(2,1)S(1)} %get-tuple-element.37), channel_id=1, source_target_pairs={{0,12},{1,67},{16,28},{17,83},{32,44},{33,99},{48,60},{49,115},{4,... | collective-permute-start | bytes 1179656 | tf_op jit(solution)/shard_map/ppermute | solution.py:40
  9.6 13.9 %collective-permute-start.6 = (bf16[192,640]{1,0:T(8,128)(2,1)S(1)}, bf16[192,640]{1,0:T(8,128)(2,1)S(1)}, u32[]{:S(2)}, u32[]{:S(2)}) collective-permute-start(bf16[192,640]{1,0:T(8,128)(2,1)S(1)} %get-tuple-element.42), channel_id=1, source_target_pairs={{0,4},{1,3},{16,20},{17,19},{32,36},{33,35},{48,52},{49,51},{4,8},... | collective-permute-start | bytes 737288 | tf_op jit(solution)/shard_map/ppermute | solution.py:40
  10.0 14.5 %collective-permute-start.7 = (bf16[192,640]{1,0:T(8,128)(2,1)S(1)}, bf16[192,640]{1,0:T(8,128)(2,1)S(1)}, u32[]{:S(2)}, u32[]{:S(2)}) collective-permute-start(bf16[192,640]{1,0:T(8,128)(2,1)S(1)} %get-tuple-element.43), channel_id=1, source_target_pairs={{0,8},{1,65},{16,24},{17,81},{32,40},{33,97},{48,56},{49,113},{4,1... | collective-permute-start | bytes 737288 | tf_op jit(solution)/shard_map/ppermute | solution.py:40
  12.5 12.8 %collective-permute-start.3 = (bf16[192,640]{1,0:T(8,128)(2,1)S(1)}, bf16[192,640]{1,0:T(8,128)(2,1)S(1)}, u32[]{:S(2)}, u32[]{:S(2)}) collective-permute-start(bf16[192,640]{1,0:T(8,128)(2,1)S(1)} %get-tuple-element.38), channel_id=1, source_target_pairs={{0,12},{1,67},{16,28},{17,83},{32,44},{33,99},{48,60},{49,115},{4,... | collective-permute-start | bytes 737288 | tf_op jit(solution)/shard_map/ppermute | solution.py:40
  19.3 9.7 %collective-permute-start.19 = (bf16[128,640]{1,0:T(8,128)(2,1)S(1)}, bf16[128,640]{1,0:T(8,128)(2,1)S(1)}, u32[]{:S(2)}, u32[]{:S(2)}) collective-permute-start(bf16[128,640]{1,0:T(8,128)(2,1)S(1)} %get-tuple-element.51), channel_id=1, source_target_pairs={{0,64},{1,33},{16,80},{17,49},{32,96},{33,1},{48,112},{49,17},{4,6... | collective-permute-start | bytes 491528 | tf_op jit(solution)/shard_map/ppermute | solution.py:40
  23.0 6.6 %collective-permute-start.18 = (bf16[128,640]{1,0:T(8,128)(2,1)S(1)}, bf16[128,640]{1,0:T(8,128)(2,1)S(1)}, u32[]{:S(2)}, u32[]{:S(2)}) collective-permute-start(bf16[128,640]{1,0:T(8,128)(2,1)S(1)} %get-tuple-element.50), channel_id=1, source_target_pairs={{0,66},{1,49},{16,82},{17,1},{32,98},{33,17},{48,114},{49,33},{4,7... | collective-permute-start | bytes 491528 | tf_op jit(solution)/shard_map/ppermute | solution.py:40
  23.4 6.2 %collective-permute-start.17 = (bf16[128,640]{1,0:T(8,128)(2,1)S(1)}, bf16[128,640]{1,0:T(8,128)(2,1)S(1)}, u32[]{:S(2)}, u32[]{:S(2)}) collective-permute-start(bf16[128,640]{1,0:T(8,128)(2,1)S(1)} %get-tuple-element.49), channel_id=1, source_target_pairs={{0,2},{1,17},{16,18},{17,33},{32,34},{33,49},{48,50},{49,1},{4,6},... | collective-permute-start | bytes 491528 | tf_op jit(solution)/shard_map/ppermute | solution.py:40
  25.8 7.4 %collective-permute-start.10 = (bf16[128,640]{1,0:T(8,128)(2,1)S(1)}, bf16[128,640]{1,0:T(8,128)(2,1)S(1)}, u32[]{:S(2)}, u32[]{:S(2)}) collective-permute-start(bf16[128,640]{1,0:T(8,128)(2,1)S(1)} %get-tuple-element.47), channel_id=1, source_target_pairs={{0,32},{1,33},{16,48},{17,49},{32,0},{33,1},{48,16},{49,17},{4,36}... | collective-permute-start | bytes 491528 | tf_op jit(solution)/shard_map/ppermute | solution.py:40
  28.2 5.7 %collective-permute-start.9 = (bf16[128,640]{1,0:T(8,128)(2,1)S(1)}, bf16[128,640]{1,0:T(8,128)(2,1)S(1)}, u32[]{:S(2)}, u32[]{:S(2)}) collective-permute-start(bf16[128,640]{1,0:T(8,128)(2,1)S(1)} %get-tuple-element.46), channel_id=1, source_target_pairs={{0,48},{1,49},{16,0},{17,1},{32,16},{33,17},{48,32},{49,33},{4,52}... | collective-permute-start | bytes 491528 | tf_op jit(solution)/shard_map/ppermute | solution.py:40
  29.1 6.9 %collective-permute-start.8 = (bf16[128,640]{1,0:T(8,128)(2,1)S(1)}, bf16[128,640]{1,0:T(8,128)(2,1)S(1)}, u32[]{:S(2)}, u32[]{:S(2)}) collective-permute-start(bf16[128,640]{1,0:T(8,128)(2,1)S(1)} %get-tuple-element.45), channel_id=1, source_target_pairs={{0,16},{1,17},{16,32},{17,33},{32,48},{33,49},{48,0},{49,1},{4,20}... | collective-permute-start | bytes 491528 | tf_op jit(solution)/shard_map/ppermute | solution.py:40
  29.7 9.9 %collective-permute-start.22 = (bf16[128,640]{1,0:T(8,128)(2,1)S(1)}, bf16[128,640]{1,0:T(8,128)(2,1)S(1)}, u32[]{:S(2)}, u32[]{:S(2)}) collective-permute-start(bf16[128,640]{1,0:T(8,128)(2,1)S(1)} %fusion.9), channel_id=1, source_target_pairs={{0,32},{1,9},{16,48},{17,25},{32,0},{33,41},{48,16},{49,57},{4,36}... | collective-permute-start | bytes 491528 | tf_op jit(solution)/shard_map/ppermute | solution.py:40
  32.4 7.9 %collective-permute-start.21 = (bf16[128,640]{1,0:T(8,128)(2,1)S(1)}, bf16[128,640]{1,0:T(8,128)(2,1)S(1)}, u32[]{:S(2)}, u32[]{:S(2)}) collective-permute-start(bf16[128,640]{1,0:T(8,128)(2,1)S(1)} %fusion.9), channel_id=1, source_target_pairs={{0,48},{1,13},{16,0},{17,29},{32,16},{33,45},{48,32},{49,61},{4,52... | collective-permute-start | bytes 491528 | tf_op jit(solution)/shard_map/ppermute | solution.py:40
  33.2 7.1 %collective-permute-start.20 = (bf16[128,640]{1,0:T(8,128)(2,1)S(1)}, bf16[128,640]{1,0:T(8,128)(2,1)S(1)}, u32[]{:S(2)}, u32[]{:S(2)}) collective-permute-start(bf16[128,640]{1,0:T(8,128)(2,1)S(1)} %fusion.9), channel_id=1, source_target_pairs={{0,16},{1,5},{16,32},{17,21},{32,48},{33,37},{48,0},{49,53},{4,20}... | collective-permute-start | bytes 491528 | tf_op jit(solution)/shard_map/ppermute | solution.py:40
  36.0 8.5 %collective-permute-start.13 = (bf16[128,640]{1,0:T(8,128)(2,1)S(1)}, bf16[128,640]{1,0:T(8,128)(2,1)S(1)}, u32[]{:S(2)}, u32[]{:S(2)}) collective-permute-start(bf16[128,640]{1,0:T(8,128)(2,1)S(1)} %fusion.8), channel_id=1, source_target_pairs={{0,64},{1,9},{16,80},{17,25},{32,96},{33,41},{48,112},{49,57},{4,6... | collective-permute-start | bytes 491528 | tf_op jit(solution)/shard_map/ppermute | solution.py:40
  38.8 5.7 %collective-permute-start.12 = (bf16[128,640]{1,0:T(8,128)(2,1)S(1)}, bf16[128,640]{1,0:T(8,128)(2,1)S(1)}, u32[]{:S(2)}, u32[]{:S(2)}) collective-permute-start(bf16[128,640]{1,0:T(8,128)(2,1)S(1)} %fusion.8), channel_id=1, source_target_pairs={{0,66},{1,13},{16,82},{17,29},{32,98},{33,45},{48,114},{49,61},{4,... | collective-permute-start | bytes 491528 | tf_op jit(solution)/shard_map/ppermute | solution.py:40
  39.7 5.6 %collective-permute-start.11 = (bf16[128,640]{1,0:T(8,128)(2,1)S(1)}, bf16[128,640]{1,0:T(8,128)(2,1)S(1)}, u32[]{:S(2)}, u32[]{:S(2)}) collective-permute-start(bf16[128,640]{1,0:T(8,128)(2,1)S(1)} %fusion.8), channel_id=1, source_target_pairs={{0,2},{1,5},{16,18},{17,21},{32,34},{33,37},{48,50},{49,53},{4,6},... | collective-permute-start | bytes 491528 | tf_op jit(solution)/shard_map/ppermute | solution.py:40
  40.5 8.5 %collective-permute-start.23 = (bf16[128,640]{1,0:T(8,128)(2,1)S(1)}, bf16[128,640]{1,0:T(8,128)(2,1)S(1)}, u32[]{:S(2)}, u32[]{:S(2)}) collective-permute-start(bf16[128,640]{1,0:T(8,128)(2,1)S(1)} %add_convert_fusion.refs_4_), channel_id=1, source_target_pairs={{0,2},{1,17},{16,18},{17,33},{32,34},{33,49},{48,50},{49,1},{4,6},... | collective-permute-start | bytes 491528 | tf_op jit(solution)/shard_map/ppermute | solution.py:40
  41.6 7.3 %collective-permute-start.24 = (bf16[128,640]{1,0:T(8,128)(2,1)S(1)}, bf16[128,640]{1,0:T(8,128)(2,1)S(1)}, u32[]{:S(2)}, u32[]{:S(2)}) collective-permute-start(bf16[128,640]{1,0:T(8,128)(2,1)S(1)} %add_convert_fusion.refs_4_), channel_id=1, source_target_pairs={{0,64},{1,33},{16,80},{17,49},{32,96},{33,1},{48,112},{49,17},{4,6... | collective-permute-start | bytes 491528 | tf_op jit(solution)/shard_map/ppermute | solution.py:40
  44.5 4.5 %collective-permute-start.25 = (bf16[128,640]{1,0:T(8,128)(2,1)S(1)}, bf16[128,640]{1,0:T(8,128)(2,1)S(1)}, u32[]{:S(2)}, u32[]{:S(2)}) collective-permute-start(bf16[128,640]{1,0:T(8,128)(2,1)S(1)} %add_convert_fusion.refs_4_), channel_id=1, source_target_pairs={{0,66},{1,49},{16,82},{17,1},{32,98},{33,17},{48,114},{49,33},{4,7... | collective-permute-start | bytes 491528 | tf_op jit(solution)/shard_map/ppermute | solution.py:40
  45.4 5.9 %collective-permute-start.14 = (bf16[128,640]{1,0:T(8,128)(2,1)S(1)}, bf16[128,640]{1,0:T(8,128)(2,1)S(1)}, u32[]{:S(2)}, u32[]{:S(2)}) collective-permute-start(bf16[128,640]{1,0:T(8,128)(2,1)S(1)} %add_convert_fusion.1.refs_0_.piece0), channel_id=1, source_target_pairs={{0,16},{1,17},{16,32},{17,33},{32,48},{33,49},{48,0},{49,1},{4,20}... | collective-permute-start | bytes 491528 | tf_op jit(solution)/shard_map/ppermute | solution.py:40
  46.3 7.2 %collective-permute-start.15 = (bf16[128,640]{1,0:T(8,128)(2,1)S(1)}, bf16[128,640]{1,0:T(8,128)(2,1)S(1)}, u32[]{:S(2)}, u32[]{:S(2)}) collective-permute-start(bf16[128,640]{1,0:T(8,128)(2,1)S(1)} %add_convert_fusion.1.refs_0_.piece0), channel_id=1, source_target_pairs={{0,32},{1,33},{16,48},{17,49},{32,0},{33,1},{48,16},{49,17},{4,36}... | collective-permute-start | bytes 491528 | tf_op jit(solution)/shard_map/ppermute | solution.py:40
  48.9 5.3 %collective-permute-start.16 = (bf16[128,640]{1,0:T(8,128)(2,1)S(1)}, bf16[128,640]{1,0:T(8,128)(2,1)S(1)}, u32[]{:S(2)}, u32[]{:S(2)}) collective-permute-start(bf16[128,640]{1,0:T(8,128)(2,1)S(1)} %add_convert_fusion.1.refs_0_.piece0), channel_id=1, source_target_pairs={{0,48},{1,49},{16,0},{17,1},{32,16},{33,17},{48,32},{49,33},{4,52}... | collective-permute-start | bytes 491528 | tf_op jit(solution)/shard_map/ppermute | solution.py:40
  54.6 5.9 %collective-permute-start.28 = (bf16[192,512]{1,0:T(8,128)(2,1)S(1)}, bf16[192,512]{1,0:T(8,128)(2,1)S(1)}, u32[]{:S(2)}, u32[]{:S(2)}) collective-permute-start(bf16[192,512]{1,0:T(8,128)(2,1)S(1)} %get-tuple-element.58), channel_id=1, source_target_pairs={{0,4},{1,3},{16,20},{17,19},{32,36},{33,35},{48,52},{49,51},{4,8},... | collective-permute-start | bytes 589832 | tf_op jit(solution)/shard_map/ppermute | solution.py:40
  55.4 7.8 %collective-permute-start.27 = (bf16[192,512]{1,0:T(8,128)(2,1)S(1)}, bf16[192,512]{1,0:T(8,128)(2,1)S(1)}, u32[]{:S(2)}, u32[]{:S(2)}) collective-permute-start(bf16[192,512]{1,0:T(8,128)(2,1)S(1)} %get-tuple-element.57), channel_id=1, source_target_pairs={{0,8},{1,65},{16,24},{17,81},{32,40},{33,97},{48,56},{49,113},{4,1... | collective-permute-start | bytes 589832 | tf_op jit(solution)/shard_map/ppermute | solution.py:40
  58.1 5.3 %collective-permute-start.26 = (bf16[192,512]{1,0:T(8,128)(2,1)S(1)}, bf16[192,512]{1,0:T(8,128)(2,1)S(1)}, u32[]{:S(2)}, u32[]{:S(2)}) collective-permute-start(bf16[192,512]{1,0:T(8,128)(2,1)S(1)} %get-tuple-element.56), channel_id=1, source_target_pairs={{0,12},{1,67},{16,28},{17,83},{32,44},{33,99},{48,60},{49,115},{4,... | collective-permute-start | bytes 589832 | tf_op jit(solution)/shard_map/ppermute | solution.py:40
  63.6 6.1 %collective-permute-start.29 = (f32[192]{0:T(256)S(1)}, f32[192]{0:T(256)S(1)}, u32[]{:S(2)}, u32[]{:S(2)}) collective-permute-start(f32[192]{0:T(256)S(1)} %fusion.5), channel_id=1, source_target_pairs={{0,1},{1,0},{2,3},{3,2},{4,5},{5,4},{6,7},{7,6},{8,9},{9,8},{10,11... | collective-permute-start | bytes 2312 | tf_op jit(solution)/shard_map/ppermute | solution.py:44

commit v17 on v16

--- a/solution.py
+++ b/solution.py
@@ -224,11 +224,12 @@
         out[:, block] = (product[k * rows : (k + 1) * rows] + sofar).astype(out.dtype)
 
 
-def apply_kept_kernel(pack, *refs):
+def apply_kept_kernel(level, pack, norm, *refs):
     places = places_here()
     pieces, (before, out, weights) = refs[:SIZE], refs[SIZE:]
     gather_weights(places[2], pieces, weights)
-    out[...] = times(pack[...], weights[...]) + before[pl.ds(0, pack.shape[0]), :]
+    kept = before[pl.ds(0, pack.shape[0]), :] + level * norm[:, pl.ds(0, out.shape[1])].astype(F32)
+    out[...] = times(pack[...], weights[...]) + kept
 
 
 def shapes(*described):
@@ -348,10 +349,14 @@
         flops // 4,
     )(stacked, far_weights[LAST], sofar, *most)
     grad_n = kernel_call(
-        apply_kept_kernel, "apply_kept", shapes(((rows, half), F32)), SIZE + 2, [weights], flops // 4
-    )(far[0], *far_weights, sofar)[0]
+        functools.partial(apply_kept_kernel, level),
+        "apply_kept",
+        shapes(((rows, half), F32)),
+        SIZE + 3,
+        [weights],
+        flops // 4,
+    )(far[0], near[0], *far_weights, sofar)[0]
     norm_f = norm_own.astype(F32)
-    grad_n = grad_n + level * norm_f
     grad_n = coef * added(grad_n, lambda by: parts[by - 1], GATHER, -1, BACK)
     inner = jnp.sum(grad_n * norm_f, axis=1)
     inner = inner + other_core(inner)

time: 70.8 us -> 70.8 us (level)
  no operation moved by 1% of the time
where the time goes in v17:
time: 70.8 us; the launch traced here: 70.6 us
  starting transfers between devices  44.8 us (63%)
  waiting for transfers between devices  15.8 us (22%)
  Pallas kernels  6.19 us (9%)
  local copies, waits for them, and re-layouts  2.06 us (3%)
  other arithmetic  1.66 us (2%)
    ppermute x27, starting transfers between devices, shifted(): return lax.ppermute(array, AXES, pairs)  38.1 us
    ppermute x27, waiting for transfers between devices, shifted(): return lax.ppermute(array, AXES, pairs)  15 us
    ppermute x3, starting transfers between devices, other_core(): return lax.ppermute(array, 'sec', [(0, 1), (1, 0)])  6.69 us
    unnamed x4, local copies, waits for them, and re-layouts  2.06 us
  transfers between devices with their start and end apart: 30, of which 10 were waited for; matrix products, arithmetic and copies ran while one was open for 1% of the time, Pallas kernels for 8%

profile of v17, /device:TPU:1, one launch (start us, length us, event | category | flops | bytes accessed | tf_op | source)
XLA Modules:
  0.0 70.6 jit_solution(14017853306763350968)
XLA Ops:
  0.0 1.4 %collective-permute-start.1 = (bf16[192,2048]{1,0:T(8,128)(2,1)}, bf16[192,2048]{1,0:T(8,128)(2,1)S(1)}, u32[]{:S(2)}, u32[]{:S(2)}) collective-permute-start(bf16[192,2048]{1,0:T(8,128)(2,1)} %t_own.3), channel_id=1, source_target_pairs={{0,1},{1,0},{2,3},{3,2},{4,5},{5,4},{6,7},{7,6},{8,9},{9,8},{10,11... | collective-permute-start | bytes 2359304 | tf_op jit(solution)/shard_map/ppermute | solution.py:44
  1.4 1.1 %copy-done = bf16[192,2048]{1,0:T(8,128)(2,1)S(1)} copy-done((bf16[192,2048]{1,0:T(8,128)(2,1)S(1)}, bf16[192,2048]{1,0:T(8,128)(2,1)}, u32[]{:S(2)}) %copy-start) | copy-done | bytes 786456
  2.6 0.9 %copy-done.1 = bf16[192,512]{1,0:T(8,128)(2,1)S(1)} copy-done((bf16[192,512]{1,0:T(8,128)(2,1)S(1)}, bf16[192,512]{1,0:T(8,128)(2,1)}, u32[]{:S(2)}) %copy-start.1) | copy-done | bytes 196632
  3.8 0.5 pack_own.1
  4.3 1.4 %collective-permute-start.4 = (bf16[192,1024]{1,0:T(8,128)(2,1)S(1)}, bf16[192,1024]{1,0:T(8,128)(2,1)S(1)}, u32[]{:S(2)}, u32[]{:S(2)}) collective-permute-start(bf16[192,1024]{1,0:T(8,128)(2,1)S(1)} %get-tuple-element.40), channel_id=1, source_target_pairs={{0,4},{1,3},{16,20},{17,19},{32,36},{33,35},{48,52},{49,51},{4,8},... | collective-permute-start | bytes 1179656 | tf_op jit(solution)/shard_map/ppermute | solution.py:40
  5.7 2.5 %collective-permute-start.5 = (bf16[192,1024]{1,0:T(8,128)(2,1)S(1)}, bf16[192,1024]{1,0:T(8,128)(2,1)S(1)}, u32[]{:S(2)}, u32[]{:S(2)}) collective-permute-start(bf16[192,1024]{1,0:T(8,128)(2,1)S(1)} %get-tuple-element.41), channel_id=1, source_target_pairs={{0,8},{1,65},{16,24},{17,81},{32,40},{33,97},{48,56},{49,113},{4,1... | collective-permute-start | bytes 1179656 | tf_op jit(solution)/shard_map/ppermute | solution.py:40
  8.1 1.2 %collective-permute-start.2 = (bf16[192,1024]{1,0:T(8,128)(2,1)S(1)}, bf16[192,1024]{1,0:T(8,128)(2,1)S(1)}, u32[]{:S(2)}, u32[]{:S(2)}) collective-permute-start(bf16[192,1024]{1,0:T(8,128)(2,1)S(1)} %get-tuple-element.38), channel_id=1, source_target_pairs={{0,12},{1,67},{16,28},{17,83},{32,44},{33,99},{48,60},{49,115},{4,... | collective-permute-start | bytes 1179656 | tf_op jit(solution)/shard_map/ppermute | solution.py:40
  9.3 0.3 pack_far.1
  9.6 0.4 collective-permute-start.6
  10.0 0.9 %collective-permute-start.7 = (bf16[192,640]{1,0:T(8,128)(2,1)S(1)}, bf16[192,640]{1,0:T(8,128)(2,1)S(1)}, u32[]{:S(2)}, u32[]{:S(2)}) collective-permute-start(bf16[192,640]{1,0:T(8,128)(2,1)S(1)} %get-tuple-element.43), channel_id=1, source_target_pairs={{0,8},{1,65},{16,24},{17,81},{32,40},{33,97},{48,56},{49,113},{4,1... | collective-permute-start | bytes 737288 | tf_op jit(solution)/shard_map/ppermute | solution.py:40
  10.8 1.7 %collective-permute-done.4.refs_1_ = bf16[192,1024]{1,0:T(8,128)(2,1)S(1)} collective-permute-done((bf16[192,1024]{1,0:T(8,128)(2,1)S(1)}, bf16[192,1024]{1,0:T(8,128)(2,1)S(1)}, u32[]{:S(2)}, u32[]{:S(2)}) %collective-permute-start.4) | collective-permute-done | bytes 393248 | tf_op jit(solution)/shard_map/ppermute | solution.py:40
  12.5 1.4 %collective-permute-start.3 = (bf16[192,640]{1,0:T(8,128)(2,1)S(1)}, bf16[192,640]{1,0:T(8,128)(2,1)S(1)}, u32[]{:S(2)}, u32[]{:S(2)}) collective-permute-start(bf16[192,640]{1,0:T(8,128)(2,1)S(1)} %get-tuple-element.39), channel_id=1, source_target_pairs={{0,12},{1,67},{16,28},{17,83},{32,44},{33,99},{48,60},{49,115},{4,... | collective-permute-start | bytes 737288 | tf_op jit(solution)/shard_map/ppermute | solution.py:40
  13.9 4.0 %collective-permute-done.5.refs_2_ = bf16[192,1024]{1,0:T(8,128)(2,1)S(1)} collective-permute-done((bf16[192,1024]{1,0:T(8,128)(2,1)S(1)}, bf16[192,1024]{1,0:T(8,128)(2,1)S(1)}, u32[]{:S(2)}, u32[]{:S(2)}) %collective-permute-start.5) | collective-permute-done | bytes 393248 | tf_op jit(solution)/shard_map/ppermute | solution.py:40
  17.9 1.0 %gram_early.1.before = f32[512,640]{1,0:T(8,128)S(1)} custom-call(bf16[192,1024]{1,0:T(8,128)(2,1)S(1)} %get-tuple-element.37.refs_0_.norm, bf16[192,1024]{1,0:T(8,128)(2,1)S(1)} %collective-permute-done.4.refs_1_, bf16[192,1024]{1,0:T(8,128)(2,1)S(1)} %collective-permute-done.5.refs_2_), custom_call_target="tpu_custom_call" | custom-call | flops 503316480 | bytes 4194304 | tf_op jit(solution)/shard_map/gram_early/pallas_call | solution.py:298
  18.9 0.5 gram_native.1
  19.3 3.7 %collective-permute-start.19 = (bf16[128,640]{1,0:T(8,128)(2,1)S(1)}, bf16[128,640]{1,0:T(8,128)(2,1)S(1)}, u32[]{:S(2)}, u32[]{:S(2)}) collective-permute-start(bf16[128,640]{1,0:T(8,128)(2,1)S(1)} %get-tuple-element.51), channel_id=1, source_target_pairs={{0,64},{1,33},{16,80},{17,49},{32,96},{33,1},{48,112},{49,17},{4,6... | collective-permute-start | bytes 491528 | tf_op jit(solution)/shard_map/ppermute | solution.py:40
  23.0 0.4 collective-permute-start.18
  23.4 1.0 %collective-permute-start.17 = (bf16[128,640]{1,0:T(8,128)(2,1)S(1)}, bf16[128,640]{1,0:T(8,128)(2,1)S(1)}, u32[]{:S(2)}, u32[]{:S(2)}) collective-permute-start(bf16[128,640]{1,0:T(8,128)(2,1)S(1)} %get-tuple-element.49), channel_id=1, source_target_pairs={{0,2},{1,17},{16,18},{17,33},{32,34},{33,49},{48,50},{49,1},{4,6},... | collective-permute-start | bytes 491528 | tf_op jit(solution)/shard_map/ppermute | solution.py:40
  24.5 0.9 %gram_far_early.1.before = f32[512,640]{1,0:T(8,128)S(1)} custom-call(bf16[192,1024]{1,0:T(8,128)(2,1)S(1)} %get-tuple-element.37.refs_0_.norm, bf16[192,1024]{1,0:T(8,128)(2,1)S(1)} %collective-permute-done.4.refs_1_, bf16[192,1024]{1,0:T(8,128)(2,1)S(1)} %collective-permute-done.5.refs_2_, bf16[192,640]{1,0:T(8,128)(2,1)S(1)} %get-tuple-element.36.refs_3_.pack, ...), custom_call_target="tpu_custom_call" | custom-call | flops 503316480 | bytes 4194304 | tf_op jit(solution)/shard_map/gram_far_early/pallas_call | solution.py:309
  25.4 0.5 gram_far.1
  25.8 2.3 %collective-permute-start.10 = (bf16[128,640]{1,0:T(8,128)(2,1)S(1)}, bf16[128,640]{1,0:T(8,128)(2,1)S(1)}, u32[]{:S(2)}, u32[]{:S(2)}) collective-permute-start(bf16[128,640]{1,0:T(8,128)(2,1)S(1)} %get-tuple-element.47), channel_id=1, source_target_pairs={{0,32},{1,33},{16,48},{17,49},{32,0},{33,1},{48,16},{49,17},{4,36}... | collective-permute-start | bytes 491528 | tf_op jit(solution)/shard_map/ppermute | solution.py:40
  28.2 0.9 %collective-permute-start.9 = (bf16[128,640]{1,0:T(8,128)(2,1)S(1)}, bf16[128,640]{1,0:T(8,128)(2,1)S(1)}, u32[]{:S(2)}, u32[]{:S(2)}) collective-permute-start(bf16[128,640]{1,0:T(8,128)(2,1)S(1)} %get-tuple-element.46), channel_id=1, source_target_pairs={{0,48},{1,49},{16,0},{17,1},{32,16},{33,17},{48,32},{49,33},{4,52}... | collective-permute-start | bytes 491528 | tf_op jit(solution)/shard_map/ppermute | solution.py:40
  29.1 0.6 collective-permute-start.8
  29.7 2.7 %collective-permute-start.22 = (bf16[128,640]{1,0:T(8,128)(2,1)S(1)}, bf16[128,640]{1,0:T(8,128)(2,1)S(1)}, u32[]{:S(2)}, u32[]{:S(2)}) collective-permute-start(bf16[128,640]{1,0:T(8,128)(2,1)S(1)} %fusion.4), channel_id=1, source_target_pairs={{0,32},{1,9},{16,48},{17,25},{32,0},{33,41},{48,16},{49,57},{4,36}... | collective-permute-start | bytes 491528 | tf_op jit(solution)/shard_map/ppermute | solution.py:40
  32.4 0.8 %collective-permute-start.21 = (bf16[128,640]{1,0:T(8,128)(2,1)S(1)}, bf16[128,640]{1,0:T(8,128)(2,1)S(1)}, u32[]{:S(2)}, u32[]{:S(2)}) collective-permute-start(bf16[128,640]{1,0:T(8,128)(2,1)S(1)} %fusion.4), channel_id=1, source_target_pairs={{0,48},{1,13},{16,0},{17,29},{32,16},{33,45},{48,32},{49,61},{4,52... | collective-permute-start | bytes 491528 | tf_op jit(solution)/shard_map/ppermute | solution.py:40
  33.2 0.7 collective-permute-start.20
  33.9 2.1 %collective-permute-done.8 = bf16[128,640]{1,0:T(8,128)(2,1)S(1)} collective-permute-done((bf16[128,640]{1,0:T(8,128)(2,1)S(1)}, bf16[128,640]{1,0:T(8,128)(2,1)S(1)}, u32[]{:S(2)}, u32[]{:S(2)}) %collective-permute-start.8) | collective-permute-done | bytes 163872 | tf_op jit(solution)/shard_map/ppermute | solution.py:40
  36.0 2.8 %collective-permute-start.13 = (bf16[128,640]{1,0:T(8,128)(2,1)S(1)}, bf16[128,640]{1,0:T(8,128)(2,1)S(1)}, u32[]{:S(2)}, u32[]{:S(2)}) collective-permute-start(bf16[128,640]{1,0:T(8,128)(2,1)S(1)} %fusion.3), channel_id=1, source_target_pairs={{0,64},{1,9},{16,80},{17,25},{32,96},{33,41},{48,112},{49,57},{4,6... | collective-permute-start | bytes 491528 | tf_op jit(solution)/shard_map/ppermute | solution.py:40
  38.8 0.8 %collective-permute-start.12 = (bf16[128,640]{1,0:T(8,128)(2,1)S(1)}, bf16[128,640]{1,0:T(8,128)(2,1)S(1)}, u32[]{:S(2)}, u32[]{:S(2)}) collective-permute-start(bf16[128,640]{1,0:T(8,128)(2,1)S(1)} %fusion.3), channel_id=1, source_target_pairs={{0,66},{1,13},{16,82},{17,29},{32,98},{33,45},{48,114},{49,61},{4,... | collective-permute-start | bytes 491528 | tf_op jit(solution)/shard_map/ppermute | solution.py:40
  39.7 0.7 collective-permute-start.11
  40.5 1.1 %collective-permute-start.23 = (bf16[128,640]{1,0:T(8,128)(2,1)S(1)}, bf16[128,640]{1,0:T(8,128)(2,1)S(1)}, u32[]{:S(2)}, u32[]{:S(2)}) collective-permute-start(bf16[128,640]{1,0:T(8,128)(2,1)S(1)} %add_convert_fusion.refs_4_), channel_id=1, source_target_pairs={{0,2},{1,17},{16,18},{17,33},{32,34},{33,49},{48,50},{49,1},{4,6},... | collective-permute-start | bytes 491528 | tf_op jit(solution)/shard_map/ppermute | solution.py:40
  41.6 2.9 %collective-permute-start.24 = (bf16[128,640]{1,0:T(8,128)(2,1)S(1)}, bf16[128,640]{1,0:T(8,128)(2,1)S(1)}, u32[]{:S(2)}, u32[]{:S(2)}) collective-permute-start(bf16[128,640]{1,0:T(8,128)(2,1)S(1)} %add_convert_fusion.refs_4_), channel_id=1, source_target_pairs={{0,64},{1,33},{16,80},{17,49},{32,96},{33,1},{48,112},{49,17},{4,6... | collective-permute-start | bytes 491528 | tf_op jit(solution)/shard_map/ppermute | solution.py:40
  44.5 0.7 collective-permute-done.11
  45.4 1.0 %collective-permute-start.14 = (bf16[128,640]{1,0:T(8,128)(2,1)S(1)}, bf16[128,640]{1,0:T(8,128)(2,1)S(1)}, u32[]{:S(2)}, u32[]{:S(2)}) collective-permute-start(bf16[128,640]{1,0:T(8,128)(2,1)S(1)} %add_convert_fusion.1.refs_0_.piece0), channel_id=1, source_target_pairs={{0,16},{1,17},{16,32},{17,33},{32,48},{33,49},{48,0},{49,1},{4,20}... | collective-permute-start | bytes 491528 | tf_op jit(solution)/shard_map/ppermute | solution.py:40
  46.3 2.6 %collective-permute-start.15 = (bf16[128,640]{1,0:T(8,128)(2,1)S(1)}, bf16[128,640]{1,0:T(8,128)(2,1)S(1)}, u32[]{:S(2)}, u32[]{:S(2)}) collective-permute-start(bf16[128,640]{1,0:T(8,128)(2,1)S(1)} %add_convert_fusion.1.refs_0_.piece0), channel_id=1, source_target_pairs={{0,32},{1,33},{16,48},{17,49},{32,0},{33,1},{48,16},{49,17},{4,36}... | collective-permute-start | bytes 491528 | tf_op jit(solution)/shard_map/ppermute | solution.py:40
  49.0 0.9 %apply_native.1.refs_4_.before = f32[768,512]{1,0:T(8,128)S(1)} custom-call(bf16[192,1024]{1,0:T(8,128)(2,1)S(1)} %get-tuple-element.37.refs_0_.norm, bf16[192,1024]{1,0:T(8,128)(2,1)S(1)} %collective-permute-done.4.refs_1_, bf16[192,1024]{1,0:T(8,128)(2,1)S(1)} %collective-permute-done.5.refs_2_, ...), custom_call_target="tpu_custom_call" | custom-call | flops 503316480 | bytes 4194304 | tf_op jit(solution)/shard_map/apply_native/pallas_call | solution.py:325
  49.8 1.5 %collective-permute-done.14.refs_1_.piece1 = bf16[128,640]{1,0:T(8,128)(2,1)S(1)} collective-permute-done((bf16[128,640]{1,0:T(8,128)(2,1)S(1)}, bf16[128,640]{1,0:T(8,128)(2,1)S(1)}, u32[]{:S(2)}, u32[]{:S(2)}) %collective-permute-start.14) | collective-permute-done | bytes 163872 | tf_op jit(solution)/shard_map/ppermute | solution.py:40
  51.3 2.2 %collective-permute-done.15.refs_2_.piece2 = bf16[128,640]{1,0:T(8,128)(2,1)S(1)} collective-permute-done((bf16[128,640]{1,0:T(8,128)(2,1)S(1)}, bf16[128,640]{1,0:T(8,128)(2,1)S(1)}, u32[]{:S(2)}, u32[]{:S(2)}) %collective-permute-start.15) | collective-permute-done | bytes 163872 | tf_op jit(solution)/shard_map/ppermute | solution.py:40
  53.5 0.7 %apply_early.1 = (bf16[192,512]{1,0:T(8,128)(2,1)S(1)}, bf16[192,512]{1,0:T(8,128)(2,1)S(1)}, bf16[192,512]{1,0:T(8,128)(2,1)S(1)}, bf16[576,640]{1,0:T(8,128)(2,1)S(1)}) custom-call(bf16[192,640]{1,0:T(8,128)(2,1)S(1)} %collective-permute-done.6.refs_4_.far1, bf16[192,640]{1,0:T(8,128)(2,1)S(1)} %collective-permute-done.7.refs_5_.far2, ...), custom_call_target="tpu_custom_call" | custom-call | flops 377487360 | bytes 4194304 | tf_op jit(solution)/shard_map/apply_early/pallas_call | solution.py:335
  54.3 0.4 apply_sent.1
  54.6 0.8 %collective-permute-start.28 = (bf16[192,512]{1,0:T(8,128)(2,1)S(1)}, bf16[192,512]{1,0:T(8,128)(2,1)S(1)}, u32[]{:S(2)}, u32[]{:S(2)}) collective-permute-start(bf16[192,512]{1,0:T(8,128)(2,1)S(1)} %get-tuple-element.58), channel_id=1, source_target_pairs={{0,4},{1,3},{16,20},{17,19},{32,36},{33,35},{48,52},{49,51},{4,8},... | collective-permute-start | bytes 589832 | tf_op jit(solution)/shard_map/ppermute | solution.py:40
  55.4 2.7 %collective-permute-start.27 = (bf16[192,512]{1,0:T(8,128)(2,1)S(1)}, bf16[192,512]{1,0:T(8,128)(2,1)S(1)}, u32[]{:S(2)}, u32[]{:S(2)}) collective-permute-start(bf16[192,512]{1,0:T(8,128)(2,1)S(1)} %get-tuple-element.57), channel_id=1, source_target_pairs={{0,8},{1,65},{16,24},{17,81},{32,40},{33,97},{48,56},{49,113},{4,1... | collective-permute-start | bytes 589832 | tf_op jit(solution)/shard_map/ppermute | solution.py:40
  58.1 2.0 %collective-permute-start.26 = (bf16[192,512]{1,0:T(8,128)(2,1)S(1)}, bf16[192,512]{1,0:T(8,128)(2,1)S(1)}, u32[]{:S(2)}, u32[]{:S(2)}) collective-permute-start(bf16[192,512]{1,0:T(8,128)(2,1)S(1)} %get-tuple-element.56), channel_id=1, source_target_pairs={{0,12},{1,67},{16,28},{17,83},{32,44},{33,99},{48,60},{49,115},{4,... | collective-permute-start | bytes 589832 | tf_op jit(solution)/shard_map/ppermute | solution.py:40
  60.1 0.4 apply_kept.1
  60.6 2.7 %collective-permute-done.27 = bf16[192,512]{1,0:T(8,128)(2,1)S(1)} collective-permute-done((bf16[192,512]{1,0:T(8,128)(2,1)S(1)}, bf16[192,512]{1,0:T(8,128)(2,1)S(1)}, u32[]{:S(2)}, u32[]{:S(2)}) %collective-permute-start.27) | collective-permute-done | bytes 196640 | tf_op jit(solution)/shard_map/ppermute | solution.py:40
  63.6 5.3 %collective-permute-start.29 = (f32[192]{0:T(256)S(1)}, f32[192]{0:T(256)S(1)}, u32[]{:S(2)}, u32[]{:S(2)}) collective-permute-start(f32[192]{0:T(256)S(1)} %fusion), channel_id=1, source_target_pairs={{0,1},{1,0},{2,3},{3,2},{4,5},{5,4},{6,7},{7,6},{8,9},{9,8},{10,11... | collective-permute-start | bytes 2312 | tf_op jit(solution)/shard_map/ppermute | solution.py:44
  69.0 0.7 %collective-permute-done.29 = f32[192]{0:T(256)S(1)} collective-permute-done((f32[192]{0:T(256)S(1)}, f32[192]{0:T(256)S(1)}, u32[]{:S(2)}, u32[]{:S(2)}) %collective-permute-start.29) | collective-permute-done | bytes 800 | tf_op jit(solution)/shard_map/ppermute | solution.py:44
  69.7 0.9 %fusion.2 = f32[192,512]{1,0:T(8,128)} fusion(f32[192]{0:T(256)S(1)} %reduce, f32[192]{0:T(256)S(1)} %add.63, bf16[192,1024]{1,0:T(8,128)(2,1)S(1)} %get-tuple-element.37.refs_0_.norm, bf16[192,512]{1,0:T(8,128)(2,1)S(1)} %collective-permute-done.28, bf16[192,512]{1,0:T(8,128)(2,1)S(1)} %collective-permute-done.27, f32[192,512]{1,0:T(8,128)S(1)} %apply_kept.1, ...), kind=kLoop, calls=%fused_computation.4 | loop fusion | flops 1081344 | bytes 1574400 | tf_op jit(solution)/shard_map/mul | solution.py:363
  (35 shorter events, 1.4 us)
Async XLA Ops:
  0.0 3.8 %collective-permute-start.1 = (bf16[192,2048]{1,0:T(8,128)(2,1)}, bf16[192,2048]{1,0:T(8,128)(2,1)S(1)}, u32[]{:S(2)}, u32[]{:S(2)}) collective-permute-start(bf16[192,2048]{1,0:T(8,128)(2,1)} %t_own.3), channel_id=1, source_target_pairs={{0,1},{1,0},{2,3},{3,2},{4,5},{5,4},{6,7},{7,6},{8,9},{9,8},{10,11... | collective-permute-start | bytes 2359304 | tf_op jit(solution)/shard_map/ppermute | solution.py:44
  1.4 2.4 %collective-permute-start = (bf16[192,512]{1,0:T(8,128)(2,1)}, bf16[192,512]{1,0:T(8,128)(2,1)S(1)}, u32[]{:S(2)}, u32[]{:S(2)}) collective-permute-start(bf16[192,512]{1,0:T(8,128)(2,1)} %s_own.3), channel_id=1, source_target_pairs={{0,1},{1,0},{2,3},{3,2},{4,5},{5,4},{6,7},{7,6},{8,9},{9,8},{10,11... | collective-permute-start | bytes 589832 | tf_op jit(solution)/shard_map/ppermute | solution.py:44
  1.4 1.1 %copy-start = (bf16[192,2048]{1,0:T(8,128)(2,1)S(1)}, bf16[192,2048]{1,0:T(8,128)(2,1)}, u32[]{:S(2)}) copy-start(bf16[192,2048]{1,0:T(8,128)(2,1)} %t_own.3) | copy-start | bytes 2359300
  2.6 0.9 %copy-start.1 = (bf16[192,512]{1,0:T(8,128)(2,1)S(1)}, bf16[192,512]{1,0:T(8,128)(2,1)}, u32[]{:S(2)}) copy-start(bf16[192,512]{1,0:T(8,128)(2,1)} %s_own.3) | copy-start | bytes 589828
  4.3 8.2 %collective-permute-start.4 = (bf16[192,1024]{1,0:T(8,128)(2,1)S(1)}, bf16[192,1024]{1,0:T(8,128)(2,1)S(1)}, u32[]{:S(2)}, u32[]{:S(2)}) collective-permute-start(bf16[192,1024]{1,0:T(8,128)(2,1)S(1)} %get-tuple-element.40), channel_id=1, source_target_pairs={{0,4},{1,3},{16,20},{17,19},{32,36},{33,35},{48,52},{49,51},{4,8},... | collective-permute-start | bytes 1179656 | tf_op jit(solution)/shard_map/ppermute | solution.py:40
  5.7 12.2 %collective-permute-start.5 = (bf16[192,1024]{1,0:T(8,128)(2,1)S(1)}, bf16[192,1024]{1,0:T(8,128)(2,1)S(1)}, u32[]{:S(2)}, u32[]{:S(2)}) collective-permute-start(bf16[192,1024]{1,0:T(8,128)(2,1)S(1)} %get-tuple-element.41), channel_id=1, source_target_pairs={{0,8},{1,65},{16,24},{17,81},{32,40},{33,97},{48,56},{49,113},{4,1... | collective-permute-start | bytes 1179656 | tf_op jit(solution)/shard_map/ppermute | solution.py:40
  8.1 10.7 %collective-permute-start.2 = (bf16[192,1024]{1,0:T(8,128)(2,1)S(1)}, bf16[192,1024]{1,0:T(8,128)(2,1)S(1)}, u32[]{:S(2)}, u32[]{:S(2)}) collective-permute-start(bf16[192,1024]{1,0:T(8,128)(2,1)S(1)} %get-tuple-element.38), channel_id=1, source_target_pairs={{0,12},{1,67},{16,28},{17,83},{32,44},{33,99},{48,60},{49,115},{4,... | collective-permute-start | bytes 1179656 | tf_op jit(solution)/shard_map/ppermute | solution.py:40
  9.6 13.9 %collective-permute-start.6 = (bf16[192,640]{1,0:T(8,128)(2,1)S(1)}, bf16[192,640]{1,0:T(8,128)(2,1)S(1)}, u32[]{:S(2)}, u32[]{:S(2)}) collective-permute-start(bf16[192,640]{1,0:T(8,128)(2,1)S(1)} %get-tuple-element.42), channel_id=1, source_target_pairs={{0,4},{1,3},{16,20},{17,19},{32,36},{33,35},{48,52},{49,51},{4,8},... | collective-permute-start | bytes 737288 | tf_op jit(solution)/shard_map/ppermute | solution.py:40
  10.0 14.5 %collective-permute-start.7 = (bf16[192,640]{1,0:T(8,128)(2,1)S(1)}, bf16[192,640]{1,0:T(8,128)(2,1)S(1)}, u32[]{:S(2)}, u32[]{:S(2)}) collective-permute-start(bf16[192,640]{1,0:T(8,128)(2,1)S(1)} %get-tuple-element.43), channel_id=1, source_target_pairs={{0,8},{1,65},{16,24},{17,81},{32,40},{33,97},{48,56},{49,113},{4,1... | collective-permute-start | bytes 737288 | tf_op jit(solution)/shard_map/ppermute | solution.py:40
  12.5 12.8 %collective-permute-start.3 = (bf16[192,640]{1,0:T(8,128)(2,1)S(1)}, bf16[192,640]{1,0:T(8,128)(2,1)S(1)}, u32[]{:S(2)}, u32[]{:S(2)}) collective-permute-start(bf16[192,640]{1,0:T(8,128)(2,1)S(1)} %get-tuple-element.39), channel_id=1, source_target_pairs={{0,12},{1,67},{16,28},{17,83},{32,44},{33,99},{48,60},{49,115},{4,... | collective-permute-start | bytes 737288 | tf_op jit(solution)/shard_map/ppermute | solution.py:40
  19.3 9.7 %collective-permute-start.19 = (bf16[128,640]{1,0:T(8,128)(2,1)S(1)}, bf16[128,640]{1,0:T(8,128)(2,1)S(1)}, u32[]{:S(2)}, u32[]{:S(2)}) collective-permute-start(bf16[128,640]{1,0:T(8,128)(2,1)S(1)} %get-tuple-element.51), channel_id=1, source_target_pairs={{0,64},{1,33},{16,80},{17,49},{32,96},{33,1},{48,112},{49,17},{4,6... | collective-permute-start | bytes 491528 | tf_op jit(solution)/shard_map/ppermute | solution.py:40
  23.0 6.6 %collective-permute-start.18 = (bf16[128,640]{1,0:T(8,128)(2,1)S(1)}, bf16[128,640]{1,0:T(8,128)(2,1)S(1)}, u32[]{:S(2)}, u32[]{:S(2)}) collective-permute-start(bf16[128,640]{1,0:T(8,128)(2,1)S(1)} %get-tuple-element.50), channel_id=1, source_target_pairs={{0,66},{1,49},{16,82},{17,1},{32,98},{33,17},{48,114},{49,33},{4,7... | collective-permute-start | bytes 491528 | tf_op jit(solution)/shard_map/ppermute | solution.py:40
  23.4 6.2 %collective-permute-start.17 = (bf16[128,640]{1,0:T(8,128)(2,1)S(1)}, bf16[128,640]{1,0:T(8,128)(2,1)S(1)}, u32[]{:S(2)}, u32[]{:S(2)}) collective-permute-start(bf16[128,640]{1,0:T(8,128)(2,1)S(1)} %get-tuple-element.49), channel_id=1, source_target_pairs={{0,2},{1,17},{16,18},{17,33},{32,34},{33,49},{48,50},{49,1},{4,6},... | collective-permute-start | bytes 491528 | tf_op jit(solution)/shard_map/ppermute | solution.py:40
  25.8 7.4 %collective-permute-start.10 = (bf16[128,640]{1,0:T(8,128)(2,1)S(1)}, bf16[128,640]{1,0:T(8,128)(2,1)S(1)}, u32[]{:S(2)}, u32[]{:S(2)}) collective-permute-start(bf16[128,640]{1,0:T(8,128)(2,1)S(1)} %get-tuple-element.47), channel_id=1, source_target_pairs={{0,32},{1,33},{16,48},{17,49},{32,0},{33,1},{48,16},{49,17},{4,36}... | collective-permute-start | bytes 491528 | tf_op jit(solution)/shard_map/ppermute | solution.py:40
  28.2 5.7 %collective-permute-start.9 = (bf16[128,640]{1,0:T(8,128)(2,1)S(1)}, bf16[128,640]{1,0:T(8,128)(2,1)S(1)}, u32[]{:S(2)}, u32[]{:S(2)}) collective-permute-start(bf16[128,640]{1,0:T(8,128)(2,1)S(1)} %get-tuple-element.46), channel_id=1, source_target_pairs={{0,48},{1,49},{16,0},{17,1},{32,16},{33,17},{48,32},{49,33},{4,52}... | collective-permute-start | bytes 491528 | tf_op jit(solution)/shard_map/ppermute | solution.py:40
  29.1 6.9 %collective-permute-start.8 = (bf16[128,640]{1,0:T(8,128)(2,1)S(1)}, bf16[128,640]{1,0:T(8,128)(2,1)S(1)}, u32[]{:S(2)}, u32[]{:S(2)}) collective-permute-start(bf16[128,640]{1,0:T(8,128)(2,1)S(1)} %get-tuple-element.45), channel_id=1, source_target_pairs={{0,16},{1,17},{16,32},{17,33},{32,48},{33,49},{48,0},{49,1},{4,20}... | collective-permute-start | bytes 491528 | tf_op jit(solution)/shard_map/ppermute | solution.py:40
  29.7 9.9 %collective-permute-start.22 = (bf16[128,640]{1,0:T(8,128)(2,1)S(1)}, bf16[128,640]{1,0:T(8,128)(2,1)S(1)}, u32[]{:S(2)}, u32[]{:S(2)}) collective-permute-start(bf16[128,640]{1,0:T(8,128)(2,1)S(1)} %fusion.4), channel_id=1, source_target_pairs={{0,32},{1,9},{16,48},{17,25},{32,0},{33,41},{48,16},{49,57},{4,36}... | collective-permute-start | bytes 491528 | tf_op jit(solution)/shard_map/ppermute | solution.py:40
  32.4 7.9 %collective-permute-start.21 = (bf16[128,640]{1,0:T(8,128)(2,1)S(1)}, bf16[128,640]{1,0:T(8,128)(2,1)S(1)}, u32[]{:S(2)}, u32[]{:S(2)}) collective-permute-start(bf16[128,640]{1,0:T(8,128)(2,1)S(1)} %fusion.4), channel_id=1, source_target_pairs={{0,48},{1,13},{16,0},{17,29},{32,16},{33,45},{48,32},{49,61},{4,52... | collective-permute-start | bytes 491528 | tf_op jit(solution)/shard_map/ppermute | solution.py:40
  33.2 7.1 %collective-permute-start.20 = (bf16[128,640]{1,0:T(8,128)(2,1)S(1)}, bf16[128,640]{1,0:T(8,128)(2,1)S(1)}, u32[]{:S(2)}, u32[]{:S(2)}) collective-permute-start(bf16[128,640]{1,0:T(8,128)(2,1)S(1)} %fusion.4), channel_id=1, source_target_pairs={{0,16},{1,5},{16,32},{17,21},{32,48},{33,37},{48,0},{49,53},{4,20}... | collective-permute-start | bytes 491528 | tf_op jit(solution)/shard_map/ppermute | solution.py:40
  36.0 8.5 %collective-permute-start.13 = (bf16[128,640]{1,0:T(8,128)(2,1)S(1)}, bf16[128,640]{1,0:T(8,128)(2,1)S(1)}, u32[]{:S(2)}, u32[]{:S(2)}) collective-permute-start(bf16[128,640]{1,0:T(8,128)(2,1)S(1)} %fusion.3), channel_id=1, source_target_pairs={{0,64},{1,9},{16,80},{17,25},{32,96},{33,41},{48,112},{49,57},{4,6... | collective-permute-start | bytes 491528 | tf_op jit(solution)/shard_map/ppermute | solution.py:40
  38.8 5.7 %collective-permute-start.12 = (bf16[128,640]{1,0:T(8,128)(2,1)S(1)}, bf16[128,640]{1,0:T(8,128)(2,1)S(1)}, u32[]{:S(2)}, u32[]{:S(2)}) collective-permute-start(bf16[128,640]{1,0:T(8,128)(2,1)S(1)} %fusion.3), channel_id=1, source_target_pairs={{0,66},{1,13},{16,82},{17,29},{32,98},{33,45},{48,114},{49,61},{4,... | collective-permute-start | bytes 491528 | tf_op jit(solution)/shard_map/ppermute | solution.py:40
  39.7 5.6 %collective-permute-start.11 = (bf16[128,640]{1,0:T(8,128)(2,1)S(1)}, bf16[128,640]{1,0:T(8,128)(2,1)S(1)}, u32[]{:S(2)}, u32[]{:S(2)}) collective-permute-start(bf16[128,640]{1,0:T(8,128)(2,1)S(1)} %fusion.3), channel_id=1, source_target_pairs={{0,2},{1,5},{16,18},{17,21},{32,34},{33,37},{48,50},{49,53},{4,6},... | collective-permute-start | bytes 491528 | tf_op jit(solution)/shard_map/ppermute | solution.py:40
  40.5 8.5 %collective-permute-start.23 = (bf16[128,640]{1,0:T(8,128)(2,1)S(1)}, bf16[128,640]{1,0:T(8,128)(2,1)S(1)}, u32[]{:S(2)}, u32[]{:S(2)}) collective-permute-start(bf16[128,640]{1,0:T(8,128)(2,1)S(1)} %add_convert_fusion.refs_4_), channel_id=1, source_target_pairs={{0,2},{1,17},{16,18},{17,33},{32,34},{33,49},{48,50},{49,1},{4,6},... | collective-permute-start | bytes 491528 | tf_op jit(solution)/shard_map/ppermute | solution.py:40
  41.6 7.3 %collective-permute-start.24 = (bf16[128,640]{1,0:T(8,128)(2,1)S(1)}, bf16[128,640]{1,0:T(8,128)(2,1)S(1)}, u32[]{:S(2)}, u32[]{:S(2)}) collective-permute-start(bf16[128,640]{1,0:T(8,128)(2,1)S(1)} %add_convert_fusion.refs_4_), channel_id=1, source_target_pairs={{0,64},{1,33},{16,80},{17,49},{32,96},{33,1},{48,112},{49,17},{4,6... | collective-permute-start | bytes 491528 | tf_op jit(solution)/shard_map/ppermute | solution.py:40
  44.5 4.5 %collective-permute-start.25 = (bf16[128,640]{1,0:T(8,128)(2,1)S(1)}, bf16[128,640]{1,0:T(8,128)(2,1)S(1)}, u32[]{:S(2)}, u32[]{:S(2)}) collective-permute-start(bf16[128,640]{1,0:T(8,128)(2,1)S(1)} %add_convert_fusion.refs_4_), channel_id=1, source_target_pairs={{0,66},{1,49},{16,82},{17,1},{32,98},{33,17},{48,114},{49,33},{4,7... | collective-permute-start | bytes 491528 | tf_op jit(solution)/shard_map/ppermute | solution.py:40
  45.4 5.9 %collective-permute-start.14 = (bf16[128,640]{1,0:T(8,128)(2,1)S(1)}, bf16[128,640]{1,0:T(8,128)(2,1)S(1)}, u32[]{:S(2)}, u32[]{:S(2)}) collective-permute-start(bf16[128,640]{1,0:T(8,128)(2,1)S(1)} %add_convert_fusion.1.refs_0_.piece0), channel_id=1, source_target_pairs={{0,16},{1,17},{16,32},{17,33},{32,48},{33,49},{48,0},{49,1},{4,20}... | collective-permute-start | bytes 491528 | tf_op jit(solution)/shard_map/ppermute | solution.py:40
  46.3 7.2 %collective-permute-start.15 = (bf16[128,640]{1,0:T(8,128)(2,1)S(1)}, bf16[128,640]{1,0:T(8,128)(2,1)S(1)}, u32[]{:S(2)}, u32[]{:S(2)}) collective-permute-start(bf16[128,640]{1,0:T(8,128)(2,1)S(1)} %add_convert_fusion.1.refs_0_.piece0), channel_id=1, source_target_pairs={{0,32},{1,33},{16,48},{17,49},{32,0},{33,1},{48,16},{49,17},{4,36}... | collective-permute-start | bytes 491528 | tf_op jit(solution)/shard_map/ppermute | solution.py:40
  48.9 5.3 %collective-permute-start.16 = (bf16[128,640]{1,0:T(8,128)(2,1)S(1)}, bf16[128,640]{1,0:T(8,128)(2,1)S(1)}, u32[]{:S(2)}, u32[]{:S(2)}) collective-permute-start(bf16[128,640]{1,0:T(8,128)(2,1)S(1)} %add_convert_fusion.1.refs_0_.piece0), channel_id=1, source_target_pairs={{0,48},{1,49},{16,0},{17,1},{32,16},{33,17},{48,32},{49,33},{4,52}... | collective-permute-start | bytes 491528 | tf_op jit(solution)/shard_map/ppermute | solution.py:40
  54.6 5.9 %collective-permute-start.28 = (bf16[192,512]{1,0:T(8,128)(2,1)S(1)}, bf16[192,512]{1,0:T(8,128)(2,1)S(1)}, u32[]{:S(2)}, u32[]{:S(2)}) collective-permute-start(bf16[192,512]{1,0:T(8,128)(2,1)S(1)} %get-tuple-element.58), channel_id=1, source_target_pairs={{0,4},{1,3},{16,20},{17,19},{32,36},{33,35},{48,52},{49,51},{4,8},... | collective-permute-start | bytes 589832 | tf_op jit(solution)/shard_map/ppermute | solution.py:40
  55.4 7.8 %collective-permute-start.27 = (bf16[192,512]{1,0:T(8,128)(2,1)S(1)}, bf16[192,512]{1,0:T(8,128)(2,1)S(1)}, u32[]{:S(2)}, u32[]{:S(2)}) collective-permute-start(bf16[192,512]{1,0:T(8,128)(2,1)S(1)} %get-tuple-element.57), channel_id=1, source_target_pairs={{0,8},{1,65},{16,24},{17,81},{32,40},{33,97},{48,56},{49,113},{4,1... | collective-permute-start | bytes 589832 | tf_op jit(solution)/shard_map/ppermute | solution.py:40
  58.1 5.3 %collective-permute-start.26 = (bf16[192,512]{1,0:T(8,128)(2,1)S(1)}, bf16[192,512]{1,0:T(8,128)(2,1)S(1)}, u32[]{:S(2)}, u32[]{:S(2)}) collective-permute-start(bf16[192,512]{1,0:T(8,128)(2,1)S(1)} %get-tuple-element.56), channel_id=1, source_target_pairs={{0,12},{1,67},{16,28},{17,83},{32,44},{33,99},{48,60},{49,115},{4,... | collective-permute-start | bytes 589832 | tf_op jit(solution)/shard_map/ppermute | solution.py:40
  63.6 6.1 %collective-permute-start.29 = (f32[192]{0:T(256)S(1)}, f32[192]{0:T(256)S(1)}, u32[]{:S(2)}, u32[]{:S(2)}) collective-permute-start(f32[192]{0:T(256)S(1)} %fusion), channel_id=1, source_target_pairs={{0,1},{1,0},{2,3},{3,2},{4,5},{5,4},{6,7},{7,6},{8,9},{9,8},{10,11... | collective-permute-start | bytes 2312 | tf_op jit(solution)/shard_map/ppermute | solution.py:44
